TPU v7x, 512 devices: a whole 4x4x16 slice. The times are simulated.
512 devices in a mesh: blk: 32 (over z, y_lo), col: 16 (over x, y_hi, core).
Axes of the slice: x: 4, y: 4 (y_hi: 2, y_lo: 2; y = y_hi * 2 + y_lo), z: 16, core: 2. Of those that a mesh axis runs over, the one named last changes fastest.
Arguments:
- iterate: float32 [4096, 18432], P('blk', 'col'), may hold values from -6 to 6
Outputs:
- updated: float32 [4096, 18432], P('blk', 'col')
All inputs are finite; a program needn't handle non-finite values.
Results may differ from a plain program's by a relative error of at most 0.012.
The roundings to bfloat16 on the way count: a program that leaves them out, or rounds other values in their place, can miss the bound.
Values may be sent and summed in bfloat16 or wider, within the bound.
No kernel may reach another device: no remote copies, remote signals or barrier semaphores. Data moves between devices by JAX's collectives and lax.ppermute only.
A program may use at most 64 MiB of HBM per device.

v0:
```python
import jax
import jax.numpy as jnp
from jax import lax
from jax.sharding import PartitionSpec as P


def per_device(iterate):
    rounded = iterate.astype(jnp.bfloat16)
    row_count = rounded.shape[0]
    col_count = rounded.shape[1]
    cycle_size = lax.axis_size("blk")
    total_rows = row_count * cycle_size
    total_cols = col_count * lax.axis_size("col")
    gathered = lax.all_gather(rounded, "blk", axis=0, tiled=True)
    partial_value = lax.dot_general(
        rounded, gathered, (((1,), (1,)), ((), ())), preferred_element_type=jnp.float32
    )
    gram_width = total_rows // lax.axis_size("col")
    gram_whole = lax.psum(partial_value, "col") / total_cols
    gram_low = gram_whole.astype(jnp.bfloat16)
    gram_piece = lax.dynamic_slice_in_dim(
        gram_whole, lax.axis_index("col") * gram_width, gram_width, 1
    )
    piece_low = gram_piece.astype(jnp.bfloat16)
    square = jnp.dot(
        gram_low,
        lax.all_gather(piece_low, "blk", axis=0, tiled=True),
        preferred_element_type=jnp.float32,
    )
    poly_piece = (-4.775 * gram_piece + 2.0315 * square).astype(jnp.bfloat16)
    poly_row = lax.all_gather(poly_piece, "col", axis=1, tiled=True)
    product = jnp.dot(poly_row, gathered, preferred_element_type=jnp.float32)
    return 3.4445 * rounded.astype(jnp.float32) + product


def solution(mesh):
    in_specs = (P("blk", "col"),)
    out_specs = P("blk", "col")
    return jax.shard_map(
        per_device, mesh=mesh, in_specs=in_specs, out_specs=out_specs, check_vma=False
    )
```

profile of v0, /device:TPU:1, one launch (start us, length us, event | category | flops | bytes accessed | tf_op | source)
XLA Modules:
  0.0 612.9 jit_solution(10804058580266662905)
XLA Ops:
  6.5 0.0 all-gather.4.cloned.1.call-start
  6.5 1.8 convert_element_type.15
  8.3 0.0 all-gather.4.cloned.1.call-update
  8.4 0.0 all-reduce.2.cloned.1.call-start
  8.4 221.6 %all-gather.4.cloned.1.call-done = bf16[4096,1152]{1,0:T(8,128)(2,1)} async-done(((bf16[128,1152]{1,0:T(8,128)(2,1)}), bf16[4096,1152]{1,0:T(8,128)(2,1)}) %all-gather.4.cloned.1.call-update) | async-done | bytes 9437200 | tf_op jit(solution)/shard_map/all_gather | solution.py:14
  230.0 8.3 %fusion.3 = f32[128,4096]{1,0:T(8,128)} fusion(bf16[128,1152]{1,0:T(8,128)(2,1)} %convert_element_type.15, bf16[4096,1152]{1,0:T(8,128)(2,1)} %all-gather.4.cloned.1.call-done), kind=kOutput, calls=%fused_computation.7 | convolution fusion | flops 1207959552 | bytes 11829248 | tf_op jit(solution)/shard_map/dot_general | solution.py:15
  238.3 0.0 all-reduce.2.cloned.1.call-update
  238.4 0.0 all-gather.6.cloned.1.call-start
  238.4 161.0 %all-reduce.2.cloned.1.call-done = f32[128,4096]{1,0:T(8,128)} async-done(((f32[128,4096]{1,0:T(8,128)}), f32[128,4096]{1,0:T(8,128)}) %all-reduce.2.cloned.1.call-update) | async-done | bytes 2097168 | tf_op jit(solution)/shard_map/psum | solution.py:19
  399.4 1.8 broadcast_multiply_fusion
  401.2 0.6 dynamic-slice_convert_fusion
  401.8 0.0 all-gather.6.cloned.1.call-update
  401.8 0.0 copy-start
  401.9 0.0 all-gather.8.cloned.1.call-start
  401.9 114.7 %all-gather.6.cloned.1.call-done = bf16[4096,256]{1,0:T(8,128)(2,1)} async-done(((bf16[128,256]{1,0:T(8,128)(2,1)}), bf16[4096,256]{1,0:T(8,128)(2,1)}) %all-gather.6.cloned.1.call-update) | async-done | bytes 2097168 | tf_op jit(solution)/shard_map/all_gather | solution.py:27
  516.6 2.7 fusion.1
  519.2 0.0 all-gather.8.cloned.1.call-update
  519.3 80.8 %all-gather.8.cloned.1.call-done = bf16[128,4096]{1,0:T(8,128)(2,1)} async-done(((bf16[128,256]{1,0:T(8,128)(2,1)}), bf16[128,4096]{1,0:T(8,128)(2,1)}) %all-gather.8.cloned.1.call-update) | async-done | bytes 1048592 | tf_op jit(solution)/shard_map/all_gather | solution.py:31
  600.0 0.0 copy-done
  600.0 6.4 %convolution_add_fusion = f32[128,1152]{1,0:T(8,128)} fusion(bf16[128,4096]{1,0:T(8,128)(2,1)} %all-gather.8.cloned.1.call-done, bf16[4096,1152]{1,0:T(8,128)(2,1)} %all-gather.4.cloned.1.call-done, bf16[128,1152]{1,0:T(8,128)(2,1)S(1)} %copy-done), kind=kOutput, calls=%fused_computation | convolution fusion | flops 1208401920 | bytes 11370496 | tf_op jit(solution)/shard_map/dot_general | solution.py:32
Async XLA Ops:
  6.5 223.5 %all-gather.4.cloned.1.call-start = ((), (), s32[]{:S(2)}) async-start(), calls=%async_computation | async-start | bytes 9732096 | tf_op jit(solution)/shard_map/all_gather | solution.py:14
  8.4 391.0 %all-reduce.2.cloned.1.call-start = ((), (), s32[]{:S(2)}) async-start(), calls=%async_computation.1 | async-start | bytes 4194304 | tf_op jit(solution)/shard_map/psum | solution.py:19
  238.4 278.2 %all-gather.6.cloned.1.call-start = ((), (), s32[]{:S(2)}) async-start(), calls=%async_computation.2 | async-start | bytes 2162688 | tf_op jit(solution)/shard_map/all_gather | solution.py:27
  401.8 198.2 %copy-start = (bf16[128,1152]{1,0:T(8,128)(2,1)S(1)}, bf16[128,1152]{1,0:T(8,128)(2,1)}, u32[]{:S(2)}) copy-start(bf16[128,1152]{1,0:T(8,128)(2,1)} %convert_element_type.15) | copy-start | bytes 884740
  401.9 198.2 %all-gather.8.cloned.1.call-start = ((), (), s32[]{:S(2)}) async-start(), calls=%async_computation.3 | async-start | bytes 1114112 | tf_op jit(solution)/shard_map/all_gather | solution.py:31
Sparse Core Ops, SparseCore 0:
  9.4 220.5 all-gather.3
  238.5 160.8 all-reduce.1
  402.0 114.5 all-gather.5
  519.6 80.4 all-gather.7
where the time goes:
time: 613 us
  waiting for transfers between devices  578 us (94%)
  matrix products  17.4 us (3%)
  between operations  13.1 us (2%)
    all_gather x1, waiting for transfers between devices, per_device(): gathered = lax.all_gather(rounded, 'blk', axis=0, tiled=True)  222 us
    psum x1, waiting for transfers between devices, per_device(): gram_whole = lax.psum(partial_value, 'col') / total_cols  161 us
    all_gather x1, waiting for transfers between devices, per_device(): lax.all_gather(piece_low, 'blk', axis=0, tiled=True)  115 us
    all_gather x1, waiting for transfers between devices, per_device(): poly_row = lax.all_gather(poly_piece, 'col', axis=1, tiled=True)  80.8 us
  transfers between devices with their start and end apart: 4, of which 4 were waited for; matrix products, arithmetic and copies ran while one was open for 0% of the time, Pallas kernels for 0%

commit v1 on v0

v1 whole, which is shorter than its diff:
```python
import jax
import jax.numpy as jnp
from jax import lax
from jax.sharding import Mesh, PartitionSpec as P

PLANE = ("ylo", "x", "yhi")
CORE_SWAP = ((0, 1), (1, 0))
TURN = ((0, 0), (1, 2), (2, 1), (3, 3))


def share(piece, size):
    copies = jnp.broadcast_to(piece[None], (size,) + piece.shape)
    return lax.all_to_all(copies, PLANE, 0, 0)


def nt(left, right):
    return lax.dot_general(
        left, right, (((1,), (1,)), ((), ())), preferred_element_type=jnp.float32
    )


def tn(left, right):
    return lax.dot_general(
        left, right, (((0,), (0,)), ((), ())), preferred_element_type=jnp.float32
    )


def per_device(iterate):
    rounded = iterate.astype(jnp.bfloat16)
    rows, cols = rounded.shape
    slabs = lax.axis_size("z")
    chips = lax.axis_size(PLANE)
    total_cols = cols * chips
    own = lax.ppermute(rounded, ("ylo", "core"), TURN)
    half = lax.all_gather(own, "z", axis=0, tiled=True)
    other = lax.ppermute(own, "core", CORE_SWAP)
    partial_gram = nt(half, jnp.concatenate([own, other], 0))
    partial_gram = partial_gram.reshape(chips, rows, 2 * rows)
    summands = lax.all_to_all(partial_gram, PLANE, 0, 0)
    gram = summands.sum(0) / total_cols
    gram_low = gram.astype(jnp.bfloat16)
    left = lax.all_gather(gram_low, "z", axis=0)
    right_own = share(gram_low, chips)
    right_other = lax.ppermute(right_own, "core", CORE_SWAP)
    right_other = jnp.concatenate(
        [right_other[:, :, rows:], right_other[:, :, :rows]], 2
    )
    square = 0.0
    for place, right in enumerate((right_own, right_other)):
        square = square + lax.dot_general(
            left[:, :, place * rows : (place + 1) * rows],
            right,
            (((0, 2), (0, 1)), ((), ())),
            preferred_element_type=jnp.float32,
        )
    poly = (-4.775 * gram + 2.0315 * square).astype(jnp.bfloat16)
    panel = share(poly, chips).reshape(chips * rows, 2 * rows)
    away = tn(panel[:, rows:], half)
    away = lax.ppermute(away, "core", CORE_SWAP)
    product = tn(panel[:, :rows], half) + away
    product = lax.ppermute(product, ("ylo", "core"), TURN)
    return 3.4445 * rounded.astype(jnp.float32) + product


def solution(mesh):
    fine = Mesh(mesh.devices.reshape(16, 2, 4, 2, 2), ("z", "ylo", "x", "yhi", "core"))
    spec = P(("z", "ylo"), ("x", "yhi", "core"))
    return jax.shard_map(
        per_device, mesh=fine, in_specs=(spec,), out_specs=spec, check_vma=False
    )
```

time: 613 us -> 247 us (0.40)
  waiting for transfers between devices: 578 us -> 124 us
  blocking collectives: 0 us -> 58.9 us
  starting transfers between devices: 0.13 us -> 36.7 us
  matrix products: 17.4 us -> 6.41 us
    all_gather x3 -> x2, waiting for transfers between devices: 417 us -> 107 us  [the longest x1 72.7 us: per_device(): half = lax.all_gather(own, 'z', axis=0, tiled=True)]
    psum x1 -> x0, waiting for transfers between devices: 161 us -> none  [per_device(): gram_whole = lax.psum(partial_value, 'col') / total_cols]
    all_to_all x0 -> x3, blocking collectives: none -> 58.9 us  [the longest x2 32.4 us: share(): return lax.all_to_all(copies, PLANE, 0, 0)]
    ppermute x0 -> x5, starting transfers between devices: none -> 36.6 us  [the longest x1 15.2 us: per_device(): away = lax.ppermute(away, 'core', CORE_SWAP)]
    ppermute x0 -> x5, waiting for transfers between devices: none -> 16.5 us  [the longest x1 8.74 us: per_device(): product = lax.ppermute(product, ('ylo', 'core'), TURN)]
    dot_general x3 -> x5, matrix products: 17.4 us -> 6.41 us  [the longest x1 3.99 us: nt(): lax.dot_general(left, right, (((1,), (1,)), ((), ())), preferred_element_...]
  transfers between devices with their start and end apart: 4 -> 7, of which waited for: 4 -> 6; matrix products, arithmetic and copies ran while one was open for 0% -> 1% of each run, Pallas kernels for 0% -> 0%
where the time goes in v1:
time: 247 us
  waiting for transfers between devices  124 us (50%)
  blocking collectives  58.9 us (24%)
  starting transfers between devices  36.7 us (15%)
  between operations  13.6 us (6%)
  matrix products  6.41 us (3%)
  local copies, waits for them, and re-layouts  5.05 us (2%)
  other arithmetic  2.73 us (1%)
    all_gather x1, waiting for transfers between devices, per_device(): half = lax.all_gather(own, 'z', axis=0, tiled=True)  72.7 us
    all_gather x1, waiting for transfers between devices, per_device(): left = lax.all_gather(gram_low, 'z', axis=0)  34.4 us
    all_to_all x2, blocking collectives, share(): return lax.all_to_all(copies, PLANE, 0, 0)  32.4 us
    all_to_all x1, blocking collectives, per_device(): summands = lax.all_to_all(partial_gram, PLANE, 0, 0)  26.5 us
    ppermute x1, starting transfers between devices, per_device(): away = lax.ppermute(away, 'core', CORE_SWAP)  15.2 us
    ppermute x1, starting transfers between devices, per_device(): right_other = lax.ppermute(right_own, 'core', CORE_SWAP)  12.5 us
    ppermute x1, waiting for transfers between devices, per_device(): product = lax.ppermute(product, ('ylo', 'core'), TURN)  8.74 us
  transfers between devices with their start and end apart: 7, of which 6 were waited for; matrix products, arithmetic and copies ran while one was open for 1% of the time, Pallas kernels for 0%

profile of v1, /device:TPU:1, one launch (start us, length us, event | category | flops | bytes accessed | tf_op | source)
XLA Modules:
  0.0 247.0 jit_solution(3742547292634436099)
XLA Ops:
  6.5 0.0 all-gather.4.cloned.1.call-start
  6.5 1.1 convert_element_type.23
  7.6 4.6 %collective-permute-start = (bf16[128,1152]{1,0:T(8,128)(2,1)S(1)}, bf16[128,1152]{1,0:T(8,128)(2,1)S(1)}, u32[]{:S(2)}, u32[]{:S(2)}) collective-permute-start(bf16[128,1152]{1,0:T(8,128)(2,1)S(1)} %convert_element_type.23), channel_id=1, source_target_pairs={{0,0},{1,16},{16,1},{17,17},{2,2},{3,18},{18,3},{19,19},{4,4},{5,2... | collective-permute-start | bytes 884744 | tf_op jit(solution)/shard_map/ppermute | solution.py:34
  12.2 4.4 %collective-permute-done = bf16[128,1152]{1,0:T(8,128)(2,1)S(1)} collective-permute-done((bf16[128,1152]{1,0:T(8,128)(2,1)S(1)}, bf16[128,1152]{1,0:T(8,128)(2,1)S(1)}, u32[]{:S(2)}, u32[]{:S(2)}) %collective-permute-start) | collective-permute-done | bytes 294944 | tf_op jit(solution)/shard_map/ppermute | solution.py:34
  16.6 0.0 copy-start.1
  16.6 0.7 copy-done.1
  17.3 0.0 all-gather.4.cloned.1.call-update
  17.4 0.0 all-gather.6.cloned.1.call-start
  17.4 1.9 collective-permute-start.1
  19.3 1.8 collective-permute-done.1
  21.1 72.7 %all-gather.4.cloned.1.call-done = bf16[2048,1152]{1,0:T(8,128)(2,1)} async-done(((bf16[128,1152]{1,0:T(8,128)(2,1)}), bf16[2048,1152]{1,0:T(8,128)(2,1)}) %all-gather.4.cloned.1.call-update) | async-done | bytes 4718608 | tf_op jit(solution)/shard_map/all_gather | solution.py:35
  93.8 4.0 %convolution_bitcast_fusion = f32[32,16,8,128]{3,2,1,0:T(8,128)S(1)} fusion(bf16[2048,1152]{1,0:T(8,128)(2,1)} %all-gather.4.cloned.1.call-done, bf16[128,1152]{1,0:T(8,128)(2,1)S(1)} %collective-permute-done.1, bf16[128,1152]{1,0:T(8,128)(2,1)} %copy-done.1), kind=kOutput, calls=%fused_computation.2 | convolution fusion | flops 1209139200 | bytes 7405568 | tf_op jit(solution)/shard_map/dot_general | solution.py:17
  97.8 0.2 copy.10
  98.0 26.5 %all_to_all.15 = f32[16,128,256]{1,2,0:T(8,128)S(1)} all-to-all(f32[16,128,256]{1,2,0:T(8,128)S(1)} %bitcast.26), channel_id=1, replica_groups=mesh['z'=16,'ylo'=2,'x'=4,'yhi'=2,'core'=2] {'ylo','x','yhi'}, dimensions={0} | all-to-all | bytes 4194304 | tf_op jit(solution)/shard_map/all_to_all | solution.py:39
  124.6 0.1 reduce_sum.9
  124.7 0.6 multiply_convert_fusion
  125.3 0.0 all-gather.6.cloned.1.call-update
  125.3 0.9 copy.6
  126.3 0.1 broadcast_in_dim.4
  126.4 14.7 %all_to_all.16 = bf16[16,128,256]{2,1,0:T(8,128)(2,1)S(1)} all-to-all(bf16[16,128,256]{2,1,0:T(8,128)(2,1)S(1)} %broadcast_in_dim.4), channel_id=1, replica_groups=mesh['z'=16,'ylo'=2,'x'=4,'yhi'=2,'core'=2] {'ylo','x','yhi'}, dimensions={0} | all-to-all | bytes 2097152 | tf_op jit(solution)/shard_map/all_to_all | solution.py:13
  141.1 12.5 %collective-permute-start.2 = (bf16[16,128,256]{2,1,0:T(8,128)(2,1)S(1)}, bf16[16,128,256]{2,1,0:T(8,128)(2,1)}, u32[]{:S(2)}, u32[]{:S(2)}) collective-permute-start(bf16[16,128,256]{2,1,0:T(8,128)(2,1)S(1)} %all_to_all.16), channel_id=1, source_target_pairs={{0,1},{1,0},{2,3},{3,2},{4,5},{5,4},{6,7},{7,6},{8,9},{9,8},{10,11... | collective-permute-start | bytes 3145736 | tf_op jit(solution)/shard_map/ppermute | solution.py:44
  153.6 0.0 slice-start
  153.6 0.1 copy.4
  153.7 34.4 %all-gather.6.cloned.1.call-done = bf16[2048,256]{0,1:T(8,128)(2,1)} async-done(((bf16[128,256]{0,1:T(8,128)(2,1)}), bf16[2048,256]{0,1:T(8,128)(2,1)}) %all-gather.6.cloned.1.call-update) | async-done | bytes 1048592 | tf_op jit(solution)/shard_map/all_gather | solution.py:42
  188.1 1.5 copy.5
  189.6 0.3 convolution_bitcast_fusion.2
  189.9 0.0 slice-start.1
  189.9 0.0 collective-permute-done.2
  189.9 1.4 fusion.17
  191.4 0.3 fusion.3
  191.7 0.1 broadcast_in_dim.5
  191.8 17.6 %all_to_all.17 = bf16[16,128,256]{2,1,0:T(8,128)(2,1)S(1)} all-to-all(bf16[16,128,256]{2,1,0:T(8,128)(2,1)S(1)} %broadcast_in_dim.5), channel_id=1, replica_groups=mesh['z'=16,'ylo'=2,'x'=4,'yhi'=2,'core'=2] {'ylo','x','yhi'}, dimensions={0} | all-to-all | bytes 2097152 | tf_op jit(solution)/shard_map/all_to_all | solution.py:13
  209.4 0.0 slice-done
  209.4 0.0 slice-done.1
  209.4 0.0 copy-start
  209.4 0.9 fusion.10
  210.3 15.2 %collective-permute-start.3 = (f32[128,1152]{1,0:T(8,128)S(1)}, f32[128,1152]{1,0:T(8,128)S(1)}, u32[]{:S(2)}, u32[]{:S(2)}) collective-permute-start(f32[128,1152]{1,0:T(8,128)S(1)} %fusion.10), channel_id=1, source_target_pairs={{0,1},{1,0},{2,3},{3,2},{4,5},{5,4},{6,7},{7,6},{8,9},{9,8},{10,11... | collective-permute-start | bytes 1769480 | tf_op jit(solution)/shard_map/ppermute | solution.py:59
  225.6 1.6 collective-permute-done.3
  227.2 0.9 convolution_add_fusion
  228.1 2.5 collective-permute-start.4
  230.5 8.7 %collective-permute-done.4 = f32[128,1152]{1,0:T(8,128)S(1)} collective-permute-done((f32[128,1152]{1,0:T(8,128)S(1)}, f32[128,1152]{1,0:T(8,128)S(1)}, u32[]{:S(2)}, u32[]{:S(2)}) %collective-permute-start.4) | collective-permute-done | bytes 589856 | tf_op jit(solution)/shard_map/ppermute | solution.py:61
  239.3 0.0 copy-done
  239.3 0.9 multiply_add_fusion
  (1 shorter events, 0.0 us)
Async XLA Ops:
  6.5 87.3 %all-gather.4.cloned.1.call-start = ((), (), s32[]{:S(2)}) async-start(), calls=%async_computation.3 | async-start | bytes 5013504 | tf_op jit(solution)/shard_map/all_gather | solution.py:35
  7.6 9.0 %collective-permute-start = (bf16[128,1152]{1,0:T(8,128)(2,1)S(1)}, bf16[128,1152]{1,0:T(8,128)(2,1)S(1)}, u32[]{:S(2)}, u32[]{:S(2)}) collective-permute-start(bf16[128,1152]{1,0:T(8,128)(2,1)S(1)} %convert_element_type.23), channel_id=1, source_target_pairs={{0,0},{1,16},{16,1},{17,17},{2,2},{3,18},{18,3},{19,19},{4,4},{5,2... | collective-permute-start | bytes 884744 | tf_op jit(solution)/shard_map/ppermute | solution.py:34
  16.6 0.7 copy-start.1
  17.4 170.7 %all-gather.6.cloned.1.call-start = ((), (), s32[]{:S(2)}) async-start(), calls=%async_computation.4 | async-start | bytes 1114112 | tf_op jit(solution)/shard_map/all_gather | solution.py:42
  17.4 3.7 %collective-permute-start.1 = (bf16[128,1152]{1,0:T(8,128)(2,1)}, bf16[128,1152]{1,0:T(8,128)(2,1)S(1)}, u32[]{:S(2)}, u32[]{:S(2)}) collective-permute-start(bf16[128,1152]{1,0:T(8,128)(2,1)} %copy-done.1), channel_id=1, source_target_pairs={{0,1},{1,0},{2,3},{3,2},{4,5},{5,4},{6,7},{7,6},{8,9},{9,8},{10,11... | collective-permute-start | bytes 884744 | tf_op jit(solution)/shard_map/ppermute | solution.py:36
  141.1 48.8 %collective-permute-start.2 = (bf16[16,128,256]{2,1,0:T(8,128)(2,1)S(1)}, bf16[16,128,256]{2,1,0:T(8,128)(2,1)}, u32[]{:S(2)}, u32[]{:S(2)}) collective-permute-start(bf16[16,128,256]{2,1,0:T(8,128)(2,1)S(1)} %all_to_all.16), channel_id=1, source_target_pairs={{0,1},{1,0},{2,3},{3,2},{4,5},{5,4},{6,7},{7,6},{8,9},{9,8},{10,11... | collective-permute-start | bytes 3145736 | tf_op jit(solution)/shard_map/ppermute | solution.py:44
  153.6 55.9 %slice-start = ((s8[4718592]{0:T(1024)(128)(4,1)}), s8[524288]{0:T(1024)(128)(4,1)S(1)}, s32[]{:S(2)}) async-start(s8[4718592]{0:T(1024)(128)(4,1)} %bitcast.24), calls=%async_computation.5 | async-start | bytes 1048576
  189.9 19.5 %slice-start.1 = ((s8[4718592]{0:T(1024)(128)(4,1)}), s8[4194304]{0:T(1024)(128)(4,1)S(1)}, s32[]{:S(2)}) async-start(s8[4718592]{0:T(1024)(128)(4,1)} %bitcast.24), calls=%async_computation.6 | async-start | bytes 8388608
  209.4 29.8 %copy-start = (f32[128,1152]{1,0:T(8,128)S(1)}, f32[128,1152]{1,0:T(8,128)}, u32[]{:S(2)}) copy-start(f32[128,1152]{1,0:T(8,128)} %param.1) | copy-start | bytes 1769476
  210.3 16.8 %collective-permute-start.3 = (f32[128,1152]{1,0:T(8,128)S(1)}, f32[128,1152]{1,0:T(8,128)S(1)}, u32[]{:S(2)}, u32[]{:S(2)}) collective-permute-start(f32[128,1152]{1,0:T(8,128)S(1)} %fusion.10), channel_id=1, source_target_pairs={{0,1},{1,0},{2,3},{3,2},{4,5},{5,4},{6,7},{7,6},{8,9},{9,8},{10,11... | collective-permute-start | bytes 1769480 | tf_op jit(solution)/shard_map/ppermute | solution.py:59
  228.1 11.2 %collective-permute-start.4 = (f32[128,1152]{1,0:T(8,128)S(1)}, f32[128,1152]{1,0:T(8,128)S(1)}, u32[]{:S(2)}, u32[]{:S(2)}) collective-permute-start(f32[128,1152]{1,0:T(8,128)S(1)} %convolution_add_fusion), channel_id=1, source_target_pairs={{0,0},{1,16},{16,1},{17,17},{2,2},{3,18},{18,3},{19,19},{4,4},{5,2... | collective-permute-start | bytes 1769480 | tf_op jit(solution)/shard_map/ppermute | solution.py:61
Sparse Core Ops, SparseCore 0:
  17.5 76.2 all-gather.3
  125.5 62.6 all-gather.5

commit v2 on v1

v2 whole, which is shorter than its diff:
```python
import jax
import jax.numpy as jnp
from jax import lax
from jax.sharding import Mesh, PartitionSpec as P

AXES = ("zg", "zp", "ylo", "x", "yhi", "core")
SIZES = (8, 2, 2, 4, 2, 2)
LINE = ("zg", "zp")
PLANE = ("ylo", "x", "yhi")
SWAP = ((0, 1), (1, 0))
TURN = ((0, 0), (1, 2), (2, 1), (3, 3))


def share(piece, size):
    copies = jnp.broadcast_to(piece[None], (size,) + piece.shape)
    return lax.all_to_all(copies, PLANE, 0, 0)


def nt(left, right):
    return lax.dot_general(
        left, right, (((1,), (1,)), ((), ())), preferred_element_type=jnp.float32
    )


def tn(left, right):
    return lax.dot_general(
        left, right, (((0,), (0,)), ((), ())), preferred_element_type=jnp.float32
    )


def per_device(iterate):
    rounded = iterate.astype(jnp.bfloat16)
    rows, cols = rounded.shape
    slabs = lax.axis_size(LINE)
    chips = lax.axis_size(PLANE)
    total_cols = cols * chips
    own = lax.ppermute(rounded, ("ylo", "core"), TURN)
    half = lax.all_gather(own, LINE, axis=0, tiled=True)
    other = lax.ppermute(own, "core", SWAP)
    partial_gram = nt(half, jnp.concatenate([own, other], 0))
    partial_gram = partial_gram.reshape(chips, rows, 2 * rows)
    summands = lax.all_to_all(partial_gram, PLANE, 0, 0)
    gram = summands.sum(0) / total_cols
    gram_low = gram.astype(jnp.bfloat16)
    same = lax.all_gather(gram_low, "zg", axis=0)
    cross = lax.ppermute(same, "zp", SWAP)
    gram_after, _ = lax.optimization_barrier((gram_low, same))
    right_own = share(gram_after, chips)
    right_other = lax.ppermute(right_own, "core", SWAP)
    right_other = jnp.concatenate(
        [right_other[:, :, rows:], right_other[:, :, :rows]], 2
    )
    even = lax.axis_index("zp") == 0
    left = jnp.stack(
        [jnp.where(even, same, cross), jnp.where(even, cross, same)], 1
    ).reshape(slabs, rows, 2 * rows)
    square = 0.0
    for place, right in enumerate((right_own, right_other)):
        square = square + lax.dot_general(
            left[:, :, place * rows : (place + 1) * rows],
            right,
            (((0, 2), (0, 1)), ((), ())),
            preferred_element_type=jnp.float32,
        )
    poly = (-4.775 * gram + 2.0315 * square).astype(jnp.bfloat16)
    panel = share(poly, chips).reshape(chips * rows, 2 * rows)
    away = tn(panel[:, rows:], half)
    away = lax.ppermute(away, "core", SWAP)
    product = tn(panel[:, :rows], half) + away
    product = lax.ppermute(product, ("ylo", "core"), TURN)
    return 3.4445 * lax.reduce_precision(iterate, 8, 7) + product


def solution(mesh):
    fine = Mesh(mesh.devices.reshape(SIZES), AXES)
    spec = P(("zg", "zp", "ylo"), ("x", "yhi", "core"))
    return jax.shard_map(
        per_device, mesh=fine, in_specs=(spec,), out_specs=spec, check_vma=False
    )
```

time: 247 us -> 234 us (0.947)
  waiting for transfers between devices: 124 us -> 99.9 us
  blocking collectives: 58.9 us -> 73.9 us
    all_gather x2 -> x1, waiting for transfers between devices: 107 us -> 72.8 us  [per_device(): half = lax.all_gather(own, LINE, axis=0, tiled=True)]
    all_gather x0 -> x1, blocking collectives: none -> 28 us  [per_device(): same = lax.all_gather(gram_low, 'zg', axis=0)]
    all_to_all x2 -> x1, blocking collectives: 32.4 us -> 19.4 us  [share(): return lax.all_to_all(copies, PLANE, 0, 0)]
    all_to_all x0 -> x1, waiting for transfers between devices: none -> 8.96 us  [share(): return lax.all_to_all(copies, PLANE, 0, 0)]
    ppermute x3 -> x4, starting transfers between devices: 29.6 us -> 24 us  [the longest x1 15.3 us: per_device(): right_other = lax.ppermute(right_own, 'core', SWAP)]
    all_to_all x0 -> x1, starting transfers between devices: none -> 3.86 us  [share(): return lax.all_to_all(copies, PLANE, 0, 0)]
    ppermute x3 -> x4, waiting for transfers between devices: 3.37 us -> 4.98 us  [the longest x1 1.76 us: per_device(): other = lax.ppermute(own, 'core', SWAP)]
  transfers between devices with their start and end apart: 7 -> 8, of which waited for: 6 -> 7; matrix products, arithmetic and copies ran while one was open for 1% -> 0% of each run, Pallas kernels for 0% -> 0%
where the time goes in v2:
time: 234 us
  waiting for transfers between devices  99.9 us (43%)
  blocking collectives  73.9 us (32%)
  starting transfers between devices  34.9 us (15%)
  between operations  13.6 us (6%)
  matrix products  6.38 us (3%)
  local copies, waits for them, and re-layouts  3.02 us (1%)
    all_gather x1, waiting for transfers between devices, per_device(): half = lax.all_gather(own, LINE, axis=0, tiled=True)  72.8 us
    all_gather x1, blocking collectives, per_device(): same = lax.all_gather(gram_low, 'zg', axis=0)  28 us
    all_to_all x1, blocking collectives, per_device(): summands = lax.all_to_all(partial_gram, PLANE, 0, 0)  26.5 us
    all_to_all x1, blocking collectives, share(): return lax.all_to_all(copies, PLANE, 0, 0)  19.4 us
    ppermute x1, starting transfers between devices, per_device(): right_other = lax.ppermute(right_own, 'core', SWAP)  15.3 us
    all_to_all x1, waiting for transfers between devices, share(): return lax.all_to_all(copies, PLANE, 0, 0)  8.96 us
    ppermute x1, waiting for transfers between devices, per_device(): product = lax.ppermute(product, ('ylo', 'core'), TURN)  8.75 us
  transfers between devices with their start and end apart: 8, of which 7 were waited for; matrix products, arithmetic and copies ran while one was open for 0% of the time, Pallas kernels for 0%

profile of v2, /device:TPU:1, one launch (start us, length us, event | category | flops | bytes accessed | tf_op | source)
XLA Modules:
  0.0 233.9 jit_solution(15976331422721148762)
XLA Ops:
  6.5 0.0 all-gather.3.cloned.1.call-start
  6.5 1.1 convert_element_type.19
  7.6 4.6 %collective-permute-start = (bf16[128,1152]{1,0:T(8,128)(2,1)S(1)}, bf16[128,1152]{1,0:T(8,128)(2,1)S(1)}, u32[]{:S(2)}, u32[]{:S(2)}) collective-permute-start(bf16[128,1152]{1,0:T(8,128)(2,1)S(1)} %convert_element_type.19), channel_id=1, source_target_pairs={{0,0},{1,16},{16,1},{17,17},{2,2},{3,18},{18,3},{19,19},{4,4},{5,2... | collective-permute-start | bytes 884744 | tf_op jit(solution)/shard_map/ppermute | solution.py:37
  12.2 4.4 %collective-permute-done = bf16[128,1152]{1,0:T(8,128)(2,1)S(1)} collective-permute-done((bf16[128,1152]{1,0:T(8,128)(2,1)S(1)}, bf16[128,1152]{1,0:T(8,128)(2,1)S(1)}, u32[]{:S(2)}, u32[]{:S(2)}) %collective-permute-start) | collective-permute-done | bytes 294944 | tf_op jit(solution)/shard_map/ppermute | solution.py:37
  16.6 0.0 copy-start.1
  16.6 0.7 copy-done.1
  17.3 0.0 all-gather.3.cloned.1.call-update
  17.4 1.9 collective-permute-start.1
  19.3 1.8 collective-permute-done.1
  21.1 72.8 %all-gather.3.cloned.1.call-done = bf16[2048,1152]{1,0:T(8,128)(2,1)} async-done(((bf16[128,1152]{1,0:T(8,128)(2,1)}), bf16[2048,1152]{1,0:T(8,128)(2,1)}) %all-gather.3.cloned.1.call-update) | async-done | bytes 4718608 | tf_op jit(solution)/shard_map/all_gather | solution.py:38
  93.8 4.0 %convolution_bitcast_fusion = f32[32,16,8,128]{3,2,1,0:T(8,128)S(1)} fusion(bf16[2048,1152]{1,0:T(8,128)(2,1)} %all-gather.3.cloned.1.call-done, bf16[128,1152]{1,0:T(8,128)(2,1)S(1)} %collective-permute-done.1, bf16[128,1152]{1,0:T(8,128)(2,1)} %copy-done.1), kind=kOutput, calls=%fused_computation.2 | convolution fusion | flops 1209139200 | bytes 7405568 | tf_op jit(solution)/shard_map/dot_general | solution.py:20
  97.8 0.2 copy.15
  98.0 26.5 %all_to_all.15 = f32[16,128,256]{1,2,0:T(8,128)S(1)} all-to-all(f32[16,128,256]{1,2,0:T(8,128)S(1)} %bitcast.36), channel_id=1, replica_groups=mesh['zg'=8,'zp'=2,'ylo'=2,'x'=4,'yhi'=2,'core'=2] {'ylo','x','yhi'}, dimensions={0} | all-to-all | bytes 4194304 | tf_op jit(solution)/shard_map/all_to_all | solution.py:42
  124.6 0.1 reduce_sum.9
  124.7 28.0 %all-gather = bf16[1024,256]{0,1:T(8,128)(2,1)S(1)} all-gather(bf16[128,256]{0,1:T(8,128)(2,1)S(1)} %multiply_convert_fusion), channel_id=2, replica_groups=mesh['zg'=8,'zp'=2,'ylo'=2,'x'=4,'yhi'=2,'core'=2] {'zg'}, dimensions={0}, use_global_device_ids=true | all-gather | bytes 589824 | tf_op jit(solution)/shard_map/all_gather | solution.py:45
  152.7 0.1 copy.13
  152.8 0.1 copy.10
  152.9 1.1 broadcast_in_dim.4
  154.0 3.9 %all-to-all-start.1 = ((bf16[16,128,256]{2,1,0:T(8,128)(2,1)}), bf16[16,128,256]{2,1,0:T(8,128)(2,1)S(1)}, u32[]{:S(2)}, u32[]{:S(2)}) async-start(bf16[16,128,256]{2,1,0:T(8,128)(2,1)} %broadcast_in_dim.4), calls=%async_computation.1 | async-start | bytes 2097152 | tf_op jit(solution)/shard_map/all_to_all | solution.py:16
  157.8 0.3 copy.7
  158.2 2.8 %collective-permute-start.2 = (bf16[8,128,256]{2,1,0:T(8,128)(2,1)S(1)}, bf16[8,128,256]{2,1,0:T(8,128)(2,1)S(1)}, u32[]{:S(2)}, u32[]{:S(2)}) collective-permute-start(bf16[8,128,256]{2,1,0:T(8,128)(2,1)S(1)} %copy.7), channel_id=1, source_target_pairs={{0,32},{32,0},{1,33},{33,1},{2,34},{34,2},{3,35},{35,3},{4,36},{36... | collective-permute-start | bytes 1572872 | tf_op jit(solution)/shard_map/ppermute | solution.py:46
  160.9 9.0 %all-to-all-done.1 = bf16[16,128,256]{2,1,0:T(8,128)(2,1)S(1)} async-done(((bf16[16,128,256]{2,1,0:T(8,128)(2,1)}), bf16[16,128,256]{2,1,0:T(8,128)(2,1)S(1)}, u32[]{:S(2)}, u32[]{:S(2)}) %all-to-all-start.1) | async-done | bytes 1048608 | tf_op jit(solution)/shard_map/all_to_all | solution.py:16
  169.9 15.3 %collective-permute-start.3 = (bf16[16,128,256]{2,1,0:T(8,128)(2,1)S(1)}, bf16[16,128,256]{2,1,0:T(8,128)(2,1)S(1)}, u32[]{:S(2)}, u32[]{:S(2)}) collective-permute-start(bf16[16,128,256]{2,1,0:T(8,128)(2,1)S(1)} %all-to-all-done.1), channel_id=1, source_target_pairs={{0,1},{1,0},{2,3},{3,2},{4,5},{5,4},{6,7},{7,6},{8,9},{9,8},{10,11... | collective-permute-start | bytes 3145736 | tf_op jit(solution)/shard_map/ppermute | solution.py:49
  185.2 0.1 copy.5
  185.3 0.0 collective-permute-done.2
  185.3 0.0 slice-start
  185.4 0.1 select_bitcast_fusion.1
  185.4 0.1 pad_maximum_fusion
  185.6 0.3 convolution_bitcast_fusion.2
  185.9 0.0 slice-start.1
  185.9 1.6 collective-permute-done.3
  187.5 0.3 fusion.17
  187.8 0.3 fusion.3
  188.1 0.1 broadcast_in_dim.5
  188.2 19.4 %all_to_all.16 = bf16[16,128,256]{2,1,0:T(8,128)(2,1)S(1)} all-to-all(bf16[16,128,256]{2,1,0:T(8,128)(2,1)S(1)} %broadcast_in_dim.5), channel_id=1, replica_groups=mesh['zg'=8,'zp'=2,'ylo'=2,'x'=4,'yhi'=2,'core'=2] {'ylo','x','yhi'}, dimensions={0} | all-to-all | bytes 2097152 | tf_op jit(solution)/shard_map/all_to_all | solution.py:16
  207.6 0.0 slice-done
  207.6 0.0 slice-done.1
  207.6 0.0 copy-start
  207.6 0.9 fusion.10
  208.5 4.0 %collective-permute-start.4 = (f32[128,1152]{1,0:T(8,128)S(1)}, f32[128,1152]{1,0:T(8,128)S(1)}, u32[]{:S(2)}, u32[]{:S(2)}) collective-permute-start(f32[128,1152]{1,0:T(8,128)S(1)} %fusion.10), channel_id=1, source_target_pairs={{0,1},{1,0},{2,3},{3,2},{4,5},{5,4},{6,7},{7,6},{8,9},{9,8},{10,11... | collective-permute-start | bytes 1769480 | tf_op jit(solution)/shard_map/ppermute | solution.py:68
  212.5 1.6 collective-permute-done.4
  214.1 0.9 convolution_add_fusion
  215.0 2.4 %collective-permute-start.5 = (f32[128,1152]{1,0:T(8,128)S(1)}, f32[128,1152]{1,0:T(8,128)S(1)}, u32[]{:S(2)}, u32[]{:S(2)}) collective-permute-start(f32[128,1152]{1,0:T(8,128)S(1)} %convolution_add_fusion), channel_id=1, source_target_pairs={{0,0},{1,16},{16,1},{17,17},{2,2},{3,18},{18,3},{19,19},{4,4},{5,2... | collective-permute-start | bytes 1769480 | tf_op jit(solution)/shard_map/ppermute | solution.py:70
  217.4 8.7 %collective-permute-done.5 = f32[128,1152]{1,0:T(8,128)S(1)} collective-permute-done((f32[128,1152]{1,0:T(8,128)S(1)}, f32[128,1152]{1,0:T(8,128)S(1)}, u32[]{:S(2)}, u32[]{:S(2)}) %collective-permute-start.5) | collective-permute-done | bytes 589856 | tf_op jit(solution)/shard_map/ppermute | solution.py:70
  226.2 0.0 copy-done
  226.2 0.9 multiply_add_fusion
  (2 shorter events, 0.0 us)
Async XLA Ops:
  6.5 87.3 %all-gather.3.cloned.1.call-start = ((), (), s32[]{:S(2)}) async-start(), calls=%async_computation.3 | async-start | bytes 5013504 | tf_op jit(solution)/shard_map/all_gather | solution.py:38
  7.6 9.0 %collective-permute-start = (bf16[128,1152]{1,0:T(8,128)(2,1)S(1)}, bf16[128,1152]{1,0:T(8,128)(2,1)S(1)}, u32[]{:S(2)}, u32[]{:S(2)}) collective-permute-start(bf16[128,1152]{1,0:T(8,128)(2,1)S(1)} %convert_element_type.19), channel_id=1, source_target_pairs={{0,0},{1,16},{16,1},{17,17},{2,2},{3,18},{18,3},{19,19},{4,4},{5,2... | collective-permute-start | bytes 884744 | tf_op jit(solution)/shard_map/ppermute | solution.py:37
  16.6 0.7 copy-start.1
  17.4 3.7 %collective-permute-start.1 = (bf16[128,1152]{1,0:T(8,128)(2,1)}, bf16[128,1152]{1,0:T(8,128)(2,1)S(1)}, u32[]{:S(2)}, u32[]{:S(2)}) collective-permute-start(bf16[128,1152]{1,0:T(8,128)(2,1)} %copy-done.1), channel_id=1, source_target_pairs={{0,1},{1,0},{2,3},{3,2},{4,5},{5,4},{6,7},{7,6},{8,9},{9,8},{10,11... | collective-permute-start | bytes 884744 | tf_op jit(solution)/shard_map/ppermute | solution.py:39
  154.0 15.9 %all-to-all-start.1 = ((bf16[16,128,256]{2,1,0:T(8,128)(2,1)}), bf16[16,128,256]{2,1,0:T(8,128)(2,1)S(1)}, u32[]{:S(2)}, u32[]{:S(2)}) async-start(bf16[16,128,256]{2,1,0:T(8,128)(2,1)} %broadcast_in_dim.4), calls=%async_computation.1 | async-start | bytes 2097152 | tf_op jit(solution)/shard_map/all_to_all | solution.py:16
  158.2 27.2 %collective-permute-start.2 = (bf16[8,128,256]{2,1,0:T(8,128)(2,1)S(1)}, bf16[8,128,256]{2,1,0:T(8,128)(2,1)S(1)}, u32[]{:S(2)}, u32[]{:S(2)}) collective-permute-start(bf16[8,128,256]{2,1,0:T(8,128)(2,1)S(1)} %copy.7), channel_id=1, source_target_pairs={{0,32},{32,0},{1,33},{33,1},{2,34},{34,2},{3,35},{35,3},{4,36},{36... | collective-permute-start | bytes 1572872 | tf_op jit(solution)/shard_map/ppermute | solution.py:46
  169.9 17.6 %collective-permute-start.3 = (bf16[16,128,256]{2,1,0:T(8,128)(2,1)S(1)}, bf16[16,128,256]{2,1,0:T(8,128)(2,1)S(1)}, u32[]{:S(2)}, u32[]{:S(2)}) collective-permute-start(bf16[16,128,256]{2,1,0:T(8,128)(2,1)S(1)} %all-to-all-done.1), channel_id=1, source_target_pairs={{0,1},{1,0},{2,3},{3,2},{4,5},{5,4},{6,7},{7,6},{8,9},{9,8},{10,11... | collective-permute-start | bytes 3145736 | tf_op jit(solution)/shard_map/ppermute | solution.py:49
  185.3 22.2 %slice-start = ((s8[4718592]{0:T(1024)(128)(4,1)}), s8[4194304]{0:T(1024)(128)(4,1)S(1)}, s32[]{:S(2)}) async-start(s8[4718592]{0:T(1024)(128)(4,1)} %bitcast.34), calls=%async_computation.4 | async-start | bytes 8388608
  185.9 21.7 %slice-start.1 = ((s8[4718592]{0:T(1024)(128)(4,1)}), s8[524288]{0:T(1024)(128)(4,1)S(1)}, s32[]{:S(2)}) async-start(s8[4718592]{0:T(1024)(128)(4,1)} %bitcast.34), calls=%async_computation.5 | async-start | bytes 1048576
  207.6 18.6 %copy-start = (f32[128,1152]{1,0:T(8,128)S(1)}, f32[128,1152]{1,0:T(8,128)}, u32[]{:S(2)}) copy-start(f32[128,1152]{1,0:T(8,128)} %param.1) | copy-start | bytes 1769476
  208.5 5.6 %collective-permute-start.4 = (f32[128,1152]{1,0:T(8,128)S(1)}, f32[128,1152]{1,0:T(8,128)S(1)}, u32[]{:S(2)}, u32[]{:S(2)}) collective-permute-start(f32[128,1152]{1,0:T(8,128)S(1)} %fusion.10), channel_id=1, source_target_pairs={{0,1},{1,0},{2,3},{3,2},{4,5},{5,4},{6,7},{7,6},{8,9},{9,8},{10,11... | collective-permute-start | bytes 1769480 | tf_op jit(solution)/shard_map/ppermute | solution.py:68
  215.0 11.2 %collective-permute-start.5 = (f32[128,1152]{1,0:T(8,128)S(1)}, f32[128,1152]{1,0:T(8,128)S(1)}, u32[]{:S(2)}, u32[]{:S(2)}) collective-permute-start(f32[128,1152]{1,0:T(8,128)S(1)} %convolution_add_fusion), channel_id=1, source_target_pairs={{0,0},{1,16},{16,1},{17,17},{2,2},{3,18},{18,3},{19,19},{4,4},{5,2... | collective-permute-start | bytes 1769480 | tf_op jit(solution)/shard_map/ppermute | solution.py:70
Sparse Core Ops, SparseCore 0:
  17.5 76.2 all-gather.2

commit v3 on v2

--- a/solution.py
+++ b/solution.py
@@ -9,6 +9,7 @@
 PLANE = ("ylo", "x", "yhi")
 SWAP = ((0, 1), (1, 0))
 TURN = ((0, 0), (1, 2), (2, 1), (3, 3))
+CROSS = ((0, 2), (1, 0), (2, 3), (3, 1))
 
 
 def share(piece, size):
@@ -64,11 +65,11 @@
         )
     poly = (-4.775 * gram + 2.0315 * square).astype(jnp.bfloat16)
     panel = share(poly, chips).reshape(chips * rows, 2 * rows)
-    away = tn(panel[:, rows:], half)
-    away = lax.ppermute(away, "core", SWAP)
-    product = tn(panel[:, :rows], half) + away
-    product = lax.ppermute(product, ("ylo", "core"), TURN)
-    return 3.4445 * lax.reduce_precision(iterate, 8, 7) + product
+    away = tn(panel[:, rows:], half).astype(jnp.bfloat16)
+    away = lax.ppermute(away, ("ylo", "core"), CROSS)
+    stay = tn(panel[:, :rows], half) + 3.4445 * own.astype(jnp.float32)
+    stay = lax.ppermute(stay.astype(jnp.bfloat16), ("ylo", "core"), TURN)
+    return stay.astype(jnp.float32) + away.astype(jnp.float32)
 
 
 def solution(mesh):

time: 234 us -> 229 us (0.979)
  waiting for transfers between devices: 99.9 us -> 95 us
    ppermute x2, waiting for transfers between devices: 10.4 us -> 5.54 us  [the longest x1 3.97 us: per_device(): away = lax.ppermute(away, ('ylo', 'core'), CROSS)]
  transfers between devices with their start and end apart: 8 -> 8, of which waited for: 7 -> 7; matrix products, arithmetic and copies ran while one was open for 0% -> 1% of each run, Pallas kernels for 0% -> 0%
where the time goes in v3:
time: 229 us
  waiting for transfers between devices  95 us (41%)
  blocking collectives  73.9 us (32%)
  starting transfers between devices  34.6 us (15%)
  between operations  13.6 us (6%)
  matrix products  6.39 us (3%)
  local copies, waits for them, and re-layouts  3.02 us (1%)
    all_gather x1, waiting for transfers between devices, per_device(): half = lax.all_gather(own, LINE, axis=0, tiled=True)  72.8 us
    all_gather x1, blocking collectives, per_device(): same = lax.all_gather(gram_low, 'zg', axis=0)  28 us
    all_to_all x1, blocking collectives, per_device(): summands = lax.all_to_all(partial_gram, PLANE, 0, 0)  26.5 us
    all_to_all x1, blocking collectives, share(): return lax.all_to_all(copies, PLANE, 0, 0)  19.4 us
    ppermute x1, starting transfers between devices, per_device(): right_other = lax.ppermute(right_own, 'core', SWAP)  15.3 us
    all_to_all x1, waiting for transfers between devices, share(): return lax.all_to_all(copies, PLANE, 0, 0)  8.96 us
    ppermute x1, starting transfers between devices, per_device(): own = lax.ppermute(rounded, ('ylo', 'core'), TURN)  4.59 us
  transfers between devices with their start and end apart: 8, of which 7 were waited for; matrix products, arithmetic and copies ran while one was open for 1% of the time, Pallas kernels for 0%

profile of v3, /device:TPU:1, one launch (start us, length us, event | category | flops | bytes accessed | tf_op | source)
XLA Modules:
  0.0 228.8 jit_solution(12805196937495465919)
XLA Ops:
  6.5 0.0 all-gather.3.cloned.1.call-start
  6.5 1.1 convert_element_type.34
  7.6 4.6 %collective-permute-start = (bf16[128,1152]{1,0:T(8,128)(2,1)S(1)}, bf16[128,1152]{1,0:T(8,128)(2,1)S(1)}, u32[]{:S(2)}, u32[]{:S(2)}) collective-permute-start(bf16[128,1152]{1,0:T(8,128)(2,1)S(1)} %convert_element_type.34), channel_id=1, source_target_pairs={{0,0},{1,16},{16,1},{17,17},{2,2},{3,18},{18,3},{19,19},{4,4},{5,2... | collective-permute-start | bytes 884744 | tf_op jit(solution)/shard_map/ppermute | solution.py:38
  12.2 4.4 %collective-permute-done = bf16[128,1152]{1,0:T(8,128)(2,1)S(1)} collective-permute-done((bf16[128,1152]{1,0:T(8,128)(2,1)S(1)}, bf16[128,1152]{1,0:T(8,128)(2,1)S(1)}, u32[]{:S(2)}, u32[]{:S(2)}) %collective-permute-start) | collective-permute-done | bytes 294944 | tf_op jit(solution)/shard_map/ppermute | solution.py:38
  16.6 0.0 copy-start
  16.6 0.7 copy-done
  17.3 0.0 all-gather.3.cloned.1.call-update
  17.4 1.9 collective-permute-start.1
  19.3 1.8 collective-permute-done.1
  21.1 72.8 %all-gather.3.cloned.1.call-done = bf16[2048,1152]{1,0:T(8,128)(2,1)} async-done(((bf16[128,1152]{1,0:T(8,128)(2,1)}), bf16[2048,1152]{1,0:T(8,128)(2,1)}) %all-gather.3.cloned.1.call-update) | async-done | bytes 4718608 | tf_op jit(solution)/shard_map/all_gather | solution.py:39
  93.8 4.0 %convolution_bitcast_fusion = f32[32,16,8,128]{3,2,1,0:T(8,128)S(1)} fusion(bf16[2048,1152]{1,0:T(8,128)(2,1)} %all-gather.3.cloned.1.call-done, bf16[128,1152]{1,0:T(8,128)(2,1)S(1)} %collective-permute-done.1, bf16[128,1152]{1,0:T(8,128)(2,1)} %copy-done), kind=kOutput, calls=%fused_computation.4 | convolution fusion | flops 1209139200 | bytes 7405568 | tf_op jit(solution)/shard_map/dot_general | solution.py:21
  97.8 0.2 copy.15
  98.0 26.5 %all_to_all.15 = f32[16,128,256]{1,2,0:T(8,128)S(1)} all-to-all(f32[16,128,256]{1,2,0:T(8,128)S(1)} %bitcast.36), channel_id=1, replica_groups=mesh['zg'=8,'zp'=2,'ylo'=2,'x'=4,'yhi'=2,'core'=2] {'ylo','x','yhi'}, dimensions={0} | all-to-all | bytes 4194304 | tf_op jit(solution)/shard_map/all_to_all | solution.py:43
  124.6 0.1 reduce_sum.9
  124.7 28.0 %all-gather = bf16[1024,256]{0,1:T(8,128)(2,1)S(1)} all-gather(bf16[128,256]{0,1:T(8,128)(2,1)S(1)} %multiply_convert_fusion), channel_id=2, replica_groups=mesh['zg'=8,'zp'=2,'ylo'=2,'x'=4,'yhi'=2,'core'=2] {'zg'}, dimensions={0}, use_global_device_ids=true | all-gather | bytes 589824 | tf_op jit(solution)/shard_map/all_gather | solution.py:46
  152.7 0.1 copy.13
  152.8 0.1 copy.10
  152.9 1.1 broadcast_in_dim.4
  154.0 3.9 %all-to-all-start.1 = ((bf16[16,128,256]{2,1,0:T(8,128)(2,1)}), bf16[16,128,256]{2,1,0:T(8,128)(2,1)S(1)}, u32[]{:S(2)}, u32[]{:S(2)}) async-start(bf16[16,128,256]{2,1,0:T(8,128)(2,1)} %broadcast_in_dim.4), calls=%async_computation.1 | async-start | bytes 2097152 | tf_op jit(solution)/shard_map/all_to_all | solution.py:17
  157.8 0.3 copy.7
  158.2 2.8 %collective-permute-start.2 = (bf16[8,128,256]{2,1,0:T(8,128)(2,1)S(1)}, bf16[8,128,256]{2,1,0:T(8,128)(2,1)S(1)}, u32[]{:S(2)}, u32[]{:S(2)}) collective-permute-start(bf16[8,128,256]{2,1,0:T(8,128)(2,1)S(1)} %copy.7), channel_id=1, source_target_pairs={{0,32},{32,0},{1,33},{33,1},{2,34},{34,2},{3,35},{35,3},{4,36},{36... | collective-permute-start | bytes 1572872 | tf_op jit(solution)/shard_map/ppermute | solution.py:47
  160.9 9.0 %all-to-all-done.1 = bf16[16,128,256]{2,1,0:T(8,128)(2,1)S(1)} async-done(((bf16[16,128,256]{2,1,0:T(8,128)(2,1)}), bf16[16,128,256]{2,1,0:T(8,128)(2,1)S(1)}, u32[]{:S(2)}, u32[]{:S(2)}) %all-to-all-start.1) | async-done | bytes 1048608 | tf_op jit(solution)/shard_map/all_to_all | solution.py:17
  169.9 15.3 %collective-permute-start.3 = (bf16[16,128,256]{2,1,0:T(8,128)(2,1)S(1)}, bf16[16,128,256]{2,1,0:T(8,128)(2,1)S(1)}, u32[]{:S(2)}, u32[]{:S(2)}) collective-permute-start(bf16[16,128,256]{2,1,0:T(8,128)(2,1)S(1)} %all-to-all-done.1), channel_id=1, source_target_pairs={{0,1},{1,0},{2,3},{3,2},{4,5},{5,4},{6,7},{7,6},{8,9},{9,8},{10,11... | collective-permute-start | bytes 3145736 | tf_op jit(solution)/shard_map/ppermute | solution.py:50
  185.2 0.1 copy.5
  185.3 0.0 collective-permute-done.2
  185.3 0.0 slice-start
  185.4 0.1 select_bitcast_fusion.1
  185.4 0.1 pad_maximum_fusion
  185.6 0.0 copy-start.1
  185.6 0.3 convolution_bitcast_fusion.2
  185.9 0.0 slice-start.1
  185.9 1.6 collective-permute-done.3
  187.5 0.3 fusion.17
  187.8 0.3 fusion.4
  188.1 0.1 broadcast_in_dim.5
  188.2 19.4 %all_to_all.16 = bf16[16,128,256]{2,1,0:T(8,128)(2,1)S(1)} all-to-all(bf16[16,128,256]{2,1,0:T(8,128)(2,1)S(1)} %broadcast_in_dim.5), channel_id=1, replica_groups=mesh['zg'=8,'zp'=2,'ylo'=2,'x'=4,'yhi'=2,'core'=2] {'ylo','x','yhi'}, dimensions={0} | all-to-all | bytes 2097152 | tf_op jit(solution)/shard_map/all_to_all | solution.py:17
  207.6 0.0 slice-done
  207.6 0.0 copy-done.1
  207.6 0.0 slice-done.1
  207.6 0.9 fusion
  208.5 4.2 %collective-permute-start.4 = (bf16[128,1152]{1,0:T(8,128)(2,1)S(1)}, bf16[128,1152]{1,0:T(8,128)(2,1)S(1)}, u32[]{:S(2)}, u32[]{:S(2)}) collective-permute-start(bf16[128,1152]{1,0:T(8,128)(2,1)S(1)} %fusion), channel_id=1, source_target_pairs={{0,0},{1,16},{16,1},{17,17},{2,2},{3,18},{18,3},{19,19},{4,4},{5,2... | collective-permute-start | bytes 884744 | tf_op jit(solution)/shard_map/ppermute | solution.py:71
  212.7 0.9 convolution_convert_fusion
  213.6 1.9 collective-permute-start.5
  215.5 1.6 collective-permute-done.4
  217.1 4.0 %collective-permute-done.5 = bf16[128,1152]{1,0:T(8,128)(2,1)S(1)} collective-permute-done((bf16[128,1152]{1,0:T(8,128)(2,1)S(1)}, bf16[128,1152]{1,0:T(8,128)(2,1)S(1)}, u32[]{:S(2)}, u32[]{:S(2)}) %collective-permute-start.5) | collective-permute-done | bytes 294944 | tf_op jit(solution)/shard_map/ppermute | solution.py:69
  221.0 0.9 convert_add_fusion
  (2 shorter events, 0.0 us)
Async XLA Ops:
  6.5 87.3 %all-gather.3.cloned.1.call-start = ((), (), s32[]{:S(2)}) async-start(), calls=%async_computation.3 | async-start | bytes 5013504 | tf_op jit(solution)/shard_map/all_gather | solution.py:39
  7.6 9.0 %collective-permute-start = (bf16[128,1152]{1,0:T(8,128)(2,1)S(1)}, bf16[128,1152]{1,0:T(8,128)(2,1)S(1)}, u32[]{:S(2)}, u32[]{:S(2)}) collective-permute-start(bf16[128,1152]{1,0:T(8,128)(2,1)S(1)} %convert_element_type.34), channel_id=1, source_target_pairs={{0,0},{1,16},{16,1},{17,17},{2,2},{3,18},{18,3},{19,19},{4,4},{5,2... | collective-permute-start | bytes 884744 | tf_op jit(solution)/shard_map/ppermute | solution.py:38
  16.6 0.7 copy-start
  17.4 3.7 %collective-permute-start.1 = (bf16[128,1152]{1,0:T(8,128)(2,1)}, bf16[128,1152]{1,0:T(8,128)(2,1)S(1)}, u32[]{:S(2)}, u32[]{:S(2)}) collective-permute-start(bf16[128,1152]{1,0:T(8,128)(2,1)} %copy-done), channel_id=1, source_target_pairs={{0,1},{1,0},{2,3},{3,2},{4,5},{5,4},{6,7},{7,6},{8,9},{9,8},{10,11... | collective-permute-start | bytes 884744 | tf_op jit(solution)/shard_map/ppermute | solution.py:40
  154.0 15.9 %all-to-all-start.1 = ((bf16[16,128,256]{2,1,0:T(8,128)(2,1)}), bf16[16,128,256]{2,1,0:T(8,128)(2,1)S(1)}, u32[]{:S(2)}, u32[]{:S(2)}) async-start(bf16[16,128,256]{2,1,0:T(8,128)(2,1)} %broadcast_in_dim.4), calls=%async_computation.1 | async-start | bytes 2097152 | tf_op jit(solution)/shard_map/all_to_all | solution.py:17
  158.2 27.2 %collective-permute-start.2 = (bf16[8,128,256]{2,1,0:T(8,128)(2,1)S(1)}, bf16[8,128,256]{2,1,0:T(8,128)(2,1)S(1)}, u32[]{:S(2)}, u32[]{:S(2)}) collective-permute-start(bf16[8,128,256]{2,1,0:T(8,128)(2,1)S(1)} %copy.7), channel_id=1, source_target_pairs={{0,32},{32,0},{1,33},{33,1},{2,34},{34,2},{3,35},{35,3},{4,36},{36... | collective-permute-start | bytes 1572872 | tf_op jit(solution)/shard_map/ppermute | solution.py:47
  169.9 17.6 %collective-permute-start.3 = (bf16[16,128,256]{2,1,0:T(8,128)(2,1)S(1)}, bf16[16,128,256]{2,1,0:T(8,128)(2,1)S(1)}, u32[]{:S(2)}, u32[]{:S(2)}) collective-permute-start(bf16[16,128,256]{2,1,0:T(8,128)(2,1)S(1)} %all-to-all-done.1), channel_id=1, source_target_pairs={{0,1},{1,0},{2,3},{3,2},{4,5},{5,4},{6,7},{7,6},{8,9},{9,8},{10,11... | collective-permute-start | bytes 3145736 | tf_op jit(solution)/shard_map/ppermute | solution.py:50
  185.3 22.2 %slice-start = ((s8[4718592]{0:T(1024)(128)(4,1)}), s8[4194304]{0:T(1024)(128)(4,1)S(1)}, s32[]{:S(2)}) async-start(s8[4718592]{0:T(1024)(128)(4,1)} %bitcast.34), calls=%async_computation.4 | async-start | bytes 8388608
  185.6 22.0 %copy-start.1 = (bf16[128,1152]{1,0:T(8,128)(2,1)S(1)}, bf16[128,1152]{1,0:T(8,128)(2,1)}, u32[]{:S(2)}) copy-start(bf16[128,1152]{1,0:T(8,128)(2,1)} %copy-done) | copy-start | bytes 884740
  185.9 21.7 %slice-start.1 = ((s8[4718592]{0:T(1024)(128)(4,1)}), s8[524288]{0:T(1024)(128)(4,1)S(1)}, s32[]{:S(2)}) async-start(s8[4718592]{0:T(1024)(128)(4,1)} %bitcast.34), calls=%async_computation.5 | async-start | bytes 1048576
  208.5 8.6 %collective-permute-start.4 = (bf16[128,1152]{1,0:T(8,128)(2,1)S(1)}, bf16[128,1152]{1,0:T(8,128)(2,1)S(1)}, u32[]{:S(2)}, u32[]{:S(2)}) collective-permute-start(bf16[128,1152]{1,0:T(8,128)(2,1)S(1)} %fusion), channel_id=1, source_target_pairs={{0,0},{1,16},{16,1},{17,17},{2,2},{3,18},{18,3},{19,19},{4,4},{5,2... | collective-permute-start | bytes 884744 | tf_op jit(solution)/shard_map/ppermute | solution.py:71
  213.6 7.5 %collective-permute-start.5 = (bf16[128,1152]{1,0:T(8,128)(2,1)S(1)}, bf16[128,1152]{1,0:T(8,128)(2,1)S(1)}, u32[]{:S(2)}, u32[]{:S(2)}) collective-permute-start(bf16[128,1152]{1,0:T(8,128)(2,1)S(1)} %convolution_convert_fusion), channel_id=1, source_target_pairs={{0,16},{1,0},{16,17},{17,1},{2,18},{3,2},{18,19},{19,3},{4,20},{5,... | collective-permute-start | bytes 884744 | tf_op jit(solution)/shard_map/ppermute | solution.py:69
Sparse Core Ops, SparseCore 0:
  17.5 76.2 all-gather.2

commit v4 on v3

v4 whole, which is shorter than its diff:
```python
import jax
import jax.numpy as jnp
from jax import lax
from jax.sharding import Mesh, PartitionSpec as P

AXES = ("zh", "zl", "ylo", "x", "yhi", "core")
SIZES = (4, 4, 2, 4, 2, 2)
LINE = ("zh", "zl")
PLANE = ("ylo", "x", "yhi")
SWAP = ((0, 1), (1, 0))
TURN = ((0, 0), (1, 2), (2, 1), (3, 3))
CROSS = ((0, 2), (1, 0), (2, 3), (3, 1))


def share(piece, size):
    copies = jnp.broadcast_to(piece[None], (size,) + piece.shape)
    return lax.all_to_all(copies, PLANE, 0, 0)


def along(piece, shift):
    size = lax.axis_size(LINE)
    pairs = [(place, (place + shift) % size) for place in range(size)]
    return lax.ppermute(piece, LINE, pairs)


def mix(left, right):
    return lax.dot_general(
        left, right, (((0, 2), (0, 1)), ((), ())), preferred_element_type=jnp.float32
    )


def per_device(iterate):
    rounded = iterate.astype(jnp.bfloat16)
    rows, cols = rounded.shape
    groups, steps = lax.axis_size("zh"), lax.axis_size("zl")
    chips = lax.axis_size(PLANE)
    total_cols = cols * chips
    own = lax.ppermute(rounded, ("ylo", "core"), TURN)
    half = lax.all_gather(own, LINE, axis=0)
    other = lax.ppermute(own, "core", SWAP)
    partial_gram = lax.dot_general(
        jnp.concatenate([own, other], 0),
        half,
        (((1,), (2,)), ((), ())),
        preferred_element_type=jnp.float32,
    )
    partial_gram = partial_gram.transpose(1, 0, 2)
    summands = lax.all_to_all(partial_gram, PLANE, 0, 0)
    gram = summands.sum(0) / total_cols
    gram_low = gram.astype(jnp.bfloat16)
    panel = share(gram_low, chips).reshape(groups, steps, 2 * rows, rows)
    here = lax.all_gather(gram_low, "zh", axis=0)
    panel, _ = lax.optimization_barrier((panel, here))
    cut = groups // 2
    right = (
        here,
        along(here, -1),
        along(here, 1),
        jnp.concatenate([along(here[:cut], -2), along(here[cut:], 2)], 0),
    )
    residue = lax.axis_index("zl")
    left_own = [
        lax.dynamic_index_in_dim(panel, (residue + shift) % steps, 1, False)
        for shift in (0, 1, steps - 1, 2)
    ]
    left_other = lax.ppermute(jnp.stack(left_own), "core", SWAP)
    left_other = jnp.concatenate(
        [left_other[:, :, rows:], left_other[:, :, :rows]], 2
    )
    square = 0.0
    for place in range(steps):
        square = square + mix(left_own[place], right[place][:, :rows])
    for place in range(steps):
        square = square + mix(left_other[place], right[place][:, rows:])
    poly = (-4.775 * gram + 2.0315 * square).astype(jnp.bfloat16)
    panel = share(poly, chips)
    away = mix(panel[:, rows:], half).astype(jnp.bfloat16)
    away = lax.ppermute(away, ("ylo", "core"), CROSS)
    stay = mix(panel[:, :rows], half) + 3.4445 * own.astype(jnp.float32)
    stay = lax.ppermute(stay.astype(jnp.bfloat16), ("ylo", "core"), TURN)
    return stay.astype(jnp.float32) + away.astype(jnp.float32)


def solution(mesh):
    fine = Mesh(mesh.devices.reshape(SIZES), AXES)
    spec = P(("zh", "zl", "ylo"), ("x", "yhi", "core"))
    return jax.shard_map(
        per_device, mesh=fine, in_specs=(spec,), out_specs=spec, check_vma=False
    )
```

time: 229 us -> 226 us (0.987)
  blocking collectives: 73.9 us -> 63.5 us
  starting transfers between devices: 34.6 us -> 44.2 us
  waiting for transfers between devices: 95 us -> 92.2 us
    all_gather x1, blocking collectives: 28 us -> 15.1 us  [per_device(): here = lax.all_gather(gram_low, 'zh', axis=0)]
    ppermute x2 -> x5, starting transfers between devices: 18.1 us -> 27.6 us  [the longest x1 14.6 us: per_device(): left_other = lax.ppermute(jnp.stack(left_own), 'core', SWAP)]
    all_to_all x1, waiting for transfers between devices: 8.96 us -> 0.01 us  [share(): return lax.all_to_all(copies, PLANE, 0, 0)]
    ppermute x2 -> x5, waiting for transfers between devices: 1.6 us -> 7.33 us  [the longest x4 7.32 us: along(): return lax.ppermute(piece, LINE, pairs)]
    ppermute x1, waiting for transfers between devices: 1.57 us -> 5.81 us  [per_device(): stay = lax.ppermute(stay.astype(jnp.bfloat16), ('ylo', 'core'), TURN)]
    ppermute x1, waiting for transfers between devices: 3.97 us -> 0.12 us  [per_device(): away = lax.ppermute(away, ('ylo', 'core'), CROSS)]
    all_to_all x1, blocking collectives: 19.4 us -> 21.8 us  [share(): return lax.all_to_all(copies, PLANE, 0, 0)]
    ppermute x1, starting transfers between devices: 1.92 us -> 4.34 us  [per_device(): away = lax.ppermute(away, ('ylo', 'core'), CROSS)]
  transfers between devices with their start and end apart: 8 -> 11, of which waited for: 7 -> 7; matrix products, arithmetic and copies ran while one was open for 1% -> 1% of each run, Pallas kernels for 0% -> 0%
where the time goes in v4:
time: 226 us; the launch traced here: 225 us
  waiting for transfers between devices  92.2 us (41%)
  blocking collectives  63.5 us (28%)
  starting transfers between devices  44.2 us (20%)
  between operations  13.7 us (6%)
  matrix products  6.92 us (3%)
  local copies, waits for them, and re-layouts  2.35 us (1%)
    all_gather x1, waiting for transfers between devices, per_device(): half = lax.all_gather(own, LINE, axis=0)  72.8 us
    all_to_all x1, blocking collectives, per_device(): summands = lax.all_to_all(partial_gram, PLANE, 0, 0)  26.5 us
    all_to_all x1, blocking collectives, share(): return lax.all_to_all(copies, PLANE, 0, 0)  21.8 us
    all_gather x1, blocking collectives, per_device(): here = lax.all_gather(gram_low, 'zh', axis=0)  15.1 us
    ppermute x1, starting transfers between devices, per_device(): left_other = lax.ppermute(jnp.stack(left_own), 'core', SWAP)  14.6 us
    ppermute x4, starting transfers between devices, along(): return lax.ppermute(piece, LINE, pairs)  13 us
    ppermute x4, waiting for transfers between devices, along(): return lax.ppermute(piece, LINE, pairs)  7.32 us
    ppermute x1, waiting for transfers between devices, per_device(): stay = lax.ppermute(stay.astype(jnp.bfloat16), ('ylo', 'core'), TURN)  5.81 us
  transfers between devices with their start and end apart: 11, of which 7 were waited for; matrix products, arithmetic and copies ran while one was open for 1% of the time, Pallas kernels for 0%

profile of v4, /device:TPU:1, one launch (start us, length us, event | category | flops | bytes accessed | tf_op | source)
XLA Modules:
  0.0 225.1 jit_solution(6647289014704117455)
XLA Ops:
  6.5 0.0 all-gather.4.cloned.1.call-start
  6.5 1.1 convert_element_type.35
  7.6 4.6 %collective-permute-start = (bf16[128,1152]{1,0:T(8,128)(2,1)S(1)}, bf16[128,1152]{1,0:T(8,128)(2,1)S(1)}, u32[]{:S(2)}, u32[]{:S(2)}) collective-permute-start(bf16[128,1152]{1,0:T(8,128)(2,1)S(1)} %convert_element_type.35), channel_id=1, source_target_pairs={{0,0},{1,16},{16,1},{17,17},{2,2},{3,18},{18,3},{19,19},{4,4},{5,2... | collective-permute-start | bytes 884744 | tf_op jit(solution)/shard_map/ppermute | solution.py:38
  12.2 4.4 %collective-permute-done = bf16[128,1152]{1,0:T(8,128)(2,1)S(1)} collective-permute-done((bf16[128,1152]{1,0:T(8,128)(2,1)S(1)}, bf16[128,1152]{1,0:T(8,128)(2,1)S(1)}, u32[]{:S(2)}, u32[]{:S(2)}) %collective-permute-start) | collective-permute-done | bytes 294944 | tf_op jit(solution)/shard_map/ppermute | solution.py:38
  16.6 0.0 copy-start
  16.6 0.7 copy-done
  17.3 0.0 all-gather.4.cloned.1.call-update
  17.4 1.9 collective-permute-start.1
  19.3 1.8 collective-permute-done.1
  21.1 72.8 %all-gather.4.cloned.1.call-done = bf16[2048,1152]{1,0:T(8,128)(2,1)} async-done(((bf16[128,1152]{1,0:T(8,128)(2,1)}), bf16[2048,1152]{1,0:T(8,128)(2,1)}) %all-gather.4.cloned.1.call-update) | async-done | bytes 4718608 | tf_op jit(solution)/shard_map/all_gather | solution.py:39
  93.8 3.5 %convolution_bitcast_fusion.2 = f32[16,256,128]{2,1,0:T(8,128)S(1)} fusion(bf16[16,128,1152]{2,1,0:T(8,128)(2,1)} %bitcast.91, bf16[128,1152]{1,0:T(8,128)(2,1)S(1)} %collective-permute-done.1, bf16[128,1152]{1,0:T(8,128)(2,1)} %copy-done), kind=kOutput, calls=%fused_computation.5 | convolution fusion | flops 1209139200 | bytes 7405568 | tf_op jit(solution)/shard_map/dot_general | solution.py:41
  97.3 26.5 %all_to_all.15 = f32[16,256,128]{2,1,0:T(8,128)S(1)} all-to-all(f32[16,256,128]{2,1,0:T(8,128)S(1)} %convolution_bitcast_fusion.2), channel_id=1, replica_groups=mesh['zh'=4,'zl'=4,'ylo'=2,'x'=4,'yhi'=2,'core'=2] {'ylo','x','yhi'}, dimensions={0} | all-to-all | bytes 4194304 | tf_op jit(solution)/shard_map/all_to_all | solution.py:48
  123.8 0.1 reduce_sum.9
  123.9 1.2 broadcast_in_dim.4
  125.2 3.7 %all-to-all-start.1 = ((bf16[16,256,128]{2,1,0:T(8,128)(2,1)}), bf16[16,256,128]{2,1,0:T(8,128)(2,1)S(1)}, u32[]{:S(2)}, u32[]{:S(2)}) async-start(bf16[16,256,128]{2,1,0:T(8,128)(2,1)} %broadcast_in_dim.4), calls=%async_computation.1 | async-start | bytes 2097152 | tf_op jit(solution)/shard_map/all_to_all | solution.py:17
  128.9 15.1 %all-gather.1 = bf16[1024,128]{1,0:T(8,128)(2,1)S(1)} all-gather(bf16[256,128]{1,0:T(8,128)(2,1)S(1)} %multiply_convert_fusion), channel_id=3, replica_groups=mesh['zh'=4,'zl'=4,'ylo'=2,'x'=4,'yhi'=2,'core'=2] {'zh'}, dimensions={0}, use_global_device_ids=true | all-gather | bytes 327680 | tf_op jit(solution)/shard_map/all_gather | solution.py:52
  144.0 0.0 all-to-all-done.1
  144.0 0.1 dynamic-slice_bitcast_fusion.3
  144.1 0.1 pad_maximum_fusion
  144.2 14.6 %collective-permute-start.6 = (bf16[4,4,256,128]{3,2,1,0:T(8,128)(2,1)S(1)}, bf16[4,4,256,128]{3,2,1,0:T(8,128)(2,1)S(1)}, u32[]{:S(2)}, u32[]{:S(2)}) collective-permute-start(bf16[4,4,256,128]{3,2,1,0:T(8,128)(2,1)S(1)} %pad_maximum_fusion), channel_id=1, source_target_pairs={{0,1},{1,0},{2,3},{3,2},{4,5},{5,4},{6,7},{7,6},{8,9},{9,8},{10,11... | collective-permute-start | bytes 3145736 | tf_op jit(solution)/shard_map/ppermute | solution.py:66
  158.8 0.0 slice-start
  158.8 4.6 %collective-permute-start.4 = (bf16[2,256,128]{2,1,0:T(8,128)(2,1)S(1)}, bf16[2,256,128]{2,1,0:T(8,128)(2,1)S(1)}, u32[]{:S(2)}, u32[]{:S(2)}) collective-permute-start(bf16[2,256,128]{2,1,0:T(8,128)(2,1)S(1)} %bitcast.106), channel_id=1, source_target_pairs={{0,448},{32,480},{64,0},{96,32},{128,64},{160,96},{192,128},{224,1... | collective-permute-start | bytes 393224 | tf_op jit(solution)/shard_map/ppermute | solution.py:23
  163.4 1.9 collective-permute-start.5
  165.4 2.7 %collective-permute-start.3 = (bf16[4,256,128]{2,1,0:T(8,128)(2,1)S(1)}, bf16[4,256,128]{2,1,0:T(8,128)(2,1)S(1)}, u32[]{:S(2)}, u32[]{:S(2)}) collective-permute-start(bf16[4,256,128]{2,1,0:T(8,128)(2,1)S(1)} %bitcast.101), channel_id=1, source_target_pairs={{0,32},{32,64},{64,96},{96,128},{128,160},{160,192},{192,224},{224... | collective-permute-start | bytes 786440 | tf_op jit(solution)/shard_map/ppermute | solution.py:23
  168.1 3.8 %collective-permute-start.2 = (bf16[4,256,128]{2,1,0:T(8,128)(2,1)S(1)}, bf16[4,256,128]{2,1,0:T(8,128)(2,1)S(1)}, u32[]{:S(2)}, u32[]{:S(2)}) collective-permute-start(bf16[4,256,128]{2,1,0:T(8,128)(2,1)S(1)} %bitcast.102), channel_id=1, source_target_pairs={{0,480},{32,0},{64,32},{96,64},{128,96},{160,128},{192,160},{224,1... | collective-permute-start | bytes 786440 | tf_op jit(solution)/shard_map/ppermute | solution.py:23
  171.9 0.0 collective-permute-done.4
  171.9 2.5 %collective-permute-done.5 = bf16[2,256,128]{2,1,0:T(8,128)(2,1)S(1)} collective-permute-done((bf16[2,256,128]{2,1,0:T(8,128)(2,1)S(1)}, bf16[2,256,128]{2,1,0:T(8,128)(2,1)S(1)}, u32[]{:S(2)}, u32[]{:S(2)}) %collective-permute-start.5) | collective-permute-done | bytes 131104 | tf_op jit(solution)/shard_map/ppermute | solution.py:23
  174.4 0.2 convolution_bitcast_fusion.10
  174.6 0.2 convolution_bitcast_fusion.7
  174.8 4.9 %collective-permute-done.3 = bf16[4,256,128]{2,1,0:T(8,128)(2,1)S(1)} collective-permute-done((bf16[4,256,128]{2,1,0:T(8,128)(2,1)S(1)}, bf16[4,256,128]{2,1,0:T(8,128)(2,1)S(1)}, u32[]{:S(2)}, u32[]{:S(2)}) %collective-permute-start.3) | collective-permute-done | bytes 262176 | tf_op jit(solution)/shard_map/ppermute | solution.py:23
  179.7 0.2 convolution_bitcast_fusion.8
  179.9 0.0 collective-permute-done.6
  179.9 0.1 fusion.54
  180.0 0.2 convolution_bitcast_fusion.6
  180.2 0.0 slice-start.1
  180.2 0.2 convolution_bitcast_fusion.3
  180.5 0.2 convolution_bitcast_fusion.4
  180.7 0.0 collective-permute-done.2
  180.7 0.2 convolution_bitcast_fusion.5
  180.9 0.2 fusion.12
  181.1 0.0 copy-start.1
  181.2 0.2 broadcast_in_dim.5
  181.4 21.8 %all_to_all.16 = bf16[16,256,128]{2,1,0:T(8,128)(2,1)S(1)} all-to-all(bf16[16,256,128]{2,1,0:T(8,128)(2,1)S(1)} %broadcast_in_dim.5), channel_id=1, replica_groups=mesh['zh'=4,'zl'=4,'ylo'=2,'x'=4,'yhi'=2,'core'=2] {'ylo','x','yhi'}, dimensions={0} | all-to-all | bytes 2097152 | tf_op jit(solution)/shard_map/all_to_all | solution.py:17
  203.2 0.0 slice-done
  203.2 0.0 slice-done.1
  203.2 0.9 fusion.1
  204.1 4.3 %collective-permute-start.8 = (bf16[128,1152]{1,0:T(8,128)(2,1)S(1)}, bf16[128,1152]{1,0:T(8,128)(2,1)S(1)}, u32[]{:S(2)}, u32[]{:S(2)}) collective-permute-start(bf16[128,1152]{1,0:T(8,128)(2,1)S(1)} %fusion.1), channel_id=1, source_target_pairs={{0,16},{1,0},{16,17},{17,1},{2,18},{3,2},{18,19},{19,3},{4,20},{5,... | collective-permute-start | bytes 884744 | tf_op jit(solution)/shard_map/ppermute | solution.py:78
  208.4 0.0 copy-done.1
  208.4 0.9 fusion.2
  209.3 2.1 collective-permute-start.7
  211.4 0.1 collective-permute-done.8
  211.6 5.8 %collective-permute-done.7 = bf16[128,1152]{1,0:T(8,128)(2,1)S(1)} collective-permute-done((bf16[128,1152]{1,0:T(8,128)(2,1)S(1)}, bf16[128,1152]{1,0:T(8,128)(2,1)S(1)}, u32[]{:S(2)}, u32[]{:S(2)}) %collective-permute-start.7) | collective-permute-done | bytes 294944 | tf_op jit(solution)/shard_map/ppermute | solution.py:80
  217.4 0.9 convert_add_fusion
  (5 shorter events, 0.1 us)
Async XLA Ops:
  6.5 87.3 %all-gather.4.cloned.1.call-start = ((), (), s32[]{:S(2)}) async-start(), calls=%async_computation.3 | async-start | bytes 5013504 | tf_op jit(solution)/shard_map/all_gather | solution.py:39
  7.6 9.0 %collective-permute-start = (bf16[128,1152]{1,0:T(8,128)(2,1)S(1)}, bf16[128,1152]{1,0:T(8,128)(2,1)S(1)}, u32[]{:S(2)}, u32[]{:S(2)}) collective-permute-start(bf16[128,1152]{1,0:T(8,128)(2,1)S(1)} %convert_element_type.35), channel_id=1, source_target_pairs={{0,0},{1,16},{16,1},{17,17},{2,2},{3,18},{18,3},{19,19},{4,4},{5,2... | collective-permute-start | bytes 884744 | tf_op jit(solution)/shard_map/ppermute | solution.py:38
  16.6 0.7 copy-start
  17.4 3.7 %collective-permute-start.1 = (bf16[128,1152]{1,0:T(8,128)(2,1)}, bf16[128,1152]{1,0:T(8,128)(2,1)S(1)}, u32[]{:S(2)}, u32[]{:S(2)}) collective-permute-start(bf16[128,1152]{1,0:T(8,128)(2,1)} %copy-done), channel_id=1, source_target_pairs={{0,1},{1,0},{2,3},{3,2},{4,5},{5,4},{6,7},{7,6},{8,9},{9,8},{10,11... | collective-permute-start | bytes 884744 | tf_op jit(solution)/shard_map/ppermute | solution.py:40
  125.2 18.8 %all-to-all-start.1 = ((bf16[16,256,128]{2,1,0:T(8,128)(2,1)}), bf16[16,256,128]{2,1,0:T(8,128)(2,1)S(1)}, u32[]{:S(2)}, u32[]{:S(2)}) async-start(bf16[16,256,128]{2,1,0:T(8,128)(2,1)} %broadcast_in_dim.4), calls=%async_computation.1 | async-start | bytes 2097152 | tf_op jit(solution)/shard_map/all_to_all | solution.py:17
  144.2 35.7 %collective-permute-start.6 = (bf16[4,4,256,128]{3,2,1,0:T(8,128)(2,1)S(1)}, bf16[4,4,256,128]{3,2,1,0:T(8,128)(2,1)S(1)}, u32[]{:S(2)}, u32[]{:S(2)}) collective-permute-start(bf16[4,4,256,128]{3,2,1,0:T(8,128)(2,1)S(1)} %pad_maximum_fusion), channel_id=1, source_target_pairs={{0,1},{1,0},{2,3},{3,2},{4,5},{5,4},{6,7},{7,6},{8,9},{9,8},{10,11... | collective-permute-start | bytes 3145736 | tf_op jit(solution)/shard_map/ppermute | solution.py:66
  158.8 44.4 %slice-start = ((s8[4718592]{0:T(1024)(128)(4,1)}), s8[4194304]{0:T(1024)(128)(4,1)S(1)}, s32[]{:S(2)}) async-start(s8[4718592]{0:T(1024)(128)(4,1)} %bitcast.92), calls=%async_computation.4 | async-start | bytes 8388608
  158.8 13.0 %collective-permute-start.4 = (bf16[2,256,128]{2,1,0:T(8,128)(2,1)S(1)}, bf16[2,256,128]{2,1,0:T(8,128)(2,1)S(1)}, u32[]{:S(2)}, u32[]{:S(2)}) collective-permute-start(bf16[2,256,128]{2,1,0:T(8,128)(2,1)S(1)} %bitcast.106), channel_id=1, source_target_pairs={{0,448},{32,480},{64,0},{96,32},{128,64},{160,96},{192,128},{224,1... | collective-permute-start | bytes 393224 | tf_op jit(solution)/shard_map/ppermute | solution.py:23
  163.4 10.9 %collective-permute-start.5 = (bf16[2,256,128]{2,1,0:T(8,128)(2,1)S(1)}, bf16[2,256,128]{2,1,0:T(8,128)(2,1)S(1)}, u32[]{:S(2)}, u32[]{:S(2)}) collective-permute-start(bf16[2,256,128]{2,1,0:T(8,128)(2,1)S(1)} %bitcast.105), channel_id=1, source_target_pairs={{0,64},{32,96},{64,128},{96,160},{128,192},{160,224},{192,256},{22... | collective-permute-start | bytes 393224 | tf_op jit(solution)/shard_map/ppermute | solution.py:23
  165.4 14.3 %collective-permute-start.3 = (bf16[4,256,128]{2,1,0:T(8,128)(2,1)S(1)}, bf16[4,256,128]{2,1,0:T(8,128)(2,1)S(1)}, u32[]{:S(2)}, u32[]{:S(2)}) collective-permute-start(bf16[4,256,128]{2,1,0:T(8,128)(2,1)S(1)} %bitcast.101), channel_id=1, source_target_pairs={{0,32},{32,64},{64,96},{96,128},{128,160},{160,192},{192,224},{224... | collective-permute-start | bytes 786440 | tf_op jit(solution)/shard_map/ppermute | solution.py:23
  168.1 12.6 %collective-permute-start.2 = (bf16[4,256,128]{2,1,0:T(8,128)(2,1)S(1)}, bf16[4,256,128]{2,1,0:T(8,128)(2,1)S(1)}, u32[]{:S(2)}, u32[]{:S(2)}) collective-permute-start(bf16[4,256,128]{2,1,0:T(8,128)(2,1)S(1)} %bitcast.102), channel_id=1, source_target_pairs={{0,480},{32,0},{64,32},{96,64},{128,96},{160,128},{192,160},{224,1... | collective-permute-start | bytes 786440 | tf_op jit(solution)/shard_map/ppermute | solution.py:23
  180.2 23.0 %slice-start.1 = ((s8[4718592]{0:T(1024)(128)(4,1)}), s8[524288]{0:T(1024)(128)(4,1)S(1)}, s32[]{:S(2)}) async-start(s8[4718592]{0:T(1024)(128)(4,1)} %bitcast.92), calls=%async_computation.5 | async-start | bytes 1048576
  181.1 27.3 %copy-start.1 = (bf16[128,1152]{1,0:T(8,128)(2,1)S(1)}, bf16[128,1152]{1,0:T(8,128)(2,1)}, u32[]{:S(2)}) copy-start(bf16[128,1152]{1,0:T(8,128)(2,1)} %copy-done) | copy-start | bytes 884740
  204.1 7.5 %collective-permute-start.8 = (bf16[128,1152]{1,0:T(8,128)(2,1)S(1)}, bf16[128,1152]{1,0:T(8,128)(2,1)S(1)}, u32[]{:S(2)}, u32[]{:S(2)}) collective-permute-start(bf16[128,1152]{1,0:T(8,128)(2,1)S(1)} %fusion.1), channel_id=1, source_target_pairs={{0,16},{1,0},{16,17},{17,1},{2,18},{3,2},{18,19},{19,3},{4,20},{5,... | collective-permute-start | bytes 884744 | tf_op jit(solution)/shard_map/ppermute | solution.py:78
  209.3 8.0 %collective-permute-start.7 = (bf16[128,1152]{1,0:T(8,128)(2,1)S(1)}, bf16[128,1152]{1,0:T(8,128)(2,1)S(1)}, u32[]{:S(2)}, u32[]{:S(2)}) collective-permute-start(bf16[128,1152]{1,0:T(8,128)(2,1)S(1)} %fusion.2), channel_id=1, source_target_pairs={{0,0},{1,16},{16,1},{17,17},{2,2},{3,18},{18,3},{19,19},{4,4},{5,2... | collective-permute-start | bytes 884744 | tf_op jit(solution)/shard_map/ppermute | solution.py:80
Sparse Core Ops, SparseCore 0:
  17.5 76.2 all-gather.3

commit v5 on v4

v5 whole, which is shorter than its diff:
```python
import jax
import jax.numpy as jnp
from jax import lax
from jax.sharding import Mesh, PartitionSpec as P

AXES = ("zh", "zl", "ylo", "x", "yhi", "core")
SIZES = (4, 4, 2, 4, 2, 2)
LINE = ("zh", "zl")
PLANE = ("ylo", "x", "yhi")
SWAP = ((0, 1), (1, 0))
TURN = ((0, 0), (1, 2), (2, 1), (3, 3))
CROSS = ((0, 2), (1, 0), (2, 3), (3, 1))


def share(piece, size):
    copies = jnp.broadcast_to(piece[None], (size,) + piece.shape)
    return lax.all_to_all(copies, PLANE, 0, 0)


def along(piece, shift):
    size = lax.axis_size(LINE)
    pairs = [(place, (place + shift) % size) for place in range(size)]
    return lax.ppermute(piece, LINE, pairs)


def onward(piece):
    size = lax.axis_size(LINE)
    pairs = [
        (2 * place + core, 2 * ((place + 1 - 2 * core) % size) + core)
        for place in range(size)
        for core in range(2)
    ]
    return lax.ppermute(piece, LINE + ("core",), pairs)


def swap(pieces):
    return list(lax.ppermute(jnp.stack(pieces), "core", SWAP))


def mix(left, right):
    return lax.dot_general(
        left, right, (((0, 2), (0, 1)), ((), ())), preferred_element_type=jnp.float32
    )


def nt(left, right):
    return lax.dot_general(
        left, right, (((1,), (1,)), ((), ())), preferred_element_type=jnp.float32
    )


def tn(left, right):
    return lax.dot_general(
        left, right, (((0,), (0,)), ((), ())), preferred_element_type=jnp.float32
    )


def turn_to(blocks, start):
    size = blocks.shape[0]
    return lax.dynamic_slice_in_dim(
        jnp.concatenate([blocks, blocks], 0), start % size, size, 0
    )


def plane_sum(blocks, both, chips):
    parts = jnp.stack([nt(block, both) for block in blocks])
    parts = parts.reshape(len(blocks), chips, -1, parts.shape[-1])
    return lax.all_to_all(parts.transpose(1, 0, 2, 3), PLANE, 0, 0).sum(0)


def per_device(iterate):
    rounded = iterate.astype(jnp.bfloat16)
    rows, cols = rounded.shape
    groups, steps = lax.axis_size("zh"), lax.axis_size("zl")
    slabs = groups * steps
    chips = lax.axis_size(PLANE)
    total_cols = cols * chips
    slab, core = lax.axis_index(LINE), lax.axis_index("core")
    own = lax.ppermute(rounded, ("ylo", "core"), TURN)
    other = lax.ppermute(own, "core", SWAP)
    both = jnp.concatenate([own, other], 0)
    near, far = [own], [other]
    for step in range(1, slabs // 2):
        near.append(onward(near[-1]))
        far.append(onward(far[-1]))
    near.append(onward(near[-1]))
    back = [None]
    for first, last in ((1, 4), (4, 6), (6, 8)):
        back.extend(swap(far[first:last]))
    order = near[::-1] + back[1:]
    early = plane_sum(order[3:14], both, chips)
    late = plane_sum(order[:3] + order[14:], both, chips)
    gram = jnp.concatenate([late[:3], early, late[3:]], 0) / total_cols
    gram = jnp.where(core == 0, gram, gram[::-1])
    gram = turn_to(gram, slabs + slabs // 2 - core - slab)
    gram_low = gram.astype(jnp.bfloat16)
    gram, gram_low = gram.reshape(rows, 2 * rows), gram_low.reshape(rows, 2 * rows)
    panel = share(gram_low, chips).reshape(chips, slabs, rows // chips, 2 * rows)
    panel = panel.transpose(1, 0, 2, 3).reshape(groups, steps, rows, 2 * rows)
    here = lax.all_gather(gram_low, "zh", axis=0)
    panel, _ = lax.optimization_barrier((panel, here))
    cut = groups // 2
    left = (
        here,
        along(here, -1),
        along(here, 1),
        jnp.concatenate([along(here[:cut], -2), along(here[cut:], 2)], 0),
    )
    residue = lax.axis_index("zl")
    right_own = [
        lax.dynamic_index_in_dim(panel, (residue + shift) % steps, 1, False)
        for shift in (0, 1, steps - 1, 2)
    ]
    right_other = lax.ppermute(jnp.stack(right_own), "core", SWAP)
    right_other = jnp.concatenate(
        [right_other[:, :, :, rows:], right_other[:, :, :, :rows]], 3
    )
    square = 0.0
    for place in range(steps):
        square = square + mix(left[place][:, :, :rows], right_own[place])
    for place in range(steps):
        square = square + mix(left[place][:, :, rows:], right_other[place])
    poly = (-4.775 * gram + 2.0315 * square).astype(jnp.bfloat16)
    poly = poly.reshape(slabs, rows // chips, 2 * rows)
    poly = turn_to(poly, slabs // 2 + slab + core)
    poly = jnp.where(core == 0, poly, poly[::-1])
    panel = share(poly, chips).transpose(1, 0, 2, 3).reshape(slabs * rows, 2 * rows)
    half = jnp.concatenate(order, 0)
    away = tn(panel[:, rows:], half).astype(jnp.bfloat16)
    away = lax.ppermute(away, ("ylo", "core"), CROSS)
    stay = tn(panel[:, :rows], half) + 3.4445 * own.astype(jnp.float32)
    stay = lax.ppermute(stay.astype(jnp.bfloat16), ("ylo", "core"), TURN)
    return stay.astype(jnp.float32) + away.astype(jnp.float32)


def solution(mesh):
    fine = Mesh(mesh.devices.reshape(SIZES), AXES)
    spec = P(("zh", "zl", "ylo"), ("x", "yhi", "core"))
    return jax.shard_map(
        per_device, mesh=fine, in_specs=(spec,), out_specs=spec, check_vma=False
    )
```

time: 226 us -> 243 us (1.075)
  starting transfers between devices: 44.2 us -> 141 us
  blocking collectives: 63.5 us -> 18.7 us
  waiting for transfers between devices: 92.2 us -> 51.8 us
  between operations: 13.7 us -> 0.91 us
  local copies, waits for them, and re-layouts: 2.35 us -> 12.7 us
  matrix products: 6.92 us -> 13 us
    all_gather x1 -> x0, waiting for transfers between devices: 72.8 us -> none  [per_device(): half = lax.all_gather(own, LINE, axis=0)]
    ppermute x1 -> x19, starting transfers between devices: 14.6 us -> 86 us  [the longest x15 67.5 us: onward(): return lax.ppermute(piece, LINE + ('core',), pairs)]
    all_to_all x2 -> x0, blocking collectives: 48.4 us -> none  [the longest x1 26.5 us: per_device(): summands = lax.all_to_all(partial_gram, PLANE, 0, 0)]
    all_to_all x0 -> x2, waiting for transfers between devices: none -> 20.1 us  [plane_sum(): return lax.all_to_all(parts.transpose(1, 0, 2, 3), PLANE, 0, 0).sum(0)]
    all_to_all x1 -> x2, waiting for transfers between devices: 0.01 us -> 14 us  [share(): return lax.all_to_all(copies, PLANE, 0, 0)]
    all_to_all x1 -> x2, starting transfers between devices: 3.65 us -> 15.5 us  [share(): return lax.all_to_all(copies, PLANE, 0, 0)]
    all_to_all x0 -> x2, starting transfers between devices: none -> 10.3 us  [plane_sum(): return lax.all_to_all(parts.transpose(1, 0, 2, 3), PLANE, 0, 0).sum(0)]
    dot_general x1 -> x18, matrix products: 3.45 us -> 11.5 us  [the longest x16 7.19 us: nt(): lax.dot_general(left, right, (((1,), (1,)), ((), ())), preferred_element_...]
  transfers between devices with their start and end apart: 11 -> 31, of which waited for: 7 -> 13; matrix products, arithmetic and copies ran while one was open for 1% -> 8% of each run, Pallas kernels for 0% -> 0%
where the time goes in v5:
time: 243 us; the launch traced here: 242 us
  starting transfers between devices  141 us (58%)
  waiting for transfers between devices  51.8 us (21%)
  blocking collectives  18.7 us (8%)
  matrix products  13 us (5%)
  local copies, waits for them, and re-layouts  12.7 us (5%)
  other arithmetic  3.53 us (1%)
    ppermute x15, starting transfers between devices, onward(): return lax.ppermute(piece, LINE + ('core',), pairs)  67.5 us
    all_to_all x2, waiting for transfers between devices, plane_sum(): return lax.all_to_all(parts.transpose(1, 0, 2, 3), PLANE, 0, 0).sum(0)  20.1 us
    all_gather x1, blocking collectives, per_device(): here = lax.all_gather(gram_low, 'zh', axis=0)  18.7 us
    ppermute x4, starting transfers between devices, along(): return lax.ppermute(piece, LINE, pairs)  15.8 us
    all_to_all x2, starting transfers between devices, share(): return lax.all_to_all(copies, PLANE, 0, 0)  15.5 us
    all_to_all x2, waiting for transfers between devices, share(): return lax.all_to_all(copies, PLANE, 0, 0)  14 us
    ppermute x3, starting transfers between devices, swap(): return list(lax.ppermute(jnp.stack(pieces), 'core', SWAP))  10.7 us
    all_to_all x2, starting transfers between devices, plane_sum(): return lax.all_to_all(parts.transpose(1, 0, 2, 3), PLANE, 0, 0).sum(0)  10.3 us
  transfers between devices with their start and end apart: 31, of which 13 were waited for; matrix products, arithmetic and copies ran while one was open for 8% of the time, Pallas kernels for 0%

profile of v5, /device:TPU:1, one launch (start us, length us, event | category | flops | bytes accessed | tf_op | source)
XLA Modules:
  0.0 241.9 jit_solution(9080726526739083205)
XLA Ops:
  0.0 1.1 convert_element_type.24
  1.1 4.6 %collective-permute-start = (bf16[128,1152]{1,0:T(8,128)(2,1)S(1)}, bf16[128,1152]{1,0:T(8,128)(2,1)S(1)}, u32[]{:S(2)}, u32[]{:S(2)}) collective-permute-start(bf16[128,1152]{1,0:T(8,128)(2,1)S(1)} %convert_element_type.24), channel_id=1, source_target_pairs={{0,0},{1,16},{16,1},{17,17},{2,2},{3,18},{18,3},{19,19},{4,4},{5,2... | collective-permute-start | bytes 884744 | tf_op jit(solution)/shard_map/ppermute | solution.py:79
  5.7 4.4 %collective-permute-done = bf16[128,1152]{1,0:T(8,128)(2,1)S(1)} collective-permute-done((bf16[128,1152]{1,0:T(8,128)(2,1)S(1)}, bf16[128,1152]{1,0:T(8,128)(2,1)S(1)}, u32[]{:S(2)}, u32[]{:S(2)}) %collective-permute-start) | collective-permute-done | bytes 294944 | tf_op jit(solution)/shard_map/ppermute | solution.py:79
  10.1 1.9 collective-permute-start.1
  12.0 11.1 %collective-permute-start.2 = (bf16[128,1152]{1,0:T(8,128)(2,1)S(1)}, bf16[128,1152]{1,0:T(8,128)(2,1)S(1)}, u32[]{:S(2)}, u32[]{:S(2)}) collective-permute-start(bf16[128,1152]{1,0:T(8,128)(2,1)S(1)} %collective-permute-done), channel_id=1, source_target_pairs={{0,32},{1,481},{32,64},{33,1},{64,96},{65,33},{96,128},{97,65},{12... | collective-permute-start | bytes 884744 | tf_op jit(solution)/shard_map/ppermute | solution.py:33
  23.2 2.6 %collective-permute-start.10 = (bf16[128,1152]{1,0:T(8,128)(2,1)S(1)}, bf16[128,1152]{1,0:T(8,128)(2,1)S(1)}, u32[]{:S(2)}, u32[]{:S(2)}) collective-permute-start(bf16[128,1152]{1,0:T(8,128)(2,1)S(1)} %collective-permute-done.1), channel_id=1, source_target_pairs={{0,32},{1,481},{32,64},{33,1},{64,96},{65,33},{96,128},{97,65},{12... | collective-permute-start | bytes 884744 | tf_op jit(solution)/shard_map/ppermute | solution.py:33
  25.8 1.0 collective-permute-done.2
  26.8 5.0 %collective-permute-start.3 = (bf16[128,1152]{1,0:T(8,128)(2,1)S(1)}, bf16[128,1152]{1,0:T(8,128)(2,1)S(1)}, u32[]{:S(2)}, u32[]{:S(2)}) collective-permute-start(bf16[128,1152]{1,0:T(8,128)(2,1)S(1)} %collective-permute-done.2), channel_id=1, source_target_pairs={{0,32},{1,481},{32,64},{33,1},{64,96},{65,33},{96,128},{97,65},{12... | collective-permute-start | bytes 884744 | tf_op jit(solution)/shard_map/ppermute | solution.py:33
  31.8 3.1 %collective-permute-start.11 = (bf16[128,1152]{1,0:T(8,128)(2,1)S(1)}, bf16[128,1152]{1,0:T(8,128)(2,1)S(1)}, u32[]{:S(2)}, u32[]{:S(2)}) collective-permute-start(bf16[128,1152]{1,0:T(8,128)(2,1)S(1)} %collective-permute-done.10), channel_id=1, source_target_pairs={{0,32},{1,481},{32,64},{33,1},{64,96},{65,33},{96,128},{97,65},{12... | collective-permute-start | bytes 884744 | tf_op jit(solution)/shard_map/ppermute | solution.py:33
  35.5 5.0 %collective-permute-start.4 = (bf16[128,1152]{1,0:T(8,128)(2,1)S(1)}, bf16[128,1152]{1,0:T(8,128)(2,1)S(1)}, u32[]{:S(2)}, u32[]{:S(2)}) collective-permute-start(bf16[128,1152]{1,0:T(8,128)(2,1)S(1)} %collective-permute-done.3), channel_id=1, source_target_pairs={{0,32},{1,481},{32,64},{33,1},{64,96},{65,33},{96,128},{97,65},{12... | collective-permute-start | bytes 884744 | tf_op jit(solution)/shard_map/ppermute | solution.py:33
  40.5 3.1 %collective-permute-start.12 = (bf16[128,1152]{1,0:T(8,128)(2,1)S(1)}, bf16[128,1152]{1,0:T(8,128)(2,1)S(1)}, u32[]{:S(2)}, u32[]{:S(2)}) collective-permute-start(bf16[128,1152]{1,0:T(8,128)(2,1)S(1)} %collective-permute-done.11), channel_id=1, source_target_pairs={{0,32},{1,481},{32,64},{33,1},{64,96},{65,33},{96,128},{97,65},{12... | collective-permute-start | bytes 884744 | tf_op jit(solution)/shard_map/ppermute | solution.py:33
  43.6 0.5 collective-permute-done.4
  44.1 5.0 %collective-permute-start.5 = (bf16[128,1152]{1,0:T(8,128)(2,1)S(1)}, bf16[128,1152]{1,0:T(8,128)(2,1)S(1)}, u32[]{:S(2)}, u32[]{:S(2)}) collective-permute-start(bf16[128,1152]{1,0:T(8,128)(2,1)S(1)} %collective-permute-done.4), channel_id=1, source_target_pairs={{0,32},{1,481},{32,64},{33,1},{64,96},{65,33},{96,128},{97,65},{12... | collective-permute-start | bytes 884744 | tf_op jit(solution)/shard_map/ppermute | solution.py:33
  49.2 3.1 %collective-permute-start.13 = (bf16[128,1152]{1,0:T(8,128)(2,1)S(1)}, bf16[128,1152]{1,0:T(8,128)(2,1)S(1)}, u32[]{:S(2)}, u32[]{:S(2)}) collective-permute-start(bf16[128,1152]{1,0:T(8,128)(2,1)S(1)} %collective-permute-done.12), channel_id=1, source_target_pairs={{0,32},{1,481},{32,64},{33,1},{64,96},{65,33},{96,128},{97,65},{12... | collective-permute-start | bytes 884744 | tf_op jit(solution)/shard_map/ppermute | solution.py:33
  52.3 0.5 collective-permute-done.5
  52.8 5.0 %collective-permute-start.6 = (bf16[128,1152]{1,0:T(8,128)(2,1)S(1)}, bf16[128,1152]{1,0:T(8,128)(2,1)S(1)}, u32[]{:S(2)}, u32[]{:S(2)}) collective-permute-start(bf16[128,1152]{1,0:T(8,128)(2,1)S(1)} %collective-permute-done.5), channel_id=1, source_target_pairs={{0,32},{1,481},{32,64},{33,1},{64,96},{65,33},{96,128},{97,65},{12... | collective-permute-start | bytes 884744 | tf_op jit(solution)/shard_map/ppermute | solution.py:33
  57.8 3.1 %collective-permute-start.14 = (bf16[128,1152]{1,0:T(8,128)(2,1)S(1)}, bf16[128,1152]{1,0:T(8,128)(2,1)S(1)}, u32[]{:S(2)}, u32[]{:S(2)}) collective-permute-start(bf16[128,1152]{1,0:T(8,128)(2,1)S(1)} %collective-permute-done.13), channel_id=1, source_target_pairs={{0,32},{1,481},{32,64},{33,1},{64,96},{65,33},{96,128},{97,65},{12... | collective-permute-start | bytes 884744 | tf_op jit(solution)/shard_map/ppermute | solution.py:33
  61.0 0.5 collective-permute-done.6
  61.5 5.0 %collective-permute-start.7 = (bf16[128,1152]{1,0:T(8,128)(2,1)S(1)}, bf16[128,1152]{1,0:T(8,128)(2,1)S(1)}, u32[]{:S(2)}, u32[]{:S(2)}) collective-permute-start(bf16[128,1152]{1,0:T(8,128)(2,1)S(1)} %collective-permute-done.6), channel_id=1, source_target_pairs={{0,32},{1,481},{32,64},{33,1},{64,96},{65,33},{96,128},{97,65},{12... | collective-permute-start | bytes 884744 | tf_op jit(solution)/shard_map/ppermute | solution.py:33
  66.5 3.1 %collective-permute-start.15 = (bf16[128,1152]{1,0:T(8,128)(2,1)S(1)}, bf16[128,1152]{1,0:T(8,128)(2,1)S(1)}, u32[]{:S(2)}, u32[]{:S(2)}) collective-permute-start(bf16[128,1152]{1,0:T(8,128)(2,1)S(1)} %collective-permute-done.14), channel_id=1, source_target_pairs={{0,32},{1,481},{32,64},{33,1},{64,96},{65,33},{96,128},{97,65},{12... | collective-permute-start | bytes 884744 | tf_op jit(solution)/shard_map/ppermute | solution.py:33
  69.6 0.5 collective-permute-done.7
  70.1 5.0 %collective-permute-start.8 = (bf16[128,1152]{1,0:T(8,128)(2,1)S(1)}, bf16[128,1152]{1,0:T(8,128)(2,1)S(1)}, u32[]{:S(2)}, u32[]{:S(2)}) collective-permute-start(bf16[128,1152]{1,0:T(8,128)(2,1)S(1)} %collective-permute-done.7), channel_id=1, source_target_pairs={{0,32},{1,481},{32,64},{33,1},{64,96},{65,33},{96,128},{97,65},{12... | collective-permute-start | bytes 884744 | tf_op jit(solution)/shard_map/ppermute | solution.py:33
  75.2 3.1 %collective-permute-start.16 = (bf16[128,1152]{1,0:T(8,128)(2,1)S(1)}, bf16[128,1152]{1,0:T(8,128)(2,1)S(1)}, u32[]{:S(2)}, u32[]{:S(2)}) collective-permute-start(bf16[128,1152]{1,0:T(8,128)(2,1)S(1)} %collective-permute-done.15), channel_id=1, source_target_pairs={{0,32},{1,481},{32,64},{33,1},{64,96},{65,33},{96,128},{97,65},{12... | collective-permute-start | bytes 884744 | tf_op jit(solution)/shard_map/ppermute | solution.py:33
  78.4 6.4 %collective-permute-start.18 = (bf16[3,128,1152]{2,1,0:T(8,128)(2,1)S(1)}, bf16[3,128,1152]{2,1,0:T(8,128)(2,1)S(1)}, u32[]{:S(2)}, u32[]{:S(2)}) collective-permute-start(bf16[3,128,1152]{2,1,0:T(8,128)(2,1)S(1)} %pad_maximum_fusion.1), channel_id=1, source_target_pairs={{0,1},{1,0},{2,3},{3,2},{4,5},{5,4},{6,7},{7,6},{8,9},{9,8},{10,11... | collective-permute-start | bytes 2654216 | tf_op jit(solution)/shard_map/ppermute | solution.py:37
  84.8 4.9 %collective-permute-start.9 = (bf16[128,1152]{1,0:T(8,128)(2,1)S(1)}, bf16[128,1152]{1,0:T(8,128)(2,1)S(1)}, u32[]{:S(2)}, u32[]{:S(2)}) collective-permute-start(bf16[128,1152]{1,0:T(8,128)(2,1)S(1)} %collective-permute-done.8), channel_id=1, source_target_pairs={{0,32},{1,481},{32,64},{33,1},{64,96},{65,33},{96,128},{97,65},{12... | collective-permute-start | bytes 884744 | tf_op jit(solution)/shard_map/ppermute | solution.py:33
  89.7 0.9 pad_maximum_fusion.3
  90.6 1.9 collective-permute-start.19
  92.6 2.4 collective-permute-start.17
  99.4 0.5 copy-done.4
  100.3 0.9 copy.3
  101.2 6.6 %all-to-all-start = ((f32[16,5,8,256]{3,2,1,0:T(8,128)}), f32[16,5,8,256]{3,2,1,0:T(8,128)S(1)}, u32[]{:S(2)}, u32[]{:S(2)}) async-start(f32[16,5,8,256]{3,2,1,0:T(8,128)} %copy.3), calls=%async_computation | async-start | bytes 1310720 | tf_op jit(solution)/shard_map/all_to_all | solution.py:68
  107.9 1.0 fusion.3
  108.9 1.0 fusion.2
  109.9 1.0 fusion.1
  110.8 2.6 %copy.4 = f32[16,11,8,256]{3,2,1,0:T(8,128)} copy(f32[16,11,8,256]{3,2,0,1:T(8,128)} %bitcast.254) | data formatting | bytes 2883584 | tf_op jit(solution)/shard_map/transpose | solution.py:68
  113.5 4.6 %all-to-all-done = f32[16,5,8,256]{3,2,1,0:T(8,128)S(1)} async-done(((f32[16,5,8,256]{3,2,1,0:T(8,128)}), f32[16,5,8,256]{3,2,1,0:T(8,128)S(1)}, u32[]{:S(2)}, u32[]{:S(2)}) %all-to-all-start) | async-done | bytes 655392 | tf_op jit(solution)/shard_map/all_to_all | solution.py:68
  118.0 3.7 %all-to-all-start.1 = ((f32[16,11,8,256]{3,2,1,0:T(8,128)}), f32[16,11,8,256]{3,2,1,0:T(8,128)S(1)}, u32[]{:S(2)}, u32[]{:S(2)}) async-start(f32[16,11,8,256]{3,2,1,0:T(8,128)} %copy.4), calls=%async_computation.1 | async-start | bytes 2883584 | tf_op jit(solution)/shard_map/all_to_all | solution.py:68
  121.8 0.7 bitcast_dynamic-update-slice_fusion.6
  122.7 15.5 %all-to-all-done.1 = f32[16,11,8,256]{3,2,1,0:T(8,128)S(1)} async-done(((f32[16,11,8,256]{3,2,1,0:T(8,128)}), f32[16,11,8,256]{3,2,1,0:T(8,128)S(1)}, u32[]{:S(2)}, u32[]{:S(2)}) %all-to-all-start.1) | async-done | bytes 1441824 | tf_op jit(solution)/shard_map/all_to_all | solution.py:68
  138.3 1.1 broadcast_in_dim.14
  139.5 9.0 %all-to-all-start.2 = ((bf16[16,128,256]{2,1,0:T(8,128)(2,1)}), bf16[16,128,256]{2,1,0:T(8,128)(2,1)S(1)}, u32[]{:S(2)}, u32[]{:S(2)}) async-start(bf16[16,128,256]{2,1,0:T(8,128)(2,1)} %broadcast_in_dim.14), calls=%async_computation.2 | async-start | bytes 2097152 | tf_op jit(solution)/shard_map/all_to_all | solution.py:17
  148.4 0.7 bitcast_dynamic-update-slice_fusion.5
  149.2 0.7 bitcast_dynamic-update-slice_fusion.4
  149.9 18.7 %all_gather.3 = bf16[4,128,256]{2,1,0:T(8,128)(2,1)S(1)} all-gather(bf16[1,128,256]{2,1,0:T(8,128)(2,1)S(1)} %get-tuple-element.7), channel_id=1, replica_groups=mesh['zh'=4,'zl'=4,'ylo'=2,'x'=4,'yhi'=2,'core'=2] {'zh'}, dimensions={0}, use_global_device_ids=true | all-gather | bytes 327680 | tf_op jit(solution)/shard_map/all_gather | solution.py:100
  168.6 5.2 %collective-permute-start.22 = (bf16[2,128,256]{2,1,0:T(8,128)(2,1)S(1)}, bf16[2,128,256]{2,1,0:T(8,128)(2,1)S(1)}, u32[]{:S(2)}, u32[]{:S(2)}) collective-permute-start(bf16[2,128,256]{2,1,0:T(8,128)(2,1)S(1)} %get-tuple-element.18), channel_id=1, source_target_pairs={{0,448},{32,480},{64,0},{96,32},{128,64},{160,96},{192,128},{224,1... | collective-permute-start | bytes 393224 | tf_op jit(solution)/shard_map/ppermute | solution.py:23
  173.8 1.9 collective-permute-start.23
  176.1 7.8 %collective-permute-start.24 = (bf16[4,4,128,256]{3,2,1,0:T(8,128)(2,1)S(1)}, bf16[4,4,128,256]{3,2,1,0:T(8,128)(2,1)S(1)}, u32[]{:S(2)}, u32[]{:S(2)}) collective-permute-start(bf16[4,4,128,256]{3,2,1,0:T(8,128)(2,1)S(1)} %pad_maximum_fusion), channel_id=1, source_target_pairs={{0,1},{1,0},{2,3},{3,2},{4,5},{5,4},{6,7},{7,6},{8,9},{9,8},{10,11... | collective-permute-start | bytes 3145736 | tf_op jit(solution)/shard_map/ppermute | solution.py:114
  183.9 0.7 bitcast_dynamic-update-slice_fusion.3
  184.7 4.1 %collective-permute-start.21 = (bf16[4,128,256]{2,1,0:T(8,128)(2,1)S(1)}, bf16[4,128,256]{2,1,0:T(8,128)(2,1)S(1)}, u32[]{:S(2)}, u32[]{:S(2)}) collective-permute-start(bf16[4,128,256]{2,1,0:T(8,128)(2,1)S(1)} %all_gather.3), channel_id=1, source_target_pairs={{0,32},{32,64},{64,96},{96,128},{128,160},{160,192},{192,224},{224... | collective-permute-start | bytes 786440 | tf_op jit(solution)/shard_map/ppermute | solution.py:23
  188.8 4.6 %collective-permute-start.20 = (bf16[4,128,256]{2,1,0:T(8,128)(2,1)S(1)}, bf16[4,128,256]{2,1,0:T(8,128)(2,1)S(1)}, u32[]{:S(2)}, u32[]{:S(2)}) collective-permute-start(bf16[4,128,256]{2,1,0:T(8,128)(2,1)S(1)} %all_gather.3), channel_id=1, source_target_pairs={{0,480},{32,0},{64,32},{96,64},{128,96},{160,128},{192,160},{224,1... | collective-permute-start | bytes 786440 | tf_op jit(solution)/shard_map/ppermute | solution.py:23
  193.8 4.3 %collective-permute-done.21 = bf16[4,128,256]{2,1,0:T(8,128)(2,1)S(1)} collective-permute-done((bf16[4,128,256]{2,1,0:T(8,128)(2,1)S(1)}, bf16[4,128,256]{2,1,0:T(8,128)(2,1)S(1)}, u32[]{:S(2)}, u32[]{:S(2)}) %collective-permute-start.21) | collective-permute-done | bytes 262176 | tf_op jit(solution)/shard_map/ppermute | solution.py:23
  199.8 1.1 broadcast_in_dim.15
  200.9 6.6 %all-to-all-start.3 = ((bf16[16,16,8,256]{3,2,1,0:T(8,128)(2,1)}), bf16[16,16,8,256]{3,2,1,0:T(8,128)(2,1)S(1)}, u32[]{:S(2)}, u32[]{:S(2)}) async-start(bf16[16,16,8,256]{3,2,1,0:T(8,128)(2,1)} %broadcast_in_dim.15), calls=%async_computation.3 | async-start | bytes 2097152 | tf_op jit(solution)/shard_map/all_to_all | solution.py:17
  207.4 0.8 bitcast_dynamic-update-slice_fusion.2
  208.2 0.8 bitcast_dynamic-update-slice_fusion.1
  209.0 0.7 bitcast_dynamic-update-slice_fusion
  209.7 14.0 %all-to-all-done.3 = bf16[16,16,8,256]{3,2,1,0:T(8,128)(2,1)S(1)} async-done(((bf16[16,16,8,256]{3,2,1,0:T(8,128)(2,1)}), bf16[16,16,8,256]{3,2,1,0:T(8,128)(2,1)S(1)}, u32[]{:S(2)}, u32[]{:S(2)}) %all-to-all-start.3) | async-done | bytes 1048608 | tf_op jit(solution)/shard_map/all_to_all | solution.py:17
  223.8 3.4 %convolution_convert_fusion = bf16[128,1152]{1,0:T(8,128)(2,1)S(1)} fusion(bf16[2048,1152]{1,0:T(8,128)(2,1)} %bitcast_dynamic-update-slice_fusion, bf16[2048,256]{1,0:T(8,128)(2,1)S(1)} %bitcast.252), kind=kOutput, calls=%fused_computation.2 | convolution fusion | flops 604127232 | bytes 5537792 | tf_op jit(solution)/shard_map/dot_general | solution.py:53
  227.4 0.9 fusion
  228.3 5.1 %collective-permute-start.25 = (bf16[128,1152]{1,0:T(8,128)(2,1)S(1)}, bf16[128,1152]{1,0:T(8,128)(2,1)S(1)}, u32[]{:S(2)}, u32[]{:S(2)}) collective-permute-start(bf16[128,1152]{1,0:T(8,128)(2,1)S(1)} %fusion), channel_id=1, source_target_pairs={{0,0},{1,16},{16,1},{17,17},{2,2},{3,18},{18,3},{19,19},{4,4},{5,2... | collective-permute-start | bytes 884744 | tf_op jit(solution)/shard_map/ppermute | solution.py:132
  233.5 1.9 collective-permute-start.26
  235.4 2.5 %collective-permute-done.25 = bf16[128,1152]{1,0:T(8,128)(2,1)S(1)} collective-permute-done((bf16[128,1152]{1,0:T(8,128)(2,1)S(1)}, bf16[128,1152]{1,0:T(8,128)(2,1)S(1)}, u32[]{:S(2)}, u32[]{:S(2)}) %collective-permute-start.25) | collective-permute-done | bytes 294944 | tf_op jit(solution)/shard_map/ppermute | solution.py:132
  237.9 3.1 %collective-permute-done.26 = bf16[128,1152]{1,0:T(8,128)(2,1)S(1)} collective-permute-done((bf16[128,1152]{1,0:T(8,128)(2,1)S(1)}, bf16[128,1152]{1,0:T(8,128)(2,1)S(1)}, u32[]{:S(2)}, u32[]{:S(2)}) %collective-permute-start.26) | collective-permute-done | bytes 294944 | tf_op jit(solution)/shard_map/ppermute | solution.py:130
  241.0 0.9 convert_add_fusion
  (83 shorter events, 8.2 us)
Async XLA Ops:
  1.1 9.0 %collective-permute-start = (bf16[128,1152]{1,0:T(8,128)(2,1)S(1)}, bf16[128,1152]{1,0:T(8,128)(2,1)S(1)}, u32[]{:S(2)}, u32[]{:S(2)}) collective-permute-start(bf16[128,1152]{1,0:T(8,128)(2,1)S(1)} %convert_element_type.24), channel_id=1, source_target_pairs={{0,0},{1,16},{16,1},{17,17},{2,2},{3,18},{18,3},{19,19},{4,4},{5,2... | collective-permute-start | bytes 884744 | tf_op jit(solution)/shard_map/ppermute | solution.py:79
  10.1 13.1 %collective-permute-start.1 = (bf16[128,1152]{1,0:T(8,128)(2,1)S(1)}, bf16[128,1152]{1,0:T(8,128)(2,1)S(1)}, u32[]{:S(2)}, u32[]{:S(2)}) collective-permute-start(bf16[128,1152]{1,0:T(8,128)(2,1)S(1)} %collective-permute-done), channel_id=1, source_target_pairs={{0,1},{1,0},{2,3},{3,2},{4,5},{5,4},{6,7},{7,6},{8,9},{9,8},{10,11... | collective-permute-start | bytes 884744 | tf_op jit(solution)/shard_map/ppermute | solution.py:80
  12.0 14.8 %collective-permute-start.2 = (bf16[128,1152]{1,0:T(8,128)(2,1)S(1)}, bf16[128,1152]{1,0:T(8,128)(2,1)S(1)}, u32[]{:S(2)}, u32[]{:S(2)}) collective-permute-start(bf16[128,1152]{1,0:T(8,128)(2,1)S(1)} %collective-permute-done), channel_id=1, source_target_pairs={{0,32},{1,481},{32,64},{33,1},{64,96},{65,33},{96,128},{97,65},{12... | collective-permute-start | bytes 884744 | tf_op jit(solution)/shard_map/ppermute | solution.py:33
  23.2 8.7 %collective-permute-start.10 = (bf16[128,1152]{1,0:T(8,128)(2,1)S(1)}, bf16[128,1152]{1,0:T(8,128)(2,1)S(1)}, u32[]{:S(2)}, u32[]{:S(2)}) collective-permute-start(bf16[128,1152]{1,0:T(8,128)(2,1)S(1)} %collective-permute-done.1), channel_id=1, source_target_pairs={{0,32},{1,481},{32,64},{33,1},{64,96},{65,33},{96,128},{97,65},{12... | collective-permute-start | bytes 884744 | tf_op jit(solution)/shard_map/ppermute | solution.py:33
  26.8 8.7 %collective-permute-start.3 = (bf16[128,1152]{1,0:T(8,128)(2,1)S(1)}, bf16[128,1152]{1,0:T(8,128)(2,1)S(1)}, u32[]{:S(2)}, u32[]{:S(2)}) collective-permute-start(bf16[128,1152]{1,0:T(8,128)(2,1)S(1)} %collective-permute-done.2), channel_id=1, source_target_pairs={{0,32},{1,481},{32,64},{33,1},{64,96},{65,33},{96,128},{97,65},{12... | collective-permute-start | bytes 884744 | tf_op jit(solution)/shard_map/ppermute | solution.py:33
  31.8 8.7 %collective-permute-start.11 = (bf16[128,1152]{1,0:T(8,128)(2,1)S(1)}, bf16[128,1152]{1,0:T(8,128)(2,1)S(1)}, u32[]{:S(2)}, u32[]{:S(2)}) collective-permute-start(bf16[128,1152]{1,0:T(8,128)(2,1)S(1)} %collective-permute-done.10), channel_id=1, source_target_pairs={{0,32},{1,481},{32,64},{33,1},{64,96},{65,33},{96,128},{97,65},{12... | collective-permute-start | bytes 884744 | tf_op jit(solution)/shard_map/ppermute | solution.py:33
  35.5 8.7 %collective-permute-start.4 = (bf16[128,1152]{1,0:T(8,128)(2,1)S(1)}, bf16[128,1152]{1,0:T(8,128)(2,1)S(1)}, u32[]{:S(2)}, u32[]{:S(2)}) collective-permute-start(bf16[128,1152]{1,0:T(8,128)(2,1)S(1)} %collective-permute-done.3), channel_id=1, source_target_pairs={{0,32},{1,481},{32,64},{33,1},{64,96},{65,33},{96,128},{97,65},{12... | collective-permute-start | bytes 884744 | tf_op jit(solution)/shard_map/ppermute | solution.py:33
  40.5 8.7 %collective-permute-start.12 = (bf16[128,1152]{1,0:T(8,128)(2,1)S(1)}, bf16[128,1152]{1,0:T(8,128)(2,1)S(1)}, u32[]{:S(2)}, u32[]{:S(2)}) collective-permute-start(bf16[128,1152]{1,0:T(8,128)(2,1)S(1)} %collective-permute-done.11), channel_id=1, source_target_pairs={{0,32},{1,481},{32,64},{33,1},{64,96},{65,33},{96,128},{97,65},{12... | collective-permute-start | bytes 884744 | tf_op jit(solution)/shard_map/ppermute | solution.py:33
  44.1 8.7 %collective-permute-start.5 = (bf16[128,1152]{1,0:T(8,128)(2,1)S(1)}, bf16[128,1152]{1,0:T(8,128)(2,1)S(1)}, u32[]{:S(2)}, u32[]{:S(2)}) collective-permute-start(bf16[128,1152]{1,0:T(8,128)(2,1)S(1)} %collective-permute-done.4), channel_id=1, source_target_pairs={{0,32},{1,481},{32,64},{33,1},{64,96},{65,33},{96,128},{97,65},{12... | collective-permute-start | bytes 884744 | tf_op jit(solution)/shard_map/ppermute | solution.py:33
  49.2 8.7 %collective-permute-start.13 = (bf16[128,1152]{1,0:T(8,128)(2,1)S(1)}, bf16[128,1152]{1,0:T(8,128)(2,1)S(1)}, u32[]{:S(2)}, u32[]{:S(2)}) collective-permute-start(bf16[128,1152]{1,0:T(8,128)(2,1)S(1)} %collective-permute-done.12), channel_id=1, source_target_pairs={{0,32},{1,481},{32,64},{33,1},{64,96},{65,33},{96,128},{97,65},{12... | collective-permute-start | bytes 884744 | tf_op jit(solution)/shard_map/ppermute | solution.py:33
  52.8 8.7 %collective-permute-start.6 = (bf16[128,1152]{1,0:T(8,128)(2,1)S(1)}, bf16[128,1152]{1,0:T(8,128)(2,1)S(1)}, u32[]{:S(2)}, u32[]{:S(2)}) collective-permute-start(bf16[128,1152]{1,0:T(8,128)(2,1)S(1)} %collective-permute-done.5), channel_id=1, source_target_pairs={{0,32},{1,481},{32,64},{33,1},{64,96},{65,33},{96,128},{97,65},{12... | collective-permute-start | bytes 884744 | tf_op jit(solution)/shard_map/ppermute | solution.py:33
  57.8 8.7 %collective-permute-start.14 = (bf16[128,1152]{1,0:T(8,128)(2,1)S(1)}, bf16[128,1152]{1,0:T(8,128)(2,1)S(1)}, u32[]{:S(2)}, u32[]{:S(2)}) collective-permute-start(bf16[128,1152]{1,0:T(8,128)(2,1)S(1)} %collective-permute-done.13), channel_id=1, source_target_pairs={{0,32},{1,481},{32,64},{33,1},{64,96},{65,33},{96,128},{97,65},{12... | collective-permute-start | bytes 884744 | tf_op jit(solution)/shard_map/ppermute | solution.py:33
  61.5 8.7 %collective-permute-start.7 = (bf16[128,1152]{1,0:T(8,128)(2,1)S(1)}, bf16[128,1152]{1,0:T(8,128)(2,1)S(1)}, u32[]{:S(2)}, u32[]{:S(2)}) collective-permute-start(bf16[128,1152]{1,0:T(8,128)(2,1)S(1)} %collective-permute-done.6), channel_id=1, source_target_pairs={{0,32},{1,481},{32,64},{33,1},{64,96},{65,33},{96,128},{97,65},{12... | collective-permute-start | bytes 884744 | tf_op jit(solution)/shard_map/ppermute | solution.py:33
  66.5 8.7 %collective-permute-start.15 = (bf16[128,1152]{1,0:T(8,128)(2,1)S(1)}, bf16[128,1152]{1,0:T(8,128)(2,1)S(1)}, u32[]{:S(2)}, u32[]{:S(2)}) collective-permute-start(bf16[128,1152]{1,0:T(8,128)(2,1)S(1)} %collective-permute-done.14), channel_id=1, source_target_pairs={{0,32},{1,481},{32,64},{33,1},{64,96},{65,33},{96,128},{97,65},{12... | collective-permute-start | bytes 884744 | tf_op jit(solution)/shard_map/ppermute | solution.py:33
  70.1 14.7 %collective-permute-start.8 = (bf16[128,1152]{1,0:T(8,128)(2,1)S(1)}, bf16[128,1152]{1,0:T(8,128)(2,1)S(1)}, u32[]{:S(2)}, u32[]{:S(2)}) collective-permute-start(bf16[128,1152]{1,0:T(8,128)(2,1)S(1)} %collective-permute-done.7), channel_id=1, source_target_pairs={{0,32},{1,481},{32,64},{33,1},{64,96},{65,33},{96,128},{97,65},{12... | collective-permute-start | bytes 884744 | tf_op jit(solution)/shard_map/ppermute | solution.py:33
  75.2 17.3 %collective-permute-start.16 = (bf16[128,1152]{1,0:T(8,128)(2,1)S(1)}, bf16[128,1152]{1,0:T(8,128)(2,1)S(1)}, u32[]{:S(2)}, u32[]{:S(2)}) collective-permute-start(bf16[128,1152]{1,0:T(8,128)(2,1)S(1)} %collective-permute-done.15), channel_id=1, source_target_pairs={{0,32},{1,481},{32,64},{33,1},{64,96},{65,33},{96,128},{97,65},{12... | collective-permute-start | bytes 884744 | tf_op jit(solution)/shard_map/ppermute | solution.py:33
  78.4 19.3 %collective-permute-start.18 = (bf16[3,128,1152]{2,1,0:T(8,128)(2,1)S(1)}, bf16[3,128,1152]{2,1,0:T(8,128)(2,1)S(1)}, u32[]{:S(2)}, u32[]{:S(2)}) collective-permute-start(bf16[3,128,1152]{2,1,0:T(8,128)(2,1)S(1)} %pad_maximum_fusion.1), channel_id=1, source_target_pairs={{0,1},{1,0},{2,3},{3,2},{4,5},{5,4},{6,7},{7,6},{8,9},{9,8},{10,11... | collective-permute-start | bytes 2654216 | tf_op jit(solution)/shard_map/ppermute | solution.py:37
  84.8 10.2 %collective-permute-start.9 = (bf16[128,1152]{1,0:T(8,128)(2,1)S(1)}, bf16[128,1152]{1,0:T(8,128)(2,1)S(1)}, u32[]{:S(2)}, u32[]{:S(2)}) collective-permute-start(bf16[128,1152]{1,0:T(8,128)(2,1)S(1)} %collective-permute-done.8), channel_id=1, source_target_pairs={{0,32},{1,481},{32,64},{33,1},{64,96},{65,33},{96,128},{97,65},{12... | collective-permute-start | bytes 884744 | tf_op jit(solution)/shard_map/ppermute | solution.py:33
  90.6 18.3 %collective-permute-start.19 = (bf16[2,128,1152]{2,1,0:T(8,128)(2,1)}, bf16[2,128,1152]{2,1,0:T(8,128)(2,1)S(1)}, u32[]{:S(2)}, u32[]{:S(2)}) collective-permute-start(bf16[2,128,1152]{2,1,0:T(8,128)(2,1)} %pad_maximum_fusion.3), channel_id=1, source_target_pairs={{0,1},{1,0},{2,3},{3,2},{4,5},{5,4},{6,7},{7,6},{8,9},{9,8},{10,11... | collective-permute-start | bytes 1769480 | tf_op jit(solution)/shard_map/ppermute | solution.py:37
  92.6 6.5 %collective-permute-start.17 = (bf16[2,128,1152]{2,1,0:T(8,128)(2,1)S(1)}, bf16[2,128,1152]{2,1,0:T(8,128)(2,1)S(1)}, u32[]{:S(2)}, u32[]{:S(2)}) collective-permute-start(bf16[2,128,1152]{2,1,0:T(8,128)(2,1)S(1)} %pad_maximum_fusion.2), channel_id=1, source_target_pairs={{0,1},{1,0},{2,3},{3,2},{4,5},{5,4},{6,7},{7,6},{8,9},{9,8},{10,11... | collective-permute-start | bytes 1769480 | tf_op jit(solution)/shard_map/ppermute | solution.py:37
  95.3 3.1 %copy-start = (bf16[2048,1152]{1,0:T(8,128)(2,1)}, bf16[2048,1152]{1,0:T(8,128)(2,1)S(1)}, u32[]{:S(2)}) copy-start(bf16[2048,1152]{1,0:T(8,128)(2,1)S(1)} %get-tuple-element.16) | copy-start | bytes 14155780
  98.4 1.9 copy-start.6
  99.1 0.9 copy-start.4
  101.2 16.8 %all-to-all-start = ((f32[16,5,8,256]{3,2,1,0:T(8,128)}), f32[16,5,8,256]{3,2,1,0:T(8,128)S(1)}, u32[]{:S(2)}, u32[]{:S(2)}) async-start(f32[16,5,8,256]{3,2,1,0:T(8,128)} %copy.3), calls=%async_computation | async-start | bytes 1310720 | tf_op jit(solution)/shard_map/all_to_all | solution.py:68
  108.9 9.2 %copy-start.2 = (bf16[2,128,1152]{2,1,0:T(8,128)(2,1)}, bf16[2,128,1152]{2,1,0:T(8,128)(2,1)S(1)}, u32[]{:S(2)}) copy-start(bf16[2,128,1152]{2,1,0:T(8,128)(2,1)S(1)} %collective-permute-done.19) | copy-start | bytes 1769476
  118.0 20.1 %all-to-all-start.1 = ((f32[16,11,8,256]{3,2,1,0:T(8,128)}), f32[16,11,8,256]{3,2,1,0:T(8,128)S(1)}, u32[]{:S(2)}, u32[]{:S(2)}) async-start(f32[16,11,8,256]{3,2,1,0:T(8,128)} %copy.4), calls=%async_computation.1 | async-start | bytes 2883584 | tf_op jit(solution)/shard_map/all_to_all | solution.py:68
  139.4 44.5 %copy-start.3 = (bf16[2,128,1152]{2,1,0:T(8,128)(2,1)S(1)}, bf16[2,128,1152]{2,1,0:T(8,128)(2,1)}, u32[]{:S(2)}) copy-start(bf16[2,128,1152]{2,1,0:T(8,128)(2,1)} %copy-done.2) | copy-start | bytes 1769476
  139.5 36.3 %all-to-all-start.2 = ((bf16[16,128,256]{2,1,0:T(8,128)(2,1)}), bf16[16,128,256]{2,1,0:T(8,128)(2,1)S(1)}, u32[]{:S(2)}, u32[]{:S(2)}) async-start(bf16[16,128,256]{2,1,0:T(8,128)(2,1)} %broadcast_in_dim.14), calls=%async_computation.2 | async-start | bytes 2097152 | tf_op jit(solution)/shard_map/all_to_all | solution.py:17
  168.6 24.8 %collective-permute-start.22 = (bf16[2,128,256]{2,1,0:T(8,128)(2,1)S(1)}, bf16[2,128,256]{2,1,0:T(8,128)(2,1)S(1)}, u32[]{:S(2)}, u32[]{:S(2)}) collective-permute-start(bf16[2,128,256]{2,1,0:T(8,128)(2,1)S(1)} %get-tuple-element.18), channel_id=1, source_target_pairs={{0,448},{32,480},{64,0},{96,32},{128,64},{160,96},{192,128},{224,1... | collective-permute-start | bytes 393224 | tf_op jit(solution)/shard_map/ppermute | solution.py:23
  173.8 19.6 %collective-permute-start.23 = (bf16[2,128,256]{2,1,0:T(8,128)(2,1)S(1)}, bf16[2,128,256]{2,1,0:T(8,128)(2,1)S(1)}, u32[]{:S(2)}, u32[]{:S(2)}) collective-permute-start(bf16[2,128,256]{2,1,0:T(8,128)(2,1)S(1)} %get-tuple-element.17), channel_id=1, source_target_pairs={{0,64},{32,96},{64,128},{96,160},{128,192},{160,224},{192,256},{22... | collective-permute-start | bytes 393224 | tf_op jit(solution)/shard_map/ppermute | solution.py:23
  176.1 22.2 %collective-permute-start.24 = (bf16[4,4,128,256]{3,2,1,0:T(8,128)(2,1)S(1)}, bf16[4,4,128,256]{3,2,1,0:T(8,128)(2,1)S(1)}, u32[]{:S(2)}, u32[]{:S(2)}) collective-permute-start(bf16[4,4,128,256]{3,2,1,0:T(8,128)(2,1)S(1)} %pad_maximum_fusion), channel_id=1, source_target_pairs={{0,1},{1,0},{2,3},{3,2},{4,5},{5,4},{6,7},{7,6},{8,9},{9,8},{10,11... | collective-permute-start | bytes 3145736 | tf_op jit(solution)/shard_map/ppermute | solution.py:114
  184.7 13.4 %collective-permute-start.21 = (bf16[4,128,256]{2,1,0:T(8,128)(2,1)S(1)}, bf16[4,128,256]{2,1,0:T(8,128)(2,1)S(1)}, u32[]{:S(2)}, u32[]{:S(2)}) collective-permute-start(bf16[4,128,256]{2,1,0:T(8,128)(2,1)S(1)} %all_gather.3), channel_id=1, source_target_pairs={{0,32},{32,64},{64,96},{96,128},{128,160},{160,192},{192,224},{224... | collective-permute-start | bytes 786440 | tf_op jit(solution)/shard_map/ppermute | solution.py:23
  188.8 10.4 %collective-permute-start.20 = (bf16[4,128,256]{2,1,0:T(8,128)(2,1)S(1)}, bf16[4,128,256]{2,1,0:T(8,128)(2,1)S(1)}, u32[]{:S(2)}, u32[]{:S(2)}) collective-permute-start(bf16[4,128,256]{2,1,0:T(8,128)(2,1)S(1)} %all_gather.3), channel_id=1, source_target_pairs={{0,480},{32,0},{64,32},{96,64},{128,96},{160,128},{192,160},{224,1... | collective-permute-start | bytes 786440 | tf_op jit(solution)/shard_map/ppermute | solution.py:23
  198.8 9.4 %copy-start.5 = (bf16[2,128,1152]{2,1,0:T(8,128)(2,1)S(1)}, bf16[2,128,1152]{2,1,0:T(8,128)(2,1)}, u32[]{:S(2)}) copy-start(bf16[2,128,1152]{2,1,0:T(8,128)(2,1)} %copy-done.4) | copy-start | bytes 1769476
  200.9 22.8 %all-to-all-start.3 = ((bf16[16,16,8,256]{3,2,1,0:T(8,128)(2,1)}), bf16[16,16,8,256]{3,2,1,0:T(8,128)(2,1)S(1)}, u32[]{:S(2)}, u32[]{:S(2)}) async-start(bf16[16,16,8,256]{3,2,1,0:T(8,128)(2,1)} %broadcast_in_dim.15), calls=%async_computation.3 | async-start | bytes 2097152 | tf_op jit(solution)/shard_map/all_to_all | solution.py:17
  223.7 3.8 %copy-start.1 = (bf16[2048,1152]{1,0:T(8,128)(2,1)S(1)}, bf16[2048,1152]{1,0:T(8,128)(2,1)}, u32[]{:S(2)}) copy-start(bf16[2048,1152]{1,0:T(8,128)(2,1)} %bitcast_dynamic-update-slice_fusion) | copy-start | bytes 14155780
  228.3 9.5 %collective-permute-start.25 = (bf16[128,1152]{1,0:T(8,128)(2,1)S(1)}, bf16[128,1152]{1,0:T(8,128)(2,1)S(1)}, u32[]{:S(2)}, u32[]{:S(2)}) collective-permute-start(bf16[128,1152]{1,0:T(8,128)(2,1)S(1)} %fusion), channel_id=1, source_target_pairs={{0,0},{1,16},{16,1},{17,17},{2,2},{3,18},{18,3},{19,19},{4,4},{5,2... | collective-permute-start | bytes 884744 | tf_op jit(solution)/shard_map/ppermute | solution.py:132
  233.5 7.6 %collective-permute-start.26 = (bf16[128,1152]{1,0:T(8,128)(2,1)S(1)}, bf16[128,1152]{1,0:T(8,128)(2,1)S(1)}, u32[]{:S(2)}, u32[]{:S(2)}) collective-permute-start(bf16[128,1152]{1,0:T(8,128)(2,1)S(1)} %convolution_convert_fusion), channel_id=1, source_target_pairs={{0,16},{1,0},{16,17},{17,1},{2,18},{3,2},{18,19},{19,3},{4,20},{5,... | collective-permute-start | bytes 884744 | tf_op jit(solution)/shard_map/ppermute | solution.py:130

commit v6 on v5

--- a/solution.py
+++ b/solution.py
@@ -62,10 +62,13 @@
     )
 
 
-def plane_sum(blocks, both, chips):
-    parts = jnp.stack([nt(block, both) for block in blocks])
-    parts = parts.reshape(len(blocks), chips, -1, parts.shape[-1])
-    return lax.all_to_all(parts.transpose(1, 0, 2, 3), PLANE, 0, 0).sum(0)
+def products(blocks, both, chips):
+    parts = [nt(block, both).reshape(chips, -1, both.shape[0]) for block in blocks]
+    return jnp.stack(parts, 1)
+
+
+def plane_sum(parts):
+    return lax.all_to_all(parts, PLANE, 0, 0).sum(0)
 
 
 def per_device(iterate):
@@ -79,17 +82,25 @@
     own = lax.ppermute(rounded, ("ylo", "core"), TURN)
     other = lax.ppermute(own, "core", SWAP)
     both = jnp.concatenate([own, other], 0)
-    near, far = [own], [other]
-    for step in range(1, slabs // 2):
+    near, far, back, early = [own], [other], [None], None
+    for step in range(1, slabs // 2 + 1):
         near.append(onward(near[-1]))
-        far.append(onward(far[-1]))
-    near.append(onward(near[-1]))
-    back = [None]
-    for first, last in ((1, 4), (4, 6), (6, 8)):
-        back.extend(swap(far[first:last]))
+        if step < slabs // 2:
+            far.append(onward(far[-1]))
+        if step in (3, 5, 7):
+            back.extend(swap(far[len(back) : step + 1]))
+        if step in (4, 6):
+            *back[1:], near[step] = lax.optimization_barrier(
+                tuple(back[1:]) + (near[step],)
+            )
+        if step == 7:
+            early = products(near[5:0:-1] + near[:1] + back[1:6], both, chips)
+            early, near[step] = lax.optimization_barrier((early, near[step]))
+            early = plane_sum(early)
     order = near[::-1] + back[1:]
-    early = plane_sum(order[3:14], both, chips)
-    late = plane_sum(order[:3] + order[14:], both, chips)
+    late = products(order[:3] + order[14:], both, chips)
+    early, late = lax.optimization_barrier((early, late))
+    late = plane_sum(late)
     gram = jnp.concatenate([late[:3], early, late[3:]], 0) / total_cols
     gram = jnp.where(core == 0, gram, gram[::-1])
     gram = turn_to(gram, slabs + slabs // 2 - core - slab)

time: 243 us -> 266 us (1.095)
  matrix products: 13 us -> 27.8 us
  local copies, waits for them, and re-layouts: 12.7 us -> 26.5 us
  starting transfers between devices: 141 us -> 137 us
    unnamed x30 -> x35, local copies, waits for them, and re-layouts: 5.55 us -> 19.9 us
    dot_general x16, matrix products: 7.19 us -> 19.7 us  [nt(): lax.dot_general(left, right, (((1,), (1,)), ((), ())), preferred_element_...]
    ppermute x15, waiting for transfers between devices: 3.44 us -> 13.9 us  [onward(): return lax.ppermute(piece, LINE + ('core',), pairs)]
    all_to_all x2, waiting for transfers between devices: 20.1 us -> 10.6 us  [plane_sum(): return lax.all_to_all(parts, PLANE, 0, 0).sum(0)]
    ppermute x15, starting transfers between devices: 67.5 us -> 60.7 us  [onward(): return lax.ppermute(piece, LINE + ('core',), pairs)]
    ppermute x3, starting transfers between devices: 10.7 us -> 15.6 us  [swap(): return list(lax.ppermute(jnp.stack(pieces), 'core', SWAP))]
    all_to_all x2, starting transfers between devices: 15.5 us -> 11.5 us  [share(): return lax.all_to_all(copies, PLANE, 0, 0)]
    ppermute x1, starting transfers between devices: 1.92 us -> 5.81 us  [per_device(): away = lax.ppermute(away, ('ylo', 'core'), CROSS)]
  transfers between devices with their start and end apart: 31 -> 31, of which waited for: 13 -> 14; matrix products, arithmetic and copies ran while one was open for 8% -> 18% of each run, Pallas kernels for 0% -> 0%
where the time goes in v6:
time: 266 us; the launch traced here: 264 us
  starting transfers between devices  137 us (52%)
  waiting for transfers between devices  50.6 us (19%)
  matrix products  27.8 us (10%)
  local copies, waits for them, and re-layouts  26.5 us (10%)
  blocking collectives  18.4 us (7%)
  other arithmetic  3.53 us (1%)
    ppermute x15, starting transfers between devices, onward(): return lax.ppermute(piece, LINE + ('core',), pairs)  60.7 us
    unnamed x35, local copies, waits for them, and re-layouts  19.9 us
    dot_general x16, matrix products, nt(): lax.dot_general(left, right, (((1,), (1,)), ((), ())), preferred_element_...  19.7 us
    all_gather x1, blocking collectives, per_device(): here = lax.all_gather(gram_low, 'zh', axis=0)  18.4 us
    ppermute x3, starting transfers between devices, swap(): return list(lax.ppermute(jnp.stack(pieces), 'core', SWAP))  15.6 us
    ppermute x15, waiting for transfers between devices, onward(): return lax.ppermute(piece, LINE + ('core',), pairs)  13.9 us
    ppermute x4, starting transfers between devices, along(): return lax.ppermute(piece, LINE, pairs)  13.9 us
    all_to_all x2, starting transfers between devices, plane_sum(): return lax.all_to_all(parts, PLANE, 0, 0).sum(0)  12.9 us
  transfers between devices with their start and end apart: 31, of which 14 were waited for; matrix products, arithmetic and copies ran while one was open for 18% of the time, Pallas kernels for 0%

profile of v6, /device:TPU:1, one launch (start us, length us, event | category | flops | bytes accessed | tf_op | source)
XLA Modules:
  0.0 264.2 jit_solution(10765476205398626857)
XLA Ops:
  0.0 1.1 convert_element_type.24
  1.1 4.6 %collective-permute-start = (bf16[128,1152]{1,0:T(8,128)(2,1)S(1)}, bf16[128,1152]{1,0:T(8,128)(2,1)S(1)}, u32[]{:S(2)}, u32[]{:S(2)}) collective-permute-start(bf16[128,1152]{1,0:T(8,128)(2,1)S(1)} %convert_element_type.24), channel_id=1, source_target_pairs={{0,0},{1,16},{16,1},{17,17},{2,2},{3,18},{18,3},{19,19},{4,4},{5,2... | collective-permute-start | bytes 884744 | tf_op jit(solution)/shard_map/ppermute | solution.py:82
  5.7 4.4 %collective-permute-done = bf16[128,1152]{1,0:T(8,128)(2,1)S(1)} collective-permute-done((bf16[128,1152]{1,0:T(8,128)(2,1)S(1)}, bf16[128,1152]{1,0:T(8,128)(2,1)S(1)}, u32[]{:S(2)}, u32[]{:S(2)}) %collective-permute-start) | collective-permute-done | bytes 294944 | tf_op jit(solution)/shard_map/ppermute | solution.py:82
  10.1 1.9 collective-permute-start.1
  12.0 1.5 collective-permute-done.1
  13.6 11.1 %collective-permute-start.2 = (bf16[128,1152]{1,0:T(8,128)(2,1)S(1)}, bf16[128,1152]{1,0:T(8,128)(2,1)S(1)}, u32[]{:S(2)}, u32[]{:S(2)}) collective-permute-start(bf16[128,1152]{1,0:T(8,128)(2,1)S(1)} %collective-permute-done.1), channel_id=1, source_target_pairs={{0,32},{1,481},{32,64},{33,1},{64,96},{65,33},{96,128},{97,65},{12... | collective-permute-start | bytes 884744 | tf_op jit(solution)/shard_map/ppermute | solution.py:33
  24.7 3.6 %collective-permute-done.2 = bf16[128,1152]{1,0:T(8,128)(2,1)S(1)} collective-permute-done((bf16[128,1152]{1,0:T(8,128)(2,1)S(1)}, bf16[128,1152]{1,0:T(8,128)(2,1)S(1)}, u32[]{:S(2)}, u32[]{:S(2)}) %collective-permute-start.2) | collective-permute-done | bytes 294944 | tf_op jit(solution)/shard_map/ppermute | solution.py:33
  28.3 5.0 %collective-permute-start.3 = (bf16[128,1152]{1,0:T(8,128)(2,1)S(1)}, bf16[128,1152]{1,0:T(8,128)(2,1)S(1)}, u32[]{:S(2)}, u32[]{:S(2)}) collective-permute-start(bf16[128,1152]{1,0:T(8,128)(2,1)S(1)} %collective-permute-done.2), channel_id=1, source_target_pairs={{0,32},{1,481},{32,64},{33,1},{64,96},{65,33},{96,128},{97,65},{12... | collective-permute-start | bytes 884744 | tf_op jit(solution)/shard_map/ppermute | solution.py:33
  33.3 3.6 %collective-permute-done.3 = bf16[128,1152]{1,0:T(8,128)(2,1)S(1)} collective-permute-done((bf16[128,1152]{1,0:T(8,128)(2,1)S(1)}, bf16[128,1152]{1,0:T(8,128)(2,1)S(1)}, u32[]{:S(2)}, u32[]{:S(2)}) %collective-permute-start.3) | collective-permute-done | bytes 294944 | tf_op jit(solution)/shard_map/ppermute | solution.py:33
  37.0 5.0 %collective-permute-start.4 = (bf16[128,1152]{1,0:T(8,128)(2,1)S(1)}, bf16[128,1152]{1,0:T(8,128)(2,1)S(1)}, u32[]{:S(2)}, u32[]{:S(2)}) collective-permute-start(bf16[128,1152]{1,0:T(8,128)(2,1)S(1)} %collective-permute-done.3), channel_id=1, source_target_pairs={{0,32},{1,481},{32,64},{33,1},{64,96},{65,33},{96,128},{97,65},{12... | collective-permute-start | bytes 884744 | tf_op jit(solution)/shard_map/ppermute | solution.py:33
  42.0 1.9 collective-permute-start.6
  43.9 1.7 collective-permute-done.4
  45.8 5.7 %collective-permute-start.5 = (bf16[3,128,1152]{2,1,0:T(8,128)(2,1)S(1)}, bf16[3,128,1152]{2,1,0:T(8,128)(2,1)S(1)}, u32[]{:S(2)}, u32[]{:S(2)}) collective-permute-start(bf16[3,128,1152]{2,1,0:T(8,128)(2,1)S(1)} %pad_maximum_fusion.1), channel_id=1, source_target_pairs={{0,1},{1,0},{2,3},{3,2},{4,5},{5,4},{6,7},{7,6},{8,9},{9,8},{10,11... | collective-permute-start | bytes 2654216 | tf_op jit(solution)/shard_map/ppermute | solution.py:37
  51.5 2.4 collective-permute-start.7
  53.8 1.9 collective-permute-start.11
  55.8 3.5 %collective-permute-done.7 = bf16[128,1152]{1,0:T(8,128)(2,1)S(1)} collective-permute-done((bf16[128,1152]{1,0:T(8,128)(2,1)S(1)}, bf16[128,1152]{1,0:T(8,128)(2,1)S(1)}, u32[]{:S(2)}, u32[]{:S(2)}) %collective-permute-start.7) | collective-permute-done | bytes 294944 | tf_op jit(solution)/shard_map/ppermute | solution.py:33
  59.2 3.3 %collective-permute-start.8 = (bf16[128,1152]{1,0:T(8,128)(2,1)S(1)}, bf16[128,1152]{1,0:T(8,128)(2,1)S(1)}, u32[]{:S(2)}, u32[]{:S(2)}) collective-permute-start(bf16[128,1152]{1,0:T(8,128)(2,1)S(1)} %collective-permute-done.7), channel_id=1, source_target_pairs={{0,32},{1,481},{32,64},{33,1},{64,96},{65,33},{96,128},{97,65},{12... | collective-permute-start | bytes 884744 | tf_op jit(solution)/shard_map/ppermute | solution.py:33
  62.5 3.1 %collective-permute-start.12 = (bf16[128,1152]{1,0:T(8,128)(2,1)S(1)}, bf16[128,1152]{1,0:T(8,128)(2,1)S(1)}, u32[]{:S(2)}, u32[]{:S(2)}) collective-permute-start(bf16[128,1152]{1,0:T(8,128)(2,1)S(1)} %collective-permute-done.11), channel_id=1, source_target_pairs={{0,32},{1,481},{32,64},{33,1},{64,96},{65,33},{96,128},{97,65},{12... | collective-permute-start | bytes 884744 | tf_op jit(solution)/shard_map/ppermute | solution.py:33
  66.7 4.5 %collective-permute-start.9 = (bf16[128,1152]{1,0:T(8,128)(2,1)S(1)}, bf16[128,1152]{1,0:T(8,128)(2,1)S(1)}, u32[]{:S(2)}, u32[]{:S(2)}) collective-permute-start(bf16[128,1152]{1,0:T(8,128)(2,1)S(1)} %collective-permute-done.8), channel_id=1, source_target_pairs={{0,32},{1,481},{32,64},{33,1},{64,96},{65,33},{96,128},{97,65},{12... | collective-permute-start | bytes 884744 | tf_op jit(solution)/shard_map/ppermute | solution.py:33
  71.2 3.1 %collective-permute-start.17 = (bf16[128,1152]{1,0:T(8,128)(2,1)S(1)}, bf16[128,1152]{1,0:T(8,128)(2,1)S(1)}, u32[]{:S(2)}, u32[]{:S(2)}) collective-permute-start(bf16[128,1152]{1,0:T(8,128)(2,1)S(1)} %collective-permute-done.12), channel_id=1, source_target_pairs={{0,32},{1,481},{32,64},{33,1},{64,96},{65,33},{96,128},{97,65},{12... | collective-permute-start | bytes 884744 | tf_op jit(solution)/shard_map/ppermute | solution.py:33
  74.8 5.0 %collective-permute-start.10 = (bf16[128,1152]{1,0:T(8,128)(2,1)S(1)}, bf16[128,1152]{1,0:T(8,128)(2,1)S(1)}, u32[]{:S(2)}, u32[]{:S(2)}) collective-permute-start(bf16[128,1152]{1,0:T(8,128)(2,1)S(1)} %collective-permute-done.9), channel_id=1, source_target_pairs={{0,32},{1,481},{32,64},{33,1},{64,96},{65,33},{96,128},{97,65},{12... | collective-permute-start | bytes 884744 | tf_op jit(solution)/shard_map/ppermute | solution.py:33
  79.9 6.0 %collective-permute-start.13 = (bf16[2,128,1152]{2,1,0:T(8,128)(2,1)S(1)}, bf16[2,128,1152]{2,1,0:T(8,128)(2,1)S(1)}, u32[]{:S(2)}, u32[]{:S(2)}) collective-permute-start(bf16[2,128,1152]{2,1,0:T(8,128)(2,1)S(1)} %pad_maximum_fusion.2), channel_id=1, source_target_pairs={{0,1},{1,0},{2,3},{3,2},{4,5},{5,4},{6,7},{7,6},{8,9},{9,8},{10,11... | collective-permute-start | bytes 1769480 | tf_op jit(solution)/shard_map/ppermute | solution.py:37
  86.0 4.9 %collective-permute-start.18 = (bf16[128,1152]{1,0:T(8,128)(2,1)S(1)}, bf16[128,1152]{1,0:T(8,128)(2,1)S(1)}, u32[]{:S(2)}, u32[]{:S(2)}) collective-permute-start(bf16[128,1152]{1,0:T(8,128)(2,1)S(1)} %collective-permute-done.17), channel_id=1, source_target_pairs={{0,32},{1,481},{32,64},{33,1},{64,96},{65,33},{96,128},{97,65},{12... | collective-permute-start | bytes 884744 | tf_op jit(solution)/shard_map/ppermute | solution.py:33
  90.9 1.9 collective-permute-start.14
  98.9 3.8 %collective-permute-start.15 = (bf16[128,1152]{1,0:T(8,128)(2,1)S(1)}, bf16[128,1152]{1,0:T(8,128)(2,1)}, u32[]{:S(2)}, u32[]{:S(2)}) collective-permute-start(bf16[128,1152]{1,0:T(8,128)(2,1)S(1)} %collective-permute-done.14), channel_id=1, source_target_pairs={{0,32},{1,481},{32,64},{33,1},{64,96},{65,33},{96,128},{97,65},{12... | collective-permute-start | bytes 884744 | tf_op jit(solution)/shard_map/ppermute | solution.py:33
  102.7 1.0 fusion.10
  107.7 3.8 %collective-permute-start.16 = (bf16[128,1152]{1,0:T(8,128)(2,1)}, bf16[128,1152]{1,0:T(8,128)(2,1)}, u32[]{:S(2)}, u32[]{:S(2)}) collective-permute-start(bf16[128,1152]{1,0:T(8,128)(2,1)} %collective-permute-done.15), channel_id=1, source_target_pairs={{0,32},{1,481},{32,64},{33,1},{64,96},{65,33},{96,128},{97,65},{12... | collective-permute-start | bytes 884744 | tf_op jit(solution)/shard_map/ppermute | solution.py:33
  112.4 4.0 %collective-permute-start.19 = (bf16[2,128,1152]{2,1,0:T(8,128)(2,1)}, bf16[2,128,1152]{2,1,0:T(8,128)(2,1)}, u32[]{:S(2)}, u32[]{:S(2)}) collective-permute-start(bf16[2,128,1152]{2,1,0:T(8,128)(2,1)} %pad_maximum_fusion.3), channel_id=1, source_target_pairs={{0,1},{1,0},{2,3},{3,2},{4,5},{5,4},{6,7},{7,6},{8,9},{9,8},{10,11... | collective-permute-start | bytes 1769480 | tf_op jit(solution)/shard_map/ppermute | solution.py:37
  116.4 7.0 %all-to-all-start = ((f32[16,11,8,256]{3,2,1,0:T(8,128)}), f32[16,11,8,256]{3,2,1,0:T(8,128)S(1)}, u32[]{:S(2)}, u32[]{:S(2)}) async-start(f32[16,11,8,256]{3,2,1,0:T(8,128)} %fusion.6), calls=%async_computation | async-start | bytes 2883584 | tf_op jit(solution)/shard_map/all_to_all | solution.py:71
  123.4 1.8 constant_dynamic-update-slice_fusion.17
  125.2 1.7 constant_dynamic-update-slice_fusion.16
  126.9 1.7 constant_dynamic-update-slice_fusion.15
  128.6 1.9 fusion.5
  130.5 1.7 constant_dynamic-update-slice_fusion.14
  132.2 1.7 constant_dynamic-update-slice_fusion.13
  133.9 1.9 fusion.4
  136.9 1.9 fusion.2
  138.8 1.9 fusion.1
  140.8 5.2 %all-to-all-done = f32[16,11,8,256]{3,2,1,0:T(8,128)S(1)} async-done(((f32[16,11,8,256]{3,2,1,0:T(8,128)}), f32[16,11,8,256]{3,2,1,0:T(8,128)S(1)}, u32[]{:S(2)}, u32[]{:S(2)}) %all-to-all-start) | async-done | bytes 1441824 | tf_op jit(solution)/shard_map/all_to_all | solution.py:71
  146.0 2.0 copy.14
  148.0 5.9 %all-to-all-start.1 = ((f32[16,5,8,256]{3,2,1,0:T(8,128)}), f32[16,5,8,256]{3,2,1,0:T(8,128)S(1)}, u32[]{:S(2)}, u32[]{:S(2)}) async-start(f32[16,5,8,256]{3,2,1,0:T(8,128)} %copy.14), calls=%async_computation.1 | async-start | bytes 1310720 | tf_op jit(solution)/shard_map/all_to_all | solution.py:71
  154.0 1.7 constant_dynamic-update-slice_fusion.12
  155.6 1.7 constant_dynamic-update-slice_fusion.11
  157.4 1.7 constant_dynamic-update-slice_fusion.10
  159.1 5.5 %all-to-all-done.1 = f32[16,5,8,256]{3,2,1,0:T(8,128)S(1)} async-done(((f32[16,5,8,256]{3,2,1,0:T(8,128)}), f32[16,5,8,256]{3,2,1,0:T(8,128)S(1)}, u32[]{:S(2)}, u32[]{:S(2)}) %all-to-all-start.1) | async-done | bytes 655392 | tf_op jit(solution)/shard_map/all_to_all | solution.py:71
  164.7 1.1 broadcast_in_dim.14
  165.8 4.7 %all-to-all-start.2 = ((bf16[16,128,256]{2,1,0:T(8,128)(2,1)}), bf16[16,128,256]{2,1,0:T(8,128)(2,1)S(1)}, u32[]{:S(2)}, u32[]{:S(2)}) async-start(bf16[16,128,256]{2,1,0:T(8,128)(2,1)} %broadcast_in_dim.14), calls=%async_computation.2 | async-start | bytes 2097152 | tf_op jit(solution)/shard_map/all_to_all | solution.py:17
  173.5 18.4 %all_gather.3 = bf16[4,128,256]{2,1,0:T(8,128)(2,1)S(1)} all-gather(bf16[1,128,256]{2,1,0:T(8,128)(2,1)S(1)} %get-tuple-element.35), channel_id=1, replica_groups=mesh['zh'=4,'zl'=4,'ylo'=2,'x'=4,'yhi'=2,'core'=2] {'zh'}, dimensions={0}, use_global_device_ids=true | all-gather | bytes 327680 | tf_op jit(solution)/shard_map/all_gather | solution.py:111
  192.3 7.4 %collective-permute-start.24 = (bf16[4,4,128,256]{3,2,1,0:T(8,128)(2,1)S(1)}, bf16[4,4,128,256]{3,2,1,0:T(8,128)(2,1)S(1)}, u32[]{:S(2)}, u32[]{:S(2)}) collective-permute-start(bf16[4,4,128,256]{3,2,1,0:T(8,128)(2,1)S(1)} %pad_maximum_fusion), channel_id=1, source_target_pairs={{0,1},{1,0},{2,3},{3,2},{4,5},{5,4},{6,7},{7,6},{8,9},{9,8},{10,11... | collective-permute-start | bytes 3145736 | tf_op jit(solution)/shard_map/ppermute | solution.py:125
  199.7 1.9 collective-permute-start.23
  201.6 5.5 %collective-permute-start.22 = (bf16[2,128,256]{2,1,0:T(8,128)(2,1)S(1)}, bf16[2,128,256]{2,1,0:T(8,128)(2,1)S(1)}, u32[]{:S(2)}, u32[]{:S(2)}) collective-permute-start(bf16[2,128,256]{2,1,0:T(8,128)(2,1)S(1)} %get-tuple-element.49), channel_id=1, source_target_pairs={{0,448},{32,480},{64,0},{96,32},{128,64},{160,96},{192,128},{224,1... | collective-permute-start | bytes 393224 | tf_op jit(solution)/shard_map/ppermute | solution.py:23
  207.9 2.4 collective-permute-start.21
  210.3 4.0 %collective-permute-start.20 = (bf16[4,128,256]{2,1,0:T(8,128)(2,1)S(1)}, bf16[4,128,256]{2,1,0:T(8,128)(2,1)S(1)}, u32[]{:S(2)}, u32[]{:S(2)}) collective-permute-start(bf16[4,128,256]{2,1,0:T(8,128)(2,1)S(1)} %all_gather.3), channel_id=1, source_target_pairs={{0,480},{32,0},{64,32},{96,64},{128,96},{160,128},{192,160},{224,1... | collective-permute-start | bytes 786440 | tf_op jit(solution)/shard_map/ppermute | solution.py:23
  214.8 3.4 %collective-permute-done.21 = bf16[4,128,256]{2,1,0:T(8,128)(2,1)S(1)} collective-permute-done((bf16[4,128,256]{2,1,0:T(8,128)(2,1)S(1)}, bf16[4,128,256]{2,1,0:T(8,128)(2,1)S(1)}, u32[]{:S(2)}, u32[]{:S(2)}) %collective-permute-start.21) | collective-permute-done | bytes 262176 | tf_op jit(solution)/shard_map/ppermute | solution.py:23
  220.1 1.1 broadcast_in_dim.15
  221.2 6.9 %all-to-all-start.3 = ((bf16[16,16,8,256]{3,2,1,0:T(8,128)(2,1)}), bf16[16,16,8,256]{3,2,1,0:T(8,128)(2,1)S(1)}, u32[]{:S(2)}, u32[]{:S(2)}) async-start(bf16[16,16,8,256]{3,2,1,0:T(8,128)(2,1)} %broadcast_in_dim.15), calls=%async_computation.3 | async-start | bytes 2097152 | tf_op jit(solution)/shard_map/all_to_all | solution.py:17
  228.8 1.7 bitcast_dynamic-update-slice_fusion.1
  230.5 1.7 bitcast_dynamic-update-slice_fusion
  232.2 10.7 %all-to-all-done.3 = bf16[16,16,8,256]{3,2,1,0:T(8,128)(2,1)S(1)} async-done(((bf16[16,16,8,256]{3,2,1,0:T(8,128)(2,1)}), bf16[16,16,8,256]{3,2,1,0:T(8,128)(2,1)S(1)}, u32[]{:S(2)}, u32[]{:S(2)}) %all-to-all-start.3) | async-done | bytes 1048608 | tf_op jit(solution)/shard_map/all_to_all | solution.py:17
  243.0 3.2 %convolution_convert_fusion = bf16[128,1152]{1,0:T(8,128)(2,1)S(1)} fusion(bf16[2048,1152]{1,0:T(8,128)(2,1)} %bitcast_dynamic-update-slice_fusion, bf16[2048,256]{1,0:T(8,128)(2,1)S(1)} %bitcast.247), kind=kOutput, calls=%fused_computation.2 | convolution fusion | flops 604127232 | bytes 5537792 | tf_op jit(solution)/shard_map/dot_general | solution.py:53
  246.2 5.8 %collective-permute-start.26 = (bf16[128,1152]{1,0:T(8,128)(2,1)S(1)}, bf16[128,1152]{1,0:T(8,128)(2,1)S(1)}, u32[]{:S(2)}, u32[]{:S(2)}) collective-permute-start(bf16[128,1152]{1,0:T(8,128)(2,1)S(1)} %convolution_convert_fusion), channel_id=1, source_target_pairs={{0,16},{1,0},{16,17},{17,1},{2,18},{3,2},{18,19},{19,3},{4,20},{5,... | collective-permute-start | bytes 884744 | tf_op jit(solution)/shard_map/ppermute | solution.py:141
  252.0 3.2 %fusion = bf16[128,1152]{1,0:T(8,128)(2,1)S(1)} fusion(bf16[2048,1152]{1,0:T(8,128)(2,1)} %bitcast_dynamic-update-slice_fusion, bf16[128,1152]{1,0:T(8,128)(2,1)S(1)} %collective-permute-done, bf16[2048,256]{1,0:T(8,128)(2,1)S(1)} %bitcast.248), kind=kOutput, calls=%fused_computation.1 | convolution fusion | flops 604569600 | bytes 5832704 | tf_op jit(solution)/shard_map/dot_general | solution.py:53
  255.3 2.1 collective-permute-start.25
  257.4 5.9 %collective-permute-done.25 = bf16[128,1152]{1,0:T(8,128)(2,1)S(1)} collective-permute-done((bf16[128,1152]{1,0:T(8,128)(2,1)S(1)}, bf16[128,1152]{1,0:T(8,128)(2,1)S(1)}, u32[]{:S(2)}, u32[]{:S(2)}) %collective-permute-start.25) | collective-permute-done | bytes 294944 | tf_op jit(solution)/shard_map/ppermute | solution.py:143
  (89 shorter events, 21.8 us)
Async XLA Ops:
  1.1 9.0 %collective-permute-start = (bf16[128,1152]{1,0:T(8,128)(2,1)S(1)}, bf16[128,1152]{1,0:T(8,128)(2,1)S(1)}, u32[]{:S(2)}, u32[]{:S(2)}) collective-permute-start(bf16[128,1152]{1,0:T(8,128)(2,1)S(1)} %convert_element_type.24), channel_id=1, source_target_pairs={{0,0},{1,16},{16,1},{17,17},{2,2},{3,18},{18,3},{19,19},{4,4},{5,2... | collective-permute-start | bytes 884744 | tf_op jit(solution)/shard_map/ppermute | solution.py:82
  10.1 3.5 %collective-permute-start.1 = (bf16[128,1152]{1,0:T(8,128)(2,1)S(1)}, bf16[128,1152]{1,0:T(8,128)(2,1)S(1)}, u32[]{:S(2)}, u32[]{:S(2)}) collective-permute-start(bf16[128,1152]{1,0:T(8,128)(2,1)S(1)} %collective-permute-done), channel_id=1, source_target_pairs={{0,1},{1,0},{2,3},{3,2},{4,5},{5,4},{6,7},{7,6},{8,9},{9,8},{10,11... | collective-permute-start | bytes 884744 | tf_op jit(solution)/shard_map/ppermute | solution.py:83
  13.6 14.8 %collective-permute-start.2 = (bf16[128,1152]{1,0:T(8,128)(2,1)S(1)}, bf16[128,1152]{1,0:T(8,128)(2,1)S(1)}, u32[]{:S(2)}, u32[]{:S(2)}) collective-permute-start(bf16[128,1152]{1,0:T(8,128)(2,1)S(1)} %collective-permute-done.1), channel_id=1, source_target_pairs={{0,32},{1,481},{32,64},{33,1},{64,96},{65,33},{96,128},{97,65},{12... | collective-permute-start | bytes 884744 | tf_op jit(solution)/shard_map/ppermute | solution.py:33
  28.3 8.7 %collective-permute-start.3 = (bf16[128,1152]{1,0:T(8,128)(2,1)S(1)}, bf16[128,1152]{1,0:T(8,128)(2,1)S(1)}, u32[]{:S(2)}, u32[]{:S(2)}) collective-permute-start(bf16[128,1152]{1,0:T(8,128)(2,1)S(1)} %collective-permute-done.2), channel_id=1, source_target_pairs={{0,32},{1,481},{32,64},{33,1},{64,96},{65,33},{96,128},{97,65},{12... | collective-permute-start | bytes 884744 | tf_op jit(solution)/shard_map/ppermute | solution.py:33
  37.0 8.7 %collective-permute-start.4 = (bf16[128,1152]{1,0:T(8,128)(2,1)S(1)}, bf16[128,1152]{1,0:T(8,128)(2,1)S(1)}, u32[]{:S(2)}, u32[]{:S(2)}) collective-permute-start(bf16[128,1152]{1,0:T(8,128)(2,1)S(1)} %collective-permute-done.3), channel_id=1, source_target_pairs={{0,32},{1,481},{32,64},{33,1},{64,96},{65,33},{96,128},{97,65},{12... | collective-permute-start | bytes 884744 | tf_op jit(solution)/shard_map/ppermute | solution.py:33
  42.0 9.4 %collective-permute-start.6 = (bf16[128,1152]{1,0:T(8,128)(2,1)S(1)}, bf16[128,1152]{1,0:T(8,128)(2,1)S(1)}, u32[]{:S(2)}, u32[]{:S(2)}) collective-permute-start(bf16[128,1152]{1,0:T(8,128)(2,1)S(1)} %collective-permute-done), channel_id=1, source_target_pairs={{0,32},{1,481},{32,64},{33,1},{64,96},{65,33},{96,128},{97,65},{12... | collective-permute-start | bytes 884744 | tf_op jit(solution)/shard_map/ppermute | solution.py:33
  45.8 28.6 %collective-permute-start.5 = (bf16[3,128,1152]{2,1,0:T(8,128)(2,1)S(1)}, bf16[3,128,1152]{2,1,0:T(8,128)(2,1)S(1)}, u32[]{:S(2)}, u32[]{:S(2)}) collective-permute-start(bf16[3,128,1152]{2,1,0:T(8,128)(2,1)S(1)} %pad_maximum_fusion.1), channel_id=1, source_target_pairs={{0,1},{1,0},{2,3},{3,2},{4,5},{5,4},{6,7},{7,6},{8,9},{9,8},{10,11... | collective-permute-start | bytes 2654216 | tf_op jit(solution)/shard_map/ppermute | solution.py:37
  51.5 46.4 %copy-start.2 = (bf16[128,1152]{1,0:T(8,128)(2,1)}, bf16[128,1152]{1,0:T(8,128)(2,1)S(1)}, u32[]{:S(2)}) copy-start(bf16[128,1152]{1,0:T(8,128)(2,1)S(1)} %collective-permute-done.6) | copy-start | bytes 884740
  51.5 7.8 %collective-permute-start.7 = (bf16[128,1152]{1,0:T(8,128)(2,1)S(1)}, bf16[128,1152]{1,0:T(8,128)(2,1)S(1)}, u32[]{:S(2)}, u32[]{:S(2)}) collective-permute-start(bf16[128,1152]{1,0:T(8,128)(2,1)S(1)} %collective-permute-done.6), channel_id=1, source_target_pairs={{0,32},{1,481},{32,64},{33,1},{64,96},{65,33},{96,128},{97,65},{12... | collective-permute-start | bytes 884744 | tf_op jit(solution)/shard_map/ppermute | solution.py:33
  53.8 8.7 %collective-permute-start.11 = (bf16[128,1152]{1,0:T(8,128)(2,1)S(1)}, bf16[128,1152]{1,0:T(8,128)(2,1)S(1)}, u32[]{:S(2)}, u32[]{:S(2)}) collective-permute-start(bf16[128,1152]{1,0:T(8,128)(2,1)S(1)} %collective-permute-done.4), channel_id=1, source_target_pairs={{0,32},{1,481},{32,64},{33,1},{64,96},{65,33},{96,128},{97,65},{12... | collective-permute-start | bytes 884744 | tf_op jit(solution)/shard_map/ppermute | solution.py:33
  59.2 38.6 %copy-start.3 = (bf16[128,1152]{1,0:T(8,128)(2,1)}, bf16[128,1152]{1,0:T(8,128)(2,1)S(1)}, u32[]{:S(2)}) copy-start(bf16[128,1152]{1,0:T(8,128)(2,1)S(1)} %collective-permute-done.7) | copy-start | bytes 884740
  59.2 7.5 %collective-permute-start.8 = (bf16[128,1152]{1,0:T(8,128)(2,1)S(1)}, bf16[128,1152]{1,0:T(8,128)(2,1)S(1)}, u32[]{:S(2)}, u32[]{:S(2)}) collective-permute-start(bf16[128,1152]{1,0:T(8,128)(2,1)S(1)} %collective-permute-done.7), channel_id=1, source_target_pairs={{0,32},{1,481},{32,64},{33,1},{64,96},{65,33},{96,128},{97,65},{12... | collective-permute-start | bytes 884744 | tf_op jit(solution)/shard_map/ppermute | solution.py:33
  62.5 8.7 %collective-permute-start.12 = (bf16[128,1152]{1,0:T(8,128)(2,1)S(1)}, bf16[128,1152]{1,0:T(8,128)(2,1)S(1)}, u32[]{:S(2)}, u32[]{:S(2)}) collective-permute-start(bf16[128,1152]{1,0:T(8,128)(2,1)S(1)} %collective-permute-done.11), channel_id=1, source_target_pairs={{0,32},{1,481},{32,64},{33,1},{64,96},{65,33},{96,128},{97,65},{12... | collective-permute-start | bytes 884744 | tf_op jit(solution)/shard_map/ppermute | solution.py:33
  66.7 31.2 %copy-start.4 = (bf16[128,1152]{1,0:T(8,128)(2,1)}, bf16[128,1152]{1,0:T(8,128)(2,1)S(1)}, u32[]{:S(2)}) copy-start(bf16[128,1152]{1,0:T(8,128)(2,1)S(1)} %collective-permute-done.8) | copy-start | bytes 884740
  66.7 8.1 %collective-permute-start.9 = (bf16[128,1152]{1,0:T(8,128)(2,1)S(1)}, bf16[128,1152]{1,0:T(8,128)(2,1)S(1)}, u32[]{:S(2)}, u32[]{:S(2)}) collective-permute-start(bf16[128,1152]{1,0:T(8,128)(2,1)S(1)} %collective-permute-done.8), channel_id=1, source_target_pairs={{0,32},{1,481},{32,64},{33,1},{64,96},{65,33},{96,128},{97,65},{12... | collective-permute-start | bytes 884744 | tf_op jit(solution)/shard_map/ppermute | solution.py:33
  71.2 14.8 %collective-permute-start.17 = (bf16[128,1152]{1,0:T(8,128)(2,1)S(1)}, bf16[128,1152]{1,0:T(8,128)(2,1)S(1)}, u32[]{:S(2)}, u32[]{:S(2)}) collective-permute-start(bf16[128,1152]{1,0:T(8,128)(2,1)S(1)} %collective-permute-done.12), channel_id=1, source_target_pairs={{0,32},{1,481},{32,64},{33,1},{64,96},{65,33},{96,128},{97,65},{12... | collective-permute-start | bytes 884744 | tf_op jit(solution)/shard_map/ppermute | solution.py:33
  74.8 20.0 %copy-start.5 = (bf16[128,1152]{1,0:T(8,128)(2,1)}, bf16[128,1152]{1,0:T(8,128)(2,1)S(1)}, u32[]{:S(2)}) copy-start(bf16[128,1152]{1,0:T(8,128)(2,1)S(1)} %collective-permute-done.9) | copy-start | bytes 884740
  74.8 16.0 %collective-permute-start.10 = (bf16[128,1152]{1,0:T(8,128)(2,1)S(1)}, bf16[128,1152]{1,0:T(8,128)(2,1)S(1)}, u32[]{:S(2)}, u32[]{:S(2)}) collective-permute-start(bf16[128,1152]{1,0:T(8,128)(2,1)S(1)} %collective-permute-done.9), channel_id=1, source_target_pairs={{0,32},{1,481},{32,64},{33,1},{64,96},{65,33},{96,128},{97,65},{12... | collective-permute-start | bytes 884744 | tf_op jit(solution)/shard_map/ppermute | solution.py:33
  79.9 14.9 %collective-permute-start.13 = (bf16[2,128,1152]{2,1,0:T(8,128)(2,1)S(1)}, bf16[2,128,1152]{2,1,0:T(8,128)(2,1)S(1)}, u32[]{:S(2)}, u32[]{:S(2)}) collective-permute-start(bf16[2,128,1152]{2,1,0:T(8,128)(2,1)S(1)} %pad_maximum_fusion.2), channel_id=1, source_target_pairs={{0,1},{1,0},{2,3},{3,2},{4,5},{5,4},{6,7},{7,6},{8,9},{9,8},{10,11... | collective-permute-start | bytes 1769480 | tf_op jit(solution)/shard_map/ppermute | solution.py:37
  86.0 25.6 %collective-permute-start.18 = (bf16[128,1152]{1,0:T(8,128)(2,1)S(1)}, bf16[128,1152]{1,0:T(8,128)(2,1)S(1)}, u32[]{:S(2)}, u32[]{:S(2)}) collective-permute-start(bf16[128,1152]{1,0:T(8,128)(2,1)S(1)} %collective-permute-done.17), channel_id=1, source_target_pairs={{0,32},{1,481},{32,64},{33,1},{64,96},{65,33},{96,128},{97,65},{12... | collective-permute-start | bytes 884744 | tf_op jit(solution)/shard_map/ppermute | solution.py:33
  90.9 14.8 %copy-start.6 = (bf16[128,1152]{1,0:T(8,128)(2,1)}, bf16[128,1152]{1,0:T(8,128)(2,1)S(1)}, u32[]{:S(2)}) copy-start(bf16[128,1152]{1,0:T(8,128)(2,1)S(1)} %collective-permute-done.10) | copy-start | bytes 884740
  90.9 8.0 %collective-permute-start.14 = (bf16[128,1152]{1,0:T(8,128)(2,1)S(1)}, bf16[128,1152]{1,0:T(8,128)(2,1)S(1)}, u32[]{:S(2)}, u32[]{:S(2)}) collective-permute-start(bf16[128,1152]{1,0:T(8,128)(2,1)S(1)} %collective-permute-done.10), channel_id=1, source_target_pairs={{0,32},{1,481},{32,64},{33,1},{64,96},{65,33},{96,128},{97,65},{12... | collective-permute-start | bytes 884744 | tf_op jit(solution)/shard_map/ppermute | solution.py:33
  94.9 17.6 %copy-start = (bf16[128,1152]{1,0:T(8,128)(2,1)}, bf16[128,1152]{1,0:T(8,128)(2,1)S(1)}, u32[]{:S(2)}) copy-start(bf16[128,1152]{1,0:T(8,128)(2,1)S(1)} %get-tuple-element.27) | copy-start | bytes 884740
  98.9 7.8 %copy-start.7 = (bf16[128,1152]{1,0:T(8,128)(2,1)}, bf16[128,1152]{1,0:T(8,128)(2,1)S(1)}, u32[]{:S(2)}) copy-start(bf16[128,1152]{1,0:T(8,128)(2,1)S(1)} %collective-permute-done.14) | copy-start | bytes 884740
  98.9 8.8 %collective-permute-start.15 = (bf16[128,1152]{1,0:T(8,128)(2,1)S(1)}, bf16[128,1152]{1,0:T(8,128)(2,1)}, u32[]{:S(2)}, u32[]{:S(2)}) collective-permute-start(bf16[128,1152]{1,0:T(8,128)(2,1)S(1)} %collective-permute-done.14), channel_id=1, source_target_pairs={{0,32},{1,481},{32,64},{33,1},{64,96},{65,33},{96,128},{97,65},{12... | collective-permute-start | bytes 884744 | tf_op jit(solution)/shard_map/ppermute | solution.py:33
  107.7 15.7 %collective-permute-start.16 = (bf16[128,1152]{1,0:T(8,128)(2,1)}, bf16[128,1152]{1,0:T(8,128)(2,1)}, u32[]{:S(2)}, u32[]{:S(2)}) collective-permute-start(bf16[128,1152]{1,0:T(8,128)(2,1)} %collective-permute-done.15), channel_id=1, source_target_pairs={{0,32},{1,481},{32,64},{33,1},{64,96},{65,33},{96,128},{97,65},{12... | collective-permute-start | bytes 884744 | tf_op jit(solution)/shard_map/ppermute | solution.py:33
  112.4 24.4 %collective-permute-start.19 = (bf16[2,128,1152]{2,1,0:T(8,128)(2,1)}, bf16[2,128,1152]{2,1,0:T(8,128)(2,1)}, u32[]{:S(2)}, u32[]{:S(2)}) collective-permute-start(bf16[2,128,1152]{2,1,0:T(8,128)(2,1)} %pad_maximum_fusion.3), channel_id=1, source_target_pairs={{0,1},{1,0},{2,3},{3,2},{4,5},{5,4},{6,7},{7,6},{8,9},{9,8},{10,11... | collective-permute-start | bytes 1769480 | tf_op jit(solution)/shard_map/ppermute | solution.py:37
  116.4 29.5 %all-to-all-start = ((f32[16,11,8,256]{3,2,1,0:T(8,128)}), f32[16,11,8,256]{3,2,1,0:T(8,128)S(1)}, u32[]{:S(2)}, u32[]{:S(2)}) async-start(f32[16,11,8,256]{3,2,1,0:T(8,128)} %fusion.6), calls=%async_computation | async-start | bytes 2883584 | tf_op jit(solution)/shard_map/all_to_all | solution.py:71
  123.4 12.5 %copy-start.8 = (bf16[128,1152]{1,0:T(8,128)(2,1)S(1)}, bf16[128,1152]{1,0:T(8,128)(2,1)}, u32[]{:S(2)}) copy-start(bf16[128,1152]{1,0:T(8,128)(2,1)} %copy-done.7) | copy-start | bytes 884740
  148.0 16.5 %all-to-all-start.1 = ((f32[16,5,8,256]{3,2,1,0:T(8,128)}), f32[16,5,8,256]{3,2,1,0:T(8,128)S(1)}, u32[]{:S(2)}, u32[]{:S(2)}) async-start(f32[16,5,8,256]{3,2,1,0:T(8,128)} %copy.14), calls=%async_computation.1 | async-start | bytes 1310720 | tf_op jit(solution)/shard_map/all_to_all | solution.py:71
  165.8 26.1 %all-to-all-start.2 = ((bf16[16,128,256]{2,1,0:T(8,128)(2,1)}), bf16[16,128,256]{2,1,0:T(8,128)(2,1)S(1)}, u32[]{:S(2)}, u32[]{:S(2)}) async-start(bf16[16,128,256]{2,1,0:T(8,128)(2,1)} %broadcast_in_dim.14), calls=%async_computation.2 | async-start | bytes 2097152 | tf_op jit(solution)/shard_map/all_to_all | solution.py:17
  170.5 36.6 %copy-start.1 = (bf16[128,1152]{1,0:T(8,128)(2,1)S(1)}, bf16[128,1152]{1,0:T(8,128)(2,1)}, u32[]{:S(2)}) copy-start(bf16[128,1152]{1,0:T(8,128)(2,1)} %copy-done) | copy-start | bytes 884740
  192.3 26.2 %collective-permute-start.24 = (bf16[4,4,128,256]{3,2,1,0:T(8,128)(2,1)S(1)}, bf16[4,4,128,256]{3,2,1,0:T(8,128)(2,1)S(1)}, u32[]{:S(2)}, u32[]{:S(2)}) collective-permute-start(bf16[4,4,128,256]{3,2,1,0:T(8,128)(2,1)S(1)} %pad_maximum_fusion), channel_id=1, source_target_pairs={{0,1},{1,0},{2,3},{3,2},{4,5},{5,4},{6,7},{7,6},{8,9},{9,8},{10,11... | collective-permute-start | bytes 3145736 | tf_op jit(solution)/shard_map/ppermute | solution.py:125
  199.7 14.7 %collective-permute-start.23 = (bf16[2,128,256]{2,1,0:T(8,128)(2,1)S(1)}, bf16[2,128,256]{2,1,0:T(8,128)(2,1)S(1)}, u32[]{:S(2)}, u32[]{:S(2)}) collective-permute-start(bf16[2,128,256]{2,1,0:T(8,128)(2,1)S(1)} %get-tuple-element.48), channel_id=1, source_target_pairs={{0,64},{32,96},{64,128},{96,160},{128,192},{160,224},{192,256},{22... | collective-permute-start | bytes 393224 | tf_op jit(solution)/shard_map/ppermute | solution.py:23
  201.6 12.7 %collective-permute-start.22 = (bf16[2,128,256]{2,1,0:T(8,128)(2,1)S(1)}, bf16[2,128,256]{2,1,0:T(8,128)(2,1)S(1)}, u32[]{:S(2)}, u32[]{:S(2)}) collective-permute-start(bf16[2,128,256]{2,1,0:T(8,128)(2,1)S(1)} %get-tuple-element.49), channel_id=1, source_target_pairs={{0,448},{32,480},{64,0},{96,32},{128,64},{160,96},{192,128},{224,1... | collective-permute-start | bytes 393224 | tf_op jit(solution)/shard_map/ppermute | solution.py:23
  207.9 10.4 %collective-permute-start.21 = (bf16[4,128,256]{2,1,0:T(8,128)(2,1)S(1)}, bf16[4,128,256]{2,1,0:T(8,128)(2,1)S(1)}, u32[]{:S(2)}, u32[]{:S(2)}) collective-permute-start(bf16[4,128,256]{2,1,0:T(8,128)(2,1)S(1)} %all_gather.3), channel_id=1, source_target_pairs={{0,32},{32,64},{64,96},{96,128},{128,160},{160,192},{192,224},{224... | collective-permute-start | bytes 786440 | tf_op jit(solution)/shard_map/ppermute | solution.py:23
  210.3 9.2 %collective-permute-start.20 = (bf16[4,128,256]{2,1,0:T(8,128)(2,1)S(1)}, bf16[4,128,256]{2,1,0:T(8,128)(2,1)S(1)}, u32[]{:S(2)}, u32[]{:S(2)}) collective-permute-start(bf16[4,128,256]{2,1,0:T(8,128)(2,1)S(1)} %all_gather.3), channel_id=1, source_target_pairs={{0,480},{32,0},{64,32},{96,64},{128,96},{160,128},{192,160},{224,1... | collective-permute-start | bytes 786440 | tf_op jit(solution)/shard_map/ppermute | solution.py:23
  221.2 21.7 %all-to-all-start.3 = ((bf16[16,16,8,256]{3,2,1,0:T(8,128)(2,1)}), bf16[16,16,8,256]{3,2,1,0:T(8,128)(2,1)S(1)}, u32[]{:S(2)}, u32[]{:S(2)}) async-start(bf16[16,16,8,256]{3,2,1,0:T(8,128)(2,1)} %broadcast_in_dim.15), calls=%async_computation.3 | async-start | bytes 2097152 | tf_op jit(solution)/shard_map/all_to_all | solution.py:17
  246.2 11.2 %collective-permute-start.26 = (bf16[128,1152]{1,0:T(8,128)(2,1)S(1)}, bf16[128,1152]{1,0:T(8,128)(2,1)S(1)}, u32[]{:S(2)}, u32[]{:S(2)}) collective-permute-start(bf16[128,1152]{1,0:T(8,128)(2,1)S(1)} %convolution_convert_fusion), channel_id=1, source_target_pairs={{0,16},{1,0},{16,17},{17,1},{2,18},{3,2},{18,19},{19,3},{4,20},{5,... | collective-permute-start | bytes 884744 | tf_op jit(solution)/shard_map/ppermute | solution.py:141
  255.3 8.0 %collective-permute-start.25 = (bf16[128,1152]{1,0:T(8,128)(2,1)S(1)}, bf16[128,1152]{1,0:T(8,128)(2,1)S(1)}, u32[]{:S(2)}, u32[]{:S(2)}) collective-permute-start(bf16[128,1152]{1,0:T(8,128)(2,1)S(1)} %fusion), channel_id=1, source_target_pairs={{0,0},{1,16},{16,1},{17,17},{2,2},{3,18},{18,3},{19,19},{4,4},{5,2... | collective-permute-start | bytes 884744 | tf_op jit(solution)/shard_map/ppermute | solution.py:143

commit v7 on v5

--- a/solution.py
+++ b/solution.py
@@ -23,12 +23,12 @@
     return lax.ppermute(piece, LINE, pairs)
 
 
-def onward(piece):
+def onward(piece, cores=(0, 1)):
     size = lax.axis_size(LINE)
     pairs = [
         (2 * place + core, 2 * ((place + 1 - 2 * core) % size) + core)
         for place in range(size)
-        for core in range(2)
+        for core in cores
     ]
     return lax.ppermute(piece, LINE + ("core",), pairs)
 
@@ -62,12 +62,6 @@
     )
 
 
-def plane_sum(blocks, both, chips):
-    parts = jnp.stack([nt(block, both) for block in blocks])
-    parts = parts.reshape(len(blocks), chips, -1, parts.shape[-1])
-    return lax.all_to_all(parts.transpose(1, 0, 2, 3), PLANE, 0, 0).sum(0)
-
-
 def per_device(iterate):
     rounded = iterate.astype(jnp.bfloat16)
     rows, cols = rounded.shape
@@ -83,14 +77,13 @@
     for step in range(1, slabs // 2):
         near.append(onward(near[-1]))
         far.append(onward(far[-1]))
-    near.append(onward(near[-1]))
-    back = [None]
-    for first, last in ((1, 4), (4, 6), (6, 8)):
-        back.extend(swap(far[first:last]))
-    order = near[::-1] + back[1:]
-    early = plane_sum(order[3:14], both, chips)
-    late = plane_sum(order[:3] + order[14:], both, chips)
-    gram = jnp.concatenate([late[:3], early, late[3:]], 0) / total_cols
+    near_last, far_last = onward(near[-1], (1,)), onward(far[-1], (1,))
+    back = swap(far[1:5]) + swap(far[5:])
+    (back_last,) = swap([far_last])
+    last = jnp.where(core == 0, back_last, near_last)
+    half = jnp.concatenate([last] + near[::-1] + back, 0)
+    gram = nt(half, both).reshape(slabs, chips, rows // chips, 2 * rows)
+    gram = lax.all_to_all(gram.transpose(1, 0, 2, 3), PLANE, 0, 0).sum(0) / total_cols
     gram = jnp.where(core == 0, gram, gram[::-1])
     gram = turn_to(gram, slabs + slabs // 2 - core - slab)
     gram_low = gram.astype(jnp.bfloat16)
@@ -125,7 +118,6 @@
     poly = turn_to(poly, slabs // 2 + slab + core)
     poly = jnp.where(core == 0, poly, poly[::-1])
     panel = share(poly, chips).transpose(1, 0, 2, 3).reshape(slabs * rows, 2 * rows)
-    half = jnp.concatenate(order, 0)
     away = tn(panel[:, rows:], half).astype(jnp.bfloat16)
     away = lax.ppermute(away, ("ylo", "core"), CROSS)
     stay = tn(panel[:, :rows], half) + 3.4445 * own.astype(jnp.float32)

time: 243 us -> 239 us (0.984)
  blocking collectives: 18.7 us -> 41.1 us
  starting transfers between devices: 141 us -> 127 us
  matrix products: 13 us -> 4.95 us
  local copies, waits for them, and re-layouts: 12.7 us -> 6.95 us
  waiting for transfers between devices: 51.8 us -> 54.9 us
    all_to_all x0 -> x1, blocking collectives: none -> 22.4 us  [share(): return lax.all_to_all(copies, PLANE, 0, 0)]
    all_to_all x2 -> x1, waiting for transfers between devices: 14 us -> 0.01 us  [share(): return lax.all_to_all(copies, PLANE, 0, 0)]
    all_to_all x2 -> x1, waiting for transfers between devices: 20.1 us -> 33.2 us  [per_device(): lax.all_to_all(gram.transpose(1, 0, 2, 3), PLANE, 0, 0).sum(0) / total_cols]
    all_to_all x2 -> x1, starting transfers between devices: 15.5 us -> 4.81 us  [share(): return lax.all_to_all(copies, PLANE, 0, 0)]
    dot_general x16 -> x1, matrix products: 7.19 us -> 1.6 us  [nt(): lax.dot_general(left, right, (((1,), (1,)), ((), ())), preferred_element_...]
    ppermute x15 -> x16, starting transfers between devices: 67.5 us -> 71.3 us  [onward(): return lax.ppermute(piece, LINE + ('core',), pairs)]
    transpose x2 -> x0, local copies, waits for them, and re-layouts: 3.58 us -> none  [plane_sum(): return lax.all_to_all(parts.transpose(1, 0, 2, 3), PLANE, 0, 0).sum(0)]
    all_to_all x2 -> x1, starting transfers between devices: 10.3 us -> 7 us  [per_device(): lax.all_to_all(gram.transpose(1, 0, 2, 3), PLANE, 0, 0).sum(0) / total_cols]
  transfers between devices with their start and end apart: 31 -> 30, of which waited for: 13 -> 15; matrix products, arithmetic and copies ran while one was open for 8% -> 2% of each run, Pallas kernels for 0% -> 0%
where the time goes in v7:
time: 239 us; the launch traced here: 238 us
  starting transfers between devices  127 us (53%)
  waiting for transfers between devices  54.9 us (23%)
  blocking collectives  41.1 us (17%)
  local copies, waits for them, and re-layouts  6.95 us (3%)
  matrix products  4.95 us (2%)
  other arithmetic  2.84 us (1%)
    ppermute x16, starting transfers between devices, onward(): return lax.ppermute(piece, LINE + ('core',), pairs)  71.3 us
    all_to_all x1, waiting for transfers between devices, per_device(): lax.all_to_all(gram.transpose(1, 0, 2, 3), PLANE, 0, 0).sum(0) / total_cols  33.2 us
    all_to_all x1, blocking collectives, share(): return lax.all_to_all(copies, PLANE, 0, 0)  22.4 us
    all_gather x1, blocking collectives, per_device(): here = lax.all_gather(gram_low, 'zh', axis=0)  18.6 us
    ppermute x4, starting transfers between devices, along(): return lax.ppermute(piece, LINE, pairs)  12.7 us
    ppermute x3, starting transfers between devices, swap(): return list(lax.ppermute(jnp.stack(pieces), 'core', SWAP))  10.3 us
    ppermute x1, starting transfers between devices, per_device(): right_other = lax.ppermute(jnp.stack(right_own), 'core', SWAP)  7.44 us
    all_to_all x1, starting transfers between devices, per_device(): lax.all_to_all(gram.transpose(1, 0, 2, 3), PLANE, 0, 0).sum(0) / total_cols  7 us
  transfers between devices with their start and end apart: 30, of which 15 were waited for; matrix products, arithmetic and copies ran while one was open for 2% of the time, Pallas kernels for 0%

profile of v7, /device:TPU:1, one launch (start us, length us, event | category | flops | bytes accessed | tf_op | source)
XLA Modules:
  0.0 238.1 jit_solution(7418888405808321290)
XLA Ops:
  0.0 1.1 convert_element_type.24
  1.1 4.6 %collective-permute-start = (bf16[128,1152]{1,0:T(8,128)(2,1)S(1)}, bf16[128,1152]{1,0:T(8,128)(2,1)S(1)}, u32[]{:S(2)}, u32[]{:S(2)}) collective-permute-start(bf16[128,1152]{1,0:T(8,128)(2,1)S(1)} %convert_element_type.24), channel_id=1, source_target_pairs={{0,0},{1,16},{16,1},{17,17},{2,2},{3,18},{18,3},{19,19},{4,4},{5,2... | collective-permute-start | bytes 884744 | tf_op jit(solution)/shard_map/ppermute | solution.py:73
  5.7 4.4 %collective-permute-done = bf16[128,1152]{1,0:T(8,128)(2,1)S(1)} collective-permute-done((bf16[128,1152]{1,0:T(8,128)(2,1)S(1)}, bf16[128,1152]{1,0:T(8,128)(2,1)S(1)}, u32[]{:S(2)}, u32[]{:S(2)}) %collective-permute-start) | collective-permute-done | bytes 294944 | tf_op jit(solution)/shard_map/ppermute | solution.py:73
  10.1 1.9 collective-permute-start.1
  12.0 1.5 collective-permute-done.1
  13.6 11.1 %collective-permute-start.2 = (bf16[128,1152]{1,0:T(8,128)(2,1)S(1)}, bf16[128,1152]{1,0:T(8,128)(2,1)S(1)}, u32[]{:S(2)}, u32[]{:S(2)}) collective-permute-start(bf16[128,1152]{1,0:T(8,128)(2,1)S(1)} %collective-permute-done.1), channel_id=1, source_target_pairs={{0,32},{1,481},{32,64},{33,1},{64,96},{65,33},{96,128},{97,65},{12... | collective-permute-start | bytes 884744 | tf_op jit(solution)/shard_map/ppermute | solution.py:33
  24.7 2.6 %collective-permute-start.11 = (bf16[128,1152]{1,0:T(8,128)(2,1)S(1)}, bf16[128,1152]{1,0:T(8,128)(2,1)S(1)}, u32[]{:S(2)}, u32[]{:S(2)}) collective-permute-start(bf16[128,1152]{1,0:T(8,128)(2,1)S(1)} %collective-permute-done), channel_id=1, source_target_pairs={{0,32},{1,481},{32,64},{33,1},{64,96},{65,33},{96,128},{97,65},{12... | collective-permute-start | bytes 884744 | tf_op jit(solution)/shard_map/ppermute | solution.py:33
  27.3 1.0 collective-permute-done.2
  28.3 5.0 %collective-permute-start.3 = (bf16[128,1152]{1,0:T(8,128)(2,1)S(1)}, bf16[128,1152]{1,0:T(8,128)(2,1)S(1)}, u32[]{:S(2)}, u32[]{:S(2)}) collective-permute-start(bf16[128,1152]{1,0:T(8,128)(2,1)S(1)} %collective-permute-done.2), channel_id=1, source_target_pairs={{0,32},{1,481},{32,64},{33,1},{64,96},{65,33},{96,128},{97,65},{12... | collective-permute-start | bytes 884744 | tf_op jit(solution)/shard_map/ppermute | solution.py:33
  33.4 3.1 %collective-permute-start.12 = (bf16[128,1152]{1,0:T(8,128)(2,1)S(1)}, bf16[128,1152]{1,0:T(8,128)(2,1)S(1)}, u32[]{:S(2)}, u32[]{:S(2)}) collective-permute-start(bf16[128,1152]{1,0:T(8,128)(2,1)S(1)} %collective-permute-done.11), channel_id=1, source_target_pairs={{0,32},{1,481},{32,64},{33,1},{64,96},{65,33},{96,128},{97,65},{12... | collective-permute-start | bytes 884744 | tf_op jit(solution)/shard_map/ppermute | solution.py:33
  36.5 0.5 collective-permute-done.3
  37.0 5.0 %collective-permute-start.4 = (bf16[128,1152]{1,0:T(8,128)(2,1)S(1)}, bf16[128,1152]{1,0:T(8,128)(2,1)S(1)}, u32[]{:S(2)}, u32[]{:S(2)}) collective-permute-start(bf16[128,1152]{1,0:T(8,128)(2,1)S(1)} %collective-permute-done.3), channel_id=1, source_target_pairs={{0,32},{1,481},{32,64},{33,1},{64,96},{65,33},{96,128},{97,65},{12... | collective-permute-start | bytes 884744 | tf_op jit(solution)/shard_map/ppermute | solution.py:33
  42.0 3.1 %collective-permute-start.13 = (bf16[128,1152]{1,0:T(8,128)(2,1)S(1)}, bf16[128,1152]{1,0:T(8,128)(2,1)S(1)}, u32[]{:S(2)}, u32[]{:S(2)}) collective-permute-start(bf16[128,1152]{1,0:T(8,128)(2,1)S(1)} %collective-permute-done.12), channel_id=1, source_target_pairs={{0,32},{1,481},{32,64},{33,1},{64,96},{65,33},{96,128},{97,65},{12... | collective-permute-start | bytes 884744 | tf_op jit(solution)/shard_map/ppermute | solution.py:33
  45.2 0.5 collective-permute-done.4
  45.7 5.0 %collective-permute-start.5 = (bf16[128,1152]{1,0:T(8,128)(2,1)S(1)}, bf16[128,1152]{1,0:T(8,128)(2,1)S(1)}, u32[]{:S(2)}, u32[]{:S(2)}) collective-permute-start(bf16[128,1152]{1,0:T(8,128)(2,1)S(1)} %collective-permute-done.4), channel_id=1, source_target_pairs={{0,32},{1,481},{32,64},{33,1},{64,96},{65,33},{96,128},{97,65},{12... | collective-permute-start | bytes 884744 | tf_op jit(solution)/shard_map/ppermute | solution.py:33
  50.7 3.1 %collective-permute-start.14 = (bf16[128,1152]{1,0:T(8,128)(2,1)S(1)}, bf16[128,1152]{1,0:T(8,128)(2,1)S(1)}, u32[]{:S(2)}, u32[]{:S(2)}) collective-permute-start(bf16[128,1152]{1,0:T(8,128)(2,1)S(1)} %collective-permute-done.13), channel_id=1, source_target_pairs={{0,32},{1,481},{32,64},{33,1},{64,96},{65,33},{96,128},{97,65},{12... | collective-permute-start | bytes 884744 | tf_op jit(solution)/shard_map/ppermute | solution.py:33
  53.8 0.5 collective-permute-done.5
  54.3 5.0 %collective-permute-start.6 = (bf16[128,1152]{1,0:T(8,128)(2,1)S(1)}, bf16[128,1152]{1,0:T(8,128)(2,1)S(1)}, u32[]{:S(2)}, u32[]{:S(2)}) collective-permute-start(bf16[128,1152]{1,0:T(8,128)(2,1)S(1)} %collective-permute-done.5), channel_id=1, source_target_pairs={{0,32},{1,481},{32,64},{33,1},{64,96},{65,33},{96,128},{97,65},{12... | collective-permute-start | bytes 884744 | tf_op jit(solution)/shard_map/ppermute | solution.py:33
  59.4 3.1 %collective-permute-start.15 = (bf16[128,1152]{1,0:T(8,128)(2,1)S(1)}, bf16[128,1152]{1,0:T(8,128)(2,1)S(1)}, u32[]{:S(2)}, u32[]{:S(2)}) collective-permute-start(bf16[128,1152]{1,0:T(8,128)(2,1)S(1)} %collective-permute-done.14), channel_id=1, source_target_pairs={{0,32},{1,481},{32,64},{33,1},{64,96},{65,33},{96,128},{97,65},{12... | collective-permute-start | bytes 884744 | tf_op jit(solution)/shard_map/ppermute | solution.py:33
  62.5 0.5 collective-permute-done.6
  63.0 5.0 %collective-permute-start.7 = (bf16[128,1152]{1,0:T(8,128)(2,1)S(1)}, bf16[128,1152]{1,0:T(8,128)(2,1)S(1)}, u32[]{:S(2)}, u32[]{:S(2)}) collective-permute-start(bf16[128,1152]{1,0:T(8,128)(2,1)S(1)} %collective-permute-done.6), channel_id=1, source_target_pairs={{0,32},{1,481},{32,64},{33,1},{64,96},{65,33},{96,128},{97,65},{12... | collective-permute-start | bytes 884744 | tf_op jit(solution)/shard_map/ppermute | solution.py:33
  68.0 3.1 %collective-permute-start.16 = (bf16[128,1152]{1,0:T(8,128)(2,1)S(1)}, bf16[128,1152]{1,0:T(8,128)(2,1)}, u32[]{:S(2)}, u32[]{:S(2)}) collective-permute-start(bf16[128,1152]{1,0:T(8,128)(2,1)S(1)} %collective-permute-done.15), channel_id=1, source_target_pairs={{0,32},{1,481},{32,64},{33,1},{64,96},{65,33},{96,128},{97,65},{12... | collective-permute-start | bytes 884744 | tf_op jit(solution)/shard_map/ppermute | solution.py:33
  71.2 0.5 collective-permute-done.7
  71.7 5.0 %collective-permute-start.8 = (bf16[128,1152]{1,0:T(8,128)(2,1)S(1)}, bf16[128,1152]{1,0:T(8,128)(2,1)S(1)}, u32[]{:S(2)}, u32[]{:S(2)}) collective-permute-start(bf16[128,1152]{1,0:T(8,128)(2,1)S(1)} %collective-permute-done.7), channel_id=1, source_target_pairs={{0,32},{1,481},{32,64},{33,1},{64,96},{65,33},{96,128},{97,65},{12... | collective-permute-start | bytes 884744 | tf_op jit(solution)/shard_map/ppermute | solution.py:33
  76.7 3.3 %collective-permute-start.17 = (bf16[128,1152]{1,0:T(8,128)(2,1)}, bf16[128,1152]{1,0:T(8,128)(2,1)}, u32[]{:S(2)}, u32[]{:S(2)}) collective-permute-start(bf16[128,1152]{1,0:T(8,128)(2,1)} %collective-permute-done.16), channel_id=1, source_target_pairs={{0,32},{1,481},{32,64},{33,1},{64,96},{65,33},{96,128},{97,65},{12... | collective-permute-start | bytes 884744 | tf_op jit(solution)/shard_map/ppermute | solution.py:33
  80.0 0.4 collective-permute-done.8
  80.3 5.0 %collective-permute-start.9 = (bf16[128,1152]{1,0:T(8,128)(2,1)S(1)}, bf16[128,1152]{1,0:T(8,128)(2,1)}, u32[]{:S(2)}, u32[]{:S(2)}) collective-permute-start(bf16[128,1152]{1,0:T(8,128)(2,1)S(1)} %collective-permute-done.8), channel_id=1, source_target_pairs={{1,481},{33,1},{65,33},{97,65},{129,97},{161,129},{193,161},{225,1... | collective-permute-start | bytes 884744 | tf_op jit(solution)/shard_map/ppermute | solution.py:33
  85.4 3.5 %collective-permute-start.18 = (bf16[128,1152]{1,0:T(8,128)(2,1)}, bf16[128,1152]{1,0:T(8,128)(2,1)S(1)}, u32[]{:S(2)}, u32[]{:S(2)}) collective-permute-start(bf16[128,1152]{1,0:T(8,128)(2,1)} %collective-permute-done.17), channel_id=1, source_target_pairs={{1,481},{33,1},{65,33},{97,65},{129,97},{161,129},{193,161},{225,1... | collective-permute-start | bytes 884744 | tf_op jit(solution)/shard_map/ppermute | solution.py:33
  89.0 5.9 %collective-permute-start.10 = (bf16[1,128,1152]{2,1,0:T(8,128)(2,1)}, bf16[1,128,1152]{2,1,0:T(8,128)(2,1)S(1)}, u32[]{:S(2)}, u32[]{:S(2)}) collective-permute-start(bf16[1,128,1152]{2,1,0:T(8,128)(2,1)} %bitcast), channel_id=1, source_target_pairs={{0,1},{1,0},{2,3},{3,2},{4,5},{5,4},{6,7},{7,6},{8,9},{9,8},{10,11... | collective-permute-start | bytes 884744 | tf_op jit(solution)/shard_map/ppermute | solution.py:37
  95.1 1.9 collective-permute-start.19
  97.1 2.5 %collective-permute-start.20 = (bf16[3,128,1152]{2,1,0:T(8,128)(2,1)S(1)}, bf16[3,128,1152]{2,1,0:T(8,128)(2,1)S(1)}, u32[]{:S(2)}, u32[]{:S(2)}) collective-permute-start(bf16[3,128,1152]{2,1,0:T(8,128)(2,1)S(1)} %pad_maximum_fusion.2), channel_id=1, source_target_pairs={{0,1},{1,0},{2,3},{3,2},{4,5},{5,4},{6,7},{7,6},{8,9},{9,8},{10,11... | collective-permute-start | bytes 2654216 | tf_op jit(solution)/shard_map/ppermute | solution.py:37
  99.8 1.0 constant_dynamic-update-slice_fusion.7
  100.8 1.0 constant_dynamic-update-slice_fusion.6
  102.3 1.6 fusion.12
  103.9 1.6 copy.7
  105.5 7.0 %all-to-all-start = ((f32[16,16,8,256]{3,2,1,0:T(8,128)}), f32[16,16,8,256]{3,2,1,0:T(8,128)S(1)}, u32[]{:S(2)}, u32[]{:S(2)}) async-start(f32[16,16,8,256]{3,2,1,0:T(8,128)} %bitcast.139), calls=%async_computation | async-start | bytes 4194304 | tf_op jit(solution)/shard_map/all_to_all | solution.py:86
  112.5 33.2 %all-to-all-done = f32[16,16,8,256]{3,2,1,0:T(8,128)S(1)} async-done(((f32[16,16,8,256]{3,2,1,0:T(8,128)}), f32[16,16,8,256]{3,2,1,0:T(8,128)S(1)}, u32[]{:S(2)}, u32[]{:S(2)}) %all-to-all-start) | async-done | bytes 2097184 | tf_op jit(solution)/shard_map/all_to_all | solution.py:86
  145.9 1.1 broadcast_in_dim.14
  147.0 4.8 %all-to-all-start.1 = ((bf16[16,128,256]{2,1,0:T(8,128)(2,1)}), bf16[16,128,256]{2,1,0:T(8,128)(2,1)S(1)}, u32[]{:S(2)}, u32[]{:S(2)}) async-start(bf16[16,128,256]{2,1,0:T(8,128)(2,1)} %broadcast_in_dim.14), calls=%async_computation.1 | async-start | bytes 2097152 | tf_op jit(solution)/shard_map/all_to_all | solution.py:17
  151.9 18.6 %all_gather.3 = bf16[4,128,256]{2,1,0:T(8,128)(2,1)S(1)} all-gather(bf16[1,128,256]{2,1,0:T(8,128)(2,1)S(1)} %get-tuple-element.7), channel_id=1, replica_groups=mesh['zh'=4,'zl'=4,'ylo'=2,'x'=4,'yhi'=2,'core'=2] {'zh'}, dimensions={0}, use_global_device_ids=true | all-gather | bytes 327680 | tf_op jit(solution)/shard_map/all_gather | solution.py:93
  170.9 7.4 %collective-permute-start.25 = (bf16[4,4,128,256]{3,2,1,0:T(8,128)(2,1)S(1)}, bf16[4,4,128,256]{3,2,1,0:T(8,128)(2,1)}, u32[]{:S(2)}, u32[]{:S(2)}) collective-permute-start(bf16[4,4,128,256]{3,2,1,0:T(8,128)(2,1)S(1)} %pad_maximum_fusion.1), channel_id=1, source_target_pairs={{0,1},{1,0},{2,3},{3,2},{4,5},{5,4},{6,7},{7,6},{8,9},{9,8},{10,11... | collective-permute-start | bytes 3145736 | tf_op jit(solution)/shard_map/ppermute | solution.py:107
  178.3 1.9 collective-permute-start.23
  180.3 4.3 %collective-permute-start.24 = (bf16[2,128,256]{2,1,0:T(8,128)(2,1)S(1)}, bf16[2,128,256]{2,1,0:T(8,128)(2,1)S(1)}, u32[]{:S(2)}, u32[]{:S(2)}) collective-permute-start(bf16[2,128,256]{2,1,0:T(8,128)(2,1)S(1)} %get-tuple-element.15), channel_id=1, source_target_pairs={{0,64},{32,96},{64,128},{96,160},{128,192},{160,224},{192,256},{22... | collective-permute-start | bytes 393224 | tf_op jit(solution)/shard_map/ppermute | solution.py:23
  184.6 1.9 collective-permute-start.22
  186.5 4.6 %collective-permute-start.21 = (bf16[4,128,256]{2,1,0:T(8,128)(2,1)S(1)}, bf16[4,128,256]{2,1,0:T(8,128)(2,1)S(1)}, u32[]{:S(2)}, u32[]{:S(2)}) collective-permute-start(bf16[4,128,256]{2,1,0:T(8,128)(2,1)S(1)} %all_gather.3), channel_id=1, source_target_pairs={{0,480},{32,0},{64,32},{96,64},{128,96},{160,128},{192,160},{224,1... | collective-permute-start | bytes 786440 | tf_op jit(solution)/shard_map/ppermute | solution.py:23
  191.1 0.2 collective-permute-done.24
  191.3 0.2 convolution_bitcast_fusion.7
  191.5 0.2 convolution_bitcast_fusion.4
  191.7 6.1 %collective-permute-done.22 = bf16[4,128,256]{2,1,0:T(8,128)(2,1)S(1)} collective-permute-done((bf16[4,128,256]{2,1,0:T(8,128)(2,1)S(1)}, bf16[4,128,256]{2,1,0:T(8,128)(2,1)S(1)}, u32[]{:S(2)}, u32[]{:S(2)}) %collective-permute-start.22) | collective-permute-done | bytes 262176 | tf_op jit(solution)/shard_map/ppermute | solution.py:23
  197.8 0.2 convolution_bitcast_fusion.5
  198.0 1.4 fusion.66
  199.4 0.2 convolution_bitcast_fusion.3
  199.6 0.2 convolution_bitcast_fusion
  199.8 0.2 convolution_bitcast_fusion.1
  200.1 0.2 convolution_bitcast_fusion.2
  200.3 0.2 fusion.11
  200.7 22.4 %all_to_all.15 = bf16[16,16,8,256]{3,2,1,0:T(8,128)(2,1)S(1)} all-to-all(bf16[16,16,8,256]{3,2,1,0:T(8,128)(2,1)S(1)} %broadcast_in_dim.15), channel_id=1, replica_groups=mesh['zh'=4,'zl'=4,'ylo'=2,'x'=4,'yhi'=2,'core'=2] {'ylo','x','yhi'}, dimensions={0} | all-to-all | bytes 2097152 | tf_op jit(solution)/shard_map/all_to_all | solution.py:17
  223.3 0.9 convolution_convert_fusion
  224.2 0.9 fusion
  225.1 4.5 %collective-permute-start.26 = (bf16[128,1152]{1,0:T(8,128)(2,1)S(1)}, bf16[128,1152]{1,0:T(8,128)(2,1)S(1)}, u32[]{:S(2)}, u32[]{:S(2)}) collective-permute-start(bf16[128,1152]{1,0:T(8,128)(2,1)S(1)} %fusion), channel_id=1, source_target_pairs={{0,0},{1,16},{16,1},{17,17},{2,2},{3,18},{18,3},{19,19},{4,4},{5,2... | collective-permute-start | bytes 884744 | tf_op jit(solution)/shard_map/ppermute | solution.py:124
  229.7 1.9 collective-permute-start.27
  231.6 2.5 %collective-permute-done.26 = bf16[128,1152]{1,0:T(8,128)(2,1)S(1)} collective-permute-done((bf16[128,1152]{1,0:T(8,128)(2,1)S(1)}, bf16[128,1152]{1,0:T(8,128)(2,1)S(1)}, u32[]{:S(2)}, u32[]{:S(2)}) %collective-permute-start.26) | collective-permute-done | bytes 294944 | tf_op jit(solution)/shard_map/ppermute | solution.py:124
  234.1 3.1 %collective-permute-done.27 = bf16[128,1152]{1,0:T(8,128)(2,1)S(1)} collective-permute-done((bf16[128,1152]{1,0:T(8,128)(2,1)S(1)}, bf16[128,1152]{1,0:T(8,128)(2,1)S(1)}, u32[]{:S(2)}, u32[]{:S(2)}) %collective-permute-start.27) | collective-permute-done | bytes 294944 | tf_op jit(solution)/shard_map/ppermute | solution.py:122
  237.2 0.9 convert_add_fusion
  (61 shorter events, 1.8 us)
Async XLA Ops:
  1.1 9.0 %collective-permute-start = (bf16[128,1152]{1,0:T(8,128)(2,1)S(1)}, bf16[128,1152]{1,0:T(8,128)(2,1)S(1)}, u32[]{:S(2)}, u32[]{:S(2)}) collective-permute-start(bf16[128,1152]{1,0:T(8,128)(2,1)S(1)} %convert_element_type.24), channel_id=1, source_target_pairs={{0,0},{1,16},{16,1},{17,17},{2,2},{3,18},{18,3},{19,19},{4,4},{5,2... | collective-permute-start | bytes 884744 | tf_op jit(solution)/shard_map/ppermute | solution.py:73
  10.1 3.5 %collective-permute-start.1 = (bf16[128,1152]{1,0:T(8,128)(2,1)S(1)}, bf16[128,1152]{1,0:T(8,128)(2,1)S(1)}, u32[]{:S(2)}, u32[]{:S(2)}) collective-permute-start(bf16[128,1152]{1,0:T(8,128)(2,1)S(1)} %collective-permute-done), channel_id=1, source_target_pairs={{0,1},{1,0},{2,3},{3,2},{4,5},{5,4},{6,7},{7,6},{8,9},{9,8},{10,11... | collective-permute-start | bytes 884744 | tf_op jit(solution)/shard_map/ppermute | solution.py:74
  13.6 13.8 %copy-start.3 = (bf16[128,1152]{1,0:T(8,128)(2,1)}, bf16[128,1152]{1,0:T(8,128)(2,1)S(1)}, u32[]{:S(2)}) copy-start(bf16[128,1152]{1,0:T(8,128)(2,1)S(1)} %collective-permute-done.1) | copy-start | bytes 884740
  13.6 14.8 %collective-permute-start.2 = (bf16[128,1152]{1,0:T(8,128)(2,1)S(1)}, bf16[128,1152]{1,0:T(8,128)(2,1)S(1)}, u32[]{:S(2)}, u32[]{:S(2)}) collective-permute-start(bf16[128,1152]{1,0:T(8,128)(2,1)S(1)} %collective-permute-done.1), channel_id=1, source_target_pairs={{0,32},{1,481},{32,64},{33,1},{64,96},{65,33},{96,128},{97,65},{12... | collective-permute-start | bytes 884744 | tf_op jit(solution)/shard_map/ppermute | solution.py:33
  24.7 8.7 %collective-permute-start.11 = (bf16[128,1152]{1,0:T(8,128)(2,1)S(1)}, bf16[128,1152]{1,0:T(8,128)(2,1)S(1)}, u32[]{:S(2)}, u32[]{:S(2)}) collective-permute-start(bf16[128,1152]{1,0:T(8,128)(2,1)S(1)} %collective-permute-done), channel_id=1, source_target_pairs={{0,32},{1,481},{32,64},{33,1},{64,96},{65,33},{96,128},{97,65},{12... | collective-permute-start | bytes 884744 | tf_op jit(solution)/shard_map/ppermute | solution.py:33
  28.3 8.7 %collective-permute-start.3 = (bf16[128,1152]{1,0:T(8,128)(2,1)S(1)}, bf16[128,1152]{1,0:T(8,128)(2,1)S(1)}, u32[]{:S(2)}, u32[]{:S(2)}) collective-permute-start(bf16[128,1152]{1,0:T(8,128)(2,1)S(1)} %collective-permute-done.2), channel_id=1, source_target_pairs={{0,32},{1,481},{32,64},{33,1},{64,96},{65,33},{96,128},{97,65},{12... | collective-permute-start | bytes 884744 | tf_op jit(solution)/shard_map/ppermute | solution.py:33
  33.4 8.7 %collective-permute-start.12 = (bf16[128,1152]{1,0:T(8,128)(2,1)S(1)}, bf16[128,1152]{1,0:T(8,128)(2,1)S(1)}, u32[]{:S(2)}, u32[]{:S(2)}) collective-permute-start(bf16[128,1152]{1,0:T(8,128)(2,1)S(1)} %collective-permute-done.11), channel_id=1, source_target_pairs={{0,32},{1,481},{32,64},{33,1},{64,96},{65,33},{96,128},{97,65},{12... | collective-permute-start | bytes 884744 | tf_op jit(solution)/shard_map/ppermute | solution.py:33
  37.0 8.7 %collective-permute-start.4 = (bf16[128,1152]{1,0:T(8,128)(2,1)S(1)}, bf16[128,1152]{1,0:T(8,128)(2,1)S(1)}, u32[]{:S(2)}, u32[]{:S(2)}) collective-permute-start(bf16[128,1152]{1,0:T(8,128)(2,1)S(1)} %collective-permute-done.3), channel_id=1, source_target_pairs={{0,32},{1,481},{32,64},{33,1},{64,96},{65,33},{96,128},{97,65},{12... | collective-permute-start | bytes 884744 | tf_op jit(solution)/shard_map/ppermute | solution.py:33
  42.0 8.7 %collective-permute-start.13 = (bf16[128,1152]{1,0:T(8,128)(2,1)S(1)}, bf16[128,1152]{1,0:T(8,128)(2,1)S(1)}, u32[]{:S(2)}, u32[]{:S(2)}) collective-permute-start(bf16[128,1152]{1,0:T(8,128)(2,1)S(1)} %collective-permute-done.12), channel_id=1, source_target_pairs={{0,32},{1,481},{32,64},{33,1},{64,96},{65,33},{96,128},{97,65},{12... | collective-permute-start | bytes 884744 | tf_op jit(solution)/shard_map/ppermute | solution.py:33
  45.7 8.7 %collective-permute-start.5 = (bf16[128,1152]{1,0:T(8,128)(2,1)S(1)}, bf16[128,1152]{1,0:T(8,128)(2,1)S(1)}, u32[]{:S(2)}, u32[]{:S(2)}) collective-permute-start(bf16[128,1152]{1,0:T(8,128)(2,1)S(1)} %collective-permute-done.4), channel_id=1, source_target_pairs={{0,32},{1,481},{32,64},{33,1},{64,96},{65,33},{96,128},{97,65},{12... | collective-permute-start | bytes 884744 | tf_op jit(solution)/shard_map/ppermute | solution.py:33
  50.7 8.7 %collective-permute-start.14 = (bf16[128,1152]{1,0:T(8,128)(2,1)S(1)}, bf16[128,1152]{1,0:T(8,128)(2,1)S(1)}, u32[]{:S(2)}, u32[]{:S(2)}) collective-permute-start(bf16[128,1152]{1,0:T(8,128)(2,1)S(1)} %collective-permute-done.13), channel_id=1, source_target_pairs={{0,32},{1,481},{32,64},{33,1},{64,96},{65,33},{96,128},{97,65},{12... | collective-permute-start | bytes 884744 | tf_op jit(solution)/shard_map/ppermute | solution.py:33
  54.3 8.7 %collective-permute-start.6 = (bf16[128,1152]{1,0:T(8,128)(2,1)S(1)}, bf16[128,1152]{1,0:T(8,128)(2,1)S(1)}, u32[]{:S(2)}, u32[]{:S(2)}) collective-permute-start(bf16[128,1152]{1,0:T(8,128)(2,1)S(1)} %collective-permute-done.5), channel_id=1, source_target_pairs={{0,32},{1,481},{32,64},{33,1},{64,96},{65,33},{96,128},{97,65},{12... | collective-permute-start | bytes 884744 | tf_op jit(solution)/shard_map/ppermute | solution.py:33
  59.4 8.7 %collective-permute-start.15 = (bf16[128,1152]{1,0:T(8,128)(2,1)S(1)}, bf16[128,1152]{1,0:T(8,128)(2,1)S(1)}, u32[]{:S(2)}, u32[]{:S(2)}) collective-permute-start(bf16[128,1152]{1,0:T(8,128)(2,1)S(1)} %collective-permute-done.14), channel_id=1, source_target_pairs={{0,32},{1,481},{32,64},{33,1},{64,96},{65,33},{96,128},{97,65},{12... | collective-permute-start | bytes 884744 | tf_op jit(solution)/shard_map/ppermute | solution.py:33
  63.0 8.7 %collective-permute-start.7 = (bf16[128,1152]{1,0:T(8,128)(2,1)S(1)}, bf16[128,1152]{1,0:T(8,128)(2,1)S(1)}, u32[]{:S(2)}, u32[]{:S(2)}) collective-permute-start(bf16[128,1152]{1,0:T(8,128)(2,1)S(1)} %collective-permute-done.6), channel_id=1, source_target_pairs={{0,32},{1,481},{32,64},{33,1},{64,96},{65,33},{96,128},{97,65},{12... | collective-permute-start | bytes 884744 | tf_op jit(solution)/shard_map/ppermute | solution.py:33
  68.0 12.3 %copy-start.1 = (bf16[128,1152]{1,0:T(8,128)(2,1)}, bf16[128,1152]{1,0:T(8,128)(2,1)S(1)}, u32[]{:S(2)}) copy-start(bf16[128,1152]{1,0:T(8,128)(2,1)S(1)} %collective-permute-done.15) | copy-start | bytes 884740
  68.0 8.6 %collective-permute-start.16 = (bf16[128,1152]{1,0:T(8,128)(2,1)S(1)}, bf16[128,1152]{1,0:T(8,128)(2,1)}, u32[]{:S(2)}, u32[]{:S(2)}) collective-permute-start(bf16[128,1152]{1,0:T(8,128)(2,1)S(1)} %collective-permute-done.15), channel_id=1, source_target_pairs={{0,32},{1,481},{32,64},{33,1},{64,96},{65,33},{96,128},{97,65},{12... | collective-permute-start | bytes 884744 | tf_op jit(solution)/shard_map/ppermute | solution.py:33
  71.7 8.7 %collective-permute-start.8 = (bf16[128,1152]{1,0:T(8,128)(2,1)S(1)}, bf16[128,1152]{1,0:T(8,128)(2,1)S(1)}, u32[]{:S(2)}, u32[]{:S(2)}) collective-permute-start(bf16[128,1152]{1,0:T(8,128)(2,1)S(1)} %collective-permute-done.7), channel_id=1, source_target_pairs={{0,32},{1,481},{32,64},{33,1},{64,96},{65,33},{96,128},{97,65},{12... | collective-permute-start | bytes 884744 | tf_op jit(solution)/shard_map/ppermute | solution.py:33
  76.7 8.7 %collective-permute-start.17 = (bf16[128,1152]{1,0:T(8,128)(2,1)}, bf16[128,1152]{1,0:T(8,128)(2,1)}, u32[]{:S(2)}, u32[]{:S(2)}) collective-permute-start(bf16[128,1152]{1,0:T(8,128)(2,1)} %collective-permute-done.16), channel_id=1, source_target_pairs={{0,32},{1,481},{32,64},{33,1},{64,96},{65,33},{96,128},{97,65},{12... | collective-permute-start | bytes 884744 | tf_op jit(solution)/shard_map/ppermute | solution.py:33
  80.3 8.7 %collective-permute-start.9 = (bf16[128,1152]{1,0:T(8,128)(2,1)S(1)}, bf16[128,1152]{1,0:T(8,128)(2,1)}, u32[]{:S(2)}, u32[]{:S(2)}) collective-permute-start(bf16[128,1152]{1,0:T(8,128)(2,1)S(1)} %collective-permute-done.8), channel_id=1, source_target_pairs={{1,481},{33,1},{65,33},{97,65},{129,97},{161,129},{193,161},{225,1... | collective-permute-start | bytes 884744 | tf_op jit(solution)/shard_map/ppermute | solution.py:33
  85.4 16.4 %copy-start.2 = (bf16[128,1152]{1,0:T(8,128)(2,1)S(1)}, bf16[128,1152]{1,0:T(8,128)(2,1)}, u32[]{:S(2)}) copy-start(bf16[128,1152]{1,0:T(8,128)(2,1)} %copy-done.1) | copy-start | bytes 884740
  85.4 14.3 %collective-permute-start.18 = (bf16[128,1152]{1,0:T(8,128)(2,1)}, bf16[128,1152]{1,0:T(8,128)(2,1)S(1)}, u32[]{:S(2)}, u32[]{:S(2)}) collective-permute-start(bf16[128,1152]{1,0:T(8,128)(2,1)} %collective-permute-done.17), channel_id=1, source_target_pairs={{1,481},{33,1},{65,33},{97,65},{129,97},{161,129},{193,161},{225,1... | collective-permute-start | bytes 884744 | tf_op jit(solution)/shard_map/ppermute | solution.py:33
  89.0 10.7 %collective-permute-start.10 = (bf16[1,128,1152]{2,1,0:T(8,128)(2,1)}, bf16[1,128,1152]{2,1,0:T(8,128)(2,1)S(1)}, u32[]{:S(2)}, u32[]{:S(2)}) collective-permute-start(bf16[1,128,1152]{2,1,0:T(8,128)(2,1)} %bitcast), channel_id=1, source_target_pairs={{0,1},{1,0},{2,3},{3,2},{4,5},{5,4},{6,7},{7,6},{8,9},{9,8},{10,11... | collective-permute-start | bytes 884744 | tf_op jit(solution)/shard_map/ppermute | solution.py:37
  95.1 6.9 %collective-permute-start.19 = (bf16[4,128,1152]{2,1,0:T(8,128)(2,1)S(1)}, bf16[4,128,1152]{2,1,0:T(8,128)(2,1)S(1)}, u32[]{:S(2)}, u32[]{:S(2)}) collective-permute-start(bf16[4,128,1152]{2,1,0:T(8,128)(2,1)S(1)} %pad_maximum_fusion), channel_id=1, source_target_pairs={{0,1},{1,0},{2,3},{3,2},{4,5},{5,4},{6,7},{7,6},{8,9},{9,8},{10,11... | collective-permute-start | bytes 3538952 | tf_op jit(solution)/shard_map/ppermute | solution.py:37
  97.1 5.2 %copy-start.4 = (bf16[128,1152]{1,0:T(8,128)(2,1)S(1)}, bf16[128,1152]{1,0:T(8,128)(2,1)}, u32[]{:S(2)}) copy-start(bf16[128,1152]{1,0:T(8,128)(2,1)} %copy-done.3) | copy-start | bytes 884740
  97.1 5.0 %collective-permute-start.20 = (bf16[3,128,1152]{2,1,0:T(8,128)(2,1)S(1)}, bf16[3,128,1152]{2,1,0:T(8,128)(2,1)S(1)}, u32[]{:S(2)}, u32[]{:S(2)}) collective-permute-start(bf16[3,128,1152]{2,1,0:T(8,128)(2,1)S(1)} %pad_maximum_fusion.2), channel_id=1, source_target_pairs={{0,1},{1,0},{2,3},{3,2},{4,5},{5,4},{6,7},{7,6},{8,9},{9,8},{10,11... | collective-permute-start | bytes 2654216 | tf_op jit(solution)/shard_map/ppermute | solution.py:37
  102.3 3.2 %copy-start = (bf16[2048,1152]{1,0:T(8,128)(2,1)}, bf16[2048,1152]{1,0:T(8,128)(2,1)S(1)}, u32[]{:S(2)}) copy-start(bf16[2048,1152]{1,0:T(8,128)(2,1)S(1)} %fusion.18) | copy-start | bytes 14155780
  105.5 40.2 %all-to-all-start = ((f32[16,16,8,256]{3,2,1,0:T(8,128)}), f32[16,16,8,256]{3,2,1,0:T(8,128)S(1)}, u32[]{:S(2)}, u32[]{:S(2)}) async-start(f32[16,16,8,256]{3,2,1,0:T(8,128)} %bitcast.139), calls=%async_computation | async-start | bytes 4194304 | tf_op jit(solution)/shard_map/all_to_all | solution.py:86
  147.0 23.5 %all-to-all-start.1 = ((bf16[16,128,256]{2,1,0:T(8,128)(2,1)}), bf16[16,128,256]{2,1,0:T(8,128)(2,1)S(1)}, u32[]{:S(2)}, u32[]{:S(2)}) async-start(bf16[16,128,256]{2,1,0:T(8,128)(2,1)} %broadcast_in_dim.14), calls=%async_computation.1 | async-start | bytes 2097152 | tf_op jit(solution)/shard_map/all_to_all | solution.py:17
  170.9 27.1 %collective-permute-start.25 = (bf16[4,4,128,256]{3,2,1,0:T(8,128)(2,1)S(1)}, bf16[4,4,128,256]{3,2,1,0:T(8,128)(2,1)}, u32[]{:S(2)}, u32[]{:S(2)}) collective-permute-start(bf16[4,4,128,256]{3,2,1,0:T(8,128)(2,1)S(1)} %pad_maximum_fusion.1), channel_id=1, source_target_pairs={{0,1},{1,0},{2,3},{3,2},{4,5},{5,4},{6,7},{7,6},{8,9},{9,8},{10,11... | collective-permute-start | bytes 3145736 | tf_op jit(solution)/shard_map/ppermute | solution.py:107
  178.3 12.7 %collective-permute-start.23 = (bf16[2,128,256]{2,1,0:T(8,128)(2,1)S(1)}, bf16[2,128,256]{2,1,0:T(8,128)(2,1)S(1)}, u32[]{:S(2)}, u32[]{:S(2)}) collective-permute-start(bf16[2,128,256]{2,1,0:T(8,128)(2,1)S(1)} %get-tuple-element.16), channel_id=1, source_target_pairs={{0,448},{32,480},{64,0},{96,32},{128,64},{160,96},{192,128},{224,1... | collective-permute-start | bytes 393224 | tf_op jit(solution)/shard_map/ppermute | solution.py:23
  180.3 11.0 %collective-permute-start.24 = (bf16[2,128,256]{2,1,0:T(8,128)(2,1)S(1)}, bf16[2,128,256]{2,1,0:T(8,128)(2,1)S(1)}, u32[]{:S(2)}, u32[]{:S(2)}) collective-permute-start(bf16[2,128,256]{2,1,0:T(8,128)(2,1)S(1)} %get-tuple-element.15), channel_id=1, source_target_pairs={{0,64},{32,96},{64,128},{96,160},{128,192},{160,224},{192,256},{22... | collective-permute-start | bytes 393224 | tf_op jit(solution)/shard_map/ppermute | solution.py:23
  184.6 13.2 %collective-permute-start.22 = (bf16[4,128,256]{2,1,0:T(8,128)(2,1)S(1)}, bf16[4,128,256]{2,1,0:T(8,128)(2,1)S(1)}, u32[]{:S(2)}, u32[]{:S(2)}) collective-permute-start(bf16[4,128,256]{2,1,0:T(8,128)(2,1)S(1)} %all_gather.3), channel_id=1, source_target_pairs={{0,32},{32,64},{64,96},{96,128},{128,160},{160,192},{192,224},{224... | collective-permute-start | bytes 786440 | tf_op jit(solution)/shard_map/ppermute | solution.py:23
  186.5 13.6 %collective-permute-start.21 = (bf16[4,128,256]{2,1,0:T(8,128)(2,1)S(1)}, bf16[4,128,256]{2,1,0:T(8,128)(2,1)S(1)}, u32[]{:S(2)}, u32[]{:S(2)}) collective-permute-start(bf16[4,128,256]{2,1,0:T(8,128)(2,1)S(1)} %all_gather.3), channel_id=1, source_target_pairs={{0,480},{32,0},{64,32},{96,64},{128,96},{160,128},{192,160},{224,1... | collective-permute-start | bytes 786440 | tf_op jit(solution)/shard_map/ppermute | solution.py:23
  198.0 25.3 %slice-start = ((s8[4718592]{0:T(1024)(128)(4,1)}), s8[4194304]{0:T(1024)(128)(4,1)S(1)}, s32[]{:S(2)}) async-start(s8[4718592]{0:T(1024)(128)(4,1)} %bitcast.132), calls=%async_computation.3 | async-start | bytes 8388608
  200.0 23.3 %slice-start.1 = ((s8[4718592]{0:T(1024)(128)(4,1)}), s8[524288]{0:T(1024)(128)(4,1)S(1)}, s32[]{:S(2)}) async-start(s8[4718592]{0:T(1024)(128)(4,1)} %bitcast.132), calls=%async_computation.4 | async-start | bytes 1048576
  225.1 9.0 %collective-permute-start.26 = (bf16[128,1152]{1,0:T(8,128)(2,1)S(1)}, bf16[128,1152]{1,0:T(8,128)(2,1)S(1)}, u32[]{:S(2)}, u32[]{:S(2)}) collective-permute-start(bf16[128,1152]{1,0:T(8,128)(2,1)S(1)} %fusion), channel_id=1, source_target_pairs={{0,0},{1,16},{16,1},{17,17},{2,2},{3,18},{18,3},{19,19},{4,4},{5,2... | collective-permute-start | bytes 884744 | tf_op jit(solution)/shard_map/ppermute | solution.py:124
  229.7 7.6 %collective-permute-start.27 = (bf16[128,1152]{1,0:T(8,128)(2,1)S(1)}, bf16[128,1152]{1,0:T(8,128)(2,1)S(1)}, u32[]{:S(2)}, u32[]{:S(2)}) collective-permute-start(bf16[128,1152]{1,0:T(8,128)(2,1)S(1)} %convolution_convert_fusion), channel_id=1, source_target_pairs={{0,16},{1,0},{16,17},{17,1},{2,18},{3,2},{18,19},{19,3},{4,20},{5,... | collective-permute-start | bytes 884744 | tf_op jit(solution)/shard_map/ppermute | solution.py:122

commit v8 on v7

--- a/solution.py
+++ b/solution.py
@@ -23,12 +23,12 @@
     return lax.ppermute(piece, LINE, pairs)
 
 
-def onward(piece, cores=(0, 1)):
+def onward(piece):
     size = lax.axis_size(LINE)
     pairs = [
         (2 * place + core, 2 * ((place + 1 - 2 * core) % size) + core)
         for place in range(size)
-        for core in cores
+        for core in range(2)
     ]
     return lax.ppermute(piece, LINE + ("core",), pairs)
 
@@ -70,6 +70,7 @@
     chips = lax.axis_size(PLANE)
     total_cols = cols * chips
     slab, core = lax.axis_index(LINE), lax.axis_index("core")
+    residue = lax.axis_index("zl")
     own = lax.ppermute(rounded, ("ylo", "core"), TURN)
     other = lax.ppermute(own, "core", SWAP)
     both = jnp.concatenate([own, other], 0)
@@ -77,13 +78,17 @@
     for step in range(1, slabs // 2):
         near.append(onward(near[-1]))
         far.append(onward(far[-1]))
-    near_last, far_last = onward(near[-1], (1,)), onward(far[-1], (1,))
-    back = swap(far[1:5]) + swap(far[5:])
-    (back_last,) = swap([far_last])
-    last = jnp.where(core == 0, back_last, near_last)
-    half = jnp.concatenate([last] + near[::-1] + back, 0)
+    near.append(onward(near[-1]))
+    back = swap(far[1:4]) + swap(far[4:6]) + swap(far[6:])
+    half = jnp.concatenate(near[::-1] + back, 0)
     gram = nt(half, both).reshape(slabs, chips, rows // chips, 2 * rows)
-    gram = lax.all_to_all(gram.transpose(1, 0, 2, 3), PLANE, 0, 0).sum(0) / total_cols
+    gram = gram.transpose(1, 0, 2, 3).reshape(chips, rows, 2 * rows)
+    gram, slab, core, residue = lax.optimization_barrier((gram, slab, core, residue))
+    gram = lax.all_to_all(gram, PLANE, 0, 0)
+    gram, half, own, slab, core, residue = lax.optimization_barrier(
+        (gram, half, own, slab, core, residue)
+    )
+    gram = gram.sum(0).reshape(slabs, rows // chips, 2 * rows) / total_cols
     gram = jnp.where(core == 0, gram, gram[::-1])
     gram = turn_to(gram, slabs + slabs // 2 - core - slab)
     gram_low = gram.astype(jnp.bfloat16)
@@ -99,7 +104,6 @@
         along(here, 1),
         jnp.concatenate([along(here[:cut], -2), along(here[cut:], 2)], 0),
     )
-    residue = lax.axis_index("zl")
     right_own = [
         lax.dynamic_index_in_dim(panel, (residue + shift) % steps, 1, False)
         for shift in (0, 1, steps - 1, 2)

time: 239 us -> 229 us (0.958)
  waiting for transfers between devices: 54.9 us -> 21.4 us
  blocking collectives: 41.1 us -> 74.1 us
  starting transfers between devices: 127 us -> 116 us
    all_to_all x0 -> x1, blocking collectives: none -> 33.6 us  [per_device(): gram = lax.all_to_all(gram, PLANE, 0, 0)]
    all_to_all x1 -> x0, waiting for transfers between devices: 33.2 us -> none  [per_device(): lax.all_to_all(gram.transpose(1, 0, 2, 3), PLANE, 0, 0).sum(0) / total_cols]
    all_to_all x1 -> x0, starting transfers between devices: 7 us -> none  [per_device(): lax.all_to_all(gram.transpose(1, 0, 2, 3), PLANE, 0, 0).sum(0) / total_cols]
    ppermute x16 -> x15, starting transfers between devices: 71.3 us -> 68 us  [onward(): return lax.ppermute(piece, LINE + ('core',), pairs)]
  transfers between devices with their start and end apart: 30 -> 28, of which waited for: 15 -> 11; matrix products, arithmetic and copies ran while one was open for 2% -> 3% of each run, Pallas kernels for 0% -> 0%
where the time goes in v8:
time: 229 us; the launch traced here: 228 us
  starting transfers between devices  116 us (51%)
  blocking collectives  74.1 us (32%)
  waiting for transfers between devices  21.4 us (9%)
  local copies, waits for them, and re-layouts  5.58 us (2%)
  matrix products  4.95 us (2%)
  other arithmetic  4.64 us (2%)
    ppermute x15, starting transfers between devices, onward(): return lax.ppermute(piece, LINE + ('core',), pairs)  68 us
    all_to_all x1, blocking collectives, per_device(): gram = lax.all_to_all(gram, PLANE, 0, 0)  33.6 us
    all_to_all x1, blocking collectives, share(): return lax.all_to_all(copies, PLANE, 0, 0)  22.4 us
    all_gather x1, blocking collectives, per_device(): here = lax.all_gather(gram_low, 'zh', axis=0)  18.1 us
    ppermute x4, starting transfers between devices, along(): return lax.ppermute(piece, LINE, pairs)  13.7 us
    ppermute x3, starting transfers between devices, swap(): return list(lax.ppermute(jnp.stack(pieces), 'core', SWAP))  10.8 us
    ppermute x4, waiting for transfers between devices, along(): return lax.ppermute(piece, LINE, pairs)  7.05 us
    ppermute x1, starting transfers between devices, per_device(): right_other = lax.ppermute(jnp.stack(right_own), 'core', SWAP)  6.59 us
  transfers between devices with their start and end apart: 28, of which 11 were waited for; matrix products, arithmetic and copies ran while one was open for 3% of the time, Pallas kernels for 0%

profile of v8, /device:TPU:1, one launch (start us, length us, event | category | flops | bytes accessed | tf_op | source)
XLA Modules:
  0.0 227.6 jit_solution(780322328729336424)
XLA Ops:
  0.0 1.1 convert_element_type.24
  1.1 4.6 %collective-permute-start = (bf16[128,1152]{1,0:T(8,128)(2,1)S(1)}, bf16[128,1152]{1,0:T(8,128)(2,1)S(1)}, u32[]{:S(2)}, u32[]{:S(2)}) collective-permute-start(bf16[128,1152]{1,0:T(8,128)(2,1)S(1)} %convert_element_type.24), channel_id=1, source_target_pairs={{0,0},{1,16},{16,1},{17,17},{2,2},{3,18},{18,3},{19,19},{4,4},{5,2... | collective-permute-start | bytes 884744 | tf_op jit(solution)/shard_map/ppermute | solution.py:74
  5.7 4.4 %collective-permute-done = bf16[128,1152]{1,0:T(8,128)(2,1)S(1)} collective-permute-done((bf16[128,1152]{1,0:T(8,128)(2,1)S(1)}, bf16[128,1152]{1,0:T(8,128)(2,1)S(1)}, u32[]{:S(2)}, u32[]{:S(2)}) %collective-permute-start) | collective-permute-done | bytes 294944 | tf_op jit(solution)/shard_map/ppermute | solution.py:74
  10.1 1.9 collective-permute-start.9
  12.0 11.1 %collective-permute-start.1 = (bf16[128,1152]{1,0:T(8,128)(2,1)S(1)}, bf16[128,1152]{1,0:T(8,128)(2,1)S(1)}, u32[]{:S(2)}, u32[]{:S(2)}) collective-permute-start(bf16[128,1152]{1,0:T(8,128)(2,1)S(1)} %collective-permute-done), channel_id=1, source_target_pairs={{0,32},{1,481},{32,64},{33,1},{64,96},{65,33},{96,128},{97,65},{12... | collective-permute-start | bytes 884744 | tf_op jit(solution)/shard_map/ppermute | solution.py:33
  23.2 2.6 %collective-permute-start.10 = (bf16[128,1152]{1,0:T(8,128)(2,1)S(1)}, bf16[128,1152]{1,0:T(8,128)(2,1)S(1)}, u32[]{:S(2)}, u32[]{:S(2)}) collective-permute-start(bf16[128,1152]{1,0:T(8,128)(2,1)S(1)} %collective-permute-done.9), channel_id=1, source_target_pairs={{0,32},{1,481},{32,64},{33,1},{64,96},{65,33},{96,128},{97,65},{12... | collective-permute-start | bytes 884744 | tf_op jit(solution)/shard_map/ppermute | solution.py:33
  25.8 1.0 collective-permute-done.1
  26.8 5.0 %collective-permute-start.2 = (bf16[128,1152]{1,0:T(8,128)(2,1)S(1)}, bf16[128,1152]{1,0:T(8,128)(2,1)S(1)}, u32[]{:S(2)}, u32[]{:S(2)}) collective-permute-start(bf16[128,1152]{1,0:T(8,128)(2,1)S(1)} %collective-permute-done.1), channel_id=1, source_target_pairs={{0,32},{1,481},{32,64},{33,1},{64,96},{65,33},{96,128},{97,65},{12... | collective-permute-start | bytes 884744 | tf_op jit(solution)/shard_map/ppermute | solution.py:33
  31.8 3.1 %collective-permute-start.11 = (bf16[128,1152]{1,0:T(8,128)(2,1)S(1)}, bf16[128,1152]{1,0:T(8,128)(2,1)S(1)}, u32[]{:S(2)}, u32[]{:S(2)}) collective-permute-start(bf16[128,1152]{1,0:T(8,128)(2,1)S(1)} %collective-permute-done.10), channel_id=1, source_target_pairs={{0,32},{1,481},{32,64},{33,1},{64,96},{65,33},{96,128},{97,65},{12... | collective-permute-start | bytes 884744 | tf_op jit(solution)/shard_map/ppermute | solution.py:33
  35.0 0.5 collective-permute-done.2
  35.5 5.0 %collective-permute-start.3 = (bf16[128,1152]{1,0:T(8,128)(2,1)S(1)}, bf16[128,1152]{1,0:T(8,128)(2,1)S(1)}, u32[]{:S(2)}, u32[]{:S(2)}) collective-permute-start(bf16[128,1152]{1,0:T(8,128)(2,1)S(1)} %collective-permute-done.2), channel_id=1, source_target_pairs={{0,32},{1,481},{32,64},{33,1},{64,96},{65,33},{96,128},{97,65},{12... | collective-permute-start | bytes 884744 | tf_op jit(solution)/shard_map/ppermute | solution.py:33
  40.5 3.1 %collective-permute-start.12 = (bf16[128,1152]{1,0:T(8,128)(2,1)S(1)}, bf16[128,1152]{1,0:T(8,128)(2,1)S(1)}, u32[]{:S(2)}, u32[]{:S(2)}) collective-permute-start(bf16[128,1152]{1,0:T(8,128)(2,1)S(1)} %collective-permute-done.11), channel_id=1, source_target_pairs={{0,32},{1,481},{32,64},{33,1},{64,96},{65,33},{96,128},{97,65},{12... | collective-permute-start | bytes 884744 | tf_op jit(solution)/shard_map/ppermute | solution.py:33
  43.6 0.5 collective-permute-done.3
  44.1 5.0 %collective-permute-start.4 = (bf16[128,1152]{1,0:T(8,128)(2,1)S(1)}, bf16[128,1152]{1,0:T(8,128)(2,1)S(1)}, u32[]{:S(2)}, u32[]{:S(2)}) collective-permute-start(bf16[128,1152]{1,0:T(8,128)(2,1)S(1)} %collective-permute-done.3), channel_id=1, source_target_pairs={{0,32},{1,481},{32,64},{33,1},{64,96},{65,33},{96,128},{97,65},{12... | collective-permute-start | bytes 884744 | tf_op jit(solution)/shard_map/ppermute | solution.py:33
  49.2 3.1 %collective-permute-start.14 = (bf16[128,1152]{1,0:T(8,128)(2,1)S(1)}, bf16[128,1152]{1,0:T(8,128)(2,1)S(1)}, u32[]{:S(2)}, u32[]{:S(2)}) collective-permute-start(bf16[128,1152]{1,0:T(8,128)(2,1)S(1)} %collective-permute-done.12), channel_id=1, source_target_pairs={{0,32},{1,481},{32,64},{33,1},{64,96},{65,33},{96,128},{97,65},{12... | collective-permute-start | bytes 884744 | tf_op jit(solution)/shard_map/ppermute | solution.py:33
  52.3 0.5 collective-permute-done.4
  52.8 5.0 %collective-permute-start.5 = (bf16[128,1152]{1,0:T(8,128)(2,1)S(1)}, bf16[128,1152]{1,0:T(8,128)(2,1)S(1)}, u32[]{:S(2)}, u32[]{:S(2)}) collective-permute-start(bf16[128,1152]{1,0:T(8,128)(2,1)S(1)} %collective-permute-done.4), channel_id=1, source_target_pairs={{0,32},{1,481},{32,64},{33,1},{64,96},{65,33},{96,128},{97,65},{12... | collective-permute-start | bytes 884744 | tf_op jit(solution)/shard_map/ppermute | solution.py:33
  57.8 3.1 %collective-permute-start.15 = (bf16[128,1152]{1,0:T(8,128)(2,1)S(1)}, bf16[128,1152]{1,0:T(8,128)(2,1)}, u32[]{:S(2)}, u32[]{:S(2)}) collective-permute-start(bf16[128,1152]{1,0:T(8,128)(2,1)S(1)} %collective-permute-done.14), channel_id=1, source_target_pairs={{0,32},{1,481},{32,64},{33,1},{64,96},{65,33},{96,128},{97,65},{12... | collective-permute-start | bytes 884744 | tf_op jit(solution)/shard_map/ppermute | solution.py:33
  61.0 0.5 collective-permute-done.5
  61.5 5.0 %collective-permute-start.6 = (bf16[128,1152]{1,0:T(8,128)(2,1)S(1)}, bf16[128,1152]{1,0:T(8,128)(2,1)S(1)}, u32[]{:S(2)}, u32[]{:S(2)}) collective-permute-start(bf16[128,1152]{1,0:T(8,128)(2,1)S(1)} %collective-permute-done.5), channel_id=1, source_target_pairs={{0,32},{1,481},{32,64},{33,1},{64,96},{65,33},{96,128},{97,65},{12... | collective-permute-start | bytes 884744 | tf_op jit(solution)/shard_map/ppermute | solution.py:33
  66.5 3.2 %collective-permute-start.17 = (bf16[128,1152]{1,0:T(8,128)(2,1)}, bf16[128,1152]{1,0:T(8,128)(2,1)}, u32[]{:S(2)}, u32[]{:S(2)}) collective-permute-start(bf16[128,1152]{1,0:T(8,128)(2,1)} %collective-permute-done.15), channel_id=1, source_target_pairs={{0,32},{1,481},{32,64},{33,1},{64,96},{65,33},{96,128},{97,65},{12... | collective-permute-start | bytes 884744 | tf_op jit(solution)/shard_map/ppermute | solution.py:33
  69.7 0.4 collective-permute-done.6
  70.1 5.0 %collective-permute-start.7 = (bf16[128,1152]{1,0:T(8,128)(2,1)S(1)}, bf16[128,1152]{1,0:T(8,128)(2,1)S(1)}, u32[]{:S(2)}, u32[]{:S(2)}) collective-permute-start(bf16[128,1152]{1,0:T(8,128)(2,1)S(1)} %collective-permute-done.6), channel_id=1, source_target_pairs={{0,32},{1,481},{32,64},{33,1},{64,96},{65,33},{96,128},{97,65},{12... | collective-permute-start | bytes 884744 | tf_op jit(solution)/shard_map/ppermute | solution.py:33
  75.2 3.6 %collective-permute-start.18 = (bf16[128,1152]{1,0:T(8,128)(2,1)}, bf16[128,1152]{1,0:T(8,128)(2,1)S(1)}, u32[]{:S(2)}, u32[]{:S(2)}) collective-permute-start(bf16[128,1152]{1,0:T(8,128)(2,1)} %collective-permute-done.17), channel_id=1, source_target_pairs={{0,32},{1,481},{32,64},{33,1},{64,96},{65,33},{96,128},{97,65},{12... | collective-permute-start | bytes 884744 | tf_op jit(solution)/shard_map/ppermute | solution.py:33
  78.9 6.4 %collective-permute-start.13 = (bf16[3,128,1152]{2,1,0:T(8,128)(2,1)S(1)}, bf16[3,128,1152]{2,1,0:T(8,128)(2,1)S(1)}, u32[]{:S(2)}, u32[]{:S(2)}) collective-permute-start(bf16[3,128,1152]{2,1,0:T(8,128)(2,1)S(1)} %pad_maximum_fusion.1), channel_id=1, source_target_pairs={{0,1},{1,0},{2,3},{3,2},{4,5},{5,4},{6,7},{7,6},{8,9},{9,8},{10,11... | collective-permute-start | bytes 2654216 | tf_op jit(solution)/shard_map/ppermute | solution.py:37
  85.2 4.9 %collective-permute-start.8 = (bf16[128,1152]{1,0:T(8,128)(2,1)S(1)}, bf16[128,1152]{1,0:T(8,128)(2,1)S(1)}, u32[]{:S(2)}, u32[]{:S(2)}) collective-permute-start(bf16[128,1152]{1,0:T(8,128)(2,1)S(1)} %collective-permute-done.7), channel_id=1, source_target_pairs={{0,32},{1,481},{32,64},{33,1},{64,96},{65,33},{96,128},{97,65},{12... | collective-permute-start | bytes 884744 | tf_op jit(solution)/shard_map/ppermute | solution.py:33
  90.1 1.0 pad_maximum_fusion.2
  91.1 1.9 collective-permute-start.16
  93.1 1.0 pad_maximum_fusion.3
  94.1 2.5 %collective-permute-start.19 = (bf16[2,128,1152]{2,1,0:T(8,128)(2,1)S(1)}, bf16[2,128,1152]{2,1,0:T(8,128)(2,1)S(1)}, u32[]{:S(2)}, u32[]{:S(2)}) collective-permute-start(bf16[2,128,1152]{2,1,0:T(8,128)(2,1)S(1)} %pad_maximum_fusion.3), channel_id=1, source_target_pairs={{0,1},{1,0},{2,3},{3,2},{4,5},{5,4},{6,7},{7,6},{8,9},{9,8},{10,11... | collective-permute-start | bytes 1769480 | tf_op jit(solution)/shard_map/ppermute | solution.py:37
  97.2 1.0 collective-permute-done.19
  98.4 1.6 fusion.12
  100.0 0.2 copy.9
  100.2 0.3 copy-done
  100.5 33.6 %all_to_all.15 = f32[16,128,256]{2,1,0:T(8,128)S(1)} all-to-all(f32[16,128,256]{2,1,0:T(8,128)S(1)} %bitcast.137), channel_id=1, replica_groups=mesh['zh'=4,'zl'=4,'ylo'=2,'x'=4,'yhi'=2,'core'=2] {'ylo','x','yhi'}, dimensions={0} | all-to-all | bytes 4194304 | tf_op jit(solution)/shard_map/all_to_all | solution.py:87
  134.3 1.1 broadcast_in_dim.14
  135.4 4.2 %all-to-all-start.1 = ((bf16[16,128,256]{2,1,0:T(8,128)(2,1)}), bf16[16,128,256]{2,1,0:T(8,128)(2,1)S(1)}, u32[]{:S(2)}, u32[]{:S(2)}) async-start(bf16[16,128,256]{2,1,0:T(8,128)(2,1)} %broadcast_in_dim.14), calls=%async_computation.1 | async-start | bytes 2097152 | tf_op jit(solution)/shard_map/all_to_all | solution.py:17
  139.7 18.1 %all_gather.3 = bf16[4,128,256]{2,1,0:T(8,128)(2,1)S(1)} all-gather(bf16[1,128,256]{2,1,0:T(8,128)(2,1)S(1)} %get-tuple-element.27), channel_id=1, replica_groups=mesh['zh'=4,'zl'=4,'ylo'=2,'x'=4,'yhi'=2,'core'=2] {'zh'}, dimensions={0}, use_global_device_ids=true | all-gather | bytes 327680 | tf_op jit(solution)/shard_map/all_gather | solution.py:98
  158.0 0.1 pad_maximum_fusion
  158.1 6.6 %collective-permute-start.24 = (bf16[4,4,128,256]{3,2,1,0:T(8,128)(2,1)S(1)}, bf16[4,4,128,256]{3,2,1,0:T(8,128)(2,1)}, u32[]{:S(2)}, u32[]{:S(2)}) collective-permute-start(bf16[4,4,128,256]{3,2,1,0:T(8,128)(2,1)S(1)} %pad_maximum_fusion), channel_id=1, source_target_pairs={{0,1},{1,0},{2,3},{3,2},{4,5},{5,4},{6,7},{7,6},{8,9},{9,8},{10,11... | collective-permute-start | bytes 3145736 | tf_op jit(solution)/shard_map/ppermute | solution.py:111
  164.7 0.7 fusion.66
  165.5 3.3 %collective-permute-start.22 = (bf16[2,128,256]{2,1,0:T(8,128)(2,1)}, bf16[2,128,256]{2,1,0:T(8,128)(2,1)}, u32[]{:S(2)}, u32[]{:S(2)}) collective-permute-start(bf16[2,128,256]{2,1,0:T(8,128)(2,1)} %get-tuple-element.36), channel_id=1, source_target_pairs={{0,448},{32,480},{64,0},{96,32},{128,64},{160,96},{192,128},{224,1... | collective-permute-start | bytes 393224 | tf_op jit(solution)/shard_map/ppermute | solution.py:23
  168.8 2.9 %collective-permute-start.23 = (bf16[2,128,256]{2,1,0:T(8,128)(2,1)}, bf16[2,128,256]{2,1,0:T(8,128)(2,1)S(1)}, u32[]{:S(2)}, u32[]{:S(2)}) collective-permute-start(bf16[2,128,256]{2,1,0:T(8,128)(2,1)} %get-tuple-element.35), channel_id=1, source_target_pairs={{0,64},{32,96},{64,128},{96,160},{128,192},{160,224},{192,256},{22... | collective-permute-start | bytes 393224 | tf_op jit(solution)/shard_map/ppermute | solution.py:23
  171.6 3.2 %collective-permute-start.21 = (bf16[4,128,256]{2,1,0:T(8,128)(2,1)S(1)}, bf16[4,128,256]{2,1,0:T(8,128)(2,1)S(1)}, u32[]{:S(2)}, u32[]{:S(2)}) collective-permute-start(bf16[4,128,256]{2,1,0:T(8,128)(2,1)S(1)} %all_gather.3), channel_id=1, source_target_pairs={{0,32},{32,64},{64,96},{96,128},{128,160},{160,192},{192,224},{224... | collective-permute-start | bytes 786440 | tf_op jit(solution)/shard_map/ppermute | solution.py:23
  174.9 4.3 %collective-permute-start.20 = (bf16[4,128,256]{2,1,0:T(8,128)(2,1)S(1)}, bf16[4,128,256]{2,1,0:T(8,128)(2,1)S(1)}, u32[]{:S(2)}, u32[]{:S(2)}) collective-permute-start(bf16[4,128,256]{2,1,0:T(8,128)(2,1)S(1)} %all_gather.3), channel_id=1, source_target_pairs={{0,480},{32,0},{64,32},{96,64},{128,96},{160,128},{192,160},{224,1... | collective-permute-start | bytes 786440 | tf_op jit(solution)/shard_map/ppermute | solution.py:23
  179.2 0.9 constant_dynamic-update-slice_fusion.10
  180.1 0.2 convolution_bitcast_fusion.7
  180.3 0.2 convolution_bitcast_fusion.4
  180.6 7.0 %collective-permute-done.21 = bf16[4,128,256]{2,1,0:T(8,128)(2,1)S(1)} collective-permute-done((bf16[4,128,256]{2,1,0:T(8,128)(2,1)S(1)}, bf16[4,128,256]{2,1,0:T(8,128)(2,1)S(1)}, u32[]{:S(2)}, u32[]{:S(2)}) %collective-permute-start.21) | collective-permute-done | bytes 262176 | tf_op jit(solution)/shard_map/ppermute | solution.py:23
  187.6 0.2 convolution_bitcast_fusion.5
  187.8 1.4 fusion.65
  189.2 0.2 convolution_bitcast_fusion.3
  189.4 0.2 convolution_bitcast_fusion
  189.6 0.2 convolution_bitcast_fusion.1
  189.9 0.2 convolution_bitcast_fusion.2
  190.1 0.2 fusion.11
  190.5 22.4 %all_to_all.16 = bf16[16,16,8,256]{3,2,1,0:T(8,128)(2,1)S(1)} all-to-all(bf16[16,16,8,256]{3,2,1,0:T(8,128)(2,1)S(1)} %broadcast_in_dim.15), channel_id=1, replica_groups=mesh['zh'=4,'zl'=4,'ylo'=2,'x'=4,'yhi'=2,'core'=2] {'ylo','x','yhi'}, dimensions={0} | all-to-all | bytes 2097152 | tf_op jit(solution)/shard_map/all_to_all | solution.py:17
  213.1 0.9 convolution_convert_fusion
  214.0 0.9 fusion
  214.9 4.3 %collective-permute-start.25 = (bf16[128,1152]{1,0:T(8,128)(2,1)S(1)}, bf16[128,1152]{1,0:T(8,128)(2,1)S(1)}, u32[]{:S(2)}, u32[]{:S(2)}) collective-permute-start(bf16[128,1152]{1,0:T(8,128)(2,1)S(1)} %fusion), channel_id=1, source_target_pairs={{0,0},{1,16},{16,1},{17,17},{2,2},{3,18},{18,3},{19,19},{4,4},{5,2... | collective-permute-start | bytes 884744 | tf_op jit(solution)/shard_map/ppermute | solution.py:128
  219.2 1.9 collective-permute-start.26
  221.1 2.5 %collective-permute-done.25 = bf16[128,1152]{1,0:T(8,128)(2,1)S(1)} collective-permute-done((bf16[128,1152]{1,0:T(8,128)(2,1)S(1)}, bf16[128,1152]{1,0:T(8,128)(2,1)S(1)}, u32[]{:S(2)}, u32[]{:S(2)}) %collective-permute-start.25) | collective-permute-done | bytes 294944 | tf_op jit(solution)/shard_map/ppermute | solution.py:128
  223.6 3.1 %collective-permute-done.26 = bf16[128,1152]{1,0:T(8,128)(2,1)S(1)} collective-permute-done((bf16[128,1152]{1,0:T(8,128)(2,1)S(1)}, bf16[128,1152]{1,0:T(8,128)(2,1)S(1)}, u32[]{:S(2)}, u32[]{:S(2)}) %collective-permute-start.26) | collective-permute-done | bytes 294944 | tf_op jit(solution)/shard_map/ppermute | solution.py:126
  226.7 0.9 convert_add_fusion
  (55 shorter events, 1.4 us)
Async XLA Ops:
  1.1 9.0 %collective-permute-start = (bf16[128,1152]{1,0:T(8,128)(2,1)S(1)}, bf16[128,1152]{1,0:T(8,128)(2,1)S(1)}, u32[]{:S(2)}, u32[]{:S(2)}) collective-permute-start(bf16[128,1152]{1,0:T(8,128)(2,1)S(1)} %convert_element_type.24), channel_id=1, source_target_pairs={{0,0},{1,16},{16,1},{17,17},{2,2},{3,18},{18,3},{19,19},{4,4},{5,2... | collective-permute-start | bytes 884744 | tf_op jit(solution)/shard_map/ppermute | solution.py:74
  10.1 13.1 %collective-permute-start.9 = (bf16[128,1152]{1,0:T(8,128)(2,1)S(1)}, bf16[128,1152]{1,0:T(8,128)(2,1)S(1)}, u32[]{:S(2)}, u32[]{:S(2)}) collective-permute-start(bf16[128,1152]{1,0:T(8,128)(2,1)S(1)} %collective-permute-done), channel_id=1, source_target_pairs={{0,1},{1,0},{2,3},{3,2},{4,5},{5,4},{6,7},{7,6},{8,9},{9,8},{10,11... | collective-permute-start | bytes 884744 | tf_op jit(solution)/shard_map/ppermute | solution.py:75
  12.0 14.8 %collective-permute-start.1 = (bf16[128,1152]{1,0:T(8,128)(2,1)S(1)}, bf16[128,1152]{1,0:T(8,128)(2,1)S(1)}, u32[]{:S(2)}, u32[]{:S(2)}) collective-permute-start(bf16[128,1152]{1,0:T(8,128)(2,1)S(1)} %collective-permute-done), channel_id=1, source_target_pairs={{0,32},{1,481},{32,64},{33,1},{64,96},{65,33},{96,128},{97,65},{12... | collective-permute-start | bytes 884744 | tf_op jit(solution)/shard_map/ppermute | solution.py:33
  23.2 8.7 %copy-start.1 = (bf16[128,1152]{1,0:T(8,128)(2,1)}, bf16[128,1152]{1,0:T(8,128)(2,1)S(1)}, u32[]{:S(2)}) copy-start(bf16[128,1152]{1,0:T(8,128)(2,1)S(1)} %collective-permute-done.9) | copy-start | bytes 884740
  23.2 8.7 %collective-permute-start.10 = (bf16[128,1152]{1,0:T(8,128)(2,1)S(1)}, bf16[128,1152]{1,0:T(8,128)(2,1)S(1)}, u32[]{:S(2)}, u32[]{:S(2)}) collective-permute-start(bf16[128,1152]{1,0:T(8,128)(2,1)S(1)} %collective-permute-done.9), channel_id=1, source_target_pairs={{0,32},{1,481},{32,64},{33,1},{64,96},{65,33},{96,128},{97,65},{12... | collective-permute-start | bytes 884744 | tf_op jit(solution)/shard_map/ppermute | solution.py:33
  26.8 8.7 %collective-permute-start.2 = (bf16[128,1152]{1,0:T(8,128)(2,1)S(1)}, bf16[128,1152]{1,0:T(8,128)(2,1)S(1)}, u32[]{:S(2)}, u32[]{:S(2)}) collective-permute-start(bf16[128,1152]{1,0:T(8,128)(2,1)S(1)} %collective-permute-done.1), channel_id=1, source_target_pairs={{0,32},{1,481},{32,64},{33,1},{64,96},{65,33},{96,128},{97,65},{12... | collective-permute-start | bytes 884744 | tf_op jit(solution)/shard_map/ppermute | solution.py:33
  31.8 8.6 %collective-permute-start.11 = (bf16[128,1152]{1,0:T(8,128)(2,1)S(1)}, bf16[128,1152]{1,0:T(8,128)(2,1)S(1)}, u32[]{:S(2)}, u32[]{:S(2)}) collective-permute-start(bf16[128,1152]{1,0:T(8,128)(2,1)S(1)} %collective-permute-done.10), channel_id=1, source_target_pairs={{0,32},{1,481},{32,64},{33,1},{64,96},{65,33},{96,128},{97,65},{12... | collective-permute-start | bytes 884744 | tf_op jit(solution)/shard_map/ppermute | solution.py:33
  35.5 8.7 %collective-permute-start.3 = (bf16[128,1152]{1,0:T(8,128)(2,1)S(1)}, bf16[128,1152]{1,0:T(8,128)(2,1)S(1)}, u32[]{:S(2)}, u32[]{:S(2)}) collective-permute-start(bf16[128,1152]{1,0:T(8,128)(2,1)S(1)} %collective-permute-done.2), channel_id=1, source_target_pairs={{0,32},{1,481},{32,64},{33,1},{64,96},{65,33},{96,128},{97,65},{12... | collective-permute-start | bytes 884744 | tf_op jit(solution)/shard_map/ppermute | solution.py:33
  40.5 8.7 %collective-permute-start.12 = (bf16[128,1152]{1,0:T(8,128)(2,1)S(1)}, bf16[128,1152]{1,0:T(8,128)(2,1)S(1)}, u32[]{:S(2)}, u32[]{:S(2)}) collective-permute-start(bf16[128,1152]{1,0:T(8,128)(2,1)S(1)} %collective-permute-done.11), channel_id=1, source_target_pairs={{0,32},{1,481},{32,64},{33,1},{64,96},{65,33},{96,128},{97,65},{12... | collective-permute-start | bytes 884744 | tf_op jit(solution)/shard_map/ppermute | solution.py:33
  44.1 8.7 %collective-permute-start.4 = (bf16[128,1152]{1,0:T(8,128)(2,1)S(1)}, bf16[128,1152]{1,0:T(8,128)(2,1)S(1)}, u32[]{:S(2)}, u32[]{:S(2)}) collective-permute-start(bf16[128,1152]{1,0:T(8,128)(2,1)S(1)} %collective-permute-done.3), channel_id=1, source_target_pairs={{0,32},{1,481},{32,64},{33,1},{64,96},{65,33},{96,128},{97,65},{12... | collective-permute-start | bytes 884744 | tf_op jit(solution)/shard_map/ppermute | solution.py:33
  49.2 8.7 %collective-permute-start.14 = (bf16[128,1152]{1,0:T(8,128)(2,1)S(1)}, bf16[128,1152]{1,0:T(8,128)(2,1)S(1)}, u32[]{:S(2)}, u32[]{:S(2)}) collective-permute-start(bf16[128,1152]{1,0:T(8,128)(2,1)S(1)} %collective-permute-done.12), channel_id=1, source_target_pairs={{0,32},{1,481},{32,64},{33,1},{64,96},{65,33},{96,128},{97,65},{12... | collective-permute-start | bytes 884744 | tf_op jit(solution)/shard_map/ppermute | solution.py:33
  52.8 8.7 %collective-permute-start.5 = (bf16[128,1152]{1,0:T(8,128)(2,1)S(1)}, bf16[128,1152]{1,0:T(8,128)(2,1)S(1)}, u32[]{:S(2)}, u32[]{:S(2)}) collective-permute-start(bf16[128,1152]{1,0:T(8,128)(2,1)S(1)} %collective-permute-done.4), channel_id=1, source_target_pairs={{0,32},{1,481},{32,64},{33,1},{64,96},{65,33},{96,128},{97,65},{12... | collective-permute-start | bytes 884744 | tf_op jit(solution)/shard_map/ppermute | solution.py:33
  57.8 8.7 %collective-permute-start.15 = (bf16[128,1152]{1,0:T(8,128)(2,1)S(1)}, bf16[128,1152]{1,0:T(8,128)(2,1)}, u32[]{:S(2)}, u32[]{:S(2)}) collective-permute-start(bf16[128,1152]{1,0:T(8,128)(2,1)S(1)} %collective-permute-done.14), channel_id=1, source_target_pairs={{0,32},{1,481},{32,64},{33,1},{64,96},{65,33},{96,128},{97,65},{12... | collective-permute-start | bytes 884744 | tf_op jit(solution)/shard_map/ppermute | solution.py:33
  61.5 8.7 %collective-permute-start.6 = (bf16[128,1152]{1,0:T(8,128)(2,1)S(1)}, bf16[128,1152]{1,0:T(8,128)(2,1)S(1)}, u32[]{:S(2)}, u32[]{:S(2)}) collective-permute-start(bf16[128,1152]{1,0:T(8,128)(2,1)S(1)} %collective-permute-done.5), channel_id=1, source_target_pairs={{0,32},{1,481},{32,64},{33,1},{64,96},{65,33},{96,128},{97,65},{12... | collective-permute-start | bytes 884744 | tf_op jit(solution)/shard_map/ppermute | solution.py:33
  66.5 8.7 %collective-permute-start.17 = (bf16[128,1152]{1,0:T(8,128)(2,1)}, bf16[128,1152]{1,0:T(8,128)(2,1)}, u32[]{:S(2)}, u32[]{:S(2)}) collective-permute-start(bf16[128,1152]{1,0:T(8,128)(2,1)} %collective-permute-done.15), channel_id=1, source_target_pairs={{0,32},{1,481},{32,64},{33,1},{64,96},{65,33},{96,128},{97,65},{12... | collective-permute-start | bytes 884744 | tf_op jit(solution)/shard_map/ppermute | solution.py:33
  70.1 15.1 %collective-permute-start.7 = (bf16[128,1152]{1,0:T(8,128)(2,1)S(1)}, bf16[128,1152]{1,0:T(8,128)(2,1)S(1)}, u32[]{:S(2)}, u32[]{:S(2)}) collective-permute-start(bf16[128,1152]{1,0:T(8,128)(2,1)S(1)} %collective-permute-done.6), channel_id=1, source_target_pairs={{0,32},{1,481},{32,64},{33,1},{64,96},{65,33},{96,128},{97,65},{12... | collective-permute-start | bytes 884744 | tf_op jit(solution)/shard_map/ppermute | solution.py:33
  75.2 17.9 %collective-permute-start.18 = (bf16[128,1152]{1,0:T(8,128)(2,1)}, bf16[128,1152]{1,0:T(8,128)(2,1)S(1)}, u32[]{:S(2)}, u32[]{:S(2)}) collective-permute-start(bf16[128,1152]{1,0:T(8,128)(2,1)} %collective-permute-done.17), channel_id=1, source_target_pairs={{0,32},{1,481},{32,64},{33,1},{64,96},{65,33},{96,128},{97,65},{12... | collective-permute-start | bytes 884744 | tf_op jit(solution)/shard_map/ppermute | solution.py:33
  78.9 18.2 %collective-permute-start.13 = (bf16[3,128,1152]{2,1,0:T(8,128)(2,1)S(1)}, bf16[3,128,1152]{2,1,0:T(8,128)(2,1)S(1)}, u32[]{:S(2)}, u32[]{:S(2)}) collective-permute-start(bf16[3,128,1152]{2,1,0:T(8,128)(2,1)S(1)} %pad_maximum_fusion.1), channel_id=1, source_target_pairs={{0,1},{1,0},{2,3},{3,2},{4,5},{5,4},{6,7},{7,6},{8,9},{9,8},{10,11... | collective-permute-start | bytes 2654216 | tf_op jit(solution)/shard_map/ppermute | solution.py:37
  85.2 11.4 %collective-permute-start.8 = (bf16[128,1152]{1,0:T(8,128)(2,1)S(1)}, bf16[128,1152]{1,0:T(8,128)(2,1)S(1)}, u32[]{:S(2)}, u32[]{:S(2)}) collective-permute-start(bf16[128,1152]{1,0:T(8,128)(2,1)S(1)} %collective-permute-done.7), channel_id=1, source_target_pairs={{0,32},{1,481},{32,64},{33,1},{64,96},{65,33},{96,128},{97,65},{12... | collective-permute-start | bytes 884744 | tf_op jit(solution)/shard_map/ppermute | solution.py:33
  91.1 6.0 %collective-permute-start.16 = (bf16[2,128,1152]{2,1,0:T(8,128)(2,1)S(1)}, bf16[2,128,1152]{2,1,0:T(8,128)(2,1)S(1)}, u32[]{:S(2)}, u32[]{:S(2)}) collective-permute-start(bf16[2,128,1152]{2,1,0:T(8,128)(2,1)S(1)} %pad_maximum_fusion.2), channel_id=1, source_target_pairs={{0,1},{1,0},{2,3},{3,2},{4,5},{5,4},{6,7},{7,6},{8,9},{9,8},{10,11... | collective-permute-start | bytes 1769480 | tf_op jit(solution)/shard_map/ppermute | solution.py:37
  94.1 4.2 %copy-start.2 = (bf16[128,1152]{1,0:T(8,128)(2,1)S(1)}, bf16[128,1152]{1,0:T(8,128)(2,1)}, u32[]{:S(2)}) copy-start(bf16[128,1152]{1,0:T(8,128)(2,1)} %copy-done.1) | copy-start | bytes 884740
  94.1 4.2 %collective-permute-start.19 = (bf16[2,128,1152]{2,1,0:T(8,128)(2,1)S(1)}, bf16[2,128,1152]{2,1,0:T(8,128)(2,1)S(1)}, u32[]{:S(2)}, u32[]{:S(2)}) collective-permute-start(bf16[2,128,1152]{2,1,0:T(8,128)(2,1)S(1)} %pad_maximum_fusion.3), channel_id=1, source_target_pairs={{0,1},{1,0},{2,3},{3,2},{4,5},{5,4},{6,7},{7,6},{8,9},{9,8},{10,11... | collective-permute-start | bytes 1769480 | tf_op jit(solution)/shard_map/ppermute | solution.py:37
  98.3 2.1 copy-start
  135.4 22.4 %all-to-all-start.1 = ((bf16[16,128,256]{2,1,0:T(8,128)(2,1)}), bf16[16,128,256]{2,1,0:T(8,128)(2,1)S(1)}, u32[]{:S(2)}, u32[]{:S(2)}) async-start(bf16[16,128,256]{2,1,0:T(8,128)(2,1)} %broadcast_in_dim.14), calls=%async_computation.1 | async-start | bytes 2097152 | tf_op jit(solution)/shard_map/all_to_all | solution.py:17
  158.1 29.6 %collective-permute-start.24 = (bf16[4,4,128,256]{3,2,1,0:T(8,128)(2,1)S(1)}, bf16[4,4,128,256]{3,2,1,0:T(8,128)(2,1)}, u32[]{:S(2)}, u32[]{:S(2)}) collective-permute-start(bf16[4,4,128,256]{3,2,1,0:T(8,128)(2,1)S(1)} %pad_maximum_fusion), channel_id=1, source_target_pairs={{0,1},{1,0},{2,3},{3,2},{4,5},{5,4},{6,7},{7,6},{8,9},{9,8},{10,11... | collective-permute-start | bytes 3145736 | tf_op jit(solution)/shard_map/ppermute | solution.py:111
  165.5 13.7 %collective-permute-start.22 = (bf16[2,128,256]{2,1,0:T(8,128)(2,1)}, bf16[2,128,256]{2,1,0:T(8,128)(2,1)}, u32[]{:S(2)}, u32[]{:S(2)}) collective-permute-start(bf16[2,128,256]{2,1,0:T(8,128)(2,1)} %get-tuple-element.36), channel_id=1, source_target_pairs={{0,448},{32,480},{64,0},{96,32},{128,64},{160,96},{192,128},{224,1... | collective-permute-start | bytes 393224 | tf_op jit(solution)/shard_map/ppermute | solution.py:23
  168.8 11.3 %collective-permute-start.23 = (bf16[2,128,256]{2,1,0:T(8,128)(2,1)}, bf16[2,128,256]{2,1,0:T(8,128)(2,1)S(1)}, u32[]{:S(2)}, u32[]{:S(2)}) collective-permute-start(bf16[2,128,256]{2,1,0:T(8,128)(2,1)} %get-tuple-element.35), channel_id=1, source_target_pairs={{0,64},{32,96},{64,128},{96,160},{128,192},{160,224},{192,256},{22... | collective-permute-start | bytes 393224 | tf_op jit(solution)/shard_map/ppermute | solution.py:23
  171.6 16.0 %collective-permute-start.21 = (bf16[4,128,256]{2,1,0:T(8,128)(2,1)S(1)}, bf16[4,128,256]{2,1,0:T(8,128)(2,1)S(1)}, u32[]{:S(2)}, u32[]{:S(2)}) collective-permute-start(bf16[4,128,256]{2,1,0:T(8,128)(2,1)S(1)} %all_gather.3), channel_id=1, source_target_pairs={{0,32},{32,64},{64,96},{96,128},{128,160},{160,192},{192,224},{224... | collective-permute-start | bytes 786440 | tf_op jit(solution)/shard_map/ppermute | solution.py:23
  174.9 15.0 %collective-permute-start.20 = (bf16[4,128,256]{2,1,0:T(8,128)(2,1)S(1)}, bf16[4,128,256]{2,1,0:T(8,128)(2,1)S(1)}, u32[]{:S(2)}, u32[]{:S(2)}) collective-permute-start(bf16[4,128,256]{2,1,0:T(8,128)(2,1)S(1)} %all_gather.3), channel_id=1, source_target_pairs={{0,480},{32,0},{64,32},{96,64},{128,96},{160,128},{192,160},{224,1... | collective-permute-start | bytes 786440 | tf_op jit(solution)/shard_map/ppermute | solution.py:23
  187.8 25.2 %slice-start = ((s8[4718592]{0:T(1024)(128)(4,1)}), s8[4194304]{0:T(1024)(128)(4,1)S(1)}, s32[]{:S(2)}) async-start(s8[4718592]{0:T(1024)(128)(4,1)} %bitcast.130), calls=%async_computation.3 | async-start | bytes 8388608
  189.8 23.2 %slice-start.1 = ((s8[4718592]{0:T(1024)(128)(4,1)}), s8[524288]{0:T(1024)(128)(4,1)S(1)}, s32[]{:S(2)}) async-start(s8[4718592]{0:T(1024)(128)(4,1)} %bitcast.130), calls=%async_computation.4 | async-start | bytes 1048576
  214.9 8.7 %collective-permute-start.25 = (bf16[128,1152]{1,0:T(8,128)(2,1)S(1)}, bf16[128,1152]{1,0:T(8,128)(2,1)S(1)}, u32[]{:S(2)}, u32[]{:S(2)}) collective-permute-start(bf16[128,1152]{1,0:T(8,128)(2,1)S(1)} %fusion), channel_id=1, source_target_pairs={{0,0},{1,16},{16,1},{17,17},{2,2},{3,18},{18,3},{19,19},{4,4},{5,2... | collective-permute-start | bytes 884744 | tf_op jit(solution)/shard_map/ppermute | solution.py:128
  219.2 7.6 %collective-permute-start.26 = (bf16[128,1152]{1,0:T(8,128)(2,1)S(1)}, bf16[128,1152]{1,0:T(8,128)(2,1)S(1)}, u32[]{:S(2)}, u32[]{:S(2)}) collective-permute-start(bf16[128,1152]{1,0:T(8,128)(2,1)S(1)} %convolution_convert_fusion), channel_id=1, source_target_pairs={{0,16},{1,0},{16,17},{17,1},{2,18},{3,2},{18,19},{19,3},{4,20},{5,... | collective-permute-start | bytes 884744 | tf_op jit(solution)/shard_map/ppermute | solution.py:126

commit v9 on v8

--- a/solution.py
+++ b/solution.py
@@ -55,10 +55,14 @@
     )
 
 
+def wide(halves):
+    return jnp.concatenate([halves[0], halves[1]], 1)
+
+
 def turn_to(blocks, start):
-    size = blocks.shape[0]
+    size = blocks.shape[1]
     return lax.dynamic_slice_in_dim(
-        jnp.concatenate([blocks, blocks], 0), start % size, size, 0
+        jnp.concatenate([blocks, blocks], 1), start % size, size, 1
     )
 
 
@@ -73,7 +77,6 @@
     residue = lax.axis_index("zl")
     own = lax.ppermute(rounded, ("ylo", "core"), TURN)
     other = lax.ppermute(own, "core", SWAP)
-    both = jnp.concatenate([own, other], 0)
     near, far = [own], [other]
     for step in range(1, slabs // 2):
         near.append(onward(near[-1]))
@@ -81,21 +84,22 @@
     near.append(onward(near[-1]))
     back = swap(far[1:4]) + swap(far[4:6]) + swap(far[6:])
     half = jnp.concatenate(near[::-1] + back, 0)
-    gram = nt(half, both).reshape(slabs, chips, rows // chips, 2 * rows)
-    gram = gram.transpose(1, 0, 2, 3).reshape(chips, rows, 2 * rows)
+    gram = jnp.stack([nt(half, own), nt(half, other)])
+    gram = gram.reshape(2, slabs, chips, rows // chips, rows)
+    gram = gram.transpose(2, 0, 1, 3, 4).reshape(chips, 2 * rows, rows)
     gram, slab, core, residue = lax.optimization_barrier((gram, slab, core, residue))
     gram = lax.all_to_all(gram, PLANE, 0, 0)
     gram, half, own, slab, core, residue = lax.optimization_barrier(
         (gram, half, own, slab, core, residue)
     )
-    gram = gram.sum(0).reshape(slabs, rows // chips, 2 * rows) / total_cols
-    gram = jnp.where(core == 0, gram, gram[::-1])
+    gram = gram.sum(0).reshape(2, slabs, rows // chips, rows) / total_cols
+    gram = jnp.where(core == 0, gram, gram[:, ::-1])
     gram = turn_to(gram, slabs + slabs // 2 - core - slab)
-    gram_low = gram.astype(jnp.bfloat16)
-    gram, gram_low = gram.reshape(rows, 2 * rows), gram_low.reshape(rows, 2 * rows)
-    panel = share(gram_low, chips).reshape(chips, slabs, rows // chips, 2 * rows)
-    panel = panel.transpose(1, 0, 2, 3).reshape(groups, steps, rows, 2 * rows)
-    here = lax.all_gather(gram_low, "zh", axis=0)
+    gram_low = gram.astype(jnp.bfloat16).reshape(2 * rows, rows)
+    gram = wide(gram.reshape(2, rows, rows))
+    panel = share(gram_low, chips).reshape(chips, 2, slabs, rows // chips, rows)
+    panel = panel.transpose(2, 0, 3, 1, 4).reshape(groups, steps, rows, 2 * rows)
+    here = lax.all_gather(gram_low, "zh", axis=0).reshape(groups, 2, rows, rows)
     panel, _ = lax.optimization_barrier((panel, here))
     cut = groups // 2
     left = (
@@ -114,14 +118,16 @@
     )
     square = 0.0
     for place in range(steps):
-        square = square + mix(left[place][:, :, :rows], right_own[place])
+        square = square + mix(left[place][:, 0], right_own[place])
     for place in range(steps):
-        square = square + mix(left[place][:, :, rows:], right_other[place])
+        square = square + mix(left[place][:, 1], right_other[place])
     poly = (-4.775 * gram + 2.0315 * square).astype(jnp.bfloat16)
-    poly = poly.reshape(slabs, rows // chips, 2 * rows)
+    poly = poly.reshape(slabs, rows // chips, 2, rows).transpose(2, 0, 1, 3)
     poly = turn_to(poly, slabs // 2 + slab + core)
-    poly = jnp.where(core == 0, poly, poly[::-1])
-    panel = share(poly, chips).transpose(1, 0, 2, 3).reshape(slabs * rows, 2 * rows)
+    poly = jnp.where(core == 0, poly, poly[:, ::-1])
+    panel = share(poly.reshape(2 * rows, rows), chips)
+    panel = panel.reshape(chips, 2, slabs, rows // chips, rows)
+    panel = panel.transpose(2, 0, 3, 1, 4).reshape(slabs * rows, 2 * rows)
     away = tn(panel[:, rows:], half).astype(jnp.bfloat16)
     away = lax.ppermute(away, ("ylo", "core"), CROSS)
     stay = tn(panel[:, :rows], half) + 3.4445 * own.astype(jnp.float32)

time: 229 us -> 234 us (1.022)
  matrix products: 4.95 us -> 8 us
  transfers between devices with their start and end apart: 28 -> 28, of which waited for: 11 -> 12; matrix products, arithmetic and copies ran while one was open for 3% -> 4% of each run, Pallas kernels for 0% -> 0%
where the time goes in v9:
time: 234 us; the launch traced here: 232 us
  starting transfers between devices  116 us (50%)
  blocking collectives  73.9 us (32%)
  waiting for transfers between devices  21.4 us (9%)
  matrix products  8 us (3%)
  local copies, waits for them, and re-layouts  7.44 us (3%)
  other arithmetic  4.91 us (2%)
    ppermute x15, starting transfers between devices, onward(): return lax.ppermute(piece, LINE + ('core',), pairs)  68.1 us
    all_to_all x1, blocking collectives, per_device(): gram = lax.all_to_all(gram, PLANE, 0, 0)  33.5 us
    all_to_all x1, blocking collectives, share(): return lax.all_to_all(copies, PLANE, 0, 0)  22.2 us
    all_gather x1, blocking collectives, per_device(): here = lax.all_gather(gram_low, 'zh', axis=0).reshape(groups, 2, rows, rows)  18.1 us
    ppermute x4, starting transfers between devices, along(): return lax.ppermute(piece, LINE, pairs)  12.7 us
    ppermute x3, starting transfers between devices, swap(): return list(lax.ppermute(jnp.stack(pieces), 'core', SWAP))  10.7 us
    ppermute x1, starting transfers between devices, per_device(): right_other = lax.ppermute(jnp.stack(right_own), 'core', SWAP)  7.14 us
    ppermute x4, waiting for transfers between devices, along(): return lax.ppermute(piece, LINE, pairs)  7.02 us
  transfers between devices with their start and end apart: 28, of which 12 were waited for; matrix products, arithmetic and copies ran while one was open for 4% of the time, Pallas kernels for 0%

profile of v9, /device:TPU:1, one launch (start us, length us, event | category | flops | bytes accessed | tf_op | source)
XLA Modules:
  0.0 232.3 jit_solution(15525462739467500972)
XLA Ops:
  0.0 1.1 convert_element_type.24
  1.1 4.6 %collective-permute-start = (bf16[128,1152]{1,0:T(8,128)(2,1)S(1)}, bf16[128,1152]{1,0:T(8,128)(2,1)S(1)}, u32[]{:S(2)}, u32[]{:S(2)}) collective-permute-start(bf16[128,1152]{1,0:T(8,128)(2,1)S(1)} %convert_element_type.24), channel_id=1, source_target_pairs={{0,0},{1,16},{16,1},{17,17},{2,2},{3,18},{18,3},{19,19},{4,4},{5,2... | collective-permute-start | bytes 884744 | tf_op jit(solution)/shard_map/ppermute | solution.py:78
  5.7 4.4 %collective-permute-done = bf16[128,1152]{1,0:T(8,128)(2,1)S(1)} collective-permute-done((bf16[128,1152]{1,0:T(8,128)(2,1)S(1)}, bf16[128,1152]{1,0:T(8,128)(2,1)S(1)}, u32[]{:S(2)}, u32[]{:S(2)}) %collective-permute-start) | collective-permute-done | bytes 294944 | tf_op jit(solution)/shard_map/ppermute | solution.py:78
  10.1 1.9 collective-permute-start.9
  12.0 11.1 %collective-permute-start.1 = (bf16[128,1152]{1,0:T(8,128)(2,1)S(1)}, bf16[128,1152]{1,0:T(8,128)(2,1)S(1)}, u32[]{:S(2)}, u32[]{:S(2)}) collective-permute-start(bf16[128,1152]{1,0:T(8,128)(2,1)S(1)} %collective-permute-done), channel_id=1, source_target_pairs={{0,32},{1,481},{32,64},{33,1},{64,96},{65,33},{96,128},{97,65},{12... | collective-permute-start | bytes 884744 | tf_op jit(solution)/shard_map/ppermute | solution.py:33
  23.2 2.6 %collective-permute-start.10 = (bf16[128,1152]{1,0:T(8,128)(2,1)S(1)}, bf16[128,1152]{1,0:T(8,128)(2,1)S(1)}, u32[]{:S(2)}, u32[]{:S(2)}) collective-permute-start(bf16[128,1152]{1,0:T(8,128)(2,1)S(1)} %collective-permute-done.9), channel_id=1, source_target_pairs={{0,32},{1,481},{32,64},{33,1},{64,96},{65,33},{96,128},{97,65},{12... | collective-permute-start | bytes 884744 | tf_op jit(solution)/shard_map/ppermute | solution.py:33
  25.8 1.0 collective-permute-done.1
  26.8 5.0 %collective-permute-start.2 = (bf16[128,1152]{1,0:T(8,128)(2,1)S(1)}, bf16[128,1152]{1,0:T(8,128)(2,1)S(1)}, u32[]{:S(2)}, u32[]{:S(2)}) collective-permute-start(bf16[128,1152]{1,0:T(8,128)(2,1)S(1)} %collective-permute-done.1), channel_id=1, source_target_pairs={{0,32},{1,481},{32,64},{33,1},{64,96},{65,33},{96,128},{97,65},{12... | collective-permute-start | bytes 884744 | tf_op jit(solution)/shard_map/ppermute | solution.py:33
  31.8 3.1 %collective-permute-start.11 = (bf16[128,1152]{1,0:T(8,128)(2,1)S(1)}, bf16[128,1152]{1,0:T(8,128)(2,1)S(1)}, u32[]{:S(2)}, u32[]{:S(2)}) collective-permute-start(bf16[128,1152]{1,0:T(8,128)(2,1)S(1)} %collective-permute-done.10), channel_id=1, source_target_pairs={{0,32},{1,481},{32,64},{33,1},{64,96},{65,33},{96,128},{97,65},{12... | collective-permute-start | bytes 884744 | tf_op jit(solution)/shard_map/ppermute | solution.py:33
  35.0 0.5 collective-permute-done.2
  35.5 5.0 %collective-permute-start.3 = (bf16[128,1152]{1,0:T(8,128)(2,1)S(1)}, bf16[128,1152]{1,0:T(8,128)(2,1)S(1)}, u32[]{:S(2)}, u32[]{:S(2)}) collective-permute-start(bf16[128,1152]{1,0:T(8,128)(2,1)S(1)} %collective-permute-done.2), channel_id=1, source_target_pairs={{0,32},{1,481},{32,64},{33,1},{64,96},{65,33},{96,128},{97,65},{12... | collective-permute-start | bytes 884744 | tf_op jit(solution)/shard_map/ppermute | solution.py:33
  40.5 3.1 %collective-permute-start.12 = (bf16[128,1152]{1,0:T(8,128)(2,1)S(1)}, bf16[128,1152]{1,0:T(8,128)(2,1)S(1)}, u32[]{:S(2)}, u32[]{:S(2)}) collective-permute-start(bf16[128,1152]{1,0:T(8,128)(2,1)S(1)} %collective-permute-done.11), channel_id=1, source_target_pairs={{0,32},{1,481},{32,64},{33,1},{64,96},{65,33},{96,128},{97,65},{12... | collective-permute-start | bytes 884744 | tf_op jit(solution)/shard_map/ppermute | solution.py:33
  43.6 0.5 collective-permute-done.3
  44.1 5.0 %collective-permute-start.4 = (bf16[128,1152]{1,0:T(8,128)(2,1)S(1)}, bf16[128,1152]{1,0:T(8,128)(2,1)S(1)}, u32[]{:S(2)}, u32[]{:S(2)}) collective-permute-start(bf16[128,1152]{1,0:T(8,128)(2,1)S(1)} %collective-permute-done.3), channel_id=1, source_target_pairs={{0,32},{1,481},{32,64},{33,1},{64,96},{65,33},{96,128},{97,65},{12... | collective-permute-start | bytes 884744 | tf_op jit(solution)/shard_map/ppermute | solution.py:33
  49.2 3.1 %collective-permute-start.14 = (bf16[128,1152]{1,0:T(8,128)(2,1)S(1)}, bf16[128,1152]{1,0:T(8,128)(2,1)S(1)}, u32[]{:S(2)}, u32[]{:S(2)}) collective-permute-start(bf16[128,1152]{1,0:T(8,128)(2,1)S(1)} %collective-permute-done.12), channel_id=1, source_target_pairs={{0,32},{1,481},{32,64},{33,1},{64,96},{65,33},{96,128},{97,65},{12... | collective-permute-start | bytes 884744 | tf_op jit(solution)/shard_map/ppermute | solution.py:33
  52.3 0.5 collective-permute-done.4
  52.8 5.0 %collective-permute-start.5 = (bf16[128,1152]{1,0:T(8,128)(2,1)S(1)}, bf16[128,1152]{1,0:T(8,128)(2,1)S(1)}, u32[]{:S(2)}, u32[]{:S(2)}) collective-permute-start(bf16[128,1152]{1,0:T(8,128)(2,1)S(1)} %collective-permute-done.4), channel_id=1, source_target_pairs={{0,32},{1,481},{32,64},{33,1},{64,96},{65,33},{96,128},{97,65},{12... | collective-permute-start | bytes 884744 | tf_op jit(solution)/shard_map/ppermute | solution.py:33
  57.8 3.1 %collective-permute-start.15 = (bf16[128,1152]{1,0:T(8,128)(2,1)S(1)}, bf16[128,1152]{1,0:T(8,128)(2,1)}, u32[]{:S(2)}, u32[]{:S(2)}) collective-permute-start(bf16[128,1152]{1,0:T(8,128)(2,1)S(1)} %collective-permute-done.14), channel_id=1, source_target_pairs={{0,32},{1,481},{32,64},{33,1},{64,96},{65,33},{96,128},{97,65},{12... | collective-permute-start | bytes 884744 | tf_op jit(solution)/shard_map/ppermute | solution.py:33
  61.0 0.5 collective-permute-done.5
  61.5 5.0 %collective-permute-start.6 = (bf16[128,1152]{1,0:T(8,128)(2,1)S(1)}, bf16[128,1152]{1,0:T(8,128)(2,1)S(1)}, u32[]{:S(2)}, u32[]{:S(2)}) collective-permute-start(bf16[128,1152]{1,0:T(8,128)(2,1)S(1)} %collective-permute-done.5), channel_id=1, source_target_pairs={{0,32},{1,481},{32,64},{33,1},{64,96},{65,33},{96,128},{97,65},{12... | collective-permute-start | bytes 884744 | tf_op jit(solution)/shard_map/ppermute | solution.py:33
  66.5 3.3 %collective-permute-start.17 = (bf16[128,1152]{1,0:T(8,128)(2,1)}, bf16[128,1152]{1,0:T(8,128)(2,1)}, u32[]{:S(2)}, u32[]{:S(2)}) collective-permute-start(bf16[128,1152]{1,0:T(8,128)(2,1)} %collective-permute-done.15), channel_id=1, source_target_pairs={{0,32},{1,481},{32,64},{33,1},{64,96},{65,33},{96,128},{97,65},{12... | collective-permute-start | bytes 884744 | tf_op jit(solution)/shard_map/ppermute | solution.py:33
  69.8 0.4 collective-permute-done.6
  70.1 5.0 %collective-permute-start.7 = (bf16[128,1152]{1,0:T(8,128)(2,1)S(1)}, bf16[128,1152]{1,0:T(8,128)(2,1)S(1)}, u32[]{:S(2)}, u32[]{:S(2)}) collective-permute-start(bf16[128,1152]{1,0:T(8,128)(2,1)S(1)} %collective-permute-done.6), channel_id=1, source_target_pairs={{0,32},{1,481},{32,64},{33,1},{64,96},{65,33},{96,128},{97,65},{12... | collective-permute-start | bytes 884744 | tf_op jit(solution)/shard_map/ppermute | solution.py:33
  75.2 3.6 %collective-permute-start.18 = (bf16[128,1152]{1,0:T(8,128)(2,1)}, bf16[128,1152]{1,0:T(8,128)(2,1)S(1)}, u32[]{:S(2)}, u32[]{:S(2)}) collective-permute-start(bf16[128,1152]{1,0:T(8,128)(2,1)} %collective-permute-done.17), channel_id=1, source_target_pairs={{0,32},{1,481},{32,64},{33,1},{64,96},{65,33},{96,128},{97,65},{12... | collective-permute-start | bytes 884744 | tf_op jit(solution)/shard_map/ppermute | solution.py:33
  78.9 6.4 %collective-permute-start.13 = (bf16[3,128,1152]{2,1,0:T(8,128)(2,1)S(1)}, bf16[3,128,1152]{2,1,0:T(8,128)(2,1)S(1)}, u32[]{:S(2)}, u32[]{:S(2)}) collective-permute-start(bf16[3,128,1152]{2,1,0:T(8,128)(2,1)S(1)} %pad_maximum_fusion.2), channel_id=1, source_target_pairs={{0,1},{1,0},{2,3},{3,2},{4,5},{5,4},{6,7},{7,6},{8,9},{9,8},{10,11... | collective-permute-start | bytes 2654216 | tf_op jit(solution)/shard_map/ppermute | solution.py:37
  85.2 4.9 %collective-permute-start.8 = (bf16[128,1152]{1,0:T(8,128)(2,1)S(1)}, bf16[128,1152]{1,0:T(8,128)(2,1)S(1)}, u32[]{:S(2)}, u32[]{:S(2)}) collective-permute-start(bf16[128,1152]{1,0:T(8,128)(2,1)S(1)} %collective-permute-done.7), channel_id=1, source_target_pairs={{0,32},{1,481},{32,64},{33,1},{64,96},{65,33},{96,128},{97,65},{12... | collective-permute-start | bytes 884744 | tf_op jit(solution)/shard_map/ppermute | solution.py:33
  90.1 1.1 pad_maximum_fusion.3
  91.2 1.9 collective-permute-start.16
  93.2 1.0 pad_maximum_fusion.4
  94.2 2.4 %collective-permute-start.19 = (bf16[2,128,1152]{2,1,0:T(8,128)(2,1)S(1)}, bf16[2,128,1152]{2,1,0:T(8,128)(2,1)S(1)}, u32[]{:S(2)}, u32[]{:S(2)}) collective-permute-start(bf16[2,128,1152]{2,1,0:T(8,128)(2,1)S(1)} %pad_maximum_fusion.4), channel_id=1, source_target_pairs={{0,1},{1,0},{2,3},{3,2},{4,5},{5,4},{6,7},{7,6},{8,9},{9,8},{10,11... | collective-permute-start | bytes 1769480 | tf_op jit(solution)/shard_map/ppermute | solution.py:37
  97.2 1.0 collective-permute-done.19
  98.3 1.4 fusion.56
  99.7 1.4 fusion.55
  101.1 0.2 pad_maximum_fusion
  101.3 0.3 copy.33
  101.6 33.5 %all_to_all.15 = f32[16,256,128]{2,1,0:T(8,128)S(1)} all-to-all(f32[16,256,128]{2,1,0:T(8,128)S(1)} %bitcast.171), channel_id=1, replica_groups=mesh['zh'=4,'zl'=4,'ylo'=2,'x'=4,'yhi'=2,'core'=2] {'ylo','x','yhi'}, dimensions={0} | all-to-all | bytes 4194304 | tf_op jit(solution)/shard_map/all_to_all | solution.py:91
  135.3 1.2 broadcast_in_dim.15
  136.5 4.2 %all-to-all-start.1 = ((bf16[16,256,128]{2,1,0:T(8,128)(2,1)}), bf16[16,256,128]{2,1,0:T(8,128)(2,1)S(1)}, u32[]{:S(2)}, u32[]{:S(2)}) async-start(bf16[16,256,128]{2,1,0:T(8,128)(2,1)} %broadcast_in_dim.15), calls=%async_computation.1 | async-start | bytes 2097152 | tf_op jit(solution)/shard_map/all_to_all | solution.py:17
  140.8 18.1 %all_gather.3 = bf16[4,256,128]{2,1,0:T(8,128)(2,1)S(1)} all-gather(bf16[1,256,128]{2,1,0:T(8,128)(2,1)S(1)} %bitcast.182), channel_id=1, replica_groups=mesh['zh'=4,'zl'=4,'ylo'=2,'x'=4,'yhi'=2,'core'=2] {'zh'}, dimensions={0}, use_global_device_ids=true | all-gather | bytes 327680 | tf_op jit(solution)/shard_map/all_gather | solution.py:102
  159.0 1.9 collective-permute-start.21
  160.9 4.6 %collective-permute-start.20 = (bf16[4,2,128,128]{3,2,0,1:T(8,128)(2,1)S(1)}, bf16[4,2,128,128]{3,2,0,1:T(8,128)(2,1)}, u32[]{:S(2)}, u32[]{:S(2)}) collective-permute-start(bf16[4,2,128,128]{3,2,0,1:T(8,128)(2,1)S(1)} %copy.24), channel_id=1, source_target_pairs={{0,480},{32,0},{64,32},{96,64},{128,96},{160,128},{192,160},{224,1... | collective-permute-start | bytes 786440 | tf_op jit(solution)/shard_map/ppermute | solution.py:23
  165.6 0.3 copy.25
  166.1 7.1 %collective-permute-start.24 = (bf16[4,4,128,256]{3,2,1,0:T(8,128)(2,1)S(1)}, bf16[4,4,128,256]{3,2,1,0:T(8,128)(2,1)}, u32[]{:S(2)}, u32[]{:S(2)}) collective-permute-start(bf16[4,4,128,256]{3,2,1,0:T(8,128)(2,1)S(1)} %pad_maximum_fusion.1), channel_id=1, source_target_pairs={{0,1},{1,0},{2,3},{3,2},{4,5},{5,4},{6,7},{7,6},{8,9},{9,8},{10,11... | collective-permute-start | bytes 3145736 | tf_op jit(solution)/shard_map/ppermute | solution.py:115
  173.3 0.7 copy.28
  173.9 2.5 %collective-permute-start.22 = (bf16[2,2,128,128]{3,2,0,1:T(8,128)(2,1)}, bf16[2,2,128,128]{3,2,0,1:T(8,128)(2,1)}, u32[]{:S(2)}, u32[]{:S(2)}) collective-permute-start(bf16[2,2,128,128]{3,2,0,1:T(8,128)(2,1)} %copy.28), channel_id=1, source_target_pairs={{0,448},{32,480},{64,0},{96,32},{128,64},{160,96},{192,128},{224,1... | collective-permute-start | bytes 393224 | tf_op jit(solution)/shard_map/ppermute | solution.py:23
  176.4 0.7 copy.29
  177.1 3.7 %collective-permute-start.23 = (bf16[2,2,128,128]{3,2,0,1:T(8,128)(2,1)}, bf16[2,2,128,128]{3,2,0,1:T(8,128)(2,1)}, u32[]{:S(2)}, u32[]{:S(2)}) collective-permute-start(bf16[2,2,128,128]{3,2,0,1:T(8,128)(2,1)} %copy.29), channel_id=1, source_target_pairs={{0,64},{32,96},{64,128},{96,160},{128,192},{160,224},{192,256},{22... | collective-permute-start | bytes 393224 | tf_op jit(solution)/shard_map/ppermute | solution.py:23
  180.8 2.7 %collective-permute-done.22 = bf16[2,2,128,128]{3,2,0,1:T(8,128)(2,1)} collective-permute-done((bf16[2,2,128,128]{3,2,0,1:T(8,128)(2,1)}, bf16[2,2,128,128]{3,2,0,1:T(8,128)(2,1)}, u32[]{:S(2)}, u32[]{:S(2)}) %collective-permute-start.22) | collective-permute-done | bytes 131104 | tf_op jit(solution)/shard_map/ppermute | solution.py:23
  183.5 0.9 constant_dynamic-update-slice_fusion.10
  184.5 4.3 %collective-permute-done.23 = bf16[2,2,128,128]{3,2,0,1:T(8,128)(2,1)} collective-permute-done((bf16[2,2,128,128]{3,2,0,1:T(8,128)(2,1)}, bf16[2,2,128,128]{3,2,0,1:T(8,128)(2,1)}, u32[]{:S(2)}, u32[]{:S(2)}) %collective-permute-start.23) | collective-permute-done | bytes 131104 | tf_op jit(solution)/shard_map/ppermute | solution.py:23
  188.7 0.9 constant_dynamic-update-slice_fusion.9
  189.9 0.2 convolution_bitcast_fusion.5
  190.3 1.4 fusion.53
  192.3 1.1 convolution_bitcast_fusion.2
  193.5 1.1 fusion.11
  195.0 22.2 %all_to_all.16 = bf16[16,256,128]{2,1,0:T(8,128)(2,1)S(1)} all-to-all(bf16[16,256,128]{2,1,0:T(8,128)(2,1)S(1)} %broadcast_in_dim.17), channel_id=1, replica_groups=mesh['zh'=4,'zl'=4,'ylo'=2,'x'=4,'yhi'=2,'core'=2] {'ylo','x','yhi'}, dimensions={0} | all-to-all | bytes 2097152 | tf_op jit(solution)/shard_map/all_to_all | solution.py:17
  217.3 0.3 copy.32
  217.6 0.9 convolution_convert_fusion
  218.5 0.9 fusion
  219.3 4.5 %collective-permute-start.25 = (bf16[128,1152]{1,0:T(8,128)(2,1)S(1)}, bf16[128,1152]{1,0:T(8,128)(2,1)S(1)}, u32[]{:S(2)}, u32[]{:S(2)}) collective-permute-start(bf16[128,1152]{1,0:T(8,128)(2,1)S(1)} %fusion), channel_id=1, source_target_pairs={{0,0},{1,16},{16,1},{17,17},{2,2},{3,18},{18,3},{19,19},{4,4},{5,2... | collective-permute-start | bytes 884744 | tf_op jit(solution)/shard_map/ppermute | solution.py:134
  223.8 1.9 collective-permute-start.26
  225.8 2.5 %collective-permute-done.25 = bf16[128,1152]{1,0:T(8,128)(2,1)S(1)} collective-permute-done((bf16[128,1152]{1,0:T(8,128)(2,1)S(1)}, bf16[128,1152]{1,0:T(8,128)(2,1)S(1)}, u32[]{:S(2)}, u32[]{:S(2)}) %collective-permute-start.25) | collective-permute-done | bytes 294944 | tf_op jit(solution)/shard_map/ppermute | solution.py:134
  228.3 3.1 %collective-permute-done.26 = bf16[128,1152]{1,0:T(8,128)(2,1)S(1)} collective-permute-done((bf16[128,1152]{1,0:T(8,128)(2,1)S(1)}, bf16[128,1152]{1,0:T(8,128)(2,1)S(1)}, u32[]{:S(2)}, u32[]{:S(2)}) %collective-permute-start.26) | collective-permute-done | bytes 294944 | tf_op jit(solution)/shard_map/ppermute | solution.py:132
  231.4 0.9 convert_add_fusion
  (59 shorter events, 2.4 us)
Async XLA Ops:
  1.1 9.0 %collective-permute-start = (bf16[128,1152]{1,0:T(8,128)(2,1)S(1)}, bf16[128,1152]{1,0:T(8,128)(2,1)S(1)}, u32[]{:S(2)}, u32[]{:S(2)}) collective-permute-start(bf16[128,1152]{1,0:T(8,128)(2,1)S(1)} %convert_element_type.24), channel_id=1, source_target_pairs={{0,0},{1,16},{16,1},{17,17},{2,2},{3,18},{18,3},{19,19},{4,4},{5,2... | collective-permute-start | bytes 884744 | tf_op jit(solution)/shard_map/ppermute | solution.py:78
  10.1 13.1 %collective-permute-start.9 = (bf16[128,1152]{1,0:T(8,128)(2,1)S(1)}, bf16[128,1152]{1,0:T(8,128)(2,1)S(1)}, u32[]{:S(2)}, u32[]{:S(2)}) collective-permute-start(bf16[128,1152]{1,0:T(8,128)(2,1)S(1)} %collective-permute-done), channel_id=1, source_target_pairs={{0,1},{1,0},{2,3},{3,2},{4,5},{5,4},{6,7},{7,6},{8,9},{9,8},{10,11... | collective-permute-start | bytes 884744 | tf_op jit(solution)/shard_map/ppermute | solution.py:79
  12.0 14.8 %collective-permute-start.1 = (bf16[128,1152]{1,0:T(8,128)(2,1)S(1)}, bf16[128,1152]{1,0:T(8,128)(2,1)S(1)}, u32[]{:S(2)}, u32[]{:S(2)}) collective-permute-start(bf16[128,1152]{1,0:T(8,128)(2,1)S(1)} %collective-permute-done), channel_id=1, source_target_pairs={{0,32},{1,481},{32,64},{33,1},{64,96},{65,33},{96,128},{97,65},{12... | collective-permute-start | bytes 884744 | tf_op jit(solution)/shard_map/ppermute | solution.py:33
  23.2 8.7 %collective-permute-start.10 = (bf16[128,1152]{1,0:T(8,128)(2,1)S(1)}, bf16[128,1152]{1,0:T(8,128)(2,1)S(1)}, u32[]{:S(2)}, u32[]{:S(2)}) collective-permute-start(bf16[128,1152]{1,0:T(8,128)(2,1)S(1)} %collective-permute-done.9), channel_id=1, source_target_pairs={{0,32},{1,481},{32,64},{33,1},{64,96},{65,33},{96,128},{97,65},{12... | collective-permute-start | bytes 884744 | tf_op jit(solution)/shard_map/ppermute | solution.py:33
  26.8 8.7 %collective-permute-start.2 = (bf16[128,1152]{1,0:T(8,128)(2,1)S(1)}, bf16[128,1152]{1,0:T(8,128)(2,1)S(1)}, u32[]{:S(2)}, u32[]{:S(2)}) collective-permute-start(bf16[128,1152]{1,0:T(8,128)(2,1)S(1)} %collective-permute-done.1), channel_id=1, source_target_pairs={{0,32},{1,481},{32,64},{33,1},{64,96},{65,33},{96,128},{97,65},{12... | collective-permute-start | bytes 884744 | tf_op jit(solution)/shard_map/ppermute | solution.py:33
  31.8 8.7 %collective-permute-start.11 = (bf16[128,1152]{1,0:T(8,128)(2,1)S(1)}, bf16[128,1152]{1,0:T(8,128)(2,1)S(1)}, u32[]{:S(2)}, u32[]{:S(2)}) collective-permute-start(bf16[128,1152]{1,0:T(8,128)(2,1)S(1)} %collective-permute-done.10), channel_id=1, source_target_pairs={{0,32},{1,481},{32,64},{33,1},{64,96},{65,33},{96,128},{97,65},{12... | collective-permute-start | bytes 884744 | tf_op jit(solution)/shard_map/ppermute | solution.py:33
  35.5 8.7 %collective-permute-start.3 = (bf16[128,1152]{1,0:T(8,128)(2,1)S(1)}, bf16[128,1152]{1,0:T(8,128)(2,1)S(1)}, u32[]{:S(2)}, u32[]{:S(2)}) collective-permute-start(bf16[128,1152]{1,0:T(8,128)(2,1)S(1)} %collective-permute-done.2), channel_id=1, source_target_pairs={{0,32},{1,481},{32,64},{33,1},{64,96},{65,33},{96,128},{97,65},{12... | collective-permute-start | bytes 884744 | tf_op jit(solution)/shard_map/ppermute | solution.py:33
  40.5 8.7 %collective-permute-start.12 = (bf16[128,1152]{1,0:T(8,128)(2,1)S(1)}, bf16[128,1152]{1,0:T(8,128)(2,1)S(1)}, u32[]{:S(2)}, u32[]{:S(2)}) collective-permute-start(bf16[128,1152]{1,0:T(8,128)(2,1)S(1)} %collective-permute-done.11), channel_id=1, source_target_pairs={{0,32},{1,481},{32,64},{33,1},{64,96},{65,33},{96,128},{97,65},{12... | collective-permute-start | bytes 884744 | tf_op jit(solution)/shard_map/ppermute | solution.py:33
  44.1 8.7 %collective-permute-start.4 = (bf16[128,1152]{1,0:T(8,128)(2,1)S(1)}, bf16[128,1152]{1,0:T(8,128)(2,1)S(1)}, u32[]{:S(2)}, u32[]{:S(2)}) collective-permute-start(bf16[128,1152]{1,0:T(8,128)(2,1)S(1)} %collective-permute-done.3), channel_id=1, source_target_pairs={{0,32},{1,481},{32,64},{33,1},{64,96},{65,33},{96,128},{97,65},{12... | collective-permute-start | bytes 884744 | tf_op jit(solution)/shard_map/ppermute | solution.py:33
  49.2 8.7 %collective-permute-start.14 = (bf16[128,1152]{1,0:T(8,128)(2,1)S(1)}, bf16[128,1152]{1,0:T(8,128)(2,1)S(1)}, u32[]{:S(2)}, u32[]{:S(2)}) collective-permute-start(bf16[128,1152]{1,0:T(8,128)(2,1)S(1)} %collective-permute-done.12), channel_id=1, source_target_pairs={{0,32},{1,481},{32,64},{33,1},{64,96},{65,33},{96,128},{97,65},{12... | collective-permute-start | bytes 884744 | tf_op jit(solution)/shard_map/ppermute | solution.py:33
  52.8 8.7 %collective-permute-start.5 = (bf16[128,1152]{1,0:T(8,128)(2,1)S(1)}, bf16[128,1152]{1,0:T(8,128)(2,1)S(1)}, u32[]{:S(2)}, u32[]{:S(2)}) collective-permute-start(bf16[128,1152]{1,0:T(8,128)(2,1)S(1)} %collective-permute-done.4), channel_id=1, source_target_pairs={{0,32},{1,481},{32,64},{33,1},{64,96},{65,33},{96,128},{97,65},{12... | collective-permute-start | bytes 884744 | tf_op jit(solution)/shard_map/ppermute | solution.py:33
  57.8 11.9 %copy-start.1 = (bf16[128,1152]{1,0:T(8,128)(2,1)}, bf16[128,1152]{1,0:T(8,128)(2,1)S(1)}, u32[]{:S(2)}) copy-start(bf16[128,1152]{1,0:T(8,128)(2,1)S(1)} %collective-permute-done.14) | copy-start | bytes 884740
  57.8 8.6 %collective-permute-start.15 = (bf16[128,1152]{1,0:T(8,128)(2,1)S(1)}, bf16[128,1152]{1,0:T(8,128)(2,1)}, u32[]{:S(2)}, u32[]{:S(2)}) collective-permute-start(bf16[128,1152]{1,0:T(8,128)(2,1)S(1)} %collective-permute-done.14), channel_id=1, source_target_pairs={{0,32},{1,481},{32,64},{33,1},{64,96},{65,33},{96,128},{97,65},{12... | collective-permute-start | bytes 884744 | tf_op jit(solution)/shard_map/ppermute | solution.py:33
  61.5 8.7 %collective-permute-start.6 = (bf16[128,1152]{1,0:T(8,128)(2,1)S(1)}, bf16[128,1152]{1,0:T(8,128)(2,1)S(1)}, u32[]{:S(2)}, u32[]{:S(2)}) collective-permute-start(bf16[128,1152]{1,0:T(8,128)(2,1)S(1)} %collective-permute-done.5), channel_id=1, source_target_pairs={{0,32},{1,481},{32,64},{33,1},{64,96},{65,33},{96,128},{97,65},{12... | collective-permute-start | bytes 884744 | tf_op jit(solution)/shard_map/ppermute | solution.py:33
  66.5 8.7 %collective-permute-start.17 = (bf16[128,1152]{1,0:T(8,128)(2,1)}, bf16[128,1152]{1,0:T(8,128)(2,1)}, u32[]{:S(2)}, u32[]{:S(2)}) collective-permute-start(bf16[128,1152]{1,0:T(8,128)(2,1)} %collective-permute-done.15), channel_id=1, source_target_pairs={{0,32},{1,481},{32,64},{33,1},{64,96},{65,33},{96,128},{97,65},{12... | collective-permute-start | bytes 884744 | tf_op jit(solution)/shard_map/ppermute | solution.py:33
  70.1 15.1 %collective-permute-start.7 = (bf16[128,1152]{1,0:T(8,128)(2,1)S(1)}, bf16[128,1152]{1,0:T(8,128)(2,1)S(1)}, u32[]{:S(2)}, u32[]{:S(2)}) collective-permute-start(bf16[128,1152]{1,0:T(8,128)(2,1)S(1)} %collective-permute-done.6), channel_id=1, source_target_pairs={{0,32},{1,481},{32,64},{33,1},{64,96},{65,33},{96,128},{97,65},{12... | collective-permute-start | bytes 884744 | tf_op jit(solution)/shard_map/ppermute | solution.py:33
  75.2 18.0 %collective-permute-start.18 = (bf16[128,1152]{1,0:T(8,128)(2,1)}, bf16[128,1152]{1,0:T(8,128)(2,1)S(1)}, u32[]{:S(2)}, u32[]{:S(2)}) collective-permute-start(bf16[128,1152]{1,0:T(8,128)(2,1)} %collective-permute-done.17), channel_id=1, source_target_pairs={{0,32},{1,481},{32,64},{33,1},{64,96},{65,33},{96,128},{97,65},{12... | collective-permute-start | bytes 884744 | tf_op jit(solution)/shard_map/ppermute | solution.py:33
  78.9 18.1 %collective-permute-start.13 = (bf16[3,128,1152]{2,1,0:T(8,128)(2,1)S(1)}, bf16[3,128,1152]{2,1,0:T(8,128)(2,1)S(1)}, u32[]{:S(2)}, u32[]{:S(2)}) collective-permute-start(bf16[3,128,1152]{2,1,0:T(8,128)(2,1)S(1)} %pad_maximum_fusion.2), channel_id=1, source_target_pairs={{0,1},{1,0},{2,3},{3,2},{4,5},{5,4},{6,7},{7,6},{8,9},{9,8},{10,11... | collective-permute-start | bytes 2654216 | tf_op jit(solution)/shard_map/ppermute | solution.py:37
  85.2 11.4 %collective-permute-start.8 = (bf16[128,1152]{1,0:T(8,128)(2,1)S(1)}, bf16[128,1152]{1,0:T(8,128)(2,1)S(1)}, u32[]{:S(2)}, u32[]{:S(2)}) collective-permute-start(bf16[128,1152]{1,0:T(8,128)(2,1)S(1)} %collective-permute-done.7), channel_id=1, source_target_pairs={{0,32},{1,481},{32,64},{33,1},{64,96},{65,33},{96,128},{97,65},{12... | collective-permute-start | bytes 884744 | tf_op jit(solution)/shard_map/ppermute | solution.py:33
  91.2 5.9 %collective-permute-start.16 = (bf16[2,128,1152]{2,1,0:T(8,128)(2,1)S(1)}, bf16[2,128,1152]{2,1,0:T(8,128)(2,1)S(1)}, u32[]{:S(2)}, u32[]{:S(2)}) collective-permute-start(bf16[2,128,1152]{2,1,0:T(8,128)(2,1)S(1)} %pad_maximum_fusion.3), channel_id=1, source_target_pairs={{0,1},{1,0},{2,3},{3,2},{4,5},{5,4},{6,7},{7,6},{8,9},{9,8},{10,11... | collective-permute-start | bytes 1769480 | tf_op jit(solution)/shard_map/ppermute | solution.py:37
  94.2 4.0 %collective-permute-start.19 = (bf16[2,128,1152]{2,1,0:T(8,128)(2,1)S(1)}, bf16[2,128,1152]{2,1,0:T(8,128)(2,1)S(1)}, u32[]{:S(2)}, u32[]{:S(2)}) collective-permute-start(bf16[2,128,1152]{2,1,0:T(8,128)(2,1)S(1)} %pad_maximum_fusion.4), channel_id=1, source_target_pairs={{0,1},{1,0},{2,3},{3,2},{4,5},{5,4},{6,7},{7,6},{8,9},{9,8},{10,11... | collective-permute-start | bytes 1769480 | tf_op jit(solution)/shard_map/ppermute | solution.py:37
  98.3 2.8 %copy-start = (bf16[2048,1152]{1,0:T(8,128)(2,1)}, bf16[2048,1152]{1,0:T(8,128)(2,1)S(1)}, u32[]{:S(2)}) copy-start(bf16[2048,1152]{1,0:T(8,128)(2,1)S(1)} %fusion.14) | copy-start | bytes 14155780
  136.5 29.0 %all-to-all-start.1 = ((bf16[16,256,128]{2,1,0:T(8,128)(2,1)}), bf16[16,256,128]{2,1,0:T(8,128)(2,1)S(1)}, u32[]{:S(2)}, u32[]{:S(2)}) async-start(bf16[16,256,128]{2,1,0:T(8,128)(2,1)} %broadcast_in_dim.15), calls=%async_computation.1 | async-start | bytes 2097152 | tf_op jit(solution)/shard_map/all_to_all | solution.py:17
  159.0 30.9 %collective-permute-start.21 = (bf16[4,2,128,128]{3,2,0,1:T(8,128)(2,1)S(1)}, bf16[4,2,128,128]{3,2,0,1:T(8,128)(2,1)S(1)}, u32[]{:S(2)}, u32[]{:S(2)}) collective-permute-start(bf16[4,2,128,128]{3,2,0,1:T(8,128)(2,1)S(1)} %copy.24), channel_id=1, source_target_pairs={{0,32},{32,64},{64,96},{96,128},{128,160},{160,192},{192,224},{224... | collective-permute-start | bytes 786440 | tf_op jit(solution)/shard_map/ppermute | solution.py:23
  160.9 31.4 %collective-permute-start.20 = (bf16[4,2,128,128]{3,2,0,1:T(8,128)(2,1)S(1)}, bf16[4,2,128,128]{3,2,0,1:T(8,128)(2,1)}, u32[]{:S(2)}, u32[]{:S(2)}) collective-permute-start(bf16[4,2,128,128]{3,2,0,1:T(8,128)(2,1)S(1)} %copy.24), channel_id=1, source_target_pairs={{0,480},{32,0},{64,32},{96,64},{128,96},{160,128},{192,160},{224,1... | collective-permute-start | bytes 786440 | tf_op jit(solution)/shard_map/ppermute | solution.py:23
  166.1 24.2 %collective-permute-start.24 = (bf16[4,4,128,256]{3,2,1,0:T(8,128)(2,1)S(1)}, bf16[4,4,128,256]{3,2,1,0:T(8,128)(2,1)}, u32[]{:S(2)}, u32[]{:S(2)}) collective-permute-start(bf16[4,4,128,256]{3,2,1,0:T(8,128)(2,1)S(1)} %pad_maximum_fusion.1), channel_id=1, source_target_pairs={{0,1},{1,0},{2,3},{3,2},{4,5},{5,4},{6,7},{7,6},{8,9},{9,8},{10,11... | collective-permute-start | bytes 3145736 | tf_op jit(solution)/shard_map/ppermute | solution.py:115
  173.9 9.6 %collective-permute-start.22 = (bf16[2,2,128,128]{3,2,0,1:T(8,128)(2,1)}, bf16[2,2,128,128]{3,2,0,1:T(8,128)(2,1)}, u32[]{:S(2)}, u32[]{:S(2)}) collective-permute-start(bf16[2,2,128,128]{3,2,0,1:T(8,128)(2,1)} %copy.28), channel_id=1, source_target_pairs={{0,448},{32,480},{64,0},{96,32},{128,64},{160,96},{192,128},{224,1... | collective-permute-start | bytes 393224 | tf_op jit(solution)/shard_map/ppermute | solution.py:23
  177.1 11.6 %collective-permute-start.23 = (bf16[2,2,128,128]{3,2,0,1:T(8,128)(2,1)}, bf16[2,2,128,128]{3,2,0,1:T(8,128)(2,1)}, u32[]{:S(2)}, u32[]{:S(2)}) collective-permute-start(bf16[2,2,128,128]{3,2,0,1:T(8,128)(2,1)} %copy.29), channel_id=1, source_target_pairs={{0,64},{32,96},{64,128},{96,160},{128,192},{160,224},{192,256},{22... | collective-permute-start | bytes 393224 | tf_op jit(solution)/shard_map/ppermute | solution.py:23
  190.3 27.2 %slice-start = ((s8[4718592]{0:T(1024)(128)(4,1)}), s8[4194304]{0:T(1024)(128)(4,1)S(1)}, s32[]{:S(2)}) async-start(s8[4718592]{0:T(1024)(128)(4,1)} %bitcast.164), calls=%async_computation.3 | async-start | bytes 8388608
  192.3 25.2 %slice-start.1 = ((s8[4718592]{0:T(1024)(128)(4,1)}), s8[524288]{0:T(1024)(128)(4,1)S(1)}, s32[]{:S(2)}) async-start(s8[4718592]{0:T(1024)(128)(4,1)} %bitcast.164), calls=%async_computation.4 | async-start | bytes 1048576
  219.3 8.9 %collective-permute-start.25 = (bf16[128,1152]{1,0:T(8,128)(2,1)S(1)}, bf16[128,1152]{1,0:T(8,128)(2,1)S(1)}, u32[]{:S(2)}, u32[]{:S(2)}) collective-permute-start(bf16[128,1152]{1,0:T(8,128)(2,1)S(1)} %fusion), channel_id=1, source_target_pairs={{0,0},{1,16},{16,1},{17,17},{2,2},{3,18},{18,3},{19,19},{4,4},{5,2... | collective-permute-start | bytes 884744 | tf_op jit(solution)/shard_map/ppermute | solution.py:134
  223.8 7.6 %collective-permute-start.26 = (bf16[128,1152]{1,0:T(8,128)(2,1)S(1)}, bf16[128,1152]{1,0:T(8,128)(2,1)S(1)}, u32[]{:S(2)}, u32[]{:S(2)}) collective-permute-start(bf16[128,1152]{1,0:T(8,128)(2,1)S(1)} %convolution_convert_fusion), channel_id=1, source_target_pairs={{0,16},{1,0},{16,17},{17,1},{2,18},{3,2},{18,19},{19,3},{4,20},{5,... | collective-permute-start | bytes 884744 | tf_op jit(solution)/shard_map/ppermute | solution.py:132

commit v10 on v9

--- a/solution.py
+++ b/solution.py
@@ -84,15 +84,30 @@
     near.append(onward(near[-1]))
     back = swap(far[1:4]) + swap(far[4:6]) + swap(far[6:])
     half = jnp.concatenate(near[::-1] + back, 0)
-    gram = jnp.stack([nt(half, own), nt(half, other)])
-    gram = gram.reshape(2, slabs, chips, rows // chips, rows)
-    gram = gram.transpose(2, 0, 1, 3, 4).reshape(chips, 2 * rows, rows)
-    gram, slab, core, residue = lax.optimization_barrier((gram, slab, core, residue))
-    gram = lax.all_to_all(gram, PLANE, 0, 0)
-    gram, half, own, slab, core, residue = lax.optimization_barrier(
-        (gram, half, own, slab, core, residue)
+    exact = [nt(half, side) for side in (own, other)]
+    parts = [lax.reduce_precision(side, 8, 7) for side in exact]
+    middle = slabs // 2
+    begin, end = middle * rows, (middle + 1) * rows
+    rest = [one[begin:end] - two[begin:end] for one, two in zip(exact, parts)]
+    parts = [
+        jnp.stack(sides).astype(jnp.bfloat16).reshape(2, -1, chips, rows // chips, rows)
+        for sides in (parts, rest)
+    ]
+    parts = [
+        part.transpose(2, 0, 1, 3, 4).reshape(chips, -1, rows) for part in parts
+    ]
+    parts = jnp.concatenate(parts, 1)
+    parts, slab, core, residue = lax.optimization_barrier((parts, slab, core, residue))
+    parts = lax.all_to_all(parts, PLANE, 0, 0)
+    parts, half, own, slab, core, residue = lax.optimization_barrier(
+        (parts, half, own, slab, core, residue)
     )
-    gram = gram.sum(0).reshape(2, slabs, rows // chips, rows) / total_cols
+    gram = parts.astype(jnp.float32).sum(0) / total_cols
+    rest = gram[2 * rows :].reshape(2, 1, rows // chips, rows)
+    gram = gram[: 2 * rows].reshape(2, slabs, rows // chips, rows)
+    gram = jnp.concatenate(
+        [gram[:, :middle], gram[:, middle : middle + 1] + rest, gram[:, middle + 1 :]], 1
+    )
     gram = jnp.where(core == 0, gram, gram[:, ::-1])
     gram = turn_to(gram, slabs + slabs // 2 - core - slab)
     gram_low = gram.astype(jnp.bfloat16).reshape(2 * rows, rows)
@@ -100,27 +115,22 @@
     panel = share(gram_low, chips).reshape(chips, 2, slabs, rows // chips, rows)
     panel = panel.transpose(2, 0, 3, 1, 4).reshape(groups, steps, rows, 2 * rows)
     here = lax.all_gather(gram_low, "zh", axis=0).reshape(groups, 2, rows, rows)
+    here = here.transpose(1, 0, 2, 3)
     panel, _ = lax.optimization_barrier((panel, here))
-    cut = groups // 2
     left = (
         here,
         along(here, -1),
         along(here, 1),
-        jnp.concatenate([along(here[:cut], -2), along(here[cut:], 2)], 0),
+        (along(here[0], -2), along(here[1], 2)),
     )
     right_own = [
         lax.dynamic_index_in_dim(panel, (residue + shift) % steps, 1, False)
         for shift in (0, 1, steps - 1, 2)
     ]
     right_other = lax.ppermute(jnp.stack(right_own), "core", SWAP)
-    right_other = jnp.concatenate(
-        [right_other[:, :, :, rows:], right_other[:, :, :, :rows]], 3
-    )
-    square = 0.0
-    for place in range(steps):
-        square = square + mix(left[place][:, 0], right_own[place])
-    for place in range(steps):
-        square = square + mix(left[place][:, 1], right_other[place])
+    square = sum(mix(left[place][0], right_own[place]) for place in range(steps))
+    across = sum(mix(left[place][1], right_other[place]) for place in range(steps))
+    square = square + jnp.concatenate([across[:, rows:], across[:, :rows]], 1)
     poly = (-4.775 * gram + 2.0315 * square).astype(jnp.bfloat16)
     poly = poly.reshape(slabs, rows // chips, 2, rows).transpose(2, 0, 1, 3)
     poly = turn_to(poly, slabs // 2 + slab + core)

time: 234 us -> 223 us (0.953)
  blocking collectives: 73.9 us -> 60 us
  matrix products: 8 us -> 11.7 us
  waiting for transfers between devices: 21.4 us -> 18.1 us
  starting transfers between devices: 116 us -> 119 us
    all_to_all x1, blocking collectives: 33.5 us -> 23.6 us  [per_device(): parts = lax.all_to_all(parts, PLANE, 0, 0)]
    all_to_all x1, blocking collectives: 22.2 us -> 18.4 us  [share(): return lax.all_to_all(copies, PLANE, 0, 0)]
    dot_general x8, matrix products: 3.43 us -> 7.12 us  [mix(): lax.dot_general(left, right, (((0, 2), (0, 1)), ((), ())), preferred_elem...]
    slice x4, local copies, waits for them, and re-layouts: 2.77 us -> 0.03 us  [the longest x1 0.01 us: per_device(): square = square + jnp.concatenate([across[:, rows:], across[:, :rows]], 1)]
    ppermute x1, starting transfers between devices: 4.49 us -> 6.98 us  [per_device(): stay = lax.ppermute(stay.astype(jnp.bfloat16), ('ylo', 'core'), TURN)]
  transfers between devices with their start and end apart: 28 -> 28, of which waited for: 12 -> 11; matrix products, arithmetic and copies ran while one was open for 4% -> 4% of each run, Pallas kernels for 0% -> 0%
where the time goes in v10:
time: 223 us; the launch traced here: 221 us
  starting transfers between devices  119 us (53%)
  blocking collectives  60 us (27%)
  waiting for transfers between devices  18.1 us (8%)
  matrix products  11.7 us (5%)
  other arithmetic  5.98 us (3%)
  local copies, waits for them, and re-layouts  5.29 us (2%)
    ppermute x15, starting transfers between devices, onward(): return lax.ppermute(piece, LINE + ('core',), pairs)  68.8 us
    all_to_all x1, blocking collectives, per_device(): parts = lax.all_to_all(parts, PLANE, 0, 0)  23.6 us
    all_to_all x1, blocking collectives, share(): return lax.all_to_all(copies, PLANE, 0, 0)  18.4 us
    all_gather x1, blocking collectives, per_device(): here = lax.all_gather(gram_low, 'zh', axis=0).reshape(groups, 2, rows, rows)  18 us
    ppermute x4, starting transfers between devices, along(): return lax.ppermute(piece, LINE, pairs)  13 us
    ppermute x3, starting transfers between devices, swap(): return list(lax.ppermute(jnp.stack(pieces), 'core', SWAP))  10.7 us
    ppermute x1, starting transfers between devices, per_device(): right_other = lax.ppermute(jnp.stack(right_own), 'core', SWAP)  7.47 us
    dot_general x8, matrix products, mix(): lax.dot_general(left, right, (((0, 2), (0, 1)), ((), ())), preferred_elem...  7.12 us
  transfers between devices with their start and end apart: 28, of which 11 were waited for; matrix products, arithmetic and copies ran while one was open for 4% of the time, Pallas kernels for 0%

profile of v10, /device:TPU:1, one launch (start us, length us, event | category | flops | bytes accessed | tf_op | source)
XLA Modules:
  0.0 221.1 jit_solution(8966091938301197999)
XLA Ops:
  0.0 1.1 convert_element_type.37
  1.1 4.6 %collective-permute-start = (bf16[128,1152]{1,0:T(8,128)(2,1)S(1)}, bf16[128,1152]{1,0:T(8,128)(2,1)S(1)}, u32[]{:S(2)}, u32[]{:S(2)}) collective-permute-start(bf16[128,1152]{1,0:T(8,128)(2,1)S(1)} %convert_element_type.37), channel_id=1, source_target_pairs={{0,0},{1,16},{16,1},{17,17},{2,2},{3,18},{18,3},{19,19},{4,4},{5,2... | collective-permute-start | bytes 884744 | tf_op jit(solution)/shard_map/ppermute | solution.py:78
  5.7 4.4 %collective-permute-done = bf16[128,1152]{1,0:T(8,128)(2,1)S(1)} collective-permute-done((bf16[128,1152]{1,0:T(8,128)(2,1)S(1)}, bf16[128,1152]{1,0:T(8,128)(2,1)S(1)}, u32[]{:S(2)}, u32[]{:S(2)}) %collective-permute-start) | collective-permute-done | bytes 294944 | tf_op jit(solution)/shard_map/ppermute | solution.py:78
  10.1 1.9 collective-permute-start.9
  12.0 11.1 %collective-permute-start.1 = (bf16[128,1152]{1,0:T(8,128)(2,1)S(1)}, bf16[128,1152]{1,0:T(8,128)(2,1)S(1)}, u32[]{:S(2)}, u32[]{:S(2)}) collective-permute-start(bf16[128,1152]{1,0:T(8,128)(2,1)S(1)} %collective-permute-done), channel_id=1, source_target_pairs={{0,32},{1,481},{32,64},{33,1},{64,96},{65,33},{96,128},{97,65},{12... | collective-permute-start | bytes 884744 | tf_op jit(solution)/shard_map/ppermute | solution.py:33
  23.2 2.6 %collective-permute-start.10 = (bf16[128,1152]{1,0:T(8,128)(2,1)S(1)}, bf16[128,1152]{1,0:T(8,128)(2,1)S(1)}, u32[]{:S(2)}, u32[]{:S(2)}) collective-permute-start(bf16[128,1152]{1,0:T(8,128)(2,1)S(1)} %collective-permute-done.9), channel_id=1, source_target_pairs={{0,32},{1,481},{32,64},{33,1},{64,96},{65,33},{96,128},{97,65},{12... | collective-permute-start | bytes 884744 | tf_op jit(solution)/shard_map/ppermute | solution.py:33
  25.8 1.0 collective-permute-done.1
  26.8 5.0 %collective-permute-start.2 = (bf16[128,1152]{1,0:T(8,128)(2,1)S(1)}, bf16[128,1152]{1,0:T(8,128)(2,1)S(1)}, u32[]{:S(2)}, u32[]{:S(2)}) collective-permute-start(bf16[128,1152]{1,0:T(8,128)(2,1)S(1)} %collective-permute-done.1), channel_id=1, source_target_pairs={{0,32},{1,481},{32,64},{33,1},{64,96},{65,33},{96,128},{97,65},{12... | collective-permute-start | bytes 884744 | tf_op jit(solution)/shard_map/ppermute | solution.py:33
  31.8 3.1 %collective-permute-start.11 = (bf16[128,1152]{1,0:T(8,128)(2,1)S(1)}, bf16[128,1152]{1,0:T(8,128)(2,1)S(1)}, u32[]{:S(2)}, u32[]{:S(2)}) collective-permute-start(bf16[128,1152]{1,0:T(8,128)(2,1)S(1)} %collective-permute-done.10), channel_id=1, source_target_pairs={{0,32},{1,481},{32,64},{33,1},{64,96},{65,33},{96,128},{97,65},{12... | collective-permute-start | bytes 884744 | tf_op jit(solution)/shard_map/ppermute | solution.py:33
  35.0 0.5 collective-permute-done.2
  35.5 5.0 %collective-permute-start.3 = (bf16[128,1152]{1,0:T(8,128)(2,1)S(1)}, bf16[128,1152]{1,0:T(8,128)(2,1)S(1)}, u32[]{:S(2)}, u32[]{:S(2)}) collective-permute-start(bf16[128,1152]{1,0:T(8,128)(2,1)S(1)} %collective-permute-done.2), channel_id=1, source_target_pairs={{0,32},{1,481},{32,64},{33,1},{64,96},{65,33},{96,128},{97,65},{12... | collective-permute-start | bytes 884744 | tf_op jit(solution)/shard_map/ppermute | solution.py:33
  40.5 3.1 %collective-permute-start.12 = (bf16[128,1152]{1,0:T(8,128)(2,1)S(1)}, bf16[128,1152]{1,0:T(8,128)(2,1)S(1)}, u32[]{:S(2)}, u32[]{:S(2)}) collective-permute-start(bf16[128,1152]{1,0:T(8,128)(2,1)S(1)} %collective-permute-done.11), channel_id=1, source_target_pairs={{0,32},{1,481},{32,64},{33,1},{64,96},{65,33},{96,128},{97,65},{12... | collective-permute-start | bytes 884744 | tf_op jit(solution)/shard_map/ppermute | solution.py:33
  43.6 0.5 collective-permute-done.3
  44.1 5.0 %collective-permute-start.4 = (bf16[128,1152]{1,0:T(8,128)(2,1)S(1)}, bf16[128,1152]{1,0:T(8,128)(2,1)S(1)}, u32[]{:S(2)}, u32[]{:S(2)}) collective-permute-start(bf16[128,1152]{1,0:T(8,128)(2,1)S(1)} %collective-permute-done.3), channel_id=1, source_target_pairs={{0,32},{1,481},{32,64},{33,1},{64,96},{65,33},{96,128},{97,65},{12... | collective-permute-start | bytes 884744 | tf_op jit(solution)/shard_map/ppermute | solution.py:33
  49.2 3.1 %collective-permute-start.14 = (bf16[128,1152]{1,0:T(8,128)(2,1)S(1)}, bf16[128,1152]{1,0:T(8,128)(2,1)}, u32[]{:S(2)}, u32[]{:S(2)}) collective-permute-start(bf16[128,1152]{1,0:T(8,128)(2,1)S(1)} %collective-permute-done.12), channel_id=1, source_target_pairs={{0,32},{1,481},{32,64},{33,1},{64,96},{65,33},{96,128},{97,65},{12... | collective-permute-start | bytes 884744 | tf_op jit(solution)/shard_map/ppermute | solution.py:33
  52.3 0.5 collective-permute-done.4
  52.8 5.0 %collective-permute-start.5 = (bf16[128,1152]{1,0:T(8,128)(2,1)S(1)}, bf16[128,1152]{1,0:T(8,128)(2,1)S(1)}, u32[]{:S(2)}, u32[]{:S(2)}) collective-permute-start(bf16[128,1152]{1,0:T(8,128)(2,1)S(1)} %collective-permute-done.4), channel_id=1, source_target_pairs={{0,32},{1,481},{32,64},{33,1},{64,96},{65,33},{96,128},{97,65},{12... | collective-permute-start | bytes 884744 | tf_op jit(solution)/shard_map/ppermute | solution.py:33
  57.8 3.2 %collective-permute-start.15 = (bf16[128,1152]{1,0:T(8,128)(2,1)}, bf16[128,1152]{1,0:T(8,128)(2,1)}, u32[]{:S(2)}, u32[]{:S(2)}) collective-permute-start(bf16[128,1152]{1,0:T(8,128)(2,1)} %collective-permute-done.14), channel_id=1, source_target_pairs={{0,32},{1,481},{32,64},{33,1},{64,96},{65,33},{96,128},{97,65},{12... | collective-permute-start | bytes 884744 | tf_op jit(solution)/shard_map/ppermute | solution.py:33
  61.1 0.4 collective-permute-done.5
  61.5 5.0 %collective-permute-start.6 = (bf16[128,1152]{1,0:T(8,128)(2,1)S(1)}, bf16[128,1152]{1,0:T(8,128)(2,1)S(1)}, u32[]{:S(2)}, u32[]{:S(2)}) collective-permute-start(bf16[128,1152]{1,0:T(8,128)(2,1)S(1)} %collective-permute-done.5), channel_id=1, source_target_pairs={{0,32},{1,481},{32,64},{33,1},{64,96},{65,33},{96,128},{97,65},{12... | collective-permute-start | bytes 884744 | tf_op jit(solution)/shard_map/ppermute | solution.py:33
  66.5 3.6 %collective-permute-start.17 = (bf16[128,1152]{1,0:T(8,128)(2,1)}, bf16[128,1152]{1,0:T(8,128)(2,1)}, u32[]{:S(2)}, u32[]{:S(2)}) collective-permute-start(bf16[128,1152]{1,0:T(8,128)(2,1)} %collective-permute-done.15), channel_id=1, source_target_pairs={{0,32},{1,481},{32,64},{33,1},{64,96},{65,33},{96,128},{97,65},{12... | collective-permute-start | bytes 884744 | tf_op jit(solution)/shard_map/ppermute | solution.py:33
  70.1 5.0 %collective-permute-start.7 = (bf16[128,1152]{1,0:T(8,128)(2,1)S(1)}, bf16[128,1152]{1,0:T(8,128)(2,1)}, u32[]{:S(2)}, u32[]{:S(2)}) collective-permute-start(bf16[128,1152]{1,0:T(8,128)(2,1)S(1)} %collective-permute-done.6), channel_id=1, source_target_pairs={{0,32},{1,481},{32,64},{33,1},{64,96},{65,33},{96,128},{97,65},{12... | collective-permute-start | bytes 884744 | tf_op jit(solution)/shard_map/ppermute | solution.py:33
  75.2 3.9 %collective-permute-start.18 = (bf16[128,1152]{1,0:T(8,128)(2,1)}, bf16[128,1152]{1,0:T(8,128)(2,1)S(1)}, u32[]{:S(2)}, u32[]{:S(2)}) collective-permute-start(bf16[128,1152]{1,0:T(8,128)(2,1)} %collective-permute-done.17), channel_id=1, source_target_pairs={{0,32},{1,481},{32,64},{33,1},{64,96},{65,33},{96,128},{97,65},{12... | collective-permute-start | bytes 884744 | tf_op jit(solution)/shard_map/ppermute | solution.py:33
  79.2 6.4 %collective-permute-start.13 = (bf16[3,128,1152]{2,1,0:T(8,128)(2,1)S(1)}, bf16[3,128,1152]{2,1,0:T(8,128)(2,1)S(1)}, u32[]{:S(2)}, u32[]{:S(2)}) collective-permute-start(bf16[3,128,1152]{2,1,0:T(8,128)(2,1)S(1)} %pad_maximum_fusion.3), channel_id=1, source_target_pairs={{0,1},{1,0},{2,3},{3,2},{4,5},{5,4},{6,7},{7,6},{8,9},{9,8},{10,11... | collective-permute-start | bytes 2654216 | tf_op jit(solution)/shard_map/ppermute | solution.py:37
  85.6 4.9 %collective-permute-start.8 = (bf16[128,1152]{1,0:T(8,128)(2,1)}, bf16[128,1152]{1,0:T(8,128)(2,1)S(1)}, u32[]{:S(2)}, u32[]{:S(2)}) collective-permute-start(bf16[128,1152]{1,0:T(8,128)(2,1)} %collective-permute-done.7), channel_id=1, source_target_pairs={{0,32},{1,481},{32,64},{33,1},{64,96},{65,33},{96,128},{97,65},{12... | collective-permute-start | bytes 884744 | tf_op jit(solution)/shard_map/ppermute | solution.py:33
  90.4 1.1 pad_maximum_fusion.4
  91.5 1.9 collective-permute-start.16
  93.5 1.0 pad_maximum_fusion.5
  94.5 2.4 %collective-permute-start.19 = (bf16[2,128,1152]{2,1,0:T(8,128)(2,1)S(1)}, bf16[2,128,1152]{2,1,0:T(8,128)(2,1)S(1)}, u32[]{:S(2)}, u32[]{:S(2)}) collective-permute-start(bf16[2,128,1152]{2,1,0:T(8,128)(2,1)S(1)} %pad_maximum_fusion.5), channel_id=1, source_target_pairs={{0,1},{1,0},{2,3},{3,2},{4,5},{5,4},{6,7},{7,6},{8,9},{9,8},{10,11... | collective-permute-start | bytes 1769480 | tf_op jit(solution)/shard_map/ppermute | solution.py:37
  97.0 1.0 constant_dynamic-update-slice_fusion.7
  98.6 1.4 reduce-precision_convert_fusion
  100.0 0.7 copy-done
  100.7 1.4 reduce-precision_convert_fusion.1
  102.3 0.3 copy.24
  102.7 23.6 %all_to_all.15 = bf16[16,272,128]{2,1,0:T(8,128)(2,1)S(1)} all-to-all(bf16[16,272,128]{2,1,0:T(8,128)(2,1)S(1)} %pad_maximum_fusion), channel_id=1, replica_groups=mesh['zh'=4,'zl'=4,'ylo'=2,'x'=4,'yhi'=2,'core'=2] {'ylo','x','yhi'}, dimensions={0} | all-to-all | bytes 2228224 | tf_op jit(solution)/shard_map/all_to_all | solution.py:101
  126.6 1.2 broadcast_in_dim.15
  127.9 3.7 %all-to-all-start.1 = ((bf16[16,256,128]{2,1,0:T(8,128)(2,1)}), bf16[16,256,128]{2,1,0:T(8,128)(2,1)S(1)}, u32[]{:S(2)}, u32[]{:S(2)}) async-start(bf16[16,256,128]{2,1,0:T(8,128)(2,1)} %broadcast_in_dim.15), calls=%async_computation.1 | async-start | bytes 2097152 | tf_op jit(solution)/shard_map/all_to_all | solution.py:17
  131.6 18.0 %all_gather.3 = bf16[4,256,128]{2,1,0:T(8,128)(2,1)S(1)} all-gather(bf16[1,256,128]{2,1,0:T(8,128)(2,1)S(1)} %bitcast.198), channel_id=1, replica_groups=mesh['zh'=4,'zl'=4,'ylo'=2,'x'=4,'yhi'=2,'core'=2] {'zh'}, dimensions={0}, use_global_device_ids=true | all-gather | bytes 327680 | tf_op jit(solution)/shard_map/all_gather | solution.py:117
  149.6 0.3 copy.21
  150.0 1.1 pad_maximum_fusion.2
  151.2 7.5 %collective-permute-start.23 = (bf16[4,4,128,256]{3,2,1,0:T(8,128)(2,1)}, bf16[4,4,128,256]{3,2,1,0:T(8,128)(2,1)S(1)}, u32[]{:S(2)}, u32[]{:S(2)}) collective-permute-start(bf16[4,4,128,256]{3,2,1,0:T(8,128)(2,1)} %pad_maximum_fusion.2), channel_id=1, source_target_pairs={{0,1},{1,0},{2,3},{3,2},{4,5},{5,4},{6,7},{7,6},{8,9},{9,8},{10,11... | collective-permute-start | bytes 3145736 | tf_op jit(solution)/shard_map/ppermute | solution.py:130
  158.6 3.7 %collective-permute-start.20 = (bf16[2,4,128,128]{3,2,1,0:T(8,128)(2,1)S(1)}, bf16[2,4,128,128]{3,2,1,0:T(8,128)(2,1)}, u32[]{:S(2)}, u32[]{:S(2)}) collective-permute-start(bf16[2,4,128,128]{3,2,1,0:T(8,128)(2,1)S(1)} %bitcast.191), channel_id=1, source_target_pairs={{0,480},{32,0},{64,32},{96,64},{128,96},{160,128},{192,160},{224,1... | collective-permute-start | bytes 786440 | tf_op jit(solution)/shard_map/ppermute | solution.py:23
  162.3 1.9 collective-permute-start.21
  164.2 0.7 slice_bitcast_fusion.19
  165.0 1.9 collective-permute-start.24
  166.9 5.5 %collective-permute-start.22 = (bf16[4,128,128]{2,1,0:T(8,128)(2,1)}, bf16[4,128,128]{2,1,0:T(8,128)(2,1)}, u32[]{:S(2)}, u32[]{:S(2)}) collective-permute-start(bf16[4,128,128]{2,1,0:T(8,128)(2,1)} %get-tuple-element.38), channel_id=1, source_target_pairs={{0,448},{32,480},{64,0},{96,32},{128,64},{160,96},{192,128},{224,1... | collective-permute-start | bytes 393224 | tf_op jit(solution)/shard_map/ppermute | solution.py:23
  172.4 0.2 convolution_bitcast_fusion.7
  172.6 5.1 %collective-permute-done.22 = bf16[4,128,128]{2,1,0:T(8,128)(2,1)} collective-permute-done((bf16[4,128,128]{2,1,0:T(8,128)(2,1)}, bf16[4,128,128]{2,1,0:T(8,128)(2,1)}, u32[]{:S(2)}, u32[]{:S(2)}) %collective-permute-start.22) | collective-permute-done | bytes 131104 | tf_op jit(solution)/shard_map/ppermute | solution.py:23
  177.7 1.1 convolution_bitcast_fusion.4
  178.8 1.1 convolution_bitcast_fusion.5
  179.9 1.1 convolution_bitcast_fusion.1
  181.0 1.1 convolution_bitcast_fusion.2
  182.2 1.2 convolution_bitcast_fusion
  183.6 1.1 fusion.11
  184.9 0.2 broadcast_in_dim.17
  185.1 18.4 %all_to_all.16 = bf16[16,256,128]{2,1,0:T(8,128)(2,1)S(1)} all-to-all(bf16[16,256,128]{2,1,0:T(8,128)(2,1)S(1)} %broadcast_in_dim.17), channel_id=1, replica_groups=mesh['zh'=4,'zl'=4,'ylo'=2,'x'=4,'yhi'=2,'core'=2] {'ylo','x','yhi'}, dimensions={0} | all-to-all | bytes 2097152 | tf_op jit(solution)/shard_map/all_to_all | solution.py:17
  203.5 0.3 copy.23
  203.8 0.9 convolution_convert_fusion
  204.7 0.9 fusion
  205.6 7.0 %collective-permute-start.25 = (bf16[128,1152]{1,0:T(8,128)(2,1)S(1)}, bf16[128,1152]{1,0:T(8,128)(2,1)S(1)}, u32[]{:S(2)}, u32[]{:S(2)}) collective-permute-start(bf16[128,1152]{1,0:T(8,128)(2,1)S(1)} %fusion), channel_id=1, source_target_pairs={{0,0},{1,16},{16,1},{17,17},{2,2},{3,18},{18,3},{19,19},{4,4},{5,2... | collective-permute-start | bytes 884744 | tf_op jit(solution)/shard_map/ppermute | solution.py:144
  212.6 1.9 collective-permute-start.26
  214.6 2.5 %collective-permute-done.25 = bf16[128,1152]{1,0:T(8,128)(2,1)S(1)} collective-permute-done((bf16[128,1152]{1,0:T(8,128)(2,1)S(1)}, bf16[128,1152]{1,0:T(8,128)(2,1)S(1)}, u32[]{:S(2)}, u32[]{:S(2)}) %collective-permute-start.25) | collective-permute-done | bytes 294944 | tf_op jit(solution)/shard_map/ppermute | solution.py:144
  217.0 3.1 %collective-permute-done.26 = bf16[128,1152]{1,0:T(8,128)(2,1)S(1)} collective-permute-done((bf16[128,1152]{1,0:T(8,128)(2,1)S(1)}, bf16[128,1152]{1,0:T(8,128)(2,1)S(1)}, u32[]{:S(2)}, u32[]{:S(2)}) %collective-permute-start.26) | collective-permute-done | bytes 294944 | tf_op jit(solution)/shard_map/ppermute | solution.py:142
  220.2 0.9 convert_add_fusion
  (62 shorter events, 1.8 us)
Async XLA Ops:
  1.1 9.0 %collective-permute-start = (bf16[128,1152]{1,0:T(8,128)(2,1)S(1)}, bf16[128,1152]{1,0:T(8,128)(2,1)S(1)}, u32[]{:S(2)}, u32[]{:S(2)}) collective-permute-start(bf16[128,1152]{1,0:T(8,128)(2,1)S(1)} %convert_element_type.37), channel_id=1, source_target_pairs={{0,0},{1,16},{16,1},{17,17},{2,2},{3,18},{18,3},{19,19},{4,4},{5,2... | collective-permute-start | bytes 884744 | tf_op jit(solution)/shard_map/ppermute | solution.py:78
  10.1 13.1 %collective-permute-start.9 = (bf16[128,1152]{1,0:T(8,128)(2,1)S(1)}, bf16[128,1152]{1,0:T(8,128)(2,1)S(1)}, u32[]{:S(2)}, u32[]{:S(2)}) collective-permute-start(bf16[128,1152]{1,0:T(8,128)(2,1)S(1)} %collective-permute-done), channel_id=1, source_target_pairs={{0,1},{1,0},{2,3},{3,2},{4,5},{5,4},{6,7},{7,6},{8,9},{9,8},{10,11... | collective-permute-start | bytes 884744 | tf_op jit(solution)/shard_map/ppermute | solution.py:79
  12.0 14.8 %collective-permute-start.1 = (bf16[128,1152]{1,0:T(8,128)(2,1)S(1)}, bf16[128,1152]{1,0:T(8,128)(2,1)S(1)}, u32[]{:S(2)}, u32[]{:S(2)}) collective-permute-start(bf16[128,1152]{1,0:T(8,128)(2,1)S(1)} %collective-permute-done), channel_id=1, source_target_pairs={{0,32},{1,481},{32,64},{33,1},{64,96},{65,33},{96,128},{97,65},{12... | collective-permute-start | bytes 884744 | tf_op jit(solution)/shard_map/ppermute | solution.py:33
  23.2 8.7 %collective-permute-start.10 = (bf16[128,1152]{1,0:T(8,128)(2,1)S(1)}, bf16[128,1152]{1,0:T(8,128)(2,1)S(1)}, u32[]{:S(2)}, u32[]{:S(2)}) collective-permute-start(bf16[128,1152]{1,0:T(8,128)(2,1)S(1)} %collective-permute-done.9), channel_id=1, source_target_pairs={{0,32},{1,481},{32,64},{33,1},{64,96},{65,33},{96,128},{97,65},{12... | collective-permute-start | bytes 884744 | tf_op jit(solution)/shard_map/ppermute | solution.py:33
  26.8 8.7 %collective-permute-start.2 = (bf16[128,1152]{1,0:T(8,128)(2,1)S(1)}, bf16[128,1152]{1,0:T(8,128)(2,1)S(1)}, u32[]{:S(2)}, u32[]{:S(2)}) collective-permute-start(bf16[128,1152]{1,0:T(8,128)(2,1)S(1)} %collective-permute-done.1), channel_id=1, source_target_pairs={{0,32},{1,481},{32,64},{33,1},{64,96},{65,33},{96,128},{97,65},{12... | collective-permute-start | bytes 884744 | tf_op jit(solution)/shard_map/ppermute | solution.py:33
  31.8 8.7 %collective-permute-start.11 = (bf16[128,1152]{1,0:T(8,128)(2,1)S(1)}, bf16[128,1152]{1,0:T(8,128)(2,1)S(1)}, u32[]{:S(2)}, u32[]{:S(2)}) collective-permute-start(bf16[128,1152]{1,0:T(8,128)(2,1)S(1)} %collective-permute-done.10), channel_id=1, source_target_pairs={{0,32},{1,481},{32,64},{33,1},{64,96},{65,33},{96,128},{97,65},{12... | collective-permute-start | bytes 884744 | tf_op jit(solution)/shard_map/ppermute | solution.py:33
  35.5 8.7 %collective-permute-start.3 = (bf16[128,1152]{1,0:T(8,128)(2,1)S(1)}, bf16[128,1152]{1,0:T(8,128)(2,1)S(1)}, u32[]{:S(2)}, u32[]{:S(2)}) collective-permute-start(bf16[128,1152]{1,0:T(8,128)(2,1)S(1)} %collective-permute-done.2), channel_id=1, source_target_pairs={{0,32},{1,481},{32,64},{33,1},{64,96},{65,33},{96,128},{97,65},{12... | collective-permute-start | bytes 884744 | tf_op jit(solution)/shard_map/ppermute | solution.py:33
  40.5 8.7 %collective-permute-start.12 = (bf16[128,1152]{1,0:T(8,128)(2,1)S(1)}, bf16[128,1152]{1,0:T(8,128)(2,1)S(1)}, u32[]{:S(2)}, u32[]{:S(2)}) collective-permute-start(bf16[128,1152]{1,0:T(8,128)(2,1)S(1)} %collective-permute-done.11), channel_id=1, source_target_pairs={{0,32},{1,481},{32,64},{33,1},{64,96},{65,33},{96,128},{97,65},{12... | collective-permute-start | bytes 884744 | tf_op jit(solution)/shard_map/ppermute | solution.py:33
  44.1 8.7 %collective-permute-start.4 = (bf16[128,1152]{1,0:T(8,128)(2,1)S(1)}, bf16[128,1152]{1,0:T(8,128)(2,1)S(1)}, u32[]{:S(2)}, u32[]{:S(2)}) collective-permute-start(bf16[128,1152]{1,0:T(8,128)(2,1)S(1)} %collective-permute-done.3), channel_id=1, source_target_pairs={{0,32},{1,481},{32,64},{33,1},{64,96},{65,33},{96,128},{97,65},{12... | collective-permute-start | bytes 884744 | tf_op jit(solution)/shard_map/ppermute | solution.py:33
  49.2 8.7 %collective-permute-start.14 = (bf16[128,1152]{1,0:T(8,128)(2,1)S(1)}, bf16[128,1152]{1,0:T(8,128)(2,1)}, u32[]{:S(2)}, u32[]{:S(2)}) collective-permute-start(bf16[128,1152]{1,0:T(8,128)(2,1)S(1)} %collective-permute-done.12), channel_id=1, source_target_pairs={{0,32},{1,481},{32,64},{33,1},{64,96},{65,33},{96,128},{97,65},{12... | collective-permute-start | bytes 884744 | tf_op jit(solution)/shard_map/ppermute | solution.py:33
  52.8 8.7 %collective-permute-start.5 = (bf16[128,1152]{1,0:T(8,128)(2,1)S(1)}, bf16[128,1152]{1,0:T(8,128)(2,1)S(1)}, u32[]{:S(2)}, u32[]{:S(2)}) collective-permute-start(bf16[128,1152]{1,0:T(8,128)(2,1)S(1)} %collective-permute-done.4), channel_id=1, source_target_pairs={{0,32},{1,481},{32,64},{33,1},{64,96},{65,33},{96,128},{97,65},{12... | collective-permute-start | bytes 884744 | tf_op jit(solution)/shard_map/ppermute | solution.py:33
  57.8 8.7 %collective-permute-start.15 = (bf16[128,1152]{1,0:T(8,128)(2,1)}, bf16[128,1152]{1,0:T(8,128)(2,1)}, u32[]{:S(2)}, u32[]{:S(2)}) collective-permute-start(bf16[128,1152]{1,0:T(8,128)(2,1)} %collective-permute-done.14), channel_id=1, source_target_pairs={{0,32},{1,481},{32,64},{33,1},{64,96},{65,33},{96,128},{97,65},{12... | collective-permute-start | bytes 884744 | tf_op jit(solution)/shard_map/ppermute | solution.py:33
  61.5 8.7 %collective-permute-start.6 = (bf16[128,1152]{1,0:T(8,128)(2,1)S(1)}, bf16[128,1152]{1,0:T(8,128)(2,1)S(1)}, u32[]{:S(2)}, u32[]{:S(2)}) collective-permute-start(bf16[128,1152]{1,0:T(8,128)(2,1)S(1)} %collective-permute-done.5), channel_id=1, source_target_pairs={{0,32},{1,481},{32,64},{33,1},{64,96},{65,33},{96,128},{97,65},{12... | collective-permute-start | bytes 884744 | tf_op jit(solution)/shard_map/ppermute | solution.py:33
  66.5 8.7 %collective-permute-start.17 = (bf16[128,1152]{1,0:T(8,128)(2,1)}, bf16[128,1152]{1,0:T(8,128)(2,1)}, u32[]{:S(2)}, u32[]{:S(2)}) collective-permute-start(bf16[128,1152]{1,0:T(8,128)(2,1)} %collective-permute-done.15), channel_id=1, source_target_pairs={{0,32},{1,481},{32,64},{33,1},{64,96},{65,33},{96,128},{97,65},{12... | collective-permute-start | bytes 884744 | tf_op jit(solution)/shard_map/ppermute | solution.py:33
  70.1 15.4 %collective-permute-start.7 = (bf16[128,1152]{1,0:T(8,128)(2,1)S(1)}, bf16[128,1152]{1,0:T(8,128)(2,1)}, u32[]{:S(2)}, u32[]{:S(2)}) collective-permute-start(bf16[128,1152]{1,0:T(8,128)(2,1)S(1)} %collective-permute-done.6), channel_id=1, source_target_pairs={{0,32},{1,481},{32,64},{33,1},{64,96},{65,33},{96,128},{97,65},{12... | collective-permute-start | bytes 884744 | tf_op jit(solution)/shard_map/ppermute | solution.py:33
  75.2 18.3 %collective-permute-start.18 = (bf16[128,1152]{1,0:T(8,128)(2,1)}, bf16[128,1152]{1,0:T(8,128)(2,1)S(1)}, u32[]{:S(2)}, u32[]{:S(2)}) collective-permute-start(bf16[128,1152]{1,0:T(8,128)(2,1)} %collective-permute-done.17), channel_id=1, source_target_pairs={{0,32},{1,481},{32,64},{33,1},{64,96},{65,33},{96,128},{97,65},{12... | collective-permute-start | bytes 884744 | tf_op jit(solution)/shard_map/ppermute | solution.py:33
  79.2 19.1 %collective-permute-start.13 = (bf16[3,128,1152]{2,1,0:T(8,128)(2,1)S(1)}, bf16[3,128,1152]{2,1,0:T(8,128)(2,1)S(1)}, u32[]{:S(2)}, u32[]{:S(2)}) collective-permute-start(bf16[3,128,1152]{2,1,0:T(8,128)(2,1)S(1)} %pad_maximum_fusion.3), channel_id=1, source_target_pairs={{0,1},{1,0},{2,3},{3,2},{4,5},{5,4},{6,7},{7,6},{8,9},{9,8},{10,11... | collective-permute-start | bytes 2654216 | tf_op jit(solution)/shard_map/ppermute | solution.py:37
  85.6 11.4 %collective-permute-start.8 = (bf16[128,1152]{1,0:T(8,128)(2,1)}, bf16[128,1152]{1,0:T(8,128)(2,1)S(1)}, u32[]{:S(2)}, u32[]{:S(2)}) collective-permute-start(bf16[128,1152]{1,0:T(8,128)(2,1)} %collective-permute-done.7), channel_id=1, source_target_pairs={{0,32},{1,481},{32,64},{33,1},{64,96},{65,33},{96,128},{97,65},{12... | collective-permute-start | bytes 884744 | tf_op jit(solution)/shard_map/ppermute | solution.py:33
  91.5 6.8 %collective-permute-start.16 = (bf16[2,128,1152]{2,1,0:T(8,128)(2,1)S(1)}, bf16[2,128,1152]{2,1,0:T(8,128)(2,1)S(1)}, u32[]{:S(2)}, u32[]{:S(2)}) collective-permute-start(bf16[2,128,1152]{2,1,0:T(8,128)(2,1)S(1)} %pad_maximum_fusion.4), channel_id=1, source_target_pairs={{0,1},{1,0},{2,3},{3,2},{4,5},{5,4},{6,7},{7,6},{8,9},{9,8},{10,11... | collective-permute-start | bytes 1769480 | tf_op jit(solution)/shard_map/ppermute | solution.py:37
  94.5 4.0 %collective-permute-start.19 = (bf16[2,128,1152]{2,1,0:T(8,128)(2,1)S(1)}, bf16[2,128,1152]{2,1,0:T(8,128)(2,1)S(1)}, u32[]{:S(2)}, u32[]{:S(2)}) collective-permute-start(bf16[2,128,1152]{2,1,0:T(8,128)(2,1)S(1)} %pad_maximum_fusion.5), channel_id=1, source_target_pairs={{0,1},{1,0},{2,3},{3,2},{4,5},{5,4},{6,7},{7,6},{8,9},{9,8},{10,11... | collective-permute-start | bytes 1769480 | tf_op jit(solution)/shard_map/ppermute | solution.py:37
  98.6 2.1 copy-start
  127.9 21.8 %all-to-all-start.1 = ((bf16[16,256,128]{2,1,0:T(8,128)(2,1)}), bf16[16,256,128]{2,1,0:T(8,128)(2,1)S(1)}, u32[]{:S(2)}, u32[]{:S(2)}) async-start(bf16[16,256,128]{2,1,0:T(8,128)(2,1)} %broadcast_in_dim.15), calls=%async_computation.1 | async-start | bytes 2097152 | tf_op jit(solution)/shard_map/all_to_all | solution.py:17
  149.9 53.9 %slice-start = ((s8[4718592]{0:T(1024)(128)(4,1)}), s8[524288]{0:T(1024)(128)(4,1)S(1)}, s32[]{:S(2)}) async-start(s8[4718592]{0:T(1024)(128)(4,1)} %bitcast.177), calls=%async_computation.3 | async-start | bytes 1048576
  151.2 28.7 %collective-permute-start.23 = (bf16[4,4,128,256]{3,2,1,0:T(8,128)(2,1)}, bf16[4,4,128,256]{3,2,1,0:T(8,128)(2,1)S(1)}, u32[]{:S(2)}, u32[]{:S(2)}) collective-permute-start(bf16[4,4,128,256]{3,2,1,0:T(8,128)(2,1)} %pad_maximum_fusion.2), channel_id=1, source_target_pairs={{0,1},{1,0},{2,3},{3,2},{4,5},{5,4},{6,7},{7,6},{8,9},{9,8},{10,11... | collective-permute-start | bytes 3145736 | tf_op jit(solution)/shard_map/ppermute | solution.py:130
  158.6 22.4 %collective-permute-start.20 = (bf16[2,4,128,128]{3,2,1,0:T(8,128)(2,1)S(1)}, bf16[2,4,128,128]{3,2,1,0:T(8,128)(2,1)}, u32[]{:S(2)}, u32[]{:S(2)}) collective-permute-start(bf16[2,4,128,128]{3,2,1,0:T(8,128)(2,1)S(1)} %bitcast.191), channel_id=1, source_target_pairs={{0,480},{32,0},{64,32},{96,64},{128,96},{160,128},{192,160},{224,1... | collective-permute-start | bytes 786440 | tf_op jit(solution)/shard_map/ppermute | solution.py:23
  162.3 16.5 %collective-permute-start.21 = (bf16[2,4,128,128]{3,2,1,0:T(8,128)(2,1)S(1)}, bf16[2,4,128,128]{3,2,1,0:T(8,128)(2,1)}, u32[]{:S(2)}, u32[]{:S(2)}) collective-permute-start(bf16[2,4,128,128]{3,2,1,0:T(8,128)(2,1)S(1)} %bitcast.192), channel_id=1, source_target_pairs={{0,32},{32,64},{64,96},{96,128},{128,160},{160,192},{192,224},{224... | collective-permute-start | bytes 786440 | tf_op jit(solution)/shard_map/ppermute | solution.py:23
  165.0 17.2 %collective-permute-start.24 = (bf16[4,128,128]{2,1,0:T(8,128)(2,1)}, bf16[4,128,128]{2,1,0:T(8,128)(2,1)}, u32[]{:S(2)}, u32[]{:S(2)}) collective-permute-start(bf16[4,128,128]{2,1,0:T(8,128)(2,1)} %get-tuple-element.37), channel_id=1, source_target_pairs={{0,64},{32,96},{64,128},{96,160},{128,192},{160,224},{192,256},{22... | collective-permute-start | bytes 393224 | tf_op jit(solution)/shard_map/ppermute | solution.py:23
  166.9 10.8 %collective-permute-start.22 = (bf16[4,128,128]{2,1,0:T(8,128)(2,1)}, bf16[4,128,128]{2,1,0:T(8,128)(2,1)}, u32[]{:S(2)}, u32[]{:S(2)}) collective-permute-start(bf16[4,128,128]{2,1,0:T(8,128)(2,1)} %get-tuple-element.38), channel_id=1, source_target_pairs={{0,448},{32,480},{64,0},{96,32},{128,64},{160,96},{192,128},{224,1... | collective-permute-start | bytes 393224 | tf_op jit(solution)/shard_map/ppermute | solution.py:23
  182.1 21.7 %slice-start.1 = ((s8[4718592]{0:T(1024)(128)(4,1)}), s8[4194304]{0:T(1024)(128)(4,1)S(1)}, s32[]{:S(2)}) async-start(s8[4718592]{0:T(1024)(128)(4,1)} %bitcast.177), calls=%async_computation.4 | async-start | bytes 8388608
  205.6 11.4 %collective-permute-start.25 = (bf16[128,1152]{1,0:T(8,128)(2,1)S(1)}, bf16[128,1152]{1,0:T(8,128)(2,1)S(1)}, u32[]{:S(2)}, u32[]{:S(2)}) collective-permute-start(bf16[128,1152]{1,0:T(8,128)(2,1)S(1)} %fusion), channel_id=1, source_target_pairs={{0,0},{1,16},{16,1},{17,17},{2,2},{3,18},{18,3},{19,19},{4,4},{5,2... | collective-permute-start | bytes 884744 | tf_op jit(solution)/shard_map/ppermute | solution.py:144
  212.6 7.6 %collective-permute-start.26 = (bf16[128,1152]{1,0:T(8,128)(2,1)S(1)}, bf16[128,1152]{1,0:T(8,128)(2,1)S(1)}, u32[]{:S(2)}, u32[]{:S(2)}) collective-permute-start(bf16[128,1152]{1,0:T(8,128)(2,1)S(1)} %convolution_convert_fusion), channel_id=1, source_target_pairs={{0,16},{1,0},{16,17},{17,1},{2,18},{3,2},{18,19},{19,3},{4,20},{5,... | collective-permute-start | bytes 884744 | tf_op jit(solution)/shard_map/ppermute | solution.py:142

commit v11 on v10

--- a/solution.py
+++ b/solution.py
@@ -17,20 +17,19 @@
     return lax.all_to_all(copies, PLANE, 0, 0)
 
 
-def along(piece, shift):
+def along(piece, shift, shift_of_core_1=None):
     size = lax.axis_size(LINE)
-    pairs = [(place, (place + shift) % size) for place in range(size)]
-    return lax.ppermute(piece, LINE, pairs)
-
-
-def onward(piece):
-    size = lax.axis_size(LINE)
+    shifts = (shift, shift if shift_of_core_1 is None else shift_of_core_1)
     pairs = [
-        (2 * place + core, 2 * ((place + 1 - 2 * core) % size) + core)
+        (2 * place + core, 2 * ((place + shifts[core]) % size) + core)
         for place in range(size)
         for core in range(2)
     ]
     return lax.ppermute(piece, LINE + ("core",), pairs)
+
+
+def onward(piece):
+    return along(piece, 1, -1)
 
 
 def swap(pieces):
@@ -55,6 +54,37 @@
     )
 
 
+def products(blocks, both, chips, whole=None):
+    rows = both.shape[0] // 2
+    exact = nt(blocks, both)
+    parts = [lax.reduce_precision(exact, 8, 7)]
+    if whole is not None:
+        here = slice(whole * rows, (whole + 1) * rows)
+        parts.append(exact[here] - parts[0][here])
+    parts = [
+        part.astype(jnp.bfloat16)
+        .reshape(-1, chips, rows // chips, 2, rows)
+        .transpose(1, 3, 0, 2, 4)
+        .reshape(chips, -1, rows)
+        for part in parts
+    ]
+    return jnp.concatenate(parts, 1)
+
+
+def plane_sum(parts):
+    return lax.all_to_all(parts, PLANE, 0, 0).astype(jnp.float32).sum(0)
+
+
+def blocks_of(summed, count):
+    rows = summed.shape[1]
+    size = 2 * count * (rows // 16)
+    blocks = summed[:size].reshape(2, count, -1, rows)
+    if summed.shape[0] == size:
+        return blocks
+    rest = summed[size:].reshape(2, 1, -1, rows)
+    return jnp.concatenate([blocks[:, :-1], blocks[:, -1:] + rest], 1)
+
+
 def wide(halves):
     return jnp.concatenate([halves[0], halves[1]], 1)
 
@@ -77,37 +107,32 @@
     residue = lax.axis_index("zl")
     own = lax.ppermute(rounded, ("ylo", "core"), TURN)
     other = lax.ppermute(own, "core", SWAP)
+    both = jnp.concatenate([own, other], 0)
     near, far = [own], [other]
     for step in range(1, slabs // 2):
         near.append(onward(near[-1]))
         far.append(onward(far[-1]))
+    first = 6
+    half_early = jnp.concatenate(near[first - 1 :: -1], 0)
+    early = plane_sum(products(half_early, both, chips, first - 1))
+    early, near[-1] = lax.optimization_barrier((early, near[-1]))
     near.append(onward(near[-1]))
     back = swap(far[1:4]) + swap(far[4:6]) + swap(far[6:])
-    half = jnp.concatenate(near[::-1] + back, 0)
-    exact = [nt(half, side) for side in (own, other)]
-    parts = [lax.reduce_precision(side, 8, 7) for side in exact]
-    middle = slabs // 2
-    begin, end = middle * rows, (middle + 1) * rows
-    rest = [one[begin:end] - two[begin:end] for one, two in zip(exact, parts)]
-    parts = [
-        jnp.stack(sides).astype(jnp.bfloat16).reshape(2, -1, chips, rows // chips, rows)
-        for sides in (parts, rest)
-    ]
-    parts = [
-        part.transpose(2, 0, 1, 3, 4).reshape(chips, -1, rows) for part in parts
-    ]
-    parts = jnp.concatenate(parts, 1)
-    parts, slab, core, residue = lax.optimization_barrier((parts, slab, core, residue))
-    parts = lax.all_to_all(parts, PLANE, 0, 0)
-    parts, half, own, slab, core, residue = lax.optimization_barrier(
-        (parts, half, own, slab, core, residue)
+    half_late = jnp.concatenate(near[: first - 1 : -1] + back, 0)
+    late = products(half_late, both, chips)
+    early = blocks_of(early, first)
+    late, early, slab, core, residue = lax.optimization_barrier(
+        (late, early, slab, core, residue)
     )
-    gram = parts.astype(jnp.float32).sum(0) / total_cols
-    rest = gram[2 * rows :].reshape(2, 1, rows // chips, rows)
-    gram = gram[: 2 * rows].reshape(2, slabs, rows // chips, rows)
-    gram = jnp.concatenate(
-        [gram[:, :middle], gram[:, middle : middle + 1] + rest, gram[:, middle + 1 :]], 1
+    late = lax.all_to_all(late, PLANE, 0, 0)
+    late, early, half_early, half_late, own, slab, core, residue = (
+        lax.optimization_barrier(
+            (late, early, half_early, half_late, own, slab, core, residue)
+        )
     )
+    late = blocks_of(late.astype(jnp.float32).sum(0), slabs - first)
+    ahead = slabs // 2 + 1 - first
+    gram = jnp.concatenate([late[:, :ahead], early, late[:, ahead:]], 1) / total_cols
     gram = jnp.where(core == 0, gram, gram[:, ::-1])
     gram = turn_to(gram, slabs + slabs // 2 - core - slab)
     gram_low = gram.astype(jnp.bfloat16).reshape(2 * rows, rows)
@@ -121,7 +146,7 @@
         here,
         along(here, -1),
         along(here, 1),
-        (along(here[0], -2), along(here[1], 2)),
+        along(here, -2, 2),
     )
     right_own = [
         lax.dynamic_index_in_dim(panel, (residue + shift) % steps, 1, False)
@@ -138,9 +163,16 @@
     panel = share(poly.reshape(2 * rows, rows), chips)
     panel = panel.reshape(chips, 2, slabs, rows // chips, rows)
     panel = panel.transpose(2, 0, 3, 1, 4).reshape(slabs * rows, 2 * rows)
-    away = tn(panel[:, rows:], half).astype(jnp.bfloat16)
-    away = lax.ppermute(away, ("ylo", "core"), CROSS)
-    stay = tn(panel[:, :rows], half) + 3.4445 * own.astype(jnp.float32)
+    panel = panel.reshape(slabs, rows, 2 * rows)
+    panel_early = panel[ahead : ahead + first].reshape(first * rows, 2 * rows)
+    panel_late = jnp.concatenate([panel[:ahead], panel[ahead + first :]], 0)
+    panel_late = panel_late.reshape((slabs - first) * rows, 2 * rows)
+    away, stay = (
+        tn(panel_early[:, part], half_early) + tn(panel_late[:, part], half_late)
+        for part in (slice(rows, None), slice(rows))
+    )
+    away = lax.ppermute(away.astype(jnp.bfloat16), ("ylo", "core"), CROSS)
+    stay = stay + 3.4445 * own.astype(jnp.float32)
     stay = lax.ppermute(stay.astype(jnp.bfloat16), ("ylo", "core"), TURN)
     return stay.astype(jnp.float32) + away.astype(jnp.float32)
 

time: 223 us -> 240 us (1.076)
  waiting for transfers between devices: 18.1 us -> 29.2 us
  local copies, waits for them, and re-layouts: 5.29 us -> 15.7 us
  starting transfers between devices: 119 us -> 112 us
  other arithmetic: 5.98 us -> 9.43 us
    ppermute x20 -> x19, waiting for transfers between devices: 11.2 us -> 22.8 us  [the longest x18 19.3 us: along(): return lax.ppermute(piece, LINE + ('core',), pairs)]
    ppermute x20 -> x19, starting transfers between devices: 83.7 us -> 73.2 us  [the longest x18 71.2 us: along(): return lax.ppermute(piece, LINE + ('core',), pairs)]
    unnamed x21 -> x35, local copies, waits for them, and re-layouts: 2.17 us -> 11.6 us
    all_to_all x0 -> x1, starting transfers between devices: none -> 6.65 us  [plane_sum(): return lax.all_to_all(parts, PLANE, 0, 0).astype(jnp.float32).sum(0)]
    all_to_all x1, blocking collectives: 23.6 us -> 19.4 us  [per_device(): late = lax.all_to_all(late, PLANE, 0, 0)]
    ppermute x1, starting transfers between devices: 7.47 us -> 4.57 us  [per_device(): right_other = lax.ppermute(jnp.stack(right_own), 'core', SWAP)]
    another operation x3, other arithmetic: 2.26 us -> 5.04 us  [swap(): return list(lax.ppermute(jnp.stack(pieces), 'core', SWAP))]
  transfers between devices with their start and end apart: 28 -> 28, of which waited for: 11 -> 11; matrix products, arithmetic and copies ran while one was open for 4% -> 10% of each run, Pallas kernels for 0% -> 0%
where the time goes in v11:
time: 240 us; the launch traced here: 238 us
  starting transfers between devices  112 us (47%)
  blocking collectives  59.3 us (25%)
  waiting for transfers between devices  29.2 us (12%)
  local copies, waits for them, and re-layouts  15.7 us (7%)
  matrix products  12.2 us (5%)
  other arithmetic  9.43 us (4%)
    ppermute x18, starting transfers between devices, along(): return lax.ppermute(piece, LINE + ('core',), pairs)  71.2 us
    all_to_all x1, blocking collectives, share(): return lax.all_to_all(copies, PLANE, 0, 0)  20.5 us
    all_to_all x1, blocking collectives, per_device(): late = lax.all_to_all(late, PLANE, 0, 0)  19.4 us
    all_gather x1, blocking collectives, per_device(): here = lax.all_gather(gram_low, 'zh', axis=0).reshape(groups, 2, rows, rows)  19.4 us
    ppermute x18, waiting for transfers between devices, along(): return lax.ppermute(piece, LINE + ('core',), pairs)  19.3 us
    unnamed x35, local copies, waits for them, and re-layouts  11.6 us
    ppermute x3, starting transfers between devices, swap(): return list(lax.ppermute(jnp.stack(pieces), 'core', SWAP))  11.6 us
    dot_general x8, matrix products, mix(): lax.dot_general(left, right, (((0, 2), (0, 1)), ((), ())), preferred_elem...  8.25 us
  transfers between devices with their start and end apart: 28, of which 11 were waited for; matrix products, arithmetic and copies ran while one was open for 10% of the time, Pallas kernels for 0%

profile of v11, /device:TPU:1, one launch (start us, length us, event | category | flops | bytes accessed | tf_op | source)
XLA Modules:
  0.0 238.3 jit_solution(1478402471826223488)
XLA Ops:
  0.0 1.1 convert_element_type.39
  1.1 4.6 %collective-permute-start = (bf16[128,1152]{1,0:T(8,128)(2,1)S(1)}, bf16[128,1152]{1,0:T(8,128)(2,1)S(1)}, u32[]{:S(2)}, u32[]{:S(2)}) collective-permute-start(bf16[128,1152]{1,0:T(8,128)(2,1)S(1)} %convert_element_type.39), channel_id=1, source_target_pairs={{0,0},{1,16},{16,1},{17,17},{2,2},{3,18},{18,3},{19,19},{4,4},{5,2... | collective-permute-start | bytes 884744 | tf_op jit(solution)/shard_map/ppermute | solution.py:108
  5.7 4.4 %collective-permute-done = bf16[128,1152]{1,0:T(8,128)(2,1)S(1)} collective-permute-done((bf16[128,1152]{1,0:T(8,128)(2,1)S(1)}, bf16[128,1152]{1,0:T(8,128)(2,1)S(1)}, u32[]{:S(2)}, u32[]{:S(2)}) %collective-permute-start) | collective-permute-done | bytes 294944 | tf_op jit(solution)/shard_map/ppermute | solution.py:108
  10.1 11.4 %collective-permute-start.1 = (bf16[128,1152]{1,0:T(8,128)(2,1)S(1)}, bf16[128,1152]{1,0:T(8,128)(2,1)S(1)}, u32[]{:S(2)}, u32[]{:S(2)}) collective-permute-start(bf16[128,1152]{1,0:T(8,128)(2,1)S(1)} %collective-permute-done), channel_id=1, source_target_pairs={{0,32},{1,481},{32,64},{33,1},{64,96},{65,33},{96,128},{97,65},{12... | collective-permute-start | bytes 884744 | tf_op jit(solution)/shard_map/ppermute | solution.py:28
  21.5 1.9 collective-permute-start.6
  23.4 1.7 collective-permute-done.1
  25.2 5.0 %collective-permute-start.2 = (bf16[128,1152]{1,0:T(8,128)(2,1)S(1)}, bf16[128,1152]{1,0:T(8,128)(2,1)S(1)}, u32[]{:S(2)}, u32[]{:S(2)}) collective-permute-start(bf16[128,1152]{1,0:T(8,128)(2,1)S(1)} %collective-permute-done.1), channel_id=1, source_target_pairs={{0,32},{1,481},{32,64},{33,1},{64,96},{65,33},{96,128},{97,65},{12... | collective-permute-start | bytes 884744 | tf_op jit(solution)/shard_map/ppermute | solution.py:28
  30.2 1.9 collective-permute-start.10
  32.1 1.7 collective-permute-done.2
  33.8 5.0 %collective-permute-start.3 = (bf16[128,1152]{1,0:T(8,128)(2,1)S(1)}, bf16[128,1152]{1,0:T(8,128)(2,1)S(1)}, u32[]{:S(2)}, u32[]{:S(2)}) collective-permute-start(bf16[128,1152]{1,0:T(8,128)(2,1)S(1)} %collective-permute-done.2), channel_id=1, source_target_pairs={{0,32},{1,481},{32,64},{33,1},{64,96},{65,33},{96,128},{97,65},{12... | collective-permute-start | bytes 884744 | tf_op jit(solution)/shard_map/ppermute | solution.py:28
  38.9 3.1 %collective-permute-start.11 = (bf16[128,1152]{1,0:T(8,128)(2,1)S(1)}, bf16[128,1152]{1,0:T(8,128)(2,1)S(1)}, u32[]{:S(2)}, u32[]{:S(2)}) collective-permute-start(bf16[128,1152]{1,0:T(8,128)(2,1)S(1)} %collective-permute-done.10), channel_id=1, source_target_pairs={{0,32},{1,481},{32,64},{33,1},{64,96},{65,33},{96,128},{97,65},{12... | collective-permute-start | bytes 884744 | tf_op jit(solution)/shard_map/ppermute | solution.py:28
  42.5 5.0 %collective-permute-start.4 = (bf16[128,1152]{1,0:T(8,128)(2,1)S(1)}, bf16[128,1152]{1,0:T(8,128)(2,1)S(1)}, u32[]{:S(2)}, u32[]{:S(2)}) collective-permute-start(bf16[128,1152]{1,0:T(8,128)(2,1)S(1)} %collective-permute-done.3), channel_id=1, source_target_pairs={{0,32},{1,481},{32,64},{33,1},{64,96},{65,33},{96,128},{97,65},{12... | collective-permute-start | bytes 884744 | tf_op jit(solution)/shard_map/ppermute | solution.py:28
  47.5 3.1 %collective-permute-start.12 = (bf16[128,1152]{1,0:T(8,128)(2,1)S(1)}, bf16[128,1152]{1,0:T(8,128)(2,1)S(1)}, u32[]{:S(2)}, u32[]{:S(2)}) collective-permute-start(bf16[128,1152]{1,0:T(8,128)(2,1)S(1)} %collective-permute-done.11), channel_id=1, source_target_pairs={{0,32},{1,481},{32,64},{33,1},{64,96},{65,33},{96,128},{97,65},{12... | collective-permute-start | bytes 884744 | tf_op jit(solution)/shard_map/ppermute | solution.py:28
  51.2 5.0 %collective-permute-start.5 = (bf16[128,1152]{1,0:T(8,128)(2,1)S(1)}, bf16[128,1152]{1,0:T(8,128)(2,1)}, u32[]{:S(2)}, u32[]{:S(2)}) collective-permute-start(bf16[128,1152]{1,0:T(8,128)(2,1)S(1)} %collective-permute-done.4), channel_id=1, source_target_pairs={{0,32},{1,481},{32,64},{33,1},{64,96},{65,33},{96,128},{97,65},{12... | collective-permute-start | bytes 884744 | tf_op jit(solution)/shard_map/ppermute | solution.py:28
  56.2 3.1 %collective-permute-start.14 = (bf16[128,1152]{1,0:T(8,128)(2,1)S(1)}, bf16[128,1152]{1,0:T(8,128)(2,1)}, u32[]{:S(2)}, u32[]{:S(2)}) collective-permute-start(bf16[128,1152]{1,0:T(8,128)(2,1)S(1)} %collective-permute-done.12), channel_id=1, source_target_pairs={{0,32},{1,481},{32,64},{33,1},{64,96},{65,33},{96,128},{97,65},{12... | collective-permute-start | bytes 884744 | tf_op jit(solution)/shard_map/ppermute | solution.py:28
  59.8 1.0 constant_dynamic-update-slice_fusion.5
  60.8 1.0 constant_dynamic-update-slice_fusion.4
  61.8 1.0 constant_dynamic-update-slice_fusion.3
  62.8 1.0 constant_dynamic-update-slice_fusion.2
  64.8 5.1 %collective-permute-start.7 = (bf16[128,1152]{1,0:T(8,128)(2,1)}, bf16[128,1152]{1,0:T(8,128)(2,1)}, u32[]{:S(2)}, u32[]{:S(2)}) collective-permute-start(bf16[128,1152]{1,0:T(8,128)(2,1)} %collective-permute-done.5), channel_id=1, source_target_pairs={{0,32},{1,481},{32,64},{33,1},{64,96},{65,33},{96,128},{97,65},{12... | collective-permute-start | bytes 884744 | tf_op jit(solution)/shard_map/ppermute | solution.py:28
  69.9 1.9 collective-permute-start.15
  72.7 6.6 %all-to-all-start = ((bf16[16,112,128]{2,1,0:T(8,128)(2,1)}), bf16[16,112,128]{2,1,0:T(8,128)(2,1)S(1)}, u32[]{:S(2)}, u32[]{:S(2)}) async-start(bf16[16,112,128]{2,1,0:T(8,128)(2,1)} %pad_maximum_fusion.5), calls=%async_computation | async-start | bytes 917504 | tf_op jit(solution)/shard_map/all_to_all | solution.py:75
  79.3 2.1 pad_maximum_fusion.1
  81.4 5.2 %collective-permute-start.13 = (bf16[3,128,1152]{2,1,0:T(8,128)(2,1)}, bf16[3,128,1152]{2,1,0:T(8,128)(2,1)}, u32[]{:S(2)}, u32[]{:S(2)}) collective-permute-start(bf16[3,128,1152]{2,1,0:T(8,128)(2,1)} %pad_maximum_fusion.1), channel_id=1, source_target_pairs={{0,1},{1,0},{2,3},{3,2},{4,5},{5,4},{6,7},{7,6},{8,9},{9,8},{10,11... | collective-permute-start | bytes 2654216 | tf_op jit(solution)/shard_map/ppermute | solution.py:36
  86.6 4.9 %collective-permute-start.8 = (bf16[128,1152]{1,0:T(8,128)(2,1)}, bf16[128,1152]{1,0:T(8,128)(2,1)S(1)}, u32[]{:S(2)}, u32[]{:S(2)}) collective-permute-start(bf16[128,1152]{1,0:T(8,128)(2,1)} %collective-permute-done.7), channel_id=1, source_target_pairs={{0,32},{1,481},{32,64},{33,1},{64,96},{65,33},{96,128},{97,65},{12... | collective-permute-start | bytes 884744 | tf_op jit(solution)/shard_map/ppermute | solution.py:28
  91.5 3.6 %collective-permute-start.17 = (bf16[128,1152]{1,0:T(8,128)(2,1)}, bf16[128,1152]{1,0:T(8,128)(2,1)}, u32[]{:S(2)}, u32[]{:S(2)}) collective-permute-start(bf16[128,1152]{1,0:T(8,128)(2,1)} %collective-permute-done.15), channel_id=1, source_target_pairs={{0,32},{1,481},{32,64},{33,1},{64,96},{65,33},{96,128},{97,65},{12... | collective-permute-start | bytes 884744 | tf_op jit(solution)/shard_map/ppermute | solution.py:28
  95.1 1.9 pad_maximum_fusion.3
  97.1 1.9 collective-permute-start.16
  99.1 1.9 collective-permute-start.9
  101.0 3.1 %collective-permute-start.18 = (bf16[128,1152]{1,0:T(8,128)(2,1)}, bf16[128,1152]{1,0:T(8,128)(2,1)S(1)}, u32[]{:S(2)}, u32[]{:S(2)}) collective-permute-start(bf16[128,1152]{1,0:T(8,128)(2,1)} %collective-permute-done.17), channel_id=1, source_target_pairs={{0,32},{1,481},{32,64},{33,1},{64,96},{65,33},{96,128},{97,65},{12... | collective-permute-start | bytes 884744 | tf_op jit(solution)/shard_map/ppermute | solution.py:28
  104.1 5.9 %collective-permute-done.18 = bf16[128,1152]{1,0:T(8,128)(2,1)S(1)} collective-permute-done((bf16[128,1152]{1,0:T(8,128)(2,1)}, bf16[128,1152]{1,0:T(8,128)(2,1)S(1)}, u32[]{:S(2)}, u32[]{:S(2)}) %collective-permute-start.18) | collective-permute-done | bytes 294944 | tf_op jit(solution)/shard_map/ppermute | solution.py:28
  110.0 1.0 pad_maximum_fusion.4
  111.0 4.5 %collective-permute-start.19 = (bf16[2,128,1152]{2,1,0:T(8,128)(2,1)S(1)}, bf16[2,128,1152]{2,1,0:T(8,128)(2,1)S(1)}, u32[]{:S(2)}, u32[]{:S(2)}) collective-permute-start(bf16[2,128,1152]{2,1,0:T(8,128)(2,1)S(1)} %pad_maximum_fusion.4), channel_id=1, source_target_pairs={{0,1},{1,0},{2,3},{3,2},{4,5},{5,4},{6,7},{7,6},{8,9},{9,8},{10,11... | collective-permute-start | bytes 1769480 | tf_op jit(solution)/shard_map/ppermute | solution.py:36
  115.6 1.0 constant_dynamic-update-slice_fusion.8
  116.6 1.0 fusion.25
  117.6 1.0 fusion.24
  118.6 1.0 fusion.23
  119.6 1.0 fusion.22
  120.6 1.0 fusion.21
  121.7 1.1 fusion
  123.3 19.4 %all_to_all.20 = bf16[16,160,128]{2,1,0:T(8,128)(2,1)S(1)} all-to-all(bf16[16,160,128]{2,1,0:T(8,128)(2,1)S(1)} %bitcast.193), channel_id=1, replica_groups=mesh['zh'=4,'zl'=4,'ylo'=2,'x'=4,'yhi'=2,'core'=2] {'ylo','x','yhi'}, dimensions={0} | all-to-all | bytes 1310720 | tf_op jit(solution)/shard_map/all_to_all | solution.py:127
  143.0 1.2 broadcast_in_dim.15
  144.2 3.7 %all-to-all-start.2 = ((bf16[16,256,128]{2,1,0:T(8,128)(2,1)}), bf16[16,256,128]{2,1,0:T(8,128)(2,1)S(1)}, u32[]{:S(2)}, u32[]{:S(2)}) async-start(bf16[16,256,128]{2,1,0:T(8,128)(2,1)} %broadcast_in_dim.15), calls=%async_computation.2 | async-start | bytes 2097152 | tf_op jit(solution)/shard_map/all_to_all | solution.py:17
  147.9 19.4 %all_gather.3 = bf16[4,256,128]{2,1,0:T(8,128)(2,1)S(1)} all-gather(bf16[1,256,128]{2,1,0:T(8,128)(2,1)S(1)} %bitcast.208), channel_id=1, replica_groups=mesh['zh'=4,'zl'=4,'ylo'=2,'x'=4,'yhi'=2,'core'=2] {'zh'}, dimensions={0}, use_global_device_ids=true | all-gather | bytes 327680 | tf_op jit(solution)/shard_map/all_gather | solution.py:142
  168.3 1.5 copy.17
  169.9 1.1 pad_maximum_fusion
  171.0 4.6 %collective-permute-start.23 = (bf16[4,4,128,256]{3,2,1,0:T(8,128)(2,1)}, bf16[4,4,128,256]{3,2,1,0:T(8,128)(2,1)}, u32[]{:S(2)}, u32[]{:S(2)}) collective-permute-start(bf16[4,4,128,256]{3,2,1,0:T(8,128)(2,1)} %pad_maximum_fusion), channel_id=1, source_target_pairs={{0,1},{1,0},{2,3},{3,2},{4,5},{5,4},{6,7},{7,6},{8,9},{9,8},{10,11... | collective-permute-start | bytes 3145736 | tf_op jit(solution)/shard_map/ppermute | solution.py:155
  175.6 4.1 %collective-permute-start.20 = (bf16[2,4,128,128]{3,2,1,0:T(8,128)(2,1)S(1)}, bf16[2,4,128,128]{3,2,1,0:T(8,128)(2,1)}, u32[]{:S(2)}, u32[]{:S(2)}) collective-permute-start(bf16[2,4,128,128]{3,2,1,0:T(8,128)(2,1)S(1)} %bitcast.200), channel_id=1, source_target_pairs={{0,480},{1,481},{32,0},{33,1},{64,32},{65,33},{96,64},{97,65},{128... | collective-permute-start | bytes 786440 | tf_op jit(solution)/shard_map/ppermute | solution.py:28
  179.7 1.9 collective-permute-start.21
  181.6 1.9 collective-permute-start.22
  184.4 6.6 %collective-permute-done.21 = bf16[2,4,128,128]{3,2,1,0:T(8,128)(2,1)} collective-permute-done((bf16[2,4,128,128]{3,2,1,0:T(8,128)(2,1)S(1)}, bf16[2,4,128,128]{3,2,1,0:T(8,128)(2,1)}, u32[]{:S(2)}, u32[]{:S(2)}) %collective-permute-start.21) | collective-permute-done | bytes 262176 | tf_op jit(solution)/shard_map/ppermute | solution.py:28
  191.1 1.1 convolution_bitcast_fusion.5
  192.2 1.9 collective-permute-done.22
  194.1 1.1 convolution_bitcast_fusion.4
  195.2 1.2 convolution_bitcast_fusion.1
  196.4 1.2 convolution_bitcast_fusion
  197.6 1.2 convolution_bitcast_fusion.2
  198.8 1.1 fusion.12
  200.0 1.1 fusion.14
  201.5 20.5 %all_to_all.21 = bf16[16,256,128]{2,1,0:T(8,128)(2,1)S(1)} all-to-all(bf16[16,256,128]{2,1,0:T(8,128)(2,1)S(1)} %broadcast_in_dim.17), channel_id=1, replica_groups=mesh['zh'=4,'zl'=4,'ylo'=2,'x'=4,'yhi'=2,'core'=2] {'ylo','x','yhi'}, dimensions={0} | all-to-all | bytes 2097152 | tf_op jit(solution)/shard_map/all_to_all | solution.py:17
  224.1 5.4 %collective-permute-start.24 = (bf16[128,1152]{1,0:T(8,128)(2,1)S(1)}, bf16[128,1152]{1,0:T(8,128)(2,1)S(1)}, u32[]{:S(2)}, u32[]{:S(2)}) collective-permute-start(bf16[128,1152]{1,0:T(8,128)(2,1)S(1)} %fusion.2), channel_id=1, source_target_pairs={{0,0},{1,16},{16,1},{17,17},{2,2},{3,18},{18,3},{19,19},{4,4},{5,2... | collective-permute-start | bytes 884744 | tf_op jit(solution)/shard_map/ppermute | solution.py:176
  230.0 1.9 collective-permute-start.25
  231.9 2.0 collective-permute-done.24
  233.9 3.5 %collective-permute-done.25 = bf16[128,1152]{1,0:T(8,128)(2,1)S(1)} collective-permute-done((bf16[128,1152]{1,0:T(8,128)(2,1)S(1)}, bf16[128,1152]{1,0:T(8,128)(2,1)S(1)}, u32[]{:S(2)}, u32[]{:S(2)}) %collective-permute-start.25) | collective-permute-done | bytes 294944 | tf_op jit(solution)/shard_map/ppermute | solution.py:174
  (82 shorter events, 9.8 us)
Async XLA Ops:
  1.1 9.0 %collective-permute-start = (bf16[128,1152]{1,0:T(8,128)(2,1)S(1)}, bf16[128,1152]{1,0:T(8,128)(2,1)S(1)}, u32[]{:S(2)}, u32[]{:S(2)}) collective-permute-start(bf16[128,1152]{1,0:T(8,128)(2,1)S(1)} %convert_element_type.39), channel_id=1, source_target_pairs={{0,0},{1,16},{16,1},{17,17},{2,2},{3,18},{18,3},{19,19},{4,4},{5,2... | collective-permute-start | bytes 884744 | tf_op jit(solution)/shard_map/ppermute | solution.py:108
  10.1 15.1 %collective-permute-start.1 = (bf16[128,1152]{1,0:T(8,128)(2,1)S(1)}, bf16[128,1152]{1,0:T(8,128)(2,1)S(1)}, u32[]{:S(2)}, u32[]{:S(2)}) collective-permute-start(bf16[128,1152]{1,0:T(8,128)(2,1)S(1)} %collective-permute-done), channel_id=1, source_target_pairs={{0,32},{1,481},{32,64},{33,1},{64,96},{65,33},{96,128},{97,65},{12... | collective-permute-start | bytes 884744 | tf_op jit(solution)/shard_map/ppermute | solution.py:28
  21.5 8.7 %collective-permute-start.6 = (bf16[128,1152]{1,0:T(8,128)(2,1)S(1)}, bf16[128,1152]{1,0:T(8,128)(2,1)S(1)}, u32[]{:S(2)}, u32[]{:S(2)}) collective-permute-start(bf16[128,1152]{1,0:T(8,128)(2,1)S(1)} %collective-permute-done), channel_id=1, source_target_pairs={{0,1},{1,0},{2,3},{3,2},{4,5},{5,4},{6,7},{7,6},{8,9},{9,8},{10,11... | collective-permute-start | bytes 884744 | tf_op jit(solution)/shard_map/ppermute | solution.py:109
  25.2 8.7 %collective-permute-start.2 = (bf16[128,1152]{1,0:T(8,128)(2,1)S(1)}, bf16[128,1152]{1,0:T(8,128)(2,1)S(1)}, u32[]{:S(2)}, u32[]{:S(2)}) collective-permute-start(bf16[128,1152]{1,0:T(8,128)(2,1)S(1)} %collective-permute-done.1), channel_id=1, source_target_pairs={{0,32},{1,481},{32,64},{33,1},{64,96},{65,33},{96,128},{97,65},{12... | collective-permute-start | bytes 884744 | tf_op jit(solution)/shard_map/ppermute | solution.py:28
  30.2 8.7 %collective-permute-start.10 = (bf16[128,1152]{1,0:T(8,128)(2,1)S(1)}, bf16[128,1152]{1,0:T(8,128)(2,1)S(1)}, u32[]{:S(2)}, u32[]{:S(2)}) collective-permute-start(bf16[128,1152]{1,0:T(8,128)(2,1)S(1)} %collective-permute-done.6), channel_id=1, source_target_pairs={{0,32},{1,481},{32,64},{33,1},{64,96},{65,33},{96,128},{97,65},{12... | collective-permute-start | bytes 884744 | tf_op jit(solution)/shard_map/ppermute | solution.py:28
  33.8 13.7 %copy-start.5 = (bf16[128,1152]{1,0:T(8,128)(2,1)}, bf16[128,1152]{1,0:T(8,128)(2,1)S(1)}, u32[]{:S(2)}) copy-start(bf16[128,1152]{1,0:T(8,128)(2,1)S(1)} %collective-permute-done.2) | copy-start | bytes 884740
  33.8 8.7 %collective-permute-start.3 = (bf16[128,1152]{1,0:T(8,128)(2,1)S(1)}, bf16[128,1152]{1,0:T(8,128)(2,1)S(1)}, u32[]{:S(2)}, u32[]{:S(2)}) collective-permute-start(bf16[128,1152]{1,0:T(8,128)(2,1)S(1)} %collective-permute-done.2), channel_id=1, source_target_pairs={{0,32},{1,481},{32,64},{33,1},{64,96},{65,33},{96,128},{97,65},{12... | collective-permute-start | bytes 884744 | tf_op jit(solution)/shard_map/ppermute | solution.py:28
  38.9 8.7 %collective-permute-start.11 = (bf16[128,1152]{1,0:T(8,128)(2,1)S(1)}, bf16[128,1152]{1,0:T(8,128)(2,1)S(1)}, u32[]{:S(2)}, u32[]{:S(2)}) collective-permute-start(bf16[128,1152]{1,0:T(8,128)(2,1)S(1)} %collective-permute-done.10), channel_id=1, source_target_pairs={{0,32},{1,481},{32,64},{33,1},{64,96},{65,33},{96,128},{97,65},{12... | collective-permute-start | bytes 884744 | tf_op jit(solution)/shard_map/ppermute | solution.py:28
  42.5 16.9 %copy-start.6 = (bf16[128,1152]{1,0:T(8,128)(2,1)}, bf16[128,1152]{1,0:T(8,128)(2,1)S(1)}, u32[]{:S(2)}) copy-start(bf16[128,1152]{1,0:T(8,128)(2,1)S(1)} %collective-permute-done.3) | copy-start | bytes 884740
  42.5 8.7 %collective-permute-start.4 = (bf16[128,1152]{1,0:T(8,128)(2,1)S(1)}, bf16[128,1152]{1,0:T(8,128)(2,1)S(1)}, u32[]{:S(2)}, u32[]{:S(2)}) collective-permute-start(bf16[128,1152]{1,0:T(8,128)(2,1)S(1)} %collective-permute-done.3), channel_id=1, source_target_pairs={{0,32},{1,481},{32,64},{33,1},{64,96},{65,33},{96,128},{97,65},{12... | collective-permute-start | bytes 884744 | tf_op jit(solution)/shard_map/ppermute | solution.py:28
  47.5 16.3 %copy-start.3 = (bf16[128,1152]{1,0:T(8,128)(2,1)}, bf16[128,1152]{1,0:T(8,128)(2,1)S(1)}, u32[]{:S(2)}) copy-start(bf16[128,1152]{1,0:T(8,128)(2,1)S(1)} %collective-permute-done.11) | copy-start | bytes 884740
  47.5 8.7 %collective-permute-start.12 = (bf16[128,1152]{1,0:T(8,128)(2,1)S(1)}, bf16[128,1152]{1,0:T(8,128)(2,1)S(1)}, u32[]{:S(2)}, u32[]{:S(2)}) collective-permute-start(bf16[128,1152]{1,0:T(8,128)(2,1)S(1)} %collective-permute-done.11), channel_id=1, source_target_pairs={{0,32},{1,481},{32,64},{33,1},{64,96},{65,33},{96,128},{97,65},{12... | collective-permute-start | bytes 884744 | tf_op jit(solution)/shard_map/ppermute | solution.py:28
  51.2 8.2 %copy-start.7 = (bf16[128,1152]{1,0:T(8,128)(2,1)}, bf16[128,1152]{1,0:T(8,128)(2,1)S(1)}, u32[]{:S(2)}) copy-start(bf16[128,1152]{1,0:T(8,128)(2,1)S(1)} %collective-permute-done.4) | copy-start | bytes 884740
  51.2 8.7 %collective-permute-start.5 = (bf16[128,1152]{1,0:T(8,128)(2,1)S(1)}, bf16[128,1152]{1,0:T(8,128)(2,1)}, u32[]{:S(2)}, u32[]{:S(2)}) collective-permute-start(bf16[128,1152]{1,0:T(8,128)(2,1)S(1)} %collective-permute-done.4), channel_id=1, source_target_pairs={{0,32},{1,481},{32,64},{33,1},{64,96},{65,33},{96,128},{97,65},{12... | collective-permute-start | bytes 884744 | tf_op jit(solution)/shard_map/ppermute | solution.py:28
  56.2 8.5 %copy-start.4 = (bf16[128,1152]{1,0:T(8,128)(2,1)}, bf16[128,1152]{1,0:T(8,128)(2,1)S(1)}, u32[]{:S(2)}) copy-start(bf16[128,1152]{1,0:T(8,128)(2,1)S(1)} %collective-permute-done.12) | copy-start | bytes 884740
  56.2 13.7 %collective-permute-start.14 = (bf16[128,1152]{1,0:T(8,128)(2,1)S(1)}, bf16[128,1152]{1,0:T(8,128)(2,1)}, u32[]{:S(2)}, u32[]{:S(2)}) collective-permute-start(bf16[128,1152]{1,0:T(8,128)(2,1)S(1)} %collective-permute-done.12), channel_id=1, source_target_pairs={{0,32},{1,481},{32,64},{33,1},{64,96},{65,33},{96,128},{97,65},{12... | collective-permute-start | bytes 884744 | tf_op jit(solution)/shard_map/ppermute | solution.py:28
  64.8 21.8 %collective-permute-start.7 = (bf16[128,1152]{1,0:T(8,128)(2,1)}, bf16[128,1152]{1,0:T(8,128)(2,1)}, u32[]{:S(2)}, u32[]{:S(2)}) collective-permute-start(bf16[128,1152]{1,0:T(8,128)(2,1)} %collective-permute-done.5), channel_id=1, source_target_pairs={{0,32},{1,481},{32,64},{33,1},{64,96},{65,33},{96,128},{97,65},{12... | collective-permute-start | bytes 884744 | tf_op jit(solution)/shard_map/ppermute | solution.py:28
  69.9 21.6 %collective-permute-start.15 = (bf16[128,1152]{1,0:T(8,128)(2,1)}, bf16[128,1152]{1,0:T(8,128)(2,1)}, u32[]{:S(2)}, u32[]{:S(2)}) collective-permute-start(bf16[128,1152]{1,0:T(8,128)(2,1)} %collective-permute-done.14), channel_id=1, source_target_pairs={{0,32},{1,481},{32,64},{33,1},{64,96},{65,33},{96,128},{97,65},{12... | collective-permute-start | bytes 884744 | tf_op jit(solution)/shard_map/ppermute | solution.py:28
  72.7 26.3 %all-to-all-start = ((bf16[16,112,128]{2,1,0:T(8,128)(2,1)}), bf16[16,112,128]{2,1,0:T(8,128)(2,1)S(1)}, u32[]{:S(2)}, u32[]{:S(2)}) async-start(bf16[16,112,128]{2,1,0:T(8,128)(2,1)} %pad_maximum_fusion.5), calls=%async_computation | async-start | bytes 917504 | tf_op jit(solution)/shard_map/all_to_all | solution.py:75
  81.4 35.2 %collective-permute-start.13 = (bf16[3,128,1152]{2,1,0:T(8,128)(2,1)}, bf16[3,128,1152]{2,1,0:T(8,128)(2,1)}, u32[]{:S(2)}, u32[]{:S(2)}) collective-permute-start(bf16[3,128,1152]{2,1,0:T(8,128)(2,1)} %pad_maximum_fusion.1), channel_id=1, source_target_pairs={{0,1},{1,0},{2,3},{3,2},{4,5},{5,4},{6,7},{7,6},{8,9},{9,8},{10,11... | collective-permute-start | bytes 2654216 | tf_op jit(solution)/shard_map/ppermute | solution.py:36
  86.6 12.5 %collective-permute-start.8 = (bf16[128,1152]{1,0:T(8,128)(2,1)}, bf16[128,1152]{1,0:T(8,128)(2,1)S(1)}, u32[]{:S(2)}, u32[]{:S(2)}) collective-permute-start(bf16[128,1152]{1,0:T(8,128)(2,1)} %collective-permute-done.7), channel_id=1, source_target_pairs={{0,32},{1,481},{32,64},{33,1},{64,96},{65,33},{96,128},{97,65},{12... | collective-permute-start | bytes 884744 | tf_op jit(solution)/shard_map/ppermute | solution.py:28
  91.5 9.5 %collective-permute-start.17 = (bf16[128,1152]{1,0:T(8,128)(2,1)}, bf16[128,1152]{1,0:T(8,128)(2,1)}, u32[]{:S(2)}, u32[]{:S(2)}) collective-permute-start(bf16[128,1152]{1,0:T(8,128)(2,1)} %collective-permute-done.15), channel_id=1, source_target_pairs={{0,32},{1,481},{32,64},{33,1},{64,96},{65,33},{96,128},{97,65},{12... | collective-permute-start | bytes 884744 | tf_op jit(solution)/shard_map/ppermute | solution.py:28
  97.1 22.5 %collective-permute-start.16 = (bf16[2,128,1152]{2,1,0:T(8,128)(2,1)}, bf16[2,128,1152]{2,1,0:T(8,128)(2,1)}, u32[]{:S(2)}, u32[]{:S(2)}) collective-permute-start(bf16[2,128,1152]{2,1,0:T(8,128)(2,1)} %pad_maximum_fusion.3), channel_id=1, source_target_pairs={{0,1},{1,0},{2,3},{3,2},{4,5},{5,4},{6,7},{7,6},{8,9},{9,8},{10,11... | collective-permute-start | bytes 1769480 | tf_op jit(solution)/shard_map/ppermute | solution.py:36
  99.1 16.4 %collective-permute-start.9 = (bf16[128,1152]{1,0:T(8,128)(2,1)S(1)}, bf16[128,1152]{1,0:T(8,128)(2,1)S(1)}, u32[]{:S(2)}, u32[]{:S(2)}) collective-permute-start(bf16[128,1152]{1,0:T(8,128)(2,1)S(1)} %collective-permute-done.8), channel_id=1, source_target_pairs={{0,32},{1,481},{32,64},{33,1},{64,96},{65,33},{96,128},{97,65},{12... | collective-permute-start | bytes 884744 | tf_op jit(solution)/shard_map/ppermute | solution.py:28
  101.0 9.0 %collective-permute-start.18 = (bf16[128,1152]{1,0:T(8,128)(2,1)}, bf16[128,1152]{1,0:T(8,128)(2,1)S(1)}, u32[]{:S(2)}, u32[]{:S(2)}) collective-permute-start(bf16[128,1152]{1,0:T(8,128)(2,1)} %collective-permute-done.17), channel_id=1, source_target_pairs={{0,32},{1,481},{32,64},{33,1},{64,96},{65,33},{96,128},{97,65},{12... | collective-permute-start | bytes 884744 | tf_op jit(solution)/shard_map/ppermute | solution.py:28
  111.0 10.6 %collective-permute-start.19 = (bf16[2,128,1152]{2,1,0:T(8,128)(2,1)S(1)}, bf16[2,128,1152]{2,1,0:T(8,128)(2,1)S(1)}, u32[]{:S(2)}, u32[]{:S(2)}) collective-permute-start(bf16[2,128,1152]{2,1,0:T(8,128)(2,1)S(1)} %pad_maximum_fusion.4), channel_id=1, source_target_pairs={{0,1},{1,0},{2,3},{3,2},{4,5},{5,4},{6,7},{7,6},{8,9},{9,8},{10,11... | collective-permute-start | bytes 1769480 | tf_op jit(solution)/shard_map/ppermute | solution.py:36
  121.7 1.6 copy-start
  144.2 23.1 %all-to-all-start.2 = ((bf16[16,256,128]{2,1,0:T(8,128)(2,1)}), bf16[16,256,128]{2,1,0:T(8,128)(2,1)S(1)}, u32[]{:S(2)}, u32[]{:S(2)}) async-start(bf16[16,256,128]{2,1,0:T(8,128)(2,1)} %broadcast_in_dim.15), calls=%async_computation.2 | async-start | bytes 2097152 | tf_op jit(solution)/shard_map/all_to_all | solution.py:17
  167.3 1.0 copy-start.2
  171.0 24.1 %collective-permute-start.23 = (bf16[4,4,128,256]{3,2,1,0:T(8,128)(2,1)}, bf16[4,4,128,256]{3,2,1,0:T(8,128)(2,1)}, u32[]{:S(2)}, u32[]{:S(2)}) collective-permute-start(bf16[4,4,128,256]{3,2,1,0:T(8,128)(2,1)} %pad_maximum_fusion), channel_id=1, source_target_pairs={{0,1},{1,0},{2,3},{3,2},{4,5},{5,4},{6,7},{7,6},{8,9},{9,8},{10,11... | collective-permute-start | bytes 3145736 | tf_op jit(solution)/shard_map/ppermute | solution.py:155
  175.6 22.0 %collective-permute-start.20 = (bf16[2,4,128,128]{3,2,1,0:T(8,128)(2,1)S(1)}, bf16[2,4,128,128]{3,2,1,0:T(8,128)(2,1)}, u32[]{:S(2)}, u32[]{:S(2)}) collective-permute-start(bf16[2,4,128,128]{3,2,1,0:T(8,128)(2,1)S(1)} %bitcast.200), channel_id=1, source_target_pairs={{0,480},{1,481},{32,0},{33,1},{64,32},{65,33},{96,64},{97,65},{128... | collective-permute-start | bytes 786440 | tf_op jit(solution)/shard_map/ppermute | solution.py:28
  179.7 11.4 %collective-permute-start.21 = (bf16[2,4,128,128]{3,2,1,0:T(8,128)(2,1)S(1)}, bf16[2,4,128,128]{3,2,1,0:T(8,128)(2,1)}, u32[]{:S(2)}, u32[]{:S(2)}) collective-permute-start(bf16[2,4,128,128]{3,2,1,0:T(8,128)(2,1)S(1)} %bitcast.201), channel_id=1, source_target_pairs={{0,32},{1,33},{32,64},{33,65},{64,96},{65,97},{96,128},{97,129},{1... | collective-permute-start | bytes 786440 | tf_op jit(solution)/shard_map/ppermute | solution.py:28
  181.6 12.4 %collective-permute-start.22 = (bf16[2,4,128,128]{3,2,1,0:T(8,128)(2,1)S(1)}, bf16[2,4,128,128]{3,2,1,0:T(8,128)(2,1)}, u32[]{:S(2)}, u32[]{:S(2)}) collective-permute-start(bf16[2,4,128,128]{3,2,1,0:T(8,128)(2,1)S(1)} %bitcast.202), channel_id=1, source_target_pairs={{0,448},{1,65},{32,480},{33,97},{64,0},{65,129},{96,32},{97,161},{... | collective-permute-start | bytes 786440 | tf_op jit(solution)/shard_map/ppermute | solution.py:28
  184.2 15.8 %copy-start.8 = (f32[128,128]{1,0:T(8,128)S(1)}, f32[128,128]{1,0:T(8,128)}, u32[]{:S(2)}) copy-start(f32[128,128]{1,0:T(8,128)} %get-tuple-element.49) | copy-start | bytes 196612
  184.2 15.8 %copy-start.9 = (f32[128,128]{1,0:T(8,128)S(1)}, f32[128,128]{1,0:T(8,128)}, u32[]{:S(2)}) copy-start(f32[128,128]{1,0:T(8,128)} %get-tuple-element.50) | copy-start | bytes 196612
  201.5 20.7 %copy-start.1 = (bf16[1280,1152]{1,0:T(8,128)(2,1)S(1)}, bf16[1280,1152]{1,0:T(8,128)(2,1)}, u32[]{:S(2)}) copy-start(bf16[1280,1152]{1,0:T(8,128)(2,1)} %copy-done) | copy-start | bytes 8847364
  224.1 9.8 %collective-permute-start.24 = (bf16[128,1152]{1,0:T(8,128)(2,1)S(1)}, bf16[128,1152]{1,0:T(8,128)(2,1)S(1)}, u32[]{:S(2)}, u32[]{:S(2)}) collective-permute-start(bf16[128,1152]{1,0:T(8,128)(2,1)S(1)} %fusion.2), channel_id=1, source_target_pairs={{0,0},{1,16},{16,1},{17,17},{2,2},{3,18},{18,3},{19,19},{4,4},{5,2... | collective-permute-start | bytes 884744 | tf_op jit(solution)/shard_map/ppermute | solution.py:176
  230.0 7.5 %collective-permute-start.25 = (bf16[128,1152]{1,0:T(8,128)(2,1)S(1)}, bf16[128,1152]{1,0:T(8,128)(2,1)S(1)}, u32[]{:S(2)}, u32[]{:S(2)}) collective-permute-start(bf16[128,1152]{1,0:T(8,128)(2,1)S(1)} %fusion.3), channel_id=1, source_target_pairs={{0,16},{1,0},{16,17},{17,1},{2,18},{3,2},{18,19},{19,3},{4,20},{5,... | collective-permute-start | bytes 884744 | tf_op jit(solution)/shard_map/ppermute | solution.py:174

commit v12 on v4

--- a/solution.py
+++ b/solution.py
@@ -17,10 +17,23 @@
     return lax.all_to_all(copies, PLANE, 0, 0)
 
 
-def along(piece, shift):
+def along(piece, shift, shift_of_core_1=None):
     size = lax.axis_size(LINE)
-    pairs = [(place, (place + shift) % size) for place in range(size)]
-    return lax.ppermute(piece, LINE, pairs)
+    shifts = (shift, shift if shift_of_core_1 is None else shift_of_core_1)
+    pairs = [
+        (2 * place + core, 2 * ((place + shifts[core]) % size) + core)
+        for place in range(size)
+        for core in range(2)
+    ]
+    return lax.ppermute(piece, LINE + ("core",), pairs)
+
+
+def split(value):
+    terms = []
+    for _ in range(3):
+        terms.append(lax.reduce_precision(value, 8, 7))
+        value = value - terms[-1]
+    return jnp.stack(terms)
 
 
 def mix(left, right):
@@ -44,21 +57,34 @@
         (((1,), (2,)), ((), ())),
         preferred_element_type=jnp.float32,
     )
-    partial_gram = partial_gram.transpose(1, 0, 2)
+    partial_gram = partial_gram.transpose(1, 0, 2).astype(jnp.bfloat16)
+    wide = own.astype(jnp.float32)
+    extra = jnp.pad(split((wide * wide).sum(1)), ((0, 13), (0, 0)))
+    extra = jnp.broadcast_to(extra.astype(jnp.bfloat16)[None], (chips, 16, rows))
+    partial_gram = jnp.concatenate([partial_gram, extra], 1)
+    met = lax.axis_index(PLANE) == lax.axis_index(LINE)
+    residue = lax.axis_index("zl")
+    partial_gram, met, residue = lax.optimization_barrier((partial_gram, met, residue))
     summands = lax.all_to_all(partial_gram, PLANE, 0, 0)
-    gram = summands.sum(0) / total_cols
+    summands, own, half, met, residue = lax.optimization_barrier(
+        (summands, own, half, met, residue)
+    )
+    gram = summands.astype(jnp.float32).sum(0) / total_cols
+    diagonal = gram[2 * rows :].sum(0)
+    gram = gram[: 2 * rows]
+    place = lax.broadcasted_iota(jnp.int32, gram.shape, 0)
+    place = place - lax.broadcasted_iota(jnp.int32, gram.shape, 1)
+    gram = jnp.where((place == 0) & met, diagonal[None], gram)
     gram_low = gram.astype(jnp.bfloat16)
     panel = share(gram_low, chips).reshape(groups, steps, 2 * rows, rows)
     here = lax.all_gather(gram_low, "zh", axis=0)
     panel, _ = lax.optimization_barrier((panel, here))
-    cut = groups // 2
     right = (
         here,
         along(here, -1),
         along(here, 1),
-        jnp.concatenate([along(here[:cut], -2), along(here[cut:], 2)], 0),
+        along(here, -2, 2),
     )
-    residue = lax.axis_index("zl")
     left_own = [
         lax.dynamic_index_in_dim(panel, (residue + shift) % steps, 1, False)
         for shift in (0, 1, steps - 1, 2)

time: 226 us -> 216 us (0.956)
  blocking collectives: 63.5 us -> 56.6 us
  starting transfers between devices: 44.2 us -> 40.1 us
    all_to_all x1, blocking collectives: 26.5 us -> 18.8 us  [per_device(): summands = lax.all_to_all(partial_gram, PLANE, 0, 0)]
    ppermute x4 -> x3, starting transfers between devices: 13 us -> 9.53 us  [along(): return lax.ppermute(piece, LINE + ('core',), pairs)]
    ppermute x4 -> x3, waiting for transfers between devices: 7.32 us -> 7.59 us  [along(): return lax.ppermute(piece, LINE + ('core',), pairs)]
  transfers between devices with their start and end apart: 11 -> 10, of which waited for: 7 -> 6; matrix products, arithmetic and copies ran while one was open for 1% -> 2% of each run, Pallas kernels for 0% -> 0%
where the time goes in v12:
time: 216 us; the launch traced here: 215 us
  waiting for transfers between devices  91.3 us (42%)
  blocking collectives  56.6 us (26%)
  starting transfers between devices  40.1 us (19%)
  between operations  13.7 us (6%)
  matrix products  7.44 us (3%)
  other arithmetic  3.52 us (2%)
  local copies, waits for them, and re-layouts  2.32 us (1%)
    all_gather x1, waiting for transfers between devices, per_device(): half = lax.all_gather(own, LINE, axis=0)  72.8 us
    all_to_all x1, blocking collectives, share(): return lax.all_to_all(copies, PLANE, 0, 0)  22.8 us
    all_to_all x1, blocking collectives, per_device(): summands = lax.all_to_all(partial_gram, PLANE, 0, 0)  18.8 us
    all_gather x1, blocking collectives, per_device(): here = lax.all_gather(gram_low, 'zh', axis=0)  15 us
    ppermute x1, starting transfers between devices, per_device(): left_other = lax.ppermute(jnp.stack(left_own), 'core', SWAP)  14.7 us
    ppermute x3, starting transfers between devices, along(): return lax.ppermute(piece, LINE + ('core',), pairs)  9.53 us
    ppermute x3, waiting for transfers between devices, along(): return lax.ppermute(piece, LINE + ('core',), pairs)  7.59 us
    ppermute x1, waiting for transfers between devices, per_device(): stay = lax.ppermute(stay.astype(jnp.bfloat16), ('ylo', 'core'), TURN)  5.05 us
  transfers between devices with their start and end apart: 10, of which 6 were waited for; matrix products, arithmetic and copies ran while one was open for 2% of the time, Pallas kernels for 0%

profile of v12, /device:TPU:1, one launch (start us, length us, event | category | flops | bytes accessed | tf_op | source)
XLA Modules:
  0.0 215.1 jit_solution(3299596472076976126)
XLA Ops:
  6.5 0.0 all-gather.4.cloned.1.call-start
  6.5 1.1 convert_element_type.39
  7.6 4.6 %collective-permute-start = (bf16[128,1152]{1,0:T(8,128)(2,1)S(1)}, bf16[128,1152]{1,0:T(8,128)(2,1)S(1)}, u32[]{:S(2)}, u32[]{:S(2)}) collective-permute-start(bf16[128,1152]{1,0:T(8,128)(2,1)S(1)} %convert_element_type.39), channel_id=1, source_target_pairs={{0,0},{1,16},{16,1},{17,17},{2,2},{3,18},{18,3},{19,19},{4,4},{5,2... | collective-permute-start | bytes 884744 | tf_op jit(solution)/shard_map/ppermute | solution.py:51
  12.2 4.4 %collective-permute-done = bf16[128,1152]{1,0:T(8,128)(2,1)S(1)} collective-permute-done((bf16[128,1152]{1,0:T(8,128)(2,1)S(1)}, bf16[128,1152]{1,0:T(8,128)(2,1)S(1)}, u32[]{:S(2)}, u32[]{:S(2)}) %collective-permute-start) | collective-permute-done | bytes 294944 | tf_op jit(solution)/shard_map/ppermute | solution.py:51
  16.6 0.0 copy-start
  16.6 0.7 copy-done
  17.3 0.0 all-gather.4.cloned.1.call-update
  17.4 1.9 collective-permute-start.1
  19.3 1.1 multiply_reduce_fusion
  20.4 0.6 collective-permute-done.1
  21.1 72.8 %all-gather.4.cloned.1.call-done = bf16[2048,1152]{1,0:T(8,128)(2,1)} async-done(((bf16[128,1152]{1,0:T(8,128)(2,1)}), bf16[2048,1152]{1,0:T(8,128)(2,1)}) %all-gather.4.cloned.1.call-update) | async-done | bytes 4718608 | tf_op jit(solution)/shard_map/all_gather | solution.py:52
  93.8 4.0 %fusion.3 = bf16[16,256,128]{2,1,0:T(8,128)(2,1)S(1)} fusion(bf16[16,128,1152]{2,1,0:T(8,128)(2,1)} %bitcast.96, bf16[128,1152]{1,0:T(8,128)(2,1)S(1)} %collective-permute-done.1, bf16[128,1152]{1,0:T(8,128)(2,1)} %copy-done), kind=kOutput, calls=%fused_computation.7 | convolution fusion | flops 1209663488 | bytes 6356992 | tf_op jit(solution)/shard_map/dot_general | solution.py:54
  97.9 0.1 pad_maximum_fusion
  97.9 18.8 %all_to_all.15 = bf16[16,272,128]{2,1,0:T(8,128)(2,1)S(1)} all-to-all(bf16[16,272,128]{2,1,0:T(8,128)(2,1)S(1)} %pad_maximum_fusion), channel_id=1, replica_groups=mesh['zh'=4,'zl'=4,'ylo'=2,'x'=4,'yhi'=2,'core'=2] {'ylo','x','yhi'}, dimensions={0} | all-to-all | bytes 2228224 | tf_op jit(solution)/shard_map/all_to_all | solution.py:68
  116.7 0.2 convert_reduce_fusion
  116.9 1.2 broadcast_in_dim.18
  118.1 3.7 %all-to-all-start.1 = ((bf16[16,256,128]{2,1,0:T(8,128)(2,1)}), bf16[16,256,128]{2,1,0:T(8,128)(2,1)S(1)}, u32[]{:S(2)}, u32[]{:S(2)}) async-start(bf16[16,256,128]{2,1,0:T(8,128)(2,1)} %broadcast_in_dim.18), calls=%async_computation.1 | async-start | bytes 2097152 | tf_op jit(solution)/shard_map/all_to_all | solution.py:17
  121.8 15.0 %all-gather.1 = bf16[1024,128]{1,0:T(8,128)(2,1)S(1)} all-gather(bf16[256,128]{1,0:T(8,128)(2,1)S(1)} %fusion.47), channel_id=3, replica_groups=mesh['zh'=4,'zl'=4,'ylo'=2,'x'=4,'yhi'=2,'core'=2] {'zh'}, dimensions={0}, use_global_device_ids=true | all-gather | bytes 327680 | tf_op jit(solution)/shard_map/all_gather | solution.py:80
  136.9 0.0 all-to-all-done.1
  136.9 0.1 dynamic-slice_bitcast_fusion.3
  137.0 0.0 slice-start
  137.0 0.1 pad_maximum_fusion.1
  137.2 14.7 %collective-permute-start.5 = (bf16[4,4,256,128]{3,2,1,0:T(8,128)(2,1)S(1)}, bf16[4,4,256,128]{3,2,1,0:T(8,128)(2,1)S(1)}, u32[]{:S(2)}, u32[]{:S(2)}) collective-permute-start(bf16[4,4,256,128]{3,2,1,0:T(8,128)(2,1)S(1)} %pad_maximum_fusion.1), channel_id=1, source_target_pairs={{0,1},{1,0},{2,3},{3,2},{4,5},{5,4},{6,7},{7,6},{8,9},{9,8},{10,11... | collective-permute-start | bytes 3145736 | tf_op jit(solution)/shard_map/ppermute | solution.py:92
  151.9 3.0 %collective-permute-start.4 = (bf16[4,256,128]{2,1,0:T(8,128)(2,1)S(1)}, bf16[4,256,128]{2,1,0:T(8,128)(2,1)S(1)}, u32[]{:S(2)}, u32[]{:S(2)}) collective-permute-start(bf16[4,256,128]{2,1,0:T(8,128)(2,1)S(1)} %bitcast.106), channel_id=1, source_target_pairs={{0,448},{1,65},{32,480},{33,97},{64,0},{65,129},{96,32},{97,161},{... | collective-permute-start | bytes 786440 | tf_op jit(solution)/shard_map/ppermute | solution.py:28
  154.9 4.4 %collective-permute-start.3 = (bf16[4,256,128]{2,1,0:T(8,128)(2,1)S(1)}, bf16[4,256,128]{2,1,0:T(8,128)(2,1)S(1)}, u32[]{:S(2)}, u32[]{:S(2)}) collective-permute-start(bf16[4,256,128]{2,1,0:T(8,128)(2,1)S(1)} %bitcast.107), channel_id=1, source_target_pairs={{0,32},{1,33},{32,64},{33,65},{64,96},{65,97},{96,128},{97,129},{1... | collective-permute-start | bytes 786440 | tf_op jit(solution)/shard_map/ppermute | solution.py:28
  159.3 2.1 collective-permute-start.2
  161.4 0.2 convolution_bitcast_fusion.9
  161.6 0.0 collective-permute-done.4
  161.7 0.2 convolution_bitcast_fusion.6
  161.9 7.6 %collective-permute-done.3 = bf16[4,256,128]{2,1,0:T(8,128)(2,1)S(1)} collective-permute-done((bf16[4,256,128]{2,1,0:T(8,128)(2,1)S(1)}, bf16[4,256,128]{2,1,0:T(8,128)(2,1)S(1)}, u32[]{:S(2)}, u32[]{:S(2)}) %collective-permute-start.3) | collective-permute-done | bytes 262176 | tf_op jit(solution)/shard_map/ppermute | solution.py:28
  169.5 0.2 convolution_bitcast_fusion.7
  169.7 0.0 collective-permute-done.5
  169.7 0.1 fusion.64
  169.8 0.2 convolution_bitcast_fusion.5
  170.0 0.0 slice-start.1
  170.0 0.2 convolution_bitcast_fusion.2
  170.2 0.2 convolution_bitcast_fusion.3
  170.5 0.0 collective-permute-done.2
  170.5 0.2 convolution_bitcast_fusion.4
  170.7 0.2 fusion.13
  170.9 0.2 broadcast_in_dim.33
  171.1 22.8 %all_to_all.16 = bf16[16,256,128]{2,1,0:T(8,128)(2,1)S(1)} all-to-all(bf16[16,256,128]{2,1,0:T(8,128)(2,1)S(1)} %broadcast_in_dim.33), channel_id=1, replica_groups=mesh['zh'=4,'zl'=4,'ylo'=2,'x'=4,'yhi'=2,'core'=2] {'ylo','x','yhi'}, dimensions={0} | all-to-all | bytes 2097152 | tf_op jit(solution)/shard_map/all_to_all | solution.py:17
  193.9 0.0 slice-done
  194.0 0.0 slice-done.1
  194.0 0.0 copy-start.1
  194.0 0.9 fusion.1
  194.8 3.6 %collective-permute-start.7 = (bf16[128,1152]{1,0:T(8,128)(2,1)S(1)}, bf16[128,1152]{1,0:T(8,128)(2,1)S(1)}, u32[]{:S(2)}, u32[]{:S(2)}) collective-permute-start(bf16[128,1152]{1,0:T(8,128)(2,1)S(1)} %fusion.1), channel_id=1, source_target_pairs={{0,16},{1,0},{16,17},{17,1},{2,18},{3,2},{18,19},{19,3},{4,20},{5,... | collective-permute-start | bytes 884744 | tf_op jit(solution)/shard_map/ppermute | solution.py:104
  198.4 0.0 copy-done.1
  198.4 0.9 fusion.2
  199.3 2.1 collective-permute-start.6
  201.4 0.9 collective-permute-done.7
  202.3 5.1 %collective-permute-done.6 = bf16[128,1152]{1,0:T(8,128)(2,1)S(1)} collective-permute-done((bf16[128,1152]{1,0:T(8,128)(2,1)S(1)}, bf16[128,1152]{1,0:T(8,128)(2,1)S(1)}, u32[]{:S(2)}, u32[]{:S(2)}) %collective-permute-start.6) | collective-permute-done | bytes 294944 | tf_op jit(solution)/shard_map/ppermute | solution.py:106
  207.3 0.9 convert_add_fusion
  (7 shorter events, 0.1 us)
Async XLA Ops:
  6.5 87.3 %all-gather.4.cloned.1.call-start = ((), (), s32[]{:S(2)}) async-start(), calls=%async_computation.3 | async-start | bytes 5013504 | tf_op jit(solution)/shard_map/all_gather | solution.py:52
  7.6 9.0 %collective-permute-start = (bf16[128,1152]{1,0:T(8,128)(2,1)S(1)}, bf16[128,1152]{1,0:T(8,128)(2,1)S(1)}, u32[]{:S(2)}, u32[]{:S(2)}) collective-permute-start(bf16[128,1152]{1,0:T(8,128)(2,1)S(1)} %convert_element_type.39), channel_id=1, source_target_pairs={{0,0},{1,16},{16,1},{17,17},{2,2},{3,18},{18,3},{19,19},{4,4},{5,2... | collective-permute-start | bytes 884744 | tf_op jit(solution)/shard_map/ppermute | solution.py:51
  16.6 0.7 copy-start
  17.4 3.7 %collective-permute-start.1 = (bf16[128,1152]{1,0:T(8,128)(2,1)}, bf16[128,1152]{1,0:T(8,128)(2,1)S(1)}, u32[]{:S(2)}, u32[]{:S(2)}) collective-permute-start(bf16[128,1152]{1,0:T(8,128)(2,1)} %copy-done), channel_id=1, source_target_pairs={{0,1},{1,0},{2,3},{3,2},{4,5},{5,4},{6,7},{7,6},{8,9},{9,8},{10,11... | collective-permute-start | bytes 884744 | tf_op jit(solution)/shard_map/ppermute | solution.py:53
  118.1 18.8 %all-to-all-start.1 = ((bf16[16,256,128]{2,1,0:T(8,128)(2,1)}), bf16[16,256,128]{2,1,0:T(8,128)(2,1)S(1)}, u32[]{:S(2)}, u32[]{:S(2)}) async-start(bf16[16,256,128]{2,1,0:T(8,128)(2,1)} %broadcast_in_dim.18), calls=%async_computation.1 | async-start | bytes 2097152 | tf_op jit(solution)/shard_map/all_to_all | solution.py:17
  137.0 57.0 %slice-start = ((s8[4718592]{0:T(1024)(128)(4,1)}), s8[4194304]{0:T(1024)(128)(4,1)S(1)}, s32[]{:S(2)}) async-start(s8[4718592]{0:T(1024)(128)(4,1)} %bitcast.97), calls=%async_computation.4 | async-start | bytes 8388608
  137.2 32.5 %collective-permute-start.5 = (bf16[4,4,256,128]{3,2,1,0:T(8,128)(2,1)S(1)}, bf16[4,4,256,128]{3,2,1,0:T(8,128)(2,1)S(1)}, u32[]{:S(2)}, u32[]{:S(2)}) collective-permute-start(bf16[4,4,256,128]{3,2,1,0:T(8,128)(2,1)S(1)} %pad_maximum_fusion.1), channel_id=1, source_target_pairs={{0,1},{1,0},{2,3},{3,2},{4,5},{5,4},{6,7},{7,6},{8,9},{9,8},{10,11... | collective-permute-start | bytes 3145736 | tf_op jit(solution)/shard_map/ppermute | solution.py:92
  151.9 9.8 %collective-permute-start.4 = (bf16[4,256,128]{2,1,0:T(8,128)(2,1)S(1)}, bf16[4,256,128]{2,1,0:T(8,128)(2,1)S(1)}, u32[]{:S(2)}, u32[]{:S(2)}) collective-permute-start(bf16[4,256,128]{2,1,0:T(8,128)(2,1)S(1)} %bitcast.106), channel_id=1, source_target_pairs={{0,448},{1,65},{32,480},{33,97},{64,0},{65,129},{96,32},{97,161},{... | collective-permute-start | bytes 786440 | tf_op jit(solution)/shard_map/ppermute | solution.py:28
  154.9 14.5 %collective-permute-start.3 = (bf16[4,256,128]{2,1,0:T(8,128)(2,1)S(1)}, bf16[4,256,128]{2,1,0:T(8,128)(2,1)S(1)}, u32[]{:S(2)}, u32[]{:S(2)}) collective-permute-start(bf16[4,256,128]{2,1,0:T(8,128)(2,1)S(1)} %bitcast.107), channel_id=1, source_target_pairs={{0,32},{1,33},{32,64},{33,65},{64,96},{65,97},{96,128},{97,129},{1... | collective-permute-start | bytes 786440 | tf_op jit(solution)/shard_map/ppermute | solution.py:28
  159.3 11.2 %collective-permute-start.2 = (bf16[4,256,128]{2,1,0:T(8,128)(2,1)S(1)}, bf16[4,256,128]{2,1,0:T(8,128)(2,1)S(1)}, u32[]{:S(2)}, u32[]{:S(2)}) collective-permute-start(bf16[4,256,128]{2,1,0:T(8,128)(2,1)S(1)} %bitcast.108), channel_id=1, source_target_pairs={{0,480},{1,481},{32,0},{33,1},{64,32},{65,33},{96,64},{97,65},{128... | collective-permute-start | bytes 786440 | tf_op jit(solution)/shard_map/ppermute | solution.py:28
  170.0 23.9 %slice-start.1 = ((s8[4718592]{0:T(1024)(128)(4,1)}), s8[524288]{0:T(1024)(128)(4,1)S(1)}, s32[]{:S(2)}) async-start(s8[4718592]{0:T(1024)(128)(4,1)} %bitcast.97), calls=%async_computation.5 | async-start | bytes 1048576
  194.0 4.5 %copy-start.1 = (bf16[128,1152]{1,0:T(8,128)(2,1)S(1)}, bf16[128,1152]{1,0:T(8,128)(2,1)}, u32[]{:S(2)}) copy-start(bf16[128,1152]{1,0:T(8,128)(2,1)} %copy-done) | copy-start | bytes 884740
  194.8 7.5 %collective-permute-start.7 = (bf16[128,1152]{1,0:T(8,128)(2,1)S(1)}, bf16[128,1152]{1,0:T(8,128)(2,1)S(1)}, u32[]{:S(2)}, u32[]{:S(2)}) collective-permute-start(bf16[128,1152]{1,0:T(8,128)(2,1)S(1)} %fusion.1), channel_id=1, source_target_pairs={{0,16},{1,0},{16,17},{17,1},{2,18},{3,2},{18,19},{19,3},{4,20},{5,... | collective-permute-start | bytes 884744 | tf_op jit(solution)/shard_map/ppermute | solution.py:104
  199.3 8.0 %collective-permute-start.6 = (bf16[128,1152]{1,0:T(8,128)(2,1)S(1)}, bf16[128,1152]{1,0:T(8,128)(2,1)S(1)}, u32[]{:S(2)}, u32[]{:S(2)}) collective-permute-start(bf16[128,1152]{1,0:T(8,128)(2,1)S(1)} %fusion.2), channel_id=1, source_target_pairs={{0,0},{1,16},{16,1},{17,17},{2,2},{3,18},{18,3},{19,19},{4,4},{5,2... | collective-permute-start | bytes 884744 | tf_op jit(solution)/shard_map/ppermute | solution.py:106
Sparse Core Ops, SparseCore 0:
  17.5 76.2 all-gather.3

commit v13 on v12

--- a/solution.py
+++ b/solution.py
@@ -28,6 +28,18 @@
     return lax.ppermute(piece, LINE + ("core",), pairs)
 
 
+def onward(piece):
+    return along(piece, 1, -1)
+
+
+def swap(pieces):
+    return list(lax.ppermute(jnp.stack(pieces), "core", SWAP))
+
+
+def put(blocks, block, place):
+    return lax.dynamic_update_index_in_dim(blocks, block, place, 0)
+
+
 def split(value):
     terms = []
     for _ in range(3):
@@ -49,8 +61,20 @@
     chips = lax.axis_size(PLANE)
     total_cols = cols * chips
     own = lax.ppermute(rounded, ("ylo", "core"), TURN)
-    half = lax.all_gather(own, LINE, axis=0)
     other = lax.ppermute(own, "core", SWAP)
+    slabs = groups * steps
+    near, far = [own], [other]
+    for step in range(1, slabs // 2):
+        near.append(onward(near[-1]))
+        far.append(onward(far[-1]))
+    near.append(onward(near[-1]))
+    back = [None] + swap(far[1:4]) + swap(far[4:6]) + swap(far[6:])
+    slab, toward = lax.axis_index(LINE), 1 - 2 * lax.axis_index("core")
+    half = jnp.zeros((slabs, rows, cols), jnp.bfloat16)
+    for step in range(slabs // 2 + 1):
+        half = put(half, near[step], (slab - step * toward) % slabs)
+        if 0 < step < slabs // 2:
+            half = put(half, back[step], (slab + step * toward) % slabs)
     partial_gram = lax.dot_general(
         jnp.concatenate([own, other], 0),
         half,

time: 216 us -> 210 us (0.972)
  starting transfers between devices: 40.1 us -> 108 us
  waiting for transfers between devices: 91.3 us -> 25 us
  between operations: 13.7 us -> 1.02 us
  blocking collectives: 56.6 us -> 63.2 us
  matrix products: 7.44 us -> 4.99 us
    all_gather x1 -> x0, waiting for transfers between devices: 72.8 us -> none  [per_device(): half = lax.all_gather(own, LINE, axis=0)]
    ppermute x3 -> x18, starting transfers between devices: 9.53 us -> 72.3 us  [along(): return lax.ppermute(piece, LINE + ('core',), pairs)]
    ppermute x0 -> x3, starting transfers between devices: none -> 10.1 us  [swap(): return list(lax.ppermute(jnp.stack(pieces), 'core', SWAP))]
    ppermute x1, starting transfers between devices: 14.7 us -> 7.69 us  [per_device(): left_other = lax.ppermute(jnp.stack(left_own), 'core', SWAP)]
    ppermute x3 -> x18, waiting for transfers between devices: 7.59 us -> 13.7 us  [along(): return lax.ppermute(piece, LINE + ('core',), pairs)]
    all_to_all x1, blocking collectives: 18.8 us -> 22.8 us  [per_device(): summands = lax.all_to_all(partial_gram, PLANE, 0, 0)]
    all_gather x1, blocking collectives: 15 us -> 18.9 us  [per_device(): here = lax.all_gather(gram_low, 'zh', axis=0)]
    ppermute x1, starting transfers between devices: 2.08 us -> 5.61 us  [per_device(): stay = lax.ppermute(stay.astype(jnp.bfloat16), ('ylo', 'core'), TURN)]
  transfers between devices with their start and end apart: 10 -> 27, of which waited for: 6 -> 13; matrix products, arithmetic and copies ran while one was open for 2% -> 2% of each run, Pallas kernels for 0% -> 0%
where the time goes in v13:
time: 210 us; the launch traced here: 209 us
  starting transfers between devices  108 us (51%)
  blocking collectives  63.2 us (30%)
  waiting for transfers between devices  25 us (12%)
  matrix products  4.99 us (2%)
  local copies, waits for them, and re-layouts  3.37 us (2%)
  other arithmetic  2.81 us (1%)
    ppermute x18, starting transfers between devices, along(): return lax.ppermute(piece, LINE + ('core',), pairs)  72.3 us
    all_to_all x1, blocking collectives, per_device(): summands = lax.all_to_all(partial_gram, PLANE, 0, 0)  22.8 us
    all_to_all x1, blocking collectives, share(): return lax.all_to_all(copies, PLANE, 0, 0)  21.5 us
    all_gather x1, blocking collectives, per_device(): here = lax.all_gather(gram_low, 'zh', axis=0)  18.9 us
    ppermute x18, waiting for transfers between devices, along(): return lax.ppermute(piece, LINE + ('core',), pairs)  13.7 us
    ppermute x3, starting transfers between devices, swap(): return list(lax.ppermute(jnp.stack(pieces), 'core', SWAP))  10.1 us
    ppermute x1, starting transfers between devices, per_device(): left_other = lax.ppermute(jnp.stack(left_own), 'core', SWAP)  7.69 us
    ppermute x1, starting transfers between devices, per_device(): stay = lax.ppermute(stay.astype(jnp.bfloat16), ('ylo', 'core'), TURN)  5.61 us
  transfers between devices with their start and end apart: 27, of which 13 were waited for; matrix products, arithmetic and copies ran while one was open for 2% of the time, Pallas kernels for 0%

profile of v13, /device:TPU:1, one launch (start us, length us, event | category | flops | bytes accessed | tf_op | source)
XLA Modules:
  0.0 208.8 jit_solution(13558408884057725767)
XLA Ops:
  0.0 1.1 convert_element_type.39
  1.1 4.6 %collective-permute-start = (bf16[128,1152]{1,0:T(8,128)(2,1)S(1)}, bf16[128,1152]{1,0:T(8,128)(2,1)S(1)}, u32[]{:S(2)}, u32[]{:S(2)}) collective-permute-start(bf16[128,1152]{1,0:T(8,128)(2,1)S(1)} %convert_element_type.39), channel_id=1, source_target_pairs={{0,0},{1,16},{16,1},{17,17},{2,2},{3,18},{18,3},{19,19},{4,4},{5,2... | collective-permute-start | bytes 884744 | tf_op jit(solution)/shard_map/ppermute | solution.py:63
  5.7 4.4 %collective-permute-done = bf16[128,1152]{1,0:T(8,128)(2,1)S(1)} collective-permute-done((bf16[128,1152]{1,0:T(8,128)(2,1)S(1)}, bf16[128,1152]{1,0:T(8,128)(2,1)S(1)}, u32[]{:S(2)}, u32[]{:S(2)}) %collective-permute-start) | collective-permute-done | bytes 294944 | tf_op jit(solution)/shard_map/ppermute | solution.py:63
  10.1 1.9 collective-permute-start.1
  12.0 11.1 %collective-permute-start.2 = (bf16[128,1152]{1,0:T(8,128)(2,1)S(1)}, bf16[128,1152]{1,0:T(8,128)(2,1)S(1)}, u32[]{:S(2)}, u32[]{:S(2)}) collective-permute-start(bf16[128,1152]{1,0:T(8,128)(2,1)S(1)} %collective-permute-done), channel_id=1, source_target_pairs={{0,32},{1,481},{32,64},{33,1},{64,96},{65,33},{96,128},{97,65},{12... | collective-permute-start | bytes 884744 | tf_op jit(solution)/shard_map/ppermute | solution.py:28
  23.2 2.6 %collective-permute-start.3 = (bf16[128,1152]{1,0:T(8,128)(2,1)S(1)}, bf16[128,1152]{1,0:T(8,128)(2,1)S(1)}, u32[]{:S(2)}, u32[]{:S(2)}) collective-permute-start(bf16[128,1152]{1,0:T(8,128)(2,1)S(1)} %collective-permute-done.1), channel_id=1, source_target_pairs={{0,32},{1,481},{32,64},{33,1},{64,96},{65,33},{96,128},{97,65},{12... | collective-permute-start | bytes 884744 | tf_op jit(solution)/shard_map/ppermute | solution.py:28
  25.8 1.0 collective-permute-done.2
  26.8 5.0 %collective-permute-start.7 = (bf16[128,1152]{1,0:T(8,128)(2,1)S(1)}, bf16[128,1152]{1,0:T(8,128)(2,1)S(1)}, u32[]{:S(2)}, u32[]{:S(2)}) collective-permute-start(bf16[128,1152]{1,0:T(8,128)(2,1)S(1)} %collective-permute-done.2), channel_id=1, source_target_pairs={{0,32},{1,481},{32,64},{33,1},{64,96},{65,33},{96,128},{97,65},{12... | collective-permute-start | bytes 884744 | tf_op jit(solution)/shard_map/ppermute | solution.py:28
  31.8 3.1 %collective-permute-start.4 = (bf16[128,1152]{1,0:T(8,128)(2,1)S(1)}, bf16[128,1152]{1,0:T(8,128)(2,1)S(1)}, u32[]{:S(2)}, u32[]{:S(2)}) collective-permute-start(bf16[128,1152]{1,0:T(8,128)(2,1)S(1)} %collective-permute-done.3), channel_id=1, source_target_pairs={{0,32},{1,481},{32,64},{33,1},{64,96},{65,33},{96,128},{97,65},{12... | collective-permute-start | bytes 884744 | tf_op jit(solution)/shard_map/ppermute | solution.py:28
  35.0 0.5 collective-permute-done.7
  35.5 5.0 %collective-permute-start.8 = (bf16[128,1152]{1,0:T(8,128)(2,1)S(1)}, bf16[128,1152]{1,0:T(8,128)(2,1)S(1)}, u32[]{:S(2)}, u32[]{:S(2)}) collective-permute-start(bf16[128,1152]{1,0:T(8,128)(2,1)S(1)} %collective-permute-done.7), channel_id=1, source_target_pairs={{0,32},{1,481},{32,64},{33,1},{64,96},{65,33},{96,128},{97,65},{12... | collective-permute-start | bytes 884744 | tf_op jit(solution)/shard_map/ppermute | solution.py:28
  40.8 2.8 %collective-permute-start.5 = (bf16[128,1152]{1,0:T(8,128)(2,1)S(1)}, bf16[128,1152]{1,0:T(8,128)(2,1)S(1)}, u32[]{:S(2)}, u32[]{:S(2)}) collective-permute-start(bf16[128,1152]{1,0:T(8,128)(2,1)S(1)} %collective-permute-done.4), channel_id=1, source_target_pairs={{0,32},{1,481},{32,64},{33,1},{64,96},{65,33},{96,128},{97,65},{12... | collective-permute-start | bytes 884744 | tf_op jit(solution)/shard_map/ppermute | solution.py:28
  43.6 0.5 collective-permute-done.8
  44.1 5.0 %collective-permute-start.9 = (bf16[128,1152]{1,0:T(8,128)(2,1)S(1)}, bf16[128,1152]{1,0:T(8,128)(2,1)S(1)}, u32[]{:S(2)}, u32[]{:S(2)}) collective-permute-start(bf16[128,1152]{1,0:T(8,128)(2,1)S(1)} %collective-permute-done.8), channel_id=1, source_target_pairs={{0,32},{1,481},{32,64},{33,1},{64,96},{65,33},{96,128},{97,65},{12... | collective-permute-start | bytes 884744 | tf_op jit(solution)/shard_map/ppermute | solution.py:28
  49.1 0.6 broadcast_in_dim.67
  49.8 2.5 %collective-permute-start.10 = (bf16[128,1152]{1,0:T(8,128)(2,1)S(1)}, bf16[128,1152]{1,0:T(8,128)(2,1)S(1)}, u32[]{:S(2)}, u32[]{:S(2)}) collective-permute-start(bf16[128,1152]{1,0:T(8,128)(2,1)S(1)} %collective-permute-done.5), channel_id=1, source_target_pairs={{0,32},{1,481},{32,64},{33,1},{64,96},{65,33},{96,128},{97,65},{12... | collective-permute-start | bytes 884744 | tf_op jit(solution)/shard_map/ppermute | solution.py:28
  52.3 0.5 collective-permute-done.9
  52.8 5.0 %collective-permute-start.13 = (bf16[128,1152]{1,0:T(8,128)(2,1)S(1)}, bf16[128,1152]{1,0:T(8,128)(2,1)S(1)}, u32[]{:S(2)}, u32[]{:S(2)}) collective-permute-start(bf16[128,1152]{1,0:T(8,128)(2,1)S(1)} %collective-permute-done.9), channel_id=1, source_target_pairs={{0,32},{1,481},{32,64},{33,1},{64,96},{65,33},{96,128},{97,65},{12... | collective-permute-start | bytes 884744 | tf_op jit(solution)/shard_map/ppermute | solution.py:28
  57.8 0.1 multiply_reduce_fusion
  58.0 0.1 pad_maximum_fusion.2
  58.1 4.1 %collective-permute-start.6 = (bf16[3,128,1152]{2,1,0:T(8,128)(2,1)S(1)}, bf16[3,128,1152]{2,1,0:T(8,128)(2,1)S(1)}, u32[]{:S(2)}, u32[]{:S(2)}) collective-permute-start(bf16[3,128,1152]{2,1,0:T(8,128)(2,1)S(1)} %pad_maximum_fusion.2), channel_id=1, source_target_pairs={{0,1},{1,0},{2,3},{3,2},{4,5},{5,4},{6,7},{7,6},{8,9},{9,8},{10,11... | collective-permute-start | bytes 2654216 | tf_op jit(solution)/shard_map/ppermute | solution.py:36
  62.2 4.9 %collective-permute-start.11 = (bf16[128,1152]{1,0:T(8,128)(2,1)S(1)}, bf16[128,1152]{1,0:T(8,128)(2,1)S(1)}, u32[]{:S(2)}, u32[]{:S(2)}) collective-permute-start(bf16[128,1152]{1,0:T(8,128)(2,1)S(1)} %collective-permute-done.10), channel_id=1, source_target_pairs={{0,32},{1,481},{32,64},{33,1},{64,96},{65,33},{96,128},{97,65},{12... | collective-permute-start | bytes 884744 | tf_op jit(solution)/shard_map/ppermute | solution.py:28
  67.0 1.9 collective-permute-start.14
  69.0 1.7 collective-permute-done.11
  70.7 5.0 %collective-permute-start.15 = (bf16[128,1152]{1,0:T(8,128)(2,1)S(1)}, bf16[128,1152]{1,0:T(8,128)(2,1)S(1)}, u32[]{:S(2)}, u32[]{:S(2)}) collective-permute-start(bf16[128,1152]{1,0:T(8,128)(2,1)S(1)} %collective-permute-done.11), channel_id=1, source_target_pairs={{0,32},{1,481},{32,64},{33,1},{64,96},{65,33},{96,128},{97,65},{12... | collective-permute-start | bytes 884744 | tf_op jit(solution)/shard_map/ppermute | solution.py:28
  75.7 3.1 %collective-permute-start.18 = (bf16[128,1152]{1,0:T(8,128)(2,1)S(1)}, bf16[128,1152]{1,0:T(8,128)(2,1)S(1)}, u32[]{:S(2)}, u32[]{:S(2)}) collective-permute-start(bf16[128,1152]{1,0:T(8,128)(2,1)S(1)} %collective-permute-done.14), channel_id=1, source_target_pairs={{0,32},{1,481},{32,64},{33,1},{64,96},{65,33},{96,128},{97,65},{12... | collective-permute-start | bytes 884744 | tf_op jit(solution)/shard_map/ppermute | solution.py:28
  79.0 2.7 %collective-permute-start.12 = (bf16[2,128,1152]{2,1,0:T(8,128)(2,1)S(1)}, bf16[2,128,1152]{2,1,0:T(8,128)(2,1)S(1)}, u32[]{:S(2)}, u32[]{:S(2)}) collective-permute-start(bf16[2,128,1152]{2,1,0:T(8,128)(2,1)S(1)} %pad_maximum_fusion.3), channel_id=1, source_target_pairs={{0,1},{1,0},{2,3},{3,2},{4,5},{5,4},{6,7},{7,6},{8,9},{9,8},{10,11... | collective-permute-start | bytes 1769480 | tf_op jit(solution)/shard_map/ppermute | solution.py:36
  81.6 4.9 %collective-permute-start.16 = (bf16[128,1152]{1,0:T(8,128)(2,1)S(1)}, bf16[128,1152]{1,0:T(8,128)(2,1)S(1)}, u32[]{:S(2)}, u32[]{:S(2)}) collective-permute-start(bf16[128,1152]{1,0:T(8,128)(2,1)S(1)} %collective-permute-done.15), channel_id=1, source_target_pairs={{0,32},{1,481},{32,64},{33,1},{64,96},{65,33},{96,128},{97,65},{12... | collective-permute-start | bytes 884744 | tf_op jit(solution)/shard_map/ppermute | solution.py:28
  86.5 1.9 collective-permute-start.19
  88.7 1.4 collective-permute-done.16
  90.2 3.4 %collective-permute-start.17 = (bf16[2,128,1152]{2,1,0:T(8,128)(2,1)S(1)}, bf16[2,128,1152]{2,1,0:T(8,128)(2,1)S(1)}, u32[]{:S(2)}, u32[]{:S(2)}) collective-permute-start(bf16[2,128,1152]{2,1,0:T(8,128)(2,1)S(1)} %pad_maximum_fusion.4), channel_id=1, source_target_pairs={{0,1},{1,0},{2,3},{3,2},{4,5},{5,4},{6,7},{7,6},{8,9},{9,8},{10,11... | collective-permute-start | bytes 1769480 | tf_op jit(solution)/shard_map/ppermute | solution.py:36
  93.8 1.4 collective-permute-done.17
  95.4 1.6 fusion.3
  97.0 0.6 copy-done
  97.6 22.8 %all_to_all.15 = bf16[16,272,128]{2,1,0:T(8,128)(2,1)S(1)} all-to-all(bf16[16,272,128]{2,1,0:T(8,128)(2,1)S(1)} %pad_maximum_fusion), channel_id=1, replica_groups=mesh['zh'=4,'zl'=4,'ylo'=2,'x'=4,'yhi'=2,'core'=2] {'ylo','x','yhi'}, dimensions={0} | all-to-all | bytes 2228224 | tf_op jit(solution)/shard_map/all_to_all | solution.py:92
  120.5 0.2 convert_reduce_fusion
  120.7 1.2 broadcast_in_dim.79
  121.9 4.2 %all-to-all-start.1 = ((bf16[16,256,128]{2,1,0:T(8,128)(2,1)}), bf16[16,256,128]{2,1,0:T(8,128)(2,1)S(1)}, u32[]{:S(2)}, u32[]{:S(2)}) async-start(bf16[16,256,128]{2,1,0:T(8,128)(2,1)} %broadcast_in_dim.79), calls=%async_computation.1 | async-start | bytes 2097152 | tf_op jit(solution)/shard_map/all_to_all | solution.py:17
  126.2 18.9 %all-gather = bf16[1024,128]{1,0:T(8,128)(2,1)S(1)} all-gather(bf16[256,128]{1,0:T(8,128)(2,1)S(1)} %fusion.47), channel_id=2, replica_groups=mesh['zh'=4,'zl'=4,'ylo'=2,'x'=4,'yhi'=2,'core'=2] {'zh'}, dimensions={0}, use_global_device_ids=true | all-gather | bytes 327680 | tf_op jit(solution)/shard_map/all_gather | solution.py:104
  145.2 0.1 pad_maximum_fusion.1
  145.3 7.7 %collective-permute-start.23 = (bf16[4,4,256,128]{3,2,1,0:T(8,128)(2,1)S(1)}, bf16[4,4,256,128]{3,2,1,0:T(8,128)(2,1)S(1)}, u32[]{:S(2)}, u32[]{:S(2)}) collective-permute-start(bf16[4,4,256,128]{3,2,1,0:T(8,128)(2,1)S(1)} %pad_maximum_fusion.1), channel_id=1, source_target_pairs={{0,1},{1,0},{2,3},{3,2},{4,5},{5,4},{6,7},{7,6},{8,9},{9,8},{10,11... | collective-permute-start | bytes 3145736 | tf_op jit(solution)/shard_map/ppermute | solution.py:116
  153.0 1.9 collective-permute-start.21
  154.9 2.6 %collective-permute-start.22 = (bf16[4,256,128]{2,1,0:T(8,128)(2,1)S(1)}, bf16[4,256,128]{2,1,0:T(8,128)(2,1)S(1)}, u32[]{:S(2)}, u32[]{:S(2)}) collective-permute-start(bf16[4,256,128]{2,1,0:T(8,128)(2,1)S(1)} %bitcast.128), channel_id=1, source_target_pairs={{0,448},{1,65},{32,480},{33,97},{64,0},{65,129},{96,32},{97,161},{... | collective-permute-start | bytes 786440 | tf_op jit(solution)/shard_map/ppermute | solution.py:28
  157.5 3.9 %collective-permute-start.20 = (bf16[4,256,128]{2,1,0:T(8,128)(2,1)S(1)}, bf16[4,256,128]{2,1,0:T(8,128)(2,1)S(1)}, u32[]{:S(2)}, u32[]{:S(2)}) collective-permute-start(bf16[4,256,128]{2,1,0:T(8,128)(2,1)S(1)} %bitcast.129), channel_id=1, source_target_pairs={{0,480},{1,481},{32,0},{33,1},{64,32},{65,33},{96,64},{97,65},{128... | collective-permute-start | bytes 786440 | tf_op jit(solution)/shard_map/ppermute | solution.py:28
  161.4 0.2 convolution_bitcast_fusion.9
  161.7 2.4 %collective-permute-done.21 = bf16[4,256,128]{2,1,0:T(8,128)(2,1)S(1)} collective-permute-done((bf16[4,256,128]{2,1,0:T(8,128)(2,1)S(1)}, bf16[4,256,128]{2,1,0:T(8,128)(2,1)S(1)}, u32[]{:S(2)}, u32[]{:S(2)}) %collective-permute-start.21) | collective-permute-done | bytes 262176 | tf_op jit(solution)/shard_map/ppermute | solution.py:28
  164.0 0.2 convolution_bitcast_fusion.7
  164.3 5.3 %collective-permute-done.22 = bf16[4,256,128]{2,1,0:T(8,128)(2,1)S(1)} collective-permute-done((bf16[4,256,128]{2,1,0:T(8,128)(2,1)S(1)}, bf16[4,256,128]{2,1,0:T(8,128)(2,1)S(1)}, u32[]{:S(2)}, u32[]{:S(2)}) %collective-permute-start.22) | collective-permute-done | bytes 262176 | tf_op jit(solution)/shard_map/ppermute | solution.py:28
  169.6 0.2 convolution_bitcast_fusion.6
  169.9 0.2 convolution_bitcast_fusion.5
  170.2 0.2 convolution_bitcast_fusion.2
  170.4 0.2 convolution_bitcast_fusion.3
  170.6 0.4 collective-permute-done.20
  171.0 0.2 convolution_bitcast_fusion.4
  171.2 0.2 fusion.13
  171.4 0.2 broadcast_in_dim.81
  171.6 21.5 %all_to_all.16 = bf16[16,256,128]{2,1,0:T(8,128)(2,1)S(1)} all-to-all(bf16[16,256,128]{2,1,0:T(8,128)(2,1)S(1)} %broadcast_in_dim.81), channel_id=1, replica_groups=mesh['zh'=4,'zl'=4,'ylo'=2,'x'=4,'yhi'=2,'core'=2] {'ylo','x','yhi'}, dimensions={0} | all-to-all | bytes 2097152 | tf_op jit(solution)/shard_map/all_to_all | solution.py:17
  193.1 0.9 fusion.2
  194.0 5.6 %collective-permute-start.24 = (bf16[128,1152]{1,0:T(8,128)(2,1)S(1)}, bf16[128,1152]{1,0:T(8,128)(2,1)S(1)}, u32[]{:S(2)}, u32[]{:S(2)}) collective-permute-start(bf16[128,1152]{1,0:T(8,128)(2,1)S(1)} %fusion.2), channel_id=1, source_target_pairs={{0,0},{1,16},{16,1},{17,17},{2,2},{3,18},{18,3},{19,19},{4,4},{5,2... | collective-permute-start | bytes 884744 | tf_op jit(solution)/shard_map/ppermute | solution.py:130
  199.6 0.9 fusion.1
  200.5 1.9 collective-permute-start.25
  202.4 1.6 collective-permute-done.24
  204.0 3.9 %collective-permute-done.25 = bf16[128,1152]{1,0:T(8,128)(2,1)S(1)} collective-permute-done((bf16[128,1152]{1,0:T(8,128)(2,1)S(1)}, bf16[128,1152]{1,0:T(8,128)(2,1)S(1)}, u32[]{:S(2)}, u32[]{:S(2)}) %collective-permute-start.25) | collective-permute-done | bytes 294944 | tf_op jit(solution)/shard_map/ppermute | solution.py:128
  207.9 0.9 convert_add_fusion
  (47 shorter events, 1.1 us)
Async XLA Ops:
  1.1 9.0 %collective-permute-start = (bf16[128,1152]{1,0:T(8,128)(2,1)S(1)}, bf16[128,1152]{1,0:T(8,128)(2,1)S(1)}, u32[]{:S(2)}, u32[]{:S(2)}) collective-permute-start(bf16[128,1152]{1,0:T(8,128)(2,1)S(1)} %convert_element_type.39), channel_id=1, source_target_pairs={{0,0},{1,16},{16,1},{17,17},{2,2},{3,18},{18,3},{19,19},{4,4},{5,2... | collective-permute-start | bytes 884744 | tf_op jit(solution)/shard_map/ppermute | solution.py:63
  10.1 13.1 %collective-permute-start.1 = (bf16[128,1152]{1,0:T(8,128)(2,1)S(1)}, bf16[128,1152]{1,0:T(8,128)(2,1)S(1)}, u32[]{:S(2)}, u32[]{:S(2)}) collective-permute-start(bf16[128,1152]{1,0:T(8,128)(2,1)S(1)} %collective-permute-done), channel_id=1, source_target_pairs={{0,1},{1,0},{2,3},{3,2},{4,5},{5,4},{6,7},{7,6},{8,9},{9,8},{10,11... | collective-permute-start | bytes 884744 | tf_op jit(solution)/shard_map/ppermute | solution.py:64
  12.0 14.8 %collective-permute-start.2 = (bf16[128,1152]{1,0:T(8,128)(2,1)S(1)}, bf16[128,1152]{1,0:T(8,128)(2,1)S(1)}, u32[]{:S(2)}, u32[]{:S(2)}) collective-permute-start(bf16[128,1152]{1,0:T(8,128)(2,1)S(1)} %collective-permute-done), channel_id=1, source_target_pairs={{0,32},{1,481},{32,64},{33,1},{64,96},{65,33},{96,128},{97,65},{12... | collective-permute-start | bytes 884744 | tf_op jit(solution)/shard_map/ppermute | solution.py:28
  23.2 8.7 %collective-permute-start.3 = (bf16[128,1152]{1,0:T(8,128)(2,1)S(1)}, bf16[128,1152]{1,0:T(8,128)(2,1)S(1)}, u32[]{:S(2)}, u32[]{:S(2)}) collective-permute-start(bf16[128,1152]{1,0:T(8,128)(2,1)S(1)} %collective-permute-done.1), channel_id=1, source_target_pairs={{0,32},{1,481},{32,64},{33,1},{64,96},{65,33},{96,128},{97,65},{12... | collective-permute-start | bytes 884744 | tf_op jit(solution)/shard_map/ppermute | solution.py:28
  26.8 8.7 %collective-permute-start.7 = (bf16[128,1152]{1,0:T(8,128)(2,1)S(1)}, bf16[128,1152]{1,0:T(8,128)(2,1)S(1)}, u32[]{:S(2)}, u32[]{:S(2)}) collective-permute-start(bf16[128,1152]{1,0:T(8,128)(2,1)S(1)} %collective-permute-done.2), channel_id=1, source_target_pairs={{0,32},{1,481},{32,64},{33,1},{64,96},{65,33},{96,128},{97,65},{12... | collective-permute-start | bytes 884744 | tf_op jit(solution)/shard_map/ppermute | solution.py:28
  31.8 9.0 %collective-permute-start.4 = (bf16[128,1152]{1,0:T(8,128)(2,1)S(1)}, bf16[128,1152]{1,0:T(8,128)(2,1)S(1)}, u32[]{:S(2)}, u32[]{:S(2)}) collective-permute-start(bf16[128,1152]{1,0:T(8,128)(2,1)S(1)} %collective-permute-done.3), channel_id=1, source_target_pairs={{0,32},{1,481},{32,64},{33,1},{64,96},{65,33},{96,128},{97,65},{12... | collective-permute-start | bytes 884744 | tf_op jit(solution)/shard_map/ppermute | solution.py:28
  35.5 8.7 %collective-permute-start.8 = (bf16[128,1152]{1,0:T(8,128)(2,1)S(1)}, bf16[128,1152]{1,0:T(8,128)(2,1)S(1)}, u32[]{:S(2)}, u32[]{:S(2)}) collective-permute-start(bf16[128,1152]{1,0:T(8,128)(2,1)S(1)} %collective-permute-done.7), channel_id=1, source_target_pairs={{0,32},{1,481},{32,64},{33,1},{64,96},{65,33},{96,128},{97,65},{12... | collective-permute-start | bytes 884744 | tf_op jit(solution)/shard_map/ppermute | solution.py:28
  40.8 9.0 %collective-permute-start.5 = (bf16[128,1152]{1,0:T(8,128)(2,1)S(1)}, bf16[128,1152]{1,0:T(8,128)(2,1)S(1)}, u32[]{:S(2)}, u32[]{:S(2)}) collective-permute-start(bf16[128,1152]{1,0:T(8,128)(2,1)S(1)} %collective-permute-done.4), channel_id=1, source_target_pairs={{0,32},{1,481},{32,64},{33,1},{64,96},{65,33},{96,128},{97,65},{12... | collective-permute-start | bytes 884744 | tf_op jit(solution)/shard_map/ppermute | solution.py:28
  44.1 8.7 %collective-permute-start.9 = (bf16[128,1152]{1,0:T(8,128)(2,1)S(1)}, bf16[128,1152]{1,0:T(8,128)(2,1)S(1)}, u32[]{:S(2)}, u32[]{:S(2)}) collective-permute-start(bf16[128,1152]{1,0:T(8,128)(2,1)S(1)} %collective-permute-done.8), channel_id=1, source_target_pairs={{0,32},{1,481},{32,64},{33,1},{64,96},{65,33},{96,128},{97,65},{12... | collective-permute-start | bytes 884744 | tf_op jit(solution)/shard_map/ppermute | solution.py:28
  49.8 12.3 %collective-permute-start.10 = (bf16[128,1152]{1,0:T(8,128)(2,1)S(1)}, bf16[128,1152]{1,0:T(8,128)(2,1)S(1)}, u32[]{:S(2)}, u32[]{:S(2)}) collective-permute-start(bf16[128,1152]{1,0:T(8,128)(2,1)S(1)} %collective-permute-done.5), channel_id=1, source_target_pairs={{0,32},{1,481},{32,64},{33,1},{64,96},{65,33},{96,128},{97,65},{12... | collective-permute-start | bytes 884744 | tf_op jit(solution)/shard_map/ppermute | solution.py:28
  52.8 14.2 %collective-permute-start.13 = (bf16[128,1152]{1,0:T(8,128)(2,1)S(1)}, bf16[128,1152]{1,0:T(8,128)(2,1)S(1)}, u32[]{:S(2)}, u32[]{:S(2)}) collective-permute-start(bf16[128,1152]{1,0:T(8,128)(2,1)S(1)} %collective-permute-done.9), channel_id=1, source_target_pairs={{0,32},{1,481},{32,64},{33,1},{64,96},{65,33},{96,128},{97,65},{12... | collective-permute-start | bytes 884744 | tf_op jit(solution)/shard_map/ppermute | solution.py:28
  58.1 30.4 %collective-permute-start.6 = (bf16[3,128,1152]{2,1,0:T(8,128)(2,1)S(1)}, bf16[3,128,1152]{2,1,0:T(8,128)(2,1)S(1)}, u32[]{:S(2)}, u32[]{:S(2)}) collective-permute-start(bf16[3,128,1152]{2,1,0:T(8,128)(2,1)S(1)} %pad_maximum_fusion.2), channel_id=1, source_target_pairs={{0,1},{1,0},{2,3},{3,2},{4,5},{5,4},{6,7},{7,6},{8,9},{9,8},{10,11... | collective-permute-start | bytes 2654216 | tf_op jit(solution)/shard_map/ppermute | solution.py:36
  62.2 8.5 %collective-permute-start.11 = (bf16[128,1152]{1,0:T(8,128)(2,1)S(1)}, bf16[128,1152]{1,0:T(8,128)(2,1)S(1)}, u32[]{:S(2)}, u32[]{:S(2)}) collective-permute-start(bf16[128,1152]{1,0:T(8,128)(2,1)S(1)} %collective-permute-done.10), channel_id=1, source_target_pairs={{0,32},{1,481},{32,64},{33,1},{64,96},{65,33},{96,128},{97,65},{12... | collective-permute-start | bytes 884744 | tf_op jit(solution)/shard_map/ppermute | solution.py:28
  67.0 8.7 %collective-permute-start.14 = (bf16[128,1152]{1,0:T(8,128)(2,1)S(1)}, bf16[128,1152]{1,0:T(8,128)(2,1)S(1)}, u32[]{:S(2)}, u32[]{:S(2)}) collective-permute-start(bf16[128,1152]{1,0:T(8,128)(2,1)S(1)} %collective-permute-done.13), channel_id=1, source_target_pairs={{0,32},{1,481},{32,64},{33,1},{64,96},{65,33},{96,128},{97,65},{12... | collective-permute-start | bytes 884744 | tf_op jit(solution)/shard_map/ppermute | solution.py:28
  70.7 11.0 %collective-permute-start.15 = (bf16[128,1152]{1,0:T(8,128)(2,1)S(1)}, bf16[128,1152]{1,0:T(8,128)(2,1)S(1)}, u32[]{:S(2)}, u32[]{:S(2)}) collective-permute-start(bf16[128,1152]{1,0:T(8,128)(2,1)S(1)} %collective-permute-done.11), channel_id=1, source_target_pairs={{0,32},{1,481},{32,64},{33,1},{64,96},{65,33},{96,128},{97,65},{12... | collective-permute-start | bytes 884744 | tf_op jit(solution)/shard_map/ppermute | solution.py:28
  75.7 10.8 %collective-permute-start.18 = (bf16[128,1152]{1,0:T(8,128)(2,1)S(1)}, bf16[128,1152]{1,0:T(8,128)(2,1)S(1)}, u32[]{:S(2)}, u32[]{:S(2)}) collective-permute-start(bf16[128,1152]{1,0:T(8,128)(2,1)S(1)} %collective-permute-done.14), channel_id=1, source_target_pairs={{0,32},{1,481},{32,64},{33,1},{64,96},{65,33},{96,128},{97,65},{12... | collective-permute-start | bytes 884744 | tf_op jit(solution)/shard_map/ppermute | solution.py:28
  79.0 14.7 %collective-permute-start.12 = (bf16[2,128,1152]{2,1,0:T(8,128)(2,1)S(1)}, bf16[2,128,1152]{2,1,0:T(8,128)(2,1)S(1)}, u32[]{:S(2)}, u32[]{:S(2)}) collective-permute-start(bf16[2,128,1152]{2,1,0:T(8,128)(2,1)S(1)} %pad_maximum_fusion.3), channel_id=1, source_target_pairs={{0,1},{1,0},{2,3},{3,2},{4,5},{5,4},{6,7},{7,6},{8,9},{9,8},{10,11... | collective-permute-start | bytes 1769480 | tf_op jit(solution)/shard_map/ppermute | solution.py:36
  81.6 8.5 %collective-permute-start.16 = (bf16[128,1152]{1,0:T(8,128)(2,1)S(1)}, bf16[128,1152]{1,0:T(8,128)(2,1)S(1)}, u32[]{:S(2)}, u32[]{:S(2)}) collective-permute-start(bf16[128,1152]{1,0:T(8,128)(2,1)S(1)} %collective-permute-done.15), channel_id=1, source_target_pairs={{0,32},{1,481},{32,64},{33,1},{64,96},{65,33},{96,128},{97,65},{12... | collective-permute-start | bytes 884744 | tf_op jit(solution)/shard_map/ppermute | solution.py:28
  86.5 8.8 %collective-permute-start.19 = (bf16[128,1152]{1,0:T(8,128)(2,1)S(1)}, bf16[128,1152]{1,0:T(8,128)(2,1)S(1)}, u32[]{:S(2)}, u32[]{:S(2)}) collective-permute-start(bf16[128,1152]{1,0:T(8,128)(2,1)S(1)} %collective-permute-done.18), channel_id=1, source_target_pairs={{0,32},{1,481},{32,64},{33,1},{64,96},{65,33},{96,128},{97,65},{12... | collective-permute-start | bytes 884744 | tf_op jit(solution)/shard_map/ppermute | solution.py:28
  90.2 5.0 %collective-permute-start.17 = (bf16[2,128,1152]{2,1,0:T(8,128)(2,1)S(1)}, bf16[2,128,1152]{2,1,0:T(8,128)(2,1)S(1)}, u32[]{:S(2)}, u32[]{:S(2)}) collective-permute-start(bf16[2,128,1152]{2,1,0:T(8,128)(2,1)S(1)} %pad_maximum_fusion.4), channel_id=1, source_target_pairs={{0,1},{1,0},{2,3},{3,2},{4,5},{5,4},{6,7},{7,6},{8,9},{9,8},{10,11... | collective-permute-start | bytes 1769480 | tf_op jit(solution)/shard_map/ppermute | solution.py:36
  95.4 2.1 %copy-start = (bf16[16,128,1152]{2,1,0:T(8,128)(2,1)}, bf16[16,128,1152]{2,1,0:T(8,128)(2,1)S(1)}, u32[]{:S(2)}) copy-start(bf16[16,128,1152]{2,1,0:T(8,128)(2,1)S(1)} %bitcast_dynamic-update-slice_fusion) | copy-start | bytes 14155780
  121.9 23.2 %all-to-all-start.1 = ((bf16[16,256,128]{2,1,0:T(8,128)(2,1)}), bf16[16,256,128]{2,1,0:T(8,128)(2,1)S(1)}, u32[]{:S(2)}, u32[]{:S(2)}) async-start(bf16[16,256,128]{2,1,0:T(8,128)(2,1)} %broadcast_in_dim.79), calls=%async_computation.1 | async-start | bytes 2097152 | tf_op jit(solution)/shard_map/all_to_all | solution.py:17
  145.2 48.0 %slice-start = ((s8[4718592]{0:T(1024)(128)(4,1)}), s8[4194304]{0:T(1024)(128)(4,1)S(1)}, s32[]{:S(2)}) async-start(s8[4718592]{0:T(1024)(128)(4,1)} %bitcast.120), calls=%async_computation.3 | async-start | bytes 8388608
  145.3 24.5 %collective-permute-start.23 = (bf16[4,4,256,128]{3,2,1,0:T(8,128)(2,1)S(1)}, bf16[4,4,256,128]{3,2,1,0:T(8,128)(2,1)S(1)}, u32[]{:S(2)}, u32[]{:S(2)}) collective-permute-start(bf16[4,4,256,128]{3,2,1,0:T(8,128)(2,1)S(1)} %pad_maximum_fusion.1), channel_id=1, source_target_pairs={{0,1},{1,0},{2,3},{3,2},{4,5},{5,4},{6,7},{7,6},{8,9},{9,8},{10,11... | collective-permute-start | bytes 3145736 | tf_op jit(solution)/shard_map/ppermute | solution.py:116
  153.0 11.0 %collective-permute-start.21 = (bf16[4,256,128]{2,1,0:T(8,128)(2,1)S(1)}, bf16[4,256,128]{2,1,0:T(8,128)(2,1)S(1)}, u32[]{:S(2)}, u32[]{:S(2)}) collective-permute-start(bf16[4,256,128]{2,1,0:T(8,128)(2,1)S(1)} %bitcast.127), channel_id=1, source_target_pairs={{0,32},{1,33},{32,64},{33,65},{64,96},{65,97},{96,128},{97,129},{1... | collective-permute-start | bytes 786440 | tf_op jit(solution)/shard_map/ppermute | solution.py:28
  154.9 14.7 %collective-permute-start.22 = (bf16[4,256,128]{2,1,0:T(8,128)(2,1)S(1)}, bf16[4,256,128]{2,1,0:T(8,128)(2,1)S(1)}, u32[]{:S(2)}, u32[]{:S(2)}) collective-permute-start(bf16[4,256,128]{2,1,0:T(8,128)(2,1)S(1)} %bitcast.128), channel_id=1, source_target_pairs={{0,448},{1,65},{32,480},{33,97},{64,0},{65,129},{96,32},{97,161},{... | collective-permute-start | bytes 786440 | tf_op jit(solution)/shard_map/ppermute | solution.py:28
  157.5 13.5 %collective-permute-start.20 = (bf16[4,256,128]{2,1,0:T(8,128)(2,1)S(1)}, bf16[4,256,128]{2,1,0:T(8,128)(2,1)S(1)}, u32[]{:S(2)}, u32[]{:S(2)}) collective-permute-start(bf16[4,256,128]{2,1,0:T(8,128)(2,1)S(1)} %bitcast.129), channel_id=1, source_target_pairs={{0,480},{1,481},{32,0},{33,1},{64,32},{65,33},{96,64},{97,65},{128... | collective-permute-start | bytes 786440 | tf_op jit(solution)/shard_map/ppermute | solution.py:28
  170.2 23.0 %slice-start.1 = ((s8[4718592]{0:T(1024)(128)(4,1)}), s8[524288]{0:T(1024)(128)(4,1)S(1)}, s32[]{:S(2)}) async-start(s8[4718592]{0:T(1024)(128)(4,1)} %bitcast.120), calls=%async_computation.4 | async-start | bytes 1048576
  194.0 10.0 %collective-permute-start.24 = (bf16[128,1152]{1,0:T(8,128)(2,1)S(1)}, bf16[128,1152]{1,0:T(8,128)(2,1)S(1)}, u32[]{:S(2)}, u32[]{:S(2)}) collective-permute-start(bf16[128,1152]{1,0:T(8,128)(2,1)S(1)} %fusion.2), channel_id=1, source_target_pairs={{0,0},{1,16},{16,1},{17,17},{2,2},{3,18},{18,3},{19,19},{4,4},{5,2... | collective-permute-start | bytes 884744 | tf_op jit(solution)/shard_map/ppermute | solution.py:130
  200.5 7.5 %collective-permute-start.25 = (bf16[128,1152]{1,0:T(8,128)(2,1)S(1)}, bf16[128,1152]{1,0:T(8,128)(2,1)S(1)}, u32[]{:S(2)}, u32[]{:S(2)}) collective-permute-start(bf16[128,1152]{1,0:T(8,128)(2,1)S(1)} %fusion.1), channel_id=1, source_target_pairs={{0,16},{1,0},{16,17},{17,1},{2,18},{3,2},{18,19},{19,3},{4,20},{5,... | collective-permute-start | bytes 884744 | tf_op jit(solution)/shard_map/ppermute | solution.py:128

commit v14 on v13

--- a/solution.py
+++ b/solution.py
@@ -32,6 +32,20 @@
     return along(piece, 1, -1)
 
 
+def launch(piece, side):
+    size = lax.axis_size(LINE)
+    pairs = []
+    for place in range(size):
+        for ylo in range(2):
+            for core in range(2):
+                to = ylo ^ side
+                ahead = (place + 1 - 2 * to) % size
+                pairs.append(
+                    (4 * place + 2 * ylo + core, 4 * ahead + 2 * core + to)
+                )
+    return lax.ppermute(piece, LINE + ("ylo", "core"), pairs)
+
+
 def swap(pieces):
     return list(lax.ppermute(jnp.stack(pieces), "core", SWAP))
 
@@ -63,8 +77,8 @@
     own = lax.ppermute(rounded, ("ylo", "core"), TURN)
     other = lax.ppermute(own, "core", SWAP)
     slabs = groups * steps
-    near, far = [own], [other]
-    for step in range(1, slabs // 2):
+    near, far = [own, launch(rounded, 0)], [None, launch(rounded, 1)]
+    for step in range(2, slabs // 2):
         near.append(onward(near[-1]))
         far.append(onward(far[-1]))
     near.append(onward(near[-1]))

time: 210 us -> 218 us (1.038)
  waiting for transfers between devices: 25 us -> 32.3 us
    ppermute x18 -> x16, starting transfers between devices: 72.3 us -> 52.8 us  [along(): return lax.ppermute(piece, LINE + ('core',), pairs)]
    ppermute x0 -> x2, starting transfers between devices: none -> 14.9 us  [launch(): return lax.ppermute(piece, LINE + ('ylo', 'core'), pairs)]
    ppermute x18 -> x16, waiting for transfers between devices: 13.7 us -> 26.4 us  [along(): return lax.ppermute(piece, LINE + ('core',), pairs)]
    ppermute x3, starting transfers between devices: 10.1 us -> 18.6 us  [swap(): return list(lax.ppermute(jnp.stack(pieces), 'core', SWAP))]
    ppermute x1, waiting for transfers between devices: 4.39 us -> 0.01 us  [per_device(): own = lax.ppermute(rounded, ('ylo', 'core'), TURN)]
  transfers between devices with their start and end apart: 27 -> 27, of which waited for: 13 -> 10; matrix products, arithmetic and copies ran while one was open for 2% -> 2% of each run, Pallas kernels for 0% -> 0%
where the time goes in v14:
time: 218 us; the launch traced here: 217 us
  starting transfers between devices  110 us (50%)
  blocking collectives  62.4 us (29%)
  waiting for transfers between devices  32.3 us (15%)
  matrix products  5.01 us (2%)
  local copies, waits for them, and re-layouts  3.33 us (2%)
  other arithmetic  2.81 us (1%)
    ppermute x16, starting transfers between devices, along(): return lax.ppermute(piece, LINE + ('core',), pairs)  52.8 us
    ppermute x16, waiting for transfers between devices, along(): return lax.ppermute(piece, LINE + ('core',), pairs)  26.4 us
    all_to_all x1, blocking collectives, share(): return lax.all_to_all(copies, PLANE, 0, 0)  22 us
    all_to_all x1, blocking collectives, per_device(): summands = lax.all_to_all(partial_gram, PLANE, 0, 0)  21 us
    all_gather x1, blocking collectives, per_device(): here = lax.all_gather(gram_low, 'zh', axis=0)  19.4 us
    ppermute x3, starting transfers between devices, swap(): return list(lax.ppermute(jnp.stack(pieces), 'core', SWAP))  18.6 us
    ppermute x2, starting transfers between devices, launch(): return lax.ppermute(piece, LINE + ('ylo', 'core'), pairs)  14.9 us
    ppermute x1, starting transfers between devices, per_device(): left_other = lax.ppermute(jnp.stack(left_own), 'core', SWAP)  7.81 us
  transfers between devices with their start and end apart: 27, of which 10 were waited for; matrix products, arithmetic and copies ran while one was open for 2% of the time, Pallas kernels for 0%

profile of v14, /device:TPU:1, one launch (start us, length us, event | category | flops | bytes accessed | tf_op | source)
XLA Modules:
  0.0 217.0 jit_solution(10951849067446678249)
XLA Ops:
  0.0 1.1 convert_element_type.39
  1.1 13.0 %collective-permute-start.3 = (bf16[128,1152]{1,0:T(8,128)(2,1)S(1)}, bf16[128,1152]{1,0:T(8,128)(2,1)S(1)}, u32[]{:S(2)}, u32[]{:S(2)}) collective-permute-start(bf16[128,1152]{1,0:T(8,128)(2,1)S(1)} %convert_element_type.39), channel_id=1, source_target_pairs={{0,481},{1,497},{16,32},{17,48},{32,1},{33,17},{48,64},{49,80},{64... | collective-permute-start | bytes 884744 | tf_op jit(solution)/shard_map/ppermute | solution.py:46
  14.1 1.9 collective-permute-start.2
  16.0 4.1 %collective-permute-start = (bf16[128,1152]{1,0:T(8,128)(2,1)S(1)}, bf16[128,1152]{1,0:T(8,128)(2,1)S(1)}, u32[]{:S(2)}, u32[]{:S(2)}) collective-permute-start(bf16[128,1152]{1,0:T(8,128)(2,1)S(1)} %convert_element_type.39), channel_id=1, source_target_pairs={{0,0},{1,16},{16,1},{17,17},{2,2},{3,18},{18,3},{19,19},{4,4},{5,2... | collective-permute-start | bytes 884744 | tf_op jit(solution)/shard_map/ppermute | solution.py:77
  20.1 0.3 collective-permute-done.3
  20.4 4.8 %collective-permute-start.4 = (bf16[128,1152]{1,0:T(8,128)(2,1)S(1)}, bf16[128,1152]{1,0:T(8,128)(2,1)S(1)}, u32[]{:S(2)}, u32[]{:S(2)}) collective-permute-start(bf16[128,1152]{1,0:T(8,128)(2,1)S(1)} %collective-permute-done.3), channel_id=1, source_target_pairs={{0,32},{1,481},{32,64},{33,1},{64,96},{65,33},{96,128},{97,65},{12... | collective-permute-start | bytes 884744 | tf_op jit(solution)/shard_map/ppermute | solution.py:28
  25.3 2.7 %collective-permute-start.7 = (bf16[128,1152]{1,0:T(8,128)(2,1)S(1)}, bf16[128,1152]{1,0:T(8,128)(2,1)S(1)}, u32[]{:S(2)}, u32[]{:S(2)}) collective-permute-start(bf16[128,1152]{1,0:T(8,128)(2,1)S(1)} %collective-permute-done.2), channel_id=1, source_target_pairs={{0,32},{1,481},{32,64},{33,1},{64,96},{65,33},{96,128},{97,65},{12... | collective-permute-start | bytes 884744 | tf_op jit(solution)/shard_map/ppermute | solution.py:28
  28.3 1.9 collective-permute-start.1
  30.3 3.8 %collective-permute-start.5 = (bf16[128,1152]{1,0:T(8,128)(2,1)S(1)}, bf16[128,1152]{1,0:T(8,128)(2,1)S(1)}, u32[]{:S(2)}, u32[]{:S(2)}) collective-permute-start(bf16[128,1152]{1,0:T(8,128)(2,1)S(1)} %collective-permute-done.4), channel_id=1, source_target_pairs={{0,32},{1,481},{32,64},{33,1},{64,96},{65,33},{96,128},{97,65},{12... | collective-permute-start | bytes 884744 | tf_op jit(solution)/shard_map/ppermute | solution.py:28
  34.1 3.6 %collective-permute-start.8 = (bf16[128,1152]{1,0:T(8,128)(2,1)S(1)}, bf16[128,1152]{1,0:T(8,128)(2,1)S(1)}, u32[]{:S(2)}, u32[]{:S(2)}) collective-permute-start(bf16[128,1152]{1,0:T(8,128)(2,1)S(1)} %collective-permute-done.7), channel_id=1, source_target_pairs={{0,32},{1,481},{32,64},{33,1},{64,96},{65,33},{96,128},{97,65},{12... | collective-permute-start | bytes 884744 | tf_op jit(solution)/shard_map/ppermute | solution.py:28
  37.8 0.6 broadcast_in_dim.67
  38.4 3.4 %collective-permute-done.8 = bf16[128,1152]{1,0:T(8,128)(2,1)S(1)} collective-permute-done((bf16[128,1152]{1,0:T(8,128)(2,1)S(1)}, bf16[128,1152]{1,0:T(8,128)(2,1)S(1)}, u32[]{:S(2)}, u32[]{:S(2)}) %collective-permute-start.8) | collective-permute-done | bytes 294944 | tf_op jit(solution)/shard_map/ppermute | solution.py:28
  41.9 4.5 %collective-permute-start.9 = (bf16[128,1152]{1,0:T(8,128)(2,1)S(1)}, bf16[128,1152]{1,0:T(8,128)(2,1)S(1)}, u32[]{:S(2)}, u32[]{:S(2)}) collective-permute-start(bf16[128,1152]{1,0:T(8,128)(2,1)S(1)} %collective-permute-done.8), channel_id=1, source_target_pairs={{0,32},{1,481},{32,64},{33,1},{64,96},{65,33},{96,128},{97,65},{12... | collective-permute-start | bytes 884744 | tf_op jit(solution)/shard_map/ppermute | solution.py:28
  46.4 2.2 %collective-permute-start.10 = (bf16[128,1152]{1,0:T(8,128)(2,1)S(1)}, bf16[128,1152]{1,0:T(8,128)(2,1)S(1)}, u32[]{:S(2)}, u32[]{:S(2)}) collective-permute-start(bf16[128,1152]{1,0:T(8,128)(2,1)S(1)} %collective-permute-done.5), channel_id=1, source_target_pairs={{0,32},{1,481},{32,64},{33,1},{64,96},{65,33},{96,128},{97,65},{12... | collective-permute-start | bytes 884744 | tf_op jit(solution)/shard_map/ppermute | solution.py:28
  48.7 0.1 multiply_reduce_fusion
  48.8 0.1 pad_maximum_fusion.2
  48.9 3.0 %collective-permute-start.6 = (bf16[3,128,1152]{2,1,0:T(8,128)(2,1)S(1)}, bf16[3,128,1152]{2,1,0:T(8,128)(2,1)S(1)}, u32[]{:S(2)}, u32[]{:S(2)}) collective-permute-start(bf16[3,128,1152]{2,1,0:T(8,128)(2,1)S(1)} %pad_maximum_fusion.2), channel_id=1, source_target_pairs={{0,1},{1,0},{2,3},{3,2},{4,5},{5,4},{6,7},{7,6},{8,9},{9,8},{10,11... | collective-permute-start | bytes 2654216 | tf_op jit(solution)/shard_map/ppermute | solution.py:50
  51.9 2.3 %collective-permute-done.10 = bf16[128,1152]{1,0:T(8,128)(2,1)S(1)} collective-permute-done((bf16[128,1152]{1,0:T(8,128)(2,1)S(1)}, bf16[128,1152]{1,0:T(8,128)(2,1)S(1)}, u32[]{:S(2)}, u32[]{:S(2)}) %collective-permute-start.10) | collective-permute-done | bytes 294944 | tf_op jit(solution)/shard_map/ppermute | solution.py:28
  54.2 4.0 %collective-permute-start.11 = (bf16[128,1152]{1,0:T(8,128)(2,1)S(1)}, bf16[128,1152]{1,0:T(8,128)(2,1)S(1)}, u32[]{:S(2)}, u32[]{:S(2)}) collective-permute-start(bf16[128,1152]{1,0:T(8,128)(2,1)S(1)} %collective-permute-done.10), channel_id=1, source_target_pairs={{0,32},{1,481},{32,64},{33,1},{64,96},{65,33},{96,128},{97,65},{12... | collective-permute-start | bytes 884744 | tf_op jit(solution)/shard_map/ppermute | solution.py:28
  58.3 2.2 %collective-permute-start.13 = (bf16[128,1152]{1,0:T(8,128)(2,1)S(1)}, bf16[128,1152]{1,0:T(8,128)(2,1)S(1)}, u32[]{:S(2)}, u32[]{:S(2)}) collective-permute-start(bf16[128,1152]{1,0:T(8,128)(2,1)S(1)} %collective-permute-done.9), channel_id=1, source_target_pairs={{0,32},{1,481},{32,64},{33,1},{64,96},{65,33},{96,128},{97,65},{12... | collective-permute-start | bytes 884744 | tf_op jit(solution)/shard_map/ppermute | solution.py:28
  60.5 5.5 %collective-permute-done.13 = bf16[128,1152]{1,0:T(8,128)(2,1)S(1)} collective-permute-done((bf16[128,1152]{1,0:T(8,128)(2,1)S(1)}, bf16[128,1152]{1,0:T(8,128)(2,1)S(1)}, u32[]{:S(2)}, u32[]{:S(2)}) %collective-permute-start.13) | collective-permute-done | bytes 294944 | tf_op jit(solution)/shard_map/ppermute | solution.py:28
  66.0 4.0 %collective-permute-start.14 = (bf16[128,1152]{1,0:T(8,128)(2,1)S(1)}, bf16[128,1152]{1,0:T(8,128)(2,1)S(1)}, u32[]{:S(2)}, u32[]{:S(2)}) collective-permute-start(bf16[128,1152]{1,0:T(8,128)(2,1)S(1)} %collective-permute-done.13), channel_id=1, source_target_pairs={{0,32},{1,481},{32,64},{33,1},{64,96},{65,33},{96,128},{97,65},{12... | collective-permute-start | bytes 884744 | tf_op jit(solution)/shard_map/ppermute | solution.py:28
  70.1 1.9 collective-permute-start.15
  72.1 5.6 %collective-permute-start.12 = (bf16[2,128,1152]{2,1,0:T(8,128)(2,1)S(1)}, bf16[2,128,1152]{2,1,0:T(8,128)(2,1)S(1)}, u32[]{:S(2)}, u32[]{:S(2)}) collective-permute-start(bf16[2,128,1152]{2,1,0:T(8,128)(2,1)S(1)} %pad_maximum_fusion.3), channel_id=1, source_target_pairs={{0,1},{1,0},{2,3},{3,2},{4,5},{5,4},{6,7},{7,6},{8,9},{9,8},{10,11... | collective-permute-start | bytes 1769480 | tf_op jit(solution)/shard_map/ppermute | solution.py:50
  77.7 4.9 %collective-permute-start.16 = (bf16[128,1152]{1,0:T(8,128)(2,1)S(1)}, bf16[128,1152]{1,0:T(8,128)(2,1)S(1)}, u32[]{:S(2)}, u32[]{:S(2)}) collective-permute-start(bf16[128,1152]{1,0:T(8,128)(2,1)S(1)} %collective-permute-done.15), channel_id=1, source_target_pairs={{0,32},{1,481},{32,64},{33,1},{64,96},{65,33},{96,128},{97,65},{12... | collective-permute-start | bytes 884744 | tf_op jit(solution)/shard_map/ppermute | solution.py:28
  82.6 3.6 %collective-permute-start.18 = (bf16[128,1152]{1,0:T(8,128)(2,1)S(1)}, bf16[128,1152]{1,0:T(8,128)(2,1)S(1)}, u32[]{:S(2)}, u32[]{:S(2)}) collective-permute-start(bf16[128,1152]{1,0:T(8,128)(2,1)S(1)} %collective-permute-done.14), channel_id=1, source_target_pairs={{0,32},{1,481},{32,64},{33,1},{64,96},{65,33},{96,128},{97,65},{12... | collective-permute-start | bytes 884744 | tf_op jit(solution)/shard_map/ppermute | solution.py:28
  86.6 10.0 %collective-permute-start.17 = (bf16[2,128,1152]{2,1,0:T(8,128)(2,1)S(1)}, bf16[2,128,1152]{2,1,0:T(8,128)(2,1)S(1)}, u32[]{:S(2)}, u32[]{:S(2)}) collective-permute-start(bf16[2,128,1152]{2,1,0:T(8,128)(2,1)S(1)} %pad_maximum_fusion.4), channel_id=1, source_target_pairs={{0,1},{1,0},{2,3},{3,2},{4,5},{5,4},{6,7},{7,6},{8,9},{9,8},{10,11... | collective-permute-start | bytes 1769480 | tf_op jit(solution)/shard_map/ppermute | solution.py:50
  96.6 1.9 collective-permute-start.19
  98.9 5.5 %collective-permute-done.19 = bf16[128,1152]{1,0:T(8,128)(2,1)S(1)} collective-permute-done((bf16[128,1152]{1,0:T(8,128)(2,1)S(1)}, bf16[128,1152]{1,0:T(8,128)(2,1)S(1)}, u32[]{:S(2)}, u32[]{:S(2)}) %collective-permute-start.19) | collective-permute-done | bytes 294944 | tf_op jit(solution)/shard_map/ppermute | solution.py:28
  104.4 1.6 fusion.3
  106.0 0.5 copy-done
  106.6 0.1 pad_maximum_fusion
  106.6 21.0 %all_to_all.15 = bf16[16,272,128]{2,1,0:T(8,128)(2,1)S(1)} all-to-all(bf16[16,272,128]{2,1,0:T(8,128)(2,1)S(1)} %pad_maximum_fusion), channel_id=1, replica_groups=mesh['zh'=4,'zl'=4,'ylo'=2,'x'=4,'yhi'=2,'core'=2] {'ylo','x','yhi'}, dimensions={0} | all-to-all | bytes 2228224 | tf_op jit(solution)/shard_map/all_to_all | solution.py:106
  127.6 0.2 convert_reduce_fusion
  127.8 1.2 broadcast_in_dim.79
  129.0 3.7 %all-to-all-start.1 = ((bf16[16,256,128]{2,1,0:T(8,128)(2,1)}), bf16[16,256,128]{2,1,0:T(8,128)(2,1)S(1)}, u32[]{:S(2)}, u32[]{:S(2)}) async-start(bf16[16,256,128]{2,1,0:T(8,128)(2,1)} %broadcast_in_dim.79), calls=%async_computation.1 | async-start | bytes 2097152 | tf_op jit(solution)/shard_map/all_to_all | solution.py:17
  132.8 19.4 %all-gather = bf16[1024,128]{1,0:T(8,128)(2,1)S(1)} all-gather(bf16[256,128]{1,0:T(8,128)(2,1)S(1)} %fusion.47), channel_id=2, replica_groups=mesh['zh'=4,'zl'=4,'ylo'=2,'x'=4,'yhi'=2,'core'=2] {'zh'}, dimensions={0}, use_global_device_ids=true | all-gather | bytes 327680 | tf_op jit(solution)/shard_map/all_gather | solution.py:118
  152.2 0.1 dynamic-slice_bitcast_fusion.3
  152.3 0.1 pad_maximum_fusion.1
  152.4 7.8 %collective-permute-start.23 = (bf16[4,4,256,128]{3,2,1,0:T(8,128)(2,1)S(1)}, bf16[4,4,256,128]{3,2,1,0:T(8,128)(2,1)S(1)}, u32[]{:S(2)}, u32[]{:S(2)}) collective-permute-start(bf16[4,4,256,128]{3,2,1,0:T(8,128)(2,1)S(1)} %pad_maximum_fusion.1), channel_id=1, source_target_pairs={{0,1},{1,0},{2,3},{3,2},{4,5},{5,4},{6,7},{7,6},{8,9},{9,8},{10,11... | collective-permute-start | bytes 3145736 | tf_op jit(solution)/shard_map/ppermute | solution.py:130
  160.2 2.1 collective-permute-start.21
  162.4 4.4 %collective-permute-start.22 = (bf16[4,256,128]{2,1,0:T(8,128)(2,1)S(1)}, bf16[4,256,128]{2,1,0:T(8,128)(2,1)S(1)}, u32[]{:S(2)}, u32[]{:S(2)}) collective-permute-start(bf16[4,256,128]{2,1,0:T(8,128)(2,1)S(1)} %bitcast.128), channel_id=1, source_target_pairs={{0,448},{1,65},{32,480},{33,97},{64,0},{65,129},{96,32},{97,161},{... | collective-permute-start | bytes 786440 | tf_op jit(solution)/shard_map/ppermute | solution.py:28
  166.8 1.9 collective-permute-start.20
  168.7 0.2 convolution_bitcast_fusion.9
  168.9 2.3 %collective-permute-done.21 = bf16[4,256,128]{2,1,0:T(8,128)(2,1)S(1)} collective-permute-done((bf16[4,256,128]{2,1,0:T(8,128)(2,1)S(1)}, bf16[4,256,128]{2,1,0:T(8,128)(2,1)S(1)}, u32[]{:S(2)}, u32[]{:S(2)}) %collective-permute-start.21) | collective-permute-done | bytes 262176 | tf_op jit(solution)/shard_map/ppermute | solution.py:28
  171.3 0.2 convolution_bitcast_fusion.7
  171.5 5.9 %collective-permute-done.22 = bf16[4,256,128]{2,1,0:T(8,128)(2,1)S(1)} collective-permute-done((bf16[4,256,128]{2,1,0:T(8,128)(2,1)S(1)}, bf16[4,256,128]{2,1,0:T(8,128)(2,1)S(1)}, u32[]{:S(2)}, u32[]{:S(2)}) %collective-permute-start.22) | collective-permute-done | bytes 262176 | tf_op jit(solution)/shard_map/ppermute | solution.py:28
  177.3 0.2 convolution_bitcast_fusion.6
  177.6 0.1 fusion.64
  177.7 0.2 convolution_bitcast_fusion.5
  177.9 0.2 convolution_bitcast_fusion.2
  178.1 0.2 convolution_bitcast_fusion.3
  178.4 1.4 collective-permute-done.20
  179.7 0.2 convolution_bitcast_fusion.4
  179.9 0.2 fusion.13
  180.2 0.2 broadcast_in_dim.81
  180.4 22.0 %all_to_all.16 = bf16[16,256,128]{2,1,0:T(8,128)(2,1)S(1)} all-to-all(bf16[16,256,128]{2,1,0:T(8,128)(2,1)S(1)} %broadcast_in_dim.81), channel_id=1, replica_groups=mesh['zh'=4,'zl'=4,'ylo'=2,'x'=4,'yhi'=2,'core'=2] {'ylo','x','yhi'}, dimensions={0} | all-to-all | bytes 2097152 | tf_op jit(solution)/shard_map/all_to_all | solution.py:17
  202.4 0.9 fusion.2
  203.2 4.5 %collective-permute-start.24 = (bf16[128,1152]{1,0:T(8,128)(2,1)S(1)}, bf16[128,1152]{1,0:T(8,128)(2,1)S(1)}, u32[]{:S(2)}, u32[]{:S(2)}) collective-permute-start(bf16[128,1152]{1,0:T(8,128)(2,1)S(1)} %fusion.2), channel_id=1, source_target_pairs={{0,0},{1,16},{16,1},{17,17},{2,2},{3,18},{18,3},{19,19},{4,4},{5,2... | collective-permute-start | bytes 884744 | tf_op jit(solution)/shard_map/ppermute | solution.py:144
  207.7 0.9 fusion.1
  208.6 1.9 collective-permute-start.25
  210.5 1.6 collective-permute-done.24
  212.1 3.9 %collective-permute-done.25 = bf16[128,1152]{1,0:T(8,128)(2,1)S(1)} collective-permute-done((bf16[128,1152]{1,0:T(8,128)(2,1)S(1)}, bf16[128,1152]{1,0:T(8,128)(2,1)S(1)}, u32[]{:S(2)}, u32[]{:S(2)}) %collective-permute-start.25) | collective-permute-done | bytes 294944 | tf_op jit(solution)/shard_map/ppermute | solution.py:142
  216.1 0.9 convert_add_fusion
  (47 shorter events, 0.9 us)
Async XLA Ops:
  1.1 19.3 %collective-permute-start.3 = (bf16[128,1152]{1,0:T(8,128)(2,1)S(1)}, bf16[128,1152]{1,0:T(8,128)(2,1)S(1)}, u32[]{:S(2)}, u32[]{:S(2)}) collective-permute-start(bf16[128,1152]{1,0:T(8,128)(2,1)S(1)} %convert_element_type.39), channel_id=1, source_target_pairs={{0,481},{1,497},{16,32},{17,48},{32,1},{33,17},{48,64},{49,80},{64... | collective-permute-start | bytes 884744 | tf_op jit(solution)/shard_map/ppermute | solution.py:46
  14.1 11.2 %collective-permute-start.2 = (bf16[128,1152]{1,0:T(8,128)(2,1)S(1)}, bf16[128,1152]{1,0:T(8,128)(2,1)S(1)}, u32[]{:S(2)}, u32[]{:S(2)}) collective-permute-start(bf16[128,1152]{1,0:T(8,128)(2,1)S(1)} %convert_element_type.39), channel_id=1, source_target_pairs={{0,32},{1,48},{16,481},{17,497},{32,64},{33,80},{48,1},{49,17},{64... | collective-permute-start | bytes 884744 | tf_op jit(solution)/shard_map/ppermute | solution.py:46
  16.0 12.3 %collective-permute-start = (bf16[128,1152]{1,0:T(8,128)(2,1)S(1)}, bf16[128,1152]{1,0:T(8,128)(2,1)S(1)}, u32[]{:S(2)}, u32[]{:S(2)}) collective-permute-start(bf16[128,1152]{1,0:T(8,128)(2,1)S(1)} %convert_element_type.39), channel_id=1, source_target_pairs={{0,0},{1,16},{16,1},{17,17},{2,2},{3,18},{18,3},{19,19},{4,4},{5,2... | collective-permute-start | bytes 884744 | tf_op jit(solution)/shard_map/ppermute | solution.py:77
  20.4 9.8 %collective-permute-start.4 = (bf16[128,1152]{1,0:T(8,128)(2,1)S(1)}, bf16[128,1152]{1,0:T(8,128)(2,1)S(1)}, u32[]{:S(2)}, u32[]{:S(2)}) collective-permute-start(bf16[128,1152]{1,0:T(8,128)(2,1)S(1)} %collective-permute-done.3), channel_id=1, source_target_pairs={{0,32},{1,481},{32,64},{33,1},{64,96},{65,33},{96,128},{97,65},{12... | collective-permute-start | bytes 884744 | tf_op jit(solution)/shard_map/ppermute | solution.py:28
  25.3 8.8 %collective-permute-start.7 = (bf16[128,1152]{1,0:T(8,128)(2,1)S(1)}, bf16[128,1152]{1,0:T(8,128)(2,1)S(1)}, u32[]{:S(2)}, u32[]{:S(2)}) collective-permute-start(bf16[128,1152]{1,0:T(8,128)(2,1)S(1)} %collective-permute-done.2), channel_id=1, source_target_pairs={{0,32},{1,481},{32,64},{33,1},{64,96},{65,33},{96,128},{97,65},{12... | collective-permute-start | bytes 884744 | tf_op jit(solution)/shard_map/ppermute | solution.py:28
  28.3 76.1 %collective-permute-start.1 = (bf16[128,1152]{1,0:T(8,128)(2,1)S(1)}, bf16[128,1152]{1,0:T(8,128)(2,1)S(1)}, u32[]{:S(2)}, u32[]{:S(2)}) collective-permute-start(bf16[128,1152]{1,0:T(8,128)(2,1)S(1)} %collective-permute-done), channel_id=1, source_target_pairs={{0,1},{1,0},{2,3},{3,2},{4,5},{5,4},{6,7},{7,6},{8,9},{9,8},{10,11... | collective-permute-start | bytes 884744 | tf_op jit(solution)/shard_map/ppermute | solution.py:78
  30.3 16.2 %collective-permute-start.5 = (bf16[128,1152]{1,0:T(8,128)(2,1)S(1)}, bf16[128,1152]{1,0:T(8,128)(2,1)S(1)}, u32[]{:S(2)}, u32[]{:S(2)}) collective-permute-start(bf16[128,1152]{1,0:T(8,128)(2,1)S(1)} %collective-permute-done.4), channel_id=1, source_target_pairs={{0,32},{1,481},{32,64},{33,1},{64,96},{65,33},{96,128},{97,65},{12... | collective-permute-start | bytes 884744 | tf_op jit(solution)/shard_map/ppermute | solution.py:28
  34.1 7.8 %collective-permute-start.8 = (bf16[128,1152]{1,0:T(8,128)(2,1)S(1)}, bf16[128,1152]{1,0:T(8,128)(2,1)S(1)}, u32[]{:S(2)}, u32[]{:S(2)}) collective-permute-start(bf16[128,1152]{1,0:T(8,128)(2,1)S(1)} %collective-permute-done.7), channel_id=1, source_target_pairs={{0,32},{1,481},{32,64},{33,1},{64,96},{65,33},{96,128},{97,65},{12... | collective-permute-start | bytes 884744 | tf_op jit(solution)/shard_map/ppermute | solution.py:28
  41.9 16.4 %collective-permute-start.9 = (bf16[128,1152]{1,0:T(8,128)(2,1)S(1)}, bf16[128,1152]{1,0:T(8,128)(2,1)S(1)}, u32[]{:S(2)}, u32[]{:S(2)}) collective-permute-start(bf16[128,1152]{1,0:T(8,128)(2,1)S(1)} %collective-permute-done.8), channel_id=1, source_target_pairs={{0,32},{1,481},{32,64},{33,1},{64,96},{65,33},{96,128},{97,65},{12... | collective-permute-start | bytes 884744 | tf_op jit(solution)/shard_map/ppermute | solution.py:28
  46.4 7.8 %collective-permute-start.10 = (bf16[128,1152]{1,0:T(8,128)(2,1)S(1)}, bf16[128,1152]{1,0:T(8,128)(2,1)S(1)}, u32[]{:S(2)}, u32[]{:S(2)}) collective-permute-start(bf16[128,1152]{1,0:T(8,128)(2,1)S(1)} %collective-permute-done.5), channel_id=1, source_target_pairs={{0,32},{1,481},{32,64},{33,1},{64,96},{65,33},{96,128},{97,65},{12... | collective-permute-start | bytes 884744 | tf_op jit(solution)/shard_map/ppermute | solution.py:28
  48.9 37.3 %collective-permute-start.6 = (bf16[3,128,1152]{2,1,0:T(8,128)(2,1)S(1)}, bf16[3,128,1152]{2,1,0:T(8,128)(2,1)S(1)}, u32[]{:S(2)}, u32[]{:S(2)}) collective-permute-start(bf16[3,128,1152]{2,1,0:T(8,128)(2,1)S(1)} %pad_maximum_fusion.2), channel_id=1, source_target_pairs={{0,1},{1,0},{2,3},{3,2},{4,5},{5,4},{6,7},{7,6},{8,9},{9,8},{10,11... | collective-permute-start | bytes 2654216 | tf_op jit(solution)/shard_map/ppermute | solution.py:50
  54.2 15.9 %collective-permute-start.11 = (bf16[128,1152]{1,0:T(8,128)(2,1)S(1)}, bf16[128,1152]{1,0:T(8,128)(2,1)S(1)}, u32[]{:S(2)}, u32[]{:S(2)}) collective-permute-start(bf16[128,1152]{1,0:T(8,128)(2,1)S(1)} %collective-permute-done.10), channel_id=1, source_target_pairs={{0,32},{1,481},{32,64},{33,1},{64,96},{65,33},{96,128},{97,65},{12... | collective-permute-start | bytes 884744 | tf_op jit(solution)/shard_map/ppermute | solution.py:28
  58.3 7.8 %collective-permute-start.13 = (bf16[128,1152]{1,0:T(8,128)(2,1)S(1)}, bf16[128,1152]{1,0:T(8,128)(2,1)S(1)}, u32[]{:S(2)}, u32[]{:S(2)}) collective-permute-start(bf16[128,1152]{1,0:T(8,128)(2,1)S(1)} %collective-permute-done.9), channel_id=1, source_target_pairs={{0,32},{1,481},{32,64},{33,1},{64,96},{65,33},{96,128},{97,65},{12... | collective-permute-start | bytes 884744 | tf_op jit(solution)/shard_map/ppermute | solution.py:28
  66.0 16.6 %collective-permute-start.14 = (bf16[128,1152]{1,0:T(8,128)(2,1)S(1)}, bf16[128,1152]{1,0:T(8,128)(2,1)S(1)}, u32[]{:S(2)}, u32[]{:S(2)}) collective-permute-start(bf16[128,1152]{1,0:T(8,128)(2,1)S(1)} %collective-permute-done.13), channel_id=1, source_target_pairs={{0,32},{1,481},{32,64},{33,1},{64,96},{65,33},{96,128},{97,65},{12... | collective-permute-start | bytes 884744 | tf_op jit(solution)/shard_map/ppermute | solution.py:28
  70.1 7.6 %collective-permute-start.15 = (bf16[128,1152]{1,0:T(8,128)(2,1)S(1)}, bf16[128,1152]{1,0:T(8,128)(2,1)S(1)}, u32[]{:S(2)}, u32[]{:S(2)}) collective-permute-start(bf16[128,1152]{1,0:T(8,128)(2,1)S(1)} %collective-permute-done.11), channel_id=1, source_target_pairs={{0,32},{1,481},{32,64},{33,1},{64,96},{65,33},{96,128},{97,65},{12... | collective-permute-start | bytes 884744 | tf_op jit(solution)/shard_map/ppermute | solution.py:28
  72.1 26.4 %collective-permute-start.12 = (bf16[2,128,1152]{2,1,0:T(8,128)(2,1)S(1)}, bf16[2,128,1152]{2,1,0:T(8,128)(2,1)S(1)}, u32[]{:S(2)}, u32[]{:S(2)}) collective-permute-start(bf16[2,128,1152]{2,1,0:T(8,128)(2,1)S(1)} %pad_maximum_fusion.3), channel_id=1, source_target_pairs={{0,1},{1,0},{2,3},{3,2},{4,5},{5,4},{6,7},{7,6},{8,9},{9,8},{10,11... | collective-permute-start | bytes 1769480 | tf_op jit(solution)/shard_map/ppermute | solution.py:50
  77.7 8.8 %collective-permute-start.16 = (bf16[128,1152]{1,0:T(8,128)(2,1)S(1)}, bf16[128,1152]{1,0:T(8,128)(2,1)S(1)}, u32[]{:S(2)}, u32[]{:S(2)}) collective-permute-start(bf16[128,1152]{1,0:T(8,128)(2,1)S(1)} %collective-permute-done.15), channel_id=1, source_target_pairs={{0,32},{1,481},{32,64},{33,1},{64,96},{65,33},{96,128},{97,65},{12... | collective-permute-start | bytes 884744 | tf_op jit(solution)/shard_map/ppermute | solution.py:28
  82.6 14.0 %collective-permute-start.18 = (bf16[128,1152]{1,0:T(8,128)(2,1)S(1)}, bf16[128,1152]{1,0:T(8,128)(2,1)S(1)}, u32[]{:S(2)}, u32[]{:S(2)}) collective-permute-start(bf16[128,1152]{1,0:T(8,128)(2,1)S(1)} %collective-permute-done.14), channel_id=1, source_target_pairs={{0,32},{1,481},{32,64},{33,1},{64,96},{65,33},{96,128},{97,65},{12... | collective-permute-start | bytes 884744 | tf_op jit(solution)/shard_map/ppermute | solution.py:28
  86.6 12.1 %collective-permute-start.17 = (bf16[2,128,1152]{2,1,0:T(8,128)(2,1)S(1)}, bf16[2,128,1152]{2,1,0:T(8,128)(2,1)S(1)}, u32[]{:S(2)}, u32[]{:S(2)}) collective-permute-start(bf16[2,128,1152]{2,1,0:T(8,128)(2,1)S(1)} %pad_maximum_fusion.4), channel_id=1, source_target_pairs={{0,1},{1,0},{2,3},{3,2},{4,5},{5,4},{6,7},{7,6},{8,9},{9,8},{10,11... | collective-permute-start | bytes 1769480 | tf_op jit(solution)/shard_map/ppermute | solution.py:50
  96.6 7.8 %collective-permute-start.19 = (bf16[128,1152]{1,0:T(8,128)(2,1)S(1)}, bf16[128,1152]{1,0:T(8,128)(2,1)S(1)}, u32[]{:S(2)}, u32[]{:S(2)}) collective-permute-start(bf16[128,1152]{1,0:T(8,128)(2,1)S(1)} %collective-permute-done.18), channel_id=1, source_target_pairs={{0,32},{1,481},{32,64},{33,1},{64,96},{65,33},{96,128},{97,65},{12... | collective-permute-start | bytes 884744 | tf_op jit(solution)/shard_map/ppermute | solution.py:28
  104.4 2.1 copy-start
  129.0 23.2 %all-to-all-start.1 = ((bf16[16,256,128]{2,1,0:T(8,128)(2,1)}), bf16[16,256,128]{2,1,0:T(8,128)(2,1)S(1)}, u32[]{:S(2)}, u32[]{:S(2)}) async-start(bf16[16,256,128]{2,1,0:T(8,128)(2,1)} %broadcast_in_dim.79), calls=%async_computation.1 | async-start | bytes 2097152 | tf_op jit(solution)/shard_map/all_to_all | solution.py:17
  152.3 50.1 %slice-start = ((s8[4718592]{0:T(1024)(128)(4,1)}), s8[4194304]{0:T(1024)(128)(4,1)S(1)}, s32[]{:S(2)}) async-start(s8[4718592]{0:T(1024)(128)(4,1)} %bitcast.120), calls=%async_computation.3 | async-start | bytes 8388608
  152.4 25.1 %collective-permute-start.23 = (bf16[4,4,256,128]{3,2,1,0:T(8,128)(2,1)S(1)}, bf16[4,4,256,128]{3,2,1,0:T(8,128)(2,1)S(1)}, u32[]{:S(2)}, u32[]{:S(2)}) collective-permute-start(bf16[4,4,256,128]{3,2,1,0:T(8,128)(2,1)S(1)} %pad_maximum_fusion.1), channel_id=1, source_target_pairs={{0,1},{1,0},{2,3},{3,2},{4,5},{5,4},{6,7},{7,6},{8,9},{9,8},{10,11... | collective-permute-start | bytes 3145736 | tf_op jit(solution)/shard_map/ppermute | solution.py:130
  160.2 11.0 %collective-permute-start.21 = (bf16[4,256,128]{2,1,0:T(8,128)(2,1)S(1)}, bf16[4,256,128]{2,1,0:T(8,128)(2,1)S(1)}, u32[]{:S(2)}, u32[]{:S(2)}) collective-permute-start(bf16[4,256,128]{2,1,0:T(8,128)(2,1)S(1)} %bitcast.127), channel_id=1, source_target_pairs={{0,32},{1,33},{32,64},{33,65},{64,96},{65,97},{96,128},{97,129},{1... | collective-permute-start | bytes 786440 | tf_op jit(solution)/shard_map/ppermute | solution.py:28
  162.4 15.0 %collective-permute-start.22 = (bf16[4,256,128]{2,1,0:T(8,128)(2,1)S(1)}, bf16[4,256,128]{2,1,0:T(8,128)(2,1)S(1)}, u32[]{:S(2)}, u32[]{:S(2)}) collective-permute-start(bf16[4,256,128]{2,1,0:T(8,128)(2,1)S(1)} %bitcast.128), channel_id=1, source_target_pairs={{0,448},{1,65},{32,480},{33,97},{64,0},{65,129},{96,32},{97,161},{... | collective-permute-start | bytes 786440 | tf_op jit(solution)/shard_map/ppermute | solution.py:28
  166.8 13.0 %collective-permute-start.20 = (bf16[4,256,128]{2,1,0:T(8,128)(2,1)S(1)}, bf16[4,256,128]{2,1,0:T(8,128)(2,1)S(1)}, u32[]{:S(2)}, u32[]{:S(2)}) collective-permute-start(bf16[4,256,128]{2,1,0:T(8,128)(2,1)S(1)} %bitcast.129), channel_id=1, source_target_pairs={{0,480},{1,481},{32,0},{33,1},{64,32},{65,33},{96,64},{97,65},{128... | collective-permute-start | bytes 786440 | tf_op jit(solution)/shard_map/ppermute | solution.py:28
  177.9 24.5 %slice-start.1 = ((s8[4718592]{0:T(1024)(128)(4,1)}), s8[524288]{0:T(1024)(128)(4,1)S(1)}, s32[]{:S(2)}) async-start(s8[4718592]{0:T(1024)(128)(4,1)} %bitcast.120), calls=%async_computation.4 | async-start | bytes 1048576
  203.2 8.9 %collective-permute-start.24 = (bf16[128,1152]{1,0:T(8,128)(2,1)S(1)}, bf16[128,1152]{1,0:T(8,128)(2,1)S(1)}, u32[]{:S(2)}, u32[]{:S(2)}) collective-permute-start(bf16[128,1152]{1,0:T(8,128)(2,1)S(1)} %fusion.2), channel_id=1, source_target_pairs={{0,0},{1,16},{16,1},{17,17},{2,2},{3,18},{18,3},{19,19},{4,4},{5,2... | collective-permute-start | bytes 884744 | tf_op jit(solution)/shard_map/ppermute | solution.py:144
  208.6 7.5 %collective-permute-start.25 = (bf16[128,1152]{1,0:T(8,128)(2,1)S(1)}, bf16[128,1152]{1,0:T(8,128)(2,1)S(1)}, u32[]{:S(2)}, u32[]{:S(2)}) collective-permute-start(bf16[128,1152]{1,0:T(8,128)(2,1)S(1)} %fusion.1), channel_id=1, source_target_pairs={{0,16},{1,0},{16,17},{17,1},{2,18},{3,2},{18,19},{19,3},{4,20},{5,... | collective-permute-start | bytes 884744 | tf_op jit(solution)/shard_map/ppermute | solution.py:142

commit v15 on v14

--- a/solution.py
+++ b/solution.py
@@ -41,7 +41,10 @@
                 to = ylo ^ side
                 ahead = (place + 1 - 2 * to) % size
                 pairs.append(
-                    (4 * place + 2 * ylo + core, 4 * ahead + 2 * core + to)
+                    (
+                        4 * place + 2 * ylo + core,
+                        4 * ahead + 2 * (core ^ side) + to,
+                    )
                 )
     return lax.ppermute(piece, LINE + ("ylo", "core"), pairs)
 
@@ -77,7 +80,7 @@
     own = lax.ppermute(rounded, ("ylo", "core"), TURN)
     other = lax.ppermute(own, "core", SWAP)
     slabs = groups * steps
-    near, far = [own, launch(rounded, 0)], [None, launch(rounded, 1)]
+    near, far = [own, launch(rounded, 0)], [None, launch(swap([rounded])[0], 1)]
     for step in range(2, slabs // 2):
         near.append(onward(near[-1]))
         far.append(onward(far[-1]))

time: 218 us -> 207 us (0.950)
  waiting for transfers between devices: 32.3 us -> 18.4 us
    ppermute x16, waiting for transfers between devices: 26.4 us -> 9.87 us  [along(): return lax.ppermute(piece, LINE + ('core',), pairs)]
    ppermute x16, starting transfers between devices: 52.8 us -> 61.3 us  [along(): return lax.ppermute(piece, LINE + ('core',), pairs)]
    ppermute x2, starting transfers between devices: 14.9 us -> 7.67 us  [launch(): return lax.ppermute(piece, LINE + ('ylo', 'core'), pairs)]
    all_to_all x1, blocking collectives: 21 us -> 24.7 us  [per_device(): summands = lax.all_to_all(partial_gram, PLANE, 0, 0)]
    all_gather x1, blocking collectives: 19.4 us -> 16.8 us  [per_device(): here = lax.all_gather(gram_low, 'zh', axis=0)]
    ppermute x3 -> x4, starting transfers between devices: 18.6 us -> 19.6 us  [swap(): return list(lax.ppermute(jnp.stack(pieces), 'core', SWAP))]
  transfers between devices with their start and end apart: 27 -> 28, of which waited for: 10 -> 10; matrix products, arithmetic and copies ran while one was open for 2% -> 2% of each run, Pallas kernels for 0% -> 0%
where the time goes in v15:
time: 207 us; the launch traced here: 206 us
  starting transfers between devices  112 us (54%)
  blocking collectives  61.7 us (30%)
  waiting for transfers between devices  18.4 us (9%)
  matrix products  5 us (2%)
  other arithmetic  3.91 us (2%)
  local copies, waits for them, and re-layouts  3.39 us (2%)
    ppermute x16, starting transfers between devices, along(): return lax.ppermute(piece, LINE + ('core',), pairs)  61.3 us
    all_to_all x1, blocking collectives, per_device(): summands = lax.all_to_all(partial_gram, PLANE, 0, 0)  24.7 us
    all_to_all x1, blocking collectives, share(): return lax.all_to_all(copies, PLANE, 0, 0)  20.3 us
    ppermute x4, starting transfers between devices, swap(): return list(lax.ppermute(jnp.stack(pieces), 'core', SWAP))  19.6 us
    all_gather x1, blocking collectives, per_device(): here = lax.all_gather(gram_low, 'zh', axis=0)  16.8 us
    ppermute x16, waiting for transfers between devices, along(): return lax.ppermute(piece, LINE + ('core',), pairs)  9.87 us
    ppermute x2, starting transfers between devices, launch(): return lax.ppermute(piece, LINE + ('ylo', 'core'), pairs)  7.67 us
    ppermute x1, starting transfers between devices, per_device(): left_other = lax.ppermute(jnp.stack(left_own), 'core', SWAP)  7.53 us
  transfers between devices with their start and end apart: 28, of which 10 were waited for; matrix products, arithmetic and copies ran while one was open for 2% of the time, Pallas kernels for 0%

profile of v15, /device:TPU:1, one launch (start us, length us, event | category | flops | bytes accessed | tf_op | source)
XLA Modules:
  0.0 205.8 jit_solution(2772450356612306665)
XLA Ops:
  0.0 1.1 convert_bitcast_fusion
  1.1 8.8 %collective-permute-start.3 = (bf16[1,128,1152]{2,1,0:T(8,128)(2,1)S(1)}, bf16[1,128,1152]{2,1,0:T(8,128)(2,1)S(1)}, u32[]{:S(2)}, u32[]{:S(2)}) collective-permute-start(bf16[1,128,1152]{2,1,0:T(8,128)(2,1)S(1)} %convert_bitcast_fusion), channel_id=1, source_target_pairs={{0,1},{1,0},{2,3},{3,2},{4,5},{5,4},{6,7},{7,6},{8,9},{9,8},{10,11... | collective-permute-start | bytes 884744 | tf_op jit(solution)/shard_map/ppermute | solution.py:53
  9.9 1.1 convert_element_type.39
  11.0 1.9 collective-permute-start.2
  12.9 5.7 %collective-permute-start.4 = (bf16[128,1152]{1,0:T(8,128)(2,1)S(1)}, bf16[128,1152]{1,0:T(8,128)(2,1)S(1)}, u32[]{:S(2)}, u32[]{:S(2)}) collective-permute-start(bf16[128,1152]{1,0:T(8,128)(2,1)S(1)} %bitcast.142), channel_id=1, source_target_pairs={{0,497},{1,481},{16,48},{17,32},{32,17},{33,1},{48,80},{49,64},{64... | collective-permute-start | bytes 884744 | tf_op jit(solution)/shard_map/ppermute | solution.py:49
  18.7 1.5 collective-permute-done.2
  20.2 9.9 %collective-permute-start.8 = (bf16[128,1152]{1,0:T(8,128)(2,1)S(1)}, bf16[128,1152]{1,0:T(8,128)(2,1)S(1)}, u32[]{:S(2)}, u32[]{:S(2)}) collective-permute-start(bf16[128,1152]{1,0:T(8,128)(2,1)S(1)} %collective-permute-done.2), channel_id=1, source_target_pairs={{0,32},{1,481},{32,64},{33,1},{64,96},{65,33},{96,128},{97,65},{12... | collective-permute-start | bytes 884744 | tf_op jit(solution)/shard_map/ppermute | solution.py:28
  30.1 1.9 collective-permute-start
  32.1 2.7 %collective-permute-start.5 = (bf16[128,1152]{1,0:T(8,128)(2,1)S(1)}, bf16[128,1152]{1,0:T(8,128)(2,1)S(1)}, u32[]{:S(2)}, u32[]{:S(2)}) collective-permute-start(bf16[128,1152]{1,0:T(8,128)(2,1)S(1)} %collective-permute-done.4), channel_id=1, source_target_pairs={{0,32},{1,481},{32,64},{33,1},{64,96},{65,33},{96,128},{97,65},{12... | collective-permute-start | bytes 884744 | tf_op jit(solution)/shard_map/ppermute | solution.py:28
  34.8 4.0 %collective-permute-start.9 = (bf16[128,1152]{1,0:T(8,128)(2,1)S(1)}, bf16[128,1152]{1,0:T(8,128)(2,1)S(1)}, u32[]{:S(2)}, u32[]{:S(2)}) collective-permute-start(bf16[128,1152]{1,0:T(8,128)(2,1)S(1)} %collective-permute-done.8), channel_id=1, source_target_pairs={{0,32},{1,481},{32,64},{33,1},{64,96},{65,33},{96,128},{97,65},{12... | collective-permute-start | bytes 884744 | tf_op jit(solution)/shard_map/ppermute | solution.py:28
  39.2 1.9 collective-permute-start.1
  41.1 2.5 %collective-permute-start.6 = (bf16[128,1152]{1,0:T(8,128)(2,1)S(1)}, bf16[128,1152]{1,0:T(8,128)(2,1)S(1)}, u32[]{:S(2)}, u32[]{:S(2)}) collective-permute-start(bf16[128,1152]{1,0:T(8,128)(2,1)S(1)} %collective-permute-done.5), channel_id=1, source_target_pairs={{0,32},{1,481},{32,64},{33,1},{64,96},{65,33},{96,128},{97,65},{12... | collective-permute-start | bytes 884744 | tf_op jit(solution)/shard_map/ppermute | solution.py:28
  43.6 3.9 %collective-permute-start.10 = (bf16[128,1152]{1,0:T(8,128)(2,1)S(1)}, bf16[128,1152]{1,0:T(8,128)(2,1)S(1)}, u32[]{:S(2)}, u32[]{:S(2)}) collective-permute-start(bf16[128,1152]{1,0:T(8,128)(2,1)S(1)} %collective-permute-done.9), channel_id=1, source_target_pairs={{0,32},{1,481},{32,64},{33,1},{64,96},{65,33},{96,128},{97,65},{12... | collective-permute-start | bytes 884744 | tf_op jit(solution)/shard_map/ppermute | solution.py:28
  47.5 0.6 broadcast_in_dim.67
  48.2 0.7 collective-permute-done.6
  48.9 3.4 %collective-permute-start.11 = (bf16[128,1152]{1,0:T(8,128)(2,1)S(1)}, bf16[128,1152]{1,0:T(8,128)(2,1)S(1)}, u32[]{:S(2)}, u32[]{:S(2)}) collective-permute-start(bf16[128,1152]{1,0:T(8,128)(2,1)S(1)} %collective-permute-done.6), channel_id=1, source_target_pairs={{0,32},{1,481},{32,64},{33,1},{64,96},{65,33},{96,128},{97,65},{12... | collective-permute-start | bytes 884744 | tf_op jit(solution)/shard_map/ppermute | solution.py:28
  52.3 3.9 %collective-permute-start.14 = (bf16[128,1152]{1,0:T(8,128)(2,1)S(1)}, bf16[128,1152]{1,0:T(8,128)(2,1)S(1)}, u32[]{:S(2)}, u32[]{:S(2)}) collective-permute-start(bf16[128,1152]{1,0:T(8,128)(2,1)S(1)} %collective-permute-done.10), channel_id=1, source_target_pairs={{0,32},{1,481},{32,64},{33,1},{64,96},{65,33},{96,128},{97,65},{12... | collective-permute-start | bytes 884744 | tf_op jit(solution)/shard_map/ppermute | solution.py:28
  56.1 0.1 multiply_reduce_fusion
  56.3 0.1 pad_maximum_fusion.2
  56.4 2.3 %collective-permute-start.7 = (bf16[3,128,1152]{2,1,0:T(8,128)(2,1)S(1)}, bf16[3,128,1152]{2,1,0:T(8,128)(2,1)S(1)}, u32[]{:S(2)}, u32[]{:S(2)}) collective-permute-start(bf16[3,128,1152]{2,1,0:T(8,128)(2,1)S(1)} %pad_maximum_fusion.2), channel_id=1, source_target_pairs={{0,1},{1,0},{2,3},{3,2},{4,5},{5,4},{6,7},{7,6},{8,9},{9,8},{10,11... | collective-permute-start | bytes 2654216 | tf_op jit(solution)/shard_map/ppermute | solution.py:53
  58.7 4.9 %collective-permute-start.12 = (bf16[128,1152]{1,0:T(8,128)(2,1)S(1)}, bf16[128,1152]{1,0:T(8,128)(2,1)S(1)}, u32[]{:S(2)}, u32[]{:S(2)}) collective-permute-start(bf16[128,1152]{1,0:T(8,128)(2,1)S(1)} %collective-permute-done.11), channel_id=1, source_target_pairs={{0,32},{1,481},{32,64},{33,1},{64,96},{65,33},{96,128},{97,65},{12... | collective-permute-start | bytes 884744 | tf_op jit(solution)/shard_map/ppermute | solution.py:28
  63.6 2.4 %collective-permute-start.15 = (bf16[128,1152]{1,0:T(8,128)(2,1)S(1)}, bf16[128,1152]{1,0:T(8,128)(2,1)S(1)}, u32[]{:S(2)}, u32[]{:S(2)}) collective-permute-start(bf16[128,1152]{1,0:T(8,128)(2,1)S(1)} %collective-permute-done.14), channel_id=1, source_target_pairs={{0,32},{1,481},{32,64},{33,1},{64,96},{65,33},{96,128},{97,65},{12... | collective-permute-start | bytes 884744 | tf_op jit(solution)/shard_map/ppermute | solution.py:28
  66.0 1.2 collective-permute-done.12
  67.2 5.0 %collective-permute-start.16 = (bf16[128,1152]{1,0:T(8,128)(2,1)S(1)}, bf16[128,1152]{1,0:T(8,128)(2,1)S(1)}, u32[]{:S(2)}, u32[]{:S(2)}) collective-permute-start(bf16[128,1152]{1,0:T(8,128)(2,1)S(1)} %collective-permute-done.12), channel_id=1, source_target_pairs={{0,32},{1,481},{32,64},{33,1},{64,96},{65,33},{96,128},{97,65},{12... | collective-permute-start | bytes 884744 | tf_op jit(solution)/shard_map/ppermute | solution.py:28
  72.3 3.1 %collective-permute-start.19 = (bf16[128,1152]{1,0:T(8,128)(2,1)S(1)}, bf16[128,1152]{1,0:T(8,128)(2,1)S(1)}, u32[]{:S(2)}, u32[]{:S(2)}) collective-permute-start(bf16[128,1152]{1,0:T(8,128)(2,1)S(1)} %collective-permute-done.15), channel_id=1, source_target_pairs={{0,32},{1,481},{32,64},{33,1},{64,96},{65,33},{96,128},{97,65},{12... | collective-permute-start | bytes 884744 | tf_op jit(solution)/shard_map/ppermute | solution.py:28
  75.5 2.7 %collective-permute-start.13 = (bf16[2,128,1152]{2,1,0:T(8,128)(2,1)S(1)}, bf16[2,128,1152]{2,1,0:T(8,128)(2,1)S(1)}, u32[]{:S(2)}, u32[]{:S(2)}) collective-permute-start(bf16[2,128,1152]{2,1,0:T(8,128)(2,1)S(1)} %pad_maximum_fusion.3), channel_id=1, source_target_pairs={{0,1},{1,0},{2,3},{3,2},{4,5},{5,4},{6,7},{7,6},{8,9},{9,8},{10,11... | collective-permute-start | bytes 1769480 | tf_op jit(solution)/shard_map/ppermute | solution.py:53
  78.2 4.9 %collective-permute-start.17 = (bf16[128,1152]{1,0:T(8,128)(2,1)S(1)}, bf16[128,1152]{1,0:T(8,128)(2,1)S(1)}, u32[]{:S(2)}, u32[]{:S(2)}) collective-permute-start(bf16[128,1152]{1,0:T(8,128)(2,1)S(1)} %collective-permute-done.16), channel_id=1, source_target_pairs={{0,32},{1,481},{32,64},{33,1},{64,96},{65,33},{96,128},{97,65},{12... | collective-permute-start | bytes 884744 | tf_op jit(solution)/shard_map/ppermute | solution.py:28
  83.1 2.4 %collective-permute-start.20 = (bf16[128,1152]{1,0:T(8,128)(2,1)S(1)}, bf16[128,1152]{1,0:T(8,128)(2,1)S(1)}, u32[]{:S(2)}, u32[]{:S(2)}) collective-permute-start(bf16[128,1152]{1,0:T(8,128)(2,1)S(1)} %collective-permute-done.19), channel_id=1, source_target_pairs={{0,32},{1,481},{32,64},{33,1},{64,96},{65,33},{96,128},{97,65},{12... | collective-permute-start | bytes 884744 | tf_op jit(solution)/shard_map/ppermute | solution.py:28
  85.8 0.9 collective-permute-done.17
  86.8 5.9 %collective-permute-start.18 = (bf16[2,128,1152]{2,1,0:T(8,128)(2,1)S(1)}, bf16[2,128,1152]{2,1,0:T(8,128)(2,1)S(1)}, u32[]{:S(2)}, u32[]{:S(2)}) collective-permute-start(bf16[2,128,1152]{2,1,0:T(8,128)(2,1)S(1)} %pad_maximum_fusion.4), channel_id=1, source_target_pairs={{0,1},{1,0},{2,3},{3,2},{4,5},{5,4},{6,7},{7,6},{8,9},{9,8},{10,11... | collective-permute-start | bytes 1769480 | tf_op jit(solution)/shard_map/ppermute | solution.py:53
  92.9 1.4 collective-permute-done.18
  94.5 1.6 fusion.3
  96.1 0.6 copy-done
  96.7 24.7 %all_to_all.15 = bf16[16,272,128]{2,1,0:T(8,128)(2,1)S(1)} all-to-all(bf16[16,272,128]{2,1,0:T(8,128)(2,1)S(1)} %pad_maximum_fusion), channel_id=1, replica_groups=mesh['zh'=4,'zl'=4,'ylo'=2,'x'=4,'yhi'=2,'core'=2] {'ylo','x','yhi'}, dimensions={0} | all-to-all | bytes 2228224 | tf_op jit(solution)/shard_map/all_to_all | solution.py:109
  121.4 0.2 convert_reduce_fusion
  121.6 1.2 broadcast_in_dim.79
  122.8 3.7 %all-to-all-start.1 = ((bf16[16,256,128]{2,1,0:T(8,128)(2,1)}), bf16[16,256,128]{2,1,0:T(8,128)(2,1)S(1)}, u32[]{:S(2)}, u32[]{:S(2)}) async-start(bf16[16,256,128]{2,1,0:T(8,128)(2,1)} %broadcast_in_dim.79), calls=%async_computation.1 | async-start | bytes 2097152 | tf_op jit(solution)/shard_map/all_to_all | solution.py:17
  126.6 16.8 %all-gather = bf16[1024,128]{1,0:T(8,128)(2,1)S(1)} all-gather(bf16[256,128]{1,0:T(8,128)(2,1)S(1)} %fusion.47), channel_id=2, replica_groups=mesh['zh'=4,'zl'=4,'ylo'=2,'x'=4,'yhi'=2,'core'=2] {'zh'}, dimensions={0}, use_global_device_ids=true | all-gather | bytes 327680 | tf_op jit(solution)/shard_map/all_gather | solution.py:121
  143.4 0.1 pad_maximum_fusion.1
  143.6 7.5 %collective-permute-start.24 = (bf16[4,4,256,128]{3,2,1,0:T(8,128)(2,1)S(1)}, bf16[4,4,256,128]{3,2,1,0:T(8,128)(2,1)S(1)}, u32[]{:S(2)}, u32[]{:S(2)}) collective-permute-start(bf16[4,4,256,128]{3,2,1,0:T(8,128)(2,1)S(1)} %pad_maximum_fusion.1), channel_id=1, source_target_pairs={{0,1},{1,0},{2,3},{3,2},{4,5},{5,4},{6,7},{7,6},{8,9},{9,8},{10,11... | collective-permute-start | bytes 3145736 | tf_op jit(solution)/shard_map/ppermute | solution.py:133
  151.1 1.9 collective-permute-start.22
  153.1 1.9 collective-permute-start.23
  155.0 4.6 %collective-permute-start.21 = (bf16[4,256,128]{2,1,0:T(8,128)(2,1)S(1)}, bf16[4,256,128]{2,1,0:T(8,128)(2,1)S(1)}, u32[]{:S(2)}, u32[]{:S(2)}) collective-permute-start(bf16[4,256,128]{2,1,0:T(8,128)(2,1)S(1)} %bitcast.132), channel_id=1, source_target_pairs={{0,480},{1,481},{32,0},{33,1},{64,32},{65,33},{96,64},{97,65},{128... | collective-permute-start | bytes 786440 | tf_op jit(solution)/shard_map/ppermute | solution.py:28
  159.6 0.2 convolution_bitcast_fusion.9
  159.8 2.7 %collective-permute-done.22 = bf16[4,256,128]{2,1,0:T(8,128)(2,1)S(1)} collective-permute-done((bf16[4,256,128]{2,1,0:T(8,128)(2,1)S(1)}, bf16[4,256,128]{2,1,0:T(8,128)(2,1)S(1)}, u32[]{:S(2)}, u32[]{:S(2)}) %collective-permute-start.22) | collective-permute-done | bytes 262176 | tf_op jit(solution)/shard_map/ppermute | solution.py:28
  162.5 0.2 convolution_bitcast_fusion.7
  162.7 2.2 %collective-permute-done.23 = bf16[4,256,128]{2,1,0:T(8,128)(2,1)S(1)} collective-permute-done((bf16[4,256,128]{2,1,0:T(8,128)(2,1)S(1)}, bf16[4,256,128]{2,1,0:T(8,128)(2,1)S(1)}, u32[]{:S(2)}, u32[]{:S(2)}) %collective-permute-start.23) | collective-permute-done | bytes 262176 | tf_op jit(solution)/shard_map/ppermute | solution.py:28
  164.9 0.2 convolution_bitcast_fusion.6
  165.1 0.1 fusion.64
  165.3 0.2 convolution_bitcast_fusion.5
  165.5 0.2 convolution_bitcast_fusion.2
  165.7 0.2 convolution_bitcast_fusion.3
  165.9 2.1 %collective-permute-done.21 = bf16[4,256,128]{2,1,0:T(8,128)(2,1)S(1)} collective-permute-done((bf16[4,256,128]{2,1,0:T(8,128)(2,1)S(1)}, bf16[4,256,128]{2,1,0:T(8,128)(2,1)S(1)}, u32[]{:S(2)}, u32[]{:S(2)}) %collective-permute-start.21) | collective-permute-done | bytes 262176 | tf_op jit(solution)/shard_map/ppermute | solution.py:28
  168.0 0.2 convolution_bitcast_fusion.4
  168.2 0.2 fusion.13
  168.5 0.2 broadcast_in_dim.81
  168.7 20.3 %all_to_all.16 = bf16[16,256,128]{2,1,0:T(8,128)(2,1)S(1)} all-to-all(bf16[16,256,128]{2,1,0:T(8,128)(2,1)S(1)} %broadcast_in_dim.81), channel_id=1, replica_groups=mesh['zh'=4,'zl'=4,'ylo'=2,'x'=4,'yhi'=2,'core'=2] {'ylo','x','yhi'}, dimensions={0} | all-to-all | bytes 2097152 | tf_op jit(solution)/shard_map/all_to_all | solution.py:17
  189.0 0.9 fusion.2
  189.8 6.7 %collective-permute-start.25 = (bf16[128,1152]{1,0:T(8,128)(2,1)S(1)}, bf16[128,1152]{1,0:T(8,128)(2,1)S(1)}, u32[]{:S(2)}, u32[]{:S(2)}) collective-permute-start(bf16[128,1152]{1,0:T(8,128)(2,1)S(1)} %fusion.2), channel_id=1, source_target_pairs={{0,0},{1,16},{16,1},{17,17},{2,2},{3,18},{18,3},{19,19},{4,4},{5,2... | collective-permute-start | bytes 884744 | tf_op jit(solution)/shard_map/ppermute | solution.py:147
  196.5 0.9 fusion.1
  197.4 1.9 collective-permute-start.26
  199.3 1.6 collective-permute-done.25
  200.9 3.9 %collective-permute-done.26 = bf16[128,1152]{1,0:T(8,128)(2,1)S(1)} collective-permute-done((bf16[128,1152]{1,0:T(8,128)(2,1)S(1)}, bf16[128,1152]{1,0:T(8,128)(2,1)S(1)}, u32[]{:S(2)}, u32[]{:S(2)}) %collective-permute-start.26) | collective-permute-done | bytes 294944 | tf_op jit(solution)/shard_map/ppermute | solution.py:145
  204.9 0.9 convert_add_fusion
  (50 shorter events, 1.0 us)
Async XLA Ops:
  1.1 11.8 %collective-permute-start.3 = (bf16[1,128,1152]{2,1,0:T(8,128)(2,1)S(1)}, bf16[1,128,1152]{2,1,0:T(8,128)(2,1)S(1)}, u32[]{:S(2)}, u32[]{:S(2)}) collective-permute-start(bf16[1,128,1152]{2,1,0:T(8,128)(2,1)S(1)} %convert_bitcast_fusion), channel_id=1, source_target_pairs={{0,1},{1,0},{2,3},{3,2},{4,5},{5,4},{6,7},{7,6},{8,9},{9,8},{10,11... | collective-permute-start | bytes 884744 | tf_op jit(solution)/shard_map/ppermute | solution.py:53
  11.0 9.2 %collective-permute-start.2 = (bf16[128,1152]{1,0:T(8,128)(2,1)S(1)}, bf16[128,1152]{1,0:T(8,128)(2,1)S(1)}, u32[]{:S(2)}, u32[]{:S(2)}) collective-permute-start(bf16[128,1152]{1,0:T(8,128)(2,1)S(1)} %convert_element_type.39), channel_id=1, source_target_pairs={{0,32},{1,48},{16,481},{17,497},{32,64},{33,80},{48,1},{49,17},{64... | collective-permute-start | bytes 884744 | tf_op jit(solution)/shard_map/ppermute | solution.py:49
  12.9 19.1 %collective-permute-start.4 = (bf16[128,1152]{1,0:T(8,128)(2,1)S(1)}, bf16[128,1152]{1,0:T(8,128)(2,1)S(1)}, u32[]{:S(2)}, u32[]{:S(2)}) collective-permute-start(bf16[128,1152]{1,0:T(8,128)(2,1)S(1)} %bitcast.142), channel_id=1, source_target_pairs={{0,497},{1,481},{16,48},{17,32},{32,17},{33,1},{48,80},{49,64},{64... | collective-permute-start | bytes 884744 | tf_op jit(solution)/shard_map/ppermute | solution.py:49
  20.2 14.6 %collective-permute-start.8 = (bf16[128,1152]{1,0:T(8,128)(2,1)S(1)}, bf16[128,1152]{1,0:T(8,128)(2,1)S(1)}, u32[]{:S(2)}, u32[]{:S(2)}) collective-permute-start(bf16[128,1152]{1,0:T(8,128)(2,1)S(1)} %collective-permute-done.2), channel_id=1, source_target_pairs={{0,32},{1,481},{32,64},{33,1},{64,96},{65,33},{96,128},{97,65},{12... | collective-permute-start | bytes 884744 | tf_op jit(solution)/shard_map/ppermute | solution.py:28
  30.1 9.0 %collective-permute-start = (bf16[128,1152]{1,0:T(8,128)(2,1)S(1)}, bf16[128,1152]{1,0:T(8,128)(2,1)S(1)}, u32[]{:S(2)}, u32[]{:S(2)}) collective-permute-start(bf16[128,1152]{1,0:T(8,128)(2,1)S(1)} %convert_element_type.39), channel_id=1, source_target_pairs={{0,0},{1,16},{16,1},{17,17},{2,2},{3,18},{18,3},{19,19},{4,4},{5,2... | collective-permute-start | bytes 884744 | tf_op jit(solution)/shard_map/ppermute | solution.py:80
  32.1 9.0 %collective-permute-start.5 = (bf16[128,1152]{1,0:T(8,128)(2,1)S(1)}, bf16[128,1152]{1,0:T(8,128)(2,1)S(1)}, u32[]{:S(2)}, u32[]{:S(2)}) collective-permute-start(bf16[128,1152]{1,0:T(8,128)(2,1)S(1)} %collective-permute-done.4), channel_id=1, source_target_pairs={{0,32},{1,481},{32,64},{33,1},{64,96},{65,33},{96,128},{97,65},{12... | collective-permute-start | bytes 884744 | tf_op jit(solution)/shard_map/ppermute | solution.py:28
  34.8 8.8 %collective-permute-start.9 = (bf16[128,1152]{1,0:T(8,128)(2,1)S(1)}, bf16[128,1152]{1,0:T(8,128)(2,1)S(1)}, u32[]{:S(2)}, u32[]{:S(2)}) collective-permute-start(bf16[128,1152]{1,0:T(8,128)(2,1)S(1)} %collective-permute-done.8), channel_id=1, source_target_pairs={{0,32},{1,481},{32,64},{33,1},{64,96},{65,33},{96,128},{97,65},{12... | collective-permute-start | bytes 884744 | tf_op jit(solution)/shard_map/ppermute | solution.py:28
  39.2 55.3 %collective-permute-start.1 = (bf16[128,1152]{1,0:T(8,128)(2,1)S(1)}, bf16[128,1152]{1,0:T(8,128)(2,1)S(1)}, u32[]{:S(2)}, u32[]{:S(2)}) collective-permute-start(bf16[128,1152]{1,0:T(8,128)(2,1)S(1)} %collective-permute-done), channel_id=1, source_target_pairs={{0,1},{1,0},{2,3},{3,2},{4,5},{5,4},{6,7},{7,6},{8,9},{9,8},{10,11... | collective-permute-start | bytes 884744 | tf_op jit(solution)/shard_map/ppermute | solution.py:81
  41.1 7.8 %collective-permute-start.6 = (bf16[128,1152]{1,0:T(8,128)(2,1)S(1)}, bf16[128,1152]{1,0:T(8,128)(2,1)S(1)}, u32[]{:S(2)}, u32[]{:S(2)}) collective-permute-start(bf16[128,1152]{1,0:T(8,128)(2,1)S(1)} %collective-permute-done.5), channel_id=1, source_target_pairs={{0,32},{1,481},{32,64},{33,1},{64,96},{65,33},{96,128},{97,65},{12... | collective-permute-start | bytes 884744 | tf_op jit(solution)/shard_map/ppermute | solution.py:28
  43.6 8.7 %collective-permute-start.10 = (bf16[128,1152]{1,0:T(8,128)(2,1)S(1)}, bf16[128,1152]{1,0:T(8,128)(2,1)S(1)}, u32[]{:S(2)}, u32[]{:S(2)}) collective-permute-start(bf16[128,1152]{1,0:T(8,128)(2,1)S(1)} %collective-permute-done.9), channel_id=1, source_target_pairs={{0,32},{1,481},{32,64},{33,1},{64,96},{65,33},{96,128},{97,65},{12... | collective-permute-start | bytes 884744 | tf_op jit(solution)/shard_map/ppermute | solution.py:28
  48.9 9.8 %collective-permute-start.11 = (bf16[128,1152]{1,0:T(8,128)(2,1)S(1)}, bf16[128,1152]{1,0:T(8,128)(2,1)S(1)}, u32[]{:S(2)}, u32[]{:S(2)}) collective-permute-start(bf16[128,1152]{1,0:T(8,128)(2,1)S(1)} %collective-permute-done.6), channel_id=1, source_target_pairs={{0,32},{1,481},{32,64},{33,1},{64,96},{65,33},{96,128},{97,65},{12... | collective-permute-start | bytes 884744 | tf_op jit(solution)/shard_map/ppermute | solution.py:28
  52.3 11.3 %collective-permute-start.14 = (bf16[128,1152]{1,0:T(8,128)(2,1)S(1)}, bf16[128,1152]{1,0:T(8,128)(2,1)S(1)}, u32[]{:S(2)}, u32[]{:S(2)}) collective-permute-start(bf16[128,1152]{1,0:T(8,128)(2,1)S(1)} %collective-permute-done.10), channel_id=1, source_target_pairs={{0,32},{1,481},{32,64},{33,1},{64,96},{65,33},{96,128},{97,65},{12... | collective-permute-start | bytes 884744 | tf_op jit(solution)/shard_map/ppermute | solution.py:28
  56.4 29.1 %collective-permute-start.7 = (bf16[3,128,1152]{2,1,0:T(8,128)(2,1)S(1)}, bf16[3,128,1152]{2,1,0:T(8,128)(2,1)S(1)}, u32[]{:S(2)}, u32[]{:S(2)}) collective-permute-start(bf16[3,128,1152]{2,1,0:T(8,128)(2,1)S(1)} %pad_maximum_fusion.2), channel_id=1, source_target_pairs={{0,1},{1,0},{2,3},{3,2},{4,5},{5,4},{6,7},{7,6},{8,9},{9,8},{10,11... | collective-permute-start | bytes 2654216 | tf_op jit(solution)/shard_map/ppermute | solution.py:53
  58.7 8.5 %collective-permute-start.12 = (bf16[128,1152]{1,0:T(8,128)(2,1)S(1)}, bf16[128,1152]{1,0:T(8,128)(2,1)S(1)}, u32[]{:S(2)}, u32[]{:S(2)}) collective-permute-start(bf16[128,1152]{1,0:T(8,128)(2,1)S(1)} %collective-permute-done.11), channel_id=1, source_target_pairs={{0,32},{1,481},{32,64},{33,1},{64,96},{65,33},{96,128},{97,65},{12... | collective-permute-start | bytes 884744 | tf_op jit(solution)/shard_map/ppermute | solution.py:28
  63.6 8.7 %collective-permute-start.15 = (bf16[128,1152]{1,0:T(8,128)(2,1)S(1)}, bf16[128,1152]{1,0:T(8,128)(2,1)S(1)}, u32[]{:S(2)}, u32[]{:S(2)}) collective-permute-start(bf16[128,1152]{1,0:T(8,128)(2,1)S(1)} %collective-permute-done.14), channel_id=1, source_target_pairs={{0,32},{1,481},{32,64},{33,1},{64,96},{65,33},{96,128},{97,65},{12... | collective-permute-start | bytes 884744 | tf_op jit(solution)/shard_map/ppermute | solution.py:28
  67.2 11.0 %collective-permute-start.16 = (bf16[128,1152]{1,0:T(8,128)(2,1)S(1)}, bf16[128,1152]{1,0:T(8,128)(2,1)S(1)}, u32[]{:S(2)}, u32[]{:S(2)}) collective-permute-start(bf16[128,1152]{1,0:T(8,128)(2,1)S(1)} %collective-permute-done.12), channel_id=1, source_target_pairs={{0,32},{1,481},{32,64},{33,1},{64,96},{65,33},{96,128},{97,65},{12... | collective-permute-start | bytes 884744 | tf_op jit(solution)/shard_map/ppermute | solution.py:28
  72.3 10.8 %collective-permute-start.19 = (bf16[128,1152]{1,0:T(8,128)(2,1)S(1)}, bf16[128,1152]{1,0:T(8,128)(2,1)S(1)}, u32[]{:S(2)}, u32[]{:S(2)}) collective-permute-start(bf16[128,1152]{1,0:T(8,128)(2,1)S(1)} %collective-permute-done.15), channel_id=1, source_target_pairs={{0,32},{1,481},{32,64},{33,1},{64,96},{65,33},{96,128},{97,65},{12... | collective-permute-start | bytes 884744 | tf_op jit(solution)/shard_map/ppermute | solution.py:28
  75.5 17.2 %collective-permute-start.13 = (bf16[2,128,1152]{2,1,0:T(8,128)(2,1)S(1)}, bf16[2,128,1152]{2,1,0:T(8,128)(2,1)S(1)}, u32[]{:S(2)}, u32[]{:S(2)}) collective-permute-start(bf16[2,128,1152]{2,1,0:T(8,128)(2,1)S(1)} %pad_maximum_fusion.3), channel_id=1, source_target_pairs={{0,1},{1,0},{2,3},{3,2},{4,5},{5,4},{6,7},{7,6},{8,9},{9,8},{10,11... | collective-permute-start | bytes 1769480 | tf_op jit(solution)/shard_map/ppermute | solution.py:53
  78.2 8.5 %collective-permute-start.17 = (bf16[128,1152]{1,0:T(8,128)(2,1)S(1)}, bf16[128,1152]{1,0:T(8,128)(2,1)S(1)}, u32[]{:S(2)}, u32[]{:S(2)}) collective-permute-start(bf16[128,1152]{1,0:T(8,128)(2,1)S(1)} %collective-permute-done.16), channel_id=1, source_target_pairs={{0,32},{1,481},{32,64},{33,1},{64,96},{65,33},{96,128},{97,65},{12... | collective-permute-start | bytes 884744 | tf_op jit(solution)/shard_map/ppermute | solution.py:28
  83.1 11.4 %collective-permute-start.20 = (bf16[128,1152]{1,0:T(8,128)(2,1)S(1)}, bf16[128,1152]{1,0:T(8,128)(2,1)S(1)}, u32[]{:S(2)}, u32[]{:S(2)}) collective-permute-start(bf16[128,1152]{1,0:T(8,128)(2,1)S(1)} %collective-permute-done.19), channel_id=1, source_target_pairs={{0,32},{1,481},{32,64},{33,1},{64,96},{65,33},{96,128},{97,65},{12... | collective-permute-start | bytes 884744 | tf_op jit(solution)/shard_map/ppermute | solution.py:28
  86.8 7.5 %collective-permute-start.18 = (bf16[2,128,1152]{2,1,0:T(8,128)(2,1)S(1)}, bf16[2,128,1152]{2,1,0:T(8,128)(2,1)S(1)}, u32[]{:S(2)}, u32[]{:S(2)}) collective-permute-start(bf16[2,128,1152]{2,1,0:T(8,128)(2,1)S(1)} %pad_maximum_fusion.4), channel_id=1, source_target_pairs={{0,1},{1,0},{2,3},{3,2},{4,5},{5,4},{6,7},{7,6},{8,9},{9,8},{10,11... | collective-permute-start | bytes 1769480 | tf_op jit(solution)/shard_map/ppermute | solution.py:53
  94.5 2.2 %copy-start = (bf16[16,128,1152]{2,1,0:T(8,128)(2,1)}, bf16[16,128,1152]{2,1,0:T(8,128)(2,1)S(1)}, u32[]{:S(2)}) copy-start(bf16[16,128,1152]{2,1,0:T(8,128)(2,1)S(1)} %bitcast_dynamic-update-slice_fusion) | copy-start | bytes 14155780
  122.8 20.5 %all-to-all-start.1 = ((bf16[16,256,128]{2,1,0:T(8,128)(2,1)}), bf16[16,256,128]{2,1,0:T(8,128)(2,1)S(1)}, u32[]{:S(2)}, u32[]{:S(2)}) async-start(bf16[16,256,128]{2,1,0:T(8,128)(2,1)} %broadcast_in_dim.79), calls=%async_computation.1 | async-start | bytes 2097152 | tf_op jit(solution)/shard_map/all_to_all | solution.py:17
  143.4 45.5 %slice-start = ((s8[4718592]{0:T(1024)(128)(4,1)}), s8[4194304]{0:T(1024)(128)(4,1)S(1)}, s32[]{:S(2)}) async-start(s8[4718592]{0:T(1024)(128)(4,1)} %bitcast.123), calls=%async_computation.3 | async-start | bytes 8388608
  143.6 21.5 %collective-permute-start.24 = (bf16[4,4,256,128]{3,2,1,0:T(8,128)(2,1)S(1)}, bf16[4,4,256,128]{3,2,1,0:T(8,128)(2,1)S(1)}, u32[]{:S(2)}, u32[]{:S(2)}) collective-permute-start(bf16[4,4,256,128]{3,2,1,0:T(8,128)(2,1)S(1)} %pad_maximum_fusion.1), channel_id=1, source_target_pairs={{0,1},{1,0},{2,3},{3,2},{4,5},{5,4},{6,7},{7,6},{8,9},{9,8},{10,11... | collective-permute-start | bytes 3145736 | tf_op jit(solution)/shard_map/ppermute | solution.py:133
  151.1 11.4 %collective-permute-start.22 = (bf16[4,256,128]{2,1,0:T(8,128)(2,1)S(1)}, bf16[4,256,128]{2,1,0:T(8,128)(2,1)S(1)}, u32[]{:S(2)}, u32[]{:S(2)}) collective-permute-start(bf16[4,256,128]{2,1,0:T(8,128)(2,1)S(1)} %bitcast.130), channel_id=1, source_target_pairs={{0,32},{1,33},{32,64},{33,65},{64,96},{65,97},{96,128},{97,129},{1... | collective-permute-start | bytes 786440 | tf_op jit(solution)/shard_map/ppermute | solution.py:28
  153.1 11.9 %collective-permute-start.23 = (bf16[4,256,128]{2,1,0:T(8,128)(2,1)S(1)}, bf16[4,256,128]{2,1,0:T(8,128)(2,1)S(1)}, u32[]{:S(2)}, u32[]{:S(2)}) collective-permute-start(bf16[4,256,128]{2,1,0:T(8,128)(2,1)S(1)} %bitcast.131), channel_id=1, source_target_pairs={{0,448},{1,65},{32,480},{33,97},{64,0},{65,129},{96,32},{97,161},{... | collective-permute-start | bytes 786440 | tf_op jit(solution)/shard_map/ppermute | solution.py:28
  155.0 13.0 %collective-permute-start.21 = (bf16[4,256,128]{2,1,0:T(8,128)(2,1)S(1)}, bf16[4,256,128]{2,1,0:T(8,128)(2,1)S(1)}, u32[]{:S(2)}, u32[]{:S(2)}) collective-permute-start(bf16[4,256,128]{2,1,0:T(8,128)(2,1)S(1)} %bitcast.132), channel_id=1, source_target_pairs={{0,480},{1,481},{32,0},{33,1},{64,32},{65,33},{96,64},{97,65},{128... | collective-permute-start | bytes 786440 | tf_op jit(solution)/shard_map/ppermute | solution.py:28
  165.5 23.5 %slice-start.1 = ((s8[4718592]{0:T(1024)(128)(4,1)}), s8[524288]{0:T(1024)(128)(4,1)S(1)}, s32[]{:S(2)}) async-start(s8[4718592]{0:T(1024)(128)(4,1)} %bitcast.123), calls=%async_computation.4 | async-start | bytes 1048576
  189.8 11.1 %collective-permute-start.25 = (bf16[128,1152]{1,0:T(8,128)(2,1)S(1)}, bf16[128,1152]{1,0:T(8,128)(2,1)S(1)}, u32[]{:S(2)}, u32[]{:S(2)}) collective-permute-start(bf16[128,1152]{1,0:T(8,128)(2,1)S(1)} %fusion.2), channel_id=1, source_target_pairs={{0,0},{1,16},{16,1},{17,17},{2,2},{3,18},{18,3},{19,19},{4,4},{5,2... | collective-permute-start | bytes 884744 | tf_op jit(solution)/shard_map/ppermute | solution.py:147
  197.4 7.5 %collective-permute-start.26 = (bf16[128,1152]{1,0:T(8,128)(2,1)S(1)}, bf16[128,1152]{1,0:T(8,128)(2,1)S(1)}, u32[]{:S(2)}, u32[]{:S(2)}) collective-permute-start(bf16[128,1152]{1,0:T(8,128)(2,1)S(1)} %fusion.1), channel_id=1, source_target_pairs={{0,16},{1,0},{16,17},{17,1},{2,18},{3,2},{18,19},{19,3},{4,20},{5,... | collective-permute-start | bytes 884744 | tf_op jit(solution)/shard_map/ppermute | solution.py:145

commit v16 on v15

--- a/solution.py
+++ b/solution.py
@@ -17,19 +17,19 @@
     return lax.all_to_all(copies, PLANE, 0, 0)
 
 
-def along(piece, shift, shift_of_core_1=None):
+def along(piece, shift, shift_of_core_1=None, cores=(0, 1)):
     size = lax.axis_size(LINE)
     shifts = (shift, shift if shift_of_core_1 is None else shift_of_core_1)
     pairs = [
         (2 * place + core, 2 * ((place + shifts[core]) % size) + core)
         for place in range(size)
-        for core in range(2)
+        for core in cores
     ]
     return lax.ppermute(piece, LINE + ("core",), pairs)
 
 
-def onward(piece):
-    return along(piece, 1, -1)
+def onward(piece, cores=(0, 1)):
+    return along(piece, 1, -1, cores)
 
 
 def launch(piece, side):
@@ -84,14 +84,17 @@
     for step in range(2, slabs // 2):
         near.append(onward(near[-1]))
         far.append(onward(far[-1]))
-    near.append(onward(near[-1]))
-    back = [None] + swap(far[1:4]) + swap(far[4:6]) + swap(far[6:])
-    slab, toward = lax.axis_index(LINE), 1 - 2 * lax.axis_index("core")
+    near_last, far_last = onward(near[-1], (1,)), onward(far[-1], (1,))
+    back = [None] + swap(far[1:4]) + swap(far[4:6]) + swap(far[6:] + [far_last])
+    slab, core = lax.axis_index(LINE), lax.axis_index("core")
     half = jnp.zeros((slabs, rows, cols), jnp.bfloat16)
-    for step in range(slabs // 2 + 1):
-        half = put(half, near[step], (slab - step * toward) % slabs)
-        if 0 < step < slabs // 2:
-            half = put(half, back[step], (slab + step * toward) % slabs)
+    half = put(half, own, slab)
+    for step in range(1, slabs // 2):
+        ahead = step * (1 - 2 * core)
+        half = put(half, near[step], (slab - ahead) % slabs)
+        half = put(half, back[step], (slab + ahead) % slabs)
+    last = jnp.where(core == 0, back[-1], near_last)
+    half = put(half, last, (slab + slabs // 2) % slabs)
     partial_gram = lax.dot_general(
         jnp.concatenate([own, other], 0),
         half,
@@ -100,8 +103,8 @@
     )
     partial_gram = partial_gram.transpose(1, 0, 2).astype(jnp.bfloat16)
     wide = own.astype(jnp.float32)
-    extra = jnp.pad(split((wide * wide).sum(1)), ((0, 13), (0, 0)))
-    extra = jnp.broadcast_to(extra.astype(jnp.bfloat16)[None], (chips, 16, rows))
+    extra = jnp.pad(split((wide * wide).sum(1)), ((0, 5), (0, 0)))
+    extra = jnp.broadcast_to(extra.astype(jnp.bfloat16)[None], (chips, 8, rows))
     partial_gram = jnp.concatenate([partial_gram, extra], 1)
     met = lax.axis_index(PLANE) == lax.axis_index(LINE)
     residue = lax.axis_index("zl")

time: 207 us -> 215 us (1.039)
  waiting for transfers between devices: 18.4 us -> 25.2 us
  blocking collectives: 61.7 us -> 64.4 us
    ppermute x16 -> x17, waiting for transfers between devices: 9.87 us -> 15.7 us  [along(): return lax.ppermute(piece, LINE + ('core',), pairs)]
    ppermute x16 -> x17, starting transfers between devices: 61.3 us -> 66.7 us  [along(): return lax.ppermute(piece, LINE + ('core',), pairs)]
    ppermute x4, starting transfers between devices: 19.6 us -> 15.6 us  [swap(): return list(lax.ppermute(jnp.stack(pieces), 'core', SWAP))]
    all_to_all x1, blocking collectives: 20.3 us -> 22.6 us  [share(): return lax.all_to_all(copies, PLANE, 0, 0)]
  transfers between devices with their start and end apart: 28 -> 29, of which waited for: 10 -> 11; matrix products, arithmetic and copies ran while one was open for 2% -> 2% of each run, Pallas kernels for 0% -> 0%
where the time goes in v16:
time: 215 us; the launch traced here: 214 us
  starting transfers between devices  111 us (52%)
  blocking collectives  64.4 us (30%)
  waiting for transfers between devices  25.2 us (12%)
  matrix products  5.02 us (2%)
  other arithmetic  4.06 us (2%)
  local copies, waits for them, and re-layouts  3.33 us (2%)
    ppermute x17, starting transfers between devices, along(): return lax.ppermute(piece, LINE + ('core',), pairs)  66.7 us
    all_to_all x1, blocking collectives, per_device(): summands = lax.all_to_all(partial_gram, PLANE, 0, 0)  24.7 us
    all_to_all x1, blocking collectives, share(): return lax.all_to_all(copies, PLANE, 0, 0)  22.6 us
    all_gather x1, blocking collectives, per_device(): here = lax.all_gather(gram_low, 'zh', axis=0)  17.1 us
    ppermute x17, waiting for transfers between devices, along(): return lax.ppermute(piece, LINE + ('core',), pairs)  15.7 us
    ppermute x4, starting transfers between devices, swap(): return list(lax.ppermute(jnp.stack(pieces), 'core', SWAP))  15.6 us
    ppermute x2, starting transfers between devices, launch(): return lax.ppermute(piece, LINE + ('ylo', 'core'), pairs)  7.67 us
    ppermute x1, starting transfers between devices, per_device(): left_other = lax.ppermute(jnp.stack(left_own), 'core', SWAP)  6.3 us
  transfers between devices with their start and end apart: 29, of which 11 were waited for; matrix products, arithmetic and copies ran while one was open for 2% of the time, Pallas kernels for 0%

profile of v16, /device:TPU:1, one launch (start us, length us, event | category | flops | bytes accessed | tf_op | source)
XLA Modules:
  0.0 213.6 jit_solution(15684109523318969698)
XLA Ops:
  0.0 1.1 convert_bitcast_fusion
  1.1 8.8 %collective-permute-start.3 = (bf16[1,128,1152]{2,1,0:T(8,128)(2,1)S(1)}, bf16[1,128,1152]{2,1,0:T(8,128)(2,1)S(1)}, u32[]{:S(2)}, u32[]{:S(2)}) collective-permute-start(bf16[1,128,1152]{2,1,0:T(8,128)(2,1)S(1)} %convert_bitcast_fusion), channel_id=1, source_target_pairs={{0,1},{1,0},{2,3},{3,2},{4,5},{5,4},{6,7},{7,6},{8,9},{9,8},{10,11... | collective-permute-start | bytes 884744 | tf_op jit(solution)/shard_map/ppermute | solution.py:53
  9.9 1.1 convert_element_type.39
  11.0 1.9 collective-permute-start.2
  12.9 5.7 %collective-permute-start.4 = (bf16[128,1152]{1,0:T(8,128)(2,1)S(1)}, bf16[128,1152]{1,0:T(8,128)(2,1)S(1)}, u32[]{:S(2)}, u32[]{:S(2)}) collective-permute-start(bf16[128,1152]{1,0:T(8,128)(2,1)S(1)} %bitcast.154), channel_id=1, source_target_pairs={{0,497},{1,481},{16,48},{17,32},{32,17},{33,1},{48,80},{49,64},{64... | collective-permute-start | bytes 884744 | tf_op jit(solution)/shard_map/ppermute | solution.py:49
  18.7 1.5 collective-permute-done.2
  20.2 9.9 %collective-permute-start.8 = (bf16[128,1152]{1,0:T(8,128)(2,1)S(1)}, bf16[128,1152]{1,0:T(8,128)(2,1)S(1)}, u32[]{:S(2)}, u32[]{:S(2)}) collective-permute-start(bf16[128,1152]{1,0:T(8,128)(2,1)S(1)} %collective-permute-done.2), channel_id=1, source_target_pairs={{0,32},{1,481},{32,64},{33,1},{64,96},{65,33},{96,128},{97,65},{12... | collective-permute-start | bytes 884744 | tf_op jit(solution)/shard_map/ppermute | solution.py:28
  30.1 1.9 collective-permute-start
  32.1 2.7 %collective-permute-start.5 = (bf16[128,1152]{1,0:T(8,128)(2,1)S(1)}, bf16[128,1152]{1,0:T(8,128)(2,1)S(1)}, u32[]{:S(2)}, u32[]{:S(2)}) collective-permute-start(bf16[128,1152]{1,0:T(8,128)(2,1)S(1)} %collective-permute-done.4), channel_id=1, source_target_pairs={{0,32},{1,481},{32,64},{33,1},{64,96},{65,33},{96,128},{97,65},{12... | collective-permute-start | bytes 884744 | tf_op jit(solution)/shard_map/ppermute | solution.py:28
  34.8 4.0 %collective-permute-start.9 = (bf16[128,1152]{1,0:T(8,128)(2,1)S(1)}, bf16[128,1152]{1,0:T(8,128)(2,1)S(1)}, u32[]{:S(2)}, u32[]{:S(2)}) collective-permute-start(bf16[128,1152]{1,0:T(8,128)(2,1)S(1)} %collective-permute-done.8), channel_id=1, source_target_pairs={{0,32},{1,481},{32,64},{33,1},{64,96},{65,33},{96,128},{97,65},{12... | collective-permute-start | bytes 884744 | tf_op jit(solution)/shard_map/ppermute | solution.py:28
  39.2 1.9 collective-permute-start.1
  41.1 2.5 %collective-permute-start.6 = (bf16[128,1152]{1,0:T(8,128)(2,1)S(1)}, bf16[128,1152]{1,0:T(8,128)(2,1)S(1)}, u32[]{:S(2)}, u32[]{:S(2)}) collective-permute-start(bf16[128,1152]{1,0:T(8,128)(2,1)S(1)} %collective-permute-done.5), channel_id=1, source_target_pairs={{0,32},{1,481},{32,64},{33,1},{64,96},{65,33},{96,128},{97,65},{12... | collective-permute-start | bytes 884744 | tf_op jit(solution)/shard_map/ppermute | solution.py:28
  43.6 3.9 %collective-permute-start.10 = (bf16[128,1152]{1,0:T(8,128)(2,1)S(1)}, bf16[128,1152]{1,0:T(8,128)(2,1)S(1)}, u32[]{:S(2)}, u32[]{:S(2)}) collective-permute-start(bf16[128,1152]{1,0:T(8,128)(2,1)S(1)} %collective-permute-done.9), channel_id=1, source_target_pairs={{0,32},{1,481},{32,64},{33,1},{64,96},{65,33},{96,128},{97,65},{12... | collective-permute-start | bytes 884744 | tf_op jit(solution)/shard_map/ppermute | solution.py:28
  47.5 0.6 broadcast_in_dim.67
  48.2 0.7 collective-permute-done.6
  48.9 3.4 %collective-permute-start.11 = (bf16[128,1152]{1,0:T(8,128)(2,1)S(1)}, bf16[128,1152]{1,0:T(8,128)(2,1)S(1)}, u32[]{:S(2)}, u32[]{:S(2)}) collective-permute-start(bf16[128,1152]{1,0:T(8,128)(2,1)S(1)} %collective-permute-done.6), channel_id=1, source_target_pairs={{0,32},{1,481},{32,64},{33,1},{64,96},{65,33},{96,128},{97,65},{12... | collective-permute-start | bytes 884744 | tf_op jit(solution)/shard_map/ppermute | solution.py:28
  52.3 3.9 %collective-permute-start.14 = (bf16[128,1152]{1,0:T(8,128)(2,1)S(1)}, bf16[128,1152]{1,0:T(8,128)(2,1)S(1)}, u32[]{:S(2)}, u32[]{:S(2)}) collective-permute-start(bf16[128,1152]{1,0:T(8,128)(2,1)S(1)} %collective-permute-done.10), channel_id=1, source_target_pairs={{0,32},{1,481},{32,64},{33,1},{64,96},{65,33},{96,128},{97,65},{12... | collective-permute-start | bytes 884744 | tf_op jit(solution)/shard_map/ppermute | solution.py:28
  56.1 0.1 multiply_reduce_fusion
  56.4 2.3 %collective-permute-start.7 = (bf16[3,128,1152]{2,1,0:T(8,128)(2,1)S(1)}, bf16[3,128,1152]{2,1,0:T(8,128)(2,1)S(1)}, u32[]{:S(2)}, u32[]{:S(2)}) collective-permute-start(bf16[3,128,1152]{2,1,0:T(8,128)(2,1)S(1)} %pad_maximum_fusion.2), channel_id=1, source_target_pairs={{0,1},{1,0},{2,3},{3,2},{4,5},{5,4},{6,7},{7,6},{8,9},{9,8},{10,11... | collective-permute-start | bytes 2654216 | tf_op jit(solution)/shard_map/ppermute | solution.py:53
  58.7 4.9 %collective-permute-start.12 = (bf16[128,1152]{1,0:T(8,128)(2,1)S(1)}, bf16[128,1152]{1,0:T(8,128)(2,1)S(1)}, u32[]{:S(2)}, u32[]{:S(2)}) collective-permute-start(bf16[128,1152]{1,0:T(8,128)(2,1)S(1)} %collective-permute-done.11), channel_id=1, source_target_pairs={{0,32},{1,481},{32,64},{33,1},{64,96},{65,33},{96,128},{97,65},{12... | collective-permute-start | bytes 884744 | tf_op jit(solution)/shard_map/ppermute | solution.py:28
  63.6 2.4 %collective-permute-start.15 = (bf16[128,1152]{1,0:T(8,128)(2,1)S(1)}, bf16[128,1152]{1,0:T(8,128)(2,1)S(1)}, u32[]{:S(2)}, u32[]{:S(2)}) collective-permute-start(bf16[128,1152]{1,0:T(8,128)(2,1)S(1)} %collective-permute-done.14), channel_id=1, source_target_pairs={{0,32},{1,481},{32,64},{33,1},{64,96},{65,33},{96,128},{97,65},{12... | collective-permute-start | bytes 884744 | tf_op jit(solution)/shard_map/ppermute | solution.py:28
  66.0 1.2 collective-permute-done.12
  67.2 5.0 %collective-permute-start.16 = (bf16[128,1152]{1,0:T(8,128)(2,1)S(1)}, bf16[128,1152]{1,0:T(8,128)(2,1)S(1)}, u32[]{:S(2)}, u32[]{:S(2)}) collective-permute-start(bf16[128,1152]{1,0:T(8,128)(2,1)S(1)} %collective-permute-done.12), channel_id=1, source_target_pairs={{0,32},{1,481},{32,64},{33,1},{64,96},{65,33},{96,128},{97,65},{12... | collective-permute-start | bytes 884744 | tf_op jit(solution)/shard_map/ppermute | solution.py:28
  72.2 3.1 %collective-permute-start.20 = (bf16[128,1152]{1,0:T(8,128)(2,1)S(1)}, bf16[128,1152]{1,0:T(8,128)(2,1)S(1)}, u32[]{:S(2)}, u32[]{:S(2)}) collective-permute-start(bf16[128,1152]{1,0:T(8,128)(2,1)S(1)} %collective-permute-done.15), channel_id=1, source_target_pairs={{0,32},{1,481},{32,64},{33,1},{64,96},{65,33},{96,128},{97,65},{12... | collective-permute-start | bytes 884744 | tf_op jit(solution)/shard_map/ppermute | solution.py:28
  75.5 2.7 %collective-permute-start.13 = (bf16[2,128,1152]{2,1,0:T(8,128)(2,1)S(1)}, bf16[2,128,1152]{2,1,0:T(8,128)(2,1)S(1)}, u32[]{:S(2)}, u32[]{:S(2)}) collective-permute-start(bf16[2,128,1152]{2,1,0:T(8,128)(2,1)S(1)} %pad_maximum_fusion.4), channel_id=1, source_target_pairs={{0,1},{1,0},{2,3},{3,2},{4,5},{5,4},{6,7},{7,6},{8,9},{9,8},{10,11... | collective-permute-start | bytes 1769480 | tf_op jit(solution)/shard_map/ppermute | solution.py:53
  78.2 4.9 %collective-permute-start.17 = (bf16[128,1152]{1,0:T(8,128)(2,1)S(1)}, bf16[128,1152]{1,0:T(8,128)(2,1)S(1)}, u32[]{:S(2)}, u32[]{:S(2)}) collective-permute-start(bf16[128,1152]{1,0:T(8,128)(2,1)S(1)} %collective-permute-done.16), channel_id=1, source_target_pairs={{0,32},{1,481},{32,64},{33,1},{64,96},{65,33},{96,128},{97,65},{12... | collective-permute-start | bytes 884744 | tf_op jit(solution)/shard_map/ppermute | solution.py:28
  83.1 2.4 %collective-permute-start.21 = (bf16[128,1152]{1,0:T(8,128)(2,1)S(1)}, bf16[128,1152]{1,0:T(8,128)(2,1)S(1)}, u32[]{:S(2)}, u32[]{:S(2)}) collective-permute-start(bf16[128,1152]{1,0:T(8,128)(2,1)S(1)} %collective-permute-done.20), channel_id=1, source_target_pairs={{1,481},{33,1},{65,33},{97,65},{129,97},{161,129},{193,161},{225,1... | collective-permute-start | bytes 884744 | tf_op jit(solution)/shard_map/ppermute | solution.py:28
  85.7 0.9 collective-permute-done.17
  86.7 5.0 %collective-permute-start.18 = (bf16[128,1152]{1,0:T(8,128)(2,1)S(1)}, bf16[128,1152]{1,0:T(8,128)(2,1)S(1)}, u32[]{:S(2)}, u32[]{:S(2)}) collective-permute-start(bf16[128,1152]{1,0:T(8,128)(2,1)S(1)} %collective-permute-done.17), channel_id=1, source_target_pairs={{1,481},{33,1},{65,33},{97,65},{129,97},{161,129},{193,161},{225,1... | collective-permute-start | bytes 884744 | tf_op jit(solution)/shard_map/ppermute | solution.py:28
  91.8 3.5 %collective-permute-done.18 = bf16[128,1152]{1,0:T(8,128)(2,1)S(1)} collective-permute-done((bf16[128,1152]{1,0:T(8,128)(2,1)S(1)}, bf16[128,1152]{1,0:T(8,128)(2,1)S(1)}, u32[]{:S(2)}, u32[]{:S(2)}) %collective-permute-start.18) | collective-permute-done | bytes 294944 | tf_op jit(solution)/shard_map/ppermute | solution.py:28
  95.5 1.9 collective-permute-start.19
  97.5 2.3 %collective-permute-done.19 = bf16[3,128,1152]{2,1,0:T(8,128)(2,1)S(1)} collective-permute-done((bf16[3,128,1152]{2,1,0:T(8,128)(2,1)S(1)}, bf16[3,128,1152]{2,1,0:T(8,128)(2,1)S(1)}, u32[]{:S(2)}, u32[]{:S(2)}) %collective-permute-start.19) | collective-permute-done | bytes 884768 | tf_op jit(solution)/shard_map/ppermute | solution.py:53
  100.0 1.6 fusion.3
  101.6 0.5 copy-done
  102.3 24.7 %all_to_all.15 = bf16[16,264,128]{2,1,0:T(8,128)(2,1)S(1)} all-to-all(bf16[16,264,128]{2,1,0:T(8,128)(2,1)S(1)} %pad_maximum_fusion), channel_id=1, replica_groups=mesh['zh'=4,'zl'=4,'ylo'=2,'x'=4,'yhi'=2,'core'=2] {'ylo','x','yhi'}, dimensions={0} | all-to-all | bytes 2162688 | tf_op jit(solution)/shard_map/all_to_all | solution.py:112
  126.9 0.1 convert_reduce_fusion
  127.1 1.2 broadcast_in_dim.79
  128.4 3.7 %all-to-all-start.1 = ((bf16[16,256,128]{2,1,0:T(8,128)(2,1)}), bf16[16,256,128]{2,1,0:T(8,128)(2,1)S(1)}, u32[]{:S(2)}, u32[]{:S(2)}) async-start(bf16[16,256,128]{2,1,0:T(8,128)(2,1)} %broadcast_in_dim.79), calls=%async_computation.1 | async-start | bytes 2097152 | tf_op jit(solution)/shard_map/all_to_all | solution.py:17
  132.1 17.1 %all-gather = bf16[1024,128]{1,0:T(8,128)(2,1)S(1)} all-gather(bf16[256,128]{1,0:T(8,128)(2,1)S(1)} %fusion.50), channel_id=2, replica_groups=mesh['zh'=4,'zl'=4,'ylo'=2,'x'=4,'yhi'=2,'core'=2] {'zh'}, dimensions={0}, use_global_device_ids=true | all-gather | bytes 327680 | tf_op jit(solution)/shard_map/all_gather | solution.py:124
  149.3 0.1 pad_maximum_fusion.1
  149.4 6.3 %collective-permute-start.25 = (bf16[4,4,256,128]{3,2,1,0:T(8,128)(2,1)S(1)}, bf16[4,4,256,128]{3,2,1,0:T(8,128)(2,1)S(1)}, u32[]{:S(2)}, u32[]{:S(2)}) collective-permute-start(bf16[4,4,256,128]{3,2,1,0:T(8,128)(2,1)S(1)} %pad_maximum_fusion.1), channel_id=1, source_target_pairs={{0,1},{1,0},{2,3},{3,2},{4,5},{5,4},{6,7},{7,6},{8,9},{9,8},{10,11... | collective-permute-start | bytes 3145736 | tf_op jit(solution)/shard_map/ppermute | solution.py:136
  155.7 1.9 collective-permute-start.23
  157.7 4.7 %collective-permute-start.24 = (bf16[4,256,128]{2,1,0:T(8,128)(2,1)S(1)}, bf16[4,256,128]{2,1,0:T(8,128)(2,1)S(1)}, u32[]{:S(2)}, u32[]{:S(2)}) collective-permute-start(bf16[4,256,128]{2,1,0:T(8,128)(2,1)S(1)} %bitcast.142), channel_id=1, source_target_pairs={{0,448},{1,65},{32,480},{33,97},{64,0},{65,129},{96,32},{97,161},{... | collective-permute-start | bytes 786440 | tf_op jit(solution)/shard_map/ppermute | solution.py:28
  162.4 2.2 %collective-permute-start.22 = (bf16[4,256,128]{2,1,0:T(8,128)(2,1)S(1)}, bf16[4,256,128]{2,1,0:T(8,128)(2,1)S(1)}, u32[]{:S(2)}, u32[]{:S(2)}) collective-permute-start(bf16[4,256,128]{2,1,0:T(8,128)(2,1)S(1)} %bitcast.143), channel_id=1, source_target_pairs={{0,480},{1,481},{32,0},{33,1},{64,32},{65,33},{96,64},{97,65},{128... | collective-permute-start | bytes 786440 | tf_op jit(solution)/shard_map/ppermute | solution.py:28
  164.6 0.2 convolution_bitcast_fusion.9
  164.8 2.6 %collective-permute-done.23 = bf16[4,256,128]{2,1,0:T(8,128)(2,1)S(1)} collective-permute-done((bf16[4,256,128]{2,1,0:T(8,128)(2,1)S(1)}, bf16[4,256,128]{2,1,0:T(8,128)(2,1)S(1)}, u32[]{:S(2)}, u32[]{:S(2)}) %collective-permute-start.23) | collective-permute-done | bytes 262176 | tf_op jit(solution)/shard_map/ppermute | solution.py:28
  167.4 0.2 convolution_bitcast_fusion.7
  167.6 6.5 %collective-permute-done.24 = bf16[4,256,128]{2,1,0:T(8,128)(2,1)S(1)} collective-permute-done((bf16[4,256,128]{2,1,0:T(8,128)(2,1)S(1)}, bf16[4,256,128]{2,1,0:T(8,128)(2,1)S(1)}, u32[]{:S(2)}, u32[]{:S(2)}) %collective-permute-start.24) | collective-permute-done | bytes 262176 | tf_op jit(solution)/shard_map/ppermute | solution.py:28
  174.1 0.2 convolution_bitcast_fusion.6
  174.4 0.2 convolution_bitcast_fusion.5
  174.6 0.2 convolution_bitcast_fusion.2
  174.9 0.2 convolution_bitcast_fusion.3
  175.1 0.3 collective-permute-done.22
  175.4 0.2 convolution_bitcast_fusion.4
  175.6 0.2 fusion.13
  175.8 0.2 broadcast_in_dim.81
  176.0 22.6 %all_to_all.16 = bf16[16,256,128]{2,1,0:T(8,128)(2,1)S(1)} all-to-all(bf16[16,256,128]{2,1,0:T(8,128)(2,1)S(1)} %broadcast_in_dim.81), channel_id=1, replica_groups=mesh['zh'=4,'zl'=4,'ylo'=2,'x'=4,'yhi'=2,'core'=2] {'ylo','x','yhi'}, dimensions={0} | all-to-all | bytes 2097152 | tf_op jit(solution)/shard_map/all_to_all | solution.py:17
  198.6 0.9 fusion.2
  199.5 4.8 %collective-permute-start.26 = (bf16[128,1152]{1,0:T(8,128)(2,1)S(1)}, bf16[128,1152]{1,0:T(8,128)(2,1)S(1)}, u32[]{:S(2)}, u32[]{:S(2)}) collective-permute-start(bf16[128,1152]{1,0:T(8,128)(2,1)S(1)} %fusion.2), channel_id=1, source_target_pairs={{0,0},{1,16},{16,1},{17,17},{2,2},{3,18},{18,3},{19,19},{4,4},{5,2... | collective-permute-start | bytes 884744 | tf_op jit(solution)/shard_map/ppermute | solution.py:150
  204.3 0.9 fusion.1
  205.2 1.9 collective-permute-start.27
  207.1 1.6 collective-permute-done.26
  208.7 3.9 %collective-permute-done.27 = bf16[128,1152]{1,0:T(8,128)(2,1)S(1)} collective-permute-done((bf16[128,1152]{1,0:T(8,128)(2,1)S(1)}, bf16[128,1152]{1,0:T(8,128)(2,1)S(1)}, u32[]{:S(2)}, u32[]{:S(2)}) %collective-permute-start.27) | collective-permute-done | bytes 294944 | tf_op jit(solution)/shard_map/ppermute | solution.py:148
  212.7 0.9 convert_add_fusion
  (52 shorter events, 1.4 us)
Async XLA Ops:
  1.1 11.8 %collective-permute-start.3 = (bf16[1,128,1152]{2,1,0:T(8,128)(2,1)S(1)}, bf16[1,128,1152]{2,1,0:T(8,128)(2,1)S(1)}, u32[]{:S(2)}, u32[]{:S(2)}) collective-permute-start(bf16[1,128,1152]{2,1,0:T(8,128)(2,1)S(1)} %convert_bitcast_fusion), channel_id=1, source_target_pairs={{0,1},{1,0},{2,3},{3,2},{4,5},{5,4},{6,7},{7,6},{8,9},{9,8},{10,11... | collective-permute-start | bytes 884744 | tf_op jit(solution)/shard_map/ppermute | solution.py:53
  11.0 9.2 %collective-permute-start.2 = (bf16[128,1152]{1,0:T(8,128)(2,1)S(1)}, bf16[128,1152]{1,0:T(8,128)(2,1)S(1)}, u32[]{:S(2)}, u32[]{:S(2)}) collective-permute-start(bf16[128,1152]{1,0:T(8,128)(2,1)S(1)} %convert_element_type.39), channel_id=1, source_target_pairs={{0,32},{1,48},{16,481},{17,497},{32,64},{33,80},{48,1},{49,17},{64... | collective-permute-start | bytes 884744 | tf_op jit(solution)/shard_map/ppermute | solution.py:49
  12.9 19.1 %collective-permute-start.4 = (bf16[128,1152]{1,0:T(8,128)(2,1)S(1)}, bf16[128,1152]{1,0:T(8,128)(2,1)S(1)}, u32[]{:S(2)}, u32[]{:S(2)}) collective-permute-start(bf16[128,1152]{1,0:T(8,128)(2,1)S(1)} %bitcast.154), channel_id=1, source_target_pairs={{0,497},{1,481},{16,48},{17,32},{32,17},{33,1},{48,80},{49,64},{64... | collective-permute-start | bytes 884744 | tf_op jit(solution)/shard_map/ppermute | solution.py:49
  20.2 14.6 %collective-permute-start.8 = (bf16[128,1152]{1,0:T(8,128)(2,1)S(1)}, bf16[128,1152]{1,0:T(8,128)(2,1)S(1)}, u32[]{:S(2)}, u32[]{:S(2)}) collective-permute-start(bf16[128,1152]{1,0:T(8,128)(2,1)S(1)} %collective-permute-done.2), channel_id=1, source_target_pairs={{0,32},{1,481},{32,64},{33,1},{64,96},{65,33},{96,128},{97,65},{12... | collective-permute-start | bytes 884744 | tf_op jit(solution)/shard_map/ppermute | solution.py:28
  30.1 9.0 %collective-permute-start = (bf16[128,1152]{1,0:T(8,128)(2,1)S(1)}, bf16[128,1152]{1,0:T(8,128)(2,1)S(1)}, u32[]{:S(2)}, u32[]{:S(2)}) collective-permute-start(bf16[128,1152]{1,0:T(8,128)(2,1)S(1)} %convert_element_type.39), channel_id=1, source_target_pairs={{0,0},{1,16},{16,1},{17,17},{2,2},{3,18},{18,3},{19,19},{4,4},{5,2... | collective-permute-start | bytes 884744 | tf_op jit(solution)/shard_map/ppermute | solution.py:80
  32.1 9.0 %collective-permute-start.5 = (bf16[128,1152]{1,0:T(8,128)(2,1)S(1)}, bf16[128,1152]{1,0:T(8,128)(2,1)S(1)}, u32[]{:S(2)}, u32[]{:S(2)}) collective-permute-start(bf16[128,1152]{1,0:T(8,128)(2,1)S(1)} %collective-permute-done.4), channel_id=1, source_target_pairs={{0,32},{1,481},{32,64},{33,1},{64,96},{65,33},{96,128},{97,65},{12... | collective-permute-start | bytes 884744 | tf_op jit(solution)/shard_map/ppermute | solution.py:28
  34.8 8.7 %collective-permute-start.9 = (bf16[128,1152]{1,0:T(8,128)(2,1)S(1)}, bf16[128,1152]{1,0:T(8,128)(2,1)S(1)}, u32[]{:S(2)}, u32[]{:S(2)}) collective-permute-start(bf16[128,1152]{1,0:T(8,128)(2,1)S(1)} %collective-permute-done.8), channel_id=1, source_target_pairs={{0,32},{1,481},{32,64},{33,1},{64,96},{65,33},{96,128},{97,65},{12... | collective-permute-start | bytes 884744 | tf_op jit(solution)/shard_map/ppermute | solution.py:28
  39.2 60.9 %collective-permute-start.1 = (bf16[128,1152]{1,0:T(8,128)(2,1)S(1)}, bf16[128,1152]{1,0:T(8,128)(2,1)S(1)}, u32[]{:S(2)}, u32[]{:S(2)}) collective-permute-start(bf16[128,1152]{1,0:T(8,128)(2,1)S(1)} %collective-permute-done), channel_id=1, source_target_pairs={{0,1},{1,0},{2,3},{3,2},{4,5},{5,4},{6,7},{7,6},{8,9},{9,8},{10,11... | collective-permute-start | bytes 884744 | tf_op jit(solution)/shard_map/ppermute | solution.py:81
  41.1 7.8 %collective-permute-start.6 = (bf16[128,1152]{1,0:T(8,128)(2,1)S(1)}, bf16[128,1152]{1,0:T(8,128)(2,1)S(1)}, u32[]{:S(2)}, u32[]{:S(2)}) collective-permute-start(bf16[128,1152]{1,0:T(8,128)(2,1)S(1)} %collective-permute-done.5), channel_id=1, source_target_pairs={{0,32},{1,481},{32,64},{33,1},{64,96},{65,33},{96,128},{97,65},{12... | collective-permute-start | bytes 884744 | tf_op jit(solution)/shard_map/ppermute | solution.py:28
  43.6 8.7 %collective-permute-start.10 = (bf16[128,1152]{1,0:T(8,128)(2,1)S(1)}, bf16[128,1152]{1,0:T(8,128)(2,1)S(1)}, u32[]{:S(2)}, u32[]{:S(2)}) collective-permute-start(bf16[128,1152]{1,0:T(8,128)(2,1)S(1)} %collective-permute-done.9), channel_id=1, source_target_pairs={{0,32},{1,481},{32,64},{33,1},{64,96},{65,33},{96,128},{97,65},{12... | collective-permute-start | bytes 884744 | tf_op jit(solution)/shard_map/ppermute | solution.py:28
  48.9 9.8 %collective-permute-start.11 = (bf16[128,1152]{1,0:T(8,128)(2,1)S(1)}, bf16[128,1152]{1,0:T(8,128)(2,1)S(1)}, u32[]{:S(2)}, u32[]{:S(2)}) collective-permute-start(bf16[128,1152]{1,0:T(8,128)(2,1)S(1)} %collective-permute-done.6), channel_id=1, source_target_pairs={{0,32},{1,481},{32,64},{33,1},{64,96},{65,33},{96,128},{97,65},{12... | collective-permute-start | bytes 884744 | tf_op jit(solution)/shard_map/ppermute | solution.py:28
  52.3 11.3 %collective-permute-start.14 = (bf16[128,1152]{1,0:T(8,128)(2,1)S(1)}, bf16[128,1152]{1,0:T(8,128)(2,1)S(1)}, u32[]{:S(2)}, u32[]{:S(2)}) collective-permute-start(bf16[128,1152]{1,0:T(8,128)(2,1)S(1)} %collective-permute-done.10), channel_id=1, source_target_pairs={{0,32},{1,481},{32,64},{33,1},{64,96},{65,33},{96,128},{97,65},{12... | collective-permute-start | bytes 884744 | tf_op jit(solution)/shard_map/ppermute | solution.py:28
  56.4 29.1 %collective-permute-start.7 = (bf16[3,128,1152]{2,1,0:T(8,128)(2,1)S(1)}, bf16[3,128,1152]{2,1,0:T(8,128)(2,1)S(1)}, u32[]{:S(2)}, u32[]{:S(2)}) collective-permute-start(bf16[3,128,1152]{2,1,0:T(8,128)(2,1)S(1)} %pad_maximum_fusion.2), channel_id=1, source_target_pairs={{0,1},{1,0},{2,3},{3,2},{4,5},{5,4},{6,7},{7,6},{8,9},{9,8},{10,11... | collective-permute-start | bytes 2654216 | tf_op jit(solution)/shard_map/ppermute | solution.py:53
  58.7 8.5 %collective-permute-start.12 = (bf16[128,1152]{1,0:T(8,128)(2,1)S(1)}, bf16[128,1152]{1,0:T(8,128)(2,1)S(1)}, u32[]{:S(2)}, u32[]{:S(2)}) collective-permute-start(bf16[128,1152]{1,0:T(8,128)(2,1)S(1)} %collective-permute-done.11), channel_id=1, source_target_pairs={{0,32},{1,481},{32,64},{33,1},{64,96},{65,33},{96,128},{97,65},{12... | collective-permute-start | bytes 884744 | tf_op jit(solution)/shard_map/ppermute | solution.py:28
  63.6 8.7 %collective-permute-start.15 = (bf16[128,1152]{1,0:T(8,128)(2,1)S(1)}, bf16[128,1152]{1,0:T(8,128)(2,1)S(1)}, u32[]{:S(2)}, u32[]{:S(2)}) collective-permute-start(bf16[128,1152]{1,0:T(8,128)(2,1)S(1)} %collective-permute-done.14), channel_id=1, source_target_pairs={{0,32},{1,481},{32,64},{33,1},{64,96},{65,33},{96,128},{97,65},{12... | collective-permute-start | bytes 884744 | tf_op jit(solution)/shard_map/ppermute | solution.py:28
  67.2 11.0 %collective-permute-start.16 = (bf16[128,1152]{1,0:T(8,128)(2,1)S(1)}, bf16[128,1152]{1,0:T(8,128)(2,1)S(1)}, u32[]{:S(2)}, u32[]{:S(2)}) collective-permute-start(bf16[128,1152]{1,0:T(8,128)(2,1)S(1)} %collective-permute-done.12), channel_id=1, source_target_pairs={{0,32},{1,481},{32,64},{33,1},{64,96},{65,33},{96,128},{97,65},{12... | collective-permute-start | bytes 884744 | tf_op jit(solution)/shard_map/ppermute | solution.py:28
  72.2 10.8 %collective-permute-start.20 = (bf16[128,1152]{1,0:T(8,128)(2,1)S(1)}, bf16[128,1152]{1,0:T(8,128)(2,1)S(1)}, u32[]{:S(2)}, u32[]{:S(2)}) collective-permute-start(bf16[128,1152]{1,0:T(8,128)(2,1)S(1)} %collective-permute-done.15), channel_id=1, source_target_pairs={{0,32},{1,481},{32,64},{33,1},{64,96},{65,33},{96,128},{97,65},{12... | collective-permute-start | bytes 884744 | tf_op jit(solution)/shard_map/ppermute | solution.py:28
  75.5 16.2 %collective-permute-start.13 = (bf16[2,128,1152]{2,1,0:T(8,128)(2,1)S(1)}, bf16[2,128,1152]{2,1,0:T(8,128)(2,1)S(1)}, u32[]{:S(2)}, u32[]{:S(2)}) collective-permute-start(bf16[2,128,1152]{2,1,0:T(8,128)(2,1)S(1)} %pad_maximum_fusion.4), channel_id=1, source_target_pairs={{0,1},{1,0},{2,3},{3,2},{4,5},{5,4},{6,7},{7,6},{8,9},{9,8},{10,11... | collective-permute-start | bytes 1769480 | tf_op jit(solution)/shard_map/ppermute | solution.py:53
  78.2 8.5 %collective-permute-start.17 = (bf16[128,1152]{1,0:T(8,128)(2,1)S(1)}, bf16[128,1152]{1,0:T(8,128)(2,1)S(1)}, u32[]{:S(2)}, u32[]{:S(2)}) collective-permute-start(bf16[128,1152]{1,0:T(8,128)(2,1)S(1)} %collective-permute-done.16), channel_id=1, source_target_pairs={{0,32},{1,481},{32,64},{33,1},{64,96},{65,33},{96,128},{97,65},{12... | collective-permute-start | bytes 884744 | tf_op jit(solution)/shard_map/ppermute | solution.py:28
  83.1 16.9 %collective-permute-start.21 = (bf16[128,1152]{1,0:T(8,128)(2,1)S(1)}, bf16[128,1152]{1,0:T(8,128)(2,1)S(1)}, u32[]{:S(2)}, u32[]{:S(2)}) collective-permute-start(bf16[128,1152]{1,0:T(8,128)(2,1)S(1)} %collective-permute-done.20), channel_id=1, source_target_pairs={{1,481},{33,1},{65,33},{97,65},{129,97},{161,129},{193,161},{225,1... | collective-permute-start | bytes 884744 | tf_op jit(solution)/shard_map/ppermute | solution.py:28
  86.7 8.7 %collective-permute-start.18 = (bf16[128,1152]{1,0:T(8,128)(2,1)S(1)}, bf16[128,1152]{1,0:T(8,128)(2,1)S(1)}, u32[]{:S(2)}, u32[]{:S(2)}) collective-permute-start(bf16[128,1152]{1,0:T(8,128)(2,1)S(1)} %collective-permute-done.17), channel_id=1, source_target_pairs={{1,481},{33,1},{65,33},{97,65},{129,97},{161,129},{193,161},{225,1... | collective-permute-start | bytes 884744 | tf_op jit(solution)/shard_map/ppermute | solution.py:28
  95.5 4.3 %collective-permute-start.19 = (bf16[3,128,1152]{2,1,0:T(8,128)(2,1)S(1)}, bf16[3,128,1152]{2,1,0:T(8,128)(2,1)S(1)}, u32[]{:S(2)}, u32[]{:S(2)}) collective-permute-start(bf16[3,128,1152]{2,1,0:T(8,128)(2,1)S(1)} %pad_maximum_fusion.3), channel_id=1, source_target_pairs={{0,1},{1,0},{2,3},{3,2},{4,5},{5,4},{6,7},{7,6},{8,9},{9,8},{10,11... | collective-permute-start | bytes 2654216 | tf_op jit(solution)/shard_map/ppermute | solution.py:53
  100.0 2.1 %copy-start = (bf16[16,128,1152]{2,1,0:T(8,128)(2,1)}, bf16[16,128,1152]{2,1,0:T(8,128)(2,1)S(1)}, u32[]{:S(2)}) copy-start(bf16[16,128,1152]{2,1,0:T(8,128)(2,1)S(1)} %fusion.20) | copy-start | bytes 14155780
  128.4 20.8 %all-to-all-start.1 = ((bf16[16,256,128]{2,1,0:T(8,128)(2,1)}), bf16[16,256,128]{2,1,0:T(8,128)(2,1)S(1)}, u32[]{:S(2)}, u32[]{:S(2)}) async-start(bf16[16,256,128]{2,1,0:T(8,128)(2,1)} %broadcast_in_dim.79), calls=%async_computation.1 | async-start | bytes 2097152 | tf_op jit(solution)/shard_map/all_to_all | solution.py:17
  149.3 49.4 %slice-start = ((s8[4718592]{0:T(1024)(128)(4,1)}), s8[4194304]{0:T(1024)(128)(4,1)S(1)}, s32[]{:S(2)}) async-start(s8[4718592]{0:T(1024)(128)(4,1)} %bitcast.134), calls=%async_computation.3 | async-start | bytes 8388608
  149.4 24.8 %collective-permute-start.25 = (bf16[4,4,256,128]{3,2,1,0:T(8,128)(2,1)S(1)}, bf16[4,4,256,128]{3,2,1,0:T(8,128)(2,1)S(1)}, u32[]{:S(2)}, u32[]{:S(2)}) collective-permute-start(bf16[4,4,256,128]{3,2,1,0:T(8,128)(2,1)S(1)} %pad_maximum_fusion.1), channel_id=1, source_target_pairs={{0,1},{1,0},{2,3},{3,2},{4,5},{5,4},{6,7},{7,6},{8,9},{9,8},{10,11... | collective-permute-start | bytes 3145736 | tf_op jit(solution)/shard_map/ppermute | solution.py:136
  155.7 11.6 %collective-permute-start.23 = (bf16[4,256,128]{2,1,0:T(8,128)(2,1)S(1)}, bf16[4,256,128]{2,1,0:T(8,128)(2,1)S(1)}, u32[]{:S(2)}, u32[]{:S(2)}) collective-permute-start(bf16[4,256,128]{2,1,0:T(8,128)(2,1)S(1)} %bitcast.141), channel_id=1, source_target_pairs={{0,32},{1,33},{32,64},{33,65},{64,96},{65,97},{96,128},{97,129},{1... | collective-permute-start | bytes 786440 | tf_op jit(solution)/shard_map/ppermute | solution.py:28
  157.7 16.4 %collective-permute-start.24 = (bf16[4,256,128]{2,1,0:T(8,128)(2,1)S(1)}, bf16[4,256,128]{2,1,0:T(8,128)(2,1)S(1)}, u32[]{:S(2)}, u32[]{:S(2)}) collective-permute-start(bf16[4,256,128]{2,1,0:T(8,128)(2,1)S(1)} %bitcast.142), channel_id=1, source_target_pairs={{0,448},{1,65},{32,480},{33,97},{64,0},{65,129},{96,32},{97,161},{... | collective-permute-start | bytes 786440 | tf_op jit(solution)/shard_map/ppermute | solution.py:28
  162.4 13.0 %collective-permute-start.22 = (bf16[4,256,128]{2,1,0:T(8,128)(2,1)S(1)}, bf16[4,256,128]{2,1,0:T(8,128)(2,1)S(1)}, u32[]{:S(2)}, u32[]{:S(2)}) collective-permute-start(bf16[4,256,128]{2,1,0:T(8,128)(2,1)S(1)} %bitcast.143), channel_id=1, source_target_pairs={{0,480},{1,481},{32,0},{33,1},{64,32},{65,33},{96,64},{97,65},{128... | collective-permute-start | bytes 786440 | tf_op jit(solution)/shard_map/ppermute | solution.py:28
  174.6 24.0 %slice-start.1 = ((s8[4718592]{0:T(1024)(128)(4,1)}), s8[524288]{0:T(1024)(128)(4,1)S(1)}, s32[]{:S(2)}) async-start(s8[4718592]{0:T(1024)(128)(4,1)} %bitcast.134), calls=%async_computation.4 | async-start | bytes 1048576
  199.5 9.2 %collective-permute-start.26 = (bf16[128,1152]{1,0:T(8,128)(2,1)S(1)}, bf16[128,1152]{1,0:T(8,128)(2,1)S(1)}, u32[]{:S(2)}, u32[]{:S(2)}) collective-permute-start(bf16[128,1152]{1,0:T(8,128)(2,1)S(1)} %fusion.2), channel_id=1, source_target_pairs={{0,0},{1,16},{16,1},{17,17},{2,2},{3,18},{18,3},{19,19},{4,4},{5,2... | collective-permute-start | bytes 884744 | tf_op jit(solution)/shard_map/ppermute | solution.py:150
  205.2 7.5 %collective-permute-start.27 = (bf16[128,1152]{1,0:T(8,128)(2,1)S(1)}, bf16[128,1152]{1,0:T(8,128)(2,1)S(1)}, u32[]{:S(2)}, u32[]{:S(2)}) collective-permute-start(bf16[128,1152]{1,0:T(8,128)(2,1)S(1)} %fusion.1), channel_id=1, source_target_pairs={{0,16},{1,0},{16,17},{17,1},{2,18},{3,2},{18,19},{19,3},{4,20},{5,... | collective-permute-start | bytes 884744 | tf_op jit(solution)/shard_map/ppermute | solution.py:148

commit v17 on v15

--- a/solution.py
+++ b/solution.py
@@ -80,7 +80,7 @@
     own = lax.ppermute(rounded, ("ylo", "core"), TURN)
     other = lax.ppermute(own, "core", SWAP)
     slabs = groups * steps
-    near, far = [own, launch(rounded, 0)], [None, launch(swap([rounded])[0], 1)]
+    near, far = [own, launch(rounded, 0)], [None, launch(lax.ppermute(rounded, "core", SWAP), 1)]
     for step in range(2, slabs // 2):
         near.append(onward(near[-1]))
         far.append(onward(far[-1]))
@@ -100,8 +100,8 @@
     )
     partial_gram = partial_gram.transpose(1, 0, 2).astype(jnp.bfloat16)
     wide = own.astype(jnp.float32)
-    extra = jnp.pad(split((wide * wide).sum(1)), ((0, 13), (0, 0)))
-    extra = jnp.broadcast_to(extra.astype(jnp.bfloat16)[None], (chips, 16, rows))
+    extra = jnp.pad(split((wide * wide).sum(1)), ((0, 5), (0, 0)))
+    extra = jnp.broadcast_to(extra.astype(jnp.bfloat16)[None], (chips, 8, rows))
     partial_gram = jnp.concatenate([partial_gram, extra], 1)
     met = lax.axis_index(PLANE) == lax.axis_index(LINE)
     residue = lax.axis_index("zl")
@@ -122,13 +122,13 @@
     panel, _ = lax.optimization_barrier((panel, here))
     right = (
         here,
+        along(here, -2, 2),
         along(here, -1),
         along(here, 1),
-        along(here, -2, 2),
     )
     left_own = [
         lax.dynamic_index_in_dim(panel, (residue + shift) % steps, 1, False)
-        for shift in (0, 1, steps - 1, 2)
+        for shift in (0, 2, 1, steps - 1)
     ]
     left_other = lax.ppermute(jnp.stack(left_own), "core", SWAP)
     left_other = jnp.concatenate(
@@ -137,8 +137,10 @@
     square = 0.0
     for place in range(steps):
         square = square + mix(left_own[place], right[place][:, :rows])
+        square = lax.optimization_barrier(square)
     for place in range(steps):
         square = square + mix(left_other[place], right[place][:, rows:])
+        square = lax.optimization_barrier(square)
     poly = (-4.775 * gram + 2.0315 * square).astype(jnp.bfloat16)
     panel = share(poly, chips)
     away = mix(panel[:, rows:], half).astype(jnp.bfloat16)

time: 207 us -> 205 us (level)
  starting transfers between devices: 112 us -> 109 us
  blocking collectives: 61.7 us -> 63.8 us
    ppermute x4 -> x3, starting transfers between devices: 19.6 us -> 10.9 us  [swap(): return list(lax.ppermute(jnp.stack(pieces), 'core', SWAP))]
    ppermute x0 -> x1, starting transfers between devices: none -> 8.79 us  [per_device(): lax.ppermute(rounded, 'core', SWAP)]
    all_to_all x1, blocking collectives: 20.3 us -> 22.7 us  [share(): return lax.all_to_all(copies, PLANE, 0, 0)]
    ppermute x1, starting transfers between devices: 6.7 us -> 4.35 us  [per_device(): stay = lax.ppermute(stay.astype(jnp.bfloat16), ('ylo', 'core'), TURN)]
  transfers between devices with their start and end apart: 28 -> 28, of which waited for: 10 -> 9; matrix products, arithmetic and copies ran while one was open for 2% -> 2% of each run, Pallas kernels for 0% -> 0%
where the time goes in v17:
time: 205 us; the launch traced here: 204 us
  starting transfers between devices  109 us (53%)
  blocking collectives  63.8 us (31%)
  waiting for transfers between devices  18.3 us (9%)
  matrix products  4.99 us (2%)
  local copies, waits for them, and re-layouts  3.37 us (2%)
  other arithmetic  2.93 us (1%)
    ppermute x16, starting transfers between devices, along(): return lax.ppermute(piece, LINE + ('core',), pairs)  61.3 us
    all_to_all x1, blocking collectives, per_device(): summands = lax.all_to_all(partial_gram, PLANE, 0, 0)  24.5 us
    all_to_all x1, blocking collectives, share(): return lax.all_to_all(copies, PLANE, 0, 0)  22.7 us
    all_gather x1, blocking collectives, per_device(): here = lax.all_gather(gram_low, 'zh', axis=0)  16.6 us
    ppermute x3, starting transfers between devices, swap(): return list(lax.ppermute(jnp.stack(pieces), 'core', SWAP))  10.9 us
    ppermute x16, waiting for transfers between devices, along(): return lax.ppermute(piece, LINE + ('core',), pairs)  9.8 us
    ppermute x1, starting transfers between devices, per_device(): lax.ppermute(rounded, 'core', SWAP)  8.79 us
    ppermute x2, starting transfers between devices, launch(): return lax.ppermute(piece, LINE + ('ylo', 'core'), pairs)  7.67 us
  transfers between devices with their start and end apart: 28, of which 9 were waited for; matrix products, arithmetic and copies ran while one was open for 2% of the time, Pallas kernels for 0%

profile of v17, /device:TPU:1, one launch (start us, length us, event | category | flops | bytes accessed | tf_op | source)
XLA Modules:
  0.0 203.8 jit_solution(11896338340428314781)
XLA Ops:
  0.0 1.1 convert_element_type.39
  1.1 8.8 %collective-permute-start.3 = (bf16[128,1152]{1,0:T(8,128)(2,1)S(1)}, bf16[128,1152]{1,0:T(8,128)(2,1)S(1)}, u32[]{:S(2)}, u32[]{:S(2)}) collective-permute-start(bf16[128,1152]{1,0:T(8,128)(2,1)S(1)} %convert_element_type.39), channel_id=1, source_target_pairs={{0,1},{1,0},{2,3},{3,2},{4,5},{5,4},{6,7},{7,6},{8,9},{9,8},{10,11... | collective-permute-start | bytes 884744 | tf_op jit(solution)/shard_map/ppermute | solution.py:83
  9.9 1.9 collective-permute-start.2
  11.8 5.7 %collective-permute-start.4 = (bf16[128,1152]{1,0:T(8,128)(2,1)S(1)}, bf16[128,1152]{1,0:T(8,128)(2,1)S(1)}, u32[]{:S(2)}, u32[]{:S(2)}) collective-permute-start(bf16[128,1152]{1,0:T(8,128)(2,1)S(1)} %collective-permute-done.3), channel_id=1, source_target_pairs={{0,497},{1,481},{16,48},{17,32},{32,17},{33,1},{48,80},{49,64},{64... | collective-permute-start | bytes 884744 | tf_op jit(solution)/shard_map/ppermute | solution.py:49
  17.6 1.5 collective-permute-done.2
  19.1 9.9 %collective-permute-start.8 = (bf16[128,1152]{1,0:T(8,128)(2,1)S(1)}, bf16[128,1152]{1,0:T(8,128)(2,1)S(1)}, u32[]{:S(2)}, u32[]{:S(2)}) collective-permute-start(bf16[128,1152]{1,0:T(8,128)(2,1)S(1)} %collective-permute-done.2), channel_id=1, source_target_pairs={{0,32},{1,481},{32,64},{33,1},{64,96},{65,33},{96,128},{97,65},{12... | collective-permute-start | bytes 884744 | tf_op jit(solution)/shard_map/ppermute | solution.py:28
  29.0 1.9 collective-permute-start
  31.0 2.7 %collective-permute-start.5 = (bf16[128,1152]{1,0:T(8,128)(2,1)S(1)}, bf16[128,1152]{1,0:T(8,128)(2,1)S(1)}, u32[]{:S(2)}, u32[]{:S(2)}) collective-permute-start(bf16[128,1152]{1,0:T(8,128)(2,1)S(1)} %collective-permute-done.4), channel_id=1, source_target_pairs={{0,32},{1,481},{32,64},{33,1},{64,96},{65,33},{96,128},{97,65},{12... | collective-permute-start | bytes 884744 | tf_op jit(solution)/shard_map/ppermute | solution.py:28
  33.7 4.0 %collective-permute-start.9 = (bf16[128,1152]{1,0:T(8,128)(2,1)S(1)}, bf16[128,1152]{1,0:T(8,128)(2,1)S(1)}, u32[]{:S(2)}, u32[]{:S(2)}) collective-permute-start(bf16[128,1152]{1,0:T(8,128)(2,1)S(1)} %collective-permute-done.8), channel_id=1, source_target_pairs={{0,32},{1,481},{32,64},{33,1},{64,96},{65,33},{96,128},{97,65},{12... | collective-permute-start | bytes 884744 | tf_op jit(solution)/shard_map/ppermute | solution.py:28
  38.1 1.9 collective-permute-start.1
  40.0 2.5 %collective-permute-start.6 = (bf16[128,1152]{1,0:T(8,128)(2,1)S(1)}, bf16[128,1152]{1,0:T(8,128)(2,1)S(1)}, u32[]{:S(2)}, u32[]{:S(2)}) collective-permute-start(bf16[128,1152]{1,0:T(8,128)(2,1)S(1)} %collective-permute-done.5), channel_id=1, source_target_pairs={{0,32},{1,481},{32,64},{33,1},{64,96},{65,33},{96,128},{97,65},{12... | collective-permute-start | bytes 884744 | tf_op jit(solution)/shard_map/ppermute | solution.py:28
  42.5 3.9 %collective-permute-start.10 = (bf16[128,1152]{1,0:T(8,128)(2,1)S(1)}, bf16[128,1152]{1,0:T(8,128)(2,1)S(1)}, u32[]{:S(2)}, u32[]{:S(2)}) collective-permute-start(bf16[128,1152]{1,0:T(8,128)(2,1)S(1)} %collective-permute-done.9), channel_id=1, source_target_pairs={{0,32},{1,481},{32,64},{33,1},{64,96},{65,33},{96,128},{97,65},{12... | collective-permute-start | bytes 884744 | tf_op jit(solution)/shard_map/ppermute | solution.py:28
  46.4 0.6 broadcast_in_dim.67
  47.1 0.7 collective-permute-done.6
  47.8 3.4 %collective-permute-start.11 = (bf16[128,1152]{1,0:T(8,128)(2,1)S(1)}, bf16[128,1152]{1,0:T(8,128)(2,1)S(1)}, u32[]{:S(2)}, u32[]{:S(2)}) collective-permute-start(bf16[128,1152]{1,0:T(8,128)(2,1)S(1)} %collective-permute-done.6), channel_id=1, source_target_pairs={{0,32},{1,481},{32,64},{33,1},{64,96},{65,33},{96,128},{97,65},{12... | collective-permute-start | bytes 884744 | tf_op jit(solution)/shard_map/ppermute | solution.py:28
  51.2 3.9 %collective-permute-start.14 = (bf16[128,1152]{1,0:T(8,128)(2,1)S(1)}, bf16[128,1152]{1,0:T(8,128)(2,1)S(1)}, u32[]{:S(2)}, u32[]{:S(2)}) collective-permute-start(bf16[128,1152]{1,0:T(8,128)(2,1)S(1)} %collective-permute-done.10), channel_id=1, source_target_pairs={{0,32},{1,481},{32,64},{33,1},{64,96},{65,33},{96,128},{97,65},{12... | collective-permute-start | bytes 884744 | tf_op jit(solution)/shard_map/ppermute | solution.py:28
  55.0 0.1 multiply_reduce_fusion
  55.2 0.1 pad_maximum_fusion.2
  55.3 2.3 %collective-permute-start.7 = (bf16[3,128,1152]{2,1,0:T(8,128)(2,1)S(1)}, bf16[3,128,1152]{2,1,0:T(8,128)(2,1)S(1)}, u32[]{:S(2)}, u32[]{:S(2)}) collective-permute-start(bf16[3,128,1152]{2,1,0:T(8,128)(2,1)S(1)} %pad_maximum_fusion.2), channel_id=1, source_target_pairs={{0,1},{1,0},{2,3},{3,2},{4,5},{5,4},{6,7},{7,6},{8,9},{9,8},{10,11... | collective-permute-start | bytes 2654216 | tf_op jit(solution)/shard_map/ppermute | solution.py:53
  57.6 4.9 %collective-permute-start.12 = (bf16[128,1152]{1,0:T(8,128)(2,1)S(1)}, bf16[128,1152]{1,0:T(8,128)(2,1)S(1)}, u32[]{:S(2)}, u32[]{:S(2)}) collective-permute-start(bf16[128,1152]{1,0:T(8,128)(2,1)S(1)} %collective-permute-done.11), channel_id=1, source_target_pairs={{0,32},{1,481},{32,64},{33,1},{64,96},{65,33},{96,128},{97,65},{12... | collective-permute-start | bytes 884744 | tf_op jit(solution)/shard_map/ppermute | solution.py:28
  62.5 2.4 %collective-permute-start.15 = (bf16[128,1152]{1,0:T(8,128)(2,1)S(1)}, bf16[128,1152]{1,0:T(8,128)(2,1)S(1)}, u32[]{:S(2)}, u32[]{:S(2)}) collective-permute-start(bf16[128,1152]{1,0:T(8,128)(2,1)S(1)} %collective-permute-done.14), channel_id=1, source_target_pairs={{0,32},{1,481},{32,64},{33,1},{64,96},{65,33},{96,128},{97,65},{12... | collective-permute-start | bytes 884744 | tf_op jit(solution)/shard_map/ppermute | solution.py:28
  64.9 1.2 collective-permute-done.12
  66.1 5.0 %collective-permute-start.16 = (bf16[128,1152]{1,0:T(8,128)(2,1)S(1)}, bf16[128,1152]{1,0:T(8,128)(2,1)S(1)}, u32[]{:S(2)}, u32[]{:S(2)}) collective-permute-start(bf16[128,1152]{1,0:T(8,128)(2,1)S(1)} %collective-permute-done.12), channel_id=1, source_target_pairs={{0,32},{1,481},{32,64},{33,1},{64,96},{65,33},{96,128},{97,65},{12... | collective-permute-start | bytes 884744 | tf_op jit(solution)/shard_map/ppermute | solution.py:28
  71.2 3.1 %collective-permute-start.19 = (bf16[128,1152]{1,0:T(8,128)(2,1)S(1)}, bf16[128,1152]{1,0:T(8,128)(2,1)S(1)}, u32[]{:S(2)}, u32[]{:S(2)}) collective-permute-start(bf16[128,1152]{1,0:T(8,128)(2,1)S(1)} %collective-permute-done.15), channel_id=1, source_target_pairs={{0,32},{1,481},{32,64},{33,1},{64,96},{65,33},{96,128},{97,65},{12... | collective-permute-start | bytes 884744 | tf_op jit(solution)/shard_map/ppermute | solution.py:28
  74.4 2.7 %collective-permute-start.13 = (bf16[2,128,1152]{2,1,0:T(8,128)(2,1)S(1)}, bf16[2,128,1152]{2,1,0:T(8,128)(2,1)S(1)}, u32[]{:S(2)}, u32[]{:S(2)}) collective-permute-start(bf16[2,128,1152]{2,1,0:T(8,128)(2,1)S(1)} %pad_maximum_fusion.3), channel_id=1, source_target_pairs={{0,1},{1,0},{2,3},{3,2},{4,5},{5,4},{6,7},{7,6},{8,9},{9,8},{10,11... | collective-permute-start | bytes 1769480 | tf_op jit(solution)/shard_map/ppermute | solution.py:53
  77.1 4.9 %collective-permute-start.17 = (bf16[128,1152]{1,0:T(8,128)(2,1)S(1)}, bf16[128,1152]{1,0:T(8,128)(2,1)S(1)}, u32[]{:S(2)}, u32[]{:S(2)}) collective-permute-start(bf16[128,1152]{1,0:T(8,128)(2,1)S(1)} %collective-permute-done.16), channel_id=1, source_target_pairs={{0,32},{1,481},{32,64},{33,1},{64,96},{65,33},{96,128},{97,65},{12... | collective-permute-start | bytes 884744 | tf_op jit(solution)/shard_map/ppermute | solution.py:28
  82.0 2.4 %collective-permute-start.20 = (bf16[128,1152]{1,0:T(8,128)(2,1)S(1)}, bf16[128,1152]{1,0:T(8,128)(2,1)S(1)}, u32[]{:S(2)}, u32[]{:S(2)}) collective-permute-start(bf16[128,1152]{1,0:T(8,128)(2,1)S(1)} %collective-permute-done.19), channel_id=1, source_target_pairs={{0,32},{1,481},{32,64},{33,1},{64,96},{65,33},{96,128},{97,65},{12... | collective-permute-start | bytes 884744 | tf_op jit(solution)/shard_map/ppermute | solution.py:28
  84.7 0.9 collective-permute-done.17
  85.7 5.9 %collective-permute-start.18 = (bf16[2,128,1152]{2,1,0:T(8,128)(2,1)S(1)}, bf16[2,128,1152]{2,1,0:T(8,128)(2,1)S(1)}, u32[]{:S(2)}, u32[]{:S(2)}) collective-permute-start(bf16[2,128,1152]{2,1,0:T(8,128)(2,1)S(1)} %pad_maximum_fusion.4), channel_id=1, source_target_pairs={{0,1},{1,0},{2,3},{3,2},{4,5},{5,4},{6,7},{7,6},{8,9},{9,8},{10,11... | collective-permute-start | bytes 1769480 | tf_op jit(solution)/shard_map/ppermute | solution.py:53
  91.8 1.4 collective-permute-done.18
  93.4 1.6 fusion.3
  95.0 0.5 copy-done
  95.5 0.1 pad_maximum_fusion
  95.6 24.5 %all_to_all.15 = bf16[16,264,128]{2,1,0:T(8,128)(2,1)S(1)} all-to-all(bf16[16,264,128]{2,1,0:T(8,128)(2,1)S(1)} %pad_maximum_fusion), channel_id=1, replica_groups=mesh['zh'=4,'zl'=4,'ylo'=2,'x'=4,'yhi'=2,'core'=2] {'ylo','x','yhi'}, dimensions={0} | all-to-all | bytes 2162688 | tf_op jit(solution)/shard_map/all_to_all | solution.py:109
  120.1 0.1 convert_reduce_fusion
  120.3 1.2 broadcast_in_dim.79
  121.5 3.7 %all-to-all-start.1 = ((bf16[16,256,128]{2,1,0:T(8,128)(2,1)}), bf16[16,256,128]{2,1,0:T(8,128)(2,1)S(1)}, u32[]{:S(2)}, u32[]{:S(2)}) async-start(bf16[16,256,128]{2,1,0:T(8,128)(2,1)} %broadcast_in_dim.79), calls=%async_computation.1 | async-start | bytes 2097152 | tf_op jit(solution)/shard_map/all_to_all | solution.py:17
  125.3 16.6 %all-gather = bf16[1024,128]{1,0:T(8,128)(2,1)S(1)} all-gather(bf16[256,128]{1,0:T(8,128)(2,1)S(1)} %fusion.39), channel_id=2, replica_groups=mesh['zh'=4,'zl'=4,'ylo'=2,'x'=4,'yhi'=2,'core'=2] {'zh'}, dimensions={0}, use_global_device_ids=true | all-gather | bytes 327680 | tf_op jit(solution)/shard_map/all_gather | solution.py:121
  141.9 0.1 dynamic-slice_bitcast_fusion.3
  142.0 0.1 pad_maximum_fusion.1
  142.1 6.9 %collective-permute-start.24 = (bf16[4,4,256,128]{3,2,1,0:T(8,128)(2,1)S(1)}, bf16[4,4,256,128]{3,2,1,0:T(8,128)(2,1)S(1)}, u32[]{:S(2)}, u32[]{:S(2)}) collective-permute-start(bf16[4,4,256,128]{3,2,1,0:T(8,128)(2,1)S(1)} %pad_maximum_fusion.1), channel_id=1, source_target_pairs={{0,1},{1,0},{2,3},{3,2},{4,5},{5,4},{6,7},{7,6},{8,9},{9,8},{10,11... | collective-permute-start | bytes 3145736 | tf_op jit(solution)/shard_map/ppermute | solution.py:133
  149.1 1.9 collective-permute-start.21
  151.0 3.1 %collective-permute-start.23 = (bf16[4,256,128]{2,1,0:T(8,128)(2,1)S(1)}, bf16[4,256,128]{2,1,0:T(8,128)(2,1)S(1)}, u32[]{:S(2)}, u32[]{:S(2)}) collective-permute-start(bf16[4,256,128]{2,1,0:T(8,128)(2,1)S(1)} %bitcast.112), channel_id=1, source_target_pairs={{0,32},{1,33},{32,64},{33,65},{64,96},{65,97},{96,128},{97,129},{1... | collective-permute-start | bytes 786440 | tf_op jit(solution)/shard_map/ppermute | solution.py:28
  154.1 3.4 %collective-permute-start.22 = (bf16[4,256,128]{2,1,0:T(8,128)(2,1)S(1)}, bf16[4,256,128]{2,1,0:T(8,128)(2,1)S(1)}, u32[]{:S(2)}, u32[]{:S(2)}) collective-permute-start(bf16[4,256,128]{2,1,0:T(8,128)(2,1)S(1)} %bitcast.113), channel_id=1, source_target_pairs={{0,480},{1,481},{32,0},{33,1},{64,32},{65,33},{96,64},{97,65},{128... | collective-permute-start | bytes 786440 | tf_op jit(solution)/shard_map/ppermute | solution.py:28
  157.5 0.2 convolution_bitcast_fusion.9
  157.7 5.4 %collective-permute-done.21 = bf16[4,256,128]{2,1,0:T(8,128)(2,1)S(1)} collective-permute-done((bf16[4,256,128]{2,1,0:T(8,128)(2,1)S(1)}, bf16[4,256,128]{2,1,0:T(8,128)(2,1)S(1)}, u32[]{:S(2)}, u32[]{:S(2)}) %collective-permute-start.21) | collective-permute-done | bytes 262176 | tf_op jit(solution)/shard_map/ppermute | solution.py:28
  163.1 0.2 fusion.4
  163.3 1.6 collective-permute-done.22
  164.9 0.2 convolution_bitcast_fusion.7
  165.1 0.2 convolution_bitcast_fusion.6
  165.4 0.1 fusion.56
  165.5 0.2 convolution_bitcast_fusion.5
  165.7 0.2 fusion.5
  166.0 0.2 convolution_bitcast_fusion.3
  166.2 0.2 convolution_bitcast_fusion.2
  166.5 0.2 broadcast_in_dim.81
  166.7 22.7 %all_to_all.16 = bf16[16,256,128]{2,1,0:T(8,128)(2,1)S(1)} all-to-all(bf16[16,256,128]{2,1,0:T(8,128)(2,1)S(1)} %broadcast_in_dim.81), channel_id=1, replica_groups=mesh['zh'=4,'zl'=4,'ylo'=2,'x'=4,'yhi'=2,'core'=2] {'ylo','x','yhi'}, dimensions={0} | all-to-all | bytes 2097152 | tf_op jit(solution)/shard_map/all_to_all | solution.py:17
  189.4 0.9 fusion.2
  190.3 4.3 %collective-permute-start.25 = (bf16[128,1152]{1,0:T(8,128)(2,1)S(1)}, bf16[128,1152]{1,0:T(8,128)(2,1)S(1)}, u32[]{:S(2)}, u32[]{:S(2)}) collective-permute-start(bf16[128,1152]{1,0:T(8,128)(2,1)S(1)} %fusion.2), channel_id=1, source_target_pairs={{0,0},{1,16},{16,1},{17,17},{2,2},{3,18},{18,3},{19,19},{4,4},{5,2... | collective-permute-start | bytes 884744 | tf_op jit(solution)/shard_map/ppermute | solution.py:149
  194.6 0.9 fusion.1
  195.5 1.9 collective-permute-start.26
  197.4 1.6 collective-permute-done.25
  199.0 3.9 %collective-permute-done.26 = bf16[128,1152]{1,0:T(8,128)(2,1)S(1)} collective-permute-done((bf16[128,1152]{1,0:T(8,128)(2,1)S(1)}, bf16[128,1152]{1,0:T(8,128)(2,1)S(1)}, u32[]{:S(2)}, u32[]{:S(2)}) %collective-permute-start.26) | collective-permute-done | bytes 294944 | tf_op jit(solution)/shard_map/ppermute | solution.py:147
  202.9 0.9 convert_add_fusion
  (55 shorter events, 1.0 us)
Async XLA Ops:
  1.1 10.7 %collective-permute-start.3 = (bf16[128,1152]{1,0:T(8,128)(2,1)S(1)}, bf16[128,1152]{1,0:T(8,128)(2,1)S(1)}, u32[]{:S(2)}, u32[]{:S(2)}) collective-permute-start(bf16[128,1152]{1,0:T(8,128)(2,1)S(1)} %convert_element_type.39), channel_id=1, source_target_pairs={{0,1},{1,0},{2,3},{3,2},{4,5},{5,4},{6,7},{7,6},{8,9},{9,8},{10,11... | collective-permute-start | bytes 884744 | tf_op jit(solution)/shard_map/ppermute | solution.py:83
  9.9 9.2 %collective-permute-start.2 = (bf16[128,1152]{1,0:T(8,128)(2,1)S(1)}, bf16[128,1152]{1,0:T(8,128)(2,1)S(1)}, u32[]{:S(2)}, u32[]{:S(2)}) collective-permute-start(bf16[128,1152]{1,0:T(8,128)(2,1)S(1)} %convert_element_type.39), channel_id=1, source_target_pairs={{0,32},{1,48},{16,481},{17,497},{32,64},{33,80},{48,1},{49,17},{64... | collective-permute-start | bytes 884744 | tf_op jit(solution)/shard_map/ppermute | solution.py:49
  11.8 19.1 %collective-permute-start.4 = (bf16[128,1152]{1,0:T(8,128)(2,1)S(1)}, bf16[128,1152]{1,0:T(8,128)(2,1)S(1)}, u32[]{:S(2)}, u32[]{:S(2)}) collective-permute-start(bf16[128,1152]{1,0:T(8,128)(2,1)S(1)} %collective-permute-done.3), channel_id=1, source_target_pairs={{0,497},{1,481},{16,48},{17,32},{32,17},{33,1},{48,80},{49,64},{64... | collective-permute-start | bytes 884744 | tf_op jit(solution)/shard_map/ppermute | solution.py:49
  19.1 14.6 %collective-permute-start.8 = (bf16[128,1152]{1,0:T(8,128)(2,1)S(1)}, bf16[128,1152]{1,0:T(8,128)(2,1)S(1)}, u32[]{:S(2)}, u32[]{:S(2)}) collective-permute-start(bf16[128,1152]{1,0:T(8,128)(2,1)S(1)} %collective-permute-done.2), channel_id=1, source_target_pairs={{0,32},{1,481},{32,64},{33,1},{64,96},{65,33},{96,128},{97,65},{12... | collective-permute-start | bytes 884744 | tf_op jit(solution)/shard_map/ppermute | solution.py:28
  29.0 9.0 %collective-permute-start = (bf16[128,1152]{1,0:T(8,128)(2,1)S(1)}, bf16[128,1152]{1,0:T(8,128)(2,1)S(1)}, u32[]{:S(2)}, u32[]{:S(2)}) collective-permute-start(bf16[128,1152]{1,0:T(8,128)(2,1)S(1)} %convert_element_type.39), channel_id=1, source_target_pairs={{0,0},{1,16},{16,1},{17,17},{2,2},{3,18},{18,3},{19,19},{4,4},{5,2... | collective-permute-start | bytes 884744 | tf_op jit(solution)/shard_map/ppermute | solution.py:80
  31.0 9.0 %collective-permute-start.5 = (bf16[128,1152]{1,0:T(8,128)(2,1)S(1)}, bf16[128,1152]{1,0:T(8,128)(2,1)S(1)}, u32[]{:S(2)}, u32[]{:S(2)}) collective-permute-start(bf16[128,1152]{1,0:T(8,128)(2,1)S(1)} %collective-permute-done.4), channel_id=1, source_target_pairs={{0,32},{1,481},{32,64},{33,1},{64,96},{65,33},{96,128},{97,65},{12... | collective-permute-start | bytes 884744 | tf_op jit(solution)/shard_map/ppermute | solution.py:28
  33.7 8.8 %collective-permute-start.9 = (bf16[128,1152]{1,0:T(8,128)(2,1)S(1)}, bf16[128,1152]{1,0:T(8,128)(2,1)S(1)}, u32[]{:S(2)}, u32[]{:S(2)}) collective-permute-start(bf16[128,1152]{1,0:T(8,128)(2,1)S(1)} %collective-permute-done.8), channel_id=1, source_target_pairs={{0,32},{1,481},{32,64},{33,1},{64,96},{65,33},{96,128},{97,65},{12... | collective-permute-start | bytes 884744 | tf_op jit(solution)/shard_map/ppermute | solution.py:28
  38.1 55.3 %collective-permute-start.1 = (bf16[128,1152]{1,0:T(8,128)(2,1)S(1)}, bf16[128,1152]{1,0:T(8,128)(2,1)S(1)}, u32[]{:S(2)}, u32[]{:S(2)}) collective-permute-start(bf16[128,1152]{1,0:T(8,128)(2,1)S(1)} %collective-permute-done), channel_id=1, source_target_pairs={{0,1},{1,0},{2,3},{3,2},{4,5},{5,4},{6,7},{7,6},{8,9},{9,8},{10,11... | collective-permute-start | bytes 884744 | tf_op jit(solution)/shard_map/ppermute | solution.py:81
  40.0 7.8 %collective-permute-start.6 = (bf16[128,1152]{1,0:T(8,128)(2,1)S(1)}, bf16[128,1152]{1,0:T(8,128)(2,1)S(1)}, u32[]{:S(2)}, u32[]{:S(2)}) collective-permute-start(bf16[128,1152]{1,0:T(8,128)(2,1)S(1)} %collective-permute-done.5), channel_id=1, source_target_pairs={{0,32},{1,481},{32,64},{33,1},{64,96},{65,33},{96,128},{97,65},{12... | collective-permute-start | bytes 884744 | tf_op jit(solution)/shard_map/ppermute | solution.py:28
  42.5 8.7 %collective-permute-start.10 = (bf16[128,1152]{1,0:T(8,128)(2,1)S(1)}, bf16[128,1152]{1,0:T(8,128)(2,1)S(1)}, u32[]{:S(2)}, u32[]{:S(2)}) collective-permute-start(bf16[128,1152]{1,0:T(8,128)(2,1)S(1)} %collective-permute-done.9), channel_id=1, source_target_pairs={{0,32},{1,481},{32,64},{33,1},{64,96},{65,33},{96,128},{97,65},{12... | collective-permute-start | bytes 884744 | tf_op jit(solution)/shard_map/ppermute | solution.py:28
  47.8 9.8 %collective-permute-start.11 = (bf16[128,1152]{1,0:T(8,128)(2,1)S(1)}, bf16[128,1152]{1,0:T(8,128)(2,1)S(1)}, u32[]{:S(2)}, u32[]{:S(2)}) collective-permute-start(bf16[128,1152]{1,0:T(8,128)(2,1)S(1)} %collective-permute-done.6), channel_id=1, source_target_pairs={{0,32},{1,481},{32,64},{33,1},{64,96},{65,33},{96,128},{97,65},{12... | collective-permute-start | bytes 884744 | tf_op jit(solution)/shard_map/ppermute | solution.py:28
  51.2 11.3 %collective-permute-start.14 = (bf16[128,1152]{1,0:T(8,128)(2,1)S(1)}, bf16[128,1152]{1,0:T(8,128)(2,1)S(1)}, u32[]{:S(2)}, u32[]{:S(2)}) collective-permute-start(bf16[128,1152]{1,0:T(8,128)(2,1)S(1)} %collective-permute-done.10), channel_id=1, source_target_pairs={{0,32},{1,481},{32,64},{33,1},{64,96},{65,33},{96,128},{97,65},{12... | collective-permute-start | bytes 884744 | tf_op jit(solution)/shard_map/ppermute | solution.py:28
  55.3 29.1 %collective-permute-start.7 = (bf16[3,128,1152]{2,1,0:T(8,128)(2,1)S(1)}, bf16[3,128,1152]{2,1,0:T(8,128)(2,1)S(1)}, u32[]{:S(2)}, u32[]{:S(2)}) collective-permute-start(bf16[3,128,1152]{2,1,0:T(8,128)(2,1)S(1)} %pad_maximum_fusion.2), channel_id=1, source_target_pairs={{0,1},{1,0},{2,3},{3,2},{4,5},{5,4},{6,7},{7,6},{8,9},{9,8},{10,11... | collective-permute-start | bytes 2654216 | tf_op jit(solution)/shard_map/ppermute | solution.py:53
  57.6 8.5 %collective-permute-start.12 = (bf16[128,1152]{1,0:T(8,128)(2,1)S(1)}, bf16[128,1152]{1,0:T(8,128)(2,1)S(1)}, u32[]{:S(2)}, u32[]{:S(2)}) collective-permute-start(bf16[128,1152]{1,0:T(8,128)(2,1)S(1)} %collective-permute-done.11), channel_id=1, source_target_pairs={{0,32},{1,481},{32,64},{33,1},{64,96},{65,33},{96,128},{97,65},{12... | collective-permute-start | bytes 884744 | tf_op jit(solution)/shard_map/ppermute | solution.py:28
  62.5 8.7 %collective-permute-start.15 = (bf16[128,1152]{1,0:T(8,128)(2,1)S(1)}, bf16[128,1152]{1,0:T(8,128)(2,1)S(1)}, u32[]{:S(2)}, u32[]{:S(2)}) collective-permute-start(bf16[128,1152]{1,0:T(8,128)(2,1)S(1)} %collective-permute-done.14), channel_id=1, source_target_pairs={{0,32},{1,481},{32,64},{33,1},{64,96},{65,33},{96,128},{97,65},{12... | collective-permute-start | bytes 884744 | tf_op jit(solution)/shard_map/ppermute | solution.py:28
  66.1 11.0 %collective-permute-start.16 = (bf16[128,1152]{1,0:T(8,128)(2,1)S(1)}, bf16[128,1152]{1,0:T(8,128)(2,1)S(1)}, u32[]{:S(2)}, u32[]{:S(2)}) collective-permute-start(bf16[128,1152]{1,0:T(8,128)(2,1)S(1)} %collective-permute-done.12), channel_id=1, source_target_pairs={{0,32},{1,481},{32,64},{33,1},{64,96},{65,33},{96,128},{97,65},{12... | collective-permute-start | bytes 884744 | tf_op jit(solution)/shard_map/ppermute | solution.py:28
  71.2 10.8 %collective-permute-start.19 = (bf16[128,1152]{1,0:T(8,128)(2,1)S(1)}, bf16[128,1152]{1,0:T(8,128)(2,1)S(1)}, u32[]{:S(2)}, u32[]{:S(2)}) collective-permute-start(bf16[128,1152]{1,0:T(8,128)(2,1)S(1)} %collective-permute-done.15), channel_id=1, source_target_pairs={{0,32},{1,481},{32,64},{33,1},{64,96},{65,33},{96,128},{97,65},{12... | collective-permute-start | bytes 884744 | tf_op jit(solution)/shard_map/ppermute | solution.py:28
  74.4 17.2 %collective-permute-start.13 = (bf16[2,128,1152]{2,1,0:T(8,128)(2,1)S(1)}, bf16[2,128,1152]{2,1,0:T(8,128)(2,1)S(1)}, u32[]{:S(2)}, u32[]{:S(2)}) collective-permute-start(bf16[2,128,1152]{2,1,0:T(8,128)(2,1)S(1)} %pad_maximum_fusion.3), channel_id=1, source_target_pairs={{0,1},{1,0},{2,3},{3,2},{4,5},{5,4},{6,7},{7,6},{8,9},{9,8},{10,11... | collective-permute-start | bytes 1769480 | tf_op jit(solution)/shard_map/ppermute | solution.py:53
  77.1 8.5 %collective-permute-start.17 = (bf16[128,1152]{1,0:T(8,128)(2,1)S(1)}, bf16[128,1152]{1,0:T(8,128)(2,1)S(1)}, u32[]{:S(2)}, u32[]{:S(2)}) collective-permute-start(bf16[128,1152]{1,0:T(8,128)(2,1)S(1)} %collective-permute-done.16), channel_id=1, source_target_pairs={{0,32},{1,481},{32,64},{33,1},{64,96},{65,33},{96,128},{97,65},{12... | collective-permute-start | bytes 884744 | tf_op jit(solution)/shard_map/ppermute | solution.py:28
  82.0 11.4 %collective-permute-start.20 = (bf16[128,1152]{1,0:T(8,128)(2,1)S(1)}, bf16[128,1152]{1,0:T(8,128)(2,1)S(1)}, u32[]{:S(2)}, u32[]{:S(2)}) collective-permute-start(bf16[128,1152]{1,0:T(8,128)(2,1)S(1)} %collective-permute-done.19), channel_id=1, source_target_pairs={{0,32},{1,481},{32,64},{33,1},{64,96},{65,33},{96,128},{97,65},{12... | collective-permute-start | bytes 884744 | tf_op jit(solution)/shard_map/ppermute | solution.py:28
  85.7 7.5 %collective-permute-start.18 = (bf16[2,128,1152]{2,1,0:T(8,128)(2,1)S(1)}, bf16[2,128,1152]{2,1,0:T(8,128)(2,1)S(1)}, u32[]{:S(2)}, u32[]{:S(2)}) collective-permute-start(bf16[2,128,1152]{2,1,0:T(8,128)(2,1)S(1)} %pad_maximum_fusion.4), channel_id=1, source_target_pairs={{0,1},{1,0},{2,3},{3,2},{4,5},{5,4},{6,7},{7,6},{8,9},{9,8},{10,11... | collective-permute-start | bytes 1769480 | tf_op jit(solution)/shard_map/ppermute | solution.py:53
  93.4 2.2 %copy-start = (bf16[16,128,1152]{2,1,0:T(8,128)(2,1)}, bf16[16,128,1152]{2,1,0:T(8,128)(2,1)S(1)}, u32[]{:S(2)}) copy-start(bf16[16,128,1152]{2,1,0:T(8,128)(2,1)S(1)} %bitcast_dynamic-update-slice_fusion) | copy-start | bytes 14155780
  121.5 20.3 %all-to-all-start.1 = ((bf16[16,256,128]{2,1,0:T(8,128)(2,1)}), bf16[16,256,128]{2,1,0:T(8,128)(2,1)S(1)}, u32[]{:S(2)}, u32[]{:S(2)}) async-start(bf16[16,256,128]{2,1,0:T(8,128)(2,1)} %broadcast_in_dim.79), calls=%async_computation.1 | async-start | bytes 2097152 | tf_op jit(solution)/shard_map/all_to_all | solution.py:17
  142.1 23.3 %collective-permute-start.24 = (bf16[4,4,256,128]{3,2,1,0:T(8,128)(2,1)S(1)}, bf16[4,4,256,128]{3,2,1,0:T(8,128)(2,1)S(1)}, u32[]{:S(2)}, u32[]{:S(2)}) collective-permute-start(bf16[4,4,256,128]{3,2,1,0:T(8,128)(2,1)S(1)} %pad_maximum_fusion.1), channel_id=1, source_target_pairs={{0,1},{1,0},{2,3},{3,2},{4,5},{5,4},{6,7},{7,6},{8,9},{9,8},{10,11... | collective-permute-start | bytes 3145736 | tf_op jit(solution)/shard_map/ppermute | solution.py:133
  149.1 14.0 %collective-permute-start.21 = (bf16[4,256,128]{2,1,0:T(8,128)(2,1)S(1)}, bf16[4,256,128]{2,1,0:T(8,128)(2,1)S(1)}, u32[]{:S(2)}, u32[]{:S(2)}) collective-permute-start(bf16[4,256,128]{2,1,0:T(8,128)(2,1)S(1)} %bitcast.111), channel_id=1, source_target_pairs={{0,448},{1,65},{32,480},{33,97},{64,0},{65,129},{96,32},{97,161},{... | collective-permute-start | bytes 786440 | tf_op jit(solution)/shard_map/ppermute | solution.py:28
  151.0 14.1 %collective-permute-start.23 = (bf16[4,256,128]{2,1,0:T(8,128)(2,1)S(1)}, bf16[4,256,128]{2,1,0:T(8,128)(2,1)S(1)}, u32[]{:S(2)}, u32[]{:S(2)}) collective-permute-start(bf16[4,256,128]{2,1,0:T(8,128)(2,1)S(1)} %bitcast.112), channel_id=1, source_target_pairs={{0,32},{1,33},{32,64},{33,65},{64,96},{65,97},{96,128},{97,129},{1... | collective-permute-start | bytes 786440 | tf_op jit(solution)/shard_map/ppermute | solution.py:28
  154.1 10.7 %collective-permute-start.22 = (bf16[4,256,128]{2,1,0:T(8,128)(2,1)S(1)}, bf16[4,256,128]{2,1,0:T(8,128)(2,1)S(1)}, u32[]{:S(2)}, u32[]{:S(2)}) collective-permute-start(bf16[4,256,128]{2,1,0:T(8,128)(2,1)S(1)} %bitcast.113), channel_id=1, source_target_pairs={{0,480},{1,481},{32,0},{33,1},{64,32},{65,33},{96,64},{97,65},{128... | collective-permute-start | bytes 786440 | tf_op jit(solution)/shard_map/ppermute | solution.py:28
  164.9 24.5 %slice-start = ((s8[4718592]{0:T(1024)(128)(4,1)}), s8[4194304]{0:T(1024)(128)(4,1)S(1)}, s32[]{:S(2)}) async-start(s8[4718592]{0:T(1024)(128)(4,1)} %bitcast.104), calls=%async_computation.3 | async-start | bytes 8388608
  165.7 23.7 %slice-start.1 = ((s8[4718592]{0:T(1024)(128)(4,1)}), s8[524288]{0:T(1024)(128)(4,1)S(1)}, s32[]{:S(2)}) async-start(s8[4718592]{0:T(1024)(128)(4,1)} %bitcast.104), calls=%async_computation.4 | async-start | bytes 1048576
  190.3 8.7 %collective-permute-start.25 = (bf16[128,1152]{1,0:T(8,128)(2,1)S(1)}, bf16[128,1152]{1,0:T(8,128)(2,1)S(1)}, u32[]{:S(2)}, u32[]{:S(2)}) collective-permute-start(bf16[128,1152]{1,0:T(8,128)(2,1)S(1)} %fusion.2), channel_id=1, source_target_pairs={{0,0},{1,16},{16,1},{17,17},{2,2},{3,18},{18,3},{19,19},{4,4},{5,2... | collective-permute-start | bytes 884744 | tf_op jit(solution)/shard_map/ppermute | solution.py:149
  195.5 7.5 %collective-permute-start.26 = (bf16[128,1152]{1,0:T(8,128)(2,1)S(1)}, bf16[128,1152]{1,0:T(8,128)(2,1)S(1)}, u32[]{:S(2)}, u32[]{:S(2)}) collective-permute-start(bf16[128,1152]{1,0:T(8,128)(2,1)S(1)} %fusion.1), channel_id=1, source_target_pairs={{0,16},{1,0},{16,17},{17,1},{2,18},{3,2},{18,19},{19,3},{4,20},{5,... | collective-permute-start | bytes 884744 | tf_op jit(solution)/shard_map/ppermute | solution.py:147

commit v18 on v17

--- a/solution.py
+++ b/solution.py
@@ -6,7 +6,7 @@
 AXES = ("zh", "zl", "ylo", "x", "yhi", "core")
 SIZES = (4, 4, 2, 4, 2, 2)
 LINE = ("zh", "zl")
-PLANE = ("ylo", "x", "yhi")
+PLANE = ("ylo", "yhi", "x")
 SWAP = ((0, 1), (1, 0))
 TURN = ((0, 0), (1, 2), (2, 1), (3, 3))
 CROSS = ((0, 2), (1, 0), (2, 3), (3, 1))
@@ -130,10 +130,10 @@
         lax.dynamic_index_in_dim(panel, (residue + shift) % steps, 1, False)
         for shift in (0, 2, 1, steps - 1)
     ]
-    left_other = lax.ppermute(jnp.stack(left_own), "core", SWAP)
-    left_other = jnp.concatenate(
-        [left_other[:, :, rows:], left_other[:, :, :rows]], 2
-    )
+    left_other = swap(left_own[:2]) + swap(left_own[2:])
+    left_other = [
+        jnp.concatenate([part[:, rows:], part[:, :rows]], 1) for part in left_other
+    ]
     square = 0.0
     for place in range(steps):
         square = square + mix(left_own[place], right[place][:, :rows])

time: 205 us -> 202 us (0.985)
  waiting for transfers between devices: 18.3 us -> 12.4 us
  starting transfers between devices: 109 us -> 114 us
    ppermute x3 -> x5, starting transfers between devices: 10.9 us -> 20.7 us  [swap(): return list(lax.ppermute(jnp.stack(pieces), 'core', SWAP))]
    ppermute x1 -> x0, starting transfers between devices: 6.95 us -> none  [per_device(): left_other = lax.ppermute(jnp.stack(left_own), 'core', SWAP)]
    ppermute x16, waiting for transfers between devices: 9.8 us -> 2.88 us  [along(): return lax.ppermute(piece, LINE + ('core',), pairs)]
  transfers between devices with their start and end apart: 28 -> 29, of which waited for: 9 -> 8; matrix products, arithmetic and copies ran while one was open for 2% -> 2% of each run, Pallas kernels for 0% -> 0%
where the time goes in v18:
time: 202 us; the launch traced here: 201 us
  starting transfers between devices  114 us (56%)
  blocking collectives  61.8 us (31%)
  waiting for transfers between devices  12.4 us (6%)
  matrix products  4.99 us (2%)
  local copies, waits for them, and re-layouts  3.39 us (2%)
  other arithmetic  2.91 us (1%)
    ppermute x16, starting transfers between devices, along(): return lax.ppermute(piece, LINE + ('core',), pairs)  61.3 us
    all_to_all x1, blocking collectives, per_device(): summands = lax.all_to_all(partial_gram, PLANE, 0, 0)  24.5 us
    all_to_all x1, blocking collectives, share(): return lax.all_to_all(copies, PLANE, 0, 0)  20.7 us
    ppermute x5, starting transfers between devices, swap(): return list(lax.ppermute(jnp.stack(pieces), 'core', SWAP))  20.7 us
    all_gather x1, blocking collectives, per_device(): here = lax.all_gather(gram_low, 'zh', axis=0)  16.6 us
    ppermute x1, starting transfers between devices, per_device(): lax.ppermute(rounded, 'core', SWAP)  8.79 us
    ppermute x2, starting transfers between devices, launch(): return lax.ppermute(piece, LINE + ('ylo', 'core'), pairs)  7.67 us
    ppermute x1, starting transfers between devices, per_device(): stay = lax.ppermute(stay.astype(jnp.bfloat16), ('ylo', 'core'), TURN)  6.01 us
  transfers between devices with their start and end apart: 29, of which 8 were waited for; matrix products, arithmetic and copies ran while one was open for 2% of the time, Pallas kernels for 0%

profile of v18, /device:TPU:1, one launch (start us, length us, event | category | flops | bytes accessed | tf_op | source)
XLA Modules:
  0.0 200.7 jit_solution(14454170601980407797)
XLA Ops:
  0.0 1.1 convert_element_type.39
  1.1 8.8 %collective-permute-start.3 = (bf16[128,1152]{1,0:T(8,128)(2,1)S(1)}, bf16[128,1152]{1,0:T(8,128)(2,1)S(1)}, u32[]{:S(2)}, u32[]{:S(2)}) collective-permute-start(bf16[128,1152]{1,0:T(8,128)(2,1)S(1)} %convert_element_type.39), channel_id=1, source_target_pairs={{0,1},{1,0},{2,3},{3,2},{4,5},{5,4},{6,7},{7,6},{8,9},{9,8},{10,11... | collective-permute-start | bytes 884744 | tf_op jit(solution)/shard_map/ppermute | solution.py:83
  9.9 1.9 collective-permute-start.2
  11.8 5.7 %collective-permute-start.4 = (bf16[128,1152]{1,0:T(8,128)(2,1)S(1)}, bf16[128,1152]{1,0:T(8,128)(2,1)S(1)}, u32[]{:S(2)}, u32[]{:S(2)}) collective-permute-start(bf16[128,1152]{1,0:T(8,128)(2,1)S(1)} %collective-permute-done.3), channel_id=1, source_target_pairs={{0,497},{1,481},{16,48},{17,32},{32,17},{33,1},{48,80},{49,64},{64... | collective-permute-start | bytes 884744 | tf_op jit(solution)/shard_map/ppermute | solution.py:49
  17.6 1.5 collective-permute-done.2
  19.1 9.9 %collective-permute-start.8 = (bf16[128,1152]{1,0:T(8,128)(2,1)S(1)}, bf16[128,1152]{1,0:T(8,128)(2,1)S(1)}, u32[]{:S(2)}, u32[]{:S(2)}) collective-permute-start(bf16[128,1152]{1,0:T(8,128)(2,1)S(1)} %collective-permute-done.2), channel_id=1, source_target_pairs={{0,32},{1,481},{32,64},{33,1},{64,96},{65,33},{96,128},{97,65},{12... | collective-permute-start | bytes 884744 | tf_op jit(solution)/shard_map/ppermute | solution.py:28
  29.0 1.9 collective-permute-start
  31.0 2.7 %collective-permute-start.5 = (bf16[128,1152]{1,0:T(8,128)(2,1)S(1)}, bf16[128,1152]{1,0:T(8,128)(2,1)S(1)}, u32[]{:S(2)}, u32[]{:S(2)}) collective-permute-start(bf16[128,1152]{1,0:T(8,128)(2,1)S(1)} %collective-permute-done.4), channel_id=1, source_target_pairs={{0,32},{1,481},{32,64},{33,1},{64,96},{65,33},{96,128},{97,65},{12... | collective-permute-start | bytes 884744 | tf_op jit(solution)/shard_map/ppermute | solution.py:28
  33.7 4.0 %collective-permute-start.9 = (bf16[128,1152]{1,0:T(8,128)(2,1)S(1)}, bf16[128,1152]{1,0:T(8,128)(2,1)S(1)}, u32[]{:S(2)}, u32[]{:S(2)}) collective-permute-start(bf16[128,1152]{1,0:T(8,128)(2,1)S(1)} %collective-permute-done.8), channel_id=1, source_target_pairs={{0,32},{1,481},{32,64},{33,1},{64,96},{65,33},{96,128},{97,65},{12... | collective-permute-start | bytes 884744 | tf_op jit(solution)/shard_map/ppermute | solution.py:28
  38.1 1.9 collective-permute-start.1
  40.0 2.5 %collective-permute-start.6 = (bf16[128,1152]{1,0:T(8,128)(2,1)S(1)}, bf16[128,1152]{1,0:T(8,128)(2,1)S(1)}, u32[]{:S(2)}, u32[]{:S(2)}) collective-permute-start(bf16[128,1152]{1,0:T(8,128)(2,1)S(1)} %collective-permute-done.5), channel_id=1, source_target_pairs={{0,32},{1,481},{32,64},{33,1},{64,96},{65,33},{96,128},{97,65},{12... | collective-permute-start | bytes 884744 | tf_op jit(solution)/shard_map/ppermute | solution.py:28
  42.5 3.9 %collective-permute-start.10 = (bf16[128,1152]{1,0:T(8,128)(2,1)S(1)}, bf16[128,1152]{1,0:T(8,128)(2,1)S(1)}, u32[]{:S(2)}, u32[]{:S(2)}) collective-permute-start(bf16[128,1152]{1,0:T(8,128)(2,1)S(1)} %collective-permute-done.9), channel_id=1, source_target_pairs={{0,32},{1,481},{32,64},{33,1},{64,96},{65,33},{96,128},{97,65},{12... | collective-permute-start | bytes 884744 | tf_op jit(solution)/shard_map/ppermute | solution.py:28
  46.4 0.6 broadcast_in_dim.67
  47.1 0.7 collective-permute-done.6
  47.8 3.4 %collective-permute-start.11 = (bf16[128,1152]{1,0:T(8,128)(2,1)S(1)}, bf16[128,1152]{1,0:T(8,128)(2,1)S(1)}, u32[]{:S(2)}, u32[]{:S(2)}) collective-permute-start(bf16[128,1152]{1,0:T(8,128)(2,1)S(1)} %collective-permute-done.6), channel_id=1, source_target_pairs={{0,32},{1,481},{32,64},{33,1},{64,96},{65,33},{96,128},{97,65},{12... | collective-permute-start | bytes 884744 | tf_op jit(solution)/shard_map/ppermute | solution.py:28
  51.2 3.9 %collective-permute-start.14 = (bf16[128,1152]{1,0:T(8,128)(2,1)S(1)}, bf16[128,1152]{1,0:T(8,128)(2,1)S(1)}, u32[]{:S(2)}, u32[]{:S(2)}) collective-permute-start(bf16[128,1152]{1,0:T(8,128)(2,1)S(1)} %collective-permute-done.10), channel_id=1, source_target_pairs={{0,32},{1,481},{32,64},{33,1},{64,96},{65,33},{96,128},{97,65},{12... | collective-permute-start | bytes 884744 | tf_op jit(solution)/shard_map/ppermute | solution.py:28
  55.0 0.1 multiply_reduce_fusion
  55.2 0.1 pad_maximum_fusion.1
  55.3 2.3 %collective-permute-start.7 = (bf16[3,128,1152]{2,1,0:T(8,128)(2,1)S(1)}, bf16[3,128,1152]{2,1,0:T(8,128)(2,1)S(1)}, u32[]{:S(2)}, u32[]{:S(2)}) collective-permute-start(bf16[3,128,1152]{2,1,0:T(8,128)(2,1)S(1)} %pad_maximum_fusion.1), channel_id=1, source_target_pairs={{0,1},{1,0},{2,3},{3,2},{4,5},{5,4},{6,7},{7,6},{8,9},{9,8},{10,11... | collective-permute-start | bytes 2654216 | tf_op jit(solution)/shard_map/ppermute | solution.py:53
  57.6 4.9 %collective-permute-start.12 = (bf16[128,1152]{1,0:T(8,128)(2,1)S(1)}, bf16[128,1152]{1,0:T(8,128)(2,1)S(1)}, u32[]{:S(2)}, u32[]{:S(2)}) collective-permute-start(bf16[128,1152]{1,0:T(8,128)(2,1)S(1)} %collective-permute-done.11), channel_id=1, source_target_pairs={{0,32},{1,481},{32,64},{33,1},{64,96},{65,33},{96,128},{97,65},{12... | collective-permute-start | bytes 884744 | tf_op jit(solution)/shard_map/ppermute | solution.py:28
  62.5 2.4 %collective-permute-start.15 = (bf16[128,1152]{1,0:T(8,128)(2,1)S(1)}, bf16[128,1152]{1,0:T(8,128)(2,1)S(1)}, u32[]{:S(2)}, u32[]{:S(2)}) collective-permute-start(bf16[128,1152]{1,0:T(8,128)(2,1)S(1)} %collective-permute-done.14), channel_id=1, source_target_pairs={{0,32},{1,481},{32,64},{33,1},{64,96},{65,33},{96,128},{97,65},{12... | collective-permute-start | bytes 884744 | tf_op jit(solution)/shard_map/ppermute | solution.py:28
  64.9 1.2 collective-permute-done.12
  66.1 5.0 %collective-permute-start.16 = (bf16[128,1152]{1,0:T(8,128)(2,1)S(1)}, bf16[128,1152]{1,0:T(8,128)(2,1)S(1)}, u32[]{:S(2)}, u32[]{:S(2)}) collective-permute-start(bf16[128,1152]{1,0:T(8,128)(2,1)S(1)} %collective-permute-done.12), channel_id=1, source_target_pairs={{0,32},{1,481},{32,64},{33,1},{64,96},{65,33},{96,128},{97,65},{12... | collective-permute-start | bytes 884744 | tf_op jit(solution)/shard_map/ppermute | solution.py:28
  71.2 3.1 %collective-permute-start.19 = (bf16[128,1152]{1,0:T(8,128)(2,1)S(1)}, bf16[128,1152]{1,0:T(8,128)(2,1)S(1)}, u32[]{:S(2)}, u32[]{:S(2)}) collective-permute-start(bf16[128,1152]{1,0:T(8,128)(2,1)S(1)} %collective-permute-done.15), channel_id=1, source_target_pairs={{0,32},{1,481},{32,64},{33,1},{64,96},{65,33},{96,128},{97,65},{12... | collective-permute-start | bytes 884744 | tf_op jit(solution)/shard_map/ppermute | solution.py:28
  74.3 0.1 pad_maximum_fusion.2
  74.4 2.7 %collective-permute-start.13 = (bf16[2,128,1152]{2,1,0:T(8,128)(2,1)S(1)}, bf16[2,128,1152]{2,1,0:T(8,128)(2,1)S(1)}, u32[]{:S(2)}, u32[]{:S(2)}) collective-permute-start(bf16[2,128,1152]{2,1,0:T(8,128)(2,1)S(1)} %pad_maximum_fusion.2), channel_id=1, source_target_pairs={{0,1},{1,0},{2,3},{3,2},{4,5},{5,4},{6,7},{7,6},{8,9},{9,8},{10,11... | collective-permute-start | bytes 1769480 | tf_op jit(solution)/shard_map/ppermute | solution.py:53
  77.1 4.9 %collective-permute-start.17 = (bf16[128,1152]{1,0:T(8,128)(2,1)S(1)}, bf16[128,1152]{1,0:T(8,128)(2,1)S(1)}, u32[]{:S(2)}, u32[]{:S(2)}) collective-permute-start(bf16[128,1152]{1,0:T(8,128)(2,1)S(1)} %collective-permute-done.16), channel_id=1, source_target_pairs={{0,32},{1,481},{32,64},{33,1},{64,96},{65,33},{96,128},{97,65},{12... | collective-permute-start | bytes 884744 | tf_op jit(solution)/shard_map/ppermute | solution.py:28
  82.0 2.4 %collective-permute-start.20 = (bf16[128,1152]{1,0:T(8,128)(2,1)S(1)}, bf16[128,1152]{1,0:T(8,128)(2,1)S(1)}, u32[]{:S(2)}, u32[]{:S(2)}) collective-permute-start(bf16[128,1152]{1,0:T(8,128)(2,1)S(1)} %collective-permute-done.19), channel_id=1, source_target_pairs={{0,32},{1,481},{32,64},{33,1},{64,96},{65,33},{96,128},{97,65},{12... | collective-permute-start | bytes 884744 | tf_op jit(solution)/shard_map/ppermute | solution.py:28
  84.7 0.9 collective-permute-done.17
  85.6 0.1 pad_maximum_fusion.3
  85.7 5.9 %collective-permute-start.18 = (bf16[2,128,1152]{2,1,0:T(8,128)(2,1)S(1)}, bf16[2,128,1152]{2,1,0:T(8,128)(2,1)S(1)}, u32[]{:S(2)}, u32[]{:S(2)}) collective-permute-start(bf16[2,128,1152]{2,1,0:T(8,128)(2,1)S(1)} %pad_maximum_fusion.3), channel_id=1, source_target_pairs={{0,1},{1,0},{2,3},{3,2},{4,5},{5,4},{6,7},{7,6},{8,9},{9,8},{10,11... | collective-permute-start | bytes 1769480 | tf_op jit(solution)/shard_map/ppermute | solution.py:53
  91.8 1.4 collective-permute-done.18
  93.4 1.6 fusion.3
  95.0 0.5 copy-done
  95.5 0.1 pad_maximum_fusion
  95.6 24.5 %all_to_all.15 = bf16[16,264,128]{2,1,0:T(8,128)(2,1)S(1)} all-to-all(bf16[16,264,128]{2,1,0:T(8,128)(2,1)S(1)} %pad_maximum_fusion), channel_id=1, replica_groups=mesh['zh'=4,'zl'=4,'ylo'=2,'x'=4,'yhi'=2,'core'=2] {'ylo','yhi','x'}, dimensions={0} | all-to-all | bytes 2162688 | tf_op jit(solution)/shard_map/all_to_all | solution.py:109
  120.1 0.1 convert_reduce_fusion
  120.3 1.2 broadcast_in_dim.79
  121.5 3.7 %all-to-all-start.1 = ((bf16[16,256,128]{2,1,0:T(8,128)(2,1)}), bf16[16,256,128]{2,1,0:T(8,128)(2,1)S(1)}, u32[]{:S(2)}, u32[]{:S(2)}) async-start(bf16[16,256,128]{2,1,0:T(8,128)(2,1)} %broadcast_in_dim.79), calls=%async_computation.1 | async-start | bytes 2097152 | tf_op jit(solution)/shard_map/all_to_all | solution.py:17
  125.2 16.6 %all-gather = bf16[1024,128]{1,0:T(8,128)(2,1)S(1)} all-gather(bf16[256,128]{1,0:T(8,128)(2,1)S(1)} %fusion.39), channel_id=2, replica_groups=mesh['zh'=4,'zl'=4,'ylo'=2,'x'=4,'yhi'=2,'core'=2] {'zh'}, dimensions={0}, use_global_device_ids=true | all-gather | bytes 327680 | tf_op jit(solution)/shard_map/all_gather | solution.py:121
  141.8 1.9 collective-permute-start.23
  143.8 4.6 %collective-permute-start.22 = (bf16[4,256,128]{2,1,0:T(8,128)(2,1)S(1)}, bf16[4,256,128]{2,1,0:T(8,128)(2,1)S(1)}, u32[]{:S(2)}, u32[]{:S(2)}) collective-permute-start(bf16[4,256,128]{2,1,0:T(8,128)(2,1)S(1)} %bitcast.108), channel_id=1, source_target_pairs={{0,480},{1,481},{32,0},{33,1},{64,32},{65,33},{96,64},{97,65},{128... | collective-permute-start | bytes 786440 | tf_op jit(solution)/shard_map/ppermute | solution.py:28
  148.3 1.9 collective-permute-start.21
  150.3 0.1 dynamic-slice_bitcast_fusion.1
  150.4 7.7 %collective-permute-start.25 = (bf16[2,4,256,128]{3,2,1,0:T(8,128)(2,1)S(1)}, bf16[2,4,256,128]{3,2,1,0:T(8,128)(2,1)S(1)}, u32[]{:S(2)}, u32[]{:S(2)}) collective-permute-start(bf16[2,4,256,128]{3,2,1,0:T(8,128)(2,1)S(1)} %pad_maximum_fusion.5), channel_id=1, source_target_pairs={{0,1},{1,0},{2,3},{3,2},{4,5},{5,4},{6,7},{7,6},{8,9},{9,8},{10,11... | collective-permute-start | bytes 1572872 | tf_op jit(solution)/shard_map/ppermute | solution.py:53
  158.1 0.2 convolution_bitcast_fusion.9
  158.4 2.2 %collective-permute-start.24 = (bf16[2,4,256,128]{3,2,1,0:T(8,128)(2,1)S(1)}, bf16[2,4,256,128]{3,2,1,0:T(8,128)(2,1)S(1)}, u32[]{:S(2)}, u32[]{:S(2)}) collective-permute-start(bf16[2,4,256,128]{3,2,1,0:T(8,128)(2,1)S(1)} %pad_maximum_fusion.4), channel_id=1, source_target_pairs={{0,1},{1,0},{2,3},{3,2},{4,5},{5,4},{6,7},{7,6},{8,9},{9,8},{10,11... | collective-permute-start | bytes 1572872 | tf_op jit(solution)/shard_map/ppermute | solution.py:53
  160.6 0.2 fusion.4
  160.9 0.2 convolution_bitcast_fusion.7
  161.1 0.2 convolution_bitcast_fusion.6
  161.5 1.0 collective-permute-done.24
  162.6 0.2 convolution_bitcast_fusion.5
  162.8 0.2 fusion.5
  163.1 0.2 convolution_bitcast_fusion.3
  163.3 0.2 convolution_bitcast_fusion.2
  163.6 0.2 broadcast_in_dim.81
  163.8 20.7 %all_to_all.16 = bf16[16,256,128]{2,1,0:T(8,128)(2,1)S(1)} all-to-all(bf16[16,256,128]{2,1,0:T(8,128)(2,1)S(1)} %broadcast_in_dim.81), channel_id=1, replica_groups=mesh['zh'=4,'zl'=4,'ylo'=2,'x'=4,'yhi'=2,'core'=2] {'ylo','yhi','x'}, dimensions={0} | all-to-all | bytes 2097152 | tf_op jit(solution)/shard_map/all_to_all | solution.py:17
  184.6 0.9 fusion.2
  185.4 6.0 %collective-permute-start.26 = (bf16[128,1152]{1,0:T(8,128)(2,1)S(1)}, bf16[128,1152]{1,0:T(8,128)(2,1)S(1)}, u32[]{:S(2)}, u32[]{:S(2)}) collective-permute-start(bf16[128,1152]{1,0:T(8,128)(2,1)S(1)} %fusion.2), channel_id=1, source_target_pairs={{0,0},{1,16},{16,1},{17,17},{2,2},{3,18},{18,3},{19,19},{4,4},{5,2... | collective-permute-start | bytes 884744 | tf_op jit(solution)/shard_map/ppermute | solution.py:149
  191.4 0.9 fusion.1
  192.3 1.9 collective-permute-start.27
  194.2 1.6 collective-permute-done.26
  195.8 3.9 %collective-permute-done.27 = bf16[128,1152]{1,0:T(8,128)(2,1)S(1)} collective-permute-done((bf16[128,1152]{1,0:T(8,128)(2,1)S(1)}, bf16[128,1152]{1,0:T(8,128)(2,1)S(1)}, u32[]{:S(2)}, u32[]{:S(2)}) %collective-permute-start.27) | collective-permute-done | bytes 294944 | tf_op jit(solution)/shard_map/ppermute | solution.py:147
  199.8 0.9 convert_add_fusion
  (63 shorter events, 1.1 us)
Async XLA Ops:
  1.1 10.7 %collective-permute-start.3 = (bf16[128,1152]{1,0:T(8,128)(2,1)S(1)}, bf16[128,1152]{1,0:T(8,128)(2,1)S(1)}, u32[]{:S(2)}, u32[]{:S(2)}) collective-permute-start(bf16[128,1152]{1,0:T(8,128)(2,1)S(1)} %convert_element_type.39), channel_id=1, source_target_pairs={{0,1},{1,0},{2,3},{3,2},{4,5},{5,4},{6,7},{7,6},{8,9},{9,8},{10,11... | collective-permute-start | bytes 884744 | tf_op jit(solution)/shard_map/ppermute | solution.py:83
  9.9 9.2 %collective-permute-start.2 = (bf16[128,1152]{1,0:T(8,128)(2,1)S(1)}, bf16[128,1152]{1,0:T(8,128)(2,1)S(1)}, u32[]{:S(2)}, u32[]{:S(2)}) collective-permute-start(bf16[128,1152]{1,0:T(8,128)(2,1)S(1)} %convert_element_type.39), channel_id=1, source_target_pairs={{0,32},{1,48},{16,481},{17,497},{32,64},{33,80},{48,1},{49,17},{64... | collective-permute-start | bytes 884744 | tf_op jit(solution)/shard_map/ppermute | solution.py:49
  11.8 19.1 %collective-permute-start.4 = (bf16[128,1152]{1,0:T(8,128)(2,1)S(1)}, bf16[128,1152]{1,0:T(8,128)(2,1)S(1)}, u32[]{:S(2)}, u32[]{:S(2)}) collective-permute-start(bf16[128,1152]{1,0:T(8,128)(2,1)S(1)} %collective-permute-done.3), channel_id=1, source_target_pairs={{0,497},{1,481},{16,48},{17,32},{32,17},{33,1},{48,80},{49,64},{64... | collective-permute-start | bytes 884744 | tf_op jit(solution)/shard_map/ppermute | solution.py:49
  19.1 14.6 %collective-permute-start.8 = (bf16[128,1152]{1,0:T(8,128)(2,1)S(1)}, bf16[128,1152]{1,0:T(8,128)(2,1)S(1)}, u32[]{:S(2)}, u32[]{:S(2)}) collective-permute-start(bf16[128,1152]{1,0:T(8,128)(2,1)S(1)} %collective-permute-done.2), channel_id=1, source_target_pairs={{0,32},{1,481},{32,64},{33,1},{64,96},{65,33},{96,128},{97,65},{12... | collective-permute-start | bytes 884744 | tf_op jit(solution)/shard_map/ppermute | solution.py:28
  29.0 9.0 %collective-permute-start = (bf16[128,1152]{1,0:T(8,128)(2,1)S(1)}, bf16[128,1152]{1,0:T(8,128)(2,1)S(1)}, u32[]{:S(2)}, u32[]{:S(2)}) collective-permute-start(bf16[128,1152]{1,0:T(8,128)(2,1)S(1)} %convert_element_type.39), channel_id=1, source_target_pairs={{0,0},{1,16},{16,1},{17,17},{2,2},{3,18},{18,3},{19,19},{4,4},{5,2... | collective-permute-start | bytes 884744 | tf_op jit(solution)/shard_map/ppermute | solution.py:80
  31.0 9.0 %collective-permute-start.5 = (bf16[128,1152]{1,0:T(8,128)(2,1)S(1)}, bf16[128,1152]{1,0:T(8,128)(2,1)S(1)}, u32[]{:S(2)}, u32[]{:S(2)}) collective-permute-start(bf16[128,1152]{1,0:T(8,128)(2,1)S(1)} %collective-permute-done.4), channel_id=1, source_target_pairs={{0,32},{1,481},{32,64},{33,1},{64,96},{65,33},{96,128},{97,65},{12... | collective-permute-start | bytes 884744 | tf_op jit(solution)/shard_map/ppermute | solution.py:28
  33.7 8.8 %collective-permute-start.9 = (bf16[128,1152]{1,0:T(8,128)(2,1)S(1)}, bf16[128,1152]{1,0:T(8,128)(2,1)S(1)}, u32[]{:S(2)}, u32[]{:S(2)}) collective-permute-start(bf16[128,1152]{1,0:T(8,128)(2,1)S(1)} %collective-permute-done.8), channel_id=1, source_target_pairs={{0,32},{1,481},{32,64},{33,1},{64,96},{65,33},{96,128},{97,65},{12... | collective-permute-start | bytes 884744 | tf_op jit(solution)/shard_map/ppermute | solution.py:28
  38.1 55.3 %collective-permute-start.1 = (bf16[128,1152]{1,0:T(8,128)(2,1)S(1)}, bf16[128,1152]{1,0:T(8,128)(2,1)S(1)}, u32[]{:S(2)}, u32[]{:S(2)}) collective-permute-start(bf16[128,1152]{1,0:T(8,128)(2,1)S(1)} %collective-permute-done), channel_id=1, source_target_pairs={{0,1},{1,0},{2,3},{3,2},{4,5},{5,4},{6,7},{7,6},{8,9},{9,8},{10,11... | collective-permute-start | bytes 884744 | tf_op jit(solution)/shard_map/ppermute | solution.py:81
  40.0 7.8 %collective-permute-start.6 = (bf16[128,1152]{1,0:T(8,128)(2,1)S(1)}, bf16[128,1152]{1,0:T(8,128)(2,1)S(1)}, u32[]{:S(2)}, u32[]{:S(2)}) collective-permute-start(bf16[128,1152]{1,0:T(8,128)(2,1)S(1)} %collective-permute-done.5), channel_id=1, source_target_pairs={{0,32},{1,481},{32,64},{33,1},{64,96},{65,33},{96,128},{97,65},{12... | collective-permute-start | bytes 884744 | tf_op jit(solution)/shard_map/ppermute | solution.py:28
  42.5 8.7 %collective-permute-start.10 = (bf16[128,1152]{1,0:T(8,128)(2,1)S(1)}, bf16[128,1152]{1,0:T(8,128)(2,1)S(1)}, u32[]{:S(2)}, u32[]{:S(2)}) collective-permute-start(bf16[128,1152]{1,0:T(8,128)(2,1)S(1)} %collective-permute-done.9), channel_id=1, source_target_pairs={{0,32},{1,481},{32,64},{33,1},{64,96},{65,33},{96,128},{97,65},{12... | collective-permute-start | bytes 884744 | tf_op jit(solution)/shard_map/ppermute | solution.py:28
  47.8 9.8 %collective-permute-start.11 = (bf16[128,1152]{1,0:T(8,128)(2,1)S(1)}, bf16[128,1152]{1,0:T(8,128)(2,1)S(1)}, u32[]{:S(2)}, u32[]{:S(2)}) collective-permute-start(bf16[128,1152]{1,0:T(8,128)(2,1)S(1)} %collective-permute-done.6), channel_id=1, source_target_pairs={{0,32},{1,481},{32,64},{33,1},{64,96},{65,33},{96,128},{97,65},{12... | collective-permute-start | bytes 884744 | tf_op jit(solution)/shard_map/ppermute | solution.py:28
  51.2 11.3 %collective-permute-start.14 = (bf16[128,1152]{1,0:T(8,128)(2,1)S(1)}, bf16[128,1152]{1,0:T(8,128)(2,1)S(1)}, u32[]{:S(2)}, u32[]{:S(2)}) collective-permute-start(bf16[128,1152]{1,0:T(8,128)(2,1)S(1)} %collective-permute-done.10), channel_id=1, source_target_pairs={{0,32},{1,481},{32,64},{33,1},{64,96},{65,33},{96,128},{97,65},{12... | collective-permute-start | bytes 884744 | tf_op jit(solution)/shard_map/ppermute | solution.py:28
  55.3 29.1 %collective-permute-start.7 = (bf16[3,128,1152]{2,1,0:T(8,128)(2,1)S(1)}, bf16[3,128,1152]{2,1,0:T(8,128)(2,1)S(1)}, u32[]{:S(2)}, u32[]{:S(2)}) collective-permute-start(bf16[3,128,1152]{2,1,0:T(8,128)(2,1)S(1)} %pad_maximum_fusion.1), channel_id=1, source_target_pairs={{0,1},{1,0},{2,3},{3,2},{4,5},{5,4},{6,7},{7,6},{8,9},{9,8},{10,11... | collective-permute-start | bytes 2654216 | tf_op jit(solution)/shard_map/ppermute | solution.py:53
  57.6 8.5 %collective-permute-start.12 = (bf16[128,1152]{1,0:T(8,128)(2,1)S(1)}, bf16[128,1152]{1,0:T(8,128)(2,1)S(1)}, u32[]{:S(2)}, u32[]{:S(2)}) collective-permute-start(bf16[128,1152]{1,0:T(8,128)(2,1)S(1)} %collective-permute-done.11), channel_id=1, source_target_pairs={{0,32},{1,481},{32,64},{33,1},{64,96},{65,33},{96,128},{97,65},{12... | collective-permute-start | bytes 884744 | tf_op jit(solution)/shard_map/ppermute | solution.py:28
  62.5 8.7 %collective-permute-start.15 = (bf16[128,1152]{1,0:T(8,128)(2,1)S(1)}, bf16[128,1152]{1,0:T(8,128)(2,1)S(1)}, u32[]{:S(2)}, u32[]{:S(2)}) collective-permute-start(bf16[128,1152]{1,0:T(8,128)(2,1)S(1)} %collective-permute-done.14), channel_id=1, source_target_pairs={{0,32},{1,481},{32,64},{33,1},{64,96},{65,33},{96,128},{97,65},{12... | collective-permute-start | bytes 884744 | tf_op jit(solution)/shard_map/ppermute | solution.py:28
  66.1 11.0 %collective-permute-start.16 = (bf16[128,1152]{1,0:T(8,128)(2,1)S(1)}, bf16[128,1152]{1,0:T(8,128)(2,1)S(1)}, u32[]{:S(2)}, u32[]{:S(2)}) collective-permute-start(bf16[128,1152]{1,0:T(8,128)(2,1)S(1)} %collective-permute-done.12), channel_id=1, source_target_pairs={{0,32},{1,481},{32,64},{33,1},{64,96},{65,33},{96,128},{97,65},{12... | collective-permute-start | bytes 884744 | tf_op jit(solution)/shard_map/ppermute | solution.py:28
  71.2 10.8 %collective-permute-start.19 = (bf16[128,1152]{1,0:T(8,128)(2,1)S(1)}, bf16[128,1152]{1,0:T(8,128)(2,1)S(1)}, u32[]{:S(2)}, u32[]{:S(2)}) collective-permute-start(bf16[128,1152]{1,0:T(8,128)(2,1)S(1)} %collective-permute-done.15), channel_id=1, source_target_pairs={{0,32},{1,481},{32,64},{33,1},{64,96},{65,33},{96,128},{97,65},{12... | collective-permute-start | bytes 884744 | tf_op jit(solution)/shard_map/ppermute | solution.py:28
  74.4 17.2 %collective-permute-start.13 = (bf16[2,128,1152]{2,1,0:T(8,128)(2,1)S(1)}, bf16[2,128,1152]{2,1,0:T(8,128)(2,1)S(1)}, u32[]{:S(2)}, u32[]{:S(2)}) collective-permute-start(bf16[2,128,1152]{2,1,0:T(8,128)(2,1)S(1)} %pad_maximum_fusion.2), channel_id=1, source_target_pairs={{0,1},{1,0},{2,3},{3,2},{4,5},{5,4},{6,7},{7,6},{8,9},{9,8},{10,11... | collective-permute-start | bytes 1769480 | tf_op jit(solution)/shard_map/ppermute | solution.py:53
  77.1 8.5 %collective-permute-start.17 = (bf16[128,1152]{1,0:T(8,128)(2,1)S(1)}, bf16[128,1152]{1,0:T(8,128)(2,1)S(1)}, u32[]{:S(2)}, u32[]{:S(2)}) collective-permute-start(bf16[128,1152]{1,0:T(8,128)(2,1)S(1)} %collective-permute-done.16), channel_id=1, source_target_pairs={{0,32},{1,481},{32,64},{33,1},{64,96},{65,33},{96,128},{97,65},{12... | collective-permute-start | bytes 884744 | tf_op jit(solution)/shard_map/ppermute | solution.py:28
  82.0 11.4 %collective-permute-start.20 = (bf16[128,1152]{1,0:T(8,128)(2,1)S(1)}, bf16[128,1152]{1,0:T(8,128)(2,1)S(1)}, u32[]{:S(2)}, u32[]{:S(2)}) collective-permute-start(bf16[128,1152]{1,0:T(8,128)(2,1)S(1)} %collective-permute-done.19), channel_id=1, source_target_pairs={{0,32},{1,481},{32,64},{33,1},{64,96},{65,33},{96,128},{97,65},{12... | collective-permute-start | bytes 884744 | tf_op jit(solution)/shard_map/ppermute | solution.py:28
  85.7 7.5 %collective-permute-start.18 = (bf16[2,128,1152]{2,1,0:T(8,128)(2,1)S(1)}, bf16[2,128,1152]{2,1,0:T(8,128)(2,1)S(1)}, u32[]{:S(2)}, u32[]{:S(2)}) collective-permute-start(bf16[2,128,1152]{2,1,0:T(8,128)(2,1)S(1)} %pad_maximum_fusion.3), channel_id=1, source_target_pairs={{0,1},{1,0},{2,3},{3,2},{4,5},{5,4},{6,7},{7,6},{8,9},{9,8},{10,11... | collective-permute-start | bytes 1769480 | tf_op jit(solution)/shard_map/ppermute | solution.py:53
  93.4 2.1 %copy-start = (bf16[16,128,1152]{2,1,0:T(8,128)(2,1)}, bf16[16,128,1152]{2,1,0:T(8,128)(2,1)S(1)}, u32[]{:S(2)}) copy-start(bf16[16,128,1152]{2,1,0:T(8,128)(2,1)S(1)} %bitcast_dynamic-update-slice_fusion) | copy-start | bytes 14155780
  121.5 28.8 %all-to-all-start.1 = ((bf16[16,256,128]{2,1,0:T(8,128)(2,1)}), bf16[16,256,128]{2,1,0:T(8,128)(2,1)S(1)}, u32[]{:S(2)}, u32[]{:S(2)}) async-start(bf16[16,256,128]{2,1,0:T(8,128)(2,1)} %broadcast_in_dim.79), calls=%async_computation.1 | async-start | bytes 2097152 | tf_op jit(solution)/shard_map/all_to_all | solution.py:17
  141.8 19.3 %collective-permute-start.23 = (bf16[4,256,128]{2,1,0:T(8,128)(2,1)S(1)}, bf16[4,256,128]{2,1,0:T(8,128)(2,1)S(1)}, u32[]{:S(2)}, u32[]{:S(2)}) collective-permute-start(bf16[4,256,128]{2,1,0:T(8,128)(2,1)S(1)} %bitcast.107), channel_id=1, source_target_pairs={{0,32},{1,33},{32,64},{33,65},{64,96},{65,97},{96,128},{97,129},{1... | collective-permute-start | bytes 786440 | tf_op jit(solution)/shard_map/ppermute | solution.py:28
  143.8 17.1 %collective-permute-start.22 = (bf16[4,256,128]{2,1,0:T(8,128)(2,1)S(1)}, bf16[4,256,128]{2,1,0:T(8,128)(2,1)S(1)}, u32[]{:S(2)}, u32[]{:S(2)}) collective-permute-start(bf16[4,256,128]{2,1,0:T(8,128)(2,1)S(1)} %bitcast.108), channel_id=1, source_target_pairs={{0,480},{1,481},{32,0},{33,1},{64,32},{65,33},{96,64},{97,65},{128... | collective-permute-start | bytes 786440 | tf_op jit(solution)/shard_map/ppermute | solution.py:28
  148.3 12.3 %collective-permute-start.21 = (bf16[4,256,128]{2,1,0:T(8,128)(2,1)S(1)}, bf16[4,256,128]{2,1,0:T(8,128)(2,1)S(1)}, u32[]{:S(2)}, u32[]{:S(2)}) collective-permute-start(bf16[4,256,128]{2,1,0:T(8,128)(2,1)S(1)} %bitcast.109), channel_id=1, source_target_pairs={{0,448},{1,65},{32,480},{33,97},{64,0},{65,129},{96,32},{97,161},{... | collective-permute-start | bytes 786440 | tf_op jit(solution)/shard_map/ppermute | solution.py:28
  150.4 10.9 %collective-permute-start.25 = (bf16[2,4,256,128]{3,2,1,0:T(8,128)(2,1)S(1)}, bf16[2,4,256,128]{3,2,1,0:T(8,128)(2,1)S(1)}, u32[]{:S(2)}, u32[]{:S(2)}) collective-permute-start(bf16[2,4,256,128]{3,2,1,0:T(8,128)(2,1)S(1)} %pad_maximum_fusion.5), channel_id=1, source_target_pairs={{0,1},{1,0},{2,3},{3,2},{4,5},{5,4},{6,7},{7,6},{8,9},{9,8},{10,11... | collective-permute-start | bytes 1572872 | tf_op jit(solution)/shard_map/ppermute | solution.py:53
  158.4 26.2 %slice-start = ((s8[4718592]{0:T(1024)(128)(4,1)}), s8[4194304]{0:T(1024)(128)(4,1)S(1)}, s32[]{:S(2)}) async-start(s8[4718592]{0:T(1024)(128)(4,1)} %bitcast.100), calls=%async_computation.3 | async-start | bytes 8388608
  158.4 4.1 %collective-permute-start.24 = (bf16[2,4,256,128]{3,2,1,0:T(8,128)(2,1)S(1)}, bf16[2,4,256,128]{3,2,1,0:T(8,128)(2,1)S(1)}, u32[]{:S(2)}, u32[]{:S(2)}) collective-permute-start(bf16[2,4,256,128]{3,2,1,0:T(8,128)(2,1)S(1)} %pad_maximum_fusion.4), channel_id=1, source_target_pairs={{0,1},{1,0},{2,3},{3,2},{4,5},{5,4},{6,7},{7,6},{8,9},{9,8},{10,11... | collective-permute-start | bytes 1572872 | tf_op jit(solution)/shard_map/ppermute | solution.py:53
  162.6 22.0 %slice-start.1 = ((s8[4718592]{0:T(1024)(128)(4,1)}), s8[524288]{0:T(1024)(128)(4,1)S(1)}, s32[]{:S(2)}) async-start(s8[4718592]{0:T(1024)(128)(4,1)} %bitcast.100), calls=%async_computation.4 | async-start | bytes 1048576
  185.4 10.4 %collective-permute-start.26 = (bf16[128,1152]{1,0:T(8,128)(2,1)S(1)}, bf16[128,1152]{1,0:T(8,128)(2,1)S(1)}, u32[]{:S(2)}, u32[]{:S(2)}) collective-permute-start(bf16[128,1152]{1,0:T(8,128)(2,1)S(1)} %fusion.2), channel_id=1, source_target_pairs={{0,0},{1,16},{16,1},{17,17},{2,2},{3,18},{18,3},{19,19},{4,4},{5,2... | collective-permute-start | bytes 884744 | tf_op jit(solution)/shard_map/ppermute | solution.py:149
  192.3 7.5 %collective-permute-start.27 = (bf16[128,1152]{1,0:T(8,128)(2,1)S(1)}, bf16[128,1152]{1,0:T(8,128)(2,1)S(1)}, u32[]{:S(2)}, u32[]{:S(2)}) collective-permute-start(bf16[128,1152]{1,0:T(8,128)(2,1)S(1)} %fusion.1), channel_id=1, source_target_pairs={{0,16},{1,0},{16,17},{17,1},{2,18},{3,2},{18,19},{19,3},{4,20},{5,... | collective-permute-start | bytes 884744 | tf_op jit(solution)/shard_map/ppermute | solution.py:147

commit v19 on v18

--- a/solution.py
+++ b/solution.py
@@ -122,13 +122,13 @@
     panel, _ = lax.optimization_barrier((panel, here))
     right = (
         here,
-        along(here, -2, 2),
         along(here, -1),
         along(here, 1),
+        along(here, -2, 2),
     )
     left_own = [
         lax.dynamic_index_in_dim(panel, (residue + shift) % steps, 1, False)
-        for shift in (0, 2, 1, steps - 1)
+        for shift in (0, 1, steps - 1, 2)
     ]
     left_other = swap(left_own[:2]) + swap(left_own[2:])
     left_other = [

time: 202 us -> 202 us (level)
  transfers between devices with their start and end apart: 29 -> 29, of which waited for: 8 -> 9; matrix products, arithmetic and copies ran while one was open for 2% -> 2% of each run, Pallas kernels for 0% -> 0%
where the time goes in v19:
time: 202 us; the launch traced here: 201 us
  starting transfers between devices  112 us (55%)
  blocking collectives  63.3 us (31%)
  waiting for transfers between devices  12.4 us (6%)
  matrix products  4.99 us (2%)
  local copies, waits for them, and re-layouts  3.39 us (2%)
  other arithmetic  2.91 us (1%)
    ppermute x16, starting transfers between devices, along(): return lax.ppermute(piece, LINE + ('core',), pairs)  61.3 us
    all_to_all x1, blocking collectives, per_device(): summands = lax.all_to_all(partial_gram, PLANE, 0, 0)  24.5 us
    all_to_all x1, blocking collectives, share(): return lax.all_to_all(copies, PLANE, 0, 0)  22.2 us
    ppermute x5, starting transfers between devices, swap(): return list(lax.ppermute(jnp.stack(pieces), 'core', SWAP))  20.7 us
    all_gather x1, blocking collectives, per_device(): here = lax.all_gather(gram_low, 'zh', axis=0)  16.6 us
    ppermute x1, starting transfers between devices, per_device(): lax.ppermute(rounded, 'core', SWAP)  8.79 us
    ppermute x2, starting transfers between devices, launch(): return lax.ppermute(piece, LINE + ('ylo', 'core'), pairs)  7.67 us
    ppermute x1, starting transfers between devices, per_device(): stay = lax.ppermute(stay.astype(jnp.bfloat16), ('ylo', 'core'), TURN)  4.5 us
  transfers between devices with their start and end apart: 29, of which 9 were waited for; matrix products, arithmetic and copies ran while one was open for 2% of the time, Pallas kernels for 0%

profile of v19, /device:TPU:1, one launch (start us, length us, event | category | flops | bytes accessed | tf_op | source)
XLA Modules:
  0.0 200.6 jit_solution(15795422868750963318)
XLA Ops:
  0.0 1.1 convert_element_type.39
  1.1 8.8 %collective-permute-start.3 = (bf16[128,1152]{1,0:T(8,128)(2,1)S(1)}, bf16[128,1152]{1,0:T(8,128)(2,1)S(1)}, u32[]{:S(2)}, u32[]{:S(2)}) collective-permute-start(bf16[128,1152]{1,0:T(8,128)(2,1)S(1)} %convert_element_type.39), channel_id=1, source_target_pairs={{0,1},{1,0},{2,3},{3,2},{4,5},{5,4},{6,7},{7,6},{8,9},{9,8},{10,11... | collective-permute-start | bytes 884744 | tf_op jit(solution)/shard_map/ppermute | solution.py:83
  9.9 1.9 collective-permute-start.2
  11.8 5.7 %collective-permute-start.4 = (bf16[128,1152]{1,0:T(8,128)(2,1)S(1)}, bf16[128,1152]{1,0:T(8,128)(2,1)S(1)}, u32[]{:S(2)}, u32[]{:S(2)}) collective-permute-start(bf16[128,1152]{1,0:T(8,128)(2,1)S(1)} %collective-permute-done.3), channel_id=1, source_target_pairs={{0,497},{1,481},{16,48},{17,32},{32,17},{33,1},{48,80},{49,64},{64... | collective-permute-start | bytes 884744 | tf_op jit(solution)/shard_map/ppermute | solution.py:49
  17.6 1.5 collective-permute-done.2
  19.1 9.9 %collective-permute-start.8 = (bf16[128,1152]{1,0:T(8,128)(2,1)S(1)}, bf16[128,1152]{1,0:T(8,128)(2,1)S(1)}, u32[]{:S(2)}, u32[]{:S(2)}) collective-permute-start(bf16[128,1152]{1,0:T(8,128)(2,1)S(1)} %collective-permute-done.2), channel_id=1, source_target_pairs={{0,32},{1,481},{32,64},{33,1},{64,96},{65,33},{96,128},{97,65},{12... | collective-permute-start | bytes 884744 | tf_op jit(solution)/shard_map/ppermute | solution.py:28
  29.0 1.9 collective-permute-start
  31.0 2.7 %collective-permute-start.5 = (bf16[128,1152]{1,0:T(8,128)(2,1)S(1)}, bf16[128,1152]{1,0:T(8,128)(2,1)S(1)}, u32[]{:S(2)}, u32[]{:S(2)}) collective-permute-start(bf16[128,1152]{1,0:T(8,128)(2,1)S(1)} %collective-permute-done.4), channel_id=1, source_target_pairs={{0,32},{1,481},{32,64},{33,1},{64,96},{65,33},{96,128},{97,65},{12... | collective-permute-start | bytes 884744 | tf_op jit(solution)/shard_map/ppermute | solution.py:28
  33.7 4.0 %collective-permute-start.9 = (bf16[128,1152]{1,0:T(8,128)(2,1)S(1)}, bf16[128,1152]{1,0:T(8,128)(2,1)S(1)}, u32[]{:S(2)}, u32[]{:S(2)}) collective-permute-start(bf16[128,1152]{1,0:T(8,128)(2,1)S(1)} %collective-permute-done.8), channel_id=1, source_target_pairs={{0,32},{1,481},{32,64},{33,1},{64,96},{65,33},{96,128},{97,65},{12... | collective-permute-start | bytes 884744 | tf_op jit(solution)/shard_map/ppermute | solution.py:28
  38.1 1.9 collective-permute-start.1
  40.0 2.5 %collective-permute-start.6 = (bf16[128,1152]{1,0:T(8,128)(2,1)S(1)}, bf16[128,1152]{1,0:T(8,128)(2,1)S(1)}, u32[]{:S(2)}, u32[]{:S(2)}) collective-permute-start(bf16[128,1152]{1,0:T(8,128)(2,1)S(1)} %collective-permute-done.5), channel_id=1, source_target_pairs={{0,32},{1,481},{32,64},{33,1},{64,96},{65,33},{96,128},{97,65},{12... | collective-permute-start | bytes 884744 | tf_op jit(solution)/shard_map/ppermute | solution.py:28
  42.5 3.9 %collective-permute-start.10 = (bf16[128,1152]{1,0:T(8,128)(2,1)S(1)}, bf16[128,1152]{1,0:T(8,128)(2,1)S(1)}, u32[]{:S(2)}, u32[]{:S(2)}) collective-permute-start(bf16[128,1152]{1,0:T(8,128)(2,1)S(1)} %collective-permute-done.9), channel_id=1, source_target_pairs={{0,32},{1,481},{32,64},{33,1},{64,96},{65,33},{96,128},{97,65},{12... | collective-permute-start | bytes 884744 | tf_op jit(solution)/shard_map/ppermute | solution.py:28
  46.4 0.6 broadcast_in_dim.67
  47.1 0.7 collective-permute-done.6
  47.8 3.4 %collective-permute-start.11 = (bf16[128,1152]{1,0:T(8,128)(2,1)S(1)}, bf16[128,1152]{1,0:T(8,128)(2,1)S(1)}, u32[]{:S(2)}, u32[]{:S(2)}) collective-permute-start(bf16[128,1152]{1,0:T(8,128)(2,1)S(1)} %collective-permute-done.6), channel_id=1, source_target_pairs={{0,32},{1,481},{32,64},{33,1},{64,96},{65,33},{96,128},{97,65},{12... | collective-permute-start | bytes 884744 | tf_op jit(solution)/shard_map/ppermute | solution.py:28
  51.2 3.9 %collective-permute-start.14 = (bf16[128,1152]{1,0:T(8,128)(2,1)S(1)}, bf16[128,1152]{1,0:T(8,128)(2,1)S(1)}, u32[]{:S(2)}, u32[]{:S(2)}) collective-permute-start(bf16[128,1152]{1,0:T(8,128)(2,1)S(1)} %collective-permute-done.10), channel_id=1, source_target_pairs={{0,32},{1,481},{32,64},{33,1},{64,96},{65,33},{96,128},{97,65},{12... | collective-permute-start | bytes 884744 | tf_op jit(solution)/shard_map/ppermute | solution.py:28
  55.0 0.1 multiply_reduce_fusion
  55.2 0.1 pad_maximum_fusion.1
  55.3 2.3 %collective-permute-start.7 = (bf16[3,128,1152]{2,1,0:T(8,128)(2,1)S(1)}, bf16[3,128,1152]{2,1,0:T(8,128)(2,1)S(1)}, u32[]{:S(2)}, u32[]{:S(2)}) collective-permute-start(bf16[3,128,1152]{2,1,0:T(8,128)(2,1)S(1)} %pad_maximum_fusion.1), channel_id=1, source_target_pairs={{0,1},{1,0},{2,3},{3,2},{4,5},{5,4},{6,7},{7,6},{8,9},{9,8},{10,11... | collective-permute-start | bytes 2654216 | tf_op jit(solution)/shard_map/ppermute | solution.py:53
  57.6 4.9 %collective-permute-start.12 = (bf16[128,1152]{1,0:T(8,128)(2,1)S(1)}, bf16[128,1152]{1,0:T(8,128)(2,1)S(1)}, u32[]{:S(2)}, u32[]{:S(2)}) collective-permute-start(bf16[128,1152]{1,0:T(8,128)(2,1)S(1)} %collective-permute-done.11), channel_id=1, source_target_pairs={{0,32},{1,481},{32,64},{33,1},{64,96},{65,33},{96,128},{97,65},{12... | collective-permute-start | bytes 884744 | tf_op jit(solution)/shard_map/ppermute | solution.py:28
  62.5 2.4 %collective-permute-start.15 = (bf16[128,1152]{1,0:T(8,128)(2,1)S(1)}, bf16[128,1152]{1,0:T(8,128)(2,1)S(1)}, u32[]{:S(2)}, u32[]{:S(2)}) collective-permute-start(bf16[128,1152]{1,0:T(8,128)(2,1)S(1)} %collective-permute-done.14), channel_id=1, source_target_pairs={{0,32},{1,481},{32,64},{33,1},{64,96},{65,33},{96,128},{97,65},{12... | collective-permute-start | bytes 884744 | tf_op jit(solution)/shard_map/ppermute | solution.py:28
  64.9 1.2 collective-permute-done.12
  66.1 5.0 %collective-permute-start.16 = (bf16[128,1152]{1,0:T(8,128)(2,1)S(1)}, bf16[128,1152]{1,0:T(8,128)(2,1)S(1)}, u32[]{:S(2)}, u32[]{:S(2)}) collective-permute-start(bf16[128,1152]{1,0:T(8,128)(2,1)S(1)} %collective-permute-done.12), channel_id=1, source_target_pairs={{0,32},{1,481},{32,64},{33,1},{64,96},{65,33},{96,128},{97,65},{12... | collective-permute-start | bytes 884744 | tf_op jit(solution)/shard_map/ppermute | solution.py:28
  71.2 3.1 %collective-permute-start.19 = (bf16[128,1152]{1,0:T(8,128)(2,1)S(1)}, bf16[128,1152]{1,0:T(8,128)(2,1)S(1)}, u32[]{:S(2)}, u32[]{:S(2)}) collective-permute-start(bf16[128,1152]{1,0:T(8,128)(2,1)S(1)} %collective-permute-done.15), channel_id=1, source_target_pairs={{0,32},{1,481},{32,64},{33,1},{64,96},{65,33},{96,128},{97,65},{12... | collective-permute-start | bytes 884744 | tf_op jit(solution)/shard_map/ppermute | solution.py:28
  74.3 0.1 pad_maximum_fusion.2
  74.4 2.7 %collective-permute-start.13 = (bf16[2,128,1152]{2,1,0:T(8,128)(2,1)S(1)}, bf16[2,128,1152]{2,1,0:T(8,128)(2,1)S(1)}, u32[]{:S(2)}, u32[]{:S(2)}) collective-permute-start(bf16[2,128,1152]{2,1,0:T(8,128)(2,1)S(1)} %pad_maximum_fusion.2), channel_id=1, source_target_pairs={{0,1},{1,0},{2,3},{3,2},{4,5},{5,4},{6,7},{7,6},{8,9},{9,8},{10,11... | collective-permute-start | bytes 1769480 | tf_op jit(solution)/shard_map/ppermute | solution.py:53
  77.1 4.9 %collective-permute-start.17 = (bf16[128,1152]{1,0:T(8,128)(2,1)S(1)}, bf16[128,1152]{1,0:T(8,128)(2,1)S(1)}, u32[]{:S(2)}, u32[]{:S(2)}) collective-permute-start(bf16[128,1152]{1,0:T(8,128)(2,1)S(1)} %collective-permute-done.16), channel_id=1, source_target_pairs={{0,32},{1,481},{32,64},{33,1},{64,96},{65,33},{96,128},{97,65},{12... | collective-permute-start | bytes 884744 | tf_op jit(solution)/shard_map/ppermute | solution.py:28
  82.0 2.4 %collective-permute-start.20 = (bf16[128,1152]{1,0:T(8,128)(2,1)S(1)}, bf16[128,1152]{1,0:T(8,128)(2,1)S(1)}, u32[]{:S(2)}, u32[]{:S(2)}) collective-permute-start(bf16[128,1152]{1,0:T(8,128)(2,1)S(1)} %collective-permute-done.19), channel_id=1, source_target_pairs={{0,32},{1,481},{32,64},{33,1},{64,96},{65,33},{96,128},{97,65},{12... | collective-permute-start | bytes 884744 | tf_op jit(solution)/shard_map/ppermute | solution.py:28
  84.7 0.9 collective-permute-done.17
  85.7 5.9 %collective-permute-start.18 = (bf16[2,128,1152]{2,1,0:T(8,128)(2,1)S(1)}, bf16[2,128,1152]{2,1,0:T(8,128)(2,1)S(1)}, u32[]{:S(2)}, u32[]{:S(2)}) collective-permute-start(bf16[2,128,1152]{2,1,0:T(8,128)(2,1)S(1)} %pad_maximum_fusion.3), channel_id=1, source_target_pairs={{0,1},{1,0},{2,3},{3,2},{4,5},{5,4},{6,7},{7,6},{8,9},{9,8},{10,11... | collective-permute-start | bytes 1769480 | tf_op jit(solution)/shard_map/ppermute | solution.py:53
  91.8 1.4 collective-permute-done.18
  93.4 1.6 fusion.3
  95.0 0.5 copy-done
  95.5 0.1 pad_maximum_fusion
  95.6 24.5 %all_to_all.15 = bf16[16,264,128]{2,1,0:T(8,128)(2,1)S(1)} all-to-all(bf16[16,264,128]{2,1,0:T(8,128)(2,1)S(1)} %pad_maximum_fusion), channel_id=1, replica_groups=mesh['zh'=4,'zl'=4,'ylo'=2,'x'=4,'yhi'=2,'core'=2] {'ylo','yhi','x'}, dimensions={0} | all-to-all | bytes 2162688 | tf_op jit(solution)/shard_map/all_to_all | solution.py:109
  120.1 0.1 convert_reduce_fusion
  120.3 1.2 broadcast_in_dim.79
  121.5 3.7 %all-to-all-start.1 = ((bf16[16,256,128]{2,1,0:T(8,128)(2,1)}), bf16[16,256,128]{2,1,0:T(8,128)(2,1)S(1)}, u32[]{:S(2)}, u32[]{:S(2)}) async-start(bf16[16,256,128]{2,1,0:T(8,128)(2,1)} %broadcast_in_dim.79), calls=%async_computation.1 | async-start | bytes 2097152 | tf_op jit(solution)/shard_map/all_to_all | solution.py:17
  125.2 16.6 %all-gather = bf16[1024,128]{1,0:T(8,128)(2,1)S(1)} all-gather(bf16[256,128]{1,0:T(8,128)(2,1)S(1)} %fusion.39), channel_id=2, replica_groups=mesh['zh'=4,'zl'=4,'ylo'=2,'x'=4,'yhi'=2,'core'=2] {'zh'}, dimensions={0}, use_global_device_ids=true | all-gather | bytes 327680 | tf_op jit(solution)/shard_map/all_gather | solution.py:121
  141.8 1.9 collective-permute-start.23
  143.8 2.7 %collective-permute-start.22 = (bf16[4,256,128]{2,1,0:T(8,128)(2,1)S(1)}, bf16[4,256,128]{2,1,0:T(8,128)(2,1)S(1)}, u32[]{:S(2)}, u32[]{:S(2)}) collective-permute-start(bf16[4,256,128]{2,1,0:T(8,128)(2,1)S(1)} %bitcast.108), channel_id=1, source_target_pairs={{0,32},{1,33},{32,64},{33,65},{64,96},{65,97},{96,128},{97,129},{1... | collective-permute-start | bytes 786440 | tf_op jit(solution)/shard_map/ppermute | solution.py:28
  146.5 3.8 %collective-permute-start.21 = (bf16[4,256,128]{2,1,0:T(8,128)(2,1)S(1)}, bf16[4,256,128]{2,1,0:T(8,128)(2,1)S(1)}, u32[]{:S(2)}, u32[]{:S(2)}) collective-permute-start(bf16[4,256,128]{2,1,0:T(8,128)(2,1)S(1)} %bitcast.109), channel_id=1, source_target_pairs={{0,480},{1,481},{32,0},{33,1},{64,32},{65,33},{96,64},{97,65},{128... | collective-permute-start | bytes 786440 | tf_op jit(solution)/shard_map/ppermute | solution.py:28
  150.3 0.1 dynamic-slice_bitcast_fusion.1
  150.4 7.7 %collective-permute-start.25 = (bf16[2,4,256,128]{3,2,1,0:T(8,128)(2,1)S(1)}, bf16[2,4,256,128]{3,2,1,0:T(8,128)(2,1)S(1)}, u32[]{:S(2)}, u32[]{:S(2)}) collective-permute-start(bf16[2,4,256,128]{3,2,1,0:T(8,128)(2,1)S(1)} %pad_maximum_fusion.5), channel_id=1, source_target_pairs={{0,1},{1,0},{2,3},{3,2},{4,5},{5,4},{6,7},{7,6},{8,9},{9,8},{10,11... | collective-permute-start | bytes 1572872 | tf_op jit(solution)/shard_map/ppermute | solution.py:53
  158.1 0.2 convolution_bitcast_fusion.9
  158.4 2.2 %collective-permute-start.24 = (bf16[2,4,256,128]{3,2,1,0:T(8,128)(2,1)S(1)}, bf16[2,4,256,128]{3,2,1,0:T(8,128)(2,1)S(1)}, u32[]{:S(2)}, u32[]{:S(2)}) collective-permute-start(bf16[2,4,256,128]{3,2,1,0:T(8,128)(2,1)S(1)} %pad_maximum_fusion.4), channel_id=1, source_target_pairs={{0,1},{1,0},{2,3},{3,2},{4,5},{5,4},{6,7},{7,6},{8,9},{9,8},{10,11... | collective-permute-start | bytes 1572872 | tf_op jit(solution)/shard_map/ppermute | solution.py:53
  160.6 0.5 collective-permute-done.21
  161.1 0.2 fusion.4
  161.3 0.2 convolution_bitcast_fusion.7
  161.6 0.2 convolution_bitcast_fusion.6
  161.9 0.6 collective-permute-done.24
  162.6 0.2 convolution_bitcast_fusion.5
  162.8 0.2 fusion.5
  163.1 0.2 convolution_bitcast_fusion.3
  163.3 0.2 convolution_bitcast_fusion.2
  163.6 0.2 broadcast_in_dim.81
  163.8 22.2 %all_to_all.16 = bf16[16,256,128]{2,1,0:T(8,128)(2,1)S(1)} all-to-all(bf16[16,256,128]{2,1,0:T(8,128)(2,1)S(1)} %broadcast_in_dim.81), channel_id=1, replica_groups=mesh['zh'=4,'zl'=4,'ylo'=2,'x'=4,'yhi'=2,'core'=2] {'ylo','yhi','x'}, dimensions={0} | all-to-all | bytes 2097152 | tf_op jit(solution)/shard_map/all_to_all | solution.py:17
  186.0 0.9 fusion.2
  186.9 4.5 %collective-permute-start.26 = (bf16[128,1152]{1,0:T(8,128)(2,1)S(1)}, bf16[128,1152]{1,0:T(8,128)(2,1)S(1)}, u32[]{:S(2)}, u32[]{:S(2)}) collective-permute-start(bf16[128,1152]{1,0:T(8,128)(2,1)S(1)} %fusion.2), channel_id=1, source_target_pairs={{0,0},{1,16},{16,1},{17,17},{2,2},{3,18},{18,3},{19,19},{4,4},{5,2... | collective-permute-start | bytes 884744 | tf_op jit(solution)/shard_map/ppermute | solution.py:149
  191.4 0.9 fusion.1
  192.3 1.9 collective-permute-start.27
  194.2 1.6 collective-permute-done.26
  195.8 3.9 %collective-permute-done.27 = bf16[128,1152]{1,0:T(8,128)(2,1)S(1)} collective-permute-done((bf16[128,1152]{1,0:T(8,128)(2,1)S(1)}, bf16[128,1152]{1,0:T(8,128)(2,1)S(1)}, u32[]{:S(2)}, u32[]{:S(2)}) %collective-permute-start.27) | collective-permute-done | bytes 294944 | tf_op jit(solution)/shard_map/ppermute | solution.py:147
  199.7 0.9 convert_add_fusion
  (63 shorter events, 1.2 us)
Async XLA Ops:
  1.1 10.7 %collective-permute-start.3 = (bf16[128,1152]{1,0:T(8,128)(2,1)S(1)}, bf16[128,1152]{1,0:T(8,128)(2,1)S(1)}, u32[]{:S(2)}, u32[]{:S(2)}) collective-permute-start(bf16[128,1152]{1,0:T(8,128)(2,1)S(1)} %convert_element_type.39), channel_id=1, source_target_pairs={{0,1},{1,0},{2,3},{3,2},{4,5},{5,4},{6,7},{7,6},{8,9},{9,8},{10,11... | collective-permute-start | bytes 884744 | tf_op jit(solution)/shard_map/ppermute | solution.py:83
  9.9 9.2 %collective-permute-start.2 = (bf16[128,1152]{1,0:T(8,128)(2,1)S(1)}, bf16[128,1152]{1,0:T(8,128)(2,1)S(1)}, u32[]{:S(2)}, u32[]{:S(2)}) collective-permute-start(bf16[128,1152]{1,0:T(8,128)(2,1)S(1)} %convert_element_type.39), channel_id=1, source_target_pairs={{0,32},{1,48},{16,481},{17,497},{32,64},{33,80},{48,1},{49,17},{64... | collective-permute-start | bytes 884744 | tf_op jit(solution)/shard_map/ppermute | solution.py:49
  11.8 19.1 %collective-permute-start.4 = (bf16[128,1152]{1,0:T(8,128)(2,1)S(1)}, bf16[128,1152]{1,0:T(8,128)(2,1)S(1)}, u32[]{:S(2)}, u32[]{:S(2)}) collective-permute-start(bf16[128,1152]{1,0:T(8,128)(2,1)S(1)} %collective-permute-done.3), channel_id=1, source_target_pairs={{0,497},{1,481},{16,48},{17,32},{32,17},{33,1},{48,80},{49,64},{64... | collective-permute-start | bytes 884744 | tf_op jit(solution)/shard_map/ppermute | solution.py:49
  19.1 14.6 %collective-permute-start.8 = (bf16[128,1152]{1,0:T(8,128)(2,1)S(1)}, bf16[128,1152]{1,0:T(8,128)(2,1)S(1)}, u32[]{:S(2)}, u32[]{:S(2)}) collective-permute-start(bf16[128,1152]{1,0:T(8,128)(2,1)S(1)} %collective-permute-done.2), channel_id=1, source_target_pairs={{0,32},{1,481},{32,64},{33,1},{64,96},{65,33},{96,128},{97,65},{12... | collective-permute-start | bytes 884744 | tf_op jit(solution)/shard_map/ppermute | solution.py:28
  29.0 9.0 %collective-permute-start = (bf16[128,1152]{1,0:T(8,128)(2,1)S(1)}, bf16[128,1152]{1,0:T(8,128)(2,1)S(1)}, u32[]{:S(2)}, u32[]{:S(2)}) collective-permute-start(bf16[128,1152]{1,0:T(8,128)(2,1)S(1)} %convert_element_type.39), channel_id=1, source_target_pairs={{0,0},{1,16},{16,1},{17,17},{2,2},{3,18},{18,3},{19,19},{4,4},{5,2... | collective-permute-start | bytes 884744 | tf_op jit(solution)/shard_map/ppermute | solution.py:80
  31.0 9.0 %collective-permute-start.5 = (bf16[128,1152]{1,0:T(8,128)(2,1)S(1)}, bf16[128,1152]{1,0:T(8,128)(2,1)S(1)}, u32[]{:S(2)}, u32[]{:S(2)}) collective-permute-start(bf16[128,1152]{1,0:T(8,128)(2,1)S(1)} %collective-permute-done.4), channel_id=1, source_target_pairs={{0,32},{1,481},{32,64},{33,1},{64,96},{65,33},{96,128},{97,65},{12... | collective-permute-start | bytes 884744 | tf_op jit(solution)/shard_map/ppermute | solution.py:28
  33.7 8.8 %collective-permute-start.9 = (bf16[128,1152]{1,0:T(8,128)(2,1)S(1)}, bf16[128,1152]{1,0:T(8,128)(2,1)S(1)}, u32[]{:S(2)}, u32[]{:S(2)}) collective-permute-start(bf16[128,1152]{1,0:T(8,128)(2,1)S(1)} %collective-permute-done.8), channel_id=1, source_target_pairs={{0,32},{1,481},{32,64},{33,1},{64,96},{65,33},{96,128},{97,65},{12... | collective-permute-start | bytes 884744 | tf_op jit(solution)/shard_map/ppermute | solution.py:28
  38.1 55.3 %collective-permute-start.1 = (bf16[128,1152]{1,0:T(8,128)(2,1)S(1)}, bf16[128,1152]{1,0:T(8,128)(2,1)S(1)}, u32[]{:S(2)}, u32[]{:S(2)}) collective-permute-start(bf16[128,1152]{1,0:T(8,128)(2,1)S(1)} %collective-permute-done), channel_id=1, source_target_pairs={{0,1},{1,0},{2,3},{3,2},{4,5},{5,4},{6,7},{7,6},{8,9},{9,8},{10,11... | collective-permute-start | bytes 884744 | tf_op jit(solution)/shard_map/ppermute | solution.py:81
  40.0 7.8 %collective-permute-start.6 = (bf16[128,1152]{1,0:T(8,128)(2,1)S(1)}, bf16[128,1152]{1,0:T(8,128)(2,1)S(1)}, u32[]{:S(2)}, u32[]{:S(2)}) collective-permute-start(bf16[128,1152]{1,0:T(8,128)(2,1)S(1)} %collective-permute-done.5), channel_id=1, source_target_pairs={{0,32},{1,481},{32,64},{33,1},{64,96},{65,33},{96,128},{97,65},{12... | collective-permute-start | bytes 884744 | tf_op jit(solution)/shard_map/ppermute | solution.py:28
  42.5 8.7 %collective-permute-start.10 = (bf16[128,1152]{1,0:T(8,128)(2,1)S(1)}, bf16[128,1152]{1,0:T(8,128)(2,1)S(1)}, u32[]{:S(2)}, u32[]{:S(2)}) collective-permute-start(bf16[128,1152]{1,0:T(8,128)(2,1)S(1)} %collective-permute-done.9), channel_id=1, source_target_pairs={{0,32},{1,481},{32,64},{33,1},{64,96},{65,33},{96,128},{97,65},{12... | collective-permute-start | bytes 884744 | tf_op jit(solution)/shard_map/ppermute | solution.py:28
  47.8 9.8 %collective-permute-start.11 = (bf16[128,1152]{1,0:T(8,128)(2,1)S(1)}, bf16[128,1152]{1,0:T(8,128)(2,1)S(1)}, u32[]{:S(2)}, u32[]{:S(2)}) collective-permute-start(bf16[128,1152]{1,0:T(8,128)(2,1)S(1)} %collective-permute-done.6), channel_id=1, source_target_pairs={{0,32},{1,481},{32,64},{33,1},{64,96},{65,33},{96,128},{97,65},{12... | collective-permute-start | bytes 884744 | tf_op jit(solution)/shard_map/ppermute | solution.py:28
  51.2 11.3 %collective-permute-start.14 = (bf16[128,1152]{1,0:T(8,128)(2,1)S(1)}, bf16[128,1152]{1,0:T(8,128)(2,1)S(1)}, u32[]{:S(2)}, u32[]{:S(2)}) collective-permute-start(bf16[128,1152]{1,0:T(8,128)(2,1)S(1)} %collective-permute-done.10), channel_id=1, source_target_pairs={{0,32},{1,481},{32,64},{33,1},{64,96},{65,33},{96,128},{97,65},{12... | collective-permute-start | bytes 884744 | tf_op jit(solution)/shard_map/ppermute | solution.py:28
  55.3 29.1 %collective-permute-start.7 = (bf16[3,128,1152]{2,1,0:T(8,128)(2,1)S(1)}, bf16[3,128,1152]{2,1,0:T(8,128)(2,1)S(1)}, u32[]{:S(2)}, u32[]{:S(2)}) collective-permute-start(bf16[3,128,1152]{2,1,0:T(8,128)(2,1)S(1)} %pad_maximum_fusion.1), channel_id=1, source_target_pairs={{0,1},{1,0},{2,3},{3,2},{4,5},{5,4},{6,7},{7,6},{8,9},{9,8},{10,11... | collective-permute-start | bytes 2654216 | tf_op jit(solution)/shard_map/ppermute | solution.py:53
  57.6 8.5 %collective-permute-start.12 = (bf16[128,1152]{1,0:T(8,128)(2,1)S(1)}, bf16[128,1152]{1,0:T(8,128)(2,1)S(1)}, u32[]{:S(2)}, u32[]{:S(2)}) collective-permute-start(bf16[128,1152]{1,0:T(8,128)(2,1)S(1)} %collective-permute-done.11), channel_id=1, source_target_pairs={{0,32},{1,481},{32,64},{33,1},{64,96},{65,33},{96,128},{97,65},{12... | collective-permute-start | bytes 884744 | tf_op jit(solution)/shard_map/ppermute | solution.py:28
  62.5 8.7 %collective-permute-start.15 = (bf16[128,1152]{1,0:T(8,128)(2,1)S(1)}, bf16[128,1152]{1,0:T(8,128)(2,1)S(1)}, u32[]{:S(2)}, u32[]{:S(2)}) collective-permute-start(bf16[128,1152]{1,0:T(8,128)(2,1)S(1)} %collective-permute-done.14), channel_id=1, source_target_pairs={{0,32},{1,481},{32,64},{33,1},{64,96},{65,33},{96,128},{97,65},{12... | collective-permute-start | bytes 884744 | tf_op jit(solution)/shard_map/ppermute | solution.py:28
  66.1 11.0 %collective-permute-start.16 = (bf16[128,1152]{1,0:T(8,128)(2,1)S(1)}, bf16[128,1152]{1,0:T(8,128)(2,1)S(1)}, u32[]{:S(2)}, u32[]{:S(2)}) collective-permute-start(bf16[128,1152]{1,0:T(8,128)(2,1)S(1)} %collective-permute-done.12), channel_id=1, source_target_pairs={{0,32},{1,481},{32,64},{33,1},{64,96},{65,33},{96,128},{97,65},{12... | collective-permute-start | bytes 884744 | tf_op jit(solution)/shard_map/ppermute | solution.py:28
  71.2 10.8 %collective-permute-start.19 = (bf16[128,1152]{1,0:T(8,128)(2,1)S(1)}, bf16[128,1152]{1,0:T(8,128)(2,1)S(1)}, u32[]{:S(2)}, u32[]{:S(2)}) collective-permute-start(bf16[128,1152]{1,0:T(8,128)(2,1)S(1)} %collective-permute-done.15), channel_id=1, source_target_pairs={{0,32},{1,481},{32,64},{33,1},{64,96},{65,33},{96,128},{97,65},{12... | collective-permute-start | bytes 884744 | tf_op jit(solution)/shard_map/ppermute | solution.py:28
  74.4 17.2 %collective-permute-start.13 = (bf16[2,128,1152]{2,1,0:T(8,128)(2,1)S(1)}, bf16[2,128,1152]{2,1,0:T(8,128)(2,1)S(1)}, u32[]{:S(2)}, u32[]{:S(2)}) collective-permute-start(bf16[2,128,1152]{2,1,0:T(8,128)(2,1)S(1)} %pad_maximum_fusion.2), channel_id=1, source_target_pairs={{0,1},{1,0},{2,3},{3,2},{4,5},{5,4},{6,7},{7,6},{8,9},{9,8},{10,11... | collective-permute-start | bytes 1769480 | tf_op jit(solution)/shard_map/ppermute | solution.py:53
  77.1 8.5 %collective-permute-start.17 = (bf16[128,1152]{1,0:T(8,128)(2,1)S(1)}, bf16[128,1152]{1,0:T(8,128)(2,1)S(1)}, u32[]{:S(2)}, u32[]{:S(2)}) collective-permute-start(bf16[128,1152]{1,0:T(8,128)(2,1)S(1)} %collective-permute-done.16), channel_id=1, source_target_pairs={{0,32},{1,481},{32,64},{33,1},{64,96},{65,33},{96,128},{97,65},{12... | collective-permute-start | bytes 884744 | tf_op jit(solution)/shard_map/ppermute | solution.py:28
  82.0 11.4 %collective-permute-start.20 = (bf16[128,1152]{1,0:T(8,128)(2,1)S(1)}, bf16[128,1152]{1,0:T(8,128)(2,1)S(1)}, u32[]{:S(2)}, u32[]{:S(2)}) collective-permute-start(bf16[128,1152]{1,0:T(8,128)(2,1)S(1)} %collective-permute-done.19), channel_id=1, source_target_pairs={{0,32},{1,481},{32,64},{33,1},{64,96},{65,33},{96,128},{97,65},{12... | collective-permute-start | bytes 884744 | tf_op jit(solution)/shard_map/ppermute | solution.py:28
  85.7 7.5 %collective-permute-start.18 = (bf16[2,128,1152]{2,1,0:T(8,128)(2,1)S(1)}, bf16[2,128,1152]{2,1,0:T(8,128)(2,1)S(1)}, u32[]{:S(2)}, u32[]{:S(2)}) collective-permute-start(bf16[2,128,1152]{2,1,0:T(8,128)(2,1)S(1)} %pad_maximum_fusion.3), channel_id=1, source_target_pairs={{0,1},{1,0},{2,3},{3,2},{4,5},{5,4},{6,7},{7,6},{8,9},{9,8},{10,11... | collective-permute-start | bytes 1769480 | tf_op jit(solution)/shard_map/ppermute | solution.py:53
  93.4 2.1 %copy-start = (bf16[16,128,1152]{2,1,0:T(8,128)(2,1)}, bf16[16,128,1152]{2,1,0:T(8,128)(2,1)S(1)}, u32[]{:S(2)}) copy-start(bf16[16,128,1152]{2,1,0:T(8,128)(2,1)S(1)} %bitcast_dynamic-update-slice_fusion) | copy-start | bytes 14155780
  121.5 28.8 %all-to-all-start.1 = ((bf16[16,256,128]{2,1,0:T(8,128)(2,1)}), bf16[16,256,128]{2,1,0:T(8,128)(2,1)S(1)}, u32[]{:S(2)}, u32[]{:S(2)}) async-start(bf16[16,256,128]{2,1,0:T(8,128)(2,1)} %broadcast_in_dim.79), calls=%async_computation.1 | async-start | bytes 2097152 | tf_op jit(solution)/shard_map/all_to_all | solution.py:17
  141.8 19.7 %collective-permute-start.23 = (bf16[4,256,128]{2,1,0:T(8,128)(2,1)S(1)}, bf16[4,256,128]{2,1,0:T(8,128)(2,1)S(1)}, u32[]{:S(2)}, u32[]{:S(2)}) collective-permute-start(bf16[4,256,128]{2,1,0:T(8,128)(2,1)S(1)} %bitcast.107), channel_id=1, source_target_pairs={{0,448},{1,65},{32,480},{33,97},{64,0},{65,129},{96,32},{97,161},{... | collective-permute-start | bytes 786440 | tf_op jit(solution)/shard_map/ppermute | solution.py:28
  143.8 17.6 %collective-permute-start.22 = (bf16[4,256,128]{2,1,0:T(8,128)(2,1)S(1)}, bf16[4,256,128]{2,1,0:T(8,128)(2,1)S(1)}, u32[]{:S(2)}, u32[]{:S(2)}) collective-permute-start(bf16[4,256,128]{2,1,0:T(8,128)(2,1)S(1)} %bitcast.108), channel_id=1, source_target_pairs={{0,32},{1,33},{32,64},{33,65},{64,96},{65,97},{96,128},{97,129},{1... | collective-permute-start | bytes 786440 | tf_op jit(solution)/shard_map/ppermute | solution.py:28
  146.5 14.6 %collective-permute-start.21 = (bf16[4,256,128]{2,1,0:T(8,128)(2,1)S(1)}, bf16[4,256,128]{2,1,0:T(8,128)(2,1)S(1)}, u32[]{:S(2)}, u32[]{:S(2)}) collective-permute-start(bf16[4,256,128]{2,1,0:T(8,128)(2,1)S(1)} %bitcast.109), channel_id=1, source_target_pairs={{0,480},{1,481},{32,0},{33,1},{64,32},{65,33},{96,64},{97,65},{128... | collective-permute-start | bytes 786440 | tf_op jit(solution)/shard_map/ppermute | solution.py:28
  150.4 11.4 %collective-permute-start.25 = (bf16[2,4,256,128]{3,2,1,0:T(8,128)(2,1)S(1)}, bf16[2,4,256,128]{3,2,1,0:T(8,128)(2,1)S(1)}, u32[]{:S(2)}, u32[]{:S(2)}) collective-permute-start(bf16[2,4,256,128]{3,2,1,0:T(8,128)(2,1)S(1)} %pad_maximum_fusion.5), channel_id=1, source_target_pairs={{0,1},{1,0},{2,3},{3,2},{4,5},{5,4},{6,7},{7,6},{8,9},{9,8},{10,11... | collective-permute-start | bytes 1572872 | tf_op jit(solution)/shard_map/ppermute | solution.py:53
  158.4 27.7 %slice-start = ((s8[4718592]{0:T(1024)(128)(4,1)}), s8[4194304]{0:T(1024)(128)(4,1)S(1)}, s32[]{:S(2)}) async-start(s8[4718592]{0:T(1024)(128)(4,1)} %bitcast.100), calls=%async_computation.3 | async-start | bytes 8388608
  158.4 4.1 %collective-permute-start.24 = (bf16[2,4,256,128]{3,2,1,0:T(8,128)(2,1)S(1)}, bf16[2,4,256,128]{3,2,1,0:T(8,128)(2,1)S(1)}, u32[]{:S(2)}, u32[]{:S(2)}) collective-permute-start(bf16[2,4,256,128]{3,2,1,0:T(8,128)(2,1)S(1)} %pad_maximum_fusion.4), channel_id=1, source_target_pairs={{0,1},{1,0},{2,3},{3,2},{4,5},{5,4},{6,7},{7,6},{8,9},{9,8},{10,11... | collective-permute-start | bytes 1572872 | tf_op jit(solution)/shard_map/ppermute | solution.py:53
  162.6 23.5 %slice-start.1 = ((s8[4718592]{0:T(1024)(128)(4,1)}), s8[524288]{0:T(1024)(128)(4,1)S(1)}, s32[]{:S(2)}) async-start(s8[4718592]{0:T(1024)(128)(4,1)} %bitcast.100), calls=%async_computation.4 | async-start | bytes 1048576
  186.9 8.9 %collective-permute-start.26 = (bf16[128,1152]{1,0:T(8,128)(2,1)S(1)}, bf16[128,1152]{1,0:T(8,128)(2,1)S(1)}, u32[]{:S(2)}, u32[]{:S(2)}) collective-permute-start(bf16[128,1152]{1,0:T(8,128)(2,1)S(1)} %fusion.2), channel_id=1, source_target_pairs={{0,0},{1,16},{16,1},{17,17},{2,2},{3,18},{18,3},{19,19},{4,4},{5,2... | collective-permute-start | bytes 884744 | tf_op jit(solution)/shard_map/ppermute | solution.py:149
  192.3 7.5 %collective-permute-start.27 = (bf16[128,1152]{1,0:T(8,128)(2,1)S(1)}, bf16[128,1152]{1,0:T(8,128)(2,1)S(1)}, u32[]{:S(2)}, u32[]{:S(2)}) collective-permute-start(bf16[128,1152]{1,0:T(8,128)(2,1)S(1)} %fusion.1), channel_id=1, source_target_pairs={{0,16},{1,0},{16,17},{17,1},{2,18},{3,2},{18,19},{19,3},{4,20},{5,... | collective-permute-start | bytes 884744 | tf_op jit(solution)/shard_map/ppermute | solution.py:147

commit v20 on v19

--- a/solution.py
+++ b/solution.py
@@ -77,21 +77,25 @@
     groups, steps = lax.axis_size("zh"), lax.axis_size("zl")
     chips = lax.axis_size(PLANE)
     total_cols = cols * chips
-    own = lax.ppermute(rounded, ("ylo", "core"), TURN)
+    slabs = groups * steps
+    near = [None, launch(rounded, 0)]
+    far = [None, launch(lax.ppermute(rounded, "core", SWAP), 1)]
+    for step in range(2, slabs // 2 + 1):
+        if step == 4:
+            late, far[-1] = lax.optimization_barrier((rounded, far[-1]))
+            own = lax.ppermute(late, ("ylo", "core"), TURN)
+        near.append(onward(near[-1]))
+        if step < slabs // 2:
+            far.append(onward(far[-1]))
     other = lax.ppermute(own, "core", SWAP)
-    slabs = groups * steps
-    near, far = [own, launch(rounded, 0)], [None, launch(lax.ppermute(rounded, "core", SWAP), 1)]
-    for step in range(2, slabs // 2):
-        near.append(onward(near[-1]))
-        far.append(onward(far[-1]))
-    near.append(onward(near[-1]))
     back = [None] + swap(far[1:4]) + swap(far[4:6]) + swap(far[6:])
     slab, toward = lax.axis_index(LINE), 1 - 2 * lax.axis_index("core")
     half = jnp.zeros((slabs, rows, cols), jnp.bfloat16)
-    for step in range(slabs // 2 + 1):
+    for step in range(1, slabs // 2 + 1):
         half = put(half, near[step], (slab - step * toward) % slabs)
-        if 0 < step < slabs // 2:
+        if step < slabs // 2:
             half = put(half, back[step], (slab + step * toward) % slabs)
+    half = put(half, own, slab)
     partial_gram = lax.dot_general(
         jnp.concatenate([own, other], 0),
         half,

time: 202 us -> 203 us (level)
  waiting for transfers between devices: 12.4 us -> 14.7 us
    ppermute x5, starting transfers between devices: 20.7 us -> 18.1 us  [swap(): return list(lax.ppermute(jnp.stack(pieces), 'core', SWAP))]
    all_gather x1, blocking collectives: 16.6 us -> 18.8 us  [per_device(): here = lax.all_gather(gram_low, 'zh', axis=0)]
  transfers between devices with their start and end apart: 29 -> 29, of which waited for: 9 -> 10; matrix products, arithmetic and copies ran while one was open for 2% -> 2% of each run, Pallas kernels for 0% -> 0%
where the time goes in v20:
time: 203 us; the launch traced here: 202 us
  starting transfers between devices  111 us (55%)
  blocking collectives  64.4 us (32%)
  waiting for transfers between devices  14.7 us (7%)
  matrix products  4.99 us (2%)
  local copies, waits for them, and re-layouts  3.4 us (2%)
  other arithmetic  2.9 us (1%)
    ppermute x16, starting transfers between devices, along(): return lax.ppermute(piece, LINE + ('core',), pairs)  62.1 us
    all_to_all x1, blocking collectives, per_device(): summands = lax.all_to_all(partial_gram, PLANE, 0, 0)  23.4 us
    all_to_all x1, blocking collectives, share(): return lax.all_to_all(copies, PLANE, 0, 0)  22.2 us
    all_gather x1, blocking collectives, per_device(): here = lax.all_gather(gram_low, 'zh', axis=0)  18.8 us
    ppermute x5, starting transfers between devices, swap(): return list(lax.ppermute(jnp.stack(pieces), 'core', SWAP))  18.1 us
    ppermute x1, starting transfers between devices, per_device(): far = [None, launch(lax.ppermute(rounded, 'core', SWAP), 1)]  8.79 us
    ppermute x2, starting transfers between devices, launch(): return lax.ppermute(piece, LINE + ('ylo', 'core'), pairs)  7.67 us
    ppermute x16, waiting for transfers between devices, along(): return lax.ppermute(piece, LINE + ('core',), pairs)  5.11 us
  transfers between devices with their start and end apart: 29, of which 10 were waited for; matrix products, arithmetic and copies ran while one was open for 2% of the time, Pallas kernels for 0%

profile of v20, /device:TPU:1, one launch (start us, length us, event | category | flops | bytes accessed | tf_op | source)
XLA Modules:
  0.0 202.3 jit_solution(14963425817498909504)
XLA Ops:
  0.0 1.1 convert_element_type.39
  1.1 8.8 %collective-permute-start = (bf16[128,1152]{1,0:T(8,128)(2,1)S(1)}, bf16[128,1152]{1,0:T(8,128)(2,1)S(1)}, u32[]{:S(2)}, u32[]{:S(2)}) collective-permute-start(bf16[128,1152]{1,0:T(8,128)(2,1)S(1)} %convert_element_type.39), channel_id=1, source_target_pairs={{0,1},{1,0},{2,3},{3,2},{4,5},{5,4},{6,7},{7,6},{8,9},{9,8},{10,11... | collective-permute-start | bytes 884744 | tf_op jit(solution)/shard_map/ppermute | solution.py:82
  9.9 1.9 collective-permute-start.6
  11.8 5.7 %collective-permute-start.1 = (bf16[128,1152]{1,0:T(8,128)(2,1)S(1)}, bf16[128,1152]{1,0:T(8,128)(2,1)S(1)}, u32[]{:S(2)}, u32[]{:S(2)}) collective-permute-start(bf16[128,1152]{1,0:T(8,128)(2,1)S(1)} %collective-permute-done), channel_id=1, source_target_pairs={{0,497},{1,481},{16,48},{17,32},{32,17},{33,1},{48,80},{49,64},{64... | collective-permute-start | bytes 884744 | tf_op jit(solution)/shard_map/ppermute | solution.py:49
  17.6 1.5 collective-permute-done.6
  19.1 9.9 %collective-permute-start.8 = (bf16[128,1152]{1,0:T(8,128)(2,1)S(1)}, bf16[128,1152]{1,0:T(8,128)(2,1)S(1)}, u32[]{:S(2)}, u32[]{:S(2)}) collective-permute-start(bf16[128,1152]{1,0:T(8,128)(2,1)S(1)} %collective-permute-done.6), channel_id=1, source_target_pairs={{0,32},{1,481},{32,64},{33,1},{64,96},{65,33},{96,128},{97,65},{12... | collective-permute-start | bytes 884744 | tf_op jit(solution)/shard_map/ppermute | solution.py:28
  29.1 1.9 collective-permute-start.2
  31.0 1.7 collective-permute-done.8
  32.7 5.0 %collective-permute-start.9 = (bf16[128,1152]{1,0:T(8,128)(2,1)S(1)}, bf16[128,1152]{1,0:T(8,128)(2,1)S(1)}, u32[]{:S(2)}, u32[]{:S(2)}) collective-permute-start(bf16[128,1152]{1,0:T(8,128)(2,1)S(1)} %collective-permute-done.8), channel_id=1, source_target_pairs={{0,32},{1,481},{32,64},{33,1},{64,96},{65,33},{96,128},{97,65},{12... | collective-permute-start | bytes 884744 | tf_op jit(solution)/shard_map/ppermute | solution.py:28
  37.7 3.1 %collective-permute-start.3 = (bf16[128,1152]{1,0:T(8,128)(2,1)S(1)}, bf16[128,1152]{1,0:T(8,128)(2,1)S(1)}, u32[]{:S(2)}, u32[]{:S(2)}) collective-permute-start(bf16[128,1152]{1,0:T(8,128)(2,1)S(1)} %collective-permute-done.2), channel_id=1, source_target_pairs={{0,32},{1,481},{32,64},{33,1},{64,96},{65,33},{96,128},{97,65},{12... | collective-permute-start | bytes 884744 | tf_op jit(solution)/shard_map/ppermute | solution.py:28
  40.9 0.5 collective-permute-done.9
  41.4 5.0 %collective-permute-start.10 = (bf16[128,1152]{1,0:T(8,128)(2,1)S(1)}, bf16[128,1152]{1,0:T(8,128)(2,1)S(1)}, u32[]{:S(2)}, u32[]{:S(2)}) collective-permute-start(bf16[128,1152]{1,0:T(8,128)(2,1)S(1)} %collective-permute-done.9), channel_id=1, source_target_pairs={{0,32},{1,481},{32,64},{33,1},{64,96},{65,33},{96,128},{97,65},{12... | collective-permute-start | bytes 884744 | tf_op jit(solution)/shard_map/ppermute | solution.py:28
  46.7 2.8 %collective-permute-start.11 = (bf16[128,1152]{1,0:T(8,128)(2,1)S(1)}, bf16[128,1152]{1,0:T(8,128)(2,1)S(1)}, u32[]{:S(2)}, u32[]{:S(2)}) collective-permute-start(bf16[128,1152]{1,0:T(8,128)(2,1)S(1)} %collective-permute-done.3), channel_id=1, source_target_pairs={{0,32},{1,481},{32,64},{33,1},{64,96},{65,33},{96,128},{97,65},{12... | collective-permute-start | bytes 884744 | tf_op jit(solution)/shard_map/ppermute | solution.py:28
  49.5 0.1 pad_maximum_fusion.1
  49.7 1.9 collective-permute-start.7
  51.6 2.1 %collective-permute-start.4 = (bf16[128,1152]{1,0:T(8,128)(2,1)S(1)}, bf16[128,1152]{1,0:T(8,128)(2,1)S(1)}, u32[]{:S(2)}, u32[]{:S(2)}) collective-permute-start(bf16[128,1152]{1,0:T(8,128)(2,1)S(1)} %convert_element_type.39), channel_id=1, source_target_pairs={{0,0},{1,16},{16,1},{17,17},{2,2},{3,18},{18,3},{19,19},{4,4},{5,2... | collective-permute-start | bytes 884744 | tf_op jit(solution)/shard_map/ppermute | solution.py:86
  53.7 4.9 %collective-permute-start.14 = (bf16[128,1152]{1,0:T(8,128)(2,1)S(1)}, bf16[128,1152]{1,0:T(8,128)(2,1)S(1)}, u32[]{:S(2)}, u32[]{:S(2)}) collective-permute-start(bf16[128,1152]{1,0:T(8,128)(2,1)S(1)} %collective-permute-done.10), channel_id=1, source_target_pairs={{0,32},{1,481},{32,64},{33,1},{64,96},{65,33},{96,128},{97,65},{12... | collective-permute-start | bytes 884744 | tf_op jit(solution)/shard_map/ppermute | solution.py:28
  58.6 0.6 broadcast_in_dim.67
  59.3 2.8 %collective-permute-start.12 = (bf16[128,1152]{1,0:T(8,128)(2,1)S(1)}, bf16[128,1152]{1,0:T(8,128)(2,1)S(1)}, u32[]{:S(2)}, u32[]{:S(2)}) collective-permute-start(bf16[128,1152]{1,0:T(8,128)(2,1)S(1)} %collective-permute-done.11), channel_id=1, source_target_pairs={{0,32},{1,481},{32,64},{33,1},{64,96},{65,33},{96,128},{97,65},{12... | collective-permute-start | bytes 884744 | tf_op jit(solution)/shard_map/ppermute | solution.py:28
  62.0 0.2 collective-permute-done.14
  62.2 5.0 %collective-permute-start.15 = (bf16[128,1152]{1,0:T(8,128)(2,1)S(1)}, bf16[128,1152]{1,0:T(8,128)(2,1)S(1)}, u32[]{:S(2)}, u32[]{:S(2)}) collective-permute-start(bf16[128,1152]{1,0:T(8,128)(2,1)S(1)} %collective-permute-done.14), channel_id=1, source_target_pairs={{0,32},{1,481},{32,64},{33,1},{64,96},{65,33},{96,128},{97,65},{12... | collective-permute-start | bytes 884744 | tf_op jit(solution)/shard_map/ppermute | solution.py:28
  67.2 0.1 multiply_reduce_fusion
  67.4 3.3 %collective-permute-start.16 = (bf16[128,1152]{1,0:T(8,128)(2,1)S(1)}, bf16[128,1152]{1,0:T(8,128)(2,1)S(1)}, u32[]{:S(2)}, u32[]{:S(2)}) collective-permute-start(bf16[128,1152]{1,0:T(8,128)(2,1)S(1)} %collective-permute-done.12), channel_id=1, source_target_pairs={{0,32},{1,481},{32,64},{33,1},{64,96},{65,33},{96,128},{97,65},{12... | collective-permute-start | bytes 884744 | tf_op jit(solution)/shard_map/ppermute | solution.py:28
  70.7 0.2 collective-permute-done.15
  70.9 5.0 %collective-permute-start.19 = (bf16[128,1152]{1,0:T(8,128)(2,1)S(1)}, bf16[128,1152]{1,0:T(8,128)(2,1)S(1)}, u32[]{:S(2)}, u32[]{:S(2)}) collective-permute-start(bf16[128,1152]{1,0:T(8,128)(2,1)S(1)} %collective-permute-done.15), channel_id=1, source_target_pairs={{0,32},{1,481},{32,64},{33,1},{64,96},{65,33},{96,128},{97,65},{12... | collective-permute-start | bytes 884744 | tf_op jit(solution)/shard_map/ppermute | solution.py:28
  75.9 1.9 collective-permute-start.5
  77.9 2.4 %collective-permute-start.13 = (bf16[2,128,1152]{2,1,0:T(8,128)(2,1)S(1)}, bf16[2,128,1152]{2,1,0:T(8,128)(2,1)S(1)}, u32[]{:S(2)}, u32[]{:S(2)}) collective-permute-start(bf16[2,128,1152]{2,1,0:T(8,128)(2,1)S(1)} %pad_maximum_fusion.2), channel_id=1, source_target_pairs={{0,1},{1,0},{2,3},{3,2},{4,5},{5,4},{6,7},{7,6},{8,9},{9,8},{10,11... | collective-permute-start | bytes 1769480 | tf_op jit(solution)/shard_map/ppermute | solution.py:53
  80.3 3.0 %collective-permute-start.17 = (bf16[128,1152]{1,0:T(8,128)(2,1)S(1)}, bf16[128,1152]{1,0:T(8,128)(2,1)S(1)}, u32[]{:S(2)}, u32[]{:S(2)}) collective-permute-start(bf16[128,1152]{1,0:T(8,128)(2,1)S(1)} %collective-permute-done.16), channel_id=1, source_target_pairs={{0,32},{1,481},{32,64},{33,1},{64,96},{65,33},{96,128},{97,65},{12... | collective-permute-start | bytes 884744 | tf_op jit(solution)/shard_map/ppermute | solution.py:28
  83.4 1.9 collective-permute-start.20
  85.6 2.5 %collective-permute-done.17 = bf16[128,1152]{1,0:T(8,128)(2,1)S(1)} collective-permute-done((bf16[128,1152]{1,0:T(8,128)(2,1)S(1)}, bf16[128,1152]{1,0:T(8,128)(2,1)S(1)}, u32[]{:S(2)}, u32[]{:S(2)}) %collective-permute-start.17) | collective-permute-done | bytes 294944 | tf_op jit(solution)/shard_map/ppermute | solution.py:28
  88.2 4.0 %collective-permute-start.18 = (bf16[2,128,1152]{2,1,0:T(8,128)(2,1)S(1)}, bf16[2,128,1152]{2,1,0:T(8,128)(2,1)S(1)}, u32[]{:S(2)}, u32[]{:S(2)}) collective-permute-start(bf16[2,128,1152]{2,1,0:T(8,128)(2,1)S(1)} %pad_maximum_fusion.3), channel_id=1, source_target_pairs={{0,1},{1,0},{2,3},{3,2},{4,5},{5,4},{6,7},{7,6},{8,9},{9,8},{10,11... | collective-permute-start | bytes 1769480 | tf_op jit(solution)/shard_map/ppermute | solution.py:53
  92.3 1.4 collective-permute-done.18
  94.0 1.6 fusion.3
  95.6 0.5 copy-done
  96.1 0.1 pad_maximum_fusion
  96.2 23.4 %all_to_all.15 = bf16[16,264,128]{2,1,0:T(8,128)(2,1)S(1)} all-to-all(bf16[16,264,128]{2,1,0:T(8,128)(2,1)S(1)} %pad_maximum_fusion), channel_id=1, replica_groups=mesh['zh'=4,'zl'=4,'ylo'=2,'x'=4,'yhi'=2,'core'=2] {'ylo','yhi','x'}, dimensions={0} | all-to-all | bytes 2162688 | tf_op jit(solution)/shard_map/all_to_all | solution.py:113
  119.6 0.1 convert_reduce_fusion
  119.8 1.2 broadcast_in_dim.79
  121.0 3.7 %all-to-all-start.1 = ((bf16[16,256,128]{2,1,0:T(8,128)(2,1)}), bf16[16,256,128]{2,1,0:T(8,128)(2,1)S(1)}, u32[]{:S(2)}, u32[]{:S(2)}) async-start(bf16[16,256,128]{2,1,0:T(8,128)(2,1)} %broadcast_in_dim.79), calls=%async_computation.1 | async-start | bytes 2097152 | tf_op jit(solution)/shard_map/all_to_all | solution.py:17
  124.7 18.8 %all-gather = bf16[1024,128]{1,0:T(8,128)(2,1)S(1)} all-gather(bf16[256,128]{1,0:T(8,128)(2,1)S(1)} %fusion.39), channel_id=2, replica_groups=mesh['zh'=4,'zl'=4,'ylo'=2,'x'=4,'yhi'=2,'core'=2] {'zh'}, dimensions={0}, use_global_device_ids=true | all-gather | bytes 327680 | tf_op jit(solution)/shard_map/all_gather | solution.py:125
  143.5 1.9 collective-permute-start.23
  145.4 3.0 %collective-permute-start.22 = (bf16[4,256,128]{2,1,0:T(8,128)(2,1)S(1)}, bf16[4,256,128]{2,1,0:T(8,128)(2,1)S(1)}, u32[]{:S(2)}, u32[]{:S(2)}) collective-permute-start(bf16[4,256,128]{2,1,0:T(8,128)(2,1)S(1)} %bitcast.108), channel_id=1, source_target_pairs={{0,32},{1,33},{32,64},{33,65},{64,96},{65,97},{96,128},{97,129},{1... | collective-permute-start | bytes 786440 | tf_op jit(solution)/shard_map/ppermute | solution.py:28
  148.5 3.5 %collective-permute-start.21 = (bf16[4,256,128]{2,1,0:T(8,128)(2,1)S(1)}, bf16[4,256,128]{2,1,0:T(8,128)(2,1)S(1)}, u32[]{:S(2)}, u32[]{:S(2)}) collective-permute-start(bf16[4,256,128]{2,1,0:T(8,128)(2,1)S(1)} %bitcast.109), channel_id=1, source_target_pairs={{0,480},{1,481},{32,0},{33,1},{64,32},{65,33},{96,64},{97,65},{128... | collective-permute-start | bytes 786440 | tf_op jit(solution)/shard_map/ppermute | solution.py:28
  152.0 0.1 dynamic-slice_bitcast_fusion.1
  152.1 7.6 %collective-permute-start.25 = (bf16[2,4,256,128]{3,2,1,0:T(8,128)(2,1)S(1)}, bf16[2,4,256,128]{3,2,1,0:T(8,128)(2,1)S(1)}, u32[]{:S(2)}, u32[]{:S(2)}) collective-permute-start(bf16[2,4,256,128]{3,2,1,0:T(8,128)(2,1)S(1)} %pad_maximum_fusion.5), channel_id=1, source_target_pairs={{0,1},{1,0},{2,3},{3,2},{4,5},{5,4},{6,7},{7,6},{8,9},{9,8},{10,11... | collective-permute-start | bytes 1572872 | tf_op jit(solution)/shard_map/ppermute | solution.py:53
  159.7 0.2 convolution_bitcast_fusion.9
  160.0 2.2 %collective-permute-start.24 = (bf16[2,4,256,128]{3,2,1,0:T(8,128)(2,1)S(1)}, bf16[2,4,256,128]{3,2,1,0:T(8,128)(2,1)S(1)}, u32[]{:S(2)}, u32[]{:S(2)}) collective-permute-start(bf16[2,4,256,128]{3,2,1,0:T(8,128)(2,1)S(1)} %pad_maximum_fusion.4), channel_id=1, source_target_pairs={{0,1},{1,0},{2,3},{3,2},{4,5},{5,4},{6,7},{7,6},{8,9},{9,8},{10,11... | collective-permute-start | bytes 1572872 | tf_op jit(solution)/shard_map/ppermute | solution.py:53
  162.2 0.2 fusion.4
  162.4 0.2 convolution_bitcast_fusion.7
  162.7 0.2 convolution_bitcast_fusion.6
  163.1 1.0 collective-permute-done.24
  164.2 0.2 convolution_bitcast_fusion.5
  164.4 0.2 fusion.5
  164.6 0.2 convolution_bitcast_fusion.3
  164.9 0.2 convolution_bitcast_fusion.2
  165.2 0.2 broadcast_in_dim.81
  165.4 22.2 %all_to_all.16 = bf16[16,256,128]{2,1,0:T(8,128)(2,1)S(1)} all-to-all(bf16[16,256,128]{2,1,0:T(8,128)(2,1)S(1)} %broadcast_in_dim.81), channel_id=1, replica_groups=mesh['zh'=4,'zl'=4,'ylo'=2,'x'=4,'yhi'=2,'core'=2] {'ylo','yhi','x'}, dimensions={0} | all-to-all | bytes 2097152 | tf_op jit(solution)/shard_map/all_to_all | solution.py:17
  187.6 0.9 fusion.2
  188.5 4.6 %collective-permute-start.26 = (bf16[128,1152]{1,0:T(8,128)(2,1)S(1)}, bf16[128,1152]{1,0:T(8,128)(2,1)S(1)}, u32[]{:S(2)}, u32[]{:S(2)}) collective-permute-start(bf16[128,1152]{1,0:T(8,128)(2,1)S(1)} %fusion.2), channel_id=1, source_target_pairs={{0,0},{1,16},{16,1},{17,17},{2,2},{3,18},{18,3},{19,19},{4,4},{5,2... | collective-permute-start | bytes 884744 | tf_op jit(solution)/shard_map/ppermute | solution.py:153
  193.1 0.9 fusion.1
  194.0 1.9 collective-permute-start.27
  195.9 1.6 collective-permute-done.26
  197.5 3.9 %collective-permute-done.27 = bf16[128,1152]{1,0:T(8,128)(2,1)S(1)} collective-permute-done((bf16[128,1152]{1,0:T(8,128)(2,1)S(1)}, bf16[128,1152]{1,0:T(8,128)(2,1)S(1)}, u32[]{:S(2)}, u32[]{:S(2)}) %collective-permute-start.27) | collective-permute-done | bytes 294944 | tf_op jit(solution)/shard_map/ppermute | solution.py:151
  201.5 0.9 convert_add_fusion
  (63 shorter events, 1.2 us)
Async XLA Ops:
  1.1 10.7 %collective-permute-start = (bf16[128,1152]{1,0:T(8,128)(2,1)S(1)}, bf16[128,1152]{1,0:T(8,128)(2,1)S(1)}, u32[]{:S(2)}, u32[]{:S(2)}) collective-permute-start(bf16[128,1152]{1,0:T(8,128)(2,1)S(1)} %convert_element_type.39), channel_id=1, source_target_pairs={{0,1},{1,0},{2,3},{3,2},{4,5},{5,4},{6,7},{7,6},{8,9},{9,8},{10,11... | collective-permute-start | bytes 884744 | tf_op jit(solution)/shard_map/ppermute | solution.py:82
  9.9 9.2 %collective-permute-start.6 = (bf16[128,1152]{1,0:T(8,128)(2,1)S(1)}, bf16[128,1152]{1,0:T(8,128)(2,1)S(1)}, u32[]{:S(2)}, u32[]{:S(2)}) collective-permute-start(bf16[128,1152]{1,0:T(8,128)(2,1)S(1)} %convert_element_type.39), channel_id=1, source_target_pairs={{0,32},{1,48},{16,481},{17,497},{32,64},{33,80},{48,1},{49,17},{64... | collective-permute-start | bytes 884744 | tf_op jit(solution)/shard_map/ppermute | solution.py:49
  11.8 17.2 %collective-permute-start.1 = (bf16[128,1152]{1,0:T(8,128)(2,1)S(1)}, bf16[128,1152]{1,0:T(8,128)(2,1)S(1)}, u32[]{:S(2)}, u32[]{:S(2)}) collective-permute-start(bf16[128,1152]{1,0:T(8,128)(2,1)S(1)} %collective-permute-done), channel_id=1, source_target_pairs={{0,497},{1,481},{16,48},{17,32},{32,17},{33,1},{48,80},{49,64},{64... | collective-permute-start | bytes 884744 | tf_op jit(solution)/shard_map/ppermute | solution.py:49
  19.1 13.6 %collective-permute-start.8 = (bf16[128,1152]{1,0:T(8,128)(2,1)S(1)}, bf16[128,1152]{1,0:T(8,128)(2,1)S(1)}, u32[]{:S(2)}, u32[]{:S(2)}) collective-permute-start(bf16[128,1152]{1,0:T(8,128)(2,1)S(1)} %collective-permute-done.6), channel_id=1, source_target_pairs={{0,32},{1,481},{32,64},{33,1},{64,96},{65,33},{96,128},{97,65},{12... | collective-permute-start | bytes 884744 | tf_op jit(solution)/shard_map/ppermute | solution.py:28
  29.1 8.7 %collective-permute-start.2 = (bf16[128,1152]{1,0:T(8,128)(2,1)S(1)}, bf16[128,1152]{1,0:T(8,128)(2,1)S(1)}, u32[]{:S(2)}, u32[]{:S(2)}) collective-permute-start(bf16[128,1152]{1,0:T(8,128)(2,1)S(1)} %collective-permute-done.1), channel_id=1, source_target_pairs={{0,32},{1,481},{32,64},{33,1},{64,96},{65,33},{96,128},{97,65},{12... | collective-permute-start | bytes 884744 | tf_op jit(solution)/shard_map/ppermute | solution.py:28
  32.7 8.7 %collective-permute-start.9 = (bf16[128,1152]{1,0:T(8,128)(2,1)S(1)}, bf16[128,1152]{1,0:T(8,128)(2,1)S(1)}, u32[]{:S(2)}, u32[]{:S(2)}) collective-permute-start(bf16[128,1152]{1,0:T(8,128)(2,1)S(1)} %collective-permute-done.8), channel_id=1, source_target_pairs={{0,32},{1,481},{32,64},{33,1},{64,96},{65,33},{96,128},{97,65},{12... | collective-permute-start | bytes 884744 | tf_op jit(solution)/shard_map/ppermute | solution.py:28
  37.7 9.0 %collective-permute-start.3 = (bf16[128,1152]{1,0:T(8,128)(2,1)S(1)}, bf16[128,1152]{1,0:T(8,128)(2,1)S(1)}, u32[]{:S(2)}, u32[]{:S(2)}) collective-permute-start(bf16[128,1152]{1,0:T(8,128)(2,1)S(1)} %collective-permute-done.2), channel_id=1, source_target_pairs={{0,32},{1,481},{32,64},{33,1},{64,96},{65,33},{96,128},{97,65},{12... | collective-permute-start | bytes 884744 | tf_op jit(solution)/shard_map/ppermute | solution.py:28
  41.4 12.3 %collective-permute-start.10 = (bf16[128,1152]{1,0:T(8,128)(2,1)S(1)}, bf16[128,1152]{1,0:T(8,128)(2,1)S(1)}, u32[]{:S(2)}, u32[]{:S(2)}) collective-permute-start(bf16[128,1152]{1,0:T(8,128)(2,1)S(1)} %collective-permute-done.9), channel_id=1, source_target_pairs={{0,32},{1,481},{32,64},{33,1},{64,96},{65,33},{96,128},{97,65},{12... | collective-permute-start | bytes 884744 | tf_op jit(solution)/shard_map/ppermute | solution.py:28
  46.7 12.5 %collective-permute-start.11 = (bf16[128,1152]{1,0:T(8,128)(2,1)S(1)}, bf16[128,1152]{1,0:T(8,128)(2,1)S(1)}, u32[]{:S(2)}, u32[]{:S(2)}) collective-permute-start(bf16[128,1152]{1,0:T(8,128)(2,1)S(1)} %collective-permute-done.3), channel_id=1, source_target_pairs={{0,32},{1,481},{32,64},{33,1},{64,96},{65,33},{96,128},{97,65},{12... | collective-permute-start | bytes 884744 | tf_op jit(solution)/shard_map/ppermute | solution.py:28
  49.7 35.7 %collective-permute-start.7 = (bf16[3,128,1152]{2,1,0:T(8,128)(2,1)S(1)}, bf16[3,128,1152]{2,1,0:T(8,128)(2,1)S(1)}, u32[]{:S(2)}, u32[]{:S(2)}) collective-permute-start(bf16[3,128,1152]{2,1,0:T(8,128)(2,1)S(1)} %pad_maximum_fusion.1), channel_id=1, source_target_pairs={{0,1},{1,0},{2,3},{3,2},{4,5},{5,4},{6,7},{7,6},{8,9},{9,8},{10,11... | collective-permute-start | bytes 2654216 | tf_op jit(solution)/shard_map/ppermute | solution.py:53
  51.6 15.6 %collective-permute-start.4 = (bf16[128,1152]{1,0:T(8,128)(2,1)S(1)}, bf16[128,1152]{1,0:T(8,128)(2,1)S(1)}, u32[]{:S(2)}, u32[]{:S(2)}) collective-permute-start(bf16[128,1152]{1,0:T(8,128)(2,1)S(1)} %convert_element_type.39), channel_id=1, source_target_pairs={{0,0},{1,16},{16,1},{17,17},{2,2},{3,18},{18,3},{19,19},{4,4},{5,2... | collective-permute-start | bytes 884744 | tf_op jit(solution)/shard_map/ppermute | solution.py:86
  53.7 8.5 %collective-permute-start.14 = (bf16[128,1152]{1,0:T(8,128)(2,1)S(1)}, bf16[128,1152]{1,0:T(8,128)(2,1)S(1)}, u32[]{:S(2)}, u32[]{:S(2)}) collective-permute-start(bf16[128,1152]{1,0:T(8,128)(2,1)S(1)} %collective-permute-done.10), channel_id=1, source_target_pairs={{0,32},{1,481},{32,64},{33,1},{64,96},{65,33},{96,128},{97,65},{12... | collective-permute-start | bytes 884744 | tf_op jit(solution)/shard_map/ppermute | solution.py:28
  59.3 8.2 %collective-permute-start.12 = (bf16[128,1152]{1,0:T(8,128)(2,1)S(1)}, bf16[128,1152]{1,0:T(8,128)(2,1)S(1)}, u32[]{:S(2)}, u32[]{:S(2)}) collective-permute-start(bf16[128,1152]{1,0:T(8,128)(2,1)S(1)} %collective-permute-done.11), channel_id=1, source_target_pairs={{0,32},{1,481},{32,64},{33,1},{64,96},{65,33},{96,128},{97,65},{12... | collective-permute-start | bytes 884744 | tf_op jit(solution)/shard_map/ppermute | solution.py:28
  62.2 8.7 %collective-permute-start.15 = (bf16[128,1152]{1,0:T(8,128)(2,1)S(1)}, bf16[128,1152]{1,0:T(8,128)(2,1)S(1)}, u32[]{:S(2)}, u32[]{:S(2)}) collective-permute-start(bf16[128,1152]{1,0:T(8,128)(2,1)S(1)} %collective-permute-done.14), channel_id=1, source_target_pairs={{0,32},{1,481},{32,64},{33,1},{64,96},{65,33},{96,128},{97,65},{12... | collective-permute-start | bytes 884744 | tf_op jit(solution)/shard_map/ppermute | solution.py:28
  67.4 12.9 %collective-permute-start.16 = (bf16[128,1152]{1,0:T(8,128)(2,1)S(1)}, bf16[128,1152]{1,0:T(8,128)(2,1)S(1)}, u32[]{:S(2)}, u32[]{:S(2)}) collective-permute-start(bf16[128,1152]{1,0:T(8,128)(2,1)S(1)} %collective-permute-done.12), channel_id=1, source_target_pairs={{0,32},{1,481},{32,64},{33,1},{64,96},{65,33},{96,128},{97,65},{12... | collective-permute-start | bytes 884744 | tf_op jit(solution)/shard_map/ppermute | solution.py:28
  70.9 12.5 %collective-permute-start.19 = (bf16[128,1152]{1,0:T(8,128)(2,1)S(1)}, bf16[128,1152]{1,0:T(8,128)(2,1)S(1)}, u32[]{:S(2)}, u32[]{:S(2)}) collective-permute-start(bf16[128,1152]{1,0:T(8,128)(2,1)S(1)} %collective-permute-done.15), channel_id=1, source_target_pairs={{0,32},{1,481},{32,64},{33,1},{64,96},{65,33},{96,128},{97,65},{12... | collective-permute-start | bytes 884744 | tf_op jit(solution)/shard_map/ppermute | solution.py:28
  75.9 18.1 %collective-permute-start.5 = (bf16[128,1152]{1,0:T(8,128)(2,1)S(1)}, bf16[128,1152]{1,0:T(8,128)(2,1)S(1)}, u32[]{:S(2)}, u32[]{:S(2)}) collective-permute-start(bf16[128,1152]{1,0:T(8,128)(2,1)S(1)} %collective-permute-done.4), channel_id=1, source_target_pairs={{0,1},{1,0},{2,3},{3,2},{4,5},{5,4},{6,7},{7,6},{8,9},{9,8},{10,11... | collective-permute-start | bytes 884744 | tf_op jit(solution)/shard_map/ppermute | solution.py:90
  77.9 14.2 %collective-permute-start.13 = (bf16[2,128,1152]{2,1,0:T(8,128)(2,1)S(1)}, bf16[2,128,1152]{2,1,0:T(8,128)(2,1)S(1)}, u32[]{:S(2)}, u32[]{:S(2)}) collective-permute-start(bf16[2,128,1152]{2,1,0:T(8,128)(2,1)S(1)} %pad_maximum_fusion.2), channel_id=1, source_target_pairs={{0,1},{1,0},{2,3},{3,2},{4,5},{5,4},{6,7},{7,6},{8,9},{9,8},{10,11... | collective-permute-start | bytes 1769480 | tf_op jit(solution)/shard_map/ppermute | solution.py:53
  80.3 7.8 %collective-permute-start.17 = (bf16[128,1152]{1,0:T(8,128)(2,1)S(1)}, bf16[128,1152]{1,0:T(8,128)(2,1)S(1)}, u32[]{:S(2)}, u32[]{:S(2)}) collective-permute-start(bf16[128,1152]{1,0:T(8,128)(2,1)S(1)} %collective-permute-done.16), channel_id=1, source_target_pairs={{0,32},{1,481},{32,64},{33,1},{64,96},{65,33},{96,128},{97,65},{12... | collective-permute-start | bytes 884744 | tf_op jit(solution)/shard_map/ppermute | solution.py:28
  83.4 10.5 %collective-permute-start.20 = (bf16[128,1152]{1,0:T(8,128)(2,1)S(1)}, bf16[128,1152]{1,0:T(8,128)(2,1)S(1)}, u32[]{:S(2)}, u32[]{:S(2)}) collective-permute-start(bf16[128,1152]{1,0:T(8,128)(2,1)S(1)} %collective-permute-done.19), channel_id=1, source_target_pairs={{0,32},{1,481},{32,64},{33,1},{64,96},{65,33},{96,128},{97,65},{12... | collective-permute-start | bytes 884744 | tf_op jit(solution)/shard_map/ppermute | solution.py:28
  88.2 5.6 %collective-permute-start.18 = (bf16[2,128,1152]{2,1,0:T(8,128)(2,1)S(1)}, bf16[2,128,1152]{2,1,0:T(8,128)(2,1)S(1)}, u32[]{:S(2)}, u32[]{:S(2)}) collective-permute-start(bf16[2,128,1152]{2,1,0:T(8,128)(2,1)S(1)} %pad_maximum_fusion.3), channel_id=1, source_target_pairs={{0,1},{1,0},{2,3},{3,2},{4,5},{5,4},{6,7},{7,6},{8,9},{9,8},{10,11... | collective-permute-start | bytes 1769480 | tf_op jit(solution)/shard_map/ppermute | solution.py:53
  94.0 2.1 %copy-start = (bf16[16,128,1152]{2,1,0:T(8,128)(2,1)}, bf16[16,128,1152]{2,1,0:T(8,128)(2,1)S(1)}, u32[]{:S(2)}) copy-start(bf16[16,128,1152]{2,1,0:T(8,128)(2,1)S(1)} %bitcast_dynamic-update-slice_fusion) | copy-start | bytes 14155780
  121.0 30.9 %all-to-all-start.1 = ((bf16[16,256,128]{2,1,0:T(8,128)(2,1)}), bf16[16,256,128]{2,1,0:T(8,128)(2,1)S(1)}, u32[]{:S(2)}, u32[]{:S(2)}) async-start(bf16[16,256,128]{2,1,0:T(8,128)(2,1)} %broadcast_in_dim.79), calls=%async_computation.1 | async-start | bytes 2097152 | tf_op jit(solution)/shard_map/all_to_all | solution.py:17
  143.5 19.2 %collective-permute-start.23 = (bf16[4,256,128]{2,1,0:T(8,128)(2,1)S(1)}, bf16[4,256,128]{2,1,0:T(8,128)(2,1)S(1)}, u32[]{:S(2)}, u32[]{:S(2)}) collective-permute-start(bf16[4,256,128]{2,1,0:T(8,128)(2,1)S(1)} %bitcast.107), channel_id=1, source_target_pairs={{0,448},{1,65},{32,480},{33,97},{64,0},{65,129},{96,32},{97,161},{... | collective-permute-start | bytes 786440 | tf_op jit(solution)/shard_map/ppermute | solution.py:28
  145.4 17.0 %collective-permute-start.22 = (bf16[4,256,128]{2,1,0:T(8,128)(2,1)S(1)}, bf16[4,256,128]{2,1,0:T(8,128)(2,1)S(1)}, u32[]{:S(2)}, u32[]{:S(2)}) collective-permute-start(bf16[4,256,128]{2,1,0:T(8,128)(2,1)S(1)} %bitcast.108), channel_id=1, source_target_pairs={{0,32},{1,33},{32,64},{33,65},{64,96},{65,97},{96,128},{97,129},{1... | collective-permute-start | bytes 786440 | tf_op jit(solution)/shard_map/ppermute | solution.py:28
  148.5 13.7 %collective-permute-start.21 = (bf16[4,256,128]{2,1,0:T(8,128)(2,1)S(1)}, bf16[4,256,128]{2,1,0:T(8,128)(2,1)S(1)}, u32[]{:S(2)}, u32[]{:S(2)}) collective-permute-start(bf16[4,256,128]{2,1,0:T(8,128)(2,1)S(1)} %bitcast.109), channel_id=1, source_target_pairs={{0,480},{1,481},{32,0},{33,1},{64,32},{65,33},{96,64},{97,65},{128... | collective-permute-start | bytes 786440 | tf_op jit(solution)/shard_map/ppermute | solution.py:28
  152.1 10.8 %collective-permute-start.25 = (bf16[2,4,256,128]{3,2,1,0:T(8,128)(2,1)S(1)}, bf16[2,4,256,128]{3,2,1,0:T(8,128)(2,1)S(1)}, u32[]{:S(2)}, u32[]{:S(2)}) collective-permute-start(bf16[2,4,256,128]{3,2,1,0:T(8,128)(2,1)S(1)} %pad_maximum_fusion.5), channel_id=1, source_target_pairs={{0,1},{1,0},{2,3},{3,2},{4,5},{5,4},{6,7},{7,6},{8,9},{9,8},{10,11... | collective-permute-start | bytes 1572872 | tf_op jit(solution)/shard_map/ppermute | solution.py:53
  159.9 27.7 %slice-start = ((s8[4718592]{0:T(1024)(128)(4,1)}), s8[4194304]{0:T(1024)(128)(4,1)S(1)}, s32[]{:S(2)}) async-start(s8[4718592]{0:T(1024)(128)(4,1)} %bitcast.100), calls=%async_computation.3 | async-start | bytes 8388608
  160.0 4.1 %collective-permute-start.24 = (bf16[2,4,256,128]{3,2,1,0:T(8,128)(2,1)S(1)}, bf16[2,4,256,128]{3,2,1,0:T(8,128)(2,1)S(1)}, u32[]{:S(2)}, u32[]{:S(2)}) collective-permute-start(bf16[2,4,256,128]{3,2,1,0:T(8,128)(2,1)S(1)} %pad_maximum_fusion.4), channel_id=1, source_target_pairs={{0,1},{1,0},{2,3},{3,2},{4,5},{5,4},{6,7},{7,6},{8,9},{9,8},{10,11... | collective-permute-start | bytes 1572872 | tf_op jit(solution)/shard_map/ppermute | solution.py:53
  164.1 23.5 %slice-start.1 = ((s8[4718592]{0:T(1024)(128)(4,1)}), s8[524288]{0:T(1024)(128)(4,1)S(1)}, s32[]{:S(2)}) async-start(s8[4718592]{0:T(1024)(128)(4,1)} %bitcast.100), calls=%async_computation.4 | async-start | bytes 1048576
  188.5 9.0 %collective-permute-start.26 = (bf16[128,1152]{1,0:T(8,128)(2,1)S(1)}, bf16[128,1152]{1,0:T(8,128)(2,1)S(1)}, u32[]{:S(2)}, u32[]{:S(2)}) collective-permute-start(bf16[128,1152]{1,0:T(8,128)(2,1)S(1)} %fusion.2), channel_id=1, source_target_pairs={{0,0},{1,16},{16,1},{17,17},{2,2},{3,18},{18,3},{19,19},{4,4},{5,2... | collective-permute-start | bytes 884744 | tf_op jit(solution)/shard_map/ppermute | solution.py:153
  194.0 7.5 %collective-permute-start.27 = (bf16[128,1152]{1,0:T(8,128)(2,1)S(1)}, bf16[128,1152]{1,0:T(8,128)(2,1)S(1)}, u32[]{:S(2)}, u32[]{:S(2)}) collective-permute-start(bf16[128,1152]{1,0:T(8,128)(2,1)S(1)} %fusion.1), channel_id=1, source_target_pairs={{0,16},{1,0},{16,17},{17,1},{2,18},{3,2},{18,19},{19,3},{4,20},{5,... | collective-permute-start | bytes 884744 | tf_op jit(solution)/shard_map/ppermute | solution.py:151

commit v21 on v18

--- a/solution.py
+++ b/solution.py
@@ -142,10 +142,12 @@
         square = square + mix(left_other[place], right[place][:, rows:])
         square = lax.optimization_barrier(square)
     poly = (-4.775 * gram + 2.0315 * square).astype(jnp.bfloat16)
+    poly, own = lax.optimization_barrier((poly, own))
     panel = share(poly, chips)
+    scaled = lax.optimization_barrier(3.4445 * own.astype(jnp.float32))
     away = mix(panel[:, rows:], half).astype(jnp.bfloat16)
     away = lax.ppermute(away, ("ylo", "core"), CROSS)
-    stay = mix(panel[:, :rows], half) + 3.4445 * own.astype(jnp.float32)
+    stay = mix(panel[:, :rows], half) + scaled
     stay = lax.ppermute(stay.astype(jnp.bfloat16), ("ylo", "core"), TURN)
     return stay.astype(jnp.float32) + away.astype(jnp.float32)
 

time: 202 us -> 208 us (1.030)
  blocking collectives: 61.8 us -> 41.1 us
  waiting for transfers between devices: 12.4 us -> 27.2 us
  starting transfers between devices: 114 us -> 120 us
  matrix products: 4.99 us -> 9.67 us
    all_to_all x1 -> x0, blocking collectives: 20.7 us -> none  [share(): return lax.all_to_all(copies, PLANE, 0, 0)]
    all_to_all x1 -> x2, waiting for transfers between devices: 0.01 us -> 14.7 us  [share(): return lax.all_to_all(copies, PLANE, 0, 0)]
    all_to_all x1 -> x2, starting transfers between devices: 3.65 us -> 10.6 us  [share(): return lax.all_to_all(copies, PLANE, 0, 0)]
    dot_general x10, matrix products: 3.42 us -> 8.1 us  [mix(): lax.dot_general(left, right, (((0, 2), (0, 1)), ((), ())), preferred_elem...]
  transfers between devices with their start and end apart: 29 -> 30, of which waited for: 8 -> 8; matrix products, arithmetic and copies ran while one was open for 2% -> 3% of each run, Pallas kernels for 0% -> 0%
where the time goes in v21:
time: 208 us; the launch traced here: 207 us
  starting transfers between devices  120 us (58%)
  blocking collectives  41.1 us (20%)
  waiting for transfers between devices  27.2 us (13%)
  matrix products  9.67 us (5%)
  local copies, waits for them, and re-layouts  4.42 us (2%)
  other arithmetic  2.95 us (1%)
    ppermute x16, starting transfers between devices, along(): return lax.ppermute(piece, LINE + ('core',), pairs)  61.3 us
    all_to_all x1, blocking collectives, per_device(): summands = lax.all_to_all(partial_gram, PLANE, 0, 0)  24.5 us
    ppermute x5, starting transfers between devices, swap(): return list(lax.ppermute(jnp.stack(pieces), 'core', SWAP))  20.5 us
    all_gather x1, blocking collectives, per_device(): here = lax.all_gather(gram_low, 'zh', axis=0)  16.6 us
    all_to_all x2, waiting for transfers between devices, share(): return lax.all_to_all(copies, PLANE, 0, 0)  14.7 us
    all_to_all x2, starting transfers between devices, share(): return lax.all_to_all(copies, PLANE, 0, 0)  10.6 us
    ppermute x1, starting transfers between devices, per_device(): lax.ppermute(rounded, 'core', SWAP)  8.79 us
    dot_general x10, matrix products, mix(): lax.dot_general(left, right, (((0, 2), (0, 1)), ((), ())), preferred_elem...  8.1 us
  transfers between devices with their start and end apart: 30, of which 8 were waited for; matrix products, arithmetic and copies ran while one was open for 3% of the time, Pallas kernels for 0%

profile of v21, /device:TPU:1, one launch (start us, length us, event | category | flops | bytes accessed | tf_op | source)
XLA Modules:
  0.0 206.6 jit_solution(1762449625082370123)
XLA Ops:
  0.0 1.1 convert_element_type.39
  1.1 8.8 %collective-permute-start.3 = (bf16[128,1152]{1,0:T(8,128)(2,1)S(1)}, bf16[128,1152]{1,0:T(8,128)(2,1)S(1)}, u32[]{:S(2)}, u32[]{:S(2)}) collective-permute-start(bf16[128,1152]{1,0:T(8,128)(2,1)S(1)} %convert_element_type.39), channel_id=1, source_target_pairs={{0,1},{1,0},{2,3},{3,2},{4,5},{5,4},{6,7},{7,6},{8,9},{9,8},{10,11... | collective-permute-start | bytes 884744 | tf_op jit(solution)/shard_map/ppermute | solution.py:83
  9.9 1.9 collective-permute-start.2
  11.8 5.7 %collective-permute-start.4 = (bf16[128,1152]{1,0:T(8,128)(2,1)S(1)}, bf16[128,1152]{1,0:T(8,128)(2,1)S(1)}, u32[]{:S(2)}, u32[]{:S(2)}) collective-permute-start(bf16[128,1152]{1,0:T(8,128)(2,1)S(1)} %collective-permute-done.3), channel_id=1, source_target_pairs={{0,497},{1,481},{16,48},{17,32},{32,17},{33,1},{48,80},{49,64},{64... | collective-permute-start | bytes 884744 | tf_op jit(solution)/shard_map/ppermute | solution.py:49
  17.6 1.5 collective-permute-done.2
  19.1 9.9 %collective-permute-start.8 = (bf16[128,1152]{1,0:T(8,128)(2,1)S(1)}, bf16[128,1152]{1,0:T(8,128)(2,1)S(1)}, u32[]{:S(2)}, u32[]{:S(2)}) collective-permute-start(bf16[128,1152]{1,0:T(8,128)(2,1)S(1)} %collective-permute-done.2), channel_id=1, source_target_pairs={{0,32},{1,481},{32,64},{33,1},{64,96},{65,33},{96,128},{97,65},{12... | collective-permute-start | bytes 884744 | tf_op jit(solution)/shard_map/ppermute | solution.py:28
  29.0 1.9 collective-permute-start
  31.0 2.7 %collective-permute-start.5 = (bf16[128,1152]{1,0:T(8,128)(2,1)S(1)}, bf16[128,1152]{1,0:T(8,128)(2,1)S(1)}, u32[]{:S(2)}, u32[]{:S(2)}) collective-permute-start(bf16[128,1152]{1,0:T(8,128)(2,1)S(1)} %collective-permute-done.4), channel_id=1, source_target_pairs={{0,32},{1,481},{32,64},{33,1},{64,96},{65,33},{96,128},{97,65},{12... | collective-permute-start | bytes 884744 | tf_op jit(solution)/shard_map/ppermute | solution.py:28
  33.7 4.0 %collective-permute-start.9 = (bf16[128,1152]{1,0:T(8,128)(2,1)S(1)}, bf16[128,1152]{1,0:T(8,128)(2,1)S(1)}, u32[]{:S(2)}, u32[]{:S(2)}) collective-permute-start(bf16[128,1152]{1,0:T(8,128)(2,1)S(1)} %collective-permute-done.8), channel_id=1, source_target_pairs={{0,32},{1,481},{32,64},{33,1},{64,96},{65,33},{96,128},{97,65},{12... | collective-permute-start | bytes 884744 | tf_op jit(solution)/shard_map/ppermute | solution.py:28
  38.1 1.9 collective-permute-start.1
  40.0 2.5 %collective-permute-start.6 = (bf16[128,1152]{1,0:T(8,128)(2,1)S(1)}, bf16[128,1152]{1,0:T(8,128)(2,1)S(1)}, u32[]{:S(2)}, u32[]{:S(2)}) collective-permute-start(bf16[128,1152]{1,0:T(8,128)(2,1)S(1)} %collective-permute-done.5), channel_id=1, source_target_pairs={{0,32},{1,481},{32,64},{33,1},{64,96},{65,33},{96,128},{97,65},{12... | collective-permute-start | bytes 884744 | tf_op jit(solution)/shard_map/ppermute | solution.py:28
  42.5 3.9 %collective-permute-start.10 = (bf16[128,1152]{1,0:T(8,128)(2,1)S(1)}, bf16[128,1152]{1,0:T(8,128)(2,1)S(1)}, u32[]{:S(2)}, u32[]{:S(2)}) collective-permute-start(bf16[128,1152]{1,0:T(8,128)(2,1)S(1)} %collective-permute-done.9), channel_id=1, source_target_pairs={{0,32},{1,481},{32,64},{33,1},{64,96},{65,33},{96,128},{97,65},{12... | collective-permute-start | bytes 884744 | tf_op jit(solution)/shard_map/ppermute | solution.py:28
  46.4 0.6 broadcast_in_dim.67
  47.1 0.7 collective-permute-done.6
  47.8 3.4 %collective-permute-start.11 = (bf16[128,1152]{1,0:T(8,128)(2,1)S(1)}, bf16[128,1152]{1,0:T(8,128)(2,1)S(1)}, u32[]{:S(2)}, u32[]{:S(2)}) collective-permute-start(bf16[128,1152]{1,0:T(8,128)(2,1)S(1)} %collective-permute-done.6), channel_id=1, source_target_pairs={{0,32},{1,481},{32,64},{33,1},{64,96},{65,33},{96,128},{97,65},{12... | collective-permute-start | bytes 884744 | tf_op jit(solution)/shard_map/ppermute | solution.py:28
  51.2 3.9 %collective-permute-start.14 = (bf16[128,1152]{1,0:T(8,128)(2,1)S(1)}, bf16[128,1152]{1,0:T(8,128)(2,1)S(1)}, u32[]{:S(2)}, u32[]{:S(2)}) collective-permute-start(bf16[128,1152]{1,0:T(8,128)(2,1)S(1)} %collective-permute-done.10), channel_id=1, source_target_pairs={{0,32},{1,481},{32,64},{33,1},{64,96},{65,33},{96,128},{97,65},{12... | collective-permute-start | bytes 884744 | tf_op jit(solution)/shard_map/ppermute | solution.py:28
  55.0 0.1 multiply_reduce_fusion
  55.2 0.1 pad_maximum_fusion.1
  55.3 2.3 %collective-permute-start.7 = (bf16[3,128,1152]{2,1,0:T(8,128)(2,1)S(1)}, bf16[3,128,1152]{2,1,0:T(8,128)(2,1)S(1)}, u32[]{:S(2)}, u32[]{:S(2)}) collective-permute-start(bf16[3,128,1152]{2,1,0:T(8,128)(2,1)S(1)} %pad_maximum_fusion.1), channel_id=1, source_target_pairs={{0,1},{1,0},{2,3},{3,2},{4,5},{5,4},{6,7},{7,6},{8,9},{9,8},{10,11... | collective-permute-start | bytes 2654216 | tf_op jit(solution)/shard_map/ppermute | solution.py:53
  57.6 4.9 %collective-permute-start.12 = (bf16[128,1152]{1,0:T(8,128)(2,1)S(1)}, bf16[128,1152]{1,0:T(8,128)(2,1)S(1)}, u32[]{:S(2)}, u32[]{:S(2)}) collective-permute-start(bf16[128,1152]{1,0:T(8,128)(2,1)S(1)} %collective-permute-done.11), channel_id=1, source_target_pairs={{0,32},{1,481},{32,64},{33,1},{64,96},{65,33},{96,128},{97,65},{12... | collective-permute-start | bytes 884744 | tf_op jit(solution)/shard_map/ppermute | solution.py:28
  62.5 2.4 %collective-permute-start.15 = (bf16[128,1152]{1,0:T(8,128)(2,1)S(1)}, bf16[128,1152]{1,0:T(8,128)(2,1)S(1)}, u32[]{:S(2)}, u32[]{:S(2)}) collective-permute-start(bf16[128,1152]{1,0:T(8,128)(2,1)S(1)} %collective-permute-done.14), channel_id=1, source_target_pairs={{0,32},{1,481},{32,64},{33,1},{64,96},{65,33},{96,128},{97,65},{12... | collective-permute-start | bytes 884744 | tf_op jit(solution)/shard_map/ppermute | solution.py:28
  64.9 1.2 collective-permute-done.12
  66.1 5.0 %collective-permute-start.16 = (bf16[128,1152]{1,0:T(8,128)(2,1)S(1)}, bf16[128,1152]{1,0:T(8,128)(2,1)S(1)}, u32[]{:S(2)}, u32[]{:S(2)}) collective-permute-start(bf16[128,1152]{1,0:T(8,128)(2,1)S(1)} %collective-permute-done.12), channel_id=1, source_target_pairs={{0,32},{1,481},{32,64},{33,1},{64,96},{65,33},{96,128},{97,65},{12... | collective-permute-start | bytes 884744 | tf_op jit(solution)/shard_map/ppermute | solution.py:28
  71.2 3.1 %collective-permute-start.19 = (bf16[128,1152]{1,0:T(8,128)(2,1)S(1)}, bf16[128,1152]{1,0:T(8,128)(2,1)S(1)}, u32[]{:S(2)}, u32[]{:S(2)}) collective-permute-start(bf16[128,1152]{1,0:T(8,128)(2,1)S(1)} %collective-permute-done.15), channel_id=1, source_target_pairs={{0,32},{1,481},{32,64},{33,1},{64,96},{65,33},{96,128},{97,65},{12... | collective-permute-start | bytes 884744 | tf_op jit(solution)/shard_map/ppermute | solution.py:28
  74.3 0.1 pad_maximum_fusion.2
  74.4 2.7 %collective-permute-start.13 = (bf16[2,128,1152]{2,1,0:T(8,128)(2,1)S(1)}, bf16[2,128,1152]{2,1,0:T(8,128)(2,1)S(1)}, u32[]{:S(2)}, u32[]{:S(2)}) collective-permute-start(bf16[2,128,1152]{2,1,0:T(8,128)(2,1)S(1)} %pad_maximum_fusion.2), channel_id=1, source_target_pairs={{0,1},{1,0},{2,3},{3,2},{4,5},{5,4},{6,7},{7,6},{8,9},{9,8},{10,11... | collective-permute-start | bytes 1769480 | tf_op jit(solution)/shard_map/ppermute | solution.py:53
  77.1 4.9 %collective-permute-start.17 = (bf16[128,1152]{1,0:T(8,128)(2,1)S(1)}, bf16[128,1152]{1,0:T(8,128)(2,1)S(1)}, u32[]{:S(2)}, u32[]{:S(2)}) collective-permute-start(bf16[128,1152]{1,0:T(8,128)(2,1)S(1)} %collective-permute-done.16), channel_id=1, source_target_pairs={{0,32},{1,481},{32,64},{33,1},{64,96},{65,33},{96,128},{97,65},{12... | collective-permute-start | bytes 884744 | tf_op jit(solution)/shard_map/ppermute | solution.py:28
  82.0 2.4 %collective-permute-start.20 = (bf16[128,1152]{1,0:T(8,128)(2,1)S(1)}, bf16[128,1152]{1,0:T(8,128)(2,1)S(1)}, u32[]{:S(2)}, u32[]{:S(2)}) collective-permute-start(bf16[128,1152]{1,0:T(8,128)(2,1)S(1)} %collective-permute-done.19), channel_id=1, source_target_pairs={{0,32},{1,481},{32,64},{33,1},{64,96},{65,33},{96,128},{97,65},{12... | collective-permute-start | bytes 884744 | tf_op jit(solution)/shard_map/ppermute | solution.py:28
  84.7 0.9 collective-permute-done.17
  85.6 0.1 pad_maximum_fusion.3
  85.7 5.9 %collective-permute-start.18 = (bf16[2,128,1152]{2,1,0:T(8,128)(2,1)S(1)}, bf16[2,128,1152]{2,1,0:T(8,128)(2,1)S(1)}, u32[]{:S(2)}, u32[]{:S(2)}) collective-permute-start(bf16[2,128,1152]{2,1,0:T(8,128)(2,1)S(1)} %pad_maximum_fusion.3), channel_id=1, source_target_pairs={{0,1},{1,0},{2,3},{3,2},{4,5},{5,4},{6,7},{7,6},{8,9},{9,8},{10,11... | collective-permute-start | bytes 1769480 | tf_op jit(solution)/shard_map/ppermute | solution.py:53
  91.8 1.4 collective-permute-done.18
  93.4 1.6 fusion.3
  95.0 0.5 copy-done
  95.5 0.1 pad_maximum_fusion
  95.6 24.5 %all_to_all.15 = bf16[16,264,128]{2,1,0:T(8,128)(2,1)S(1)} all-to-all(bf16[16,264,128]{2,1,0:T(8,128)(2,1)S(1)} %pad_maximum_fusion), channel_id=1, replica_groups=mesh['zh'=4,'zl'=4,'ylo'=2,'x'=4,'yhi'=2,'core'=2] {'ylo','yhi','x'}, dimensions={0} | all-to-all | bytes 2162688 | tf_op jit(solution)/shard_map/all_to_all | solution.py:109
  120.1 0.1 convert_reduce_fusion
  120.3 1.2 broadcast_in_dim.79
  121.5 3.7 %all-to-all-start.1 = ((bf16[16,256,128]{2,1,0:T(8,128)(2,1)}), bf16[16,256,128]{2,1,0:T(8,128)(2,1)S(1)}, u32[]{:S(2)}, u32[]{:S(2)}) async-start(bf16[16,256,128]{2,1,0:T(8,128)(2,1)} %broadcast_in_dim.79), calls=%async_computation.1 | async-start | bytes 2097152 | tf_op jit(solution)/shard_map/all_to_all | solution.py:17
  125.3 16.6 %all-gather = bf16[1024,128]{1,0:T(8,128)(2,1)S(1)} all-gather(bf16[256,128]{1,0:T(8,128)(2,1)S(1)} %fusion.39), channel_id=2, replica_groups=mesh['zh'=4,'zl'=4,'ylo'=2,'x'=4,'yhi'=2,'core'=2] {'zh'}, dimensions={0}, use_global_device_ids=true | all-gather | bytes 327680 | tf_op jit(solution)/shard_map/all_gather | solution.py:121
  141.9 1.9 collective-permute-start.23
  143.8 4.6 %collective-permute-start.22 = (bf16[4,256,128]{2,1,0:T(8,128)(2,1)S(1)}, bf16[4,256,128]{2,1,0:T(8,128)(2,1)S(1)}, u32[]{:S(2)}, u32[]{:S(2)}) collective-permute-start(bf16[4,256,128]{2,1,0:T(8,128)(2,1)S(1)} %bitcast.106), channel_id=1, source_target_pairs={{0,480},{1,481},{32,0},{33,1},{64,32},{65,33},{96,64},{97,65},{128... | collective-permute-start | bytes 786440 | tf_op jit(solution)/shard_map/ppermute | solution.py:28
  148.4 1.9 collective-permute-start.21
  150.3 0.1 dynamic-slice_bitcast_fusion.1
  150.5 7.7 %collective-permute-start.25 = (bf16[2,4,256,128]{3,2,1,0:T(8,128)(2,1)S(1)}, bf16[2,4,256,128]{3,2,1,0:T(8,128)(2,1)S(1)}, u32[]{:S(2)}, u32[]{:S(2)}) collective-permute-start(bf16[2,4,256,128]{3,2,1,0:T(8,128)(2,1)S(1)} %pad_maximum_fusion.5), channel_id=1, source_target_pairs={{0,1},{1,0},{2,3},{3,2},{4,5},{5,4},{6,7},{7,6},{8,9},{9,8},{10,11... | collective-permute-start | bytes 1572872 | tf_op jit(solution)/shard_map/ppermute | solution.py:53
  158.2 0.2 convolution_bitcast_fusion.9
  158.4 1.9 collective-permute-start.24
  160.4 0.2 fusion.4
  160.6 0.2 convolution_bitcast_fusion.7
  160.9 0.2 convolution_bitcast_fusion.6
  161.2 1.0 collective-permute-done.24
  162.3 0.2 convolution_bitcast_fusion.5
  162.6 0.2 fusion.5
  162.8 0.2 convolution_bitcast_fusion.3
  163.0 0.2 convolution_bitcast_fusion.2
  163.3 1.2 broadcast_in_dim.81
  164.6 7.0 %all-to-all-start.2 = ((bf16[16,256,128]{2,1,0:T(8,128)(2,1)}), bf16[16,256,128]{2,1,0:T(8,128)(2,1)S(1)}, u32[]{:S(2)}, u32[]{:S(2)}) async-start(bf16[16,256,128]{2,1,0:T(8,128)(2,1)} %broadcast_in_dim.81), calls=%async_computation.2 | async-start | bytes 2097152 | tf_op jit(solution)/shard_map/all_to_all | solution.py:17
  171.6 14.7 %all-to-all-done.2 = bf16[16,256,128]{2,1,0:T(8,128)(2,1)S(1)} async-done(((bf16[16,256,128]{2,1,0:T(8,128)(2,1)}), bf16[16,256,128]{2,1,0:T(8,128)(2,1)S(1)}, u32[]{:S(2)}, u32[]{:S(2)}) %all-to-all-start.2) | async-done | bytes 1048608 | tf_op jit(solution)/shard_map/all_to_all | solution.py:17
  186.3 3.2 %fusion.2 = bf16[128,1152]{1,0:T(8,128)(2,1)S(1)} fusion(f32[128,1152]{1,0:T(8,128)S(1)} %convert_multiply_fusion, bf16[16,128,1152]{2,1,0:T(8,128)(2,1)} %copy-done, bf16[16,256,128]{2,1,0:T(8,128)(2,1)S(1)} %all-to-all-done.2), kind=kOutput, calls=%fused_computation.4 | convolution fusion | flops 604274688 | bytes 6127616 | tf_op jit(solution)/shard_map/dot_general | solution.py:69
  189.5 5.5 %collective-permute-start.26 = (bf16[128,1152]{1,0:T(8,128)(2,1)S(1)}, bf16[128,1152]{1,0:T(8,128)(2,1)S(1)}, u32[]{:S(2)}, u32[]{:S(2)}) collective-permute-start(bf16[128,1152]{1,0:T(8,128)(2,1)S(1)} %fusion.2), channel_id=1, source_target_pairs={{0,0},{1,16},{16,1},{17,17},{2,2},{3,18},{18,3},{19,19},{4,4},{5,2... | collective-permute-start | bytes 884744 | tf_op jit(solution)/shard_map/ppermute | solution.py:151
  195.0 3.2 %fusion.1 = bf16[128,1152]{1,0:T(8,128)(2,1)S(1)} fusion(bf16[16,128,1152]{2,1,0:T(8,128)(2,1)} %copy-done, bf16[16,256,128]{2,1,0:T(8,128)(2,1)S(1)} %all-to-all-done.2), kind=kOutput, calls=%fused_computation.3 | convolution fusion | flops 604127232 | bytes 5537792 | tf_op jit(solution)/shard_map/dot_general | solution.py:69
  198.2 1.9 collective-permute-start.27
  200.2 5.5 %collective-permute-done.27 = bf16[128,1152]{1,0:T(8,128)(2,1)S(1)} collective-permute-done((bf16[128,1152]{1,0:T(8,128)(2,1)S(1)}, bf16[128,1152]{1,0:T(8,128)(2,1)S(1)}, u32[]{:S(2)}, u32[]{:S(2)}) %collective-permute-start.27) | collective-permute-done | bytes 294944 | tf_op jit(solution)/shard_map/ppermute | solution.py:149
  205.7 0.9 convert_add_fusion
  (60 shorter events, 1.2 us)
Async XLA Ops:
  1.1 10.7 %collective-permute-start.3 = (bf16[128,1152]{1,0:T(8,128)(2,1)S(1)}, bf16[128,1152]{1,0:T(8,128)(2,1)S(1)}, u32[]{:S(2)}, u32[]{:S(2)}) collective-permute-start(bf16[128,1152]{1,0:T(8,128)(2,1)S(1)} %convert_element_type.39), channel_id=1, source_target_pairs={{0,1},{1,0},{2,3},{3,2},{4,5},{5,4},{6,7},{7,6},{8,9},{9,8},{10,11... | collective-permute-start | bytes 884744 | tf_op jit(solution)/shard_map/ppermute | solution.py:83
  9.9 9.2 %collective-permute-start.2 = (bf16[128,1152]{1,0:T(8,128)(2,1)S(1)}, bf16[128,1152]{1,0:T(8,128)(2,1)S(1)}, u32[]{:S(2)}, u32[]{:S(2)}) collective-permute-start(bf16[128,1152]{1,0:T(8,128)(2,1)S(1)} %convert_element_type.39), channel_id=1, source_target_pairs={{0,32},{1,48},{16,481},{17,497},{32,64},{33,80},{48,1},{49,17},{64... | collective-permute-start | bytes 884744 | tf_op jit(solution)/shard_map/ppermute | solution.py:49
  11.8 19.1 %collective-permute-start.4 = (bf16[128,1152]{1,0:T(8,128)(2,1)S(1)}, bf16[128,1152]{1,0:T(8,128)(2,1)S(1)}, u32[]{:S(2)}, u32[]{:S(2)}) collective-permute-start(bf16[128,1152]{1,0:T(8,128)(2,1)S(1)} %collective-permute-done.3), channel_id=1, source_target_pairs={{0,497},{1,481},{16,48},{17,32},{32,17},{33,1},{48,80},{49,64},{64... | collective-permute-start | bytes 884744 | tf_op jit(solution)/shard_map/ppermute | solution.py:49
  19.1 14.6 %collective-permute-start.8 = (bf16[128,1152]{1,0:T(8,128)(2,1)S(1)}, bf16[128,1152]{1,0:T(8,128)(2,1)S(1)}, u32[]{:S(2)}, u32[]{:S(2)}) collective-permute-start(bf16[128,1152]{1,0:T(8,128)(2,1)S(1)} %collective-permute-done.2), channel_id=1, source_target_pairs={{0,32},{1,481},{32,64},{33,1},{64,96},{65,33},{96,128},{97,65},{12... | collective-permute-start | bytes 884744 | tf_op jit(solution)/shard_map/ppermute | solution.py:28
  29.0 9.0 %collective-permute-start = (bf16[128,1152]{1,0:T(8,128)(2,1)S(1)}, bf16[128,1152]{1,0:T(8,128)(2,1)S(1)}, u32[]{:S(2)}, u32[]{:S(2)}) collective-permute-start(bf16[128,1152]{1,0:T(8,128)(2,1)S(1)} %convert_element_type.39), channel_id=1, source_target_pairs={{0,0},{1,16},{16,1},{17,17},{2,2},{3,18},{18,3},{19,19},{4,4},{5,2... | collective-permute-start | bytes 884744 | tf_op jit(solution)/shard_map/ppermute | solution.py:80
  31.0 9.0 %collective-permute-start.5 = (bf16[128,1152]{1,0:T(8,128)(2,1)S(1)}, bf16[128,1152]{1,0:T(8,128)(2,1)S(1)}, u32[]{:S(2)}, u32[]{:S(2)}) collective-permute-start(bf16[128,1152]{1,0:T(8,128)(2,1)S(1)} %collective-permute-done.4), channel_id=1, source_target_pairs={{0,32},{1,481},{32,64},{33,1},{64,96},{65,33},{96,128},{97,65},{12... | collective-permute-start | bytes 884744 | tf_op jit(solution)/shard_map/ppermute | solution.py:28
  33.7 8.8 %collective-permute-start.9 = (bf16[128,1152]{1,0:T(8,128)(2,1)S(1)}, bf16[128,1152]{1,0:T(8,128)(2,1)S(1)}, u32[]{:S(2)}, u32[]{:S(2)}) collective-permute-start(bf16[128,1152]{1,0:T(8,128)(2,1)S(1)} %collective-permute-done.8), channel_id=1, source_target_pairs={{0,32},{1,481},{32,64},{33,1},{64,96},{65,33},{96,128},{97,65},{12... | collective-permute-start | bytes 884744 | tf_op jit(solution)/shard_map/ppermute | solution.py:28
  38.1 55.3 %collective-permute-start.1 = (bf16[128,1152]{1,0:T(8,128)(2,1)S(1)}, bf16[128,1152]{1,0:T(8,128)(2,1)S(1)}, u32[]{:S(2)}, u32[]{:S(2)}) collective-permute-start(bf16[128,1152]{1,0:T(8,128)(2,1)S(1)} %collective-permute-done), channel_id=1, source_target_pairs={{0,1},{1,0},{2,3},{3,2},{4,5},{5,4},{6,7},{7,6},{8,9},{9,8},{10,11... | collective-permute-start | bytes 884744 | tf_op jit(solution)/shard_map/ppermute | solution.py:81
  40.0 7.8 %collective-permute-start.6 = (bf16[128,1152]{1,0:T(8,128)(2,1)S(1)}, bf16[128,1152]{1,0:T(8,128)(2,1)S(1)}, u32[]{:S(2)}, u32[]{:S(2)}) collective-permute-start(bf16[128,1152]{1,0:T(8,128)(2,1)S(1)} %collective-permute-done.5), channel_id=1, source_target_pairs={{0,32},{1,481},{32,64},{33,1},{64,96},{65,33},{96,128},{97,65},{12... | collective-permute-start | bytes 884744 | tf_op jit(solution)/shard_map/ppermute | solution.py:28
  42.5 8.7 %collective-permute-start.10 = (bf16[128,1152]{1,0:T(8,128)(2,1)S(1)}, bf16[128,1152]{1,0:T(8,128)(2,1)S(1)}, u32[]{:S(2)}, u32[]{:S(2)}) collective-permute-start(bf16[128,1152]{1,0:T(8,128)(2,1)S(1)} %collective-permute-done.9), channel_id=1, source_target_pairs={{0,32},{1,481},{32,64},{33,1},{64,96},{65,33},{96,128},{97,65},{12... | collective-permute-start | bytes 884744 | tf_op jit(solution)/shard_map/ppermute | solution.py:28
  47.8 9.8 %collective-permute-start.11 = (bf16[128,1152]{1,0:T(8,128)(2,1)S(1)}, bf16[128,1152]{1,0:T(8,128)(2,1)S(1)}, u32[]{:S(2)}, u32[]{:S(2)}) collective-permute-start(bf16[128,1152]{1,0:T(8,128)(2,1)S(1)} %collective-permute-done.6), channel_id=1, source_target_pairs={{0,32},{1,481},{32,64},{33,1},{64,96},{65,33},{96,128},{97,65},{12... | collective-permute-start | bytes 884744 | tf_op jit(solution)/shard_map/ppermute | solution.py:28
  51.2 11.3 %collective-permute-start.14 = (bf16[128,1152]{1,0:T(8,128)(2,1)S(1)}, bf16[128,1152]{1,0:T(8,128)(2,1)S(1)}, u32[]{:S(2)}, u32[]{:S(2)}) collective-permute-start(bf16[128,1152]{1,0:T(8,128)(2,1)S(1)} %collective-permute-done.10), channel_id=1, source_target_pairs={{0,32},{1,481},{32,64},{33,1},{64,96},{65,33},{96,128},{97,65},{12... | collective-permute-start | bytes 884744 | tf_op jit(solution)/shard_map/ppermute | solution.py:28
  55.3 29.1 %collective-permute-start.7 = (bf16[3,128,1152]{2,1,0:T(8,128)(2,1)S(1)}, bf16[3,128,1152]{2,1,0:T(8,128)(2,1)S(1)}, u32[]{:S(2)}, u32[]{:S(2)}) collective-permute-start(bf16[3,128,1152]{2,1,0:T(8,128)(2,1)S(1)} %pad_maximum_fusion.1), channel_id=1, source_target_pairs={{0,1},{1,0},{2,3},{3,2},{4,5},{5,4},{6,7},{7,6},{8,9},{9,8},{10,11... | collective-permute-start | bytes 2654216 | tf_op jit(solution)/shard_map/ppermute | solution.py:53
  57.6 8.5 %collective-permute-start.12 = (bf16[128,1152]{1,0:T(8,128)(2,1)S(1)}, bf16[128,1152]{1,0:T(8,128)(2,1)S(1)}, u32[]{:S(2)}, u32[]{:S(2)}) collective-permute-start(bf16[128,1152]{1,0:T(8,128)(2,1)S(1)} %collective-permute-done.11), channel_id=1, source_target_pairs={{0,32},{1,481},{32,64},{33,1},{64,96},{65,33},{96,128},{97,65},{12... | collective-permute-start | bytes 884744 | tf_op jit(solution)/shard_map/ppermute | solution.py:28
  62.5 8.7 %collective-permute-start.15 = (bf16[128,1152]{1,0:T(8,128)(2,1)S(1)}, bf16[128,1152]{1,0:T(8,128)(2,1)S(1)}, u32[]{:S(2)}, u32[]{:S(2)}) collective-permute-start(bf16[128,1152]{1,0:T(8,128)(2,1)S(1)} %collective-permute-done.14), channel_id=1, source_target_pairs={{0,32},{1,481},{32,64},{33,1},{64,96},{65,33},{96,128},{97,65},{12... | collective-permute-start | bytes 884744 | tf_op jit(solution)/shard_map/ppermute | solution.py:28
  66.1 11.0 %collective-permute-start.16 = (bf16[128,1152]{1,0:T(8,128)(2,1)S(1)}, bf16[128,1152]{1,0:T(8,128)(2,1)S(1)}, u32[]{:S(2)}, u32[]{:S(2)}) collective-permute-start(bf16[128,1152]{1,0:T(8,128)(2,1)S(1)} %collective-permute-done.12), channel_id=1, source_target_pairs={{0,32},{1,481},{32,64},{33,1},{64,96},{65,33},{96,128},{97,65},{12... | collective-permute-start | bytes 884744 | tf_op jit(solution)/shard_map/ppermute | solution.py:28
  71.2 10.8 %collective-permute-start.19 = (bf16[128,1152]{1,0:T(8,128)(2,1)S(1)}, bf16[128,1152]{1,0:T(8,128)(2,1)S(1)}, u32[]{:S(2)}, u32[]{:S(2)}) collective-permute-start(bf16[128,1152]{1,0:T(8,128)(2,1)S(1)} %collective-permute-done.15), channel_id=1, source_target_pairs={{0,32},{1,481},{32,64},{33,1},{64,96},{65,33},{96,128},{97,65},{12... | collective-permute-start | bytes 884744 | tf_op jit(solution)/shard_map/ppermute | solution.py:28
  74.4 17.2 %collective-permute-start.13 = (bf16[2,128,1152]{2,1,0:T(8,128)(2,1)S(1)}, bf16[2,128,1152]{2,1,0:T(8,128)(2,1)S(1)}, u32[]{:S(2)}, u32[]{:S(2)}) collective-permute-start(bf16[2,128,1152]{2,1,0:T(8,128)(2,1)S(1)} %pad_maximum_fusion.2), channel_id=1, source_target_pairs={{0,1},{1,0},{2,3},{3,2},{4,5},{5,4},{6,7},{7,6},{8,9},{9,8},{10,11... | collective-permute-start | bytes 1769480 | tf_op jit(solution)/shard_map/ppermute | solution.py:53
  77.1 8.5 %collective-permute-start.17 = (bf16[128,1152]{1,0:T(8,128)(2,1)S(1)}, bf16[128,1152]{1,0:T(8,128)(2,1)S(1)}, u32[]{:S(2)}, u32[]{:S(2)}) collective-permute-start(bf16[128,1152]{1,0:T(8,128)(2,1)S(1)} %collective-permute-done.16), channel_id=1, source_target_pairs={{0,32},{1,481},{32,64},{33,1},{64,96},{65,33},{96,128},{97,65},{12... | collective-permute-start | bytes 884744 | tf_op jit(solution)/shard_map/ppermute | solution.py:28
  82.0 11.4 %collective-permute-start.20 = (bf16[128,1152]{1,0:T(8,128)(2,1)S(1)}, bf16[128,1152]{1,0:T(8,128)(2,1)S(1)}, u32[]{:S(2)}, u32[]{:S(2)}) collective-permute-start(bf16[128,1152]{1,0:T(8,128)(2,1)S(1)} %collective-permute-done.19), channel_id=1, source_target_pairs={{0,32},{1,481},{32,64},{33,1},{64,96},{65,33},{96,128},{97,65},{12... | collective-permute-start | bytes 884744 | tf_op jit(solution)/shard_map/ppermute | solution.py:28
  85.7 7.5 %collective-permute-start.18 = (bf16[2,128,1152]{2,1,0:T(8,128)(2,1)S(1)}, bf16[2,128,1152]{2,1,0:T(8,128)(2,1)S(1)}, u32[]{:S(2)}, u32[]{:S(2)}) collective-permute-start(bf16[2,128,1152]{2,1,0:T(8,128)(2,1)S(1)} %pad_maximum_fusion.3), channel_id=1, source_target_pairs={{0,1},{1,0},{2,3},{3,2},{4,5},{5,4},{6,7},{7,6},{8,9},{9,8},{10,11... | collective-permute-start | bytes 1769480 | tf_op jit(solution)/shard_map/ppermute | solution.py:53
  93.4 2.2 %copy-start = (bf16[16,128,1152]{2,1,0:T(8,128)(2,1)}, bf16[16,128,1152]{2,1,0:T(8,128)(2,1)S(1)}, u32[]{:S(2)}) copy-start(bf16[16,128,1152]{2,1,0:T(8,128)(2,1)S(1)} %bitcast_dynamic-update-slice_fusion) | copy-start | bytes 14155780
  121.5 28.8 %all-to-all-start.1 = ((bf16[16,256,128]{2,1,0:T(8,128)(2,1)}), bf16[16,256,128]{2,1,0:T(8,128)(2,1)S(1)}, u32[]{:S(2)}, u32[]{:S(2)}) async-start(bf16[16,256,128]{2,1,0:T(8,128)(2,1)} %broadcast_in_dim.79), calls=%async_computation.1 | async-start | bytes 2097152 | tf_op jit(solution)/shard_map/all_to_all | solution.py:17
  141.9 19.0 %collective-permute-start.23 = (bf16[4,256,128]{2,1,0:T(8,128)(2,1)S(1)}, bf16[4,256,128]{2,1,0:T(8,128)(2,1)S(1)}, u32[]{:S(2)}, u32[]{:S(2)}) collective-permute-start(bf16[4,256,128]{2,1,0:T(8,128)(2,1)S(1)} %bitcast.105), channel_id=1, source_target_pairs={{0,32},{1,33},{32,64},{33,65},{64,96},{65,97},{96,128},{97,129},{1... | collective-permute-start | bytes 786440 | tf_op jit(solution)/shard_map/ppermute | solution.py:28
  143.8 16.8 %collective-permute-start.22 = (bf16[4,256,128]{2,1,0:T(8,128)(2,1)S(1)}, bf16[4,256,128]{2,1,0:T(8,128)(2,1)S(1)}, u32[]{:S(2)}, u32[]{:S(2)}) collective-permute-start(bf16[4,256,128]{2,1,0:T(8,128)(2,1)S(1)} %bitcast.106), channel_id=1, source_target_pairs={{0,480},{1,481},{32,0},{33,1},{64,32},{65,33},{96,64},{97,65},{128... | collective-permute-start | bytes 786440 | tf_op jit(solution)/shard_map/ppermute | solution.py:28
  148.4 12.0 %collective-permute-start.21 = (bf16[4,256,128]{2,1,0:T(8,128)(2,1)S(1)}, bf16[4,256,128]{2,1,0:T(8,128)(2,1)S(1)}, u32[]{:S(2)}, u32[]{:S(2)}) collective-permute-start(bf16[4,256,128]{2,1,0:T(8,128)(2,1)S(1)} %bitcast.107), channel_id=1, source_target_pairs={{0,448},{1,65},{32,480},{33,97},{64,0},{65,129},{96,32},{97,161},{... | collective-permute-start | bytes 786440 | tf_op jit(solution)/shard_map/ppermute | solution.py:28
  150.5 10.6 %collective-permute-start.25 = (bf16[2,4,256,128]{3,2,1,0:T(8,128)(2,1)S(1)}, bf16[2,4,256,128]{3,2,1,0:T(8,128)(2,1)S(1)}, u32[]{:S(2)}, u32[]{:S(2)}) collective-permute-start(bf16[2,4,256,128]{3,2,1,0:T(8,128)(2,1)S(1)} %pad_maximum_fusion.5), channel_id=1, source_target_pairs={{0,1},{1,0},{2,3},{3,2},{4,5},{5,4},{6,7},{7,6},{8,9},{9,8},{10,11... | collective-permute-start | bytes 1572872 | tf_op jit(solution)/shard_map/ppermute | solution.py:53
  158.4 3.8 %collective-permute-start.24 = (bf16[2,4,256,128]{3,2,1,0:T(8,128)(2,1)S(1)}, bf16[2,4,256,128]{3,2,1,0:T(8,128)(2,1)S(1)}, u32[]{:S(2)}, u32[]{:S(2)}) collective-permute-start(bf16[2,4,256,128]{3,2,1,0:T(8,128)(2,1)S(1)} %pad_maximum_fusion.4), channel_id=1, source_target_pairs={{0,1},{1,0},{2,3},{3,2},{4,5},{5,4},{6,7},{7,6},{8,9},{9,8},{10,11... | collective-permute-start | bytes 1572872 | tf_op jit(solution)/shard_map/ppermute | solution.py:53
  164.6 21.8 %all-to-all-start.2 = ((bf16[16,256,128]{2,1,0:T(8,128)(2,1)}), bf16[16,256,128]{2,1,0:T(8,128)(2,1)S(1)}, u32[]{:S(2)}, u32[]{:S(2)}) async-start(bf16[16,256,128]{2,1,0:T(8,128)(2,1)} %broadcast_in_dim.81), calls=%async_computation.2 | async-start | bytes 2097152 | tf_op jit(solution)/shard_map/all_to_all | solution.py:17
  189.5 10.6 %collective-permute-start.26 = (bf16[128,1152]{1,0:T(8,128)(2,1)S(1)}, bf16[128,1152]{1,0:T(8,128)(2,1)S(1)}, u32[]{:S(2)}, u32[]{:S(2)}) collective-permute-start(bf16[128,1152]{1,0:T(8,128)(2,1)S(1)} %fusion.2), channel_id=1, source_target_pairs={{0,0},{1,16},{16,1},{17,17},{2,2},{3,18},{18,3},{19,19},{4,4},{5,2... | collective-permute-start | bytes 884744 | tf_op jit(solution)/shard_map/ppermute | solution.py:151
  198.2 7.5 %collective-permute-start.27 = (bf16[128,1152]{1,0:T(8,128)(2,1)S(1)}, bf16[128,1152]{1,0:T(8,128)(2,1)S(1)}, u32[]{:S(2)}, u32[]{:S(2)}) collective-permute-start(bf16[128,1152]{1,0:T(8,128)(2,1)S(1)} %fusion.1), channel_id=1, source_target_pairs={{0,16},{1,0},{16,17},{17,1},{2,18},{3,2},{18,19},{19,3},{4,20},{5,... | collective-permute-start | bytes 884744 | tf_op jit(solution)/shard_map/ppermute | solution.py:149

commit v22 on v18

--- a/solution.py
+++ b/solution.py
@@ -143,9 +143,10 @@
         square = lax.optimization_barrier(square)
     poly = (-4.775 * gram + 2.0315 * square).astype(jnp.bfloat16)
     panel = share(poly, chips)
-    away = mix(panel[:, rows:], half).astype(jnp.bfloat16)
+    product = mix(panel, half)
+    away = product[rows:].astype(jnp.bfloat16)
     away = lax.ppermute(away, ("ylo", "core"), CROSS)
-    stay = mix(panel[:, :rows], half) + 3.4445 * own.astype(jnp.float32)
+    stay = product[:rows] + 3.4445 * own.astype(jnp.float32)
     stay = lax.ppermute(stay.astype(jnp.bfloat16), ("ylo", "core"), TURN)
     return stay.astype(jnp.float32) + away.astype(jnp.float32)
 

time: 202 us -> 202 us (level)
  transfers between devices with their start and end apart: 29 -> 29, of which waited for: 8 -> 8; matrix products, arithmetic and copies ran while one was open for 2% -> 1% of each run, Pallas kernels for 0% -> 0%
where the time goes in v22:
time: 202 us; the launch traced here: 201 us
  starting transfers between devices  114 us (56%)
  blocking collectives  61.8 us (31%)
  waiting for transfers between devices  12.5 us (6%)
  matrix products  4.8 us (2%)
  local copies, waits for them, and re-layouts  3.43 us (2%)
  other arithmetic  2.99 us (1%)
    ppermute x16, starting transfers between devices, along(): return lax.ppermute(piece, LINE + ('core',), pairs)  61.3 us
    all_to_all x1, blocking collectives, per_device(): summands = lax.all_to_all(partial_gram, PLANE, 0, 0)  24.5 us
    all_to_all x1, blocking collectives, share(): return lax.all_to_all(copies, PLANE, 0, 0)  20.7 us
    ppermute x5, starting transfers between devices, swap(): return list(lax.ppermute(jnp.stack(pieces), 'core', SWAP))  20.7 us
    all_gather x1, blocking collectives, per_device(): here = lax.all_gather(gram_low, 'zh', axis=0)  16.6 us
    ppermute x1, starting transfers between devices, per_device(): lax.ppermute(rounded, 'core', SWAP)  8.79 us
    ppermute x2, starting transfers between devices, launch(): return lax.ppermute(piece, LINE + ('ylo', 'core'), pairs)  7.67 us
    ppermute x1, starting transfers between devices, per_device(): stay = lax.ppermute(stay.astype(jnp.bfloat16), ('ylo', 'core'), TURN)  6.01 us
  transfers between devices with their start and end apart: 29, of which 8 were waited for; matrix products, arithmetic and copies ran while one was open for 1% of the time, Pallas kernels for 0%

profile of v22, /device:TPU:1, one launch (start us, length us, event | category | flops | bytes accessed | tf_op | source)
XLA Modules:
  0.0 200.7 jit_solution(9120550881784632912)
XLA Ops:
  0.0 1.1 convert_element_type.37
  1.1 8.8 %collective-permute-start.3 = (bf16[128,1152]{1,0:T(8,128)(2,1)S(1)}, bf16[128,1152]{1,0:T(8,128)(2,1)S(1)}, u32[]{:S(2)}, u32[]{:S(2)}) collective-permute-start(bf16[128,1152]{1,0:T(8,128)(2,1)S(1)} %convert_element_type.37), channel_id=1, source_target_pairs={{0,1},{1,0},{2,3},{3,2},{4,5},{5,4},{6,7},{7,6},{8,9},{9,8},{10,11... | collective-permute-start | bytes 884744 | tf_op jit(solution)/shard_map/ppermute | solution.py:83
  9.9 1.9 collective-permute-start.2
  11.8 5.7 %collective-permute-start.4 = (bf16[128,1152]{1,0:T(8,128)(2,1)S(1)}, bf16[128,1152]{1,0:T(8,128)(2,1)S(1)}, u32[]{:S(2)}, u32[]{:S(2)}) collective-permute-start(bf16[128,1152]{1,0:T(8,128)(2,1)S(1)} %collective-permute-done.3), channel_id=1, source_target_pairs={{0,497},{1,481},{16,48},{17,32},{32,17},{33,1},{48,80},{49,64},{64... | collective-permute-start | bytes 884744 | tf_op jit(solution)/shard_map/ppermute | solution.py:49
  17.6 1.5 collective-permute-done.2
  19.1 9.9 %collective-permute-start.8 = (bf16[128,1152]{1,0:T(8,128)(2,1)S(1)}, bf16[128,1152]{1,0:T(8,128)(2,1)S(1)}, u32[]{:S(2)}, u32[]{:S(2)}) collective-permute-start(bf16[128,1152]{1,0:T(8,128)(2,1)S(1)} %collective-permute-done.2), channel_id=1, source_target_pairs={{0,32},{1,481},{32,64},{33,1},{64,96},{65,33},{96,128},{97,65},{12... | collective-permute-start | bytes 884744 | tf_op jit(solution)/shard_map/ppermute | solution.py:28
  29.0 1.9 collective-permute-start
  31.0 2.7 %collective-permute-start.5 = (bf16[128,1152]{1,0:T(8,128)(2,1)S(1)}, bf16[128,1152]{1,0:T(8,128)(2,1)S(1)}, u32[]{:S(2)}, u32[]{:S(2)}) collective-permute-start(bf16[128,1152]{1,0:T(8,128)(2,1)S(1)} %collective-permute-done.4), channel_id=1, source_target_pairs={{0,32},{1,481},{32,64},{33,1},{64,96},{65,33},{96,128},{97,65},{12... | collective-permute-start | bytes 884744 | tf_op jit(solution)/shard_map/ppermute | solution.py:28
  33.7 4.0 %collective-permute-start.9 = (bf16[128,1152]{1,0:T(8,128)(2,1)S(1)}, bf16[128,1152]{1,0:T(8,128)(2,1)S(1)}, u32[]{:S(2)}, u32[]{:S(2)}) collective-permute-start(bf16[128,1152]{1,0:T(8,128)(2,1)S(1)} %collective-permute-done.8), channel_id=1, source_target_pairs={{0,32},{1,481},{32,64},{33,1},{64,96},{65,33},{96,128},{97,65},{12... | collective-permute-start | bytes 884744 | tf_op jit(solution)/shard_map/ppermute | solution.py:28
  38.1 1.9 collective-permute-start.1
  40.0 2.5 %collective-permute-start.6 = (bf16[128,1152]{1,0:T(8,128)(2,1)S(1)}, bf16[128,1152]{1,0:T(8,128)(2,1)S(1)}, u32[]{:S(2)}, u32[]{:S(2)}) collective-permute-start(bf16[128,1152]{1,0:T(8,128)(2,1)S(1)} %collective-permute-done.5), channel_id=1, source_target_pairs={{0,32},{1,481},{32,64},{33,1},{64,96},{65,33},{96,128},{97,65},{12... | collective-permute-start | bytes 884744 | tf_op jit(solution)/shard_map/ppermute | solution.py:28
  42.5 3.9 %collective-permute-start.10 = (bf16[128,1152]{1,0:T(8,128)(2,1)S(1)}, bf16[128,1152]{1,0:T(8,128)(2,1)S(1)}, u32[]{:S(2)}, u32[]{:S(2)}) collective-permute-start(bf16[128,1152]{1,0:T(8,128)(2,1)S(1)} %collective-permute-done.9), channel_id=1, source_target_pairs={{0,32},{1,481},{32,64},{33,1},{64,96},{65,33},{96,128},{97,65},{12... | collective-permute-start | bytes 884744 | tf_op jit(solution)/shard_map/ppermute | solution.py:28
  46.4 0.6 broadcast_in_dim.67
  47.1 0.7 collective-permute-done.6
  47.8 3.4 %collective-permute-start.11 = (bf16[128,1152]{1,0:T(8,128)(2,1)S(1)}, bf16[128,1152]{1,0:T(8,128)(2,1)S(1)}, u32[]{:S(2)}, u32[]{:S(2)}) collective-permute-start(bf16[128,1152]{1,0:T(8,128)(2,1)S(1)} %collective-permute-done.6), channel_id=1, source_target_pairs={{0,32},{1,481},{32,64},{33,1},{64,96},{65,33},{96,128},{97,65},{12... | collective-permute-start | bytes 884744 | tf_op jit(solution)/shard_map/ppermute | solution.py:28
  51.2 3.9 %collective-permute-start.14 = (bf16[128,1152]{1,0:T(8,128)(2,1)S(1)}, bf16[128,1152]{1,0:T(8,128)(2,1)S(1)}, u32[]{:S(2)}, u32[]{:S(2)}) collective-permute-start(bf16[128,1152]{1,0:T(8,128)(2,1)S(1)} %collective-permute-done.10), channel_id=1, source_target_pairs={{0,32},{1,481},{32,64},{33,1},{64,96},{65,33},{96,128},{97,65},{12... | collective-permute-start | bytes 884744 | tf_op jit(solution)/shard_map/ppermute | solution.py:28
  55.0 0.1 multiply_reduce_fusion
  55.2 0.1 pad_maximum_fusion.1
  55.3 2.3 %collective-permute-start.7 = (bf16[3,128,1152]{2,1,0:T(8,128)(2,1)S(1)}, bf16[3,128,1152]{2,1,0:T(8,128)(2,1)S(1)}, u32[]{:S(2)}, u32[]{:S(2)}) collective-permute-start(bf16[3,128,1152]{2,1,0:T(8,128)(2,1)S(1)} %pad_maximum_fusion.1), channel_id=1, source_target_pairs={{0,1},{1,0},{2,3},{3,2},{4,5},{5,4},{6,7},{7,6},{8,9},{9,8},{10,11... | collective-permute-start | bytes 2654216 | tf_op jit(solution)/shard_map/ppermute | solution.py:53
  57.6 4.9 %collective-permute-start.12 = (bf16[128,1152]{1,0:T(8,128)(2,1)S(1)}, bf16[128,1152]{1,0:T(8,128)(2,1)S(1)}, u32[]{:S(2)}, u32[]{:S(2)}) collective-permute-start(bf16[128,1152]{1,0:T(8,128)(2,1)S(1)} %collective-permute-done.11), channel_id=1, source_target_pairs={{0,32},{1,481},{32,64},{33,1},{64,96},{65,33},{96,128},{97,65},{12... | collective-permute-start | bytes 884744 | tf_op jit(solution)/shard_map/ppermute | solution.py:28
  62.5 2.4 %collective-permute-start.15 = (bf16[128,1152]{1,0:T(8,128)(2,1)S(1)}, bf16[128,1152]{1,0:T(8,128)(2,1)S(1)}, u32[]{:S(2)}, u32[]{:S(2)}) collective-permute-start(bf16[128,1152]{1,0:T(8,128)(2,1)S(1)} %collective-permute-done.14), channel_id=1, source_target_pairs={{0,32},{1,481},{32,64},{33,1},{64,96},{65,33},{96,128},{97,65},{12... | collective-permute-start | bytes 884744 | tf_op jit(solution)/shard_map/ppermute | solution.py:28
  64.9 1.2 collective-permute-done.12
  66.1 5.0 %collective-permute-start.16 = (bf16[128,1152]{1,0:T(8,128)(2,1)S(1)}, bf16[128,1152]{1,0:T(8,128)(2,1)S(1)}, u32[]{:S(2)}, u32[]{:S(2)}) collective-permute-start(bf16[128,1152]{1,0:T(8,128)(2,1)S(1)} %collective-permute-done.12), channel_id=1, source_target_pairs={{0,32},{1,481},{32,64},{33,1},{64,96},{65,33},{96,128},{97,65},{12... | collective-permute-start | bytes 884744 | tf_op jit(solution)/shard_map/ppermute | solution.py:28
  71.2 3.1 %collective-permute-start.19 = (bf16[128,1152]{1,0:T(8,128)(2,1)S(1)}, bf16[128,1152]{1,0:T(8,128)(2,1)S(1)}, u32[]{:S(2)}, u32[]{:S(2)}) collective-permute-start(bf16[128,1152]{1,0:T(8,128)(2,1)S(1)} %collective-permute-done.15), channel_id=1, source_target_pairs={{0,32},{1,481},{32,64},{33,1},{64,96},{65,33},{96,128},{97,65},{12... | collective-permute-start | bytes 884744 | tf_op jit(solution)/shard_map/ppermute | solution.py:28
  74.3 0.1 pad_maximum_fusion.2
  74.4 2.7 %collective-permute-start.13 = (bf16[2,128,1152]{2,1,0:T(8,128)(2,1)S(1)}, bf16[2,128,1152]{2,1,0:T(8,128)(2,1)S(1)}, u32[]{:S(2)}, u32[]{:S(2)}) collective-permute-start(bf16[2,128,1152]{2,1,0:T(8,128)(2,1)S(1)} %pad_maximum_fusion.2), channel_id=1, source_target_pairs={{0,1},{1,0},{2,3},{3,2},{4,5},{5,4},{6,7},{7,6},{8,9},{9,8},{10,11... | collective-permute-start | bytes 1769480 | tf_op jit(solution)/shard_map/ppermute | solution.py:53
  77.1 4.9 %collective-permute-start.17 = (bf16[128,1152]{1,0:T(8,128)(2,1)S(1)}, bf16[128,1152]{1,0:T(8,128)(2,1)S(1)}, u32[]{:S(2)}, u32[]{:S(2)}) collective-permute-start(bf16[128,1152]{1,0:T(8,128)(2,1)S(1)} %collective-permute-done.16), channel_id=1, source_target_pairs={{0,32},{1,481},{32,64},{33,1},{64,96},{65,33},{96,128},{97,65},{12... | collective-permute-start | bytes 884744 | tf_op jit(solution)/shard_map/ppermute | solution.py:28
  82.0 2.4 %collective-permute-start.20 = (bf16[128,1152]{1,0:T(8,128)(2,1)S(1)}, bf16[128,1152]{1,0:T(8,128)(2,1)S(1)}, u32[]{:S(2)}, u32[]{:S(2)}) collective-permute-start(bf16[128,1152]{1,0:T(8,128)(2,1)S(1)} %collective-permute-done.19), channel_id=1, source_target_pairs={{0,32},{1,481},{32,64},{33,1},{64,96},{65,33},{96,128},{97,65},{12... | collective-permute-start | bytes 884744 | tf_op jit(solution)/shard_map/ppermute | solution.py:28
  84.7 0.9 collective-permute-done.17
  85.6 0.1 pad_maximum_fusion.3
  85.7 5.9 %collective-permute-start.18 = (bf16[2,128,1152]{2,1,0:T(8,128)(2,1)S(1)}, bf16[2,128,1152]{2,1,0:T(8,128)(2,1)S(1)}, u32[]{:S(2)}, u32[]{:S(2)}) collective-permute-start(bf16[2,128,1152]{2,1,0:T(8,128)(2,1)S(1)} %pad_maximum_fusion.3), channel_id=1, source_target_pairs={{0,1},{1,0},{2,3},{3,2},{4,5},{5,4},{6,7},{7,6},{8,9},{9,8},{10,11... | collective-permute-start | bytes 1769480 | tf_op jit(solution)/shard_map/ppermute | solution.py:53
  91.8 1.4 collective-permute-done.18
  93.4 1.6 fusion
  95.0 0.5 copy-done
  95.5 0.1 pad_maximum_fusion
  95.6 24.5 %all_to_all.15 = bf16[16,264,128]{2,1,0:T(8,128)(2,1)S(1)} all-to-all(bf16[16,264,128]{2,1,0:T(8,128)(2,1)S(1)} %pad_maximum_fusion), channel_id=1, replica_groups=mesh['zh'=4,'zl'=4,'ylo'=2,'x'=4,'yhi'=2,'core'=2] {'ylo','yhi','x'}, dimensions={0} | all-to-all | bytes 2162688 | tf_op jit(solution)/shard_map/all_to_all | solution.py:109
  120.1 0.1 convert_reduce_fusion
  120.3 1.2 broadcast_in_dim.79
  121.5 3.7 %all-to-all-start.1 = ((bf16[16,256,128]{2,1,0:T(8,128)(2,1)}), bf16[16,256,128]{2,1,0:T(8,128)(2,1)S(1)}, u32[]{:S(2)}, u32[]{:S(2)}) async-start(bf16[16,256,128]{2,1,0:T(8,128)(2,1)} %broadcast_in_dim.79), calls=%async_computation.1 | async-start | bytes 2097152 | tf_op jit(solution)/shard_map/all_to_all | solution.py:17
  125.2 16.6 %all-gather = bf16[1024,128]{1,0:T(8,128)(2,1)S(1)} all-gather(bf16[256,128]{1,0:T(8,128)(2,1)S(1)} %fusion.35), channel_id=2, replica_groups=mesh['zh'=4,'zl'=4,'ylo'=2,'x'=4,'yhi'=2,'core'=2] {'zh'}, dimensions={0}, use_global_device_ids=true | all-gather | bytes 327680 | tf_op jit(solution)/shard_map/all_gather | solution.py:121
  141.8 1.9 collective-permute-start.23
  143.8 4.6 %collective-permute-start.22 = (bf16[4,256,128]{2,1,0:T(8,128)(2,1)S(1)}, bf16[4,256,128]{2,1,0:T(8,128)(2,1)S(1)}, u32[]{:S(2)}, u32[]{:S(2)}) collective-permute-start(bf16[4,256,128]{2,1,0:T(8,128)(2,1)S(1)} %bitcast.100), channel_id=1, source_target_pairs={{0,480},{1,481},{32,0},{33,1},{64,32},{65,33},{96,64},{97,65},{128... | collective-permute-start | bytes 786440 | tf_op jit(solution)/shard_map/ppermute | solution.py:28
  148.3 1.9 collective-permute-start.21
  150.3 0.1 dynamic-slice_bitcast_fusion.1
  150.4 7.7 %collective-permute-start.25 = (bf16[2,4,256,128]{3,2,1,0:T(8,128)(2,1)S(1)}, bf16[2,4,256,128]{3,2,1,0:T(8,128)(2,1)S(1)}, u32[]{:S(2)}, u32[]{:S(2)}) collective-permute-start(bf16[2,4,256,128]{3,2,1,0:T(8,128)(2,1)S(1)} %pad_maximum_fusion.5), channel_id=1, source_target_pairs={{0,1},{1,0},{2,3},{3,2},{4,5},{5,4},{6,7},{7,6},{8,9},{9,8},{10,11... | collective-permute-start | bytes 1572872 | tf_op jit(solution)/shard_map/ppermute | solution.py:53
  158.1 0.2 convolution_bitcast_fusion.8
  158.4 2.2 %collective-permute-start.24 = (bf16[2,4,256,128]{3,2,1,0:T(8,128)(2,1)S(1)}, bf16[2,4,256,128]{3,2,1,0:T(8,128)(2,1)S(1)}, u32[]{:S(2)}, u32[]{:S(2)}) collective-permute-start(bf16[2,4,256,128]{3,2,1,0:T(8,128)(2,1)S(1)} %pad_maximum_fusion.4), channel_id=1, source_target_pairs={{0,1},{1,0},{2,3},{3,2},{4,5},{5,4},{6,7},{7,6},{8,9},{9,8},{10,11... | collective-permute-start | bytes 1572872 | tf_op jit(solution)/shard_map/ppermute | solution.py:53
  160.6 0.2 fusion.1
  160.9 0.2 convolution_bitcast_fusion.6
  161.1 0.2 convolution_bitcast_fusion.5
  161.5 1.0 collective-permute-done.24
  162.6 0.2 convolution_bitcast_fusion.4
  162.8 0.2 fusion.2
  163.1 0.2 convolution_bitcast_fusion.2
  163.3 0.2 convolution_bitcast_fusion.1
  163.6 0.2 broadcast_in_dim.81
  163.8 20.7 %all_to_all.16 = bf16[16,256,128]{2,1,0:T(8,128)(2,1)S(1)} all-to-all(bf16[16,256,128]{2,1,0:T(8,128)(2,1)S(1)} %broadcast_in_dim.81), channel_id=1, replica_groups=mesh['zh'=4,'zl'=4,'ylo'=2,'x'=4,'yhi'=2,'core'=2] {'ylo','yhi','x'}, dimensions={0} | all-to-all | bytes 2097152 | tf_op jit(solution)/shard_map/all_to_all | solution.py:17
  184.6 1.5 convolution_bitcast_fusion
  186.1 0.1 fusion.3
  186.2 6.0 %collective-permute-start.26 = (bf16[128,1152]{1,0:T(8,128)(2,1)S(1)}, bf16[128,1152]{1,0:T(8,128)(2,1)S(1)}, u32[]{:S(2)}, u32[]{:S(2)}) collective-permute-start(bf16[128,1152]{1,0:T(8,128)(2,1)S(1)} %fusion.3), channel_id=1, source_target_pairs={{0,0},{1,16},{16,1},{17,17},{2,2},{3,18},{18,3},{19,19},{4,4},{5,2... | collective-permute-start | bytes 884744 | tf_op jit(solution)/shard_map/ppermute | solution.py:150
  192.2 1.9 collective-permute-start.27
  194.2 2.5 %collective-permute-done.26 = bf16[128,1152]{1,0:T(8,128)(2,1)S(1)} collective-permute-done((bf16[128,1152]{1,0:T(8,128)(2,1)S(1)}, bf16[128,1152]{1,0:T(8,128)(2,1)S(1)}, u32[]{:S(2)}, u32[]{:S(2)}) %collective-permute-start.26) | collective-permute-done | bytes 294944 | tf_op jit(solution)/shard_map/ppermute | solution.py:150
  196.6 3.1 %collective-permute-done.27 = bf16[128,1152]{1,0:T(8,128)(2,1)S(1)} collective-permute-done((bf16[128,1152]{1,0:T(8,128)(2,1)S(1)}, bf16[128,1152]{1,0:T(8,128)(2,1)S(1)}, u32[]{:S(2)}, u32[]{:S(2)}) %collective-permute-start.27) | collective-permute-done | bytes 294944 | tf_op jit(solution)/shard_map/ppermute | solution.py:148
  199.8 0.9 convert_add_fusion
  (64 shorter events, 1.2 us)
Async XLA Ops:
  1.1 10.7 %collective-permute-start.3 = (bf16[128,1152]{1,0:T(8,128)(2,1)S(1)}, bf16[128,1152]{1,0:T(8,128)(2,1)S(1)}, u32[]{:S(2)}, u32[]{:S(2)}) collective-permute-start(bf16[128,1152]{1,0:T(8,128)(2,1)S(1)} %convert_element_type.37), channel_id=1, source_target_pairs={{0,1},{1,0},{2,3},{3,2},{4,5},{5,4},{6,7},{7,6},{8,9},{9,8},{10,11... | collective-permute-start | bytes 884744 | tf_op jit(solution)/shard_map/ppermute | solution.py:83
  9.9 9.2 %collective-permute-start.2 = (bf16[128,1152]{1,0:T(8,128)(2,1)S(1)}, bf16[128,1152]{1,0:T(8,128)(2,1)S(1)}, u32[]{:S(2)}, u32[]{:S(2)}) collective-permute-start(bf16[128,1152]{1,0:T(8,128)(2,1)S(1)} %convert_element_type.37), channel_id=1, source_target_pairs={{0,32},{1,48},{16,481},{17,497},{32,64},{33,80},{48,1},{49,17},{64... | collective-permute-start | bytes 884744 | tf_op jit(solution)/shard_map/ppermute | solution.py:49
  11.8 19.1 %collective-permute-start.4 = (bf16[128,1152]{1,0:T(8,128)(2,1)S(1)}, bf16[128,1152]{1,0:T(8,128)(2,1)S(1)}, u32[]{:S(2)}, u32[]{:S(2)}) collective-permute-start(bf16[128,1152]{1,0:T(8,128)(2,1)S(1)} %collective-permute-done.3), channel_id=1, source_target_pairs={{0,497},{1,481},{16,48},{17,32},{32,17},{33,1},{48,80},{49,64},{64... | collective-permute-start | bytes 884744 | tf_op jit(solution)/shard_map/ppermute | solution.py:49
  19.1 14.6 %collective-permute-start.8 = (bf16[128,1152]{1,0:T(8,128)(2,1)S(1)}, bf16[128,1152]{1,0:T(8,128)(2,1)S(1)}, u32[]{:S(2)}, u32[]{:S(2)}) collective-permute-start(bf16[128,1152]{1,0:T(8,128)(2,1)S(1)} %collective-permute-done.2), channel_id=1, source_target_pairs={{0,32},{1,481},{32,64},{33,1},{64,96},{65,33},{96,128},{97,65},{12... | collective-permute-start | bytes 884744 | tf_op jit(solution)/shard_map/ppermute | solution.py:28
  29.0 9.0 %collective-permute-start = (bf16[128,1152]{1,0:T(8,128)(2,1)S(1)}, bf16[128,1152]{1,0:T(8,128)(2,1)S(1)}, u32[]{:S(2)}, u32[]{:S(2)}) collective-permute-start(bf16[128,1152]{1,0:T(8,128)(2,1)S(1)} %convert_element_type.37), channel_id=1, source_target_pairs={{0,0},{1,16},{16,1},{17,17},{2,2},{3,18},{18,3},{19,19},{4,4},{5,2... | collective-permute-start | bytes 884744 | tf_op jit(solution)/shard_map/ppermute | solution.py:80
  31.0 9.0 %collective-permute-start.5 = (bf16[128,1152]{1,0:T(8,128)(2,1)S(1)}, bf16[128,1152]{1,0:T(8,128)(2,1)S(1)}, u32[]{:S(2)}, u32[]{:S(2)}) collective-permute-start(bf16[128,1152]{1,0:T(8,128)(2,1)S(1)} %collective-permute-done.4), channel_id=1, source_target_pairs={{0,32},{1,481},{32,64},{33,1},{64,96},{65,33},{96,128},{97,65},{12... | collective-permute-start | bytes 884744 | tf_op jit(solution)/shard_map/ppermute | solution.py:28
  33.7 8.8 %collective-permute-start.9 = (bf16[128,1152]{1,0:T(8,128)(2,1)S(1)}, bf16[128,1152]{1,0:T(8,128)(2,1)S(1)}, u32[]{:S(2)}, u32[]{:S(2)}) collective-permute-start(bf16[128,1152]{1,0:T(8,128)(2,1)S(1)} %collective-permute-done.8), channel_id=1, source_target_pairs={{0,32},{1,481},{32,64},{33,1},{64,96},{65,33},{96,128},{97,65},{12... | collective-permute-start | bytes 884744 | tf_op jit(solution)/shard_map/ppermute | solution.py:28
  38.1 55.3 %collective-permute-start.1 = (bf16[128,1152]{1,0:T(8,128)(2,1)S(1)}, bf16[128,1152]{1,0:T(8,128)(2,1)S(1)}, u32[]{:S(2)}, u32[]{:S(2)}) collective-permute-start(bf16[128,1152]{1,0:T(8,128)(2,1)S(1)} %collective-permute-done), channel_id=1, source_target_pairs={{0,1},{1,0},{2,3},{3,2},{4,5},{5,4},{6,7},{7,6},{8,9},{9,8},{10,11... | collective-permute-start | bytes 884744 | tf_op jit(solution)/shard_map/ppermute | solution.py:81
  40.0 7.8 %collective-permute-start.6 = (bf16[128,1152]{1,0:T(8,128)(2,1)S(1)}, bf16[128,1152]{1,0:T(8,128)(2,1)S(1)}, u32[]{:S(2)}, u32[]{:S(2)}) collective-permute-start(bf16[128,1152]{1,0:T(8,128)(2,1)S(1)} %collective-permute-done.5), channel_id=1, source_target_pairs={{0,32},{1,481},{32,64},{33,1},{64,96},{65,33},{96,128},{97,65},{12... | collective-permute-start | bytes 884744 | tf_op jit(solution)/shard_map/ppermute | solution.py:28
  42.5 8.7 %collective-permute-start.10 = (bf16[128,1152]{1,0:T(8,128)(2,1)S(1)}, bf16[128,1152]{1,0:T(8,128)(2,1)S(1)}, u32[]{:S(2)}, u32[]{:S(2)}) collective-permute-start(bf16[128,1152]{1,0:T(8,128)(2,1)S(1)} %collective-permute-done.9), channel_id=1, source_target_pairs={{0,32},{1,481},{32,64},{33,1},{64,96},{65,33},{96,128},{97,65},{12... | collective-permute-start | bytes 884744 | tf_op jit(solution)/shard_map/ppermute | solution.py:28
  47.8 9.8 %collective-permute-start.11 = (bf16[128,1152]{1,0:T(8,128)(2,1)S(1)}, bf16[128,1152]{1,0:T(8,128)(2,1)S(1)}, u32[]{:S(2)}, u32[]{:S(2)}) collective-permute-start(bf16[128,1152]{1,0:T(8,128)(2,1)S(1)} %collective-permute-done.6), channel_id=1, source_target_pairs={{0,32},{1,481},{32,64},{33,1},{64,96},{65,33},{96,128},{97,65},{12... | collective-permute-start | bytes 884744 | tf_op jit(solution)/shard_map/ppermute | solution.py:28
  51.2 11.3 %collective-permute-start.14 = (bf16[128,1152]{1,0:T(8,128)(2,1)S(1)}, bf16[128,1152]{1,0:T(8,128)(2,1)S(1)}, u32[]{:S(2)}, u32[]{:S(2)}) collective-permute-start(bf16[128,1152]{1,0:T(8,128)(2,1)S(1)} %collective-permute-done.10), channel_id=1, source_target_pairs={{0,32},{1,481},{32,64},{33,1},{64,96},{65,33},{96,128},{97,65},{12... | collective-permute-start | bytes 884744 | tf_op jit(solution)/shard_map/ppermute | solution.py:28
  55.3 29.1 %collective-permute-start.7 = (bf16[3,128,1152]{2,1,0:T(8,128)(2,1)S(1)}, bf16[3,128,1152]{2,1,0:T(8,128)(2,1)S(1)}, u32[]{:S(2)}, u32[]{:S(2)}) collective-permute-start(bf16[3,128,1152]{2,1,0:T(8,128)(2,1)S(1)} %pad_maximum_fusion.1), channel_id=1, source_target_pairs={{0,1},{1,0},{2,3},{3,2},{4,5},{5,4},{6,7},{7,6},{8,9},{9,8},{10,11... | collective-permute-start | bytes 2654216 | tf_op jit(solution)/shard_map/ppermute | solution.py:53
  57.6 8.5 %collective-permute-start.12 = (bf16[128,1152]{1,0:T(8,128)(2,1)S(1)}, bf16[128,1152]{1,0:T(8,128)(2,1)S(1)}, u32[]{:S(2)}, u32[]{:S(2)}) collective-permute-start(bf16[128,1152]{1,0:T(8,128)(2,1)S(1)} %collective-permute-done.11), channel_id=1, source_target_pairs={{0,32},{1,481},{32,64},{33,1},{64,96},{65,33},{96,128},{97,65},{12... | collective-permute-start | bytes 884744 | tf_op jit(solution)/shard_map/ppermute | solution.py:28
  62.5 8.7 %collective-permute-start.15 = (bf16[128,1152]{1,0:T(8,128)(2,1)S(1)}, bf16[128,1152]{1,0:T(8,128)(2,1)S(1)}, u32[]{:S(2)}, u32[]{:S(2)}) collective-permute-start(bf16[128,1152]{1,0:T(8,128)(2,1)S(1)} %collective-permute-done.14), channel_id=1, source_target_pairs={{0,32},{1,481},{32,64},{33,1},{64,96},{65,33},{96,128},{97,65},{12... | collective-permute-start | bytes 884744 | tf_op jit(solution)/shard_map/ppermute | solution.py:28
  66.1 11.0 %collective-permute-start.16 = (bf16[128,1152]{1,0:T(8,128)(2,1)S(1)}, bf16[128,1152]{1,0:T(8,128)(2,1)S(1)}, u32[]{:S(2)}, u32[]{:S(2)}) collective-permute-start(bf16[128,1152]{1,0:T(8,128)(2,1)S(1)} %collective-permute-done.12), channel_id=1, source_target_pairs={{0,32},{1,481},{32,64},{33,1},{64,96},{65,33},{96,128},{97,65},{12... | collective-permute-start | bytes 884744 | tf_op jit(solution)/shard_map/ppermute | solution.py:28
  71.2 10.8 %collective-permute-start.19 = (bf16[128,1152]{1,0:T(8,128)(2,1)S(1)}, bf16[128,1152]{1,0:T(8,128)(2,1)S(1)}, u32[]{:S(2)}, u32[]{:S(2)}) collective-permute-start(bf16[128,1152]{1,0:T(8,128)(2,1)S(1)} %collective-permute-done.15), channel_id=1, source_target_pairs={{0,32},{1,481},{32,64},{33,1},{64,96},{65,33},{96,128},{97,65},{12... | collective-permute-start | bytes 884744 | tf_op jit(solution)/shard_map/ppermute | solution.py:28
  74.4 17.2 %collective-permute-start.13 = (bf16[2,128,1152]{2,1,0:T(8,128)(2,1)S(1)}, bf16[2,128,1152]{2,1,0:T(8,128)(2,1)S(1)}, u32[]{:S(2)}, u32[]{:S(2)}) collective-permute-start(bf16[2,128,1152]{2,1,0:T(8,128)(2,1)S(1)} %pad_maximum_fusion.2), channel_id=1, source_target_pairs={{0,1},{1,0},{2,3},{3,2},{4,5},{5,4},{6,7},{7,6},{8,9},{9,8},{10,11... | collective-permute-start | bytes 1769480 | tf_op jit(solution)/shard_map/ppermute | solution.py:53
  77.1 8.5 %collective-permute-start.17 = (bf16[128,1152]{1,0:T(8,128)(2,1)S(1)}, bf16[128,1152]{1,0:T(8,128)(2,1)S(1)}, u32[]{:S(2)}, u32[]{:S(2)}) collective-permute-start(bf16[128,1152]{1,0:T(8,128)(2,1)S(1)} %collective-permute-done.16), channel_id=1, source_target_pairs={{0,32},{1,481},{32,64},{33,1},{64,96},{65,33},{96,128},{97,65},{12... | collective-permute-start | bytes 884744 | tf_op jit(solution)/shard_map/ppermute | solution.py:28
  82.0 11.4 %collective-permute-start.20 = (bf16[128,1152]{1,0:T(8,128)(2,1)S(1)}, bf16[128,1152]{1,0:T(8,128)(2,1)S(1)}, u32[]{:S(2)}, u32[]{:S(2)}) collective-permute-start(bf16[128,1152]{1,0:T(8,128)(2,1)S(1)} %collective-permute-done.19), channel_id=1, source_target_pairs={{0,32},{1,481},{32,64},{33,1},{64,96},{65,33},{96,128},{97,65},{12... | collective-permute-start | bytes 884744 | tf_op jit(solution)/shard_map/ppermute | solution.py:28
  85.7 7.5 %collective-permute-start.18 = (bf16[2,128,1152]{2,1,0:T(8,128)(2,1)S(1)}, bf16[2,128,1152]{2,1,0:T(8,128)(2,1)S(1)}, u32[]{:S(2)}, u32[]{:S(2)}) collective-permute-start(bf16[2,128,1152]{2,1,0:T(8,128)(2,1)S(1)} %pad_maximum_fusion.3), channel_id=1, source_target_pairs={{0,1},{1,0},{2,3},{3,2},{4,5},{5,4},{6,7},{7,6},{8,9},{9,8},{10,11... | collective-permute-start | bytes 1769480 | tf_op jit(solution)/shard_map/ppermute | solution.py:53
  93.4 2.1 %copy-start = (bf16[16,128,1152]{2,1,0:T(8,128)(2,1)}, bf16[16,128,1152]{2,1,0:T(8,128)(2,1)S(1)}, u32[]{:S(2)}) copy-start(bf16[16,128,1152]{2,1,0:T(8,128)(2,1)S(1)} %bitcast_dynamic-update-slice_fusion) | copy-start | bytes 14155780
  121.5 28.8 %all-to-all-start.1 = ((bf16[16,256,128]{2,1,0:T(8,128)(2,1)}), bf16[16,256,128]{2,1,0:T(8,128)(2,1)S(1)}, u32[]{:S(2)}, u32[]{:S(2)}) async-start(bf16[16,256,128]{2,1,0:T(8,128)(2,1)} %broadcast_in_dim.79), calls=%async_computation.1 | async-start | bytes 2097152 | tf_op jit(solution)/shard_map/all_to_all | solution.py:17
  141.8 19.3 %collective-permute-start.23 = (bf16[4,256,128]{2,1,0:T(8,128)(2,1)S(1)}, bf16[4,256,128]{2,1,0:T(8,128)(2,1)S(1)}, u32[]{:S(2)}, u32[]{:S(2)}) collective-permute-start(bf16[4,256,128]{2,1,0:T(8,128)(2,1)S(1)} %bitcast.99), channel_id=1, source_target_pairs={{0,32},{1,33},{32,64},{33,65},{64,96},{65,97},{96,128},{97,129},{1... | collective-permute-start | bytes 786440 | tf_op jit(solution)/shard_map/ppermute | solution.py:28
  143.8 17.1 %collective-permute-start.22 = (bf16[4,256,128]{2,1,0:T(8,128)(2,1)S(1)}, bf16[4,256,128]{2,1,0:T(8,128)(2,1)S(1)}, u32[]{:S(2)}, u32[]{:S(2)}) collective-permute-start(bf16[4,256,128]{2,1,0:T(8,128)(2,1)S(1)} %bitcast.100), channel_id=1, source_target_pairs={{0,480},{1,481},{32,0},{33,1},{64,32},{65,33},{96,64},{97,65},{128... | collective-permute-start | bytes 786440 | tf_op jit(solution)/shard_map/ppermute | solution.py:28
  148.3 12.3 %collective-permute-start.21 = (bf16[4,256,128]{2,1,0:T(8,128)(2,1)S(1)}, bf16[4,256,128]{2,1,0:T(8,128)(2,1)S(1)}, u32[]{:S(2)}, u32[]{:S(2)}) collective-permute-start(bf16[4,256,128]{2,1,0:T(8,128)(2,1)S(1)} %bitcast.101), channel_id=1, source_target_pairs={{0,448},{1,65},{32,480},{33,97},{64,0},{65,129},{96,32},{97,161},{... | collective-permute-start | bytes 786440 | tf_op jit(solution)/shard_map/ppermute | solution.py:28
  150.4 10.9 %collective-permute-start.25 = (bf16[2,4,256,128]{3,2,1,0:T(8,128)(2,1)S(1)}, bf16[2,4,256,128]{3,2,1,0:T(8,128)(2,1)S(1)}, u32[]{:S(2)}, u32[]{:S(2)}) collective-permute-start(bf16[2,4,256,128]{3,2,1,0:T(8,128)(2,1)S(1)} %pad_maximum_fusion.5), channel_id=1, source_target_pairs={{0,1},{1,0},{2,3},{3,2},{4,5},{5,4},{6,7},{7,6},{8,9},{9,8},{10,11... | collective-permute-start | bytes 1572872 | tf_op jit(solution)/shard_map/ppermute | solution.py:53
  158.4 26.2 %slice-start = ((s8[4718592]{0:T(1024)(128)(4,1)}), s8[4194304]{0:T(1024)(128)(4,1)S(1)}, s32[]{:S(2)}) async-start(s8[4718592]{0:T(1024)(128)(4,1)} %bitcast.97), calls=%async_computation.3 | async-start | bytes 8388608
  158.4 4.1 %collective-permute-start.24 = (bf16[2,4,256,128]{3,2,1,0:T(8,128)(2,1)S(1)}, bf16[2,4,256,128]{3,2,1,0:T(8,128)(2,1)S(1)}, u32[]{:S(2)}, u32[]{:S(2)}) collective-permute-start(bf16[2,4,256,128]{3,2,1,0:T(8,128)(2,1)S(1)} %pad_maximum_fusion.4), channel_id=1, source_target_pairs={{0,1},{1,0},{2,3},{3,2},{4,5},{5,4},{6,7},{7,6},{8,9},{9,8},{10,11... | collective-permute-start | bytes 1572872 | tf_op jit(solution)/shard_map/ppermute | solution.py:53
  162.6 22.0 %slice-start.1 = ((s8[4718592]{0:T(1024)(128)(4,1)}), s8[524288]{0:T(1024)(128)(4,1)S(1)}, s32[]{:S(2)}) async-start(s8[4718592]{0:T(1024)(128)(4,1)} %bitcast.97), calls=%async_computation.4 | async-start | bytes 1048576
  186.2 10.4 %collective-permute-start.26 = (bf16[128,1152]{1,0:T(8,128)(2,1)S(1)}, bf16[128,1152]{1,0:T(8,128)(2,1)S(1)}, u32[]{:S(2)}, u32[]{:S(2)}) collective-permute-start(bf16[128,1152]{1,0:T(8,128)(2,1)S(1)} %fusion.3), channel_id=1, source_target_pairs={{0,0},{1,16},{16,1},{17,17},{2,2},{3,18},{18,3},{19,19},{4,4},{5,2... | collective-permute-start | bytes 884744 | tf_op jit(solution)/shard_map/ppermute | solution.py:150
  192.2 7.6 %collective-permute-start.27 = (bf16[128,1152]{1,0:T(8,128)(2,1)S(1)}, bf16[128,1152]{1,0:T(8,128)(2,1)S(1)}, u32[]{:S(2)}, u32[]{:S(2)}) collective-permute-start(bf16[128,1152]{1,0:T(8,128)(2,1)S(1)} %slice.127), channel_id=1, source_target_pairs={{0,16},{1,0},{16,17},{17,1},{2,18},{3,2},{18,19},{19,3},{4,20},{5,... | collective-permute-start | bytes 884744 | tf_op jit(solution)/shard_map/ppermute | solution.py:148

commit v23 on v18

--- a/solution.py
+++ b/solution.py
@@ -85,7 +85,7 @@
         near.append(onward(near[-1]))
         far.append(onward(far[-1]))
     near.append(onward(near[-1]))
-    back = [None] + swap(far[1:4]) + swap(far[4:6]) + swap(far[6:])
+    back = [None] + swap(far[1:6]) + swap(far[6:])
     slab, toward = lax.axis_index(LINE), 1 - 2 * lax.axis_index("core")
     half = jnp.zeros((slabs, rows, cols), jnp.bfloat16)
     for step in range(slabs // 2 + 1):

time: 202 us -> 207 us (1.025)
  waiting for transfers between devices: 12.4 us -> 18.2 us
  blocking collectives: 61.8 us -> 56.9 us
  starting transfers between devices: 114 us -> 118 us
    ppermute x16, waiting for transfers between devices: 2.88 us -> 11.3 us  [along(): return lax.ppermute(piece, LINE + ('core',), pairs)]
    ppermute x1, starting transfers between devices: 1.92 us -> 7.2 us  [per_device(): own = lax.ppermute(rounded, ('ylo', 'core'), TURN)]
    all_to_all x1, blocking collectives: 24.5 us -> 20.8 us  [per_device(): summands = lax.all_to_all(partial_gram, PLANE, 0, 0)]
    ppermute x2, starting transfers between devices: 7.67 us -> 4.56 us  [launch(): return lax.ppermute(piece, LINE + ('ylo', 'core'), pairs)]
    ppermute x5 -> x4, starting transfers between devices: 20.7 us -> 22.8 us  [swap(): return list(lax.ppermute(jnp.stack(pieces), 'core', SWAP))]
  transfers between devices with their start and end apart: 29 -> 28, of which waited for: 8 -> 11; matrix products, arithmetic and copies ran while one was open for 2% -> 2% of each run, Pallas kernels for 0% -> 0%
where the time goes in v23:
time: 207 us; the launch traced here: 206 us
  starting transfers between devices  118 us (57%)
  blocking collectives  56.9 us (27%)
  waiting for transfers between devices  18.2 us (9%)
  matrix products  4.99 us (2%)
  local copies, waits for them, and re-layouts  3.55 us (2%)
  other arithmetic  2.73 us (1%)
    ppermute x16, starting transfers between devices, along(): return lax.ppermute(piece, LINE + ('core',), pairs)  60.1 us
    ppermute x4, starting transfers between devices, swap(): return list(lax.ppermute(jnp.stack(pieces), 'core', SWAP))  22.8 us
    all_to_all x1, blocking collectives, per_device(): summands = lax.all_to_all(partial_gram, PLANE, 0, 0)  20.8 us
    all_to_all x1, blocking collectives, share(): return lax.all_to_all(copies, PLANE, 0, 0)  19.7 us
    all_gather x1, blocking collectives, per_device(): here = lax.all_gather(gram_low, 'zh', axis=0)  16.4 us
    ppermute x16, waiting for transfers between devices, along(): return lax.ppermute(piece, LINE + ('core',), pairs)  11.3 us
    ppermute x1, starting transfers between devices, per_device(): lax.ppermute(rounded, 'core', SWAP)  8.79 us
    ppermute x1, starting transfers between devices, per_device(): own = lax.ppermute(rounded, ('ylo', 'core'), TURN)  7.2 us
  transfers between devices with their start and end apart: 28, of which 11 were waited for; matrix products, arithmetic and copies ran while one was open for 2% of the time, Pallas kernels for 0%

profile of v23, /device:TPU:1, one launch (start us, length us, event | category | flops | bytes accessed | tf_op | source)
XLA Modules:
  0.0 205.5 jit_solution(2209848024078745787)
XLA Ops:
  0.0 1.1 convert_element_type.39
  1.1 8.8 %collective-permute-start.3 = (bf16[128,1152]{1,0:T(8,128)(2,1)S(1)}, bf16[128,1152]{1,0:T(8,128)(2,1)S(1)}, u32[]{:S(2)}, u32[]{:S(2)}) collective-permute-start(bf16[128,1152]{1,0:T(8,128)(2,1)S(1)} %convert_element_type.39), channel_id=1, source_target_pairs={{0,1},{1,0},{2,3},{3,2},{4,5},{5,4},{6,7},{7,6},{8,9},{9,8},{10,11... | collective-permute-start | bytes 884744 | tf_op jit(solution)/shard_map/ppermute | solution.py:83
  9.9 1.9 collective-permute-start.2
  11.8 7.2 %collective-permute-start = (bf16[128,1152]{1,0:T(8,128)(2,1)S(1)}, bf16[128,1152]{1,0:T(8,128)(2,1)S(1)}, u32[]{:S(2)}, u32[]{:S(2)}) collective-permute-start(bf16[128,1152]{1,0:T(8,128)(2,1)S(1)} %convert_element_type.39), channel_id=1, source_target_pairs={{0,0},{1,16},{16,1},{17,17},{2,2},{3,18},{18,3},{19,19},{4,4},{5,2... | collective-permute-start | bytes 884744 | tf_op jit(solution)/shard_map/ppermute | solution.py:80
  19.0 2.6 %collective-permute-start.4 = (bf16[128,1152]{1,0:T(8,128)(2,1)S(1)}, bf16[128,1152]{1,0:T(8,128)(2,1)S(1)}, u32[]{:S(2)}, u32[]{:S(2)}) collective-permute-start(bf16[128,1152]{1,0:T(8,128)(2,1)S(1)} %collective-permute-done.3), channel_id=1, source_target_pairs={{0,497},{1,481},{16,48},{17,32},{32,17},{33,1},{48,80},{49,64},{64... | collective-permute-start | bytes 884744 | tf_op jit(solution)/shard_map/ppermute | solution.py:49
  21.7 7.8 %collective-permute-start.10 = (bf16[128,1152]{1,0:T(8,128)(2,1)S(1)}, bf16[128,1152]{1,0:T(8,128)(2,1)S(1)}, u32[]{:S(2)}, u32[]{:S(2)}) collective-permute-start(bf16[128,1152]{1,0:T(8,128)(2,1)S(1)} %collective-permute-done.2), channel_id=1, source_target_pairs={{0,32},{1,481},{32,64},{33,1},{64,96},{65,33},{96,128},{97,65},{12... | collective-permute-start | bytes 884744 | tf_op jit(solution)/shard_map/ppermute | solution.py:28
  29.9 1.9 collective-permute-start.1
  31.8 0.1 multiply_reduce_fusion
  31.9 2.6 %collective-permute-start.5 = (bf16[128,1152]{1,0:T(8,128)(2,1)S(1)}, bf16[128,1152]{1,0:T(8,128)(2,1)S(1)}, u32[]{:S(2)}, u32[]{:S(2)}) collective-permute-start(bf16[128,1152]{1,0:T(8,128)(2,1)S(1)} %collective-permute-done.4), channel_id=1, source_target_pairs={{0,32},{1,481},{32,64},{33,1},{64,96},{65,33},{96,128},{97,65},{12... | collective-permute-start | bytes 884744 | tf_op jit(solution)/shard_map/ppermute | solution.py:28
  34.6 3.6 %collective-permute-start.11 = (bf16[128,1152]{1,0:T(8,128)(2,1)S(1)}, bf16[128,1152]{1,0:T(8,128)(2,1)S(1)}, u32[]{:S(2)}, u32[]{:S(2)}) collective-permute-start(bf16[128,1152]{1,0:T(8,128)(2,1)S(1)} %collective-permute-done.10), channel_id=1, source_target_pairs={{0,32},{1,481},{32,64},{33,1},{64,96},{65,33},{96,128},{97,65},{12... | collective-permute-start | bytes 884744 | tf_op jit(solution)/shard_map/ppermute | solution.py:28
  38.2 1.5 collective-permute-done.5
  39.7 3.5 %collective-permute-start.6 = (bf16[128,1152]{1,0:T(8,128)(2,1)S(1)}, bf16[128,1152]{1,0:T(8,128)(2,1)S(1)}, u32[]{:S(2)}, u32[]{:S(2)}) collective-permute-start(bf16[128,1152]{1,0:T(8,128)(2,1)S(1)} %collective-permute-done.5), channel_id=1, source_target_pairs={{0,32},{1,481},{32,64},{33,1},{64,96},{65,33},{96,128},{97,65},{12... | collective-permute-start | bytes 884744 | tf_op jit(solution)/shard_map/ppermute | solution.py:28
  43.3 3.6 %collective-permute-start.12 = (bf16[128,1152]{1,0:T(8,128)(2,1)S(1)}, bf16[128,1152]{1,0:T(8,128)(2,1)S(1)}, u32[]{:S(2)}, u32[]{:S(2)}) collective-permute-start(bf16[128,1152]{1,0:T(8,128)(2,1)S(1)} %collective-permute-done.11), channel_id=1, source_target_pairs={{0,32},{1,481},{32,64},{33,1},{64,96},{65,33},{96,128},{97,65},{12... | collective-permute-start | bytes 884744 | tf_op jit(solution)/shard_map/ppermute | solution.py:28
  46.9 0.3 collective-permute-done.6
  47.2 4.7 %collective-permute-start.7 = (bf16[128,1152]{1,0:T(8,128)(2,1)S(1)}, bf16[128,1152]{1,0:T(8,128)(2,1)S(1)}, u32[]{:S(2)}, u32[]{:S(2)}) collective-permute-start(bf16[128,1152]{1,0:T(8,128)(2,1)S(1)} %collective-permute-done.6), channel_id=1, source_target_pairs={{0,32},{1,481},{32,64},{33,1},{64,96},{65,33},{96,128},{97,65},{12... | collective-permute-start | bytes 884744 | tf_op jit(solution)/shard_map/ppermute | solution.py:28
  51.9 3.6 %collective-permute-start.13 = (bf16[128,1152]{1,0:T(8,128)(2,1)S(1)}, bf16[128,1152]{1,0:T(8,128)(2,1)S(1)}, u32[]{:S(2)}, u32[]{:S(2)}) collective-permute-start(bf16[128,1152]{1,0:T(8,128)(2,1)S(1)} %collective-permute-done.12), channel_id=1, source_target_pairs={{0,32},{1,481},{32,64},{33,1},{64,96},{65,33},{96,128},{97,65},{12... | collective-permute-start | bytes 884744 | tf_op jit(solution)/shard_map/ppermute | solution.py:28
  55.6 5.0 %collective-permute-start.8 = (bf16[128,1152]{1,0:T(8,128)(2,1)S(1)}, bf16[128,1152]{1,0:T(8,128)(2,1)S(1)}, u32[]{:S(2)}, u32[]{:S(2)}) collective-permute-start(bf16[128,1152]{1,0:T(8,128)(2,1)S(1)} %collective-permute-done.7), channel_id=1, source_target_pairs={{0,32},{1,481},{32,64},{33,1},{64,96},{65,33},{96,128},{97,65},{12... | collective-permute-start | bytes 884744 | tf_op jit(solution)/shard_map/ppermute | solution.py:28
  60.6 3.6 %collective-permute-done.8 = bf16[128,1152]{1,0:T(8,128)(2,1)S(1)} collective-permute-done((bf16[128,1152]{1,0:T(8,128)(2,1)S(1)}, bf16[128,1152]{1,0:T(8,128)(2,1)S(1)}, u32[]{:S(2)}, u32[]{:S(2)}) %collective-permute-start.8) | collective-permute-done | bytes 294944 | tf_op jit(solution)/shard_map/ppermute | solution.py:28
  64.3 9.4 %collective-permute-start.9 = (bf16[5,128,1152]{2,1,0:T(8,128)(2,1)S(1)}, bf16[5,128,1152]{2,1,0:T(8,128)(2,1)S(1)}, u32[]{:S(2)}, u32[]{:S(2)}) collective-permute-start(bf16[5,128,1152]{2,1,0:T(8,128)(2,1)S(1)} %bitcast_dynamic-update-slice_fusion.7), channel_id=1, source_target_pairs={{0,1},{1,0},{2,3},{3,2},{4,5},{5,4},{6,7},{7,6},{8,9},{9,8},{10,11... | collective-permute-start | bytes 4423688 | tf_op jit(solution)/shard_map/ppermute | solution.py:53
  73.7 1.9 collective-permute-start.14
  75.6 1.9 collective-permute-start.15
  77.6 0.6 broadcast_in_dim.67
  78.2 3.2 %collective-permute-done.14 = bf16[128,1152]{1,0:T(8,128)(2,1)S(1)} collective-permute-done((bf16[128,1152]{1,0:T(8,128)(2,1)S(1)}, bf16[128,1152]{1,0:T(8,128)(2,1)S(1)}, u32[]{:S(2)}, u32[]{:S(2)}) %collective-permute-start.14) | collective-permute-done | bytes 294944 | tf_op jit(solution)/shard_map/ppermute | solution.py:28
  81.5 2.8 %collective-permute-start.18 = (bf16[128,1152]{1,0:T(8,128)(2,1)S(1)}, bf16[128,1152]{1,0:T(8,128)(2,1)S(1)}, u32[]{:S(2)}, u32[]{:S(2)}) collective-permute-start(bf16[128,1152]{1,0:T(8,128)(2,1)S(1)} %collective-permute-done.14), channel_id=1, source_target_pairs={{0,32},{1,481},{32,64},{33,1},{64,96},{65,33},{96,128},{97,65},{12... | collective-permute-start | bytes 884744 | tf_op jit(solution)/shard_map/ppermute | solution.py:28
  84.3 0.3 collective-permute-done.15
  84.6 2.8 %collective-permute-start.16 = (bf16[128,1152]{1,0:T(8,128)(2,1)S(1)}, bf16[128,1152]{1,0:T(8,128)(2,1)S(1)}, u32[]{:S(2)}, u32[]{:S(2)}) collective-permute-start(bf16[128,1152]{1,0:T(8,128)(2,1)S(1)} %collective-permute-done.15), channel_id=1, source_target_pairs={{0,32},{1,481},{32,64},{33,1},{64,96},{65,33},{96,128},{97,65},{12... | collective-permute-start | bytes 884744 | tf_op jit(solution)/shard_map/ppermute | solution.py:28
  87.5 1.4 collective-permute-done.18
  88.9 4.0 %collective-permute-start.19 = (bf16[128,1152]{1,0:T(8,128)(2,1)S(1)}, bf16[128,1152]{1,0:T(8,128)(2,1)S(1)}, u32[]{:S(2)}, u32[]{:S(2)}) collective-permute-start(bf16[128,1152]{1,0:T(8,128)(2,1)S(1)} %collective-permute-done.18), channel_id=1, source_target_pairs={{0,32},{1,481},{32,64},{33,1},{64,96},{65,33},{96,128},{97,65},{12... | collective-permute-start | bytes 884744 | tf_op jit(solution)/shard_map/ppermute | solution.py:28
  93.0 0.1 pad_maximum_fusion.1
  93.0 5.4 %collective-permute-start.17 = (bf16[2,128,1152]{2,1,0:T(8,128)(2,1)S(1)}, bf16[2,128,1152]{2,1,0:T(8,128)(2,1)S(1)}, u32[]{:S(2)}, u32[]{:S(2)}) collective-permute-start(bf16[2,128,1152]{2,1,0:T(8,128)(2,1)S(1)} %pad_maximum_fusion.1), channel_id=1, source_target_pairs={{0,1},{1,0},{2,3},{3,2},{4,5},{5,4},{6,7},{7,6},{8,9},{9,8},{10,11... | collective-permute-start | bytes 1769480 | tf_op jit(solution)/shard_map/ppermute | solution.py:53
  98.9 1.2 collective-permute-done.17
  100.3 1.6 fusion.3
  101.9 0.5 copy-done
  102.4 0.1 pad_maximum_fusion
  102.5 20.8 %all_to_all.15 = bf16[16,264,128]{2,1,0:T(8,128)(2,1)S(1)} all-to-all(bf16[16,264,128]{2,1,0:T(8,128)(2,1)S(1)} %pad_maximum_fusion), channel_id=1, replica_groups=mesh['zh'=4,'zl'=4,'ylo'=2,'x'=4,'yhi'=2,'core'=2] {'ylo','yhi','x'}, dimensions={0} | all-to-all | bytes 2162688 | tf_op jit(solution)/shard_map/all_to_all | solution.py:109
  123.3 0.1 convert_reduce_fusion
  123.5 1.2 broadcast_in_dim.79
  124.7 3.7 %all-to-all-start.1 = ((bf16[16,256,128]{2,1,0:T(8,128)(2,1)}), bf16[16,256,128]{2,1,0:T(8,128)(2,1)S(1)}, u32[]{:S(2)}, u32[]{:S(2)}) async-start(bf16[16,256,128]{2,1,0:T(8,128)(2,1)} %broadcast_in_dim.79), calls=%async_computation.1 | async-start | bytes 2097152 | tf_op jit(solution)/shard_map/all_to_all | solution.py:17
  128.4 16.4 %all-gather = bf16[1024,128]{1,0:T(8,128)(2,1)S(1)} all-gather(bf16[256,128]{1,0:T(8,128)(2,1)S(1)} %fusion.39), channel_id=2, replica_groups=mesh['zh'=4,'zl'=4,'ylo'=2,'x'=4,'yhi'=2,'core'=2] {'zh'}, dimensions={0}, use_global_device_ids=true | all-gather | bytes 327680 | tf_op jit(solution)/shard_map/all_gather | solution.py:121
  144.9 1.9 collective-permute-start.22
  146.8 6.1 %collective-permute-start.21 = (bf16[4,256,128]{2,1,0:T(8,128)(2,1)S(1)}, bf16[4,256,128]{2,1,0:T(8,128)(2,1)S(1)}, u32[]{:S(2)}, u32[]{:S(2)}) collective-permute-start(bf16[4,256,128]{2,1,0:T(8,128)(2,1)S(1)} %bitcast.113), channel_id=1, source_target_pairs={{0,480},{1,481},{32,0},{33,1},{64,32},{65,33},{96,64},{97,65},{128... | collective-permute-start | bytes 786440 | tf_op jit(solution)/shard_map/ppermute | solution.py:28
  152.9 4.2 %collective-permute-start.20 = (bf16[4,256,128]{2,1,0:T(8,128)(2,1)S(1)}, bf16[4,256,128]{2,1,0:T(8,128)(2,1)S(1)}, u32[]{:S(2)}, u32[]{:S(2)}) collective-permute-start(bf16[4,256,128]{2,1,0:T(8,128)(2,1)S(1)} %bitcast.114), channel_id=1, source_target_pairs={{0,448},{1,65},{32,480},{33,97},{64,0},{65,129},{96,32},{97,161},{... | collective-permute-start | bytes 786440 | tf_op jit(solution)/shard_map/ppermute | solution.py:28
  157.1 0.1 dynamic-slice_bitcast_fusion.1
  157.2 5.8 %collective-permute-start.24 = (bf16[2,4,256,128]{3,2,1,0:T(8,128)(2,1)S(1)}, bf16[2,4,256,128]{3,2,1,0:T(8,128)(2,1)S(1)}, u32[]{:S(2)}, u32[]{:S(2)}) collective-permute-start(bf16[2,4,256,128]{3,2,1,0:T(8,128)(2,1)S(1)} %pad_maximum_fusion.3), channel_id=1, source_target_pairs={{0,1},{1,0},{2,3},{3,2},{4,5},{5,4},{6,7},{7,6},{8,9},{9,8},{10,11... | collective-permute-start | bytes 1572872 | tf_op jit(solution)/shard_map/ppermute | solution.py:53
  163.0 0.2 convolution_bitcast_fusion.9
  163.3 2.2 %collective-permute-start.23 = (bf16[2,4,256,128]{3,2,1,0:T(8,128)(2,1)S(1)}, bf16[2,4,256,128]{3,2,1,0:T(8,128)(2,1)S(1)}, u32[]{:S(2)}, u32[]{:S(2)}) collective-permute-start(bf16[2,4,256,128]{3,2,1,0:T(8,128)(2,1)S(1)} %pad_maximum_fusion.2), channel_id=1, source_target_pairs={{0,1},{1,0},{2,3},{3,2},{4,5},{5,4},{6,7},{7,6},{8,9},{9,8},{10,11... | collective-permute-start | bytes 1572872 | tf_op jit(solution)/shard_map/ppermute | solution.py:53
  165.5 0.8 collective-permute-done.20
  166.3 0.2 fusion.4
  166.6 0.2 convolution_bitcast_fusion.7
  166.8 0.2 convolution_bitcast_fusion.6
  167.2 0.2 collective-permute-done.23
  167.5 0.2 convolution_bitcast_fusion.5
  167.7 0.2 fusion.5
  168.0 0.2 convolution_bitcast_fusion.3
  168.2 0.2 convolution_bitcast_fusion.2
  168.5 0.2 broadcast_in_dim.81
  168.7 19.7 %all_to_all.16 = bf16[16,256,128]{2,1,0:T(8,128)(2,1)S(1)} all-to-all(bf16[16,256,128]{2,1,0:T(8,128)(2,1)S(1)} %broadcast_in_dim.81), channel_id=1, replica_groups=mesh['zh'=4,'zl'=4,'ylo'=2,'x'=4,'yhi'=2,'core'=2] {'ylo','yhi','x'}, dimensions={0} | all-to-all | bytes 2097152 | tf_op jit(solution)/shard_map/all_to_all | solution.py:17
  188.4 0.9 fusion.2
  189.3 7.0 %collective-permute-start.25 = (bf16[128,1152]{1,0:T(8,128)(2,1)S(1)}, bf16[128,1152]{1,0:T(8,128)(2,1)S(1)}, u32[]{:S(2)}, u32[]{:S(2)}) collective-permute-start(bf16[128,1152]{1,0:T(8,128)(2,1)S(1)} %fusion.2), channel_id=1, source_target_pairs={{0,0},{1,16},{16,1},{17,17},{2,2},{3,18},{18,3},{19,19},{4,4},{5,2... | collective-permute-start | bytes 884744 | tf_op jit(solution)/shard_map/ppermute | solution.py:149
  196.3 0.9 fusion.1
  197.2 1.9 collective-permute-start.26
  199.1 1.6 collective-permute-done.25
  200.7 3.9 %collective-permute-done.26 = bf16[128,1152]{1,0:T(8,128)(2,1)S(1)} collective-permute-done((bf16[128,1152]{1,0:T(8,128)(2,1)S(1)}, bf16[128,1152]{1,0:T(8,128)(2,1)S(1)}, u32[]{:S(2)}, u32[]{:S(2)}) %collective-permute-start.26) | collective-permute-done | bytes 294944 | tf_op jit(solution)/shard_map/ppermute | solution.py:147
  204.7 0.9 convert_add_fusion
  (64 shorter events, 1.3 us)
Async XLA Ops:
  1.1 17.9 %collective-permute-start.3 = (bf16[128,1152]{1,0:T(8,128)(2,1)S(1)}, bf16[128,1152]{1,0:T(8,128)(2,1)S(1)}, u32[]{:S(2)}, u32[]{:S(2)}) collective-permute-start(bf16[128,1152]{1,0:T(8,128)(2,1)S(1)} %convert_element_type.39), channel_id=1, source_target_pairs={{0,1},{1,0},{2,3},{3,2},{4,5},{5,4},{6,7},{7,6},{8,9},{9,8},{10,11... | collective-permute-start | bytes 884744 | tf_op jit(solution)/shard_map/ppermute | solution.py:83
  9.9 11.8 %collective-permute-start.2 = (bf16[128,1152]{1,0:T(8,128)(2,1)S(1)}, bf16[128,1152]{1,0:T(8,128)(2,1)S(1)}, u32[]{:S(2)}, u32[]{:S(2)}) collective-permute-start(bf16[128,1152]{1,0:T(8,128)(2,1)S(1)} %convert_element_type.39), channel_id=1, source_target_pairs={{0,32},{1,48},{16,481},{17,497},{32,64},{33,80},{48,1},{49,17},{64... | collective-permute-start | bytes 884744 | tf_op jit(solution)/shard_map/ppermute | solution.py:49
  11.8 18.0 %collective-permute-start = (bf16[128,1152]{1,0:T(8,128)(2,1)S(1)}, bf16[128,1152]{1,0:T(8,128)(2,1)S(1)}, u32[]{:S(2)}, u32[]{:S(2)}) collective-permute-start(bf16[128,1152]{1,0:T(8,128)(2,1)S(1)} %convert_element_type.39), channel_id=1, source_target_pairs={{0,0},{1,16},{16,1},{17,17},{2,2},{3,18},{18,3},{19,19},{4,4},{5,2... | collective-permute-start | bytes 884744 | tf_op jit(solution)/shard_map/ppermute | solution.py:80
  19.0 12.9 %collective-permute-start.4 = (bf16[128,1152]{1,0:T(8,128)(2,1)S(1)}, bf16[128,1152]{1,0:T(8,128)(2,1)S(1)}, u32[]{:S(2)}, u32[]{:S(2)}) collective-permute-start(bf16[128,1152]{1,0:T(8,128)(2,1)S(1)} %collective-permute-done.3), channel_id=1, source_target_pairs={{0,497},{1,481},{16,48},{17,32},{32,17},{33,1},{48,80},{49,64},{64... | collective-permute-start | bytes 884744 | tf_op jit(solution)/shard_map/ppermute | solution.py:49
  21.7 12.9 %collective-permute-start.10 = (bf16[128,1152]{1,0:T(8,128)(2,1)S(1)}, bf16[128,1152]{1,0:T(8,128)(2,1)S(1)}, u32[]{:S(2)}, u32[]{:S(2)}) collective-permute-start(bf16[128,1152]{1,0:T(8,128)(2,1)S(1)} %collective-permute-done.2), channel_id=1, source_target_pairs={{0,32},{1,481},{32,64},{33,1},{64,96},{65,33},{96,128},{97,65},{12... | collective-permute-start | bytes 884744 | tf_op jit(solution)/shard_map/ppermute | solution.py:28
  29.9 70.4 %collective-permute-start.1 = (bf16[128,1152]{1,0:T(8,128)(2,1)S(1)}, bf16[128,1152]{1,0:T(8,128)(2,1)S(1)}, u32[]{:S(2)}, u32[]{:S(2)}) collective-permute-start(bf16[128,1152]{1,0:T(8,128)(2,1)S(1)} %collective-permute-done), channel_id=1, source_target_pairs={{0,1},{1,0},{2,3},{3,2},{4,5},{5,4},{6,7},{7,6},{8,9},{9,8},{10,11... | collective-permute-start | bytes 884744 | tf_op jit(solution)/shard_map/ppermute | solution.py:81
  31.9 7.8 %collective-permute-start.5 = (bf16[128,1152]{1,0:T(8,128)(2,1)S(1)}, bf16[128,1152]{1,0:T(8,128)(2,1)S(1)}, u32[]{:S(2)}, u32[]{:S(2)}) collective-permute-start(bf16[128,1152]{1,0:T(8,128)(2,1)S(1)} %collective-permute-done.4), channel_id=1, source_target_pairs={{0,32},{1,481},{32,64},{33,1},{64,96},{65,33},{96,128},{97,65},{12... | collective-permute-start | bytes 884744 | tf_op jit(solution)/shard_map/ppermute | solution.py:28
  34.6 8.7 %collective-permute-start.11 = (bf16[128,1152]{1,0:T(8,128)(2,1)S(1)}, bf16[128,1152]{1,0:T(8,128)(2,1)S(1)}, u32[]{:S(2)}, u32[]{:S(2)}) collective-permute-start(bf16[128,1152]{1,0:T(8,128)(2,1)S(1)} %collective-permute-done.10), channel_id=1, source_target_pairs={{0,32},{1,481},{32,64},{33,1},{64,96},{65,33},{96,128},{97,65},{12... | collective-permute-start | bytes 884744 | tf_op jit(solution)/shard_map/ppermute | solution.py:28
  39.7 7.5 %collective-permute-start.6 = (bf16[128,1152]{1,0:T(8,128)(2,1)S(1)}, bf16[128,1152]{1,0:T(8,128)(2,1)S(1)}, u32[]{:S(2)}, u32[]{:S(2)}) collective-permute-start(bf16[128,1152]{1,0:T(8,128)(2,1)S(1)} %collective-permute-done.5), channel_id=1, source_target_pairs={{0,32},{1,481},{32,64},{33,1},{64,96},{65,33},{96,128},{97,65},{12... | collective-permute-start | bytes 884744 | tf_op jit(solution)/shard_map/ppermute | solution.py:28
  43.3 8.7 %collective-permute-start.12 = (bf16[128,1152]{1,0:T(8,128)(2,1)S(1)}, bf16[128,1152]{1,0:T(8,128)(2,1)S(1)}, u32[]{:S(2)}, u32[]{:S(2)}) collective-permute-start(bf16[128,1152]{1,0:T(8,128)(2,1)S(1)} %collective-permute-done.11), channel_id=1, source_target_pairs={{0,32},{1,481},{32,64},{33,1},{64,96},{65,33},{96,128},{97,65},{12... | collective-permute-start | bytes 884744 | tf_op jit(solution)/shard_map/ppermute | solution.py:28
  47.2 8.4 %collective-permute-start.7 = (bf16[128,1152]{1,0:T(8,128)(2,1)S(1)}, bf16[128,1152]{1,0:T(8,128)(2,1)S(1)}, u32[]{:S(2)}, u32[]{:S(2)}) collective-permute-start(bf16[128,1152]{1,0:T(8,128)(2,1)S(1)} %collective-permute-done.6), channel_id=1, source_target_pairs={{0,32},{1,481},{32,64},{33,1},{64,96},{65,33},{96,128},{97,65},{12... | collective-permute-start | bytes 884744 | tf_op jit(solution)/shard_map/ppermute | solution.py:28
  51.9 21.8 %collective-permute-start.13 = (bf16[128,1152]{1,0:T(8,128)(2,1)S(1)}, bf16[128,1152]{1,0:T(8,128)(2,1)S(1)}, u32[]{:S(2)}, u32[]{:S(2)}) collective-permute-start(bf16[128,1152]{1,0:T(8,128)(2,1)S(1)} %collective-permute-done.12), channel_id=1, source_target_pairs={{0,32},{1,481},{32,64},{33,1},{64,96},{65,33},{96,128},{97,65},{12... | collective-permute-start | bytes 884744 | tf_op jit(solution)/shard_map/ppermute | solution.py:28
  55.6 8.7 %collective-permute-start.8 = (bf16[128,1152]{1,0:T(8,128)(2,1)S(1)}, bf16[128,1152]{1,0:T(8,128)(2,1)S(1)}, u32[]{:S(2)}, u32[]{:S(2)}) collective-permute-start(bf16[128,1152]{1,0:T(8,128)(2,1)S(1)} %collective-permute-done.7), channel_id=1, source_target_pairs={{0,32},{1,481},{32,64},{33,1},{64,96},{65,33},{96,128},{97,65},{12... | collective-permute-start | bytes 884744 | tf_op jit(solution)/shard_map/ppermute | solution.py:28
  64.3 34.3 %collective-permute-start.9 = (bf16[5,128,1152]{2,1,0:T(8,128)(2,1)S(1)}, bf16[5,128,1152]{2,1,0:T(8,128)(2,1)S(1)}, u32[]{:S(2)}, u32[]{:S(2)}) collective-permute-start(bf16[5,128,1152]{2,1,0:T(8,128)(2,1)S(1)} %bitcast_dynamic-update-slice_fusion.7), channel_id=1, source_target_pairs={{0,1},{1,0},{2,3},{3,2},{4,5},{5,4},{6,7},{7,6},{8,9},{9,8},{10,11... | collective-permute-start | bytes 4423688 | tf_op jit(solution)/shard_map/ppermute | solution.py:53
  73.7 7.8 %collective-permute-start.14 = (bf16[128,1152]{1,0:T(8,128)(2,1)S(1)}, bf16[128,1152]{1,0:T(8,128)(2,1)S(1)}, u32[]{:S(2)}, u32[]{:S(2)}) collective-permute-start(bf16[128,1152]{1,0:T(8,128)(2,1)S(1)} %collective-permute-done.13), channel_id=1, source_target_pairs={{0,32},{1,481},{32,64},{33,1},{64,96},{65,33},{96,128},{97,65},{12... | collective-permute-start | bytes 884744 | tf_op jit(solution)/shard_map/ppermute | solution.py:28
  75.6 9.0 %collective-permute-start.15 = (bf16[128,1152]{1,0:T(8,128)(2,1)S(1)}, bf16[128,1152]{1,0:T(8,128)(2,1)S(1)}, u32[]{:S(2)}, u32[]{:S(2)}) collective-permute-start(bf16[128,1152]{1,0:T(8,128)(2,1)S(1)} %collective-permute-done.8), channel_id=1, source_target_pairs={{0,32},{1,481},{32,64},{33,1},{64,96},{65,33},{96,128},{97,65},{12... | collective-permute-start | bytes 884744 | tf_op jit(solution)/shard_map/ppermute | solution.py:28
  81.5 7.5 %collective-permute-start.18 = (bf16[128,1152]{1,0:T(8,128)(2,1)S(1)}, bf16[128,1152]{1,0:T(8,128)(2,1)S(1)}, u32[]{:S(2)}, u32[]{:S(2)}) collective-permute-start(bf16[128,1152]{1,0:T(8,128)(2,1)S(1)} %collective-permute-done.14), channel_id=1, source_target_pairs={{0,32},{1,481},{32,64},{33,1},{64,96},{65,33},{96,128},{97,65},{12... | collective-permute-start | bytes 884744 | tf_op jit(solution)/shard_map/ppermute | solution.py:28
  84.6 8.3 %collective-permute-start.16 = (bf16[128,1152]{1,0:T(8,128)(2,1)S(1)}, bf16[128,1152]{1,0:T(8,128)(2,1)S(1)}, u32[]{:S(2)}, u32[]{:S(2)}) collective-permute-start(bf16[128,1152]{1,0:T(8,128)(2,1)S(1)} %collective-permute-done.15), channel_id=1, source_target_pairs={{0,32},{1,481},{32,64},{33,1},{64,96},{65,33},{96,128},{97,65},{12... | collective-permute-start | bytes 884744 | tf_op jit(solution)/shard_map/ppermute | solution.py:28
  88.9 11.3 %collective-permute-start.19 = (bf16[128,1152]{1,0:T(8,128)(2,1)S(1)}, bf16[128,1152]{1,0:T(8,128)(2,1)S(1)}, u32[]{:S(2)}, u32[]{:S(2)}) collective-permute-start(bf16[128,1152]{1,0:T(8,128)(2,1)S(1)} %collective-permute-done.18), channel_id=1, source_target_pairs={{0,32},{1,481},{32,64},{33,1},{64,96},{65,33},{96,128},{97,65},{12... | collective-permute-start | bytes 884744 | tf_op jit(solution)/shard_map/ppermute | solution.py:28
  93.0 7.1 %collective-permute-start.17 = (bf16[2,128,1152]{2,1,0:T(8,128)(2,1)S(1)}, bf16[2,128,1152]{2,1,0:T(8,128)(2,1)S(1)}, u32[]{:S(2)}, u32[]{:S(2)}) collective-permute-start(bf16[2,128,1152]{2,1,0:T(8,128)(2,1)S(1)} %pad_maximum_fusion.1), channel_id=1, source_target_pairs={{0,1},{1,0},{2,3},{3,2},{4,5},{5,4},{6,7},{7,6},{8,9},{9,8},{10,11... | collective-permute-start | bytes 1769480 | tf_op jit(solution)/shard_map/ppermute | solution.py:53
  100.3 2.1 %copy-start = (bf16[16,128,1152]{2,1,0:T(8,128)(2,1)}, bf16[16,128,1152]{2,1,0:T(8,128)(2,1)S(1)}, u32[]{:S(2)}) copy-start(bf16[16,128,1152]{2,1,0:T(8,128)(2,1)S(1)} %bitcast_dynamic-update-slice_fusion) | copy-start | bytes 14155780
  124.7 32.4 %all-to-all-start.1 = ((bf16[16,256,128]{2,1,0:T(8,128)(2,1)}), bf16[16,256,128]{2,1,0:T(8,128)(2,1)S(1)}, u32[]{:S(2)}, u32[]{:S(2)}) async-start(bf16[16,256,128]{2,1,0:T(8,128)(2,1)} %broadcast_in_dim.79), calls=%async_computation.1 | async-start | bytes 2097152 | tf_op jit(solution)/shard_map/all_to_all | solution.py:17
  144.9 21.9 %collective-permute-start.22 = (bf16[4,256,128]{2,1,0:T(8,128)(2,1)S(1)}, bf16[4,256,128]{2,1,0:T(8,128)(2,1)S(1)}, u32[]{:S(2)}, u32[]{:S(2)}) collective-permute-start(bf16[4,256,128]{2,1,0:T(8,128)(2,1)S(1)} %bitcast.112), channel_id=1, source_target_pairs={{0,32},{1,33},{32,64},{33,65},{64,96},{65,97},{96,128},{97,129},{1... | collective-permute-start | bytes 786440 | tf_op jit(solution)/shard_map/ppermute | solution.py:28
  146.8 19.8 %collective-permute-start.21 = (bf16[4,256,128]{2,1,0:T(8,128)(2,1)S(1)}, bf16[4,256,128]{2,1,0:T(8,128)(2,1)S(1)}, u32[]{:S(2)}, u32[]{:S(2)}) collective-permute-start(bf16[4,256,128]{2,1,0:T(8,128)(2,1)S(1)} %bitcast.113), channel_id=1, source_target_pairs={{0,480},{1,481},{32,0},{33,1},{64,32},{65,33},{96,64},{97,65},{128... | collective-permute-start | bytes 786440 | tf_op jit(solution)/shard_map/ppermute | solution.py:28
  152.9 13.5 %collective-permute-start.20 = (bf16[4,256,128]{2,1,0:T(8,128)(2,1)S(1)}, bf16[4,256,128]{2,1,0:T(8,128)(2,1)S(1)}, u32[]{:S(2)}, u32[]{:S(2)}) collective-permute-start(bf16[4,256,128]{2,1,0:T(8,128)(2,1)S(1)} %bitcast.114), channel_id=1, source_target_pairs={{0,448},{1,65},{32,480},{33,97},{64,0},{65,129},{96,32},{97,161},{... | collective-permute-start | bytes 786440 | tf_op jit(solution)/shard_map/ppermute | solution.py:28
  157.2 9.8 %collective-permute-start.24 = (bf16[2,4,256,128]{3,2,1,0:T(8,128)(2,1)S(1)}, bf16[2,4,256,128]{3,2,1,0:T(8,128)(2,1)S(1)}, u32[]{:S(2)}, u32[]{:S(2)}) collective-permute-start(bf16[2,4,256,128]{3,2,1,0:T(8,128)(2,1)S(1)} %pad_maximum_fusion.3), channel_id=1, source_target_pairs={{0,1},{1,0},{2,3},{3,2},{4,5},{5,4},{6,7},{7,6},{8,9},{9,8},{10,11... | collective-permute-start | bytes 1572872 | tf_op jit(solution)/shard_map/ppermute | solution.py:53
  163.3 25.2 %slice-start = ((s8[4718592]{0:T(1024)(128)(4,1)}), s8[4194304]{0:T(1024)(128)(4,1)S(1)}, s32[]{:S(2)}) async-start(s8[4718592]{0:T(1024)(128)(4,1)} %bitcast.105), calls=%async_computation.3 | async-start | bytes 8388608
  163.3 4.1 %collective-permute-start.23 = (bf16[2,4,256,128]{3,2,1,0:T(8,128)(2,1)S(1)}, bf16[2,4,256,128]{3,2,1,0:T(8,128)(2,1)S(1)}, u32[]{:S(2)}, u32[]{:S(2)}) collective-permute-start(bf16[2,4,256,128]{3,2,1,0:T(8,128)(2,1)S(1)} %pad_maximum_fusion.2), channel_id=1, source_target_pairs={{0,1},{1,0},{2,3},{3,2},{4,5},{5,4},{6,7},{7,6},{8,9},{9,8},{10,11... | collective-permute-start | bytes 1572872 | tf_op jit(solution)/shard_map/ppermute | solution.py:53
  167.5 21.0 %slice-start.1 = ((s8[4718592]{0:T(1024)(128)(4,1)}), s8[524288]{0:T(1024)(128)(4,1)S(1)}, s32[]{:S(2)}) async-start(s8[4718592]{0:T(1024)(128)(4,1)} %bitcast.105), calls=%async_computation.4 | async-start | bytes 1048576
  189.3 11.4 %collective-permute-start.25 = (bf16[128,1152]{1,0:T(8,128)(2,1)S(1)}, bf16[128,1152]{1,0:T(8,128)(2,1)S(1)}, u32[]{:S(2)}, u32[]{:S(2)}) collective-permute-start(bf16[128,1152]{1,0:T(8,128)(2,1)S(1)} %fusion.2), channel_id=1, source_target_pairs={{0,0},{1,16},{16,1},{17,17},{2,2},{3,18},{18,3},{19,19},{4,4},{5,2... | collective-permute-start | bytes 884744 | tf_op jit(solution)/shard_map/ppermute | solution.py:149
  197.2 7.5 %collective-permute-start.26 = (bf16[128,1152]{1,0:T(8,128)(2,1)S(1)}, bf16[128,1152]{1,0:T(8,128)(2,1)S(1)}, u32[]{:S(2)}, u32[]{:S(2)}) collective-permute-start(bf16[128,1152]{1,0:T(8,128)(2,1)S(1)} %fusion.1), channel_id=1, source_target_pairs={{0,16},{1,0},{16,17},{17,1},{2,18},{3,2},{18,19},{19,3},{4,20},{5,... | collective-permute-start | bytes 884744 | tf_op jit(solution)/shard_map/ppermute | solution.py:147
